TPU v7x, 256 devices: a whole 4x4x8 slice. The times are simulated.
256 devices in a mesh: kgrp: 4 (over x_hi, core), band: 64 (over y, x_lo, z).
Axes of the slice: x: 4 (x_hi: 2, x_lo: 2; x = x_hi * 2 + x_lo), y: 4, z: 8, core: 2. Of those that a mesh axis runs over, the one named last changes fastest.
Arguments:
- orbitals: bfloat16 [4, 2, 4096, 432], P('kgrp', None, 'band'), may hold values from -1.75 to 1.75
- kernels: bfloat16 [4, 2, 4096, 4096], P(None, None, 'band'), may hold values from -0.0014648438 to 0.0014648438
- pair_kdiff: int32 [4], P('kgrp'), may hold values from 0 to 7
- stored_kernel_index: int32 [8], replicated, may hold values from 0 to 3
Outputs:
- exchange: float32 [4, 2, 186624], P('kgrp', None, 'band')
All inputs are finite; a program needn't handle non-finite values.
Results may differ from a plain program's by a relative error of at most 0.0041.
Values may be sent and summed in bfloat16 or wider, within the bound.
No kernel may reach another device: no remote copies, remote signals or barrier semaphores. Data moves between devices by JAX's collectives and lax.ppermute only.
A program may use at most 128 MiB of HBM per device.

v0:
```python
import jax
import jax.numpy as jnp
from jax import lax
from jax.sharding import PartitionSpec as P


def from_behind(block, axis, distance):
    devices = range(lax.axis_size(axis))
    route = [((i - distance) % len(devices), i) for i in devices]
    return lax.ppermute(block, axis, route)


def contract_last(leading, trailing):
    return lax.dot_general(
        leading, trailing, (((1,), (1,)), ((), ())), preferred_element_type=jnp.float32
    )


def contract_first(leading, trailing):
    return lax.dot_general(
        leading, trailing, (((0,), (0,)), ((), ())), preferred_element_type=jnp.float32
    )


def product(leading, trailing):
    return jnp.dot(leading, trailing, preferred_element_type=jnp.float32)


def density(first_rows, second_rows):
    real_part = contract_last(first_rows[0], second_rows[0]) + contract_last(
        first_rows[1], second_rows[1]
    )
    imag_part = contract_last(first_rows[1], second_rows[0]) - contract_last(
        first_rows[0], second_rows[1]
    )
    return (real_part, imag_part)


def project(orbit_rows, real_part, imag_part):
    real_half = real_part.astype(jnp.bfloat16)
    imag_half = imag_part.astype(jnp.bfloat16)
    matrix_real = -(
        contract_first(orbit_rows[0], real_half) + contract_first(orbit_rows[1], imag_half)
    )
    matrix_imag = -(
        contract_first(orbit_rows[0], imag_half) - contract_first(orbit_rows[1], real_half)
    )
    return jnp.stack([matrix_real, matrix_imag]).reshape(1, 2, -1)


def kernel_columns(kernel):
    kern_real = kernel[0].astype(jnp.float32)
    kern_imag = kernel[1].astype(jnp.float32)
    return (kern_real, kern_imag)


def accumulate(
    near_rows,
    near_piece,
    self_rows,
    self_piece,
    first_kernel,
    second_kernel,
    first_mult,
    second_mult,
):
    kern_real, kern_imag = kernel_columns(first_kernel)
    back_real, back_imag = kernel_columns(second_kernel)
    near_real, near_imag = density(near_rows, near_piece)
    self_real, self_imag = density(self_rows, self_piece)
    first_real = (kern_real * near_real - kern_imag * near_imag).astype(jnp.bfloat16)
    first_imag = (kern_real * near_imag + kern_imag * near_real).astype(jnp.bfloat16)
    second_real = (back_real * self_real + back_imag * self_imag).astype(jnp.bfloat16)
    second_imag = (back_real * self_imag - back_imag * self_real).astype(jnp.bfloat16)
    ones_real = product(first_real, first_mult[0]) - product(first_imag, first_mult[1])
    ones_imag = product(first_real, first_mult[1]) + product(first_imag, first_mult[0])
    twos_real = product(second_real, second_mult[0]) - product(second_imag, second_mult[1])
    twos_imag = product(second_real, second_mult[1]) + product(second_imag, second_mult[0])
    return (ones_real, ones_imag, twos_real, twos_imag)


def pick_kernel(kernels, stored_kernel_index, kpoint_difference):
    table_entries = jnp.arange(stored_kernel_index.shape[0], dtype=jnp.int32)
    kernel_slot = jnp.sum(jnp.where(table_entries == kpoint_difference, stored_kernel_index, 0))
    return lax.dynamic_index_in_dim(kernels, kernel_slot, 0, keepdims=False)


def on_device(orbitals, kernels, pair_kdiff, stored_kernel_index):
    own_rows = orbitals[0]
    kernel = pick_kernel(kernels, stored_kernel_index, pair_kdiff[0])
    partner_rows = from_behind(own_rows, "kgrp", 1)
    pieces = (
        lax.all_gather(own_rows, "band", axis=1, tiled=True),
        lax.all_gather(partner_rows, "band", axis=1, tiled=True),
    )
    totals = accumulate(
        partner_rows, pieces[1], own_rows, pieces[0], kernel, kernel, pieces[0], pieces[1]
    )
    own_term = project(own_rows, totals[0], totals[1])
    partner_term = project(partner_rows, totals[2], totals[3])
    returned = from_behind(partner_term, "kgrp", -1)
    return lax.psum_scatter(own_term + returned, "band", scatter_dimension=2, tiled=True)


def solution(mesh):
    return jax.shard_map(
        on_device,
        mesh=mesh,
        in_specs=(P("kgrp", None, "band", None), P(None, None, "band", None), P("kgrp"), P()),
        out_specs=P("kgrp", None, "band"),
        check_vma=False,
    )
```

profile of v0, /device:TPU:6, one launch (start us, length us, event | category | flops | bytes accessed | tf_op | source)
XLA Modules:
  0.0 1284.8 jit_solution(141974709856938587)
XLA Ops:
  7.4 6.1 collective-permute-done
  14.9 1.3 fusion.56
  17.9 295.3 %all-gather.6.cloned.1.call-done = bf16[1,2,4096,432]{3,2,1,0:T(8,128)(2,1)} async-done(((bf16[1,2,64,432]{3,2,1,0:T(8,128)(2,1)}), bf16[1,2,4096,432]{3,2,1,0:T(8,128)(2,1)}) %all-gather.6.cloned.1.call-update) | async-done | bytes 7077904 | tf_op jit(solution)/shard_map/all_gather | solution.py:93
  313.2 3.7 fusion.7
  317.0 3.6 fusion.6
  320.6 1.4 convolution_add_fusion
  321.9 1.4 convolution_subtract_fusion
  323.3 301.2 %all-gather.4.cloned.1.call-done = bf16[2,4096,432]{2,1,0:T(8,128)(2,1)} async-done(((bf16[2,64,432]{2,1,0:T(8,128)(2,1)}), bf16[2,4096,432]{2,1,0:T(8,128)(2,1)}) %all-gather.4.cloned.1.call-update) | async-done | bytes 7077904 | tf_op jit(solution)/shard_map/all_gather | solution.py:94
  624.6 3.7 fusion.4
  628.3 3.6 fusion.5
  631.9 1.4 convolution_subtract_fusion.1
  633.2 2.9 fusion.29
  636.2 0.8 fusion.9
  637.1 0.8 fusion.27
  638.2 0.8 fusion
  639.1 0.8 fusion.3
  639.9 0.8 fusion.25
  641.4 0.8 fusion.24
  643.4 2.2 stack.21
  645.7 1.1 fusion.46
  646.8 1.1 fusion.13
  648.3 1.6 stack.22
  649.8 3.2 pad_maximum_fusion
  653.1 3.2 fusion.8
  656.2 3.0 fusion.26
  660.2 1.4 stack.18
  661.6 1.1 fusion.42
  663.3 1.4 stack.19
  664.7 5.7 collective-permute-done.1
  670.4 3.7 maximum_add_fusion
  675.4 601.4 %all-reduce.3.cloned.1.call-done = f32[1,2,186624]{2,1,0:T(2,128)} async-done(((f32[1,2,186624]{2,1,0:T(2,128)}), f32[1,2,186624]{2,1,0:T(2,128)}) %all-reduce.3.cloned.1.call-update) | async-done | bytes 1493008
  1276.9 1.4 constant_dynamic-slice_fusion
  (43 shorter events, 6.1 us)
Async XLA Ops:
  6.5 310.4 %copy-start.2 = (bf16[1,2,64,432]{3,2,1,0:T(8,128)(2,1)S(1)}, bf16[1,2,64,432]{3,2,1,0:T(8,128)(2,1)}, u32[]{:S(2)}) copy-start(bf16[1,2,64,432]{3,2,1,0:T(8,128)(2,1)} %param.4) | copy-start | bytes 331780
  6.5 306.7 %all-gather.6.cloned.1.call-start = ((), (), s32[]{:S(2)}) async-start(), calls=%async_computation.1 | async-start | bytes 8519680 | tf_op jit(solution)/shard_map/all_gather | solution.py:93
  7.3 617.3 %all-gather.4.cloned.1.call-start = ((), (), s32[]{:S(2)}) async-start(), calls=%async_computation | async-start | bytes 8519680 | tf_op jit(solution)/shard_map/all_gather | solution.py:94
  7.3 6.2 collective-permute-start
  13.5 0.6 copy-start.3
  14.2 1262.7 %all-reduce.3.cloned.1.call-start = ((), (), s32[]{:S(2)}) async-start(), calls=%async_computation.2 | async-start | bytes 2985984
  313.2 7.3 copy-start.1
  321.9 302.6 %copy-start.4 = (bf16[2,64,432]{2,1,0:T(8,128)(2,1)S(1)}, bf16[2,64,432]{2,1,0:T(8,128)(2,1)}, u32[]{:S(2)}) copy-start(bf16[2,64,432]{2,1,0:T(8,128)(2,1)} %copy-done.3) | copy-start | bytes 331780
  624.6 7.3 copy-start
  631.8 4.3 slice-start
  633.2 3.0 slice-start.1
  636.2 1.7 copy-start.5
  640.7 0.6 copy-start.6
  642.2 0.6 copy-start.7
  653.0 17.4 %collective-permute-start.1 = (f32[1,2,186624]{2,1,0:T(2,128)}, f32[1,2,186624]{2,1,0:T(2,128)}, u32[]{:S(2)}, u32[]{:S(2)}) collective-permute-start(f32[1,2,186624]{2,1,0:T(2,128)} %pad_maximum_fusion), channel_id=1, source_target_pairs={{64,0},{128,64},{192,128},{0,192},{65,1},{129,65},{193,129},{1,193... | collective-permute-start | bytes 4478984 | tf_op jit(solution)/shard_map/ppermute | solution.py:10
  659.3 0.6 copy-start.8
  663.3 10.9 copy-start.9
Sparse Core Ops, SparseCore 0:
  9.2 304.0 all-gather.5
  315.0 309.4 all-gather.3
  674.3 602.5 all-reduce.2
where the time goes:
time: 1290 us; the launch traced here: 1280 us
  waiting for transfers between devices  1210 us (94%)
  matrix products  37.7 us (3%)
  between operations  16.4 us (1%)
    unnamed x4, waiting for transfers between devices  602 us
    all_gather x1, waiting for transfers between devices, on_device(): lax.all_gather(partner_rows, 'band', axis=1, tiled=True)  301 us
    all_gather x1, waiting for transfers between devices, on_device(): lax.all_gather(own_rows, 'band', axis=1, tiled=True)  295 us
  transfers between devices with their start and end apart: 5, of which 5 were waited for; matrix products, arithmetic and copies ran while one was open for 2% of the time, Pallas kernels for 0%

commit v1 on v0

v1 whole, which is shorter than its diff:
```python
import functools

import jax
import jax.numpy as jnp
import numpy as np
from jax import lax
from jax.experimental import pallas as pl
from jax.experimental.pallas import tpu as pltpu
from jax.sharding import PartitionSpec as P

NB = 432
SLAB = 64
NY, NX, NZ = 4, 2, 8
GROUPS = NY * NX
BLOCK = NZ * SLAB
KEEP = 16
VMEM = 56 * 1024 * 1024

OFFSETS = [(dy, dx) for dy in range(NY) for dx in range(NX)]
Z_OFFSETS = [0, 1, -1, 2, -2, 3, -3, 4]


def band_route(dy, dx, dz):
    route = []
    for y in range(NY):
        for x in range(NX):
            for z in range(NZ):
                there = ((y + dy) % NY * NX + (x + dx) % NX) * NZ + (z + dz) % NZ
                route.append(((y * NX + x) * NZ + z, there))
    return route


def shift(block, dy, dx, dz):
    return lax.ppermute(block, "band", band_route(dy, dx, dz))


def swap_groups(block, bit):
    return lax.ppermute(block, "kgrp", [(k, k ^ bit) for k in range(4)])


def dot(a, b, dims):
    return lax.dot_general(a, b, ((dims[0], dims[1]), ((), ())), preferred_element_type=jnp.float32)


def pack_body(slot_ref, dest_ref, kernels_ref, *refs):
    outs, sem = refs[:GROUPS], refs[GROUPS]
    copies = []
    for which in range(2):
        for i in range(GROUPS):
            start = pl.multiple_of(dest_ref[i] * BLOCK, BLOCK)
            copies.append(
                pltpu.make_async_copy(
                    kernels_ref.at[slot_ref[which], :, :, pl.ds(start, BLOCK)],
                    outs[i].at[which],
                    sem.at[which, i],
                )
            )
    for copy in copies:
        copy.start()
    for copy in copies:
        copy.wait()


def pack(slots, dests, kernels):
    piece = jax.ShapeDtypeStruct((2, 2, SLAB, BLOCK), jnp.bfloat16)
    return pl.pallas_call(
        pack_body,
        out_shape=[piece] * GROUPS,
        in_specs=[
            pl.BlockSpec(memory_space=pltpu.SMEM),
            pl.BlockSpec(memory_space=pltpu.SMEM),
            pl.BlockSpec(memory_space=pl.ANY),
        ],
        out_specs=[pl.BlockSpec(memory_space=pl.ANY)] * GROUPS,
        scratch_shapes=[pltpu.SemaphoreType.DMA((2, GROUPS))],
        name="pack",
    )(slots, dests, kernels)


def mix_body(n_rows, n_cols, place_ref, sign_ref, *refs):
    rows, refs = refs[:n_rows], refs[n_rows:]
    cols, refs = refs[:n_cols], refs[n_cols:]
    kerns, refs = refs[:GROUPS], refs[GROUPS:]
    m_ref, row_ref, col_ref, other_rows, other_cols = refs
    for i in range(GROUPS):
        at = pl.ds(i * SLAB, SLAB)
        row_ref[:, at, :] = rows[i][0]
        other_rows[:, at, :] = rows[i][1]
    for i in range(NZ):
        at = pl.ds(pl.multiple_of(place_ref[i] * SLAB, SLAB), SLAB)
        col_ref[:, at, :] = cols[i][0]
        other_cols[:, at, :] = cols[i][1]
    last = ((1,), (1,))
    per = 2 * SLAB
    for part in range(GROUPS // 2):
        at = pl.ds(part * per, per)
        total_re = total_im = None
        for which, (a_ref, b_ref) in enumerate(((row_ref, col_ref), (other_rows, other_cols))):
            a_re, a_im = a_ref[0, at, :], a_ref[1, at, :]
            p_re = dot(a_re, b_ref[0], last) + dot(a_im, b_ref[1], last)
            p_im = dot(a_im, b_ref[0], last) - dot(a_re, b_ref[1], last)
            sign = sign_ref[which]
            k_re = jnp.concatenate(
                [kerns[2 * part][which, 0], kerns[2 * part + 1][which, 0]], axis=0
            ).astype(jnp.float32)
            k_im = jnp.concatenate(
                [kerns[2 * part][which, 1], kerns[2 * part + 1][which, 1]], axis=0
            ).astype(jnp.float32) * sign
            m_re = k_re * p_re - k_im * p_im
            m_im = k_re * p_im + k_im * p_re
            total_re = m_re if total_re is None else total_re + m_re
            total_im = m_im if total_im is None else total_im + m_im
        m_ref[0, at, :] = total_re.astype(jnp.bfloat16)
        m_ref[1, at, :] = total_im.astype(jnp.bfloat16)


def mix(place, sign, rows, cols, kerns):
    vmem = pl.BlockSpec(memory_space=pltpu.VMEM)
    smem = pl.BlockSpec(memory_space=pltpu.SMEM)
    points = jax.ShapeDtypeStruct((2, BLOCK, NB), jnp.bfloat16)
    return pl.pallas_call(
        functools.partial(mix_body, len(rows), len(cols)),
        out_shape=[jax.ShapeDtypeStruct((2, BLOCK, BLOCK), jnp.bfloat16), points, points],
        in_specs=[smem, smem] + [vmem] * (len(rows) + len(cols) + len(kerns)),
        out_specs=[vmem] * 3,
        scratch_shapes=[pltpu.VMEM((2, BLOCK, NB), jnp.bfloat16)] * 2,
        compiler_params=pltpu.CompilerParams(vmem_limit_bytes=VMEM),
        name="mix",
    )(place, sign, *rows, *cols, *kerns)


def project_body(m_ref, row_ref, col_ref, out_ref, x_ref):
    mid = ((1,), (0,))
    first = ((0,), (0,))
    m_re, m_im = m_ref[0], m_ref[1]
    c_re, c_im = col_ref[0], col_ref[1]
    y_re = (dot(m_re, c_re, mid) - dot(m_im, c_im, mid)).astype(jnp.bfloat16)
    y_im = (dot(m_re, c_im, mid) + dot(m_im, c_re, mid)).astype(jnp.bfloat16)
    r_re, r_im = row_ref[0], row_ref[1]
    x_ref[:, pl.ds(NB, 8), :] = jnp.zeros((2, 8, NB), jnp.float32)
    x_ref[0, pl.ds(0, NB), :] = -(dot(r_re, y_re, first) + dot(r_im, y_im, first))
    x_ref[1, pl.ds(0, NB), :] = dot(r_im, y_re, first) - dot(r_re, y_im, first)
    for d in range(GROUPS * NZ):
        at = pl.ds(27 * d // 4, 8)
        window = jnp.concatenate([x_ref[0, at, :], x_ref[1, at, :]], axis=0)
        out_ref[d] = window.astype(jnp.bfloat16)


def project(m, rows, cols):
    vmem = pl.BlockSpec(memory_space=pltpu.VMEM)
    return pl.pallas_call(
        project_body,
        out_shape=jax.ShapeDtypeStruct((GROUPS * NZ, KEEP, NB), jnp.bfloat16),
        in_specs=[vmem] * 3,
        out_specs=vmem,
        scratch_shapes=[pltpu.VMEM((2, NB + 8, NB), jnp.float32)],
        compiler_params=pltpu.CompilerParams(vmem_limit_bytes=VMEM),
        name="project",
    )(m, rows, cols)


def reduce_windows(windows):
    over_yx = [[g * NZ + z for g in range(GROUPS)] for z in range(NZ)]
    over_z = [[g * NZ + z for z in range(NZ)] for g in range(GROUPS)]
    parts = windows.reshape(GROUPS, NZ, KEEP, NB)
    parts = lax.all_to_all(parts, "band", 0, 0, axis_index_groups=over_yx)
    parts = jnp.sum(parts.astype(jnp.float32), axis=0)
    parts = lax.all_to_all(parts, "band", 0, 0, axis_index_groups=over_z)
    return jnp.sum(parts, axis=0)


def on_device(orbitals, kernels, pair_kdiff, stored_kernel_index):
    group = lax.axis_index("kgrp")
    band = lax.axis_index("band")
    y, x, z = band // (NX * NZ), band // NZ % NX, band % NZ
    odd = group % 2

    own = orbitals[0]
    diff_core = swap_groups(pair_kdiff, 1)
    diff_far = swap_groups(pair_kdiff, 2)
    far = swap_groups(own, 2)

    first = jnp.where(odd == 1, pair_kdiff[0], diff_core[0])
    second = jnp.where(odd == 1, diff_core[0], diff_far[0])
    slots = jnp.stack([stored_kernel_index[first], stored_kernel_index[second]])
    sign_own = jnp.where(odd == 1, -1.0, 1.0).astype(jnp.float32)
    sign = jnp.stack([sign_own, -sign_own])
    dests = jnp.stack([(y + dy) % NY * NX + (x + dx) % NX for dy, dx in OFFSETS])
    sends = pack(slots, dests, kernels)
    kerns = [sends[0]] + [
        shift(block, dy, dx, 0) for block, (dy, dx) in zip(sends[1:], OFFSETS[1:])
    ]

    both = jnp.stack([own, far])
    up, down = both, both
    cols = [both]
    for _ in range(3):
        up, down = shift(up, 0, 0, 1), shift(down, 0, 0, -1)
        cols += [down, up]
    last = jnp.stack([shift(up[0], 0, 0, 1), shift(down[1], 0, 0, -1)])
    cols.append(last)
    pair = jnp.stack([both, shift(both, 0, 1, 0)])
    up, down = shift(pair, 1, 0, 0), shift(pair, -1, 0, 0)
    over = jnp.stack([shift(up[:, 0], 1, 0, 0), shift(down[:, 1], -1, 0, 0)], axis=1)
    rows = [block[i] for block in (pair, up, over, down) for i in range(NX)]

    place = jnp.stack([(z + dz) % NZ for dz in Z_OFFSETS])
    m_out, own_rows, own_cols = mix(place, sign, rows, cols, kerns)
    m_own = swap_groups(m_out, 1)
    total = reduce_windows(project(m_own, own_rows, own_cols))
    flat = total.reshape(2, 8 * NB)
    flat = lax.dynamic_slice(flat, (0, band * 27 % 4 * 108), (2, 27 * 108))
    return flat[None]


def solution(mesh):
    return jax.shard_map(
        on_device,
        mesh=mesh,
        in_specs=(P("kgrp", None, "band", None), P(None, None, "band", None), P("kgrp"), P()),
        out_specs=P("kgrp", None, "band"),
        check_vma=False,
    )
```

time: 1290 us -> 214 us (0.17)
  waiting for transfers between devices: 1210 us -> 54.6 us
  Pallas kernels: 0 us -> 80.5 us
  starting transfers between devices: 0.17 us -> 39.9 us
  matrix products: 37.7 us -> 0 us
  blocking collectives: 0 us -> 22.6 us
  between operations: 16.4 us -> 2.8 us
    unnamed x4 -> x0, waiting for transfers between devices: 602 us -> none
    all_gather x2 -> x0, waiting for transfers between devices: 597 us -> none  [the longest x1 301 us: on_device(): lax.all_gather(partner_rows, 'band', axis=1, tiled=True)]
    pallas_call x0 -> x3, Pallas kernels: none -> 80.5 us  [the longest x1 65.4 us: pack(): pl.pallas_call(pack_body, out_shape=[piece] * GROUPS, in_specs=[pl.BlockS...]
    dot_general x24 -> x0, matrix products: 37.7 us -> none  [the longest x8 21.7 us: contract_last(): lax.dot_general(leading, trailing, (((1,), (1,)), ((), ())), preferred_el...]
    ppermute x2 -> x24, starting transfers between devices: 0.09 us -> 34.3 us  [the longest x20 31.4 us: shift(): return lax.ppermute(block, 'band', band_route(dy, dx, dz))]
    ppermute x2 -> x24, waiting for transfers between devices: 11.8 us -> 43.6 us  [the longest x20 34 us: shift(): return lax.ppermute(block, 'band', band_route(dy, dx, dz))]
    all_to_all x0 -> x1, blocking collectives: none -> 22.6 us  [reduce_windows(): parts = lax.all_to_all(parts, 'band', 0, 0, axis_index_groups=over_yx)]
  transfers between devices with their start and end apart: 5 -> 25, of which waited for: 5 -> 10; matrix products, arithmetic and copies ran while one was open for 2% -> 4% of each run, Pallas kernels for 0% -> 31%
where the time goes in v1:
time: 214 us; the launch traced here: 213 us
  Pallas kernels  80.5 us (38%)
  waiting for transfers between devices  54.6 us (26%)
  starting transfers between devices  39.9 us (19%)
  blocking collectives  22.6 us (11%)
  local copies, waits for them, and re-layouts  6.96 us (3%)
  other arithmetic  6.04 us (3%)
  between operations  2.8 us (1%)
    pallas_call x1, Pallas kernels, pack(): pl.pallas_call(pack_body, out_shape=[piece] * GROUPS, in_specs=[pl.BlockS...  65.4 us
    ppermute x20, waiting for transfers between devices, shift(): return lax.ppermute(block, 'band', band_route(dy, dx, dz))  34 us
    ppermute x20, starting transfers between devices, shift(): return lax.ppermute(block, 'band', band_route(dy, dx, dz))  31.4 us
    all_to_all x1, blocking collectives, reduce_windows(): parts = lax.all_to_all(parts, 'band', 0, 0, axis_index_groups=over_yx)  22.6 us
    all_to_all x1, waiting for transfers between devices, reduce_windows(): parts = lax.all_to_all(parts, 'band', 0, 0, axis_index_groups=over_z)  11 us
    pallas_call x1, Pallas kernels, mix(): pl.pallas_call(functools.partial(mix_body, len(rows), len(cols)), out_sha...  9.78 us
    ppermute x4, waiting for transfers between devices, swap_groups(): return lax.ppermute(block, 'kgrp', [(k, k ^ bit) for k in range(4)])  9.68 us
    all_to_all x1, starting transfers between devices, reduce_windows(): parts = lax.all_to_all(parts, 'band', 0, 0, axis_index_groups=over_z)  5.56 us
  transfers between devices with their start and end apart: 25, of which 10 were waited for; matrix products, arithmetic and copies ran while one was open for 4% of the time, Pallas kernels for 31%

profile of v1, /device:TPU:6, one launch (start us, length us, event | category | flops | bytes accessed | tf_op | source)
XLA Modules:
  0.0 213.3 jit_solution(7619932322505880732)
XLA Ops:
  0.0 1.4 collective-permute-start
  1.4 5.5 %collective-permute-done = bf16[2,64,432]{2,1,0:T(8,128)(2,1)S(1)} collective-permute-done((bf16[2,64,432]{2,1,0:T(8,128)(2,1)}, bf16[2,64,432]{2,1,0:T(8,128)(2,1)S(1)}, u32[]{:S(2)}, u32[]{:S(2)}) %collective-permute-start) | collective-permute-done | bytes 110624 | tf_op jit(solution)/shard_map/ppermute | solution.py:38
  7.0 0.9 fusion.3
  7.9 2.0 collective-permute-start.7
  9.9 4.0 %collective-permute-start.6 = (bf16[2,2,64,432]{3,2,1,0:T(8,128)(2,1)S(1)}, bf16[2,2,64,432]{3,2,1,0:T(8,128)(2,1)S(1)}, u32[]{:S(2)}, u32[]{:S(2)}) collective-permute-start(bf16[2,2,64,432]{3,2,1,0:T(8,128)(2,1)S(1)} %get-tuple-element.34.refs_0_.refs_8_), channel_id=1, source_target_pairs={{0,7},{1,0},{2,1},{3,2},{4,3},{5,4},{6,5},{7,6},{8,15},{9,8},{10,9... | collective-permute-start | bytes 663560 | tf_op jit(solution)/shard_map/ppermute | solution.py:34
  13.9 5.3 %collective-permute-done.7.refs_10_ = bf16[2,2,64,432]{3,2,1,0:T(8,128)(2,1)S(1)} collective-permute-done((bf16[2,2,64,432]{3,2,1,0:T(8,128)(2,1)S(1)}, bf16[2,2,64,432]{3,2,1,0:T(8,128)(2,1)S(1)}, u32[]{:S(2)}, u32[]{:S(2)}) %collective-permute-start.7) | collective-permute-done | bytes 221216 | tf_op jit(solution)/shard_map/ppermute | solution.py:34
  19.3 1.4 collective-permute-start.15
  23.3 1.3 collective-permute-done.15
  26.3 1.4 fusion.4
  27.7 3.3 %collective-permute-start.8 = (bf16[2,2,64,432]{3,2,1,0:T(8,128)(2,1)S(1)}, bf16[2,2,64,432]{3,2,1,0:T(8,128)(2,1)S(1)}, u32[]{:S(2)}, u32[]{:S(2)}) collective-permute-start(bf16[2,2,64,432]{3,2,1,0:T(8,128)(2,1)S(1)} %collective-permute-done.6.refs_9_), channel_id=1, source_target_pairs={{0,7},{1,0},{2,1},{3,2},{4,3},{5,4},{6,5},{7,6},{8,15},{9,8},{10,9... | collective-permute-start | bytes 663560 | tf_op jit(solution)/shard_map/ppermute | solution.py:34
  31.0 1.9 pad_add_fusion.slot_ref
  33.0 65.4 %pack.1 = (bf16[2,2,64,512]{3,2,1,0:T(8,128)(2,1)}, bf16[2,2,64,512]{3,2,1,0:T(8,128)(2,1)}, bf16[2,2,64,512]{3,2,1,0:T(8,128)(2,1)}, bf16[2,2,64,512]{3,2,1,0:T...) custom-call(s32[2]{0:T(128)} %pad_add_fusion.slot_ref, ...), custom_call_target="tpu_custom_call" | custom-call | tf_op jit(solution)/shard_map/pack/pallas_call | solution.py:66
  99.4 1.6 collective-permute-start.17
  101.1 1.7 collective-permute-start.4
  103.2 3.2 %collective-permute-start.10 = (bf16[2,2,64,432]{3,2,1,0:T(8,128)(2,1)S(1)}, bf16[2,2,64,432]{3,2,1,0:T(8,128)(2,1)S(1)}, u32[]{:S(2)}, u32[]{:S(2)}) collective-permute-start(bf16[2,2,64,432]{3,2,1,0:T(8,128)(2,1)S(1)} %collective-permute-done.8.refs_11_), channel_id=1, source_target_pairs={{0,7},{1,0},{2,1},{3,2},{4,3},{5,4},{6,5},{7,6},{8,15},{9,8},{10,9... | collective-permute-start | bytes 663560 | tf_op jit(solution)/shard_map/ppermute | solution.py:34
  106.4 4.2 %collective-permute-done.10.refs_13_ = bf16[2,2,64,432]{3,2,1,0:T(8,128)(2,1)S(1)} collective-permute-done((bf16[2,2,64,432]{3,2,1,0:T(8,128)(2,1)S(1)}, bf16[2,2,64,432]{3,2,1,0:T(8,128)(2,1)S(1)}, u32[]{:S(2)}, u32[]{:S(2)}) %collective-permute-start.10) | collective-permute-done | bytes 221216 | tf_op jit(solution)/shard_map/ppermute | solution.py:34
  111.3 8.6 %collective-permute-done.2 = bf16[2,2,2,64,432]{4,3,2,0,1:T(8,128)(2,1)S(1)} collective-permute-done((bf16[2,2,2,64,432]{4,3,2,0,1:T(8,128)(2,1)S(1)}, bf16[2,2,2,64,432]{4,3,2,0,1:T(8,128)(2,1)S(1)}, u32[]{:S(2)}, u32[]{:S(2)}) %collective-permute-start.2) | collective-permute-done | bytes 442400 | tf_op jit(solution)/shard_map/ppermute | solution.py:34
  119.9 3.0 %collective-permute-start.13 = (bf16[2,64,432]{2,1,0:T(8,128)(2,1)S(1)}, bf16[2,64,432]{2,1,0:T(8,128)(2,1)S(1)}, u32[]{:S(2)}, u32[]{:S(2)}) collective-permute-start(bf16[2,64,432]{2,1,0:T(8,128)(2,1)S(1)} %slice_bitcast_fusion.6), channel_id=1, source_target_pairs={{0,7},{1,0},{2,1},{3,2},{4,3},{5,4},{6,5},{7,6},{8,15},{9,8},{10,9... | collective-permute-start | bytes 331784 | tf_op jit(solution)/shard_map/ppermute | solution.py:34
  123.5 3.0 %collective-permute-start.5 = (bf16[2,2,64,432]{3,2,1,0:T(8,128)(2,1)S(1)}, bf16[2,2,64,432]{3,2,1,0:T(8,128)(2,1)S(1)}, u32[]{:S(2)}, u32[]{:S(2)}) collective-permute-start(bf16[2,2,64,432]{3,2,1,0:T(8,128)(2,1)S(1)} %slice_bitcast_fusion.2), channel_id=1, source_target_pairs={{0,48},{1,49},{2,50},{3,51},{4,52},{5,53},{6,54},{7,55},{8,56},{9,... | collective-permute-start | bytes 663560 | tf_op jit(solution)/shard_map/ppermute | solution.py:34
  127.5 1.8 collective-permute-start.19
  129.2 1.7 collective-permute-start.20
  131.0 12.7 %collective-permute-done.3 = bf16[2,2,64,432]{3,2,1,0:T(8,128)(2,1)S(1)} collective-permute-done((bf16[2,2,64,432]{3,2,1,0:T(8,128)(2,1)S(1)}, bf16[2,2,64,432]{3,2,1,0:T(8,128)(2,1)S(1)}, u32[]{:S(2)}, u32[]{:S(2)}) %collective-permute-start.3) | collective-permute-done | bytes 221216 | tf_op jit(solution)/shard_map/ppermute | solution.py:34
  143.6 1.4 collective-permute-start.21
  145.5 2.2 %collective-permute-start.22 = (bf16[2,2,64,512]{3,2,1,0:T(8,128)(2,1)S(1)}, bf16[2,2,64,512]{3,2,1,0:T(8,128)(2,1)S(1)}, u32[]{:S(2)}, u32[]{:S(2)}) collective-permute-start(bf16[2,2,64,512]{3,2,1,0:T(8,128)(2,1)S(1)} %copy-done.16), channel_id=1, source_target_pairs={{0,56},{1,57},{2,58},{3,59},{4,60},{5,61},{6,62},{7,63},{8,48},{9,... | collective-permute-start | bytes 786440 | tf_op jit(solution)/shard_map/ppermute | solution.py:34
  150.2 2.6 %collective-permute-done.22.refs_23_ = bf16[2,2,64,512]{3,2,1,0:T(8,128)(2,1)S(1)} collective-permute-done((bf16[2,2,64,512]{3,2,1,0:T(8,128)(2,1)S(1)}, bf16[2,2,64,512]{3,2,1,0:T(8,128)(2,1)S(1)}, u32[]{:S(2)}, u32[]{:S(2)}) %collective-permute-start.22) | collective-permute-done | bytes 262176 | tf_op jit(solution)/shard_map/ppermute | solution.py:34
  153.5 9.8 %mix.1 = (bf16[2,512,512]{2,1,0:T(8,128)(2,1)}, bf16[2,512,432]{2,1,0:T(8,128)(2,1)}, bf16[2,512,432]{2,1,0:T(8,128)(2,1)}) custom-call(s32[8]{0:T(128)} %stack.107.place_ref, f32[2]{0:T(128)} %pad_maximum_fusion.4.sign_ref, bf16[2,2,64,432]{3,2,1,0:T(8,128)(2,1)} %copy-done, bf16[2,2,64,432]{3,2,1,0:T(8,128)(2,1)} %copy-done.2, ...), custom_call_target="tpu_custom_call" | custom-call | tf_op jit(solution)/shard_map/mix/pallas_call | solution.py:121
  163.4 2.9 %collective-permute-done.23.m_ref = bf16[2,512,512]{2,1,0:T(8,128)(2,1)S(1)} collective-permute-done((bf16[2,512,512]{2,1,0:T(8,128)(2,1)}, bf16[2,512,512]{2,1,0:T(8,128)(2,1)S(1)}, u32[]{:S(2)}, u32[]{:S(2)}) %collective-permute-start.23) | collective-permute-done | bytes 1048608 | tf_op jit(solution)/shard_map/ppermute | solution.py:38
  166.3 1.0 copy-done.1
  167.3 5.2 %project.1 = bf16[64,16,432]{2,1,0:T(8,128)(2,1)} custom-call(bf16[2,512,512]{2,1,0:T(8,128)(2,1)} %copy-done.1, bf16[2,512,432]{2,1,0:T(8,128)(2,1)} %get-tuple-element.25.row_ref, bf16[2,512,432]{2,1,0:T(8,128)(2,1)} %get-tuple-element.26.col_ref), custom_call_target="tpu_custom_call" | custom-call | tf_op jit(solution)/shard_map/project/pallas_call | solution.py:151
  172.5 22.6 %all_to_all.10 = bf16[8,8,16,432]{3,2,1,0:T(8,128)(2,1)S(1)} all-to-all(bf16[8,8,16,432]{3,2,1,0:T(8,128)(2,1)} %bitcast.54), channel_id=1, replica_groups={{0,8,16,24,32,40,48,56},{1,9,17,25,33,41,49,57},{2,10,18,26,34,42,50,58..., dimensions={0} | all-to-all | bytes 1769472 | tf_op jit(solution)/shard_map/all_to_all | solution.py:166
  195.9 5.6 %all-to-all-start.1 = ((f32[8,16,432]{2,1,0:T(8,128)}), f32[8,16,432]{2,1,0:T(8,128)S(1)}, u32[]{:S(2)}, u32[]{:S(2)}) async-start(f32[8,16,432]{2,1,0:T(8,128)} %convert_reduce_fusion), calls=%async_computation.1 | async-start | bytes 524288 | tf_op jit(solution)/shard_map/all_to_all | solution.py:168
  201.5 11.0 %all-to-all-done.1 = f32[8,16,432]{2,1,0:T(8,128)S(1)} async-done(((f32[8,16,432]{2,1,0:T(8,128)}), f32[8,16,432]{2,1,0:T(8,128)S(1)}, u32[]{:S(2)}, u32[]{:S(2)}) %all-to-all-start.1) | async-done | bytes 221216 | tf_op jit(solution)/shard_map/all_to_all | solution.py:168
  (84 shorter events, 10.9 us)
Async XLA Ops:
  0.0 7.0 %collective-permute-start = (bf16[2,64,432]{2,1,0:T(8,128)(2,1)}, bf16[2,64,432]{2,1,0:T(8,128)(2,1)S(1)}, u32[]{:S(2)}, u32[]{:S(2)}) collective-permute-start(bf16[2,64,432]{2,1,0:T(8,128)(2,1)} %bitcast.58), channel_id=1, source_target_pairs={{0,128},{64,192},{128,0},{192,64},{1,129},{65,193},{129,1},{193,65... | collective-permute-start | bytes 331784 | tf_op jit(solution)/shard_map/ppermute | solution.py:38
  7.9 115.5 %copy-start = (bf16[2,2,64,432]{3,2,1,0:T(8,128)(2,1)}, bf16[2,2,64,432]{3,2,1,0:T(8,128)(2,1)S(1)}, u32[]{:S(2)}) copy-start(bf16[2,2,64,432]{3,2,1,0:T(8,128)(2,1)S(1)} %get-tuple-element.34.refs_0_.refs_8_) | copy-start | bytes 663556
  7.9 11.4 %collective-permute-start.7 = (bf16[2,2,64,432]{3,2,1,0:T(8,128)(2,1)S(1)}, bf16[2,2,64,432]{3,2,1,0:T(8,128)(2,1)S(1)}, u32[]{:S(2)}, u32[]{:S(2)}) collective-permute-start(bf16[2,2,64,432]{3,2,1,0:T(8,128)(2,1)S(1)} %get-tuple-element.34.refs_0_.refs_8_), channel_id=1, source_target_pairs={{0,1},{1,2},{2,3},{3,4},{4,5},{5,6},{6,7},{7,0},{8,9},{9,10},{10,1... | collective-permute-start | bytes 663560 | tf_op jit(solution)/shard_map/ppermute | solution.py:34
  9.9 17.8 %collective-permute-start.6 = (bf16[2,2,64,432]{3,2,1,0:T(8,128)(2,1)S(1)}, bf16[2,2,64,432]{3,2,1,0:T(8,128)(2,1)S(1)}, u32[]{:S(2)}, u32[]{:S(2)}) collective-permute-start(bf16[2,2,64,432]{3,2,1,0:T(8,128)(2,1)S(1)} %get-tuple-element.34.refs_0_.refs_8_), channel_id=1, source_target_pairs={{0,7},{1,0},{2,1},{3,2},{4,3},{5,4},{6,5},{7,6},{8,15},{9,8},{10,9... | collective-permute-start | bytes 663560 | tf_op jit(solution)/shard_map/ppermute | solution.py:34
  19.3 104.2 %copy-start.5 = (bf16[2,2,64,432]{3,2,1,0:T(8,128)(2,1)}, bf16[2,2,64,432]{3,2,1,0:T(8,128)(2,1)S(1)}, u32[]{:S(2)}) copy-start(bf16[2,2,64,432]{3,2,1,0:T(8,128)(2,1)S(1)} %collective-permute-done.7.refs_10_) | copy-start | bytes 663556
  19.3 11.7 %collective-permute-start.9 = (bf16[2,2,64,432]{3,2,1,0:T(8,128)(2,1)S(1)}, bf16[2,2,64,432]{3,2,1,0:T(8,128)(2,1)S(1)}, u32[]{:S(2)}, u32[]{:S(2)}) collective-permute-start(bf16[2,2,64,432]{3,2,1,0:T(8,128)(2,1)S(1)} %collective-permute-done.7.refs_10_), channel_id=1, source_target_pairs={{0,1},{1,2},{2,3},{3,4},{4,5},{5,6},{6,7},{7,0},{8,9},{9,10},{10,1... | collective-permute-start | bytes 663560 | tf_op jit(solution)/shard_map/ppermute | solution.py:34
  19.3 5.3 %collective-permute-start.15 = (s32[1]{0:T(128)}, s32[1]{0:T(128)}, u32[]{:S(2)}, u32[]{:S(2)}) collective-permute-start(s32[1]{0:T(128)} %param.6), channel_id=1, source_target_pairs={{0,128},{64,192},{128,0},{192,64},{1,129},{65,193},{129,1},{193,65... | collective-permute-start | bytes 20 | tf_op jit(solution)/shard_map/ppermute | solution.py:38
  20.7 3.9 %collective-permute-start.14 = (s32[1]{0:T(128)}, s32[1]{0:T(128)}, u32[]{:S(2)}, u32[]{:S(2)}) collective-permute-start(s32[1]{0:T(128)} %param.6), channel_id=1, source_target_pairs={{0,64},{64,0},{128,192},{192,128},{1,65},{65,1},{129,193},{193,129... | collective-permute-start | bytes 20 | tf_op jit(solution)/shard_map/ppermute | solution.py:38
  22.7 78.3 %collective-permute-start.1 = (bf16[2,2,64,432]{3,2,1,0:T(8,128)(2,1)S(1)}, bf16[2,2,64,432]{3,2,1,0:T(8,128)(2,1)S(1)}, u32[]{:S(2)}, u32[]{:S(2)}) collective-permute-start(bf16[2,2,64,432]{3,2,1,0:T(8,128)(2,1)S(1)} %get-tuple-element.34.refs_0_.refs_8_), channel_id=1, source_target_pairs={{0,8},{1,9},{2,10},{3,11},{4,12},{5,13},{6,14},{7,15},{8,0},{9,1},... | collective-permute-start | bytes 663560 | tf_op jit(solution)/shard_map/ppermute | solution.py:34
  27.7 99.6 %copy-start.6 = (bf16[2,2,64,432]{3,2,1,0:T(8,128)(2,1)}, bf16[2,2,64,432]{3,2,1,0:T(8,128)(2,1)S(1)}, u32[]{:S(2)}) copy-start(bf16[2,2,64,432]{3,2,1,0:T(8,128)(2,1)S(1)} %collective-permute-done.6.refs_9_) | copy-start | bytes 663556
  27.7 75.1 %collective-permute-start.8 = (bf16[2,2,64,432]{3,2,1,0:T(8,128)(2,1)S(1)}, bf16[2,2,64,432]{3,2,1,0:T(8,128)(2,1)S(1)}, u32[]{:S(2)}, u32[]{:S(2)}) collective-permute-start(bf16[2,2,64,432]{3,2,1,0:T(8,128)(2,1)S(1)} %collective-permute-done.6.refs_9_), channel_id=1, source_target_pairs={{0,7},{1,0},{2,1},{3,2},{4,3},{5,4},{6,5},{7,6},{8,15},{9,8},{10,9... | collective-permute-start | bytes 663560 | tf_op jit(solution)/shard_map/ppermute | solution.py:34
  31.0 96.3 %copy-start.7 = (bf16[2,2,64,432]{3,2,1,0:T(8,128)(2,1)}, bf16[2,2,64,432]{3,2,1,0:T(8,128)(2,1)S(1)}, u32[]{:S(2)}) copy-start(bf16[2,2,64,432]{3,2,1,0:T(8,128)(2,1)S(1)} %collective-permute-done.9.refs_12_) | copy-start | bytes 663556
  31.0 72.2 %collective-permute-start.11 = (bf16[2,2,64,432]{3,2,1,0:T(8,128)(2,1)S(1)}, bf16[2,2,64,432]{3,2,1,0:T(8,128)(2,1)S(1)}, u32[]{:S(2)}, u32[]{:S(2)}) collective-permute-start(bf16[2,2,64,432]{3,2,1,0:T(8,128)(2,1)S(1)} %collective-permute-done.9.refs_12_), channel_id=1, source_target_pairs={{0,1},{1,2},{2,3},{3,4},{4,5},{5,6},{6,7},{7,0},{8,9},{9,10},{10,1... | collective-permute-start | bytes 663560 | tf_op jit(solution)/shard_map/ppermute | solution.py:34
  98.5 25.0 %collective-permute-start.16 = (bf16[2,2,64,512]{3,2,1,0:T(8,128)(2,1)}, bf16[2,2,64,512]{3,2,1,0:T(8,128)(2,1)S(1)}, u32[]{:S(2)}, u32[]{:S(2)}) collective-permute-start(bf16[2,2,64,512]{3,2,1,0:T(8,128)(2,1)} %get-tuple-element.17), channel_id=1, source_target_pairs={{0,8},{1,9},{2,10},{3,11},{4,12},{5,13},{6,14},{7,15},{8,0},{9,1},... | collective-permute-start | bytes 786440 | tf_op jit(solution)/shard_map/ppermute | solution.py:34
  99.4 27.9 %collective-permute-start.17 = (bf16[2,2,64,512]{3,2,1,0:T(8,128)(2,1)}, bf16[2,2,64,512]{3,2,1,0:T(8,128)(2,1)S(1)}, u32[]{:S(2)}, u32[]{:S(2)}) collective-permute-start(bf16[2,2,64,512]{3,2,1,0:T(8,128)(2,1)} %get-tuple-element.18), channel_id=1, source_target_pairs={{0,16},{1,17},{2,18},{3,19},{4,20},{5,21},{6,22},{7,23},{8,24},{9,... | collective-permute-start | bytes 786440 | tf_op jit(solution)/shard_map/ppermute | solution.py:34
  101.0 51.9 %copy-start.2 = (bf16[2,2,64,432]{3,2,1,0:T(8,128)(2,1)}, bf16[2,2,64,432]{3,2,1,0:T(8,128)(2,1)S(1)}, u32[]{:S(2)}) copy-start(bf16[2,2,64,432]{3,2,1,0:T(8,128)(2,1)S(1)} %collective-permute-done.1.refs_1_) | copy-start | bytes 663556
  101.1 21.8 %collective-permute-start.4 = (bf16[2,2,2,64,432]{4,3,2,1,0:T(8,128)(2,1)S(1)}, bf16[2,2,2,64,432]{4,3,2,1,0:T(8,128)(2,1)S(1)}, u32[]{:S(2)}, u32[]{:S(2)}) collective-permute-start(bf16[2,2,2,64,432]{4,3,2,1,0:T(8,128)(2,1)S(1)} %pad_maximum_fusion), channel_id=1, source_target_pairs={{0,48},{1,49},{2,50},{3,51},{4,52},{5,53},{6,54},{7,55},{8,56},{9,... | collective-permute-start | bytes 1327112 | tf_op jit(solution)/shard_map/ppermute | solution.py:34
  102.8 50.0 %copy-start.8 = (bf16[2,2,64,432]{3,2,1,0:T(8,128)(2,1)}, bf16[2,2,64,432]{3,2,1,0:T(8,128)(2,1)S(1)}, u32[]{:S(2)}) copy-start(bf16[2,2,64,432]{3,2,1,0:T(8,128)(2,1)S(1)} %collective-permute-done.8.refs_11_) | copy-start | bytes 663556
  102.8 17.1 %collective-permute-start.2 = (bf16[2,2,2,64,432]{4,3,2,0,1:T(8,128)(2,1)S(1)}, bf16[2,2,2,64,432]{4,3,2,0,1:T(8,128)(2,1)S(1)}, u32[]{:S(2)}, u32[]{:S(2)}) collective-permute-start(bf16[2,2,2,64,432]{4,3,2,0,1:T(8,128)(2,1)S(1)} %copy.6), channel_id=1, source_target_pairs={{0,16},{1,17},{2,18},{3,19},{4,20},{5,21},{6,22},{7,23},{8,24},{9,... | collective-permute-start | bytes 1327112 | tf_op jit(solution)/shard_map/ppermute | solution.py:34
  103.2 49.6 %copy-start.3 = (bf16[2,2,64,432]{3,2,1,0:T(8,128)(2,1)}, bf16[2,2,64,432]{3,2,1,0:T(8,128)(2,1)S(1)}, u32[]{:S(2)}) copy-start(bf16[2,2,64,432]{3,2,1,0:T(8,128)(2,1)S(1)} %collective-permute-done.11.refs_14_) | copy-start | bytes 663556
  103.2 7.5 %collective-permute-start.10 = (bf16[2,2,64,432]{3,2,1,0:T(8,128)(2,1)S(1)}, bf16[2,2,64,432]{3,2,1,0:T(8,128)(2,1)S(1)}, u32[]{:S(2)}, u32[]{:S(2)}) collective-permute-start(bf16[2,2,64,432]{3,2,1,0:T(8,128)(2,1)S(1)} %collective-permute-done.8.refs_11_), channel_id=1, source_target_pairs={{0,7},{1,0},{2,1},{3,2},{4,3},{5,4},{6,5},{7,6},{8,15},{9,8},{10,9... | collective-permute-start | bytes 663560 | tf_op jit(solution)/shard_map/ppermute | solution.py:34
  110.7 16.8 %collective-permute-start.12 = (bf16[2,64,432]{2,1,0:T(8,128)(2,1)S(1)}, bf16[2,64,432]{2,1,0:T(8,128)(2,1)S(1)}, u32[]{:S(2)}, u32[]{:S(2)}) collective-permute-start(bf16[2,64,432]{2,1,0:T(8,128)(2,1)S(1)} %slice_bitcast_fusion.7), channel_id=1, source_target_pairs={{0,1},{1,2},{2,3},{3,4},{4,5},{5,6},{6,7},{7,0},{8,9},{9,10},{10,1... | collective-permute-start | bytes 331784 | tf_op jit(solution)/shard_map/ppermute | solution.py:34
  119.9 9.4 %collective-permute-start.13 = (bf16[2,64,432]{2,1,0:T(8,128)(2,1)S(1)}, bf16[2,64,432]{2,1,0:T(8,128)(2,1)S(1)}, u32[]{:S(2)}, u32[]{:S(2)}) collective-permute-start(bf16[2,64,432]{2,1,0:T(8,128)(2,1)S(1)} %slice_bitcast_fusion.6), channel_id=1, source_target_pairs={{0,7},{1,0},{2,1},{3,2},{4,3},{5,4},{6,5},{7,6},{8,15},{9,8},{10,9... | collective-permute-start | bytes 331784 | tf_op jit(solution)/shard_map/ppermute | solution.py:34
  122.9 20.8 %collective-permute-start.3 = (bf16[2,2,64,432]{3,2,1,0:T(8,128)(2,1)S(1)}, bf16[2,2,64,432]{3,2,1,0:T(8,128)(2,1)S(1)}, u32[]{:S(2)}, u32[]{:S(2)}) collective-permute-start(bf16[2,2,64,432]{3,2,1,0:T(8,128)(2,1)S(1)} %slice_bitcast_fusion.3), channel_id=1, source_target_pairs={{0,16},{1,17},{2,18},{3,19},{4,20},{5,21},{6,22},{7,23},{8,24},{9,... | collective-permute-start | bytes 663560 | tf_op jit(solution)/shard_map/ppermute | solution.py:34
  123.5 22.0 %collective-permute-start.5 = (bf16[2,2,64,432]{3,2,1,0:T(8,128)(2,1)S(1)}, bf16[2,2,64,432]{3,2,1,0:T(8,128)(2,1)S(1)}, u32[]{:S(2)}, u32[]{:S(2)}) collective-permute-start(bf16[2,2,64,432]{3,2,1,0:T(8,128)(2,1)S(1)} %slice_bitcast_fusion.2), channel_id=1, source_target_pairs={{0,48},{1,49},{2,50},{3,51},{4,52},{5,53},{6,54},{7,55},{8,56},{9,... | collective-permute-start | bytes 663560 | tf_op jit(solution)/shard_map/ppermute | solution.py:34
  127.4 22.8 %collective-permute-start.18 = (bf16[2,2,64,512]{3,2,1,0:T(8,128)(2,1)S(1)}, bf16[2,2,64,512]{3,2,1,0:T(8,128)(2,1)S(1)}, u32[]{:S(2)}, u32[]{:S(2)}) collective-permute-start(bf16[2,2,64,512]{3,2,1,0:T(8,128)(2,1)S(1)} %copy-done.20), channel_id=1, source_target_pairs={{0,24},{1,25},{2,26},{3,27},{4,28},{5,29},{6,30},{7,31},{8,16},{9,... | collective-permute-start | bytes 786440 | tf_op jit(solution)/shard_map/ppermute | solution.py:34
  127.5 22.7 %collective-permute-start.19 = (bf16[2,2,64,512]{3,2,1,0:T(8,128)(2,1)S(1)}, bf16[2,2,64,512]{3,2,1,0:T(8,128)(2,1)S(1)}, u32[]{:S(2)}, u32[]{:S(2)}) collective-permute-start(bf16[2,2,64,512]{3,2,1,0:T(8,128)(2,1)S(1)} %copy-done.19), channel_id=1, source_target_pairs={{0,32},{1,33},{2,34},{3,35},{4,36},{5,37},{6,38},{7,39},{8,40},{9,... | collective-permute-start | bytes 786440 | tf_op jit(solution)/shard_map/ppermute | solution.py:34
  129.2 20.9 %collective-permute-start.20 = (bf16[2,2,64,512]{3,2,1,0:T(8,128)(2,1)S(1)}, bf16[2,2,64,512]{3,2,1,0:T(8,128)(2,1)S(1)}, u32[]{:S(2)}, u32[]{:S(2)}) collective-permute-start(bf16[2,2,64,512]{3,2,1,0:T(8,128)(2,1)S(1)} %copy-done.18), channel_id=1, source_target_pairs={{0,40},{1,41},{2,42},{3,43},{4,44},{5,45},{6,46},{7,47},{8,32},{9,... | collective-permute-start | bytes 786440 | tf_op jit(solution)/shard_map/ppermute | solution.py:34
  143.6 6.5 %collective-permute-start.21 = (bf16[2,2,64,512]{3,2,1,0:T(8,128)(2,1)S(1)}, bf16[2,2,64,512]{3,2,1,0:T(8,128)(2,1)S(1)}, u32[]{:S(2)}, u32[]{:S(2)}) collective-permute-start(bf16[2,2,64,512]{3,2,1,0:T(8,128)(2,1)S(1)} %copy-done.17), channel_id=1, source_target_pairs={{0,48},{1,49},{2,50},{3,51},{4,52},{5,53},{6,54},{7,55},{8,56},{9,... | collective-permute-start | bytes 786440 | tf_op jit(solution)/shard_map/ppermute | solution.py:34
  145.5 7.3 %collective-permute-start.22 = (bf16[2,2,64,512]{3,2,1,0:T(8,128)(2,1)S(1)}, bf16[2,2,64,512]{3,2,1,0:T(8,128)(2,1)S(1)}, u32[]{:S(2)}, u32[]{:S(2)}) collective-permute-start(bf16[2,2,64,512]{3,2,1,0:T(8,128)(2,1)S(1)} %copy-done.16), channel_id=1, source_target_pairs={{0,56},{1,57},{2,58},{3,59},{4,60},{5,61},{6,62},{7,63},{8,48},{9,... | collective-permute-start | bytes 786440 | tf_op jit(solution)/shard_map/ppermute | solution.py:34
  163.3 3.0 %collective-permute-start.23 = (bf16[2,512,512]{2,1,0:T(8,128)(2,1)}, bf16[2,512,512]{2,1,0:T(8,128)(2,1)S(1)}, u32[]{:S(2)}, u32[]{:S(2)}) collective-permute-start(bf16[2,512,512]{2,1,0:T(8,128)(2,1)} %get-tuple-element.24), channel_id=1, source_target_pairs={{0,64},{64,0},{128,192},{192,128},{1,65},{65,1},{129,193},{193,129... | collective-permute-start | bytes 3145736 | tf_op jit(solution)/shard_map/ppermute | solution.py:38
  195.9 16.6 %all-to-all-start.1 = ((f32[8,16,432]{2,1,0:T(8,128)}), f32[8,16,432]{2,1,0:T(8,128)S(1)}, u32[]{:S(2)}, u32[]{:S(2)}) async-start(f32[8,16,432]{2,1,0:T(8,128)} %convert_reduce_fusion), calls=%async_computation.1 | async-start | bytes 524288 | tf_op jit(solution)/shard_map/all_to_all | solution.py:168
  (14 other events, 290.7 us)

commit v2 on v1

--- a/solution.py
+++ b/solution.py
@@ -43,22 +43,18 @@
 
 
 def pack_body(slot_ref, dest_ref, kernels_ref, *refs):
-    outs, sem = refs[:GROUPS], refs[GROUPS]
-    copies = []
-    for which in range(2):
+    outs, held, sem = refs[:GROUPS], refs[GROUPS], refs[GROUPS + 1]
+    copies = [
+        pltpu.make_async_copy(kernels_ref.at[slot_ref[which]], held.at[which], sem.at[which])
+        for which in range(2)
+    ]
+    for copy in copies:
+        copy.start()
+    for which, copy in enumerate(copies):
+        copy.wait()
         for i in range(GROUPS):
             start = pl.multiple_of(dest_ref[i] * BLOCK, BLOCK)
-            copies.append(
-                pltpu.make_async_copy(
-                    kernels_ref.at[slot_ref[which], :, :, pl.ds(start, BLOCK)],
-                    outs[i].at[which],
-                    sem.at[which, i],
-                )
-            )
-    for copy in copies:
-        copy.start()
-    for copy in copies:
-        copy.wait()
+            outs[i][which] = held[which, :, :, pl.ds(start, BLOCK)]
 
 
 def pack(slots, dests, kernels):
@@ -71,8 +67,12 @@
             pl.BlockSpec(memory_space=pltpu.SMEM),
             pl.BlockSpec(memory_space=pl.ANY),
         ],
-        out_specs=[pl.BlockSpec(memory_space=pl.ANY)] * GROUPS,
-        scratch_shapes=[pltpu.SemaphoreType.DMA((2, GROUPS))],
+        out_specs=[pl.BlockSpec(memory_space=pltpu.VMEM)] * GROUPS,
+        scratch_shapes=[
+            pltpu.VMEM((2, 2, SLAB, GROUPS * BLOCK), jnp.bfloat16),
+            pltpu.SemaphoreType.DMA((2,)),
+        ],
+        compiler_params=pltpu.CompilerParams(vmem_limit_bytes=VMEM),
         name="pack",
     )(slots, dests, kernels)
 
@@ -91,27 +91,23 @@
         col_ref[:, at, :] = cols[i][0]
         other_cols[:, at, :] = cols[i][1]
     last = ((1,), (1,))
-    per = 2 * SLAB
-    for part in range(GROUPS // 2):
+    per = BLOCK // 2
+    for part in range(2):
         at = pl.ds(part * per, per)
         total_re = total_im = None
         for which, (a_ref, b_ref) in enumerate(((row_ref, col_ref), (other_rows, other_cols))):
-            a_re, a_im = a_ref[0, at, :], a_ref[1, at, :]
-            p_re = dot(a_re, b_ref[0], last) + dot(a_im, b_ref[1], last)
-            p_im = dot(a_im, b_ref[0], last) - dot(a_re, b_ref[1], last)
-            sign = sign_ref[which]
-            k_re = jnp.concatenate(
-                [kerns[2 * part][which, 0], kerns[2 * part + 1][which, 0]], axis=0
-            ).astype(jnp.float32)
-            k_im = jnp.concatenate(
-                [kerns[2 * part][which, 1], kerns[2 * part + 1][which, 1]], axis=0
-            ).astype(jnp.float32) * sign
+            a_re, a_im, b_re, b_im = a_ref[0], a_ref[1], b_ref[0, at, :], b_ref[1, at, :]
+            p_re = dot(a_re, b_re, last) + dot(a_im, b_im, last)
+            p_im = dot(a_im, b_re, last) - dot(a_re, b_im, last)
+            k_re = jnp.concatenate([k[which, 0, :, at] for k in kerns], axis=0).astype(jnp.float32)
+            k_im = jnp.concatenate([k[which, 1, :, at] for k in kerns], axis=0).astype(jnp.float32)
+            k_im = k_im * sign_ref[which]
             m_re = k_re * p_re - k_im * p_im
             m_im = k_re * p_im + k_im * p_re
             total_re = m_re if total_re is None else total_re + m_re
             total_im = m_im if total_im is None else total_im + m_im
-        m_ref[0, at, :] = total_re.astype(jnp.bfloat16)
-        m_ref[1, at, :] = total_im.astype(jnp.bfloat16)
+        m_ref[0, :, at] = total_re.astype(jnp.bfloat16)
+        m_ref[1, :, at] = total_im.astype(jnp.bfloat16)
 
 
 def mix(place, sign, rows, cols, kerns):
@@ -129,17 +125,26 @@
     )(place, sign, *rows, *cols, *kerns)
 
 
+def halves(value):
+    high = value.astype(jnp.bfloat16)
+    return high, (value - high.astype(jnp.float32)).astype(jnp.bfloat16)
+
+
 def project_body(m_ref, row_ref, col_ref, out_ref, x_ref):
     mid = ((1,), (0,))
     first = ((0,), (0,))
     m_re, m_im = m_ref[0], m_ref[1]
     c_re, c_im = col_ref[0], col_ref[1]
-    y_re = (dot(m_re, c_re, mid) - dot(m_im, c_im, mid)).astype(jnp.bfloat16)
-    y_im = (dot(m_re, c_im, mid) + dot(m_im, c_re, mid)).astype(jnp.bfloat16)
+    y_re = halves(dot(m_re, c_re, mid) - dot(m_im, c_im, mid))
+    y_im = halves(dot(m_re, c_im, mid) + dot(m_im, c_re, mid))
     r_re, r_im = row_ref[0], row_ref[1]
+
+    def meet(a, pair):
+        return dot(a, pair[0], first) + dot(a, pair[1], first)
+
     x_ref[:, pl.ds(NB, 8), :] = jnp.zeros((2, 8, NB), jnp.float32)
-    x_ref[0, pl.ds(0, NB), :] = -(dot(r_re, y_re, first) + dot(r_im, y_im, first))
-    x_ref[1, pl.ds(0, NB), :] = dot(r_im, y_re, first) - dot(r_re, y_im, first)
+    x_ref[0, pl.ds(0, NB), :] = -(meet(r_re, y_re) + meet(r_im, y_im))
+    x_ref[1, pl.ds(0, NB), :] = meet(r_im, y_re) - meet(r_re, y_im)
     for d in range(GROUPS * NZ):
         at = pl.ds(27 * d // 4, 8)
         window = jnp.concatenate([x_ref[0, at, :], x_ref[1, at, :]], axis=0)

time: 214 us -> 150 us (0.70)
  Pallas kernels: 80.5 us -> 16.2 us
    pallas_call x1, Pallas kernels: 65.4 us -> 3.65 us  [pack(): pl.pallas_call(pack_body, out_shape=[piece] * GROUPS, in_specs=[pl.BlockS...]
    pallas_call x1, Pallas kernels: 9.78 us -> 6.47 us  [mix(): pl.pallas_call(functools.partial(mix_body, len(rows), len(cols)), out_sha...]
  transfers between devices with their start and end apart: 25 -> 25, of which waited for: 10 -> 10; matrix products, arithmetic and copies ran while one was open for 4% -> 6% of each run, Pallas kernels for 31% -> 2%
where the time goes in v2:
time: 150 us; the launch traced here: 149 us
  waiting for transfers between devices  54.6 us (36%)
  starting transfers between devices  39.9 us (27%)
  blocking collectives  22.5 us (15%)
  Pallas kernels  16.2 us (11%)
  local copies, waits for them, and re-layouts  6.96 us (5%)
  other arithmetic  6.04 us (4%)
  between operations  2.8 us (2%)
    ppermute x20, waiting for transfers between devices, shift(): return lax.ppermute(block, 'band', band_route(dy, dx, dz))  34 us
    ppermute x20, starting transfers between devices, shift(): return lax.ppermute(block, 'band', band_route(dy, dx, dz))  31.4 us
    all_to_all x1, blocking collectives, reduce_windows(): parts = lax.all_to_all(parts, 'band', 0, 0, axis_index_groups=over_yx)  22.5 us
    all_to_all x1, waiting for transfers between devices, reduce_windows(): parts = lax.all_to_all(parts, 'band', 0, 0, axis_index_groups=over_z)  11 us
    ppermute x4, waiting for transfers between devices, swap_groups(): return lax.ppermute(block, 'kgrp', [(k, k ^ bit) for k in range(4)])  9.68 us
    pallas_call x1, Pallas kernels, mix(): pl.pallas_call(functools.partial(mix_body, len(rows), len(cols)), out_sha...  6.47 us
    pallas_call x1, Pallas kernels, project(): pl.pallas_call(project_body, out_shape=jax.ShapeDtypeStruct((GROUPS * NZ,...  6.06 us
    all_to_all x1, starting transfers between devices, reduce_windows(): parts = lax.all_to_all(parts, 'band', 0, 0, axis_index_groups=over_z)  5.57 us
  transfers between devices with their start and end apart: 25, of which 10 were waited for; matrix products, arithmetic and copies ran while one was open for 6% of the time, Pallas kernels for 2%

profile of v2, /device:TPU:6, one launch (start us, length us, event | category | flops | bytes accessed | tf_op | source)
XLA Modules:
  0.0 149.0 jit_solution(6451632959433523870)
XLA Ops:
  0.0 1.4 collective-permute-start
  1.4 5.5 %collective-permute-done = bf16[2,64,432]{2,1,0:T(8,128)(2,1)S(1)} collective-permute-done((bf16[2,64,432]{2,1,0:T(8,128)(2,1)}, bf16[2,64,432]{2,1,0:T(8,128)(2,1)S(1)}, u32[]{:S(2)}, u32[]{:S(2)}) %collective-permute-start) | collective-permute-done | bytes 110624 | tf_op jit(solution)/shard_map/ppermute | solution.py:38
  7.0 0.9 fusion.3
  7.9 2.0 %collective-permute-start.7 = (bf16[2,2,64,432]{3,2,1,0:T(8,128)(2,1)S(1)}, bf16[2,2,64,432]{3,2,1,0:T(8,128)(2,1)S(1)}, u32[]{:S(2)}, u32[]{:S(2)}) collective-permute-start(bf16[2,2,64,432]{3,2,1,0:T(8,128)(2,1)S(1)} %get-tuple-element.34.refs_0_.refs_8_), channel_id=1, source_target_pairs={{0,1},{1,2},{2,3},{3,4},{4,5},{5,6},{6,7},{7,0},{8,9},{9,10},{10,1... | collective-permute-start | bytes 663560 | tf_op jit(solution)/shard_map/ppermute | solution.py:34
  9.9 4.0 %collective-permute-start.6 = (bf16[2,2,64,432]{3,2,1,0:T(8,128)(2,1)S(1)}, bf16[2,2,64,432]{3,2,1,0:T(8,128)(2,1)S(1)}, u32[]{:S(2)}, u32[]{:S(2)}) collective-permute-start(bf16[2,2,64,432]{3,2,1,0:T(8,128)(2,1)S(1)} %get-tuple-element.34.refs_0_.refs_8_), channel_id=1, source_target_pairs={{0,7},{1,0},{2,1},{3,2},{4,3},{5,4},{6,5},{7,6},{8,15},{9,8},{10,9... | collective-permute-start | bytes 663560 | tf_op jit(solution)/shard_map/ppermute | solution.py:34
  13.9 5.3 %collective-permute-done.7.refs_10_ = bf16[2,2,64,432]{3,2,1,0:T(8,128)(2,1)S(1)} collective-permute-done((bf16[2,2,64,432]{3,2,1,0:T(8,128)(2,1)S(1)}, bf16[2,2,64,432]{3,2,1,0:T(8,128)(2,1)S(1)}, u32[]{:S(2)}, u32[]{:S(2)}) %collective-permute-start.7) | collective-permute-done | bytes 221216 | tf_op jit(solution)/shard_map/ppermute | solution.py:34
  19.3 1.4 collective-permute-start.15
  23.3 1.3 collective-permute-done.15
  26.3 1.4 fusion.4
  27.7 3.3 %collective-permute-start.8 = (bf16[2,2,64,432]{3,2,1,0:T(8,128)(2,1)S(1)}, bf16[2,2,64,432]{3,2,1,0:T(8,128)(2,1)S(1)}, u32[]{:S(2)}, u32[]{:S(2)}) collective-permute-start(bf16[2,2,64,432]{3,2,1,0:T(8,128)(2,1)S(1)} %collective-permute-done.6.refs_9_), channel_id=1, source_target_pairs={{0,7},{1,0},{2,1},{3,2},{4,3},{5,4},{6,5},{7,6},{8,15},{9,8},{10,9... | collective-permute-start | bytes 663560 | tf_op jit(solution)/shard_map/ppermute | solution.py:34
  31.0 1.9 %pad_add_fusion.slot_ref = s32[2]{0:T(128)} fusion(s32[1]{0:T(128)} %get-tuple-element.36, s32[1]{0:T(128)} %get-tuple-element.35), kind=kLoop, calls=%fused_computation.20 | loop fusion | flops 2 | bytes 16 | tf_op jit(solution)/shard_map/stack | solution.py:190
  33.0 3.7 %pack.1 = (bf16[2,2,64,512]{3,2,1,0:T(8,128)(2,1)}, bf16[2,2,64,512]{3,2,1,0:T(8,128)(2,1)}, bf16[2,2,64,512]{3,2,1,0:T(8,128)(2,1)}, bf16[2,2,64,512]{3,2,1,0:T...) custom-call(s32[2]{0:T(128)} %pad_add_fusion.slot_ref, ...), custom_call_target="tpu_custom_call" | custom-call | tf_op jit(solution)/shard_map/pack/pallas_call | solution.py:62
  37.6 1.6 %collective-permute-start.17 = (bf16[2,2,64,512]{3,2,1,0:T(8,128)(2,1)}, bf16[2,2,64,512]{3,2,1,0:T(8,128)(2,1)S(1)}, u32[]{:S(2)}, u32[]{:S(2)}) collective-permute-start(bf16[2,2,64,512]{3,2,1,0:T(8,128)(2,1)} %get-tuple-element.18), channel_id=1, source_target_pairs={{0,16},{1,17},{2,18},{3,19},{4,20},{5,21},{6,22},{7,23},{8,24},{9,... | collective-permute-start | bytes 786440 | tf_op jit(solution)/shard_map/ppermute | solution.py:34
  39.3 1.7 %collective-permute-start.4 = (bf16[2,2,2,64,432]{4,3,2,1,0:T(8,128)(2,1)S(1)}, bf16[2,2,2,64,432]{4,3,2,1,0:T(8,128)(2,1)S(1)}, u32[]{:S(2)}, u32[]{:S(2)}) collective-permute-start(bf16[2,2,2,64,432]{4,3,2,1,0:T(8,128)(2,1)S(1)} %pad_maximum_fusion), channel_id=1, source_target_pairs={{0,48},{1,49},{2,50},{3,51},{4,52},{5,53},{6,54},{7,55},{8,56},{9,... | collective-permute-start | bytes 1327112 | tf_op jit(solution)/shard_map/ppermute | solution.py:34
  41.4 3.2 %collective-permute-start.10 = (bf16[2,2,64,432]{3,2,1,0:T(8,128)(2,1)S(1)}, bf16[2,2,64,432]{3,2,1,0:T(8,128)(2,1)S(1)}, u32[]{:S(2)}, u32[]{:S(2)}) collective-permute-start(bf16[2,2,64,432]{3,2,1,0:T(8,128)(2,1)S(1)} %collective-permute-done.8.refs_11_), channel_id=1, source_target_pairs={{0,7},{1,0},{2,1},{3,2},{4,3},{5,4},{6,5},{7,6},{8,15},{9,8},{10,9... | collective-permute-start | bytes 663560 | tf_op jit(solution)/shard_map/ppermute | solution.py:34
  44.6 4.2 %collective-permute-done.10.refs_13_ = bf16[2,2,64,432]{3,2,1,0:T(8,128)(2,1)S(1)} collective-permute-done((bf16[2,2,64,432]{3,2,1,0:T(8,128)(2,1)S(1)}, bf16[2,2,64,432]{3,2,1,0:T(8,128)(2,1)S(1)}, u32[]{:S(2)}, u32[]{:S(2)}) %collective-permute-start.10) | collective-permute-done | bytes 221216 | tf_op jit(solution)/shard_map/ppermute | solution.py:34
  49.5 8.6 %collective-permute-done.2 = bf16[2,2,2,64,432]{4,3,2,0,1:T(8,128)(2,1)S(1)} collective-permute-done((bf16[2,2,2,64,432]{4,3,2,0,1:T(8,128)(2,1)S(1)}, bf16[2,2,2,64,432]{4,3,2,0,1:T(8,128)(2,1)S(1)}, u32[]{:S(2)}, u32[]{:S(2)}) %collective-permute-start.2) | collective-permute-done | bytes 442400 | tf_op jit(solution)/shard_map/ppermute | solution.py:34
  58.1 3.0 %collective-permute-start.13 = (bf16[2,64,432]{2,1,0:T(8,128)(2,1)S(1)}, bf16[2,64,432]{2,1,0:T(8,128)(2,1)S(1)}, u32[]{:S(2)}, u32[]{:S(2)}) collective-permute-start(bf16[2,64,432]{2,1,0:T(8,128)(2,1)S(1)} %slice_bitcast_fusion.6), channel_id=1, source_target_pairs={{0,7},{1,0},{2,1},{3,2},{4,3},{5,4},{6,5},{7,6},{8,15},{9,8},{10,9... | collective-permute-start | bytes 331784 | tf_op jit(solution)/shard_map/ppermute | solution.py:34
  61.7 3.0 %collective-permute-start.5 = (bf16[2,2,64,432]{3,2,1,0:T(8,128)(2,1)S(1)}, bf16[2,2,64,432]{3,2,1,0:T(8,128)(2,1)S(1)}, u32[]{:S(2)}, u32[]{:S(2)}) collective-permute-start(bf16[2,2,64,432]{3,2,1,0:T(8,128)(2,1)S(1)} %slice_bitcast_fusion.2), channel_id=1, source_target_pairs={{0,48},{1,49},{2,50},{3,51},{4,52},{5,53},{6,54},{7,55},{8,56},{9,... | collective-permute-start | bytes 663560 | tf_op jit(solution)/shard_map/ppermute | solution.py:34
  65.7 1.8 %collective-permute-start.19 = (bf16[2,2,64,512]{3,2,1,0:T(8,128)(2,1)S(1)}, bf16[2,2,64,512]{3,2,1,0:T(8,128)(2,1)S(1)}, u32[]{:S(2)}, u32[]{:S(2)}) collective-permute-start(bf16[2,2,64,512]{3,2,1,0:T(8,128)(2,1)S(1)} %copy-done.19), channel_id=1, source_target_pairs={{0,32},{1,33},{2,34},{3,35},{4,36},{5,37},{6,38},{7,39},{8,40},{9,... | collective-permute-start | bytes 786440 | tf_op jit(solution)/shard_map/ppermute | solution.py:34
  67.5 1.7 %collective-permute-start.20 = (bf16[2,2,64,512]{3,2,1,0:T(8,128)(2,1)S(1)}, bf16[2,2,64,512]{3,2,1,0:T(8,128)(2,1)S(1)}, u32[]{:S(2)}, u32[]{:S(2)}) collective-permute-start(bf16[2,2,64,512]{3,2,1,0:T(8,128)(2,1)S(1)} %copy-done.18), channel_id=1, source_target_pairs={{0,40},{1,41},{2,42},{3,43},{4,44},{5,45},{6,46},{7,47},{8,32},{9,... | collective-permute-start | bytes 786440 | tf_op jit(solution)/shard_map/ppermute | solution.py:34
  69.2 12.7 %collective-permute-done.3 = bf16[2,2,64,432]{3,2,1,0:T(8,128)(2,1)S(1)} collective-permute-done((bf16[2,2,64,432]{3,2,1,0:T(8,128)(2,1)S(1)}, bf16[2,2,64,432]{3,2,1,0:T(8,128)(2,1)S(1)}, u32[]{:S(2)}, u32[]{:S(2)}) %collective-permute-start.3) | collective-permute-done | bytes 221216 | tf_op jit(solution)/shard_map/ppermute | solution.py:34
  81.8 1.4 collective-permute-start.21
  83.7 2.2 %collective-permute-start.22 = (bf16[2,2,64,512]{3,2,1,0:T(8,128)(2,1)S(1)}, bf16[2,2,64,512]{3,2,1,0:T(8,128)(2,1)S(1)}, u32[]{:S(2)}, u32[]{:S(2)}) collective-permute-start(bf16[2,2,64,512]{3,2,1,0:T(8,128)(2,1)S(1)} %copy-done.16), channel_id=1, source_target_pairs={{0,56},{1,57},{2,58},{3,59},{4,60},{5,61},{6,62},{7,63},{8,48},{9,... | collective-permute-start | bytes 786440 | tf_op jit(solution)/shard_map/ppermute | solution.py:34
  88.4 2.6 %collective-permute-done.22.refs_23_ = bf16[2,2,64,512]{3,2,1,0:T(8,128)(2,1)S(1)} collective-permute-done((bf16[2,2,64,512]{3,2,1,0:T(8,128)(2,1)S(1)}, bf16[2,2,64,512]{3,2,1,0:T(8,128)(2,1)S(1)}, u32[]{:S(2)}, u32[]{:S(2)}) %collective-permute-start.22) | collective-permute-done | bytes 262176 | tf_op jit(solution)/shard_map/ppermute | solution.py:34
  91.7 6.5 %mix.1 = (bf16[2,512,512]{2,1,0:T(8,128)(2,1)}, bf16[2,512,432]{2,1,0:T(8,128)(2,1)}, bf16[2,512,432]{2,1,0:T(8,128)(2,1)}) custom-call(s32[8]{0:T(128)} %stack.107.place_ref, f32[2]{0:T(128)} %pad_maximum_fusion.4.sign_ref, bf16[2,2,64,432]{3,2,1,0:T(8,128)(2,1)} %copy-done, bf16[2,2,64,432]{3,2,1,0:T(8,128)(2,1)} %copy-done.2, ...), custom_call_target="tpu_custom_call" | custom-call | tf_op jit(solution)/shard_map/mix/pallas_call | solution.py:117
  98.3 2.9 %collective-permute-done.23.m_ref = bf16[2,512,512]{2,1,0:T(8,128)(2,1)S(1)} collective-permute-done((bf16[2,512,512]{2,1,0:T(8,128)(2,1)}, bf16[2,512,512]{2,1,0:T(8,128)(2,1)S(1)}, u32[]{:S(2)}, u32[]{:S(2)}) %collective-permute-start.23) | collective-permute-done | bytes 1048608 | tf_op jit(solution)/shard_map/ppermute | solution.py:38
  101.2 1.0 copy-done.1
  102.1 6.1 %project.1 = bf16[64,16,432]{2,1,0:T(8,128)(2,1)} custom-call(bf16[2,512,512]{2,1,0:T(8,128)(2,1)} %copy-done.1, bf16[2,512,432]{2,1,0:T(8,128)(2,1)} %get-tuple-element.25.row_ref, bf16[2,512,432]{2,1,0:T(8,128)(2,1)} %get-tuple-element.26.col_ref), custom_call_target="tpu_custom_call" | custom-call | tf_op jit(solution)/shard_map/project/pallas_call | solution.py:156
  108.2 22.5 %all_to_all.10 = bf16[8,8,16,432]{3,2,1,0:T(8,128)(2,1)S(1)} all-to-all(bf16[8,8,16,432]{3,2,1,0:T(8,128)(2,1)} %bitcast.54), channel_id=1, replica_groups={{0,8,16,24,32,40,48,56},{1,9,17,25,33,41,49,57},{2,10,18,26,34,42,50,58..., dimensions={0} | all-to-all | bytes 1769472 | tf_op jit(solution)/shard_map/all_to_all | solution.py:171
  131.6 5.6 %all-to-all-start.1 = ((f32[8,16,432]{2,1,0:T(8,128)}), f32[8,16,432]{2,1,0:T(8,128)S(1)}, u32[]{:S(2)}, u32[]{:S(2)}) async-start(f32[8,16,432]{2,1,0:T(8,128)} %convert_reduce_fusion), calls=%async_computation.1 | async-start | bytes 524288 | tf_op jit(solution)/shard_map/all_to_all | solution.py:173
  137.2 11.0 %all-to-all-done.1 = f32[8,16,432]{2,1,0:T(8,128)S(1)} async-done(((f32[8,16,432]{2,1,0:T(8,128)}), f32[8,16,432]{2,1,0:T(8,128)S(1)}, u32[]{:S(2)}, u32[]{:S(2)}) %all-to-all-start.1) | async-done | bytes 221216 | tf_op jit(solution)/shard_map/all_to_all | solution.py:173
  (84 shorter events, 10.9 us)
Async XLA Ops:
  0.0 7.0 %collective-permute-start = (bf16[2,64,432]{2,1,0:T(8,128)(2,1)}, bf16[2,64,432]{2,1,0:T(8,128)(2,1)S(1)}, u32[]{:S(2)}, u32[]{:S(2)}) collective-permute-start(bf16[2,64,432]{2,1,0:T(8,128)(2,1)} %bitcast.58), channel_id=1, source_target_pairs={{0,128},{64,192},{128,0},{192,64},{1,129},{65,193},{129,1},{193,65... | collective-permute-start | bytes 331784 | tf_op jit(solution)/shard_map/ppermute | solution.py:38
  7.9 53.7 %copy-start = (bf16[2,2,64,432]{3,2,1,0:T(8,128)(2,1)}, bf16[2,2,64,432]{3,2,1,0:T(8,128)(2,1)S(1)}, u32[]{:S(2)}) copy-start(bf16[2,2,64,432]{3,2,1,0:T(8,128)(2,1)S(1)} %get-tuple-element.34.refs_0_.refs_8_) | copy-start | bytes 663556
  7.9 11.4 %collective-permute-start.7 = (bf16[2,2,64,432]{3,2,1,0:T(8,128)(2,1)S(1)}, bf16[2,2,64,432]{3,2,1,0:T(8,128)(2,1)S(1)}, u32[]{:S(2)}, u32[]{:S(2)}) collective-permute-start(bf16[2,2,64,432]{3,2,1,0:T(8,128)(2,1)S(1)} %get-tuple-element.34.refs_0_.refs_8_), channel_id=1, source_target_pairs={{0,1},{1,2},{2,3},{3,4},{4,5},{5,6},{6,7},{7,0},{8,9},{9,10},{10,1... | collective-permute-start | bytes 663560 | tf_op jit(solution)/shard_map/ppermute | solution.py:34
  9.9 17.8 %collective-permute-start.6 = (bf16[2,2,64,432]{3,2,1,0:T(8,128)(2,1)S(1)}, bf16[2,2,64,432]{3,2,1,0:T(8,128)(2,1)S(1)}, u32[]{:S(2)}, u32[]{:S(2)}) collective-permute-start(bf16[2,2,64,432]{3,2,1,0:T(8,128)(2,1)S(1)} %get-tuple-element.34.refs_0_.refs_8_), channel_id=1, source_target_pairs={{0,7},{1,0},{2,1},{3,2},{4,3},{5,4},{6,5},{7,6},{8,15},{9,8},{10,9... | collective-permute-start | bytes 663560 | tf_op jit(solution)/shard_map/ppermute | solution.py:34
  19.3 42.4 %copy-start.5 = (bf16[2,2,64,432]{3,2,1,0:T(8,128)(2,1)}, bf16[2,2,64,432]{3,2,1,0:T(8,128)(2,1)S(1)}, u32[]{:S(2)}) copy-start(bf16[2,2,64,432]{3,2,1,0:T(8,128)(2,1)S(1)} %collective-permute-done.7.refs_10_) | copy-start | bytes 663556
  19.3 11.7 %collective-permute-start.9 = (bf16[2,2,64,432]{3,2,1,0:T(8,128)(2,1)S(1)}, bf16[2,2,64,432]{3,2,1,0:T(8,128)(2,1)S(1)}, u32[]{:S(2)}, u32[]{:S(2)}) collective-permute-start(bf16[2,2,64,432]{3,2,1,0:T(8,128)(2,1)S(1)} %collective-permute-done.7.refs_10_), channel_id=1, source_target_pairs={{0,1},{1,2},{2,3},{3,4},{4,5},{5,6},{6,7},{7,0},{8,9},{9,10},{10,1... | collective-permute-start | bytes 663560 | tf_op jit(solution)/shard_map/ppermute | solution.py:34
  19.3 5.3 %collective-permute-start.15 = (s32[1]{0:T(128)}, s32[1]{0:T(128)}, u32[]{:S(2)}, u32[]{:S(2)}) collective-permute-start(s32[1]{0:T(128)} %param.6), channel_id=1, source_target_pairs={{0,128},{64,192},{128,0},{192,64},{1,129},{65,193},{129,1},{193,65... | collective-permute-start | bytes 20 | tf_op jit(solution)/shard_map/ppermute | solution.py:38
  20.7 3.9 %collective-permute-start.14 = (s32[1]{0:T(128)}, s32[1]{0:T(128)}, u32[]{:S(2)}, u32[]{:S(2)}) collective-permute-start(s32[1]{0:T(128)} %param.6), channel_id=1, source_target_pairs={{0,64},{64,0},{128,192},{192,128},{1,65},{65,1},{129,193},{193,129... | collective-permute-start | bytes 20 | tf_op jit(solution)/shard_map/ppermute | solution.py:38
  22.7 16.5 %collective-permute-start.1 = (bf16[2,2,64,432]{3,2,1,0:T(8,128)(2,1)S(1)}, bf16[2,2,64,432]{3,2,1,0:T(8,128)(2,1)S(1)}, u32[]{:S(2)}, u32[]{:S(2)}) collective-permute-start(bf16[2,2,64,432]{3,2,1,0:T(8,128)(2,1)S(1)} %get-tuple-element.34.refs_0_.refs_8_), channel_id=1, source_target_pairs={{0,8},{1,9},{2,10},{3,11},{4,12},{5,13},{6,14},{7,15},{8,0},{9,1},... | collective-permute-start | bytes 663560 | tf_op jit(solution)/shard_map/ppermute | solution.py:34
  27.7 13.3 %collective-permute-start.8 = (bf16[2,2,64,432]{3,2,1,0:T(8,128)(2,1)S(1)}, bf16[2,2,64,432]{3,2,1,0:T(8,128)(2,1)S(1)}, u32[]{:S(2)}, u32[]{:S(2)}) collective-permute-start(bf16[2,2,64,432]{3,2,1,0:T(8,128)(2,1)S(1)} %collective-permute-done.6.refs_9_), channel_id=1, source_target_pairs={{0,7},{1,0},{2,1},{3,2},{4,3},{5,4},{6,5},{7,6},{8,15},{9,8},{10,9... | collective-permute-start | bytes 663560 | tf_op jit(solution)/shard_map/ppermute | solution.py:34
  31.0 10.4 %collective-permute-start.11 = (bf16[2,2,64,432]{3,2,1,0:T(8,128)(2,1)S(1)}, bf16[2,2,64,432]{3,2,1,0:T(8,128)(2,1)S(1)}, u32[]{:S(2)}, u32[]{:S(2)}) collective-permute-start(bf16[2,2,64,432]{3,2,1,0:T(8,128)(2,1)S(1)} %collective-permute-done.9.refs_12_), channel_id=1, source_target_pairs={{0,1},{1,2},{2,3},{3,4},{4,5},{5,6},{6,7},{7,0},{8,9},{9,10},{10,1... | collective-permute-start | bytes 663560 | tf_op jit(solution)/shard_map/ppermute | solution.py:34
  36.7 45.2 %copy-start.17 = (bf16[2,2,64,512]{3,2,1,0:T(8,128)(2,1)S(1)}, bf16[2,2,64,512]{3,2,1,0:T(8,128)(2,1)}, u32[]{:S(2)}) copy-start(bf16[2,2,64,512]{3,2,1,0:T(8,128)(2,1)} %get-tuple-element.22) | copy-start | bytes 786436
  36.7 47.0 %copy-start.16 = (bf16[2,2,64,512]{3,2,1,0:T(8,128)(2,1)S(1)}, bf16[2,2,64,512]{3,2,1,0:T(8,128)(2,1)}, u32[]{:S(2)}) copy-start(bf16[2,2,64,512]{3,2,1,0:T(8,128)(2,1)} %get-tuple-element.23) | copy-start | bytes 786436
  36.7 25.0 %collective-permute-start.16 = (bf16[2,2,64,512]{3,2,1,0:T(8,128)(2,1)}, bf16[2,2,64,512]{3,2,1,0:T(8,128)(2,1)S(1)}, u32[]{:S(2)}, u32[]{:S(2)}) collective-permute-start(bf16[2,2,64,512]{3,2,1,0:T(8,128)(2,1)} %get-tuple-element.17), channel_id=1, source_target_pairs={{0,8},{1,9},{2,10},{3,11},{4,12},{5,13},{6,14},{7,15},{8,0},{9,1},... | collective-permute-start | bytes 786440 | tf_op jit(solution)/shard_map/ppermute | solution.py:34
  37.6 27.9 %collective-permute-start.17 = (bf16[2,2,64,512]{3,2,1,0:T(8,128)(2,1)}, bf16[2,2,64,512]{3,2,1,0:T(8,128)(2,1)S(1)}, u32[]{:S(2)}, u32[]{:S(2)}) collective-permute-start(bf16[2,2,64,512]{3,2,1,0:T(8,128)(2,1)} %get-tuple-element.18), channel_id=1, source_target_pairs={{0,16},{1,17},{2,18},{3,19},{4,20},{5,21},{6,22},{7,23},{8,24},{9,... | collective-permute-start | bytes 786440 | tf_op jit(solution)/shard_map/ppermute | solution.py:34
  39.2 51.9 %copy-start.2 = (bf16[2,2,64,432]{3,2,1,0:T(8,128)(2,1)}, bf16[2,2,64,432]{3,2,1,0:T(8,128)(2,1)S(1)}, u32[]{:S(2)}) copy-start(bf16[2,2,64,432]{3,2,1,0:T(8,128)(2,1)S(1)} %collective-permute-done.1.refs_1_) | copy-start | bytes 663556
  39.3 21.8 %collective-permute-start.4 = (bf16[2,2,2,64,432]{4,3,2,1,0:T(8,128)(2,1)S(1)}, bf16[2,2,2,64,432]{4,3,2,1,0:T(8,128)(2,1)S(1)}, u32[]{:S(2)}, u32[]{:S(2)}) collective-permute-start(bf16[2,2,2,64,432]{4,3,2,1,0:T(8,128)(2,1)S(1)} %pad_maximum_fusion), channel_id=1, source_target_pairs={{0,48},{1,49},{2,50},{3,51},{4,52},{5,53},{6,54},{7,55},{8,56},{9,... | collective-permute-start | bytes 1327112 | tf_op jit(solution)/shard_map/ppermute | solution.py:34
  41.0 50.0 %copy-start.8 = (bf16[2,2,64,432]{3,2,1,0:T(8,128)(2,1)}, bf16[2,2,64,432]{3,2,1,0:T(8,128)(2,1)S(1)}, u32[]{:S(2)}) copy-start(bf16[2,2,64,432]{3,2,1,0:T(8,128)(2,1)S(1)} %collective-permute-done.8.refs_11_) | copy-start | bytes 663556
  41.0 17.1 %collective-permute-start.2 = (bf16[2,2,2,64,432]{4,3,2,0,1:T(8,128)(2,1)S(1)}, bf16[2,2,2,64,432]{4,3,2,0,1:T(8,128)(2,1)S(1)}, u32[]{:S(2)}, u32[]{:S(2)}) collective-permute-start(bf16[2,2,2,64,432]{4,3,2,0,1:T(8,128)(2,1)S(1)} %copy.6), channel_id=1, source_target_pairs={{0,16},{1,17},{2,18},{3,19},{4,20},{5,21},{6,22},{7,23},{8,24},{9,... | collective-permute-start | bytes 1327112 | tf_op jit(solution)/shard_map/ppermute | solution.py:34
  41.4 49.6 %copy-start.3 = (bf16[2,2,64,432]{3,2,1,0:T(8,128)(2,1)}, bf16[2,2,64,432]{3,2,1,0:T(8,128)(2,1)S(1)}, u32[]{:S(2)}) copy-start(bf16[2,2,64,432]{3,2,1,0:T(8,128)(2,1)S(1)} %collective-permute-done.11.refs_14_) | copy-start | bytes 663556
  41.4 7.5 %collective-permute-start.10 = (bf16[2,2,64,432]{3,2,1,0:T(8,128)(2,1)S(1)}, bf16[2,2,64,432]{3,2,1,0:T(8,128)(2,1)S(1)}, u32[]{:S(2)}, u32[]{:S(2)}) collective-permute-start(bf16[2,2,64,432]{3,2,1,0:T(8,128)(2,1)S(1)} %collective-permute-done.8.refs_11_), channel_id=1, source_target_pairs={{0,7},{1,0},{2,1},{3,2},{4,3},{5,4},{6,5},{7,6},{8,15},{9,8},{10,9... | collective-permute-start | bytes 663560 | tf_op jit(solution)/shard_map/ppermute | solution.py:34
  48.9 16.8 %collective-permute-start.12 = (bf16[2,64,432]{2,1,0:T(8,128)(2,1)S(1)}, bf16[2,64,432]{2,1,0:T(8,128)(2,1)S(1)}, u32[]{:S(2)}, u32[]{:S(2)}) collective-permute-start(bf16[2,64,432]{2,1,0:T(8,128)(2,1)S(1)} %slice_bitcast_fusion.7), channel_id=1, source_target_pairs={{0,1},{1,2},{2,3},{3,4},{4,5},{5,6},{6,7},{7,0},{8,9},{9,10},{10,1... | collective-permute-start | bytes 331784 | tf_op jit(solution)/shard_map/ppermute | solution.py:34
  58.1 9.4 %collective-permute-start.13 = (bf16[2,64,432]{2,1,0:T(8,128)(2,1)S(1)}, bf16[2,64,432]{2,1,0:T(8,128)(2,1)S(1)}, u32[]{:S(2)}, u32[]{:S(2)}) collective-permute-start(bf16[2,64,432]{2,1,0:T(8,128)(2,1)S(1)} %slice_bitcast_fusion.6), channel_id=1, source_target_pairs={{0,7},{1,0},{2,1},{3,2},{4,3},{5,4},{6,5},{7,6},{8,15},{9,8},{10,9... | collective-permute-start | bytes 331784 | tf_op jit(solution)/shard_map/ppermute | solution.py:34
  61.1 20.8 %collective-permute-start.3 = (bf16[2,2,64,432]{3,2,1,0:T(8,128)(2,1)S(1)}, bf16[2,2,64,432]{3,2,1,0:T(8,128)(2,1)S(1)}, u32[]{:S(2)}, u32[]{:S(2)}) collective-permute-start(bf16[2,2,64,432]{3,2,1,0:T(8,128)(2,1)S(1)} %slice_bitcast_fusion.3), channel_id=1, source_target_pairs={{0,16},{1,17},{2,18},{3,19},{4,20},{5,21},{6,22},{7,23},{8,24},{9,... | collective-permute-start | bytes 663560 | tf_op jit(solution)/shard_map/ppermute | solution.py:34
  61.7 22.0 %collective-permute-start.5 = (bf16[2,2,64,432]{3,2,1,0:T(8,128)(2,1)S(1)}, bf16[2,2,64,432]{3,2,1,0:T(8,128)(2,1)S(1)}, u32[]{:S(2)}, u32[]{:S(2)}) collective-permute-start(bf16[2,2,64,432]{3,2,1,0:T(8,128)(2,1)S(1)} %slice_bitcast_fusion.2), channel_id=1, source_target_pairs={{0,48},{1,49},{2,50},{3,51},{4,52},{5,53},{6,54},{7,55},{8,56},{9,... | collective-permute-start | bytes 663560 | tf_op jit(solution)/shard_map/ppermute | solution.py:34
  65.6 22.8 %collective-permute-start.18 = (bf16[2,2,64,512]{3,2,1,0:T(8,128)(2,1)S(1)}, bf16[2,2,64,512]{3,2,1,0:T(8,128)(2,1)S(1)}, u32[]{:S(2)}, u32[]{:S(2)}) collective-permute-start(bf16[2,2,64,512]{3,2,1,0:T(8,128)(2,1)S(1)} %copy-done.20), channel_id=1, source_target_pairs={{0,24},{1,25},{2,26},{3,27},{4,28},{5,29},{6,30},{7,31},{8,16},{9,... | collective-permute-start | bytes 786440 | tf_op jit(solution)/shard_map/ppermute | solution.py:34
  65.7 22.7 %collective-permute-start.19 = (bf16[2,2,64,512]{3,2,1,0:T(8,128)(2,1)S(1)}, bf16[2,2,64,512]{3,2,1,0:T(8,128)(2,1)S(1)}, u32[]{:S(2)}, u32[]{:S(2)}) collective-permute-start(bf16[2,2,64,512]{3,2,1,0:T(8,128)(2,1)S(1)} %copy-done.19), channel_id=1, source_target_pairs={{0,32},{1,33},{2,34},{3,35},{4,36},{5,37},{6,38},{7,39},{8,40},{9,... | collective-permute-start | bytes 786440 | tf_op jit(solution)/shard_map/ppermute | solution.py:34
  67.5 20.9 %collective-permute-start.20 = (bf16[2,2,64,512]{3,2,1,0:T(8,128)(2,1)S(1)}, bf16[2,2,64,512]{3,2,1,0:T(8,128)(2,1)S(1)}, u32[]{:S(2)}, u32[]{:S(2)}) collective-permute-start(bf16[2,2,64,512]{3,2,1,0:T(8,128)(2,1)S(1)} %copy-done.18), channel_id=1, source_target_pairs={{0,40},{1,41},{2,42},{3,43},{4,44},{5,45},{6,46},{7,47},{8,32},{9,... | collective-permute-start | bytes 786440 | tf_op jit(solution)/shard_map/ppermute | solution.py:34
  81.8 6.5 %collective-permute-start.21 = (bf16[2,2,64,512]{3,2,1,0:T(8,128)(2,1)S(1)}, bf16[2,2,64,512]{3,2,1,0:T(8,128)(2,1)S(1)}, u32[]{:S(2)}, u32[]{:S(2)}) collective-permute-start(bf16[2,2,64,512]{3,2,1,0:T(8,128)(2,1)S(1)} %copy-done.17), channel_id=1, source_target_pairs={{0,48},{1,49},{2,50},{3,51},{4,52},{5,53},{6,54},{7,55},{8,56},{9,... | collective-permute-start | bytes 786440 | tf_op jit(solution)/shard_map/ppermute | solution.py:34
  83.7 7.3 %collective-permute-start.22 = (bf16[2,2,64,512]{3,2,1,0:T(8,128)(2,1)S(1)}, bf16[2,2,64,512]{3,2,1,0:T(8,128)(2,1)S(1)}, u32[]{:S(2)}, u32[]{:S(2)}) collective-permute-start(bf16[2,2,64,512]{3,2,1,0:T(8,128)(2,1)S(1)} %copy-done.16), channel_id=1, source_target_pairs={{0,56},{1,57},{2,58},{3,59},{4,60},{5,61},{6,62},{7,63},{8,48},{9,... | collective-permute-start | bytes 786440 | tf_op jit(solution)/shard_map/ppermute | solution.py:34
  98.2 3.0 %collective-permute-start.23 = (bf16[2,512,512]{2,1,0:T(8,128)(2,1)}, bf16[2,512,512]{2,1,0:T(8,128)(2,1)S(1)}, u32[]{:S(2)}, u32[]{:S(2)}) collective-permute-start(bf16[2,512,512]{2,1,0:T(8,128)(2,1)} %get-tuple-element.24), channel_id=1, source_target_pairs={{0,64},{64,0},{128,192},{192,128},{1,65},{65,1},{129,193},{193,129... | collective-permute-start | bytes 3145736 | tf_op jit(solution)/shard_map/ppermute | solution.py:38
  131.6 16.6 %all-to-all-start.1 = ((f32[8,16,432]{2,1,0:T(8,128)}), f32[8,16,432]{2,1,0:T(8,128)S(1)}, u32[]{:S(2)}, u32[]{:S(2)}) async-start(f32[8,16,432]{2,1,0:T(8,128)} %convert_reduce_fusion), calls=%async_computation.1 | async-start | bytes 524288 | tf_op jit(solution)/shard_map/all_to_all | solution.py:173
  (14 other events, 270.8 us)

commit v3 on v2

v3 whole, which is shorter than its diff:
```python
import functools

import jax
import jax.numpy as jnp
import numpy as np
from jax import lax
from jax.experimental import pallas as pl
from jax.experimental.pallas import tpu as pltpu
from jax.sharding import PartitionSpec as P

NB = 432
SLAB = 64
NY, NX, NZ = 4, 2, 8
GROUPS = NY * NX
BLOCK = NZ * SLAB
WHOLE = 384
LANES = 2 * WHOLE + 128
VMEM = 56 * 1024 * 1024

OFFSETS = [(0, 0), (0, 1), (1, 0), (1, 1), (2, 0), (2, 1), (3, 0), (3, 1)]


def band_route(dy, dx, dz):
    route = []
    for y in range(NY):
        for x in range(NX):
            for z in range(NZ):
                there = ((y + dy) % NY * NX + (x + dx) % NX) * NZ + (z + dz) % NZ
                route.append(((y * NX + x) * NZ + z, there))
    return route


def shift(block, dy, dx, dz):
    return lax.ppermute(block, "band", band_route(dy, dx, dz))


def swap_groups(block, bit):
    return lax.ppermute(block, "kgrp", [(k, k ^ bit) for k in range(4)])


def dot(a, b, dims):
    return lax.dot_general(a, b, ((dims[0], dims[1]), ((), ())), preferred_element_type=jnp.float32)


def pack_body(slot_ref, kernels_ref, *refs):
    outs, held, sem = refs[:2], refs[2], refs[3]
    copies = [
        pltpu.make_async_copy(kernels_ref.at[slot_ref[which]], held.at[which], sem.at[which])
        for which in range(2)
    ]
    for copy in copies:
        copy.start()
    for which, copy in enumerate(copies):
        copy.wait()
        for i in range(GROUPS):
            outs[which][i] = held[which, :, :, pl.ds(i * BLOCK, BLOCK)]


def pack(slots, kernels):
    piece = jax.ShapeDtypeStruct((GROUPS, 2, SLAB, BLOCK), jnp.bfloat16)
    return pl.pallas_call(
        pack_body,
        out_shape=[piece] * 2,
        in_specs=[pl.BlockSpec(memory_space=pltpu.SMEM), pl.BlockSpec(memory_space=pl.ANY)],
        out_specs=[pl.BlockSpec(memory_space=pltpu.VMEM)] * 2,
        scratch_shapes=[
            pltpu.VMEM((2, 2, SLAB, GROUPS * BLOCK), jnp.bfloat16),
            pltpu.SemaphoreType.DMA((2,)),
        ],
        compiler_params=pltpu.CompilerParams(vmem_limit_bytes=VMEM),
        name="pack",
    )(slots, kernels)


def mix_body(place_ref, sign_ref, *refs):
    rows, refs = refs[:GROUPS], refs[GROUPS:]
    gathered_ref, kerns, refs = refs[0], refs[1:3], refs[3:]
    m_ref, row_ref, col_ref, other_rows, other_cols = refs
    for i in range(GROUPS):
        at = pl.ds(pl.multiple_of(place_ref[i] * SLAB, SLAB), SLAB)
        row_ref[:, at, :] = rows[i][0]
        other_rows[:, at, :] = rows[i][1]
    for i in range(NZ):
        at = pl.ds(i * SLAB, SLAB)
        col_ref[:, at, :] = gathered_ref[i, 0]
        other_cols[:, at, :] = gathered_ref[i, 1]
    last = ((1,), (1,))
    per = BLOCK // 2
    for part in range(2):
        at = pl.ds(part * per, per)
        total_re = total_im = None
        for which, (a_ref, b_ref) in enumerate(((row_ref, col_ref), (other_rows, other_cols))):
            a_re, a_im, b_re, b_im = a_ref[0], a_ref[1], b_ref[0, at, :], b_ref[1, at, :]
            p_re = dot(a_re, b_re, last) + dot(a_im, b_im, last)
            p_im = dot(a_im, b_re, last) - dot(a_re, b_im, last)
            k_re = kerns[which][:, 0, :, at].reshape(BLOCK, per).astype(jnp.float32)
            k_im = kerns[which][:, 1, :, at].reshape(BLOCK, per).astype(jnp.float32)
            k_im = k_im * sign_ref[which]
            m_re = k_re * p_re - k_im * p_im
            m_im = k_re * p_im + k_im * p_re
            total_re = m_re if total_re is None else total_re + m_re
            total_im = m_im if total_im is None else total_im + m_im
        m_ref[0, :, at] = total_re.astype(jnp.bfloat16)
        m_ref[1, :, at] = total_im.astype(jnp.bfloat16)


def mix(place, sign, rows, gathered, kerns):
    vmem = pl.BlockSpec(memory_space=pltpu.VMEM)
    smem = pl.BlockSpec(memory_space=pltpu.SMEM)
    points = jax.ShapeDtypeStruct((2, BLOCK, NB), jnp.bfloat16)
    return pl.pallas_call(
        mix_body,
        out_shape=[jax.ShapeDtypeStruct((2, BLOCK, BLOCK), jnp.bfloat16), points, points],
        in_specs=[smem, smem] + [vmem] * (GROUPS + 3),
        out_specs=[vmem] * 3,
        scratch_shapes=[pltpu.VMEM((2, BLOCK, NB), jnp.bfloat16)] * 2,
        compiler_params=pltpu.CompilerParams(vmem_limit_bytes=VMEM),
        name="mix",
    )(place, sign, *rows, gathered, *kerns)


def halves(value):
    high = value.astype(jnp.bfloat16)
    return high, (value - high.astype(jnp.float32)).astype(jnp.bfloat16)


def project_body(m_ref, row_ref, col_ref, out_ref, x_ref):
    mid = ((1,), (0,))
    first = ((0,), (0,))
    m_re, m_im = m_ref[0], m_ref[1]
    c_re, c_im = col_ref[0], col_ref[1]
    y_re = halves(dot(m_re, c_re, mid) - dot(m_im, c_im, mid))
    y_im = halves(dot(m_re, c_im, mid) + dot(m_im, c_re, mid))
    r_re, r_im = row_ref[0], row_ref[1]

    def meet(a, pair):
        return dot(a, pair[0], first) + dot(a, pair[1], first)

    x_re = -(meet(r_re, y_re) + meet(r_im, y_im))
    x_im = meet(r_im, y_re) - meet(r_re, y_im)
    gap = jnp.zeros((NB, 64 - (NB - WHOLE)), jnp.float32)
    x_ref[pl.ds(NB, 8), :] = jnp.zeros((8, LANES), jnp.float32)
    x_ref[pl.ds(0, NB), pl.ds(0, WHOLE)] = x_re[:, :WHOLE]
    x_ref[pl.ds(0, NB), pl.ds(WHOLE, WHOLE)] = x_im[:, :WHOLE]
    x_ref[pl.ds(0, NB), pl.ds(2 * WHOLE, 128)] = jnp.concatenate(
        [x_re[:, WHOLE:], gap, x_im[:, WHOLE:], gap], axis=1
    )
    for d in range(GROUPS * NZ):
        out_ref[d] = x_ref[pl.ds(27 * d // 4, 8), :].astype(jnp.bfloat16)


def project(m, rows, cols):
    vmem = pl.BlockSpec(memory_space=pltpu.VMEM)
    return pl.pallas_call(
        project_body,
        out_shape=jax.ShapeDtypeStruct((GROUPS * NZ, 8, LANES), jnp.bfloat16),
        in_specs=[vmem] * 3,
        out_specs=vmem,
        scratch_shapes=[pltpu.VMEM((NB + 8, LANES), jnp.float32)],
        compiler_params=pltpu.CompilerParams(vmem_limit_bytes=VMEM),
        name="project",
    )(m, rows, cols)


def reduce_windows(windows):
    parts = lax.all_to_all(windows, "band", 0, 0)
    total = jnp.sum(parts.astype(jnp.float32), axis=0)
    tail = 2 * WHOLE
    rest = NB - WHOLE
    real = jnp.concatenate([total[:, :WHOLE], total[:, tail : tail + rest]], axis=1)
    imag = jnp.concatenate([total[:, WHOLE:tail], total[:, tail + 64 : tail + 64 + rest]], axis=1)
    return jnp.stack([real, imag])


def on_device(orbitals, kernels, pair_kdiff, stored_kernel_index):
    group = lax.axis_index("kgrp")
    band = lax.axis_index("band")
    y, x, z = band // (NX * NZ), band // NZ % NX, band % NZ
    odd = group % 2

    own = orbitals[0]
    diff_core = swap_groups(pair_kdiff, 1)
    diff_far = swap_groups(pair_kdiff, 2)
    far = swap_groups(own, 2)

    first = jnp.where(odd == 1, pair_kdiff[0], diff_core[0])
    second = jnp.where(odd == 1, diff_core[0], diff_far[0])
    slots = jnp.stack([stored_kernel_index[first], stored_kernel_index[second]])
    sign_own = jnp.where(odd == 1, -1.0, 1.0).astype(jnp.float32)
    sign = jnp.stack([sign_own, -sign_own])
    over_yx = [[g * NZ + z_at for g in range(GROUPS)] for z_at in range(NZ)]
    over_z = [[g * NZ + z_at for z_at in range(NZ)] for g in range(GROUPS)]
    kerns = [
        lax.all_to_all(block, "band", 0, 0, axis_index_groups=over_yx)
        for block in pack(slots, kernels)
    ]

    both = jnp.stack([own, far])
    gathered = lax.all_gather(both, "band", axis_index_groups=over_z)
    pair = jnp.stack([both, shift(both, 0, 1, 0)])
    up, down = shift(pair, 1, 0, 0), shift(pair, -1, 0, 0)
    over = jnp.stack([shift(up[:, 0], 1, 0, 0), shift(down[:, 1], -1, 0, 0)], axis=1)
    rows = [block[i] for block in (pair, up, over, down) for i in range(NX)]

    place = jnp.stack([(y - dy) % NY * NX + (x - dx) % NX for dy, dx in OFFSETS])
    m_out, own_rows, own_cols = mix(place, sign, rows, gathered, kerns)
    m_own = swap_groups(m_out, 1)
    total = reduce_windows(project(m_own, own_rows, own_cols))
    flat = total.reshape(2, 8 * NB)
    flat = lax.dynamic_slice(flat, (0, band * 27 % 4 * 108), (2, 27 * 108))
    return flat[None]


def solution(mesh):
    return jax.shard_map(
        on_device,
        mesh=mesh,
        in_specs=(P("kgrp", None, "band", None), P(None, None, "band", None), P("kgrp"), P()),
        out_specs=P("kgrp", None, "band"),
        check_vma=False,
    )
```

time: 150 us -> 152 us (1.013)
  blocking collectives: 22.5 us -> 0 us
  waiting for transfers between devices: 54.6 us -> 70.7 us
  between operations: 2.8 us -> 16.2 us
  starting transfers between devices: 39.9 us -> 32.2 us
  local copies, waits for them, and re-layouts: 6.96 us -> 8.94 us
    ppermute x20 -> x5, starting transfers between devices: 31.4 us -> 6.98 us  [shift(): return lax.ppermute(block, 'band', band_route(dy, dx, dz))]
    all_to_all x1 -> x0, blocking collectives: 22.5 us -> none  [reduce_windows(): parts = lax.all_to_all(parts, 'band', 0, 0, axis_index_groups=over_yx)]
    all_to_all x1 -> x3, starting transfers between devices: 5.57 us -> 22.3 us  [the longest x2 12.1 us: on_device(): lax.all_to_all(block, 'band', 0, 0, axis_index_groups=over_yx)]
    all_to_all x1 -> x3, waiting for transfers between devices: 11 us -> 25.5 us  [the longest x1 25.5 us: reduce_windows(): parts = lax.all_to_all(windows, 'band', 0, 0)]
    ppermute x4, waiting for transfers between devices: 9.68 us -> 11.6 us  [swap_groups(): return lax.ppermute(block, 'kgrp', [(k, k ^ bit) for k in range(4)])]
    ppermute x20 -> x5, waiting for transfers between devices: 34 us -> 33.5 us  [shift(): return lax.ppermute(block, 'band', band_route(dy, dx, dz))]
  transfers between devices with their start and end apart: 25 -> 13, of which waited for: 10 -> 7; matrix products, arithmetic and copies ran while one was open for 6% -> 7% of each run, Pallas kernels for 2% -> 2%
where the time goes in v3:
time: 152 us; the launch traced here: 150 us
  waiting for transfers between devices  70.7 us (47%)
  starting transfers between devices  32.2 us (21%)
  Pallas kernels  16.2 us (11%)
  between operations  16.2 us (11%)
  local copies, waits for them, and re-layouts  8.94 us (6%)
  other arithmetic  5.95 us (4%)
    ppermute x5, waiting for transfers between devices, shift(): return lax.ppermute(block, 'band', band_route(dy, dx, dz))  33.5 us
    all_to_all x1, waiting for transfers between devices, reduce_windows(): parts = lax.all_to_all(windows, 'band', 0, 0)  25.5 us
    all_to_all x2, starting transfers between devices, on_device(): lax.all_to_all(block, 'band', 0, 0, axis_index_groups=over_yx)  12.1 us
    ppermute x4, waiting for transfers between devices, swap_groups(): return lax.ppermute(block, 'kgrp', [(k, k ^ bit) for k in range(4)])  11.6 us
    all_to_all x1, starting transfers between devices, reduce_windows(): parts = lax.all_to_all(windows, 'band', 0, 0)  10.3 us
    ppermute x5, starting transfers between devices, shift(): return lax.ppermute(block, 'band', band_route(dy, dx, dz))  6.98 us
    pallas_call x1, Pallas kernels, mix(): pl.pallas_call(mix_body, out_shape=[jax.ShapeDtypeStruct((2, BLOCK, BLOCK...  6.45 us
    pallas_call x1, Pallas kernels, project(): pl.pallas_call(project_body, out_shape=jax.ShapeDtypeStruct((GROUPS * NZ,...  6.17 us
  transfers between devices with their start and end apart: 13, of which 7 were waited for; matrix products, arithmetic and copies ran while one was open for 7% of the time, Pallas kernels for 2%

profile of v3, /device:TPU:6, one launch (start us, length us, event | category | flops | bytes accessed | tf_op | source)
XLA Modules:
  0.0 150.1 jit_solution(13900994451157179476)
XLA Ops:
  6.5 1.4 collective-permute-start
  7.9 5.5 %collective-permute-done = bf16[2,64,432]{2,1,0:T(8,128)(2,1)S(1)} collective-permute-done((bf16[2,64,432]{2,1,0:T(8,128)(2,1)}, bf16[2,64,432]{2,1,0:T(8,128)(2,1)S(1)}, u32[]{:S(2)}, u32[]{:S(2)}) %collective-permute-start) | collective-permute-done | bytes 110624 | tf_op jit(solution)/shard_map/ppermute | solution.py:38
  13.5 1.6 %fusion.5 = (bf16[1,2,2,64,432]{4,3,2,0,1:T(8,128)(2,1)S(1)}, bf16[2,2,64,432]{3,2,1,0:T(8,128)(2,1)}) fusion(bf16[1,2,64,432]{3,2,1,0:T(8,128)(2,1)S(1)} %bitcast.47, bf16[1,2,64,432]{3,2,1,0:T(8,128)(2,1)} %param.4), kind=kLoop, calls=%fused_computation.23 | loop fusion | flops 110592 | bytes 663552 | tf_op jit(solution)/shard_map/stack | solution.py:200
  15.2 1.5 collective-permute-start.7
  17.3 3.2 %collective-permute-done.7 = s32[1]{0:T(128)} collective-permute-done((s32[1]{0:T(128)}, s32[1]{0:T(128)}, u32[]{:S(2)}, u32[]{:S(2)}) %collective-permute-start.7) | collective-permute-done | bytes 36 | tf_op jit(solution)/shard_map/ppermute | solution.py:38
  22.5 1.4 fusion.8
  23.9 1.9 %pad_add_fusion.slot_ref = s32[2]{0:T(128)} fusion(s32[1]{0:T(128)} %get-tuple-element.28, s32[1]{0:T(128)} %get-tuple-element.27), kind=kLoop, calls=%fused_computation.22 | loop fusion | flops 2 | bytes 16 | tf_op jit(solution)/shard_map/stack | solution.py:188
  25.9 3.6 %pack.1 = (bf16[8,2,64,512]{3,2,1,0:T(8,128)(2,1)}, bf16[8,2,64,512]{3,2,1,0:T(8,128)(2,1)}) custom-call(s32[2]{0:T(128)} %pad_add_fusion.slot_ref, bf16[4,2,64,4096]{3,2,1,0:T(8,128)(2,1)} %kernels_ref.1), custom_call_target="tpu_custom_call" | custom-call | tf_op jit(solution)/shard_map/pack/pallas_call | solution.py:61
  29.4 6.1 %all-to-all-start = ((bf16[8,2,64,512]{3,2,1,0:T(8,128)(2,1)}), bf16[8,2,64,512]{3,2,1,0:T(8,128)(2,1)S(1)}, u32[]{:S(2)}, u32[]{:S(2)}) async-start(bf16[8,2,64,512]{3,2,1,0:T(8,128)(2,1)} %get-tuple-element.10), calls=%async_computation | async-start | bytes 2097152 | tf_op jit(solution)/shard_map/all_to_all | solution.py:194
  35.6 15.2 %collective-permute-done.1.refs_1_ = bf16[2,2,64,432]{3,2,1,0:T(8,128)(2,1)S(1)} collective-permute-done((bf16[2,2,64,432]{3,2,1,0:T(8,128)(2,1)S(1)}, bf16[2,2,64,432]{3,2,1,0:T(8,128)(2,1)S(1)}, u32[]{:S(2)}, u32[]{:S(2)}) %collective-permute-start.1) | collective-permute-done | bytes 221216 | tf_op jit(solution)/shard_map/ppermute | solution.py:34
  50.9 0.9 copy.8
  51.8 3.0 %collective-permute-start.4 = (bf16[2,2,2,64,432]{4,3,2,1,0:T(8,128)(2,1)}, bf16[2,2,2,64,432]{4,3,2,1,0:T(8,128)(2,1)S(1)}, u32[]{:S(2)}, u32[]{:S(2)}) collective-permute-start(bf16[2,2,2,64,432]{4,3,2,1,0:T(8,128)(2,1)} %copy.8), channel_id=1, source_target_pairs={{0,48},{1,49},{2,50},{3,51},{4,52},{5,53},{6,54},{7,55},{8,56},{9,... | collective-permute-start | bytes 1327112 | tf_op jit(solution)/shard_map/ppermute | solution.py:34
  54.8 0.6 stack.80.place_ref
  55.4 0.6 pad_maximum_fusion.5.sign_ref
  56.0 6.0 %all-to-all-start.1 = ((bf16[8,2,64,512]{3,2,1,0:T(8,128)(2,1)}), bf16[8,2,64,512]{3,2,1,0:T(8,128)(2,1)S(1)}, u32[]{:S(2)}, u32[]{:S(2)}) async-start(bf16[8,2,64,512]{3,2,1,0:T(8,128)(2,1)} %get-tuple-element.11), calls=%async_computation.1 | async-start | bytes 2097152 | tf_op jit(solution)/shard_map/all_to_all | solution.py:194
  62.0 13.6 %collective-permute-done.4 = bf16[2,2,2,64,432]{4,3,2,1,0:T(8,128)(2,1)S(1)} collective-permute-done((bf16[2,2,2,64,432]{4,3,2,1,0:T(8,128)(2,1)}, bf16[2,2,2,64,432]{4,3,2,1,0:T(8,128)(2,1)S(1)}, u32[]{:S(2)}, u32[]{:S(2)}) %collective-permute-start.4) | collective-permute-done | bytes 442400 | tf_op jit(solution)/shard_map/ppermute | solution.py:34
  75.6 3.8 %collective-permute-start.5 = (bf16[2,2,64,432]{3,2,1,0:T(8,128)(2,1)S(1)}, bf16[2,2,64,432]{3,2,1,0:T(8,128)(2,1)S(1)}, u32[]{:S(2)}, u32[]{:S(2)}) collective-permute-start(bf16[2,2,64,432]{3,2,1,0:T(8,128)(2,1)S(1)} %slice_bitcast_fusion.2), channel_id=1, source_target_pairs={{0,48},{1,49},{2,50},{3,51},{4,52},{5,53},{6,54},{7,55},{8,56},{9,... | collective-permute-start | bytes 663560 | tf_op jit(solution)/shard_map/ppermute | solution.py:34
  79.4 1.0 slice_bitcast_fusion.3
  80.4 0.9 slice_bitcast_fusion
  81.4 1.9 %slice_bitcast_fusion.4 = (bf16[2,2,64,432]{3,2,1,0:T(8,128)(2,1)}, bf16[2,2,64,432]{3,2,1,0:T(8,128)(2,1)}) fusion(bf16[2,2,2,64,432]{4,3,2,0,1:T(8,128)(2,1)} %collective-permute-done.2), kind=kLoop, calls=%fused_computation.12 | loop fusion | bytes 884736 | tf_op jit(solution)/shard_map/squeeze | solution.py:203
  83.3 4.7 %collective-permute-done.3 = bf16[2,2,64,432]{3,2,1,0:T(8,128)(2,1)S(1)} collective-permute-done((bf16[2,2,64,432]{3,2,1,0:T(8,128)(2,1)S(1)}, bf16[2,2,64,432]{3,2,1,0:T(8,128)(2,1)S(1)}, u32[]{:S(2)}, u32[]{:S(2)}) %collective-permute-start.3) | collective-permute-done | bytes 221216 | tf_op jit(solution)/shard_map/ppermute | solution.py:34
  88.0 0.9 fusion.2
  88.9 1.0 copy-done.1
  89.8 6.5 %mix.1 = (bf16[2,512,512]{2,1,0:T(8,128)(2,1)}, bf16[2,512,432]{2,1,0:T(8,128)(2,1)}, bf16[2,512,432]{2,1,0:T(8,128)(2,1)}) custom-call(s32[8]{0:T(128)} %stack.80.place_ref, f32[2]{0:T(128)} %pad_maximum_fusion.5.sign_ref, bf16[2,2,64,432]{3,2,1,0:T(8,128)(2,1)} %get-tuple-element.22.refs_0_, bf16[2,2,64,432]{3,2,1,0:T(8,128)(2,1)} %copy-done.4, ...), custom_call_target="tpu_custom_call" | custom-call | tf_op jit(solution)/shard_map/mix/pallas_call | solution.py:111
  96.3 2.9 %collective-permute-done.8.m_ref = bf16[2,512,512]{2,1,0:T(8,128)(2,1)S(1)} collective-permute-done((bf16[2,512,512]{2,1,0:T(8,128)(2,1)}, bf16[2,512,512]{2,1,0:T(8,128)(2,1)S(1)}, u32[]{:S(2)}, u32[]{:S(2)}) %collective-permute-start.8) | collective-permute-done | bytes 1048608 | tf_op jit(solution)/shard_map/ppermute | solution.py:38
  99.2 1.0 copy-done.3
  100.1 6.2 %project.1 = bf16[64,8,896]{2,1,0:T(8,128)(2,1)} custom-call(bf16[2,512,512]{2,1,0:T(8,128)(2,1)} %copy-done.3, bf16[2,512,432]{2,1,0:T(8,128)(2,1)} %get-tuple-element.13.row_ref, bf16[2,512,432]{2,1,0:T(8,128)(2,1)} %get-tuple-element.14.col_ref), custom_call_target="tpu_custom_call" | custom-call | tf_op jit(solution)/shard_map/project/pallas_call | solution.py:154
  106.3 10.3 %all-to-all-start.2 = ((bf16[64,8,896]{2,1,0:T(8,128)(2,1)}), bf16[64,8,896]{2,1,0:T(8,128)(2,1)S(1)}, u32[]{:S(2)}, u32[]{:S(2)}) async-start(bf16[64,8,896]{2,1,0:T(8,128)(2,1)} %project.1), calls=%async_computation.2 | async-start | bytes 1835008 | tf_op jit(solution)/shard_map/all_to_all | solution.py:166
  116.6 25.5 %all-to-all-done.2 = bf16[64,8,896]{2,1,0:T(8,128)(2,1)S(1)} async-done(((bf16[64,8,896]{2,1,0:T(8,128)(2,1)}), bf16[64,8,896]{2,1,0:T(8,128)(2,1)S(1)}, u32[]{:S(2)}, u32[]{:S(2)}) %all-to-all-start.2) | async-done | bytes 917536 | tf_op jit(solution)/shard_map/all_to_all | solution.py:166
  142.1 0.2 convert_reduce_fusion
  142.4 0.1 stack.93
  142.5 0.7 fusion.4
  (27 shorter events, 0.5 us)
Async XLA Ops:
  6.5 82.3 %all-gather.3.cloned.1.call-start = ((), (), s32[]{:S(2)}) async-start(), calls=%async_computation.3 | async-start | bytes 2359296 | tf_op jit(solution)/shard_map/all_gather | solution.py:199
  6.5 7.0 %collective-permute-start = (bf16[2,64,432]{2,1,0:T(8,128)(2,1)}, bf16[2,64,432]{2,1,0:T(8,128)(2,1)S(1)}, u32[]{:S(2)}, u32[]{:S(2)}) collective-permute-start(bf16[2,64,432]{2,1,0:T(8,128)(2,1)} %bitcast.46), channel_id=1, source_target_pairs={{0,128},{64,192},{128,0},{192,64},{1,129},{65,193},{129,1},{193,65... | collective-permute-start | bytes 331784 | tf_op jit(solution)/shard_map/ppermute | solution.py:38
  15.2 5.4 %collective-permute-start.7 = (s32[1]{0:T(128)}, s32[1]{0:T(128)}, u32[]{:S(2)}, u32[]{:S(2)}) collective-permute-start(s32[1]{0:T(128)} %param.6), channel_id=1, source_target_pairs={{0,128},{64,192},{128,0},{192,64},{1,129},{65,193},{129,1},{193,65... | collective-permute-start | bytes 20 | tf_op jit(solution)/shard_map/ppermute | solution.py:38
  16.6 3.9 %collective-permute-start.6 = (s32[1]{0:T(128)}, s32[1]{0:T(128)}, u32[]{:S(2)}, u32[]{:S(2)}) collective-permute-start(s32[1]{0:T(128)} %param.6), channel_id=1, source_target_pairs={{0,64},{64,0},{128,192},{192,128},{1,65},{65,1},{129,193},{193,129... | collective-permute-start | bytes 20 | tf_op jit(solution)/shard_map/ppermute | solution.py:38
  29.4 6.1 %copy-start.2 = (bf16[2,2,64,432]{3,2,1,0:T(8,128)(2,1)S(1)}, bf16[2,2,64,432]{3,2,1,0:T(8,128)(2,1)}, u32[]{:S(2)}) copy-start(bf16[2,2,64,432]{3,2,1,0:T(8,128)(2,1)} %get-tuple-element.22.refs_0_) | copy-start | bytes 663556
  29.4 26.6 %all-to-all-start = ((bf16[8,2,64,512]{3,2,1,0:T(8,128)(2,1)}), bf16[8,2,64,512]{3,2,1,0:T(8,128)(2,1)S(1)}, u32[]{:S(2)}, u32[]{:S(2)}) async-start(bf16[8,2,64,512]{3,2,1,0:T(8,128)(2,1)} %get-tuple-element.10), calls=%async_computation | async-start | bytes 2097152 | tf_op jit(solution)/shard_map/all_to_all | solution.py:194
  35.5 15.3 %collective-permute-start.1 = (bf16[2,2,64,432]{3,2,1,0:T(8,128)(2,1)S(1)}, bf16[2,2,64,432]{3,2,1,0:T(8,128)(2,1)S(1)}, u32[]{:S(2)}, u32[]{:S(2)}) collective-permute-start(bf16[2,2,64,432]{3,2,1,0:T(8,128)(2,1)S(1)} %copy-done.2), channel_id=1, source_target_pairs={{0,8},{1,9},{2,10},{3,11},{4,12},{5,13},{6,14},{7,15},{8,0},{9,1},... | collective-permute-start | bytes 663560 | tf_op jit(solution)/shard_map/ppermute | solution.py:34
  50.8 5.2 %copy-start.4 = (bf16[2,2,64,432]{3,2,1,0:T(8,128)(2,1)}, bf16[2,2,64,432]{3,2,1,0:T(8,128)(2,1)S(1)}, u32[]{:S(2)}) copy-start(bf16[2,2,64,432]{3,2,1,0:T(8,128)(2,1)S(1)} %collective-permute-done.1.refs_1_) | copy-start | bytes 663556
  51.8 23.8 %collective-permute-start.4 = (bf16[2,2,2,64,432]{4,3,2,1,0:T(8,128)(2,1)}, bf16[2,2,2,64,432]{4,3,2,1,0:T(8,128)(2,1)S(1)}, u32[]{:S(2)}, u32[]{:S(2)}) collective-permute-start(bf16[2,2,2,64,432]{4,3,2,1,0:T(8,128)(2,1)} %copy.8), channel_id=1, source_target_pairs={{0,48},{1,49},{2,50},{3,51},{4,52},{5,53},{6,54},{7,55},{8,56},{9,... | collective-permute-start | bytes 1327112 | tf_op jit(solution)/shard_map/ppermute | solution.py:34
  54.8 24.6 %collective-permute-start.2 = (bf16[2,2,2,64,432]{4,3,2,0,1:T(8,128)(2,1)S(1)}, bf16[2,2,2,64,432]{4,3,2,0,1:T(8,128)(2,1)}, u32[]{:S(2)}, u32[]{:S(2)}) collective-permute-start(bf16[2,2,2,64,432]{4,3,2,0,1:T(8,128)(2,1)S(1)} %pad_maximum_fusion), channel_id=1, source_target_pairs={{0,16},{1,17},{2,18},{3,19},{4,20},{5,21},{6,22},{7,23},{8,24},{9,... | collective-permute-start | bytes 1327112 | tf_op jit(solution)/shard_map/ppermute | solution.py:34
  56.0 25.3 %copy-start = (bf16[8,2,64,512]{3,2,1,0:T(8,128)(2,1)}, bf16[8,2,64,512]{3,2,1,0:T(8,128)(2,1)S(1)}, u32[]{:S(2)}) copy-start(bf16[8,2,64,512]{3,2,1,0:T(8,128)(2,1)S(1)} %all-to-all-done.refs_9_) | copy-start | bytes 3145732
  56.0 32.8 %all-to-all-start.1 = ((bf16[8,2,64,512]{3,2,1,0:T(8,128)(2,1)}), bf16[8,2,64,512]{3,2,1,0:T(8,128)(2,1)S(1)}, u32[]{:S(2)}, u32[]{:S(2)}) async-start(bf16[8,2,64,512]{3,2,1,0:T(8,128)(2,1)} %get-tuple-element.11), calls=%async_computation.1 | async-start | bytes 2097152 | tf_op jit(solution)/shard_map/all_to_all | solution.py:194
  75.6 7.7 %collective-permute-start.5 = (bf16[2,2,64,432]{3,2,1,0:T(8,128)(2,1)S(1)}, bf16[2,2,64,432]{3,2,1,0:T(8,128)(2,1)S(1)}, u32[]{:S(2)}, u32[]{:S(2)}) collective-permute-start(bf16[2,2,64,432]{3,2,1,0:T(8,128)(2,1)S(1)} %slice_bitcast_fusion.2), channel_id=1, source_target_pairs={{0,48},{1,49},{2,50},{3,51},{4,52},{5,53},{6,54},{7,55},{8,56},{9,... | collective-permute-start | bytes 663560 | tf_op jit(solution)/shard_map/ppermute | solution.py:34
  80.3 7.7 %collective-permute-start.3 = (bf16[2,2,64,432]{3,2,1,0:T(8,128)(2,1)S(1)}, bf16[2,2,64,432]{3,2,1,0:T(8,128)(2,1)S(1)}, u32[]{:S(2)}, u32[]{:S(2)}) collective-permute-start(bf16[2,2,64,432]{3,2,1,0:T(8,128)(2,1)S(1)} %slice_bitcast_fusion.3), channel_id=1, source_target_pairs={{0,16},{1,17},{2,18},{3,19},{4,20},{5,21},{6,22},{7,23},{8,24},{9,... | collective-permute-start | bytes 663560 | tf_op jit(solution)/shard_map/ppermute | solution.py:34
  88.9 1.0 copy-start.1
  96.3 2.9 %collective-permute-start.8 = (bf16[2,512,512]{2,1,0:T(8,128)(2,1)}, bf16[2,512,512]{2,1,0:T(8,128)(2,1)S(1)}, u32[]{:S(2)}, u32[]{:S(2)}) collective-permute-start(bf16[2,512,512]{2,1,0:T(8,128)(2,1)} %get-tuple-element.12), channel_id=1, source_target_pairs={{0,64},{64,0},{128,192},{192,128},{1,65},{65,1},{129,193},{193,129... | collective-permute-start | bytes 3145736 | tf_op jit(solution)/shard_map/ppermute | solution.py:38
  99.2 1.0 copy-start.3
  106.3 35.8 %all-to-all-start.2 = ((bf16[64,8,896]{2,1,0:T(8,128)(2,1)}), bf16[64,8,896]{2,1,0:T(8,128)(2,1)S(1)}, u32[]{:S(2)}, u32[]{:S(2)}) async-start(bf16[64,8,896]{2,1,0:T(8,128)(2,1)} %project.1), calls=%async_computation.2 | async-start | bytes 1835008 | tf_op jit(solution)/shard_map/all_to_all | solution.py:166
Sparse Core Ops, SparseCore 0:
  15.3 43.9 all-gather.2

commit v4 on v3

v4 whole, which is shorter than its diff:
```python
import functools

import jax
import jax.numpy as jnp
import numpy as np
from jax import lax
from jax.experimental import pallas as pl
from jax.experimental.pallas import tpu as pltpu
from jax.sharding import PartitionSpec as P

NB = 432
SLAB = 64
NY, NX, NZ = 4, 2, 8
GROUPS = NY * NX
BLOCK = NZ * SLAB
WHOLE = 384
LANES = 2 * WHOLE + 128
VMEM = 56 * 1024 * 1024

OFFSETS = [(dy, dx) for dx in range(NX) for dy in range(NY)]


def band_route(dy, dx, dz):
    route = []
    for y in range(NY):
        for x in range(NX):
            for z in range(NZ):
                there = ((y + dy) % NY * NX + (x + dx) % NX) * NZ + (z + dz) % NZ
                route.append(((y * NX + x) * NZ + z, there))
    return route


def shift(block, dy, dx, dz):
    return lax.ppermute(block, "band", band_route(dy, dx, dz))


def swap_groups(block, bit):
    return lax.ppermute(block, "kgrp", [(k, k ^ bit) for k in range(4)])


def other_side(block):
    route = [(i, j) for i, j in band_route(0, 1, 0)]
    both = [((k ^ 2) * 64 + i, k * 64 + j) for k in range(4) for i, j in route]
    return lax.ppermute(block, ("kgrp", "band"), both)


def dot(a, b, dims):
    return lax.dot_general(a, b, ((dims[0], dims[1]), ((), ())), preferred_element_type=jnp.float32)


def pack_body(odd_ref, own_ref, core_ref, far_ref, stored_ref, kernels_ref, out_ref, held, sem):
    odd = odd_ref[0] == 1
    own, core, far = stored_ref[own_ref[0]], stored_ref[core_ref[0]], stored_ref[far_ref[0]]
    shared = jnp.where(odd, own, core)
    single = jnp.where(odd, core, far)
    copies = [
        pltpu.make_async_copy(kernels_ref.at[shared, odd_ref[0]], held.at[0], sem.at[0]),
        pltpu.make_async_copy(kernels_ref.at[single, 0], held.at[1], sem.at[1]),
        pltpu.make_async_copy(kernels_ref.at[single, 1], held.at[2], sem.at[2]),
    ]
    for copy in copies:
        copy.start()
    for which, copy in enumerate(copies):
        copy.wait()
        for i in range(GROUPS):
            out_ref[i, which] = held[which, :, pl.ds(i * BLOCK, BLOCK)]


def pack(odd, own, core, far, stored, kernels):
    smem = pl.BlockSpec(memory_space=pltpu.SMEM)
    return pl.pallas_call(
        pack_body,
        out_shape=jax.ShapeDtypeStruct((GROUPS, 3, SLAB, BLOCK), jnp.bfloat16),
        in_specs=[smem] * 5 + [pl.BlockSpec(memory_space=pl.ANY)],
        out_specs=pl.BlockSpec(memory_space=pltpu.VMEM),
        scratch_shapes=[
            pltpu.VMEM((3, SLAB, GROUPS * BLOCK), jnp.bfloat16),
            pltpu.SemaphoreType.DMA((3,)),
        ],
        compiler_params=pltpu.CompilerParams(vmem_limit_bytes=VMEM),
        name="pack",
    )(odd, own, core, far, stored, kernels)


def mix_body(place_ref, odd_ref, *refs):
    near_ref, own_side, far_side, gathered_ref, kern_ref, half_ref = refs[:6]
    m_ref, row_ref, col_ref, other_rows, other_cols = refs[6:]
    for i in range(NY):
        at = pl.ds(pl.multiple_of(place_ref[i] * SLAB, SLAB), SLAB)
        row_ref[:, at, :] = near_ref[i, 0]
        other_rows[:, at, :] = near_ref[i, 1]
        at = pl.ds(pl.multiple_of(place_ref[NY + i] * SLAB, SLAB), SLAB)
        row_ref[:, at, :] = own_side[i]
        other_rows[:, at, :] = far_side[i]
    for i in range(NZ):
        at = pl.ds(i * SLAB, SLAB)
        col_ref[:, at, :] = gathered_ref[i, 0]
        other_cols[:, at, :] = gathered_ref[i, 1]
    last = ((1,), (1,))
    per = BLOCK // 2
    odd = odd_ref[0] == 1
    sign = jnp.where(odd, -1.0, 1.0).astype(jnp.float32)

    def density(a_ref, b_ref, at):
        a_re, a_im, b_re, b_im = a_ref[0], a_ref[1], b_ref[0, at, :], b_ref[1, at, :]
        p_re = dot(a_re, b_re, last) + dot(a_im, b_im, last)
        p_im = dot(a_im, b_re, last) - dot(a_re, b_im, last)
        return p_re, p_im

    for part in range(2):
        at = pl.ds(part * per, per)
        p_re, p_im = density(row_ref, col_ref, at)
        mine = kern_ref[:, 0, :, at].reshape(BLOCK, per)
        other = half_ref[:, :, at].reshape(BLOCK, per)
        k_re = jnp.where(odd, other, mine).astype(jnp.float32)
        k_im = jnp.where(odd, mine, other).astype(jnp.float32) * sign
        total_re = k_re * p_re - k_im * p_im
        total_im = k_re * p_im + k_im * p_re
        p_re, p_im = density(other_rows, other_cols, at)
        k_re = kern_ref[:, 1, :, at].reshape(BLOCK, per).astype(jnp.float32)
        k_im = kern_ref[:, 2, :, at].reshape(BLOCK, per).astype(jnp.float32) * -sign
        total_re += k_re * p_re - k_im * p_im
        total_im += k_re * p_im + k_im * p_re
        m_ref[0, :, at] = total_re.astype(jnp.bfloat16)
        m_ref[1, :, at] = total_im.astype(jnp.bfloat16)


def mix(place, odd, *arrays):
    vmem = pl.BlockSpec(memory_space=pltpu.VMEM)
    smem = pl.BlockSpec(memory_space=pltpu.SMEM)
    points = jax.ShapeDtypeStruct((2, BLOCK, NB), jnp.bfloat16)
    return pl.pallas_call(
        mix_body,
        out_shape=[jax.ShapeDtypeStruct((2, BLOCK, BLOCK), jnp.bfloat16), points, points],
        in_specs=[smem, smem] + [vmem] * len(arrays),
        out_specs=[vmem] * 3,
        scratch_shapes=[pltpu.VMEM((2, BLOCK, NB), jnp.bfloat16)] * 2,
        compiler_params=pltpu.CompilerParams(vmem_limit_bytes=VMEM),
        name="mix",
    )(place, odd, *arrays)


def halves(value):
    high = value.astype(jnp.bfloat16)
    return high, (value - high.astype(jnp.float32)).astype(jnp.bfloat16)


def project_body(m_ref, row_ref, col_ref, out_ref, x_ref):
    mid = ((1,), (0,))
    first = ((0,), (0,))
    m_re, m_im = m_ref[0], m_ref[1]
    c_re, c_im = col_ref[0], col_ref[1]
    y_re = halves(dot(m_re, c_re, mid) - dot(m_im, c_im, mid))
    y_im = halves(dot(m_re, c_im, mid) + dot(m_im, c_re, mid))
    r_re, r_im = row_ref[0], row_ref[1]

    def meet(a, pair):
        return dot(a, pair[0], first) + dot(a, pair[1], first)

    x_re = -(meet(r_re, y_re) + meet(r_im, y_im))
    x_im = meet(r_im, y_re) - meet(r_re, y_im)
    gap = jnp.zeros((NB, 64 - (NB - WHOLE)), jnp.float32)
    x_ref[pl.ds(NB, 8), :] = jnp.zeros((8, LANES), jnp.float32)
    x_ref[pl.ds(0, NB), pl.ds(0, WHOLE)] = x_re[:, :WHOLE]
    x_ref[pl.ds(0, NB), pl.ds(WHOLE, WHOLE)] = x_im[:, :WHOLE]
    x_ref[pl.ds(0, NB), pl.ds(2 * WHOLE, 128)] = jnp.concatenate(
        [x_re[:, WHOLE:], gap, x_im[:, WHOLE:], gap], axis=1
    )
    for d in range(GROUPS * NZ):
        out_ref[d] = x_ref[pl.ds(27 * d // 4, 8), :].astype(jnp.bfloat16)


def project(m, rows, cols):
    vmem = pl.BlockSpec(memory_space=pltpu.VMEM)
    return pl.pallas_call(
        project_body,
        out_shape=jax.ShapeDtypeStruct((GROUPS * NZ, 8, LANES), jnp.bfloat16),
        in_specs=[vmem] * 3,
        out_specs=vmem,
        scratch_shapes=[pltpu.VMEM((NB + 8, LANES), jnp.float32)],
        compiler_params=pltpu.CompilerParams(vmem_limit_bytes=VMEM),
        name="project",
    )(m, rows, cols)


def reduce_windows(windows):
    parts = lax.all_to_all(windows, "band", 0, 0)
    total = jnp.sum(parts.astype(jnp.float32), axis=0)
    tail = 2 * WHOLE
    rest = NB - WHOLE
    real = jnp.concatenate([total[:, :WHOLE], total[:, tail : tail + rest]], axis=1)
    imag = jnp.concatenate([total[:, WHOLE:tail], total[:, tail + 64 : tail + 64 + rest]], axis=1)
    return jnp.stack([real, imag])


def on_device(orbitals, kernels, pair_kdiff, stored_kernel_index):
    group = lax.axis_index("kgrp")
    band = lax.axis_index("band")
    y, x, z = band // (NX * NZ), band // NZ % NX, band % NZ
    odd = (group % 2).reshape(1)

    own = orbitals[0]
    diff_core = swap_groups(pair_kdiff, 1)
    diff_far = swap_groups(pair_kdiff, 2)
    far = swap_groups(own, 2)

    over_yx = [[g * NZ + z_at for g in range(GROUPS)] for z_at in range(NZ)]
    over_z = [[g * NZ + z_at for z_at in range(NZ)] for g in range(GROUPS)]
    sends = pack(odd, pair_kdiff, diff_core, diff_far, stored_kernel_index, kernels)
    kern = lax.all_to_all(sends, "band", 0, 0, axis_index_groups=over_yx)
    half = swap_groups(kern[:, 0], 1)

    both = jnp.stack([own, far])
    gathered = lax.all_gather(both, "band", axis_index_groups=over_z)
    up, down = shift(both, 1, 0, 0), shift(both, -1, 0, 0)
    over = jnp.stack([shift(up[0], 1, 0, 0), shift(down[1], -1, 0, 0)])
    near = jnp.stack([both, up, over, down])
    own_side = shift(near[:, 0], 0, 1, 0)
    far_side = other_side(near[:, 0])

    place = jnp.stack([(y - dy) % NY * NX + (x - dx) % NX for dy, dx in OFFSETS])
    m_out, own_rows, own_cols = mix(place, odd, near, own_side, far_side, gathered, kern, half)
    m_own = swap_groups(m_out, 1)
    total = reduce_windows(project(m_own, own_rows, own_cols))
    flat = total.reshape(2, 8 * NB)
    flat = lax.dynamic_slice(flat, (0, band * 27 % 4 * 108), (2, 27 * 108))
    return flat[None]


def solution(mesh):
    return jax.shard_map(
        on_device,
        mesh=mesh,
        in_specs=(P("kgrp", None, "band", None), P(None, None, "band", None), P("kgrp"), P()),
        out_specs=P("kgrp", None, "band"),
        check_vma=False,
    )
```

time: 152 us -> 142 us (0.934)
  starting transfers between devices: 32.2 us -> 26.2 us
  waiting for transfers between devices: 70.7 us -> 76.4 us
  local copies, waits for them, and re-layouts: 8.94 us -> 4.04 us
  other arithmetic: 5.95 us -> 2.73 us
  between operations: 16.2 us -> 14.2 us
    ppermute x0 -> x1, waiting for transfers between devices: none -> 12.6 us  [other_side(): return lax.ppermute(block, ('kgrp', 'band'), both)]
    ppermute x5, waiting for transfers between devices: 33.5 us -> 26.7 us  [shift(): return lax.ppermute(block, 'band', band_route(dy, dx, dz))]
    all_to_all x2 -> x1, starting transfers between devices: 12.1 us -> 6.07 us  [on_device(): kern = lax.all_to_all(sends, 'band', 0, 0, axis_index_groups=over_yx)]
    squeeze x4, local copies, waits for them, and re-layouts: 3.82 us -> 1.06 us  [the longest x1 1 us: on_device(): own_side = shift(near[:, 0], 0, 1, 0)]
    another operation x4 -> x3, other arithmetic: 4.2 us -> 1.83 us  [on_device(): near = jnp.stack([both, up, over, down])]
    ppermute x4 -> x5, starting transfers between devices: 2.9 us -> 3.09 us  [swap_groups(): return lax.ppermute(block, 'kgrp', [(k, k ^ bit) for k in range(4)])]
    ppermute x4 -> x5, waiting for transfers between devices: 11.6 us -> 11.6 us  [swap_groups(): return lax.ppermute(block, 'kgrp', [(k, k ^ bit) for k in range(4)])]
  transfers between devices with their start and end apart: 13 -> 14, of which waited for: 7 -> 8; matrix products, arithmetic and copies ran while one was open for 7% -> 2% of each run, Pallas kernels for 2% -> 3%
where the time goes in v4:
time: 142 us; the launch traced here: 141 us
  waiting for transfers between devices  76.4 us (54%)
  starting transfers between devices  26.2 us (18%)
  Pallas kernels  17.1 us (12%)
  between operations  14.2 us (10%)
  local copies, waits for them, and re-layouts  4.04 us (3%)
  other arithmetic  2.73 us (2%)
    ppermute x5, waiting for transfers between devices, shift(): return lax.ppermute(block, 'band', band_route(dy, dx, dz))  26.7 us
    all_to_all x1, waiting for transfers between devices, reduce_windows(): parts = lax.all_to_all(windows, 'band', 0, 0)  25.5 us
    ppermute x1, waiting for transfers between devices, other_side(): return lax.ppermute(block, ('kgrp', 'band'), both)  12.6 us
    ppermute x5, waiting for transfers between devices, swap_groups(): return lax.ppermute(block, 'kgrp', [(k, k ^ bit) for k in range(4)])  11.6 us
    all_to_all x1, starting transfers between devices, reduce_windows(): parts = lax.all_to_all(windows, 'band', 0, 0)  10.9 us
    pallas_call x1, Pallas kernels, mix(): pl.pallas_call(mix_body, out_shape=[jax.ShapeDtypeStruct((2, BLOCK, BLOCK...  6.43 us
    pallas_call x1, Pallas kernels, project(): pl.pallas_call(project_body, out_shape=jax.ShapeDtypeStruct((GROUPS * NZ,...  6.15 us
    all_to_all x1, starting transfers between devices, on_device(): kern = lax.all_to_all(sends, 'band', 0, 0, axis_index_groups=over_yx)  6.07 us
  transfers between devices with their start and end apart: 14, of which 8 were waited for; matrix products, arithmetic and copies ran while one was open for 2% of the time, Pallas kernels for 3%

profile of v4, /device:TPU:6, one launch (start us, length us, event | category | flops | bytes accessed | tf_op | source)
XLA Modules:
  0.0 140.7 jit_solution(17327247806199694784)
XLA Ops:
  6.5 1.4 collective-permute-start
  7.9 5.5 %collective-permute-done = bf16[2,64,432]{2,1,0:T(8,128)(2,1)S(1)} collective-permute-done((bf16[2,64,432]{2,1,0:T(8,128)(2,1)}, bf16[2,64,432]{2,1,0:T(8,128)(2,1)S(1)}, u32[]{:S(2)}, u32[]{:S(2)}) %collective-permute-start) | collective-permute-done | bytes 110624 | tf_op jit(solution)/shard_map/ppermute | solution.py:38
  13.5 1.6 %fusion.2 = (bf16[1,2,2,64,432]{4,3,2,0,1:T(8,128)(2,1)S(1)}, bf16[2,2,64,432]{3,2,1,0:T(8,128)(2,1)}) fusion(bf16[1,2,64,432]{3,2,1,0:T(8,128)(2,1)S(1)} %bitcast.44, bf16[1,2,64,432]{3,2,1,0:T(8,128)(2,1)} %param.4), kind=kLoop, calls=%fused_computation.14 | loop fusion | flops 110592 | bytes 663552 | tf_op jit(solution)/shard_map/stack | solution.py:217
  15.2 0.1 collective-permute-start.7
  15.3 1.5 %collective-permute-start.8 = (s32[1]{0:T(128)}, s32[1]{0:T(128)}, u32[]{:S(2)}, u32[]{:S(2)}) collective-permute-start(s32[1]{0:T(128)} %param.6), channel_id=1, source_target_pairs={{0,128},{64,192},{128,0},{192,64},{1,129},{65,193},{129,1},{193,65... | collective-permute-start | bytes 20 | tf_op jit(solution)/shard_map/ppermute | solution.py:38
  17.4 3.2 %collective-permute-done.8.far_ref = s32[1]{0:T(128)} collective-permute-done((s32[1]{0:T(128)}, s32[1]{0:T(128)}, u32[]{:S(2)}, u32[]{:S(2)}) %collective-permute-start.8) | collective-permute-done | bytes 36 | tf_op jit(solution)/shard_map/ppermute | solution.py:38
  20.6 4.5 %pack.1 = bf16[8,3,64,512]{3,2,1,0:T(8,128)(2,1)} custom-call(s32[1]{0:T(128)} %bitcast.8.odd_ref, s32[1]{0:T(128)S(6)} %copy.17.own_ref, s32[1]{0:T(128)} %collective-permute-done.7.core_ref, s32[1]{0:T(128)} %collective-permute-done.8.far_ref, s32[8]{0:T(128)} %stored_ref.1, bf16[4,2,64,4096]{3,2,1,0:T(8,128)(2,1)} %kernels_ref.1), custom_call_target="tpu_custom_call" | custom-call | tf_op jit(solution)/shard_map/pack/pallas_call | solution.py:71
  25.1 6.1 %all-to-all-start = ((bf16[8,3,64,512]{3,2,1,0:T(8,128)(2,1)}), bf16[8,3,64,512]{3,2,1,0:T(8,128)(2,1)S(1)}, u32[]{:S(2)}, u32[]{:S(2)}) async-start(bf16[8,3,64,512]{3,2,1,0:T(8,128)(2,1)} %pack.1), calls=%async_computation | async-start | bytes 3145728 | tf_op jit(solution)/shard_map/all_to_all | solution.py:210
  31.2 2.7 %collective-permute-start.3 = (bf16[2,2,64,432]{3,2,1,0:T(8,128)(2,1)S(1)}, bf16[2,2,64,432]{3,2,1,0:T(8,128)(2,1)S(1)}, u32[]{:S(2)}, u32[]{:S(2)}) collective-permute-start(bf16[2,2,64,432]{3,2,1,0:T(8,128)(2,1)S(1)} %copy-done.1), channel_id=1, source_target_pairs={{0,48},{1,49},{2,50},{3,51},{4,52},{5,53},{6,54},{7,55},{8,56},{9,... | collective-permute-start | bytes 663560 | tf_op jit(solution)/shard_map/ppermute | solution.py:34
  33.9 20.9 %collective-permute-done.3 = bf16[2,2,64,432]{3,2,1,0:T(8,128)(2,1)S(1)} collective-permute-done((bf16[2,2,64,432]{3,2,1,0:T(8,128)(2,1)S(1)}, bf16[2,2,64,432]{3,2,1,0:T(8,128)(2,1)S(1)}, u32[]{:S(2)}, u32[]{:S(2)}) %collective-permute-start.3) | collective-permute-done | bytes 221216 | tf_op jit(solution)/shard_map/ppermute | solution.py:34
  54.8 1.6 %collective-permute-start.4 = (bf16[2,64,432]{2,1,0:T(8,128)(2,1)S(1)}, bf16[2,64,432]{2,1,0:T(8,128)(2,1)S(1)}, u32[]{:S(2)}, u32[]{:S(2)}) collective-permute-start(bf16[2,64,432]{2,1,0:T(8,128)(2,1)S(1)} %slice_bitcast_fusion.2), channel_id=1, source_target_pairs={{0,48},{1,49},{2,50},{3,51},{4,52},{5,53},{6,54},{7,55},{8,56},{9,... | collective-permute-start | bytes 331784 | tf_op jit(solution)/shard_map/ppermute | solution.py:34
  56.4 0.6 collective-permute-start.2
  57.0 3.4 %collective-permute-done.4 = bf16[2,64,432]{2,1,0:T(8,128)(2,1)S(1)} collective-permute-done((bf16[2,64,432]{2,1,0:T(8,128)(2,1)S(1)}, bf16[2,64,432]{2,1,0:T(8,128)(2,1)S(1)}, u32[]{:S(2)}, u32[]{:S(2)}) %collective-permute-start.4) | collective-permute-done | bytes 110624 | tf_op jit(solution)/shard_map/ppermute | solution.py:34
  60.4 2.4 %collective-permute-done.2 = bf16[2,64,432]{2,1,0:T(8,128)(2,1)S(1)} collective-permute-done((bf16[2,64,432]{2,1,0:T(8,128)(2,1)S(1)}, bf16[2,64,432]{2,1,0:T(8,128)(2,1)S(1)}, u32[]{:S(2)}, u32[]{:S(2)}) %collective-permute-start.2) | collective-permute-done | bytes 110624 | tf_op jit(solution)/shard_map/ppermute | solution.py:34
  62.8 0.2 pad_maximum_fusion
  63.1 0.1 collective-permute-start.9
  63.2 1.0 slice_bitcast_fusion.1
  64.2 0.3 collective-permute-start.6
  64.5 1.0 collective-permute-start.5
  65.5 0.6 stack.74.place_ref
  66.2 1.1 copy.15.refs_0_
  67.2 12.6 %collective-permute-done.6.refs_2_ = bf16[4,2,64,432]{3,2,1,0:T(8,128)(2,1)} collective-permute-done((bf16[4,2,64,432]{3,2,1,0:T(8,128)(2,1)}, bf16[4,2,64,432]{3,2,1,0:T(8,128)(2,1)}, u32[]{:S(2)}, u32[]{:S(2)}) %collective-permute-start.6) | collective-permute-done | bytes 442400 | tf_op jit(solution)/shard_map/ppermute | solution.py:44
  79.9 6.4 %mix.1 = (bf16[2,512,512]{2,1,0:T(8,128)(2,1)}, bf16[2,512,432]{2,1,0:T(8,128)(2,1)}, bf16[2,512,432]{2,1,0:T(8,128)(2,1)}) custom-call(s32[8]{0:T(128)} %stack.74.place_ref, s32[1]{0:T(128)} %bitcast.8.odd_ref, bf16[4,2,2,64,432]{4,3,2,1,0:T(8,128)(2,1)} %copy.15.refs_0_, bf16[4,2,64,432]{3,2,1,0:T(8,128)(2,1)} %collective-permute-done.5.refs_1_, ...), custom_call_target="tpu_custom_call" | custom-call | tf_op jit(solution)/shard_map/mix/pallas_call | solution.py:132
  86.3 2.9 %collective-permute-done.10.m_ref = bf16[2,512,512]{2,1,0:T(8,128)(2,1)S(1)} collective-permute-done((bf16[2,512,512]{2,1,0:T(8,128)(2,1)}, bf16[2,512,512]{2,1,0:T(8,128)(2,1)S(1)}, u32[]{:S(2)}, u32[]{:S(2)}) %collective-permute-start.10) | collective-permute-done | bytes 1048608 | tf_op jit(solution)/shard_map/ppermute | solution.py:38
  89.2 1.0 copy-done.2
  90.2 6.1 %project.1 = bf16[64,8,896]{2,1,0:T(8,128)(2,1)} custom-call(bf16[2,512,512]{2,1,0:T(8,128)(2,1)} %copy-done.2, bf16[2,512,432]{2,1,0:T(8,128)(2,1)} %get-tuple-element.9.row_ref, bf16[2,512,432]{2,1,0:T(8,128)(2,1)} %get-tuple-element.10.col_ref), custom_call_target="tpu_custom_call" | custom-call | tf_op jit(solution)/shard_map/project/pallas_call | solution.py:175
  96.3 10.9 %all-to-all-start.1 = ((bf16[64,8,896]{2,1,0:T(8,128)(2,1)}), bf16[64,8,896]{2,1,0:T(8,128)(2,1)S(1)}, u32[]{:S(2)}, u32[]{:S(2)}) async-start(bf16[64,8,896]{2,1,0:T(8,128)(2,1)} %project.1), calls=%async_computation.1 | async-start | bytes 1835008 | tf_op jit(solution)/shard_map/all_to_all | solution.py:187
  107.2 25.5 %all-to-all-done.1 = bf16[64,8,896]{2,1,0:T(8,128)(2,1)S(1)} async-done(((bf16[64,8,896]{2,1,0:T(8,128)(2,1)}), bf16[64,8,896]{2,1,0:T(8,128)(2,1)S(1)}, u32[]{:S(2)}, u32[]{:S(2)}) %all-to-all-start.1) | async-done | bytes 917536 | tf_op jit(solution)/shard_map/all_to_all | solution.py:187
  132.7 0.2 convert_reduce_fusion
  132.9 0.1 stack.85
  133.0 0.1 stack.86
  133.1 0.7 fusion.1
  (22 shorter events, 0.2 us)
Async XLA Ops:
  6.5 73.3 %all-gather.3.cloned.1.call-start = ((), (), s32[]{:S(2)}) async-start(), calls=%async_computation.2 | async-start | bytes 2359296 | tf_op jit(solution)/shard_map/all_gather | solution.py:214
  6.5 7.0 %collective-permute-start = (bf16[2,64,432]{2,1,0:T(8,128)(2,1)}, bf16[2,64,432]{2,1,0:T(8,128)(2,1)S(1)}, u32[]{:S(2)}, u32[]{:S(2)}) collective-permute-start(bf16[2,64,432]{2,1,0:T(8,128)(2,1)} %bitcast.41), channel_id=1, source_target_pairs={{0,128},{64,192},{128,0},{192,64},{1,129},{65,193},{129,1},{193,65... | collective-permute-start | bytes 331784 | tf_op jit(solution)/shard_map/ppermute | solution.py:38
  15.2 2.3 %collective-permute-start.7 = (s32[1]{0:T(128)}, s32[1]{0:T(128)}, u32[]{:S(2)}, u32[]{:S(2)}) collective-permute-start(s32[1]{0:T(128)} %param.6), channel_id=1, source_target_pairs={{0,64},{64,0},{128,192},{192,128},{1,65},{65,1},{129,193},{193,129... | collective-permute-start | bytes 20 | tf_op jit(solution)/shard_map/ppermute | solution.py:38
  15.3 5.4 %collective-permute-start.8 = (s32[1]{0:T(128)}, s32[1]{0:T(128)}, u32[]{:S(2)}, u32[]{:S(2)}) collective-permute-start(s32[1]{0:T(128)} %param.6), channel_id=1, source_target_pairs={{0,128},{64,192},{128,0},{192,64},{1,129},{65,193},{129,1},{193,65... | collective-permute-start | bytes 20 | tf_op jit(solution)/shard_map/ppermute | solution.py:38
  25.1 6.1 %copy-start.1 = (bf16[2,2,64,432]{3,2,1,0:T(8,128)(2,1)S(1)}, bf16[2,2,64,432]{3,2,1,0:T(8,128)(2,1)}, u32[]{:S(2)}) copy-start(bf16[2,2,64,432]{3,2,1,0:T(8,128)(2,1)} %get-tuple-element.12) | copy-start | bytes 663556
  25.1 37.9 %all-to-all-start = ((bf16[8,3,64,512]{3,2,1,0:T(8,128)(2,1)}), bf16[8,3,64,512]{3,2,1,0:T(8,128)(2,1)S(1)}, u32[]{:S(2)}, u32[]{:S(2)}) async-start(bf16[8,3,64,512]{3,2,1,0:T(8,128)(2,1)} %pack.1), calls=%async_computation | async-start | bytes 3145728 | tf_op jit(solution)/shard_map/all_to_all | solution.py:210
  31.2 23.6 %collective-permute-start.3 = (bf16[2,2,64,432]{3,2,1,0:T(8,128)(2,1)S(1)}, bf16[2,2,64,432]{3,2,1,0:T(8,128)(2,1)S(1)}, u32[]{:S(2)}, u32[]{:S(2)}) collective-permute-start(bf16[2,2,64,432]{3,2,1,0:T(8,128)(2,1)S(1)} %copy-done.1), channel_id=1, source_target_pairs={{0,48},{1,49},{2,50},{3,51},{4,52},{5,53},{6,54},{7,55},{8,56},{9,... | collective-permute-start | bytes 663560 | tf_op jit(solution)/shard_map/ppermute | solution.py:34
  33.9 22.5 %collective-permute-start.1 = (bf16[2,2,64,432]{3,2,1,0:T(8,128)(2,1)S(1)}, bf16[2,2,64,432]{3,2,1,0:T(8,128)(2,1)S(1)}, u32[]{:S(2)}, u32[]{:S(2)}) collective-permute-start(bf16[2,2,64,432]{3,2,1,0:T(8,128)(2,1)S(1)} %copy-done.1), channel_id=1, source_target_pairs={{0,16},{1,17},{2,18},{3,19},{4,20},{5,21},{6,22},{7,23},{8,24},{9,... | collective-permute-start | bytes 663560 | tf_op jit(solution)/shard_map/ppermute | solution.py:34
  54.8 5.6 %collective-permute-start.4 = (bf16[2,64,432]{2,1,0:T(8,128)(2,1)S(1)}, bf16[2,64,432]{2,1,0:T(8,128)(2,1)S(1)}, u32[]{:S(2)}, u32[]{:S(2)}) collective-permute-start(bf16[2,64,432]{2,1,0:T(8,128)(2,1)S(1)} %slice_bitcast_fusion.2), channel_id=1, source_target_pairs={{0,48},{1,49},{2,50},{3,51},{4,52},{5,53},{6,54},{7,55},{8,56},{9,... | collective-permute-start | bytes 331784 | tf_op jit(solution)/shard_map/ppermute | solution.py:34
  56.4 6.4 %collective-permute-start.2 = (bf16[2,64,432]{2,1,0:T(8,128)(2,1)S(1)}, bf16[2,64,432]{2,1,0:T(8,128)(2,1)S(1)}, u32[]{:S(2)}, u32[]{:S(2)}) collective-permute-start(bf16[2,64,432]{2,1,0:T(8,128)(2,1)S(1)} %slice_bitcast_fusion.3), channel_id=1, source_target_pairs={{0,16},{1,17},{2,18},{3,19},{4,20},{5,21},{6,22},{7,23},{8,24},{9,... | collective-permute-start | bytes 331784 | tf_op jit(solution)/shard_map/ppermute | solution.py:34
  63.0 4.2 %copy-start = (bf16[8,3,64,512]{3,2,1,0:T(8,128)(2,1)}, bf16[8,3,64,512]{3,2,1,0:T(8,128)(2,1)S(1)}, u32[]{:S(2)}) copy-start(bf16[8,3,64,512]{3,2,1,0:T(8,128)(2,1)S(1)} %all-to-all-done.refs_4_) | copy-start | bytes 4718596
  63.1 16.8 %collective-permute-start.9 = (bf16[8,64,512]{2,1,0:T(8,128)(2,1)S(1)}, bf16[8,64,512]{2,1,0:T(8,128)(2,1)}, u32[]{:S(2)}, u32[]{:S(2)}) collective-permute-start(bf16[8,64,512]{2,1,0:T(8,128)(2,1)S(1)} %slice_bitcast_fusion), channel_id=1, source_target_pairs={{0,64},{64,0},{128,192},{192,128},{1,65},{65,1},{129,193},{193,129... | collective-permute-start | bytes 1572872 | tf_op jit(solution)/shard_map/ppermute | solution.py:38
  64.2 15.7 %collective-permute-start.6 = (bf16[4,2,64,432]{3,2,1,0:T(8,128)(2,1)}, bf16[4,2,64,432]{3,2,1,0:T(8,128)(2,1)}, u32[]{:S(2)}, u32[]{:S(2)}) collective-permute-start(bf16[4,2,64,432]{3,2,1,0:T(8,128)(2,1)} %slice_bitcast_fusion.1), channel_id=1, source_target_pairs={{128,8},{129,9},{130,10},{131,11},{132,12},{133,13},{134,14},{135,... | collective-permute-start | bytes 1327112 | tf_op jit(solution)/shard_map/ppermute | solution.py:44
  64.5 15.3 %collective-permute-start.5 = (bf16[4,2,64,432]{3,2,1,0:T(8,128)(2,1)}, bf16[4,2,64,432]{3,2,1,0:T(8,128)(2,1)}, u32[]{:S(2)}, u32[]{:S(2)}) collective-permute-start(bf16[4,2,64,432]{3,2,1,0:T(8,128)(2,1)} %slice_bitcast_fusion.1), channel_id=1, source_target_pairs={{0,8},{1,9},{2,10},{3,11},{4,12},{5,13},{6,14},{7,15},{8,0},{9,1},... | collective-permute-start | bytes 1327112 | tf_op jit(solution)/shard_map/ppermute | solution.py:34
  86.3 2.9 %collective-permute-start.10 = (bf16[2,512,512]{2,1,0:T(8,128)(2,1)}, bf16[2,512,512]{2,1,0:T(8,128)(2,1)S(1)}, u32[]{:S(2)}, u32[]{:S(2)}) collective-permute-start(bf16[2,512,512]{2,1,0:T(8,128)(2,1)} %get-tuple-element.8), channel_id=1, source_target_pairs={{0,64},{64,0},{128,192},{192,128},{1,65},{65,1},{129,193},{193,129... | collective-permute-start | bytes 3145736 | tf_op jit(solution)/shard_map/ppermute | solution.py:38
  89.2 1.0 copy-start.2
  96.3 36.4 %all-to-all-start.1 = ((bf16[64,8,896]{2,1,0:T(8,128)(2,1)}), bf16[64,8,896]{2,1,0:T(8,128)(2,1)S(1)}, u32[]{:S(2)}, u32[]{:S(2)}) async-start(bf16[64,8,896]{2,1,0:T(8,128)(2,1)} %project.1), calls=%async_computation.1 | async-start | bytes 1835008 | tf_op jit(solution)/shard_map/all_to_all | solution.py:187
Sparse Core Ops, SparseCore 0:
  15.3 44.0 all-gather.2

commit v5 on v4

--- a/solution.py
+++ b/solution.py
@@ -207,13 +207,13 @@
     over_yx = [[g * NZ + z_at for g in range(GROUPS)] for z_at in range(NZ)]
     over_z = [[g * NZ + z_at for z_at in range(NZ)] for g in range(GROUPS)]
     sends = pack(odd, pair_kdiff, diff_core, diff_far, stored_kernel_index, kernels)
-    kern = lax.all_to_all(sends, "band", 0, 0, axis_index_groups=over_yx)
-    half = swap_groups(kern[:, 0], 1)
-
     both = jnp.stack([own, far])
     gathered = lax.all_gather(both, "band", axis_index_groups=over_z)
     up, down = shift(both, 1, 0, 0), shift(both, -1, 0, 0)
-    over = jnp.stack([shift(up[0], 1, 0, 0), shift(down[1], -1, 0, 0)])
+    sends, up, down = lax.optimization_barrier((sends, up, down))
+    kern = lax.all_to_all(sends, "band", 0, 0, axis_index_groups=over_yx)
+    half = swap_groups(kern[:, 0], 1)
+    over = shift(down, -1, 0, 0)
     near = jnp.stack([both, up, over, down])
     own_side = shift(near[:, 0], 0, 1, 0)
     far_side = other_side(near[:, 0])

time: 142 us -> 139 us (0.979)
  waiting for transfers between devices: 76.4 us -> 70.5 us
  starting transfers between devices: 26.2 us -> 28.9 us
    ppermute x5 -> x4, waiting for transfers between devices: 26.7 us -> 21.3 us  [shift(): return lax.ppermute(block, 'band', band_route(dy, dx, dz))]
    all_to_all x1, starting transfers between devices: 10.9 us -> 12.6 us  [reduce_windows(): parts = lax.all_to_all(windows, 'band', 0, 0)]
    ppermute x5 -> x4, starting transfers between devices: 5.89 us -> 6.77 us  [shift(): return lax.ppermute(block, 'band', band_route(dy, dx, dz))]
  transfers between devices with their start and end apart: 14 -> 13, of which waited for: 8 -> 6; matrix products, arithmetic and copies ran while one was open for 2% -> 2% of each run, Pallas kernels for 3% -> 3%
where the time goes in v5:
time: 139 us; the launch traced here: 137 us
  waiting for transfers between devices  70.5 us (51%)
  starting transfers between devices  28.9 us (21%)
  Pallas kernels  17.1 us (12%)
  between operations  14.2 us (10%)
  local copies, waits for them, and re-layouts  4.02 us (3%)
  other arithmetic  2.7 us (2%)
    all_to_all x1, waiting for transfers between devices, reduce_windows(): parts = lax.all_to_all(windows, 'band', 0, 0)  25.5 us
    ppermute x4, waiting for transfers between devices, shift(): return lax.ppermute(block, 'band', band_route(dy, dx, dz))  21.3 us
    all_to_all x1, starting transfers between devices, reduce_windows(): parts = lax.all_to_all(windows, 'band', 0, 0)  12.6 us
    ppermute x1, waiting for transfers between devices, other_side(): return lax.ppermute(block, ('kgrp', 'band'), both)  12.3 us
    ppermute x5, waiting for transfers between devices, swap_groups(): return lax.ppermute(block, 'kgrp', [(k, k ^ bit) for k in range(4)])  11.4 us
    ppermute x4, starting transfers between devices, shift(): return lax.ppermute(block, 'band', band_route(dy, dx, dz))  6.77 us
    pallas_call x1, Pallas kernels, mix(): pl.pallas_call(mix_body, out_shape=[jax.ShapeDtypeStruct((2, BLOCK, BLOCK...  6.44 us
    pallas_call x1, Pallas kernels, project(): pl.pallas_call(project_body, out_shape=jax.ShapeDtypeStruct((GROUPS * NZ,...  6.15 us
  transfers between devices with their start and end apart: 13, of which 6 were waited for; matrix products, arithmetic and copies ran while one was open for 2% of the time, Pallas kernels for 3%

profile of v5, /device:TPU:6, one launch (start us, length us, event | category | flops | bytes accessed | tf_op | source)
XLA Modules:
  0.0 137.5 jit_solution(4256130734680185495)
XLA Ops:
  6.5 1.4 %collective-permute-start = (bf16[2,64,432]{2,1,0:T(8,128)(2,1)}, bf16[2,64,432]{2,1,0:T(8,128)(2,1)S(1)}, u32[]{:S(2)}, u32[]{:S(2)}) collective-permute-start(bf16[2,64,432]{2,1,0:T(8,128)(2,1)} %bitcast.35), channel_id=1, source_target_pairs={{0,128},{64,192},{128,0},{192,64},{1,129},{65,193},{129,1},{193,65... | collective-permute-start | bytes 331784 | tf_op jit(solution)/shard_map/ppermute | solution.py:38
  7.9 5.5 %collective-permute-done = bf16[2,64,432]{2,1,0:T(8,128)(2,1)S(1)} collective-permute-done((bf16[2,64,432]{2,1,0:T(8,128)(2,1)}, bf16[2,64,432]{2,1,0:T(8,128)(2,1)S(1)}, u32[]{:S(2)}, u32[]{:S(2)}) %collective-permute-start) | collective-permute-done | bytes 110624 | tf_op jit(solution)/shard_map/ppermute | solution.py:38
  13.5 1.6 %fusion.2 = (bf16[1,2,2,64,432]{4,3,2,0,1:T(8,128)(2,1)S(1)}, bf16[2,2,64,432]{3,2,1,0:T(8,128)(2,1)}) fusion(bf16[1,2,64,432]{3,2,1,0:T(8,128)(2,1)S(1)} %bitcast.36, bf16[1,2,64,432]{3,2,1,0:T(8,128)(2,1)} %param.4), kind=kLoop, calls=%fused_computation.11 | loop fusion | flops 110592 | bytes 663552 | tf_op jit(solution)/shard_map/stack | solution.py:217
  15.1 0.0 all-gather.3.cloned.1.call-update
  15.2 3.1 %collective-permute-start.4 = (bf16[2,2,64,432]{3,2,1,0:T(8,128)(2,1)}, bf16[2,2,64,432]{3,2,1,0:T(8,128)(2,1)S(1)}, u32[]{:S(2)}, u32[]{:S(2)}) collective-permute-start(bf16[2,2,64,432]{3,2,1,0:T(8,128)(2,1)} %get-tuple-element.18), channel_id=1, source_target_pairs={{0,48},{1,49},{2,50},{3,51},{4,52},{5,53},{6,54},{7,55},{8,56},{9,... | collective-permute-start | bytes 663560 | tf_op jit(solution)/shard_map/ppermute | solution.py:34
  18.3 1.4 %collective-permute-start.2 = (s32[1]{0:T(128)}, s32[1]{0:T(128)}, u32[]{:S(2)}, u32[]{:S(2)}) collective-permute-start(s32[1]{0:T(128)} %param.6), channel_id=1, source_target_pairs={{0,128},{64,192},{128,0},{192,64},{1,129},{65,193},{129,1},{193,65... | collective-permute-start | bytes 20 | tf_op jit(solution)/shard_map/ppermute | solution.py:38
  20.4 0.0 collective-permute-done.1.core_ref
  20.4 3.0 %collective-permute-done.2.far_ref = s32[1]{0:T(128)} collective-permute-done((s32[1]{0:T(128)}, s32[1]{0:T(128)}, u32[]{:S(2)}, u32[]{:S(2)}) %collective-permute-start.2) | collective-permute-done | bytes 36 | tf_op jit(solution)/shard_map/ppermute | solution.py:38
  23.4 4.5 %pack.1 = bf16[8,3,64,512]{3,2,1,0:T(8,128)(2,1)} custom-call(s32[1]{0:T(128)} %bitcast.8.odd_ref, s32[1]{0:T(128)S(6)} %copy.17.own_ref, s32[1]{0:T(128)} %collective-permute-done.1.core_ref, s32[1]{0:T(128)} %collective-permute-done.2.far_ref, s32[8]{0:T(128)} %stored_ref.1, bf16[4,2,64,4096]{3,2,1,0:T(8,128)(2,1)} %kernels_ref.1), custom_call_target="tpu_custom_call" | custom-call | tf_op jit(solution)/shard_map/pack/pallas_call | solution.py:71
  27.9 6.0 %all-to-all-start = ((bf16[8,3,64,512]{3,2,1,0:T(8,128)(2,1)}), bf16[8,3,64,512]{3,2,1,0:T(8,128)(2,1)S(1)}, u32[]{:S(2)}, u32[]{:S(2)}) async-start(bf16[8,3,64,512]{3,2,1,0:T(8,128)(2,1)} %pack.1), calls=%async_computation | async-start | bytes 3145728 | tf_op jit(solution)/shard_map/all_to_all | solution.py:214
  33.9 2.7 %collective-permute-start.5 = (bf16[2,2,64,432]{3,2,1,0:T(8,128)(2,1)S(1)}, bf16[2,2,64,432]{3,2,1,0:T(8,128)(2,1)S(1)}, u32[]{:S(2)}, u32[]{:S(2)}) collective-permute-start(bf16[2,2,64,432]{3,2,1,0:T(8,128)(2,1)S(1)} %collective-permute-done.4), channel_id=1, source_target_pairs={{0,48},{1,49},{2,50},{3,51},{4,52},{5,53},{6,54},{7,55},{8,56},{9,... | collective-permute-start | bytes 663560 | tf_op jit(solution)/shard_map/ppermute | solution.py:34
  36.6 21.3 %collective-permute-done.5 = bf16[2,2,64,432]{3,2,1,0:T(8,128)(2,1)S(1)} collective-permute-done((bf16[2,2,64,432]{3,2,1,0:T(8,128)(2,1)S(1)}, bf16[2,2,64,432]{3,2,1,0:T(8,128)(2,1)S(1)}, u32[]{:S(2)}, u32[]{:S(2)}) %collective-permute-start.5) | collective-permute-done | bytes 221216 | tf_op jit(solution)/shard_map/ppermute | solution.py:34
  57.9 0.2 pad_maximum_fusion
  58.1 0.2 collective-permute-start.8
  58.3 1.0 slice_bitcast_fusion.1
  59.3 0.5 collective-permute-start.7
  59.9 1.0 collective-permute-start.6
  60.9 0.6 stack.65.place_ref
  61.5 1.1 copy.15.refs_0_
  62.6 12.3 %collective-permute-done.7.refs_2_ = bf16[4,2,64,432]{3,2,1,0:T(8,128)(2,1)} collective-permute-done((bf16[4,2,64,432]{3,2,1,0:T(8,128)(2,1)}, bf16[4,2,64,432]{3,2,1,0:T(8,128)(2,1)}, u32[]{:S(2)}, u32[]{:S(2)}) %collective-permute-start.7) | collective-permute-done | bytes 442400 | tf_op jit(solution)/shard_map/ppermute | solution.py:44
  74.9 0.0 all-gather.3.cloned.1.call-done
  74.9 6.4 %mix.1 = (bf16[2,512,512]{2,1,0:T(8,128)(2,1)}, bf16[2,512,432]{2,1,0:T(8,128)(2,1)}, bf16[2,512,432]{2,1,0:T(8,128)(2,1)}) custom-call(s32[8]{0:T(128)} %stack.65.place_ref, s32[1]{0:T(128)} %bitcast.8.odd_ref, bf16[4,2,2,64,432]{4,3,2,1,0:T(8,128)(2,1)} %copy.15.refs_0_, bf16[4,2,64,432]{3,2,1,0:T(8,128)(2,1)} %collective-permute-done.6.refs_1_, ...), custom_call_target="tpu_custom_call" | custom-call | tf_op jit(solution)/shard_map/mix/pallas_call | solution.py:132
  81.3 2.9 %collective-permute-done.9.m_ref = bf16[2,512,512]{2,1,0:T(8,128)(2,1)S(1)} collective-permute-done((bf16[2,512,512]{2,1,0:T(8,128)(2,1)}, bf16[2,512,512]{2,1,0:T(8,128)(2,1)S(1)}, u32[]{:S(2)}, u32[]{:S(2)}) %collective-permute-start.9) | collective-permute-done | bytes 1048608 | tf_op jit(solution)/shard_map/ppermute | solution.py:38
  84.2 1.0 copy-done.1
  85.2 6.1 %project.1 = bf16[64,8,896]{2,1,0:T(8,128)(2,1)} custom-call(bf16[2,512,512]{2,1,0:T(8,128)(2,1)} %copy-done.1, bf16[2,512,432]{2,1,0:T(8,128)(2,1)} %get-tuple-element.15.row_ref, bf16[2,512,432]{2,1,0:T(8,128)(2,1)} %get-tuple-element.16.col_ref), custom_call_target="tpu_custom_call" | custom-call | tf_op jit(solution)/shard_map/project/pallas_call | solution.py:175
  91.3 12.6 %all-to-all-start.1 = ((bf16[64,8,896]{2,1,0:T(8,128)(2,1)}), bf16[64,8,896]{2,1,0:T(8,128)(2,1)S(1)}, u32[]{:S(2)}, u32[]{:S(2)}) async-start(bf16[64,8,896]{2,1,0:T(8,128)(2,1)} %project.1), calls=%async_computation.1 | async-start | bytes 1835008 | tf_op jit(solution)/shard_map/all_to_all | solution.py:187
  104.0 25.5 %all-to-all-done.1 = bf16[64,8,896]{2,1,0:T(8,128)(2,1)S(1)} async-done(((bf16[64,8,896]{2,1,0:T(8,128)(2,1)}), bf16[64,8,896]{2,1,0:T(8,128)(2,1)S(1)}, u32[]{:S(2)}, u32[]{:S(2)}) %all-to-all-start.1) | async-done | bytes 917536 | tf_op jit(solution)/shard_map/all_to_all | solution.py:187
  129.5 0.2 convert_reduce_fusion
  129.6 0.1 fusion.4
  129.7 0.1 stack.73
  129.8 0.1 stack.74
  129.9 0.7 fusion.1
  (15 shorter events, 0.1 us)
Async XLA Ops:
  6.5 68.3 %all-gather.3.cloned.1.call-start = ((), (), s32[]{:S(2)}) async-start(), calls=%async_computation.2 | async-start | bytes 2359296 | tf_op jit(solution)/shard_map/all_gather | solution.py:211
  6.5 7.0 %collective-permute-start = (bf16[2,64,432]{2,1,0:T(8,128)(2,1)}, bf16[2,64,432]{2,1,0:T(8,128)(2,1)S(1)}, u32[]{:S(2)}, u32[]{:S(2)}) collective-permute-start(bf16[2,64,432]{2,1,0:T(8,128)(2,1)} %bitcast.35), channel_id=1, source_target_pairs={{0,128},{64,192},{128,0},{192,64},{1,129},{65,193},{129,1},{193,65... | collective-permute-start | bytes 331784 | tf_op jit(solution)/shard_map/ppermute | solution.py:38
  15.2 12.8 %collective-permute-start.4 = (bf16[2,2,64,432]{3,2,1,0:T(8,128)(2,1)}, bf16[2,2,64,432]{3,2,1,0:T(8,128)(2,1)S(1)}, u32[]{:S(2)}, u32[]{:S(2)}) collective-permute-start(bf16[2,2,64,432]{3,2,1,0:T(8,128)(2,1)} %get-tuple-element.18), channel_id=1, source_target_pairs={{0,48},{1,49},{2,50},{3,51},{4,52},{5,53},{6,54},{7,55},{8,56},{9,... | collective-permute-start | bytes 663560 | tf_op jit(solution)/shard_map/ppermute | solution.py:34
  18.3 9.7 %collective-permute-start.3 = (bf16[2,2,64,432]{3,2,1,0:T(8,128)(2,1)}, bf16[2,2,64,432]{3,2,1,0:T(8,128)(2,1)S(1)}, u32[]{:S(2)}, u32[]{:S(2)}) collective-permute-start(bf16[2,2,64,432]{3,2,1,0:T(8,128)(2,1)} %get-tuple-element.18), channel_id=1, source_target_pairs={{0,16},{1,17},{2,18},{3,19},{4,20},{5,21},{6,22},{7,23},{8,24},{9,... | collective-permute-start | bytes 663560 | tf_op jit(solution)/shard_map/ppermute | solution.py:34
  18.3 2.1 %collective-permute-start.1 = (s32[1]{0:T(128)}, s32[1]{0:T(128)}, u32[]{:S(2)}, u32[]{:S(2)}) collective-permute-start(s32[1]{0:T(128)} %param.6), channel_id=1, source_target_pairs={{0,64},{64,0},{128,192},{192,128},{1,65},{65,1},{129,193},{193,129... | collective-permute-start | bytes 20 | tf_op jit(solution)/shard_map/ppermute | solution.py:38
  18.3 5.1 %collective-permute-start.2 = (s32[1]{0:T(128)}, s32[1]{0:T(128)}, u32[]{:S(2)}, u32[]{:S(2)}) collective-permute-start(s32[1]{0:T(128)} %param.6), channel_id=1, source_target_pairs={{0,128},{64,192},{128,0},{192,64},{1,129},{65,193},{129,1},{193,65... | collective-permute-start | bytes 20 | tf_op jit(solution)/shard_map/ppermute | solution.py:38
  27.9 30.1 %all-to-all-start = ((bf16[8,3,64,512]{3,2,1,0:T(8,128)(2,1)}), bf16[8,3,64,512]{3,2,1,0:T(8,128)(2,1)S(1)}, u32[]{:S(2)}, u32[]{:S(2)}) async-start(bf16[8,3,64,512]{3,2,1,0:T(8,128)(2,1)} %pack.1), calls=%async_computation | async-start | bytes 3145728 | tf_op jit(solution)/shard_map/all_to_all | solution.py:214
  33.9 23.9 %collective-permute-start.5 = (bf16[2,2,64,432]{3,2,1,0:T(8,128)(2,1)S(1)}, bf16[2,2,64,432]{3,2,1,0:T(8,128)(2,1)S(1)}, u32[]{:S(2)}, u32[]{:S(2)}) collective-permute-start(bf16[2,2,64,432]{3,2,1,0:T(8,128)(2,1)S(1)} %collective-permute-done.4), channel_id=1, source_target_pairs={{0,48},{1,49},{2,50},{3,51},{4,52},{5,53},{6,54},{7,55},{8,56},{9,... | collective-permute-start | bytes 663560 | tf_op jit(solution)/shard_map/ppermute | solution.py:34
  58.0 4.5 %copy-start = (bf16[8,3,64,512]{3,2,1,0:T(8,128)(2,1)}, bf16[8,3,64,512]{3,2,1,0:T(8,128)(2,1)S(1)}, u32[]{:S(2)}) copy-start(bf16[8,3,64,512]{3,2,1,0:T(8,128)(2,1)S(1)} %all-to-all-done.refs_4_) | copy-start | bytes 4718596
  58.1 16.8 %collective-permute-start.8 = (bf16[8,64,512]{2,1,0:T(8,128)(2,1)S(1)}, bf16[8,64,512]{2,1,0:T(8,128)(2,1)}, u32[]{:S(2)}, u32[]{:S(2)}) collective-permute-start(bf16[8,64,512]{2,1,0:T(8,128)(2,1)S(1)} %slice_bitcast_fusion), channel_id=1, source_target_pairs={{0,64},{64,0},{128,192},{192,128},{1,65},{65,1},{129,193},{193,129... | collective-permute-start | bytes 1572872 | tf_op jit(solution)/shard_map/ppermute | solution.py:38
  59.3 15.5 %collective-permute-start.7 = (bf16[4,2,64,432]{3,2,1,0:T(8,128)(2,1)}, bf16[4,2,64,432]{3,2,1,0:T(8,128)(2,1)}, u32[]{:S(2)}, u32[]{:S(2)}) collective-permute-start(bf16[4,2,64,432]{3,2,1,0:T(8,128)(2,1)} %slice_bitcast_fusion.1), channel_id=1, source_target_pairs={{128,8},{129,9},{130,10},{131,11},{132,12},{133,13},{134,14},{135,... | collective-permute-start | bytes 1327112 | tf_op jit(solution)/shard_map/ppermute | solution.py:44
  59.9 15.0 %collective-permute-start.6 = (bf16[4,2,64,432]{3,2,1,0:T(8,128)(2,1)}, bf16[4,2,64,432]{3,2,1,0:T(8,128)(2,1)}, u32[]{:S(2)}, u32[]{:S(2)}) collective-permute-start(bf16[4,2,64,432]{3,2,1,0:T(8,128)(2,1)} %slice_bitcast_fusion.1), channel_id=1, source_target_pairs={{0,8},{1,9},{2,10},{3,11},{4,12},{5,13},{6,14},{7,15},{8,0},{9,1},... | collective-permute-start | bytes 1327112 | tf_op jit(solution)/shard_map/ppermute | solution.py:34
  81.3 2.9 %collective-permute-start.9 = (bf16[2,512,512]{2,1,0:T(8,128)(2,1)}, bf16[2,512,512]{2,1,0:T(8,128)(2,1)S(1)}, u32[]{:S(2)}, u32[]{:S(2)}) collective-permute-start(bf16[2,512,512]{2,1,0:T(8,128)(2,1)} %get-tuple-element.14), channel_id=1, source_target_pairs={{0,64},{64,0},{128,192},{192,128},{1,65},{65,1},{129,193},{193,129... | collective-permute-start | bytes 3145736 | tf_op jit(solution)/shard_map/ppermute | solution.py:38
  84.2 1.0 copy-start.1
  91.3 38.1 %all-to-all-start.1 = ((bf16[64,8,896]{2,1,0:T(8,128)(2,1)}), bf16[64,8,896]{2,1,0:T(8,128)(2,1)S(1)}, u32[]{:S(2)}, u32[]{:S(2)}) async-start(bf16[64,8,896]{2,1,0:T(8,128)(2,1)} %project.1), calls=%async_computation.1 | async-start | bytes 1835008 | tf_op jit(solution)/shard_map/all_to_all | solution.py:187
Sparse Core Ops, SparseCore 0:
  15.3 44.0 all-gather.2

commit v6 on v5

--- a/solution.py
+++ b/solution.py
@@ -213,7 +213,7 @@
     sends, up, down = lax.optimization_barrier((sends, up, down))
     kern = lax.all_to_all(sends, "band", 0, 0, axis_index_groups=over_yx)
     half = swap_groups(kern[:, 0], 1)
-    over = shift(down, -1, 0, 0)
+    over = shift(up, 1, 0, 0)
     near = jnp.stack([both, up, over, down])
     own_side = shift(near[:, 0], 0, 1, 0)
     far_side = other_side(near[:, 0])

time: 139 us -> 138 us (level)
  starting transfers between devices: 28.9 us -> 25.8 us
  waiting for transfers between devices: 70.5 us -> 73 us
    ppermute x4, waiting for transfers between devices: 21.3 us -> 23.6 us  [shift(): return lax.ppermute(block, 'band', band_route(dy, dx, dz))]
    all_to_all x1, starting transfers between devices: 12.6 us -> 10.8 us  [reduce_windows(): parts = lax.all_to_all(windows, 'band', 0, 0)]
where the time goes in v6:
time: 138 us; the launch traced here: 137 us
  waiting for transfers between devices  73 us (53%)
  starting transfers between devices  25.8 us (19%)
  Pallas kernels  17.2 us (12%)
  between operations  14.2 us (10%)
  local copies, waits for them, and re-layouts  3.98 us (3%)
  other arithmetic  2.7 us (2%)
    all_to_all x1, waiting for transfers between devices, reduce_windows(): parts = lax.all_to_all(windows, 'band', 0, 0)  25.5 us
    ppermute x4, waiting for transfers between devices, shift(): return lax.ppermute(block, 'band', band_route(dy, dx, dz))  23.6 us
    ppermute x1, waiting for transfers between devices, other_side(): return lax.ppermute(block, ('kgrp', 'band'), both)  12.4 us
    ppermute x5, waiting for transfers between devices, swap_groups(): return lax.ppermute(block, 'kgrp', [(k, k ^ bit) for k in range(4)])  11.4 us
    all_to_all x1, starting transfers between devices, reduce_windows(): parts = lax.all_to_all(windows, 'band', 0, 0)  10.8 us
    pallas_call x1, Pallas kernels, mix(): pl.pallas_call(mix_body, out_shape=[jax.ShapeDtypeStruct((2, BLOCK, BLOCK...  6.44 us
    pallas_call x1, Pallas kernels, project(): pl.pallas_call(project_body, out_shape=jax.ShapeDtypeStruct((GROUPS * NZ,...  6.15 us
    all_to_all x1, starting transfers between devices, on_device(): kern = lax.all_to_all(sends, 'band', 0, 0, axis_index_groups=over_yx)  5.98 us
  transfers between devices with their start and end apart: 13, of which 6 were waited for; matrix products, arithmetic and copies ran while one was open for 2% of the time, Pallas kernels for 3%

profile of v6, /device:TPU:6, one launch (start us, length us, event | category | flops | bytes accessed | tf_op | source)
XLA Modules:
  0.0 136.9 jit_solution(13200521056227425589)
XLA Ops:
  6.5 1.4 %collective-permute-start = (bf16[2,64,432]{2,1,0:T(8,128)(2,1)}, bf16[2,64,432]{2,1,0:T(8,128)(2,1)S(1)}, u32[]{:S(2)}, u32[]{:S(2)}) collective-permute-start(bf16[2,64,432]{2,1,0:T(8,128)(2,1)} %bitcast.35), channel_id=1, source_target_pairs={{0,128},{64,192},{128,0},{192,64},{1,129},{65,193},{129,1},{193,65... | collective-permute-start | bytes 331784 | tf_op jit(solution)/shard_map/ppermute | solution.py:38
  7.9 5.5 %collective-permute-done = bf16[2,64,432]{2,1,0:T(8,128)(2,1)S(1)} collective-permute-done((bf16[2,64,432]{2,1,0:T(8,128)(2,1)}, bf16[2,64,432]{2,1,0:T(8,128)(2,1)S(1)}, u32[]{:S(2)}, u32[]{:S(2)}) %collective-permute-start) | collective-permute-done | bytes 110624 | tf_op jit(solution)/shard_map/ppermute | solution.py:38
  13.5 1.6 %fusion.2 = (bf16[1,2,2,64,432]{4,3,2,0,1:T(8,128)(2,1)S(1)}, bf16[2,2,64,432]{3,2,1,0:T(8,128)(2,1)}) fusion(bf16[1,2,64,432]{3,2,1,0:T(8,128)(2,1)S(1)} %bitcast.36, bf16[1,2,64,432]{3,2,1,0:T(8,128)(2,1)} %param.4), kind=kLoop, calls=%fused_computation.11 | loop fusion | flops 110592 | bytes 663552 | tf_op jit(solution)/shard_map/stack | solution.py:217
  15.1 0.0 all-gather.3.cloned.1.call-update
  15.2 3.1 %collective-permute-start.4 = (bf16[2,2,64,432]{3,2,1,0:T(8,128)(2,1)}, bf16[2,2,64,432]{3,2,1,0:T(8,128)(2,1)S(1)}, u32[]{:S(2)}, u32[]{:S(2)}) collective-permute-start(bf16[2,2,64,432]{3,2,1,0:T(8,128)(2,1)} %get-tuple-element.18), channel_id=1, source_target_pairs={{0,48},{1,49},{2,50},{3,51},{4,52},{5,53},{6,54},{7,55},{8,56},{9,... | collective-permute-start | bytes 663560 | tf_op jit(solution)/shard_map/ppermute | solution.py:34
  18.3 1.4 %collective-permute-start.2 = (s32[1]{0:T(128)}, s32[1]{0:T(128)}, u32[]{:S(2)}, u32[]{:S(2)}) collective-permute-start(s32[1]{0:T(128)} %param.6), channel_id=1, source_target_pairs={{0,128},{64,192},{128,0},{192,64},{1,129},{65,193},{129,1},{193,65... | collective-permute-start | bytes 20 | tf_op jit(solution)/shard_map/ppermute | solution.py:38
  20.4 0.0 collective-permute-done.1.core_ref
  20.4 3.0 %collective-permute-done.2.far_ref = s32[1]{0:T(128)} collective-permute-done((s32[1]{0:T(128)}, s32[1]{0:T(128)}, u32[]{:S(2)}, u32[]{:S(2)}) %collective-permute-start.2) | collective-permute-done | bytes 36 | tf_op jit(solution)/shard_map/ppermute | solution.py:38
  23.4 4.6 %pack.1 = bf16[8,3,64,512]{3,2,1,0:T(8,128)(2,1)} custom-call(s32[1]{0:T(128)} %bitcast.8.odd_ref, s32[1]{0:T(128)S(6)} %copy.17.own_ref, s32[1]{0:T(128)} %collective-permute-done.1.core_ref, s32[1]{0:T(128)} %collective-permute-done.2.far_ref, s32[8]{0:T(128)} %stored_ref.1, bf16[4,2,64,4096]{3,2,1,0:T(8,128)(2,1)} %kernels_ref.1), custom_call_target="tpu_custom_call" | custom-call | tf_op jit(solution)/shard_map/pack/pallas_call | solution.py:71
  28.0 6.0 %all-to-all-start = ((bf16[8,3,64,512]{3,2,1,0:T(8,128)(2,1)}), bf16[8,3,64,512]{3,2,1,0:T(8,128)(2,1)S(1)}, u32[]{:S(2)}, u32[]{:S(2)}) async-start(bf16[8,3,64,512]{3,2,1,0:T(8,128)(2,1)} %pack.1), calls=%async_computation | async-start | bytes 3145728 | tf_op jit(solution)/shard_map/all_to_all | solution.py:214
  34.0 1.5 %collective-permute-start.5 = (bf16[2,2,64,432]{3,2,1,0:T(8,128)(2,1)S(1)}, bf16[2,2,64,432]{3,2,1,0:T(8,128)(2,1)S(1)}, u32[]{:S(2)}, u32[]{:S(2)}) collective-permute-start(bf16[2,2,64,432]{3,2,1,0:T(8,128)(2,1)S(1)} %collective-permute-done.3), channel_id=1, source_target_pairs={{0,16},{1,17},{2,18},{3,19},{4,20},{5,21},{6,22},{7,23},{8,24},{9,... | collective-permute-start | bytes 663560 | tf_op jit(solution)/shard_map/ppermute | solution.py:34
  35.5 23.6 %collective-permute-done.5 = bf16[2,2,64,432]{3,2,1,0:T(8,128)(2,1)S(1)} collective-permute-done((bf16[2,2,64,432]{3,2,1,0:T(8,128)(2,1)S(1)}, bf16[2,2,64,432]{3,2,1,0:T(8,128)(2,1)S(1)}, u32[]{:S(2)}, u32[]{:S(2)}) %collective-permute-start.5) | collective-permute-done | bytes 221216 | tf_op jit(solution)/shard_map/ppermute | solution.py:34
  59.1 0.2 pad_maximum_fusion
  59.3 0.1 collective-permute-start.8
  59.4 1.0 slice_bitcast_fusion.1
  60.4 0.7 collective-permute-start.7
  61.1 0.9 collective-permute-start.6
  62.0 0.6 stack.65.place_ref
  62.6 1.1 copy.15.refs_0_
  63.6 12.4 %collective-permute-done.7.refs_2_ = bf16[4,2,64,432]{3,2,1,0:T(8,128)(2,1)} collective-permute-done((bf16[4,2,64,432]{3,2,1,0:T(8,128)(2,1)}, bf16[4,2,64,432]{3,2,1,0:T(8,128)(2,1)}, u32[]{:S(2)}, u32[]{:S(2)}) %collective-permute-start.7) | collective-permute-done | bytes 442400 | tf_op jit(solution)/shard_map/ppermute | solution.py:44
  76.1 0.0 all-gather.3.cloned.1.call-done
  76.1 6.4 %mix.1 = (bf16[2,512,512]{2,1,0:T(8,128)(2,1)}, bf16[2,512,432]{2,1,0:T(8,128)(2,1)}, bf16[2,512,432]{2,1,0:T(8,128)(2,1)}) custom-call(s32[8]{0:T(128)} %stack.65.place_ref, s32[1]{0:T(128)} %bitcast.8.odd_ref, bf16[4,2,2,64,432]{4,3,2,1,0:T(8,128)(2,1)} %copy.15.refs_0_, bf16[4,2,64,432]{3,2,1,0:T(8,128)(2,1)} %collective-permute-done.6.refs_1_, ...), custom_call_target="tpu_custom_call" | custom-call | tf_op jit(solution)/shard_map/mix/pallas_call | solution.py:132
  82.5 2.9 %collective-permute-done.9.m_ref = bf16[2,512,512]{2,1,0:T(8,128)(2,1)S(1)} collective-permute-done((bf16[2,512,512]{2,1,0:T(8,128)(2,1)}, bf16[2,512,512]{2,1,0:T(8,128)(2,1)S(1)}, u32[]{:S(2)}, u32[]{:S(2)}) %collective-permute-start.9) | collective-permute-done | bytes 1048608 | tf_op jit(solution)/shard_map/ppermute | solution.py:38
  85.4 1.0 copy-done.1
  86.4 6.1 %project.1 = bf16[64,8,896]{2,1,0:T(8,128)(2,1)} custom-call(bf16[2,512,512]{2,1,0:T(8,128)(2,1)} %copy-done.1, bf16[2,512,432]{2,1,0:T(8,128)(2,1)} %get-tuple-element.15.row_ref, bf16[2,512,432]{2,1,0:T(8,128)(2,1)} %get-tuple-element.16.col_ref), custom_call_target="tpu_custom_call" | custom-call | tf_op jit(solution)/shard_map/project/pallas_call | solution.py:175
  92.5 10.8 %all-to-all-start.1 = ((bf16[64,8,896]{2,1,0:T(8,128)(2,1)}), bf16[64,8,896]{2,1,0:T(8,128)(2,1)S(1)}, u32[]{:S(2)}, u32[]{:S(2)}) async-start(bf16[64,8,896]{2,1,0:T(8,128)(2,1)} %project.1), calls=%async_computation.1 | async-start | bytes 1835008 | tf_op jit(solution)/shard_map/all_to_all | solution.py:187
  103.4 25.5 %all-to-all-done.1 = bf16[64,8,896]{2,1,0:T(8,128)(2,1)S(1)} async-done(((bf16[64,8,896]{2,1,0:T(8,128)(2,1)}), bf16[64,8,896]{2,1,0:T(8,128)(2,1)S(1)}, u32[]{:S(2)}, u32[]{:S(2)}) %all-to-all-start.1) | async-done | bytes 917536 | tf_op jit(solution)/shard_map/all_to_all | solution.py:187
  128.9 0.2 convert_reduce_fusion
  129.0 0.1 fusion.4
  129.1 0.1 stack.73
  129.2 0.1 stack.74
  129.3 0.7 fusion.1
  (15 shorter events, 0.1 us)
Async XLA Ops:
  6.5 69.6 %all-gather.3.cloned.1.call-start = ((), (), s32[]{:S(2)}) async-start(), calls=%async_computation.2 | async-start | bytes 2359296 | tf_op jit(solution)/shard_map/all_gather | solution.py:211
  6.5 7.0 %collective-permute-start = (bf16[2,64,432]{2,1,0:T(8,128)(2,1)}, bf16[2,64,432]{2,1,0:T(8,128)(2,1)S(1)}, u32[]{:S(2)}, u32[]{:S(2)}) collective-permute-start(bf16[2,64,432]{2,1,0:T(8,128)(2,1)} %bitcast.35), channel_id=1, source_target_pairs={{0,128},{64,192},{128,0},{192,64},{1,129},{65,193},{129,1},{193,65... | collective-permute-start | bytes 331784 | tf_op jit(solution)/shard_map/ppermute | solution.py:38
  15.2 12.8 %collective-permute-start.4 = (bf16[2,2,64,432]{3,2,1,0:T(8,128)(2,1)}, bf16[2,2,64,432]{3,2,1,0:T(8,128)(2,1)S(1)}, u32[]{:S(2)}, u32[]{:S(2)}) collective-permute-start(bf16[2,2,64,432]{3,2,1,0:T(8,128)(2,1)} %get-tuple-element.18), channel_id=1, source_target_pairs={{0,48},{1,49},{2,50},{3,51},{4,52},{5,53},{6,54},{7,55},{8,56},{9,... | collective-permute-start | bytes 663560 | tf_op jit(solution)/shard_map/ppermute | solution.py:34
  18.3 9.8 %collective-permute-start.3 = (bf16[2,2,64,432]{3,2,1,0:T(8,128)(2,1)}, bf16[2,2,64,432]{3,2,1,0:T(8,128)(2,1)S(1)}, u32[]{:S(2)}, u32[]{:S(2)}) collective-permute-start(bf16[2,2,64,432]{3,2,1,0:T(8,128)(2,1)} %get-tuple-element.18), channel_id=1, source_target_pairs={{0,16},{1,17},{2,18},{3,19},{4,20},{5,21},{6,22},{7,23},{8,24},{9,... | collective-permute-start | bytes 663560 | tf_op jit(solution)/shard_map/ppermute | solution.py:34
  18.3 2.1 %collective-permute-start.1 = (s32[1]{0:T(128)}, s32[1]{0:T(128)}, u32[]{:S(2)}, u32[]{:S(2)}) collective-permute-start(s32[1]{0:T(128)} %param.6), channel_id=1, source_target_pairs={{0,64},{64,0},{128,192},{192,128},{1,65},{65,1},{129,193},{193,129... | collective-permute-start | bytes 20 | tf_op jit(solution)/shard_map/ppermute | solution.py:38
  18.3 5.1 %collective-permute-start.2 = (s32[1]{0:T(128)}, s32[1]{0:T(128)}, u32[]{:S(2)}, u32[]{:S(2)}) collective-permute-start(s32[1]{0:T(128)} %param.6), channel_id=1, source_target_pairs={{0,128},{64,192},{128,0},{192,64},{1,129},{65,193},{129,1},{193,65... | collective-permute-start | bytes 20 | tf_op jit(solution)/shard_map/ppermute | solution.py:38
  28.0 31.2 %all-to-all-start = ((bf16[8,3,64,512]{3,2,1,0:T(8,128)(2,1)}), bf16[8,3,64,512]{3,2,1,0:T(8,128)(2,1)S(1)}, u32[]{:S(2)}, u32[]{:S(2)}) async-start(bf16[8,3,64,512]{3,2,1,0:T(8,128)(2,1)} %pack.1), calls=%async_computation | async-start | bytes 3145728 | tf_op jit(solution)/shard_map/all_to_all | solution.py:214
  34.0 25.1 %collective-permute-start.5 = (bf16[2,2,64,432]{3,2,1,0:T(8,128)(2,1)S(1)}, bf16[2,2,64,432]{3,2,1,0:T(8,128)(2,1)S(1)}, u32[]{:S(2)}, u32[]{:S(2)}) collective-permute-start(bf16[2,2,64,432]{3,2,1,0:T(8,128)(2,1)S(1)} %collective-permute-done.3), channel_id=1, source_target_pairs={{0,16},{1,17},{2,18},{3,19},{4,20},{5,21},{6,22},{7,23},{8,24},{9,... | collective-permute-start | bytes 663560 | tf_op jit(solution)/shard_map/ppermute | solution.py:34
  59.2 4.4 %copy-start = (bf16[8,3,64,512]{3,2,1,0:T(8,128)(2,1)}, bf16[8,3,64,512]{3,2,1,0:T(8,128)(2,1)S(1)}, u32[]{:S(2)}) copy-start(bf16[8,3,64,512]{3,2,1,0:T(8,128)(2,1)S(1)} %all-to-all-done.refs_4_) | copy-start | bytes 4718596
  59.3 16.8 %collective-permute-start.8 = (bf16[8,64,512]{2,1,0:T(8,128)(2,1)S(1)}, bf16[8,64,512]{2,1,0:T(8,128)(2,1)}, u32[]{:S(2)}, u32[]{:S(2)}) collective-permute-start(bf16[8,64,512]{2,1,0:T(8,128)(2,1)S(1)} %slice_bitcast_fusion), channel_id=1, source_target_pairs={{0,64},{64,0},{128,192},{192,128},{1,65},{65,1},{129,193},{193,129... | collective-permute-start | bytes 1572872 | tf_op jit(solution)/shard_map/ppermute | solution.py:38
  60.4 15.7 %collective-permute-start.7 = (bf16[4,2,64,432]{3,2,1,0:T(8,128)(2,1)}, bf16[4,2,64,432]{3,2,1,0:T(8,128)(2,1)}, u32[]{:S(2)}, u32[]{:S(2)}) collective-permute-start(bf16[4,2,64,432]{3,2,1,0:T(8,128)(2,1)} %slice_bitcast_fusion.1), channel_id=1, source_target_pairs={{128,8},{129,9},{130,10},{131,11},{132,12},{133,13},{134,14},{135,... | collective-permute-start | bytes 1327112 | tf_op jit(solution)/shard_map/ppermute | solution.py:44
  61.1 15.0 %collective-permute-start.6 = (bf16[4,2,64,432]{3,2,1,0:T(8,128)(2,1)}, bf16[4,2,64,432]{3,2,1,0:T(8,128)(2,1)}, u32[]{:S(2)}, u32[]{:S(2)}) collective-permute-start(bf16[4,2,64,432]{3,2,1,0:T(8,128)(2,1)} %slice_bitcast_fusion.1), channel_id=1, source_target_pairs={{0,8},{1,9},{2,10},{3,11},{4,12},{5,13},{6,14},{7,15},{8,0},{9,1},... | collective-permute-start | bytes 1327112 | tf_op jit(solution)/shard_map/ppermute | solution.py:34
  82.5 2.9 %collective-permute-start.9 = (bf16[2,512,512]{2,1,0:T(8,128)(2,1)}, bf16[2,512,512]{2,1,0:T(8,128)(2,1)S(1)}, u32[]{:S(2)}, u32[]{:S(2)}) collective-permute-start(bf16[2,512,512]{2,1,0:T(8,128)(2,1)} %get-tuple-element.14), channel_id=1, source_target_pairs={{0,64},{64,0},{128,192},{192,128},{1,65},{65,1},{129,193},{193,129... | collective-permute-start | bytes 3145736 | tf_op jit(solution)/shard_map/ppermute | solution.py:38
  85.4 1.0 copy-start.1
  92.5 36.3 %all-to-all-start.1 = ((bf16[64,8,896]{2,1,0:T(8,128)(2,1)}), bf16[64,8,896]{2,1,0:T(8,128)(2,1)S(1)}, u32[]{:S(2)}, u32[]{:S(2)}) async-start(bf16[64,8,896]{2,1,0:T(8,128)(2,1)} %project.1), calls=%async_computation.1 | async-start | bytes 1835008 | tf_op jit(solution)/shard_map/all_to_all | solution.py:187
Sparse Core Ops, SparseCore 0:
  15.3 44.0 all-gather.2

commit v7 on v6

--- a/solution.py
+++ b/solution.py
@@ -48,7 +48,8 @@
     return lax.dot_general(a, b, ((dims[0], dims[1]), ((), ())), preferred_element_type=jnp.float32)
 
 
-def pack_body(odd_ref, own_ref, core_ref, far_ref, stored_ref, kernels_ref, out_ref, held, sem):
+def pack_body(odd_ref, own_ref, core_ref, far_ref, stored_ref, dest_ref, kernels_ref, *refs):
+    outs, held, sem = refs[:GROUPS], refs[GROUPS], refs[GROUPS + 1]
     odd = odd_ref[0] == 1
     own, core, far = stored_ref[own_ref[0]], stored_ref[core_ref[0]], stored_ref[far_ref[0]]
     shared = jnp.where(odd, own, core)
@@ -63,35 +64,42 @@
     for which, copy in enumerate(copies):
         copy.wait()
         for i in range(GROUPS):
-            out_ref[i, which] = held[which, :, pl.ds(i * BLOCK, BLOCK)]
-
-
-def pack(odd, own, core, far, stored, kernels):
+            start = pl.multiple_of(dest_ref[i] * BLOCK, BLOCK)
+            outs[i][which] = held[which, :, pl.ds(start, BLOCK)]
+
+
+def pack(odd, own, core, far, stored, dests, kernels):
     smem = pl.BlockSpec(memory_space=pltpu.SMEM)
     return pl.pallas_call(
         pack_body,
-        out_shape=jax.ShapeDtypeStruct((GROUPS, 3, SLAB, BLOCK), jnp.bfloat16),
-        in_specs=[smem] * 5 + [pl.BlockSpec(memory_space=pl.ANY)],
-        out_specs=pl.BlockSpec(memory_space=pltpu.VMEM),
+        out_shape=[jax.ShapeDtypeStruct((3, SLAB, BLOCK), jnp.bfloat16)] * GROUPS,
+        in_specs=[smem] * 6 + [pl.BlockSpec(memory_space=pl.ANY)],
+        out_specs=[pl.BlockSpec(memory_space=pltpu.VMEM)] * GROUPS,
         scratch_shapes=[
             pltpu.VMEM((3, SLAB, GROUPS * BLOCK), jnp.bfloat16),
             pltpu.SemaphoreType.DMA((3,)),
         ],
         compiler_params=pltpu.CompilerParams(vmem_limit_bytes=VMEM),
         name="pack",
-    )(odd, own, core, far, stored, kernels)
+    )(odd, own, core, far, stored, dests, kernels)
 
 
 def mix_body(place_ref, odd_ref, *refs):
-    near_ref, own_side, far_side, gathered_ref, kern_ref, half_ref = refs[:6]
-    m_ref, row_ref, col_ref, other_rows, other_cols = refs[6:]
+    near, (own_side, far_side, gathered_ref, half_ref) = refs[:NY], refs[NY : NY + 4]
+    kerns, refs = refs[NY + 4 : NY + 4 + GROUPS], refs[NY + 4 + GROUPS :]
+    m_ref, row_ref, col_ref, other_rows, other_cols, kern_ref = refs
+
+    def rows_of(i):
+        return pl.ds(pl.multiple_of(place_ref[i] * SLAB, SLAB), SLAB)
+
     for i in range(NY):
-        at = pl.ds(pl.multiple_of(place_ref[i] * SLAB, SLAB), SLAB)
-        row_ref[:, at, :] = near_ref[i, 0]
-        other_rows[:, at, :] = near_ref[i, 1]
-        at = pl.ds(pl.multiple_of(place_ref[NY + i] * SLAB, SLAB), SLAB)
-        row_ref[:, at, :] = own_side[i]
-        other_rows[:, at, :] = far_side[i]
+        row_ref[:, rows_of(i), :] = near[i][0]
+        other_rows[:, rows_of(i), :] = near[i][1]
+        row_ref[:, rows_of(NY + i), :] = own_side[i]
+        other_rows[:, rows_of(NY + i), :] = far_side[i]
+    for i in range(GROUPS):
+        kern_ref[:3, rows_of(i), :] = kerns[i][...]
+        kern_ref[3, rows_of(i), :] = half_ref[i]
     for i in range(NZ):
         at = pl.ds(i * SLAB, SLAB)
         col_ref[:, at, :] = gathered_ref[i, 0]
@@ -110,15 +118,14 @@
     for part in range(2):
         at = pl.ds(part * per, per)
         p_re, p_im = density(row_ref, col_ref, at)
-        mine = kern_ref[:, 0, :, at].reshape(BLOCK, per)
-        other = half_ref[:, :, at].reshape(BLOCK, per)
+        mine, other = kern_ref[0, :, at], kern_ref[3, :, at]
         k_re = jnp.where(odd, other, mine).astype(jnp.float32)
         k_im = jnp.where(odd, mine, other).astype(jnp.float32) * sign
         total_re = k_re * p_re - k_im * p_im
         total_im = k_re * p_im + k_im * p_re
         p_re, p_im = density(other_rows, other_cols, at)
-        k_re = kern_ref[:, 1, :, at].reshape(BLOCK, per).astype(jnp.float32)
-        k_im = kern_ref[:, 2, :, at].reshape(BLOCK, per).astype(jnp.float32) * -sign
+        k_re = kern_ref[1, :, at].astype(jnp.float32)
+        k_im = kern_ref[2, :, at].astype(jnp.float32) * -sign
         total_re += k_re * p_re - k_im * p_im
         total_im += k_re * p_im + k_im * p_re
         m_ref[0, :, at] = total_re.astype(jnp.bfloat16)
@@ -134,7 +141,8 @@
         out_shape=[jax.ShapeDtypeStruct((2, BLOCK, BLOCK), jnp.bfloat16), points, points],
         in_specs=[smem, smem] + [vmem] * len(arrays),
         out_specs=[vmem] * 3,
-        scratch_shapes=[pltpu.VMEM((2, BLOCK, NB), jnp.bfloat16)] * 2,
+        scratch_shapes=[pltpu.VMEM((2, BLOCK, NB), jnp.bfloat16)] * 2
+        + [pltpu.VMEM((4, BLOCK, BLOCK), jnp.bfloat16)],
         compiler_params=pltpu.CompilerParams(vmem_limit_bytes=VMEM),
         name="mix",
     )(place, odd, *arrays)
@@ -204,22 +212,33 @@
     diff_far = swap_groups(pair_kdiff, 2)
     far = swap_groups(own, 2)
 
-    over_yx = [[g * NZ + z_at for g in range(GROUPS)] for z_at in range(NZ)]
     over_z = [[g * NZ + z_at for z_at in range(NZ)] for g in range(GROUPS)]
-    sends = pack(odd, pair_kdiff, diff_core, diff_far, stored_kernel_index, kernels)
+    dests = jnp.stack([(y + dy) % NY * NX + (x + dx) % NX for dy, dx in OFFSETS])
+    sends = pack(odd, pair_kdiff, diff_core, diff_far, stored_kernel_index, dests, kernels)
+
     both = jnp.stack([own, far])
     gathered = lax.all_gather(both, "band", axis_index_groups=over_z)
     up, down = shift(both, 1, 0, 0), shift(both, -1, 0, 0)
     sends, up, down = lax.optimization_barrier((sends, up, down))
-    kern = lax.all_to_all(sends, "band", 0, 0, axis_index_groups=over_yx)
-    half = swap_groups(kern[:, 0], 1)
     over = shift(up, 1, 0, 0)
-    near = jnp.stack([both, up, over, down])
-    own_side = shift(near[:, 0], 0, 1, 0)
-    far_side = other_side(near[:, 0])
+    kerns = {(0, 0): sends[0]}
+    send_of = dict(zip(OFFSETS, sends))
+    for offset in ((2, 0), (2, 1), (1, 0), (3, 0)):
+        kerns[offset] = shift(send_of[offset], *offset, 0)
+    later = ((1, 1), (3, 1), (0, 1))
+    held, over = lax.optimization_barrier(([send_of[offset] for offset in later], over))
+    near = [both, up, over, down]
+    owns = jnp.stack([block[0] for block in near])
+    own_side, far_side = shift(owns, 0, 1, 0), other_side(owns)
+    for offset, block in zip(later, held):
+        kerns[offset] = shift(block, *offset, 0)
+    kerns = [kerns[offset] for offset in OFFSETS]
+    half = swap_groups(jnp.stack([block[0] for block in kerns]), 1)
 
     place = jnp.stack([(y - dy) % NY * NX + (x - dx) % NX for dy, dx in OFFSETS])
-    m_out, own_rows, own_cols = mix(place, odd, near, own_side, far_side, gathered, kern, half)
+    m_out, own_rows, own_cols = mix(
+        place, odd, *near, own_side, far_side, gathered, half, *kerns
+    )
     m_own = swap_groups(m_out, 1)
     total = reduce_windows(project(m_own, own_rows, own_cols))
     flat = total.reshape(2, 8 * NB)

time: 138 us -> 148 us (1.072)
  starting transfers between devices: 25.8 us -> 33.6 us
  local copies, waits for them, and re-layouts: 3.98 us -> 9.79 us
  waiting for transfers between devices: 73 us -> 68.6 us
    ppermute x4 -> x11, starting transfers between devices: 5.42 us -> 15.8 us  [shift(): return lax.ppermute(block, 'band', band_route(dy, dx, dz))]
    unnamed x4 -> x37, local copies, waits for them, and re-layouts: 0.99 us -> 7.57 us
    all_to_all x1 -> x0, starting transfers between devices: 5.98 us -> none  [on_device(): kern = lax.all_to_all(sends, 'band', 0, 0, axis_index_groups=over_yx)]
    ppermute x4 -> x11, waiting for transfers between devices: 23.6 us -> 18.5 us  [shift(): return lax.ppermute(block, 'band', band_route(dy, dx, dz))]
    all_to_all x1, starting transfers between devices: 10.8 us -> 13.7 us  [reduce_windows(): parts = lax.all_to_all(windows, 'band', 0, 0)]
  transfers between devices with their start and end apart: 13 -> 19, of which waited for: 6 -> 9; matrix products, arithmetic and copies ran while one was open for 2% -> 5% of each run, Pallas kernels for 3% -> 3%
where the time goes in v7:
time: 148 us; the launch traced here: 146 us
  waiting for transfers between devices  68.6 us (46%)
  starting transfers between devices  33.6 us (23%)
  Pallas kernels  17.3 us (12%)
  between operations  14.3 us (10%)
  local copies, waits for them, and re-layouts  9.79 us (7%)
  other arithmetic  2.61 us (2%)
    all_to_all x1, waiting for transfers between devices, reduce_windows(): parts = lax.all_to_all(windows, 'band', 0, 0)  25.5 us
    ppermute x11, waiting for transfers between devices, shift(): return lax.ppermute(block, 'band', band_route(dy, dx, dz))  18.5 us
    ppermute x11, starting transfers between devices, shift(): return lax.ppermute(block, 'band', band_route(dy, dx, dz))  15.8 us
    ppermute x1, waiting for transfers between devices, other_side(): return lax.ppermute(block, ('kgrp', 'band'), both)  13.8 us
    all_to_all x1, starting transfers between devices, reduce_windows(): parts = lax.all_to_all(windows, 'band', 0, 0)  13.7 us
    ppermute x5, waiting for transfers between devices, swap_groups(): return lax.ppermute(block, 'kgrp', [(k, k ^ bit) for k in range(4)])  10.8 us
    unnamed x37, local copies, waits for them, and re-layouts  7.57 us
    pallas_call x1, Pallas kernels, mix(): pl.pallas_call(mix_body, out_shape=[jax.ShapeDtypeStruct((2, BLOCK, BLOCK...  6.59 us
  transfers between devices with their start and end apart: 19, of which 9 were waited for; matrix products, arithmetic and copies ran while one was open for 5% of the time, Pallas kernels for 3%

profile of v7, /device:TPU:6, one launch (start us, length us, event | category | flops | bytes accessed | tf_op | source)
XLA Modules:
  0.0 146.1 jit_solution(8724295691704921121)
XLA Ops:
  6.5 1.4 collective-permute-start
  7.9 5.5 %collective-permute-done = bf16[2,64,432]{2,1,0:T(8,128)(2,1)S(1)} collective-permute-done((bf16[2,64,432]{2,1,0:T(8,128)(2,1)}, bf16[2,64,432]{2,1,0:T(8,128)(2,1)S(1)}, u32[]{:S(2)}, u32[]{:S(2)}) %collective-permute-start) | collective-permute-done | bytes 110624 | tf_op jit(solution)/shard_map/ppermute | solution.py:38
  13.5 1.6 %pad_maximum_fusion.1.refs_0_ = bf16[2,2,64,432]{3,2,1,0:T(8,128)(2,1)} fusion(bf16[1,2,64,432]{3,2,1,0:T(8,128)(2,1)S(1)} %bitcast.23, bf16[1,2,64,432]{3,2,1,0:T(8,128)(2,1)} %param.4), kind=kLoop, calls=%fused_computation.2 | loop fusion | flops 110592 | bytes 442368 | tf_op jit(solution)/shard_map/stack | solution.py:219
  15.1 3.1 %collective-permute-start.4 = (bf16[2,2,64,432]{3,2,1,0:T(8,128)(2,1)}, bf16[2,2,64,432]{3,2,1,0:T(8,128)(2,1)S(1)}, u32[]{:S(2)}, u32[]{:S(2)}) collective-permute-start(bf16[2,2,64,432]{3,2,1,0:T(8,128)(2,1)} %pad_maximum_fusion.1.refs_0_), channel_id=1, source_target_pairs={{0,48},{1,49},{2,50},{3,51},{4,52},{5,53},{6,54},{7,55},{8,56},{9,... | collective-permute-start | bytes 663560 | tf_op jit(solution)/shard_map/ppermute | solution.py:34
  18.2 1.4 collective-permute-start.2
  20.3 0.7 stack.91.dest_ref
  21.0 2.4 %collective-permute-done.2.far_ref = s32[1]{0:T(128)} collective-permute-done((s32[1]{0:T(128)}, s32[1]{0:T(128)}, u32[]{:S(2)}, u32[]{:S(2)}) %collective-permute-start.2) | collective-permute-done | bytes 36 | tf_op jit(solution)/shard_map/ppermute | solution.py:38
  23.4 4.5 %pack.1 = (bf16[3,64,512]{2,1,0:T(8,128)(2,1)}, bf16[3,64,512]{2,1,0:T(8,128)(2,1)}, bf16[3,64,512]{2,1,0:T(8,128)(2,1)}, bf16[3,64,512]{2,1,0:T(8,128)(2,1)}, b...) custom-call(s32[1]{0:T(128)} %bitcast.8.odd_ref, ...), custom_call_target="tpu_custom_call" | custom-call | tf_op jit(solution)/shard_map/pack/pallas_call | solution.py:73
  28.6 1.7 %collective-permute-start.8 = (bf16[3,64,512]{2,1,0:T(8,128)(2,1)}, bf16[3,64,512]{2,1,0:T(8,128)(2,1)S(1)}, u32[]{:S(2)}, u32[]{:S(2)}) collective-permute-start(bf16[3,64,512]{2,1,0:T(8,128)(2,1)} %get-tuple-element.45), channel_id=1, source_target_pairs={{0,16},{1,17},{2,18},{3,19},{4,20},{5,21},{6,22},{7,23},{8,24},{9,... | collective-permute-start | bytes 589832 | tf_op jit(solution)/shard_map/ppermute | solution.py:34
  30.3 2.6 %collective-permute-start.9 = (bf16[3,64,512]{2,1,0:T(8,128)(2,1)}, bf16[3,64,512]{2,1,0:T(8,128)(2,1)S(1)}, u32[]{:S(2)}, u32[]{:S(2)}) collective-permute-start(bf16[3,64,512]{2,1,0:T(8,128)(2,1)} %get-tuple-element.46), channel_id=1, source_target_pairs={{0,32},{1,33},{2,34},{3,35},{4,36},{5,37},{6,38},{7,39},{8,40},{9,... | collective-permute-start | bytes 589832 | tf_op jit(solution)/shard_map/ppermute | solution.py:34
  32.9 2.5 %collective-permute-start.10 = (bf16[3,64,512]{2,1,0:T(8,128)(2,1)}, bf16[3,64,512]{2,1,0:T(8,128)(2,1)S(1)}, u32[]{:S(2)}, u32[]{:S(2)}) collective-permute-start(bf16[3,64,512]{2,1,0:T(8,128)(2,1)} %get-tuple-element.47), channel_id=1, source_target_pairs={{0,48},{1,49},{2,50},{3,51},{4,52},{5,53},{6,54},{7,55},{8,56},{9,... | collective-permute-start | bytes 589832 | tf_op jit(solution)/shard_map/ppermute | solution.py:34
  35.5 1.5 slice_dynamic-update-slice_fusion.7
  36.9 9.1 %collective-permute-done.8.refs_9_ = bf16[3,64,512]{2,1,0:T(8,128)(2,1)S(1)} collective-permute-done((bf16[3,64,512]{2,1,0:T(8,128)(2,1)}, bf16[3,64,512]{2,1,0:T(8,128)(2,1)S(1)}, u32[]{:S(2)}, u32[]{:S(2)}) %collective-permute-start.8) | collective-permute-done | bytes 196640 | tf_op jit(solution)/shard_map/ppermute | solution.py:34
  46.0 0.7 slice_dynamic-update-slice_fusion.6
  46.7 4.4 %collective-permute-done.9.refs_10_ = bf16[3,64,512]{2,1,0:T(8,128)(2,1)S(1)} collective-permute-done((bf16[3,64,512]{2,1,0:T(8,128)(2,1)}, bf16[3,64,512]{2,1,0:T(8,128)(2,1)S(1)}, u32[]{:S(2)}, u32[]{:S(2)}) %collective-permute-start.9) | collective-permute-done | bytes 196640 | tf_op jit(solution)/shard_map/ppermute | solution.py:34
  51.7 1.0 collective-permute-start.11
  52.8 0.7 slice_dynamic-update-slice_fusion.4
  53.5 4.1 %collective-permute-start.14 = (bf16[3,64,512]{2,1,0:T(8,128)(2,1)}, bf16[3,64,512]{2,1,0:T(8,128)(2,1)S(1)}, u32[]{:S(2)}, u32[]{:S(2)}) collective-permute-start(bf16[3,64,512]{2,1,0:T(8,128)(2,1)} %get-tuple-element.51), channel_id=1, source_target_pairs={{0,56},{1,57},{2,58},{3,59},{4,60},{5,61},{6,62},{7,63},{8,48},{9,... | collective-permute-start | bytes 589832 | tf_op jit(solution)/shard_map/ppermute | solution.py:34
  57.6 2.1 %collective-permute-done.11.refs_12_ = bf16[3,64,512]{2,1,0:T(8,128)(2,1)S(1)} collective-permute-done((bf16[3,64,512]{2,1,0:T(8,128)(2,1)}, bf16[3,64,512]{2,1,0:T(8,128)(2,1)S(1)}, u32[]{:S(2)}, u32[]{:S(2)}) %collective-permute-start.11) | collective-permute-done | bytes 196640 | tf_op jit(solution)/shard_map/ppermute | solution.py:34
  60.4 2.8 %collective-permute-done.12.refs_13_ = bf16[3,64,512]{2,1,0:T(8,128)(2,1)S(1)} collective-permute-done((bf16[3,64,512]{2,1,0:T(8,128)(2,1)}, bf16[3,64,512]{2,1,0:T(8,128)(2,1)S(1)}, u32[]{:S(2)}, u32[]{:S(2)}) %collective-permute-start.12) | collective-permute-done | bytes 196640 | tf_op jit(solution)/shard_map/ppermute | solution.py:34
  63.3 0.7 slice_dynamic-update-slice_fusion.2
  63.9 0.7 slice_dynamic-update-slice_fusion.1
  65.5 1.2 collective-permute-start.7
  67.3 13.8 %collective-permute-done.7.refs_5_ = bf16[4,2,64,432]{3,2,1,0:T(8,128)(2,1)S(1)} collective-permute-done((bf16[4,2,64,432]{3,2,1,0:T(8,128)(2,1)S(1)}, bf16[4,2,64,432]{3,2,1,0:T(8,128)(2,1)S(1)}, u32[]{:S(2)}, u32[]{:S(2)}) %collective-permute-start.7) | collective-permute-done | bytes 442400 | tf_op jit(solution)/shard_map/ppermute | solution.py:44
  81.2 0.7 copy-done.6
  82.3 6.6 %mix.1 = (bf16[2,512,512]{2,1,0:T(8,128)(2,1)}, bf16[2,512,432]{2,1,0:T(8,128)(2,1)}, bf16[2,512,432]{2,1,0:T(8,128)(2,1)}) custom-call(s32[8]{0:T(128)} %stack.81.place_ref, s32[1]{0:T(128)} %bitcast.8.odd_ref, bf16[2,2,64,432]{3,2,1,0:T(8,128)(2,1)} %pad_maximum_fusion.1.refs_0_, bf16[2,2,64,432]{3,2,1,0:T(8,128)(2,1)} %copy-done.2, ...), custom_call_target="tpu_custom_call" | custom-call | tf_op jit(solution)/shard_map/mix/pallas_call | solution.py:139
  88.9 2.9 %collective-permute-done.16.m_ref = bf16[2,512,512]{2,1,0:T(8,128)(2,1)S(1)} collective-permute-done((bf16[2,512,512]{2,1,0:T(8,128)(2,1)}, bf16[2,512,512]{2,1,0:T(8,128)(2,1)S(1)}, u32[]{:S(2)}, u32[]{:S(2)}) %collective-permute-start.16) | collective-permute-done | bytes 1048608 | tf_op jit(solution)/shard_map/ppermute | solution.py:38
  91.7 1.0 copy-done
  92.7 6.1 %project.1 = bf16[64,8,896]{2,1,0:T(8,128)(2,1)} custom-call(bf16[2,512,512]{2,1,0:T(8,128)(2,1)} %copy-done, bf16[2,512,432]{2,1,0:T(8,128)(2,1)} %get-tuple-element.53.row_ref, bf16[2,512,432]{2,1,0:T(8,128)(2,1)} %get-tuple-element.54.col_ref), custom_call_target="tpu_custom_call" | custom-call | tf_op jit(solution)/shard_map/project/pallas_call | solution.py:183
  98.9 13.7 %all-to-all-start = ((bf16[64,8,896]{2,1,0:T(8,128)(2,1)}), bf16[64,8,896]{2,1,0:T(8,128)(2,1)S(1)}, u32[]{:S(2)}, u32[]{:S(2)}) async-start(bf16[64,8,896]{2,1,0:T(8,128)(2,1)} %project.1), calls=%async_computation | async-start | bytes 1835008 | tf_op jit(solution)/shard_map/all_to_all | solution.py:195
  112.6 25.5 %all-to-all-done = bf16[64,8,896]{2,1,0:T(8,128)(2,1)S(1)} async-done(((bf16[64,8,896]{2,1,0:T(8,128)(2,1)}), bf16[64,8,896]{2,1,0:T(8,128)(2,1)S(1)}, u32[]{:S(2)}, u32[]{:S(2)}) %all-to-all-start) | async-done | bytes 917536 | tf_op jit(solution)/shard_map/all_to_all | solution.py:195
  138.6 0.7 fusion.1
  (62 shorter events, 4.4 us)
Async XLA Ops:
  6.5 74.6 %all-gather.3.cloned.1.call-start = ((), (), s32[]{:S(2)}) async-start(), calls=%async_computation.1 | async-start | bytes 2359296 | tf_op jit(solution)/shard_map/all_gather | solution.py:220
  6.5 7.0 %collective-permute-start = (bf16[2,64,432]{2,1,0:T(8,128)(2,1)}, bf16[2,64,432]{2,1,0:T(8,128)(2,1)S(1)}, u32[]{:S(2)}, u32[]{:S(2)}) collective-permute-start(bf16[2,64,432]{2,1,0:T(8,128)(2,1)} %bitcast.22), channel_id=1, source_target_pairs={{0,128},{64,192},{128,0},{192,64},{1,129},{65,193},{129,1},{193,65... | collective-permute-start | bytes 331784 | tf_op jit(solution)/shard_map/ppermute | solution.py:38
  15.1 12.8 %collective-permute-start.4 = (bf16[2,2,64,432]{3,2,1,0:T(8,128)(2,1)}, bf16[2,2,64,432]{3,2,1,0:T(8,128)(2,1)S(1)}, u32[]{:S(2)}, u32[]{:S(2)}) collective-permute-start(bf16[2,2,64,432]{3,2,1,0:T(8,128)(2,1)} %pad_maximum_fusion.1.refs_0_), channel_id=1, source_target_pairs={{0,48},{1,49},{2,50},{3,51},{4,52},{5,53},{6,54},{7,55},{8,56},{9,... | collective-permute-start | bytes 663560 | tf_op jit(solution)/shard_map/ppermute | solution.py:34
  18.2 9.7 %collective-permute-start.3 = (bf16[2,2,64,432]{3,2,1,0:T(8,128)(2,1)}, bf16[2,2,64,432]{3,2,1,0:T(8,128)(2,1)S(1)}, u32[]{:S(2)}, u32[]{:S(2)}) collective-permute-start(bf16[2,2,64,432]{3,2,1,0:T(8,128)(2,1)} %pad_maximum_fusion.1.refs_0_), channel_id=1, source_target_pairs={{0,16},{1,17},{2,18},{3,19},{4,20},{5,21},{6,22},{7,23},{8,24},{9,... | collective-permute-start | bytes 663560 | tf_op jit(solution)/shard_map/ppermute | solution.py:34
  18.2 2.8 %collective-permute-start.1 = (s32[1]{0:T(128)}, s32[1]{0:T(128)}, u32[]{:S(2)}, u32[]{:S(2)}) collective-permute-start(s32[1]{0:T(128)} %param.6), channel_id=1, source_target_pairs={{0,64},{64,0},{128,192},{192,128},{1,65},{65,1},{129,193},{193,129... | collective-permute-start | bytes 20 | tf_op jit(solution)/shard_map/ppermute | solution.py:38
  18.2 5.1 %collective-permute-start.2 = (s32[1]{0:T(128)}, s32[1]{0:T(128)}, u32[]{:S(2)}, u32[]{:S(2)}) collective-permute-start(s32[1]{0:T(128)} %param.6), channel_id=1, source_target_pairs={{0,128},{64,192},{128,0},{192,64},{1,129},{65,193},{129,1},{193,65... | collective-permute-start | bytes 20 | tf_op jit(solution)/shard_map/ppermute | solution.py:38
  23.4 42.0 %copy-start.4 = (bf16[1,2,64,432]{3,2,1,0:T(8,128)(2,1)S(1)}, bf16[1,2,64,432]{3,2,1,0:T(8,128)(2,1)}, u32[]{:S(2)}) copy-start(bf16[1,2,64,432]{3,2,1,0:T(8,128)(2,1)} %param.4) | copy-start | bytes 331780
  27.9 53.3 %copy-start.1 = (bf16[2,2,64,432]{3,2,1,0:T(8,128)(2,1)}, bf16[2,2,64,432]{3,2,1,0:T(8,128)(2,1)S(1)}, u32[]{:S(2)}) copy-start(bf16[2,2,64,432]{3,2,1,0:T(8,128)(2,1)S(1)} %collective-permute-done.4.refs_3_) | copy-start | bytes 663556
  27.9 53.2 %copy-start.2 = (bf16[2,2,64,432]{3,2,1,0:T(8,128)(2,1)}, bf16[2,2,64,432]{3,2,1,0:T(8,128)(2,1)S(1)}, u32[]{:S(2)}) copy-start(bf16[2,2,64,432]{3,2,1,0:T(8,128)(2,1)S(1)} %collective-permute-done.3.refs_1_) | copy-start | bytes 663556
  28.0 23.8 %collective-permute-start.5 = (bf16[2,2,64,432]{3,2,1,0:T(8,128)(2,1)S(1)}, bf16[2,2,64,432]{3,2,1,0:T(8,128)(2,1)S(1)}, u32[]{:S(2)}, u32[]{:S(2)}) collective-permute-start(bf16[2,2,64,432]{3,2,1,0:T(8,128)(2,1)S(1)} %collective-permute-done.3.refs_1_), channel_id=1, source_target_pairs={{0,16},{1,17},{2,18},{3,19},{4,20},{5,21},{6,22},{7,23},{8,24},{9,... | collective-permute-start | bytes 663560 | tf_op jit(solution)/shard_map/ppermute | solution.py:34
  28.6 17.4 %collective-permute-start.8 = (bf16[3,64,512]{2,1,0:T(8,128)(2,1)}, bf16[3,64,512]{2,1,0:T(8,128)(2,1)S(1)}, u32[]{:S(2)}, u32[]{:S(2)}) collective-permute-start(bf16[3,64,512]{2,1,0:T(8,128)(2,1)} %get-tuple-element.45), channel_id=1, source_target_pairs={{0,16},{1,17},{2,18},{3,19},{4,20},{5,21},{6,22},{7,23},{8,24},{9,... | collective-permute-start | bytes 589832 | tf_op jit(solution)/shard_map/ppermute | solution.py:34
  30.3 20.8 %collective-permute-start.9 = (bf16[3,64,512]{2,1,0:T(8,128)(2,1)}, bf16[3,64,512]{2,1,0:T(8,128)(2,1)S(1)}, u32[]{:S(2)}, u32[]{:S(2)}) collective-permute-start(bf16[3,64,512]{2,1,0:T(8,128)(2,1)} %get-tuple-element.46), channel_id=1, source_target_pairs={{0,32},{1,33},{2,34},{3,35},{4,36},{5,37},{6,38},{7,39},{8,40},{9,... | collective-permute-start | bytes 589832 | tf_op jit(solution)/shard_map/ppermute | solution.py:34
  32.9 19.8 %collective-permute-start.10 = (bf16[3,64,512]{2,1,0:T(8,128)(2,1)}, bf16[3,64,512]{2,1,0:T(8,128)(2,1)S(1)}, u32[]{:S(2)}, u32[]{:S(2)}) collective-permute-start(bf16[3,64,512]{2,1,0:T(8,128)(2,1)} %get-tuple-element.47), channel_id=1, source_target_pairs={{0,48},{1,49},{2,50},{3,51},{4,52},{5,53},{6,54},{7,55},{8,56},{9,... | collective-permute-start | bytes 589832 | tf_op jit(solution)/shard_map/ppermute | solution.py:34
  35.5 28.5 %collective-permute-start.13 = (bf16[3,64,512]{2,1,0:T(8,128)(2,1)}, bf16[3,64,512]{2,1,0:T(8,128)(2,1)S(1)}, u32[]{:S(2)}, u32[]{:S(2)}) collective-permute-start(bf16[3,64,512]{2,1,0:T(8,128)(2,1)} %get-tuple-element.50), channel_id=1, source_target_pairs={{0,40},{1,41},{2,42},{3,43},{4,44},{5,45},{6,46},{7,47},{8,32},{9,... | collective-permute-start | bytes 589832 | tf_op jit(solution)/shard_map/ppermute | solution.py:34
  46.0 35.2 %copy-start.8 = (bf16[3,64,512]{2,1,0:T(8,128)(2,1)}, bf16[3,64,512]{2,1,0:T(8,128)(2,1)S(1)}, u32[]{:S(2)}) copy-start(bf16[3,64,512]{2,1,0:T(8,128)(2,1)S(1)} %collective-permute-done.8.refs_9_) | copy-start | bytes 589828
  51.1 30.1 %copy-start.9 = (bf16[3,64,512]{2,1,0:T(8,128)(2,1)}, bf16[3,64,512]{2,1,0:T(8,128)(2,1)S(1)}, u32[]{:S(2)}) copy-start(bf16[3,64,512]{2,1,0:T(8,128)(2,1)S(1)} %collective-permute-done.9.refs_10_) | copy-start | bytes 589828
  51.7 29.5 %copy-start.3 = (bf16[2,2,64,432]{3,2,1,0:T(8,128)(2,1)}, bf16[2,2,64,432]{3,2,1,0:T(8,128)(2,1)S(1)}, u32[]{:S(2)}) copy-start(bf16[2,2,64,432]{3,2,1,0:T(8,128)(2,1)S(1)} %collective-permute-done.5.refs_2_) | copy-start | bytes 663556
  51.7 8.0 %collective-permute-start.11 = (bf16[3,64,512]{2,1,0:T(8,128)(2,1)}, bf16[3,64,512]{2,1,0:T(8,128)(2,1)S(1)}, u32[]{:S(2)}, u32[]{:S(2)}) collective-permute-start(bf16[3,64,512]{2,1,0:T(8,128)(2,1)} %get-tuple-element.48), channel_id=1, source_target_pairs={{0,8},{1,9},{2,10},{3,11},{4,12},{5,13},{6,14},{7,15},{8,0},{9,1},... | collective-permute-start | bytes 589832 | tf_op jit(solution)/shard_map/ppermute | solution.py:34
  52.7 28.5 %copy-start.10 = (bf16[3,64,512]{2,1,0:T(8,128)(2,1)}, bf16[3,64,512]{2,1,0:T(8,128)(2,1)S(1)}, u32[]{:S(2)}) copy-start(bf16[3,64,512]{2,1,0:T(8,128)(2,1)S(1)} %collective-permute-done.10.refs_11_) | copy-start | bytes 589828
  53.4 9.8 %collective-permute-start.12 = (bf16[3,64,512]{2,1,0:T(8,128)(2,1)}, bf16[3,64,512]{2,1,0:T(8,128)(2,1)S(1)}, u32[]{:S(2)}, u32[]{:S(2)}) collective-permute-start(bf16[3,64,512]{2,1,0:T(8,128)(2,1)} %get-tuple-element.49), channel_id=1, source_target_pairs={{0,24},{1,25},{2,26},{3,27},{4,28},{5,29},{6,30},{7,31},{8,16},{9,... | collective-permute-start | bytes 589832 | tf_op jit(solution)/shard_map/ppermute | solution.py:34
  53.5 11.1 %collective-permute-start.14 = (bf16[3,64,512]{2,1,0:T(8,128)(2,1)}, bf16[3,64,512]{2,1,0:T(8,128)(2,1)S(1)}, u32[]{:S(2)}, u32[]{:S(2)}) collective-permute-start(bf16[3,64,512]{2,1,0:T(8,128)(2,1)} %get-tuple-element.51), channel_id=1, source_target_pairs={{0,56},{1,57},{2,58},{3,59},{4,60},{5,61},{6,62},{7,63},{8,48},{9,... | collective-permute-start | bytes 589832 | tf_op jit(solution)/shard_map/ppermute | solution.py:34
  59.8 5.5 %copy-start.12 = (bf16[3,64,512]{2,1,0:T(8,128)(2,1)}, bf16[3,64,512]{2,1,0:T(8,128)(2,1)S(1)}, u32[]{:S(2)}) copy-start(bf16[3,64,512]{2,1,0:T(8,128)(2,1)S(1)} %collective-permute-done.11.refs_12_) | copy-start | bytes 589828
  63.3 2.0 %copy-start.13 = (bf16[3,64,512]{2,1,0:T(8,128)(2,1)}, bf16[3,64,512]{2,1,0:T(8,128)(2,1)S(1)}, u32[]{:S(2)}) copy-start(bf16[3,64,512]{2,1,0:T(8,128)(2,1)S(1)} %collective-permute-done.12.refs_13_) | copy-start | bytes 589828
  63.9 1.4 copy-start.11
  65.3 15.8 %collective-permute-start.15 = (bf16[8,64,512]{2,1,0:T(8,128)(2,1)}, bf16[8,64,512]{2,1,0:T(8,128)(2,1)S(1)}, u32[]{:S(2)}, u32[]{:S(2)}) collective-permute-start(bf16[8,64,512]{2,1,0:T(8,128)(2,1)} %slice_dynamic-update-slice_fusion), channel_id=1, source_target_pairs={{0,64},{64,0},{128,192},{192,128},{1,65},{65,1},{129,193},{193,129... | collective-permute-start | bytes 1572872 | tf_op jit(solution)/shard_map/ppermute | solution.py:38
  65.5 15.6 %collective-permute-start.7 = (bf16[4,2,64,432]{3,2,1,0:T(8,128)(2,1)S(1)}, bf16[4,2,64,432]{3,2,1,0:T(8,128)(2,1)S(1)}, u32[]{:S(2)}, u32[]{:S(2)}) collective-permute-start(bf16[4,2,64,432]{3,2,1,0:T(8,128)(2,1)S(1)} %pad_maximum_fusion), channel_id=1, source_target_pairs={{128,8},{129,9},{130,10},{131,11},{132,12},{133,13},{134,14},{135,... | collective-permute-start | bytes 1327112 | tf_op jit(solution)/shard_map/ppermute | solution.py:44
  66.7 14.4 %collective-permute-start.6 = (bf16[4,2,64,432]{3,2,1,0:T(8,128)(2,1)S(1)}, bf16[4,2,64,432]{3,2,1,0:T(8,128)(2,1)S(1)}, u32[]{:S(2)}, u32[]{:S(2)}) collective-permute-start(bf16[4,2,64,432]{3,2,1,0:T(8,128)(2,1)S(1)} %pad_maximum_fusion), channel_id=1, source_target_pairs={{0,8},{1,9},{2,10},{3,11},{4,12},{5,13},{6,14},{7,15},{8,0},{9,1},... | collective-permute-start | bytes 1327112 | tf_op jit(solution)/shard_map/ppermute | solution.py:34
  81.1 1.0 copy-start.7
  81.1 1.1 copy-start.5
  88.9 2.9 %collective-permute-start.16 = (bf16[2,512,512]{2,1,0:T(8,128)(2,1)}, bf16[2,512,512]{2,1,0:T(8,128)(2,1)S(1)}, u32[]{:S(2)}, u32[]{:S(2)}) collective-permute-start(bf16[2,512,512]{2,1,0:T(8,128)(2,1)} %get-tuple-element.52), channel_id=1, source_target_pairs={{0,64},{64,0},{128,192},{192,128},{1,65},{65,1},{129,193},{193,129... | collective-permute-start | bytes 3145736 | tf_op jit(solution)/shard_map/ppermute | solution.py:38
  91.7 1.0 copy-start
  98.9 39.3 %all-to-all-start = ((bf16[64,8,896]{2,1,0:T(8,128)(2,1)}), bf16[64,8,896]{2,1,0:T(8,128)(2,1)S(1)}, u32[]{:S(2)}, u32[]{:S(2)}) async-start(bf16[64,8,896]{2,1,0:T(8,128)(2,1)} %project.1), calls=%async_computation | async-start | bytes 1835008 | tf_op jit(solution)/shard_map/all_to_all | solution.py:195
  (2 other events, 1.5 us)
Sparse Core Ops, SparseCore 0:
  15.3 44.0 all-gather.2

commit v8 on v6

--- a/solution.py
+++ b/solution.py
@@ -16,8 +16,6 @@
 WHOLE = 384
 LANES = 2 * WHOLE + 128
 VMEM = 56 * 1024 * 1024
-
-OFFSETS = [(dy, dx) for dx in range(NX) for dy in range(NY)]
 
 
 def band_route(dy, dx, dz):
@@ -83,15 +81,13 @@
 
 
 def mix_body(place_ref, odd_ref, *refs):
-    near_ref, own_side, far_side, gathered_ref, kern_ref, half_ref = refs[:6]
-    m_ref, row_ref, col_ref, other_rows, other_cols = refs[6:]
+    rows, (gathered_ref, kern_ref, half_ref) = refs[:NY], refs[NY : NY + 3]
+    m_ref, row_ref, col_ref, other_rows, other_cols = refs[NY + 3 :]
     for i in range(NY):
-        at = pl.ds(pl.multiple_of(place_ref[i] * SLAB, SLAB), SLAB)
-        row_ref[:, at, :] = near_ref[i, 0]
-        other_rows[:, at, :] = near_ref[i, 1]
-        at = pl.ds(pl.multiple_of(place_ref[NY + i] * SLAB, SLAB), SLAB)
-        row_ref[:, at, :] = own_side[i]
-        other_rows[:, at, :] = far_side[i]
+        for side in range(NX):
+            at = pl.ds(pl.multiple_of(place_ref[i * NX + side] * SLAB, SLAB), SLAB)
+            row_ref[:, at, :] = rows[i][2 * side]
+            other_rows[:, at, :] = rows[i][2 * side + 1]
     for i in range(NZ):
         at = pl.ds(i * SLAB, SLAB)
         col_ref[:, at, :] = gathered_ref[i, 0]
@@ -203,23 +199,22 @@
     diff_core = swap_groups(pair_kdiff, 1)
     diff_far = swap_groups(pair_kdiff, 2)
     far = swap_groups(own, 2)
+    own_side, far_side = shift(own, 0, 1, 0), other_side(own)
 
     over_yx = [[g * NZ + z_at for g in range(GROUPS)] for z_at in range(NZ)]
     over_z = [[g * NZ + z_at for z_at in range(NZ)] for g in range(GROUPS)]
     sends = pack(odd, pair_kdiff, diff_core, diff_far, stored_kernel_index, kernels)
-    both = jnp.stack([own, far])
-    gathered = lax.all_gather(both, "band", axis_index_groups=over_z)
-    up, down = shift(both, 1, 0, 0), shift(both, -1, 0, 0)
+
+    gathered = lax.all_gather(jnp.stack([own, far]), "band", axis_index_groups=over_z)
+    four = jnp.stack([own, far, own_side, far_side])
+    up, down = shift(four, 1, 0, 0), shift(four, -1, 0, 0)
     sends, up, down = lax.optimization_barrier((sends, up, down))
+    over = shift(up, 1, 0, 0)
     kern = lax.all_to_all(sends, "band", 0, 0, axis_index_groups=over_yx)
     half = swap_groups(kern[:, 0], 1)
-    over = shift(up, 1, 0, 0)
-    near = jnp.stack([both, up, over, down])
-    own_side = shift(near[:, 0], 0, 1, 0)
-    far_side = other_side(near[:, 0])
-
-    place = jnp.stack([(y - dy) % NY * NX + (x - dx) % NX for dy, dx in OFFSETS])
-    m_out, own_rows, own_cols = mix(place, odd, near, own_side, far_side, gathered, kern, half)
+
+    place = jnp.stack([(y - dy) % NY * NX + (x - dx) % NX for dy in range(NY) for dx in range(NX)])
+    m_out, own_rows, own_cols = mix(place, odd, four, up, over, down, gathered, kern, half)
     m_own = swap_groups(m_out, 1)
     total = reduce_windows(project(m_own, own_rows, own_cols))
     flat = total.reshape(2, 8 * NB)

time: 138 us -> 140 us (1.014)
  blocking collectives: 0 us -> 23 us
  waiting for transfers between devices: 73 us -> 59 us
  starting transfers between devices: 25.8 us -> 18.7 us
    all_to_all x0 -> x1, blocking collectives: none -> 23 us  [on_device(): kern = lax.all_to_all(sends, 'band', 0, 0, axis_index_groups=over_yx)]
    ppermute x1, waiting for transfers between devices: 12.4 us -> 4.44 us  [other_side(): return lax.ppermute(block, ('kgrp', 'band'), both)]
    all_to_all x1 -> x0, starting transfers between devices: 5.98 us -> none  [on_device(): kern = lax.all_to_all(sends, 'band', 0, 0, axis_index_groups=over_yx)]
    ppermute x4, waiting for transfers between devices: 23.6 us -> 17.8 us  [shift(): return lax.ppermute(block, 'band', band_route(dy, dx, dz))]
    ppermute x4, starting transfers between devices: 5.42 us -> 3.01 us  [shift(): return lax.ppermute(block, 'band', band_route(dy, dx, dz))]
  transfers between devices with their start and end apart: 13 -> 12, of which waited for: 6 -> 8; matrix products, arithmetic and copies ran while one was open for 2% -> 1% of each run, Pallas kernels for 3% -> 3%
where the time goes in v8:
time: 140 us; the launch traced here: 138 us
  waiting for transfers between devices  59 us (42%)
  blocking collectives  23 us (16%)
  starting transfers between devices  18.7 us (13%)
  Pallas kernels  17.2 us (12%)
  between operations  14.2 us (10%)
  other arithmetic  3.51 us (3%)
  local copies, waits for them, and re-layouts  2.73 us (2%)
    all_to_all x1, waiting for transfers between devices, reduce_windows(): parts = lax.all_to_all(windows, 'band', 0, 0)  25.5 us
    all_to_all x1, blocking collectives, on_device(): kern = lax.all_to_all(sends, 'band', 0, 0, axis_index_groups=over_yx)  23 us
    ppermute x4, waiting for transfers between devices, shift(): return lax.ppermute(block, 'band', band_route(dy, dx, dz))  17.8 us
    ppermute x5, waiting for transfers between devices, swap_groups(): return lax.ppermute(block, 'kgrp', [(k, k ^ bit) for k in range(4)])  11.2 us
    all_to_all x1, starting transfers between devices, reduce_windows(): parts = lax.all_to_all(windows, 'band', 0, 0)  10.5 us
    pallas_call x1, Pallas kernels, mix(): pl.pallas_call(mix_body, out_shape=[jax.ShapeDtypeStruct((2, BLOCK, BLOCK...  6.46 us
    pallas_call x1, Pallas kernels, project(): pl.pallas_call(project_body, out_shape=jax.ShapeDtypeStruct((GROUPS * NZ,...  6.15 us
    pallas_call x1, Pallas kernels, pack(): pl.pallas_call(pack_body, out_shape=jax.ShapeDtypeStruct((GROUPS, 3, SLAB...  4.59 us
  transfers between devices with their start and end apart: 12, of which 8 were waited for; matrix products, arithmetic and copies ran while one was open for 1% of the time, Pallas kernels for 3%

profile of v8, /device:TPU:6, one launch (start us, length us, event | category | flops | bytes accessed | tf_op | source)
XLA Modules:
  0.0 138.4 jit_solution(15590030897442368187)
XLA Ops:
  6.5 1.4 %collective-permute-start = (bf16[2,64,432]{2,1,0:T(8,128)(2,1)}, bf16[2,64,432]{2,1,0:T(8,128)(2,1)S(1)}, u32[]{:S(2)}, u32[]{:S(2)}) collective-permute-start(bf16[2,64,432]{2,1,0:T(8,128)(2,1)} %bitcast.21), channel_id=1, source_target_pairs={{0,128},{64,192},{128,0},{192,64},{1,129},{65,193},{129,1},{193,65... | collective-permute-start | bytes 331784 | tf_op jit(solution)/shard_map/ppermute | solution.py:36
  7.9 5.5 %collective-permute-done = bf16[2,64,432]{2,1,0:T(8,128)(2,1)S(1)} collective-permute-done((bf16[2,64,432]{2,1,0:T(8,128)(2,1)}, bf16[2,64,432]{2,1,0:T(8,128)(2,1)S(1)}, u32[]{:S(2)}, u32[]{:S(2)}) %collective-permute-start) | collective-permute-done | bytes 110624 | tf_op jit(solution)/shard_map/ppermute | solution.py:36
  13.5 1.6 %pad_maximum_fusion.1 = bf16[2,2,64,432]{3,2,1,0:T(8,128)(2,1)} fusion(bf16[1,2,64,432]{3,2,1,0:T(8,128)(2,1)S(1)} %bitcast.24, bf16[1,2,64,432]{3,2,1,0:T(8,128)(2,1)} %param.4), kind=kLoop, calls=%fused_computation.3 | loop fusion | flops 110592 | bytes 442368 | tf_op jit(solution)/shard_map/stack | solution.py:208
  15.1 0.0 all-gather.3.cloned.1.call-update
  15.1 2.0 %collective-permute-start.2 = (bf16[2,64,432]{2,1,0:T(8,128)(2,1)}, bf16[2,64,432]{2,1,0:T(8,128)(2,1)S(1)}, u32[]{:S(2)}, u32[]{:S(2)}) collective-permute-start(bf16[2,64,432]{2,1,0:T(8,128)(2,1)} %bitcast.22), channel_id=1, source_target_pairs={{128,8},{129,9},{130,10},{131,11},{132,12},{133,13},{134,14},{135,... | collective-permute-start | bytes 331784 | tf_op jit(solution)/shard_map/ppermute | solution.py:42
  17.2 0.0 collective-permute-start.1
  17.2 4.4 %collective-permute-done.2 = bf16[2,64,432]{2,1,0:T(8,128)(2,1)S(1)} collective-permute-done((bf16[2,64,432]{2,1,0:T(8,128)(2,1)}, bf16[2,64,432]{2,1,0:T(8,128)(2,1)S(1)}, u32[]{:S(2)}, u32[]{:S(2)}) %collective-permute-start.2) | collective-permute-done | bytes 110624 | tf_op jit(solution)/shard_map/ppermute | solution.py:42
  21.6 0.7 collective-permute-done.1
  22.4 1.0 pad_maximum_fusion.refs_0_
  23.3 2.4 %collective-permute-start.6 = (bf16[4,2,64,432]{3,2,1,0:T(8,128)(2,1)S(1)}, bf16[4,2,64,432]{3,2,1,0:T(8,128)(2,1)S(1)}, u32[]{:S(2)}, u32[]{:S(2)}) collective-permute-start(bf16[4,2,64,432]{3,2,1,0:T(8,128)(2,1)S(1)} %pad_maximum_fusion.refs_0_), channel_id=1, source_target_pairs={{0,48},{1,49},{2,50},{3,51},{4,52},{5,53},{6,54},{7,55},{8,56},{9,... | collective-permute-start | bytes 1327112 | tf_op jit(solution)/shard_map/ppermute | solution.py:32
  25.7 0.0 collective-permute-start.5
  25.7 1.7 %collective-permute-start.4 = (s32[1]{0:T(128)}, s32[1]{0:T(128)}, u32[]{:S(2)}, u32[]{:S(2)}) collective-permute-start(s32[1]{0:T(128)} %param.6), channel_id=1, source_target_pairs={{0,128},{64,192},{128,0},{192,64},{1,129},{65,193},{129,1},{193,65... | collective-permute-start | bytes 20 | tf_op jit(solution)/shard_map/ppermute | solution.py:36
  28.1 2.7 %collective-permute-done.4.far_ref = s32[1]{0:T(128)} collective-permute-done((s32[1]{0:T(128)}, s32[1]{0:T(128)}, u32[]{:S(2)}, u32[]{:S(2)}) %collective-permute-start.4) | collective-permute-done | bytes 36 | tf_op jit(solution)/shard_map/ppermute | solution.py:36
  30.8 4.6 %pack.1 = bf16[8,3,64,512]{3,2,1,0:T(8,128)(2,1)} custom-call(s32[1]{0:T(128)} %bitcast.8.odd_ref, s32[1]{0:T(128)S(6)} %copy.9.own_ref, s32[1]{0:T(128)} %collective-permute-done.3.core_ref, s32[1]{0:T(128)} %collective-permute-done.4.far_ref, s32[8]{0:T(128)} %stored_ref.1, bf16[4,2,64,4096]{3,2,1,0:T(8,128)(2,1)} %kernels_ref.1), custom_call_target="tpu_custom_call" | custom-call | tf_op jit(solution)/shard_map/pack/pallas_call | solution.py:69
  35.5 2.8 %collective-permute-done.5.refs_1_ = bf16[4,2,64,432]{3,2,1,0:T(8,128)(2,1)S(1)} collective-permute-done((bf16[4,2,64,432]{3,2,1,0:T(8,128)(2,1)S(1)}, bf16[4,2,64,432]{3,2,1,0:T(8,128)(2,1)S(1)}, u32[]{:S(2)}, u32[]{:S(2)}) %collective-permute-start.5) | collective-permute-done | bytes 442400 | tf_op jit(solution)/shard_map/ppermute | solution.py:32
  38.3 23.0 %all_to_all.10.refs_5_ = bf16[8,3,64,512]{3,2,1,0:T(8,128)(2,1)S(1)} all-to-all(bf16[8,3,64,512]{3,2,1,0:T(8,128)(2,1)} %pack.1), channel_id=1, replica_groups={{0,8,16,24,32,40,48,56},{1,9,17,25,33,41,49,57},{2,10,18,26,34,42,50,58..., dimensions={0} | all-to-all | bytes 3145728 | tf_op jit(solution)/shard_map/all_to_all | solution.py:213
  61.4 0.1 collective-permute-start.8
  61.5 0.6 collective-permute-start.7
  62.1 0.6 stack.60.place_ref
  62.7 14.3 %collective-permute-done.7.refs_2_ = bf16[4,2,64,432]{3,2,1,0:T(8,128)(2,1)S(1)} collective-permute-done((bf16[4,2,64,432]{3,2,1,0:T(8,128)(2,1)S(1)}, bf16[4,2,64,432]{3,2,1,0:T(8,128)(2,1)S(1)}, u32[]{:S(2)}, u32[]{:S(2)}) %collective-permute-start.7) | collective-permute-done | bytes 442400 | tf_op jit(solution)/shard_map/ppermute | solution.py:32
  77.0 0.8 copy-done.5
  77.8 6.5 %mix.1 = (bf16[2,512,512]{2,1,0:T(8,128)(2,1)}, bf16[2,512,432]{2,1,0:T(8,128)(2,1)}, bf16[2,512,432]{2,1,0:T(8,128)(2,1)}) custom-call(s32[8]{0:T(128)} %stack.60.place_ref, s32[1]{0:T(128)} %bitcast.8.odd_ref, bf16[4,2,64,432]{3,2,1,0:T(8,128)(2,1)} %copy-done.1, bf16[4,2,64,432]{3,2,1,0:T(8,128)(2,1)} %copy-done.4, bf16[4,2,64,432]{3,2,1,0:T(8,128)(2,1)} %copy-done.5, ...), custom_call_target="tpu_custom_call" | custom-call | tf_op jit(solution)/shard_map/mix/pallas_call | solution.py:128
  84.3 2.9 %collective-permute-done.9.m_ref = bf16[2,512,512]{2,1,0:T(8,128)(2,1)S(1)} collective-permute-done((bf16[2,512,512]{2,1,0:T(8,128)(2,1)}, bf16[2,512,512]{2,1,0:T(8,128)(2,1)S(1)}, u32[]{:S(2)}, u32[]{:S(2)}) %collective-permute-start.9) | collective-permute-done | bytes 1048608 | tf_op jit(solution)/shard_map/ppermute | solution.py:36
  87.2 1.0 copy-done.2
  88.2 6.1 %project.1 = bf16[64,8,896]{2,1,0:T(8,128)(2,1)} custom-call(bf16[2,512,512]{2,1,0:T(8,128)(2,1)} %copy-done.2, bf16[2,512,432]{2,1,0:T(8,128)(2,1)} %get-tuple-element.15.row_ref, bf16[2,512,432]{2,1,0:T(8,128)(2,1)} %get-tuple-element.16.col_ref), custom_call_target="tpu_custom_call" | custom-call | tf_op jit(solution)/shard_map/project/pallas_call | solution.py:171
  94.3 10.5 %all-to-all-start.1 = ((bf16[64,8,896]{2,1,0:T(8,128)(2,1)}), bf16[64,8,896]{2,1,0:T(8,128)(2,1)S(1)}, u32[]{:S(2)}, u32[]{:S(2)}) async-start(bf16[64,8,896]{2,1,0:T(8,128)(2,1)} %project.1), calls=%async_computation.1 | async-start | bytes 1835008 | tf_op jit(solution)/shard_map/all_to_all | solution.py:183
  104.8 25.5 %all-to-all-done.1 = bf16[64,8,896]{2,1,0:T(8,128)(2,1)S(1)} async-done(((bf16[64,8,896]{2,1,0:T(8,128)(2,1)}), bf16[64,8,896]{2,1,0:T(8,128)(2,1)S(1)}, u32[]{:S(2)}, u32[]{:S(2)}) %all-to-all-start.1) | async-done | bytes 917536 | tf_op jit(solution)/shard_map/all_to_all | solution.py:183
  130.3 0.2 convert_reduce_fusion
  130.5 0.1 fusion.3
  130.6 0.1 stack.66
  130.7 0.1 stack.67
  130.8 0.7 fusion.1
  (20 shorter events, 0.1 us)
Async XLA Ops:
  6.5 70.5 %all-gather.3.cloned.1.call-start = ((), (), s32[]{:S(2)}) async-start(), calls=%async_computation.2 | async-start | bytes 2359296 | tf_op jit(solution)/shard_map/all_gather | solution.py:208
  6.5 7.0 %collective-permute-start = (bf16[2,64,432]{2,1,0:T(8,128)(2,1)}, bf16[2,64,432]{2,1,0:T(8,128)(2,1)S(1)}, u32[]{:S(2)}, u32[]{:S(2)}) collective-permute-start(bf16[2,64,432]{2,1,0:T(8,128)(2,1)} %bitcast.21), channel_id=1, source_target_pairs={{0,128},{64,192},{128,0},{192,64},{1,129},{65,193},{129,1},{193,65... | collective-permute-start | bytes 331784 | tf_op jit(solution)/shard_map/ppermute | solution.py:36
  15.1 6.5 %collective-permute-start.2 = (bf16[2,64,432]{2,1,0:T(8,128)(2,1)}, bf16[2,64,432]{2,1,0:T(8,128)(2,1)S(1)}, u32[]{:S(2)}, u32[]{:S(2)}) collective-permute-start(bf16[2,64,432]{2,1,0:T(8,128)(2,1)} %bitcast.22), channel_id=1, source_target_pairs={{128,8},{129,9},{130,10},{131,11},{132,12},{133,13},{134,14},{135,... | collective-permute-start | bytes 331784 | tf_op jit(solution)/shard_map/ppermute | solution.py:42
  17.2 5.2 %collective-permute-start.1 = (bf16[2,64,432]{2,1,0:T(8,128)(2,1)}, bf16[2,64,432]{2,1,0:T(8,128)(2,1)S(1)}, u32[]{:S(2)}, u32[]{:S(2)}) collective-permute-start(bf16[2,64,432]{2,1,0:T(8,128)(2,1)} %bitcast.23), channel_id=1, source_target_pairs={{0,8},{1,9},{2,10},{3,11},{4,12},{5,13},{6,14},{7,15},{8,0},{9,1},... | collective-permute-start | bytes 331784 | tf_op jit(solution)/shard_map/ppermute | solution.py:32
  23.3 12.1 %copy-start.1 = (bf16[4,2,64,432]{3,2,1,0:T(8,128)(2,1)}, bf16[4,2,64,432]{3,2,1,0:T(8,128)(2,1)S(1)}, u32[]{:S(2)}) copy-start(bf16[4,2,64,432]{3,2,1,0:T(8,128)(2,1)S(1)} %pad_maximum_fusion.refs_0_) | copy-start | bytes 1327108
  23.3 12.1 %collective-permute-start.6 = (bf16[4,2,64,432]{3,2,1,0:T(8,128)(2,1)S(1)}, bf16[4,2,64,432]{3,2,1,0:T(8,128)(2,1)S(1)}, u32[]{:S(2)}, u32[]{:S(2)}) collective-permute-start(bf16[4,2,64,432]{3,2,1,0:T(8,128)(2,1)S(1)} %pad_maximum_fusion.refs_0_), channel_id=1, source_target_pairs={{0,48},{1,49},{2,50},{3,51},{4,52},{5,53},{6,54},{7,55},{8,56},{9,... | collective-permute-start | bytes 1327112 | tf_op jit(solution)/shard_map/ppermute | solution.py:32
  25.7 12.6 %collective-permute-start.5 = (bf16[4,2,64,432]{3,2,1,0:T(8,128)(2,1)S(1)}, bf16[4,2,64,432]{3,2,1,0:T(8,128)(2,1)S(1)}, u32[]{:S(2)}, u32[]{:S(2)}) collective-permute-start(bf16[4,2,64,432]{3,2,1,0:T(8,128)(2,1)S(1)} %pad_maximum_fusion.refs_0_), channel_id=1, source_target_pairs={{0,16},{1,17},{2,18},{3,19},{4,20},{5,21},{6,22},{7,23},{8,24},{9,... | collective-permute-start | bytes 1327112 | tf_op jit(solution)/shard_map/ppermute | solution.py:32
  25.7 2.4 %collective-permute-start.3 = (s32[1]{0:T(128)}, s32[1]{0:T(128)}, u32[]{:S(2)}, u32[]{:S(2)}) collective-permute-start(s32[1]{0:T(128)} %param.6), channel_id=1, source_target_pairs={{0,64},{64,0},{128,192},{192,128},{1,65},{65,1},{129,193},{193,129... | collective-permute-start | bytes 20 | tf_op jit(solution)/shard_map/ppermute | solution.py:36
  25.7 5.1 %collective-permute-start.4 = (s32[1]{0:T(128)}, s32[1]{0:T(128)}, u32[]{:S(2)}, u32[]{:S(2)}) collective-permute-start(s32[1]{0:T(128)} %param.6), channel_id=1, source_target_pairs={{0,128},{64,192},{128,0},{192,64},{1,129},{65,193},{129,1},{193,65... | collective-permute-start | bytes 20 | tf_op jit(solution)/shard_map/ppermute | solution.py:36
  35.5 25.9 %copy-start.3 = (bf16[4,2,64,432]{3,2,1,0:T(8,128)(2,1)}, bf16[4,2,64,432]{3,2,1,0:T(8,128)(2,1)S(1)}, u32[]{:S(2)}) copy-start(bf16[4,2,64,432]{3,2,1,0:T(8,128)(2,1)S(1)} %collective-permute-done.6.refs_3_) | copy-start | bytes 1327108
  38.3 23.2 %copy-start.4 = (bf16[4,2,64,432]{3,2,1,0:T(8,128)(2,1)}, bf16[4,2,64,432]{3,2,1,0:T(8,128)(2,1)S(1)}, u32[]{:S(2)}) copy-start(bf16[4,2,64,432]{3,2,1,0:T(8,128)(2,1)S(1)} %collective-permute-done.5.refs_1_) | copy-start | bytes 1327108
  61.3 15.7 %copy-start = (bf16[8,3,64,512]{3,2,1,0:T(8,128)(2,1)}, bf16[8,3,64,512]{3,2,1,0:T(8,128)(2,1)S(1)}, u32[]{:S(2)}) copy-start(bf16[8,3,64,512]{3,2,1,0:T(8,128)(2,1)S(1)} %all_to_all.10.refs_5_) | copy-start | bytes 4718596
  61.4 15.7 %collective-permute-start.8 = (bf16[8,64,512]{2,1,0:T(8,128)(2,1)S(1)}, bf16[8,64,512]{2,1,0:T(8,128)(2,1)}, u32[]{:S(2)}, u32[]{:S(2)}) collective-permute-start(bf16[8,64,512]{2,1,0:T(8,128)(2,1)S(1)} %slice_bitcast_fusion), channel_id=1, source_target_pairs={{0,64},{64,0},{128,192},{192,128},{1,65},{65,1},{129,193},{193,129... | collective-permute-start | bytes 1572872 | tf_op jit(solution)/shard_map/ppermute | solution.py:36
  61.5 15.5 %collective-permute-start.7 = (bf16[4,2,64,432]{3,2,1,0:T(8,128)(2,1)S(1)}, bf16[4,2,64,432]{3,2,1,0:T(8,128)(2,1)S(1)}, u32[]{:S(2)}, u32[]{:S(2)}) collective-permute-start(bf16[4,2,64,432]{3,2,1,0:T(8,128)(2,1)S(1)} %collective-permute-done.5.refs_1_), channel_id=1, source_target_pairs={{0,16},{1,17},{2,18},{3,19},{4,20},{5,21},{6,22},{7,23},{8,24},{9,... | collective-permute-start | bytes 1327112 | tf_op jit(solution)/shard_map/ppermute | solution.py:32
  77.0 0.8 copy-start.5
  84.3 2.9 %collective-permute-start.9 = (bf16[2,512,512]{2,1,0:T(8,128)(2,1)}, bf16[2,512,512]{2,1,0:T(8,128)(2,1)S(1)}, u32[]{:S(2)}, u32[]{:S(2)}) collective-permute-start(bf16[2,512,512]{2,1,0:T(8,128)(2,1)} %get-tuple-element.14), channel_id=1, source_target_pairs={{0,64},{64,0},{128,192},{192,128},{1,65},{65,1},{129,193},{193,129... | collective-permute-start | bytes 3145736 | tf_op jit(solution)/shard_map/ppermute | solution.py:36
  87.2 1.0 copy-start.2
  94.3 36.0 %all-to-all-start.1 = ((bf16[64,8,896]{2,1,0:T(8,128)(2,1)}), bf16[64,8,896]{2,1,0:T(8,128)(2,1)S(1)}, u32[]{:S(2)}, u32[]{:S(2)}) async-start(bf16[64,8,896]{2,1,0:T(8,128)(2,1)} %project.1), calls=%async_computation.1 | async-start | bytes 1835008 | tf_op jit(solution)/shard_map/all_to_all | solution.py:183
Sparse Core Ops, SparseCore 0:
  15.3 44.3 all-gather.2

commit v9 on v8

--- a/solution.py
+++ b/solution.py
@@ -46,7 +46,7 @@
     return lax.dot_general(a, b, ((dims[0], dims[1]), ((), ())), preferred_element_type=jnp.float32)
 
 
-def pack_body(odd_ref, own_ref, core_ref, far_ref, stored_ref, kernels_ref, out_ref, held, sem):
+def pack_body(odd_ref, own_ref, core_ref, far_ref, stored_ref, kernels_ref, shared_ref, single_ref, held, sem):
     odd = odd_ref[0] == 1
     own, core, far = stored_ref[own_ref[0]], stored_ref[core_ref[0]], stored_ref[far_ref[0]]
     shared = jnp.where(odd, own, core)
@@ -61,16 +61,23 @@
     for which, copy in enumerate(copies):
         copy.wait()
         for i in range(GROUPS):
-            out_ref[i, which] = held[which, :, pl.ds(i * BLOCK, BLOCK)]
+            block = held[which, :, pl.ds(i * BLOCK, BLOCK)]
+            if which == 0:
+                shared_ref[i] = block
+            else:
+                single_ref[i, which - 1] = block
 
 
 def pack(odd, own, core, far, stored, kernels):
     smem = pl.BlockSpec(memory_space=pltpu.SMEM)
     return pl.pallas_call(
         pack_body,
-        out_shape=jax.ShapeDtypeStruct((GROUPS, 3, SLAB, BLOCK), jnp.bfloat16),
+        out_shape=[
+            jax.ShapeDtypeStruct((GROUPS, SLAB, BLOCK), jnp.bfloat16),
+            jax.ShapeDtypeStruct((GROUPS, 2, SLAB, BLOCK), jnp.bfloat16),
+        ],
         in_specs=[smem] * 5 + [pl.BlockSpec(memory_space=pl.ANY)],
-        out_specs=pl.BlockSpec(memory_space=pltpu.VMEM),
+        out_specs=[pl.BlockSpec(memory_space=pltpu.VMEM)] * 2,
         scratch_shapes=[
             pltpu.VMEM((3, SLAB, GROUPS * BLOCK), jnp.bfloat16),
             pltpu.SemaphoreType.DMA((3,)),
@@ -81,13 +88,17 @@
 
 
 def mix_body(place_ref, odd_ref, *refs):
-    rows, (gathered_ref, kern_ref, half_ref) = refs[:NY], refs[NY : NY + 3]
-    m_ref, row_ref, col_ref, other_rows, other_cols = refs[NY + 3 :]
+    four_ref, up_ref, over_here, over_side, down_ref, gathered_ref = refs[:6]
+    mine_ref, half_ref, kern_ref = refs[6:9]
+    m_ref, row_ref, col_ref, other_rows, other_cols = refs[9:]
+    rows = ((four_ref, four_ref), (up_ref, up_ref), (over_here, over_side), (down_ref, down_ref))
     for i in range(NY):
         for side in range(NX):
             at = pl.ds(pl.multiple_of(place_ref[i * NX + side] * SLAB, SLAB), SLAB)
-            row_ref[:, at, :] = rows[i][2 * side]
-            other_rows[:, at, :] = rows[i][2 * side + 1]
+            piece = rows[i][side]
+            first = 0 if piece is over_side else 2 * side
+            row_ref[:, at, :] = piece[first]
+            other_rows[:, at, :] = piece[first + 1]
     for i in range(NZ):
         at = pl.ds(i * SLAB, SLAB)
         col_ref[:, at, :] = gathered_ref[i, 0]
@@ -106,15 +117,15 @@
     for part in range(2):
         at = pl.ds(part * per, per)
         p_re, p_im = density(row_ref, col_ref, at)
-        mine = kern_ref[:, 0, :, at].reshape(BLOCK, per)
+        mine = mine_ref[:, :, at].reshape(BLOCK, per)
         other = half_ref[:, :, at].reshape(BLOCK, per)
         k_re = jnp.where(odd, other, mine).astype(jnp.float32)
         k_im = jnp.where(odd, mine, other).astype(jnp.float32) * sign
         total_re = k_re * p_re - k_im * p_im
         total_im = k_re * p_im + k_im * p_re
         p_re, p_im = density(other_rows, other_cols, at)
-        k_re = kern_ref[:, 1, :, at].reshape(BLOCK, per).astype(jnp.float32)
-        k_im = kern_ref[:, 2, :, at].reshape(BLOCK, per).astype(jnp.float32) * -sign
+        k_re = kern_ref[:, 0, :, at].reshape(BLOCK, per).astype(jnp.float32)
+        k_im = kern_ref[:, 1, :, at].reshape(BLOCK, per).astype(jnp.float32) * -sign
         total_re += k_re * p_re - k_im * p_im
         total_im += k_re * p_im + k_im * p_re
         m_ref[0, :, at] = total_re.astype(jnp.bfloat16)
@@ -200,6 +211,7 @@
     diff_far = swap_groups(pair_kdiff, 2)
     far = swap_groups(own, 2)
     own_side, far_side = shift(own, 0, 1, 0), other_side(own)
+    far, own_side, far_side = lax.optimization_barrier((far, own_side, far_side))
 
     over_yx = [[g * NZ + z_at for g in range(GROUPS)] for z_at in range(NZ)]
     over_z = [[g * NZ + z_at for z_at in range(NZ)] for g in range(GROUPS)]
@@ -208,13 +220,18 @@
     gathered = lax.all_gather(jnp.stack([own, far]), "band", axis_index_groups=over_z)
     four = jnp.stack([own, far, own_side, far_side])
     up, down = shift(four, 1, 0, 0), shift(four, -1, 0, 0)
-    sends, up, down = lax.optimization_barrier((sends, up, down))
-    over = shift(up, 1, 0, 0)
-    kern = lax.all_to_all(sends, "band", 0, 0, axis_index_groups=over_yx)
-    half = swap_groups(kern[:, 0], 1)
+    shared, single = sends
+    shared, up, down = lax.optimization_barrier((shared, up, down))
+    over = shift(up[:2], 1, 0, 0), shift(down[2:], -1, 0, 0)
+    mine = lax.all_to_all(shared, "band", 0, 0, axis_index_groups=over_yx)
+    half = swap_groups(mine, 1)
+    single, over = lax.optimization_barrier((single, over))
+    kern = lax.all_to_all(single, "band", 0, 0, axis_index_groups=over_yx)
 
     place = jnp.stack([(y - dy) % NY * NX + (x - dx) % NX for dy in range(NY) for dx in range(NX)])
-    m_out, own_rows, own_cols = mix(place, odd, four, up, over, down, gathered, kern, half)
+    m_out, own_rows, own_cols = mix(
+        place, odd, four, up, *over, down, gathered, mine, half, kern
+    )
     m_own = swap_groups(m_out, 1)
     total = reduce_windows(project(m_own, own_rows, own_cols))
     flat = total.reshape(2, 8 * NB)

time: 140 us -> 135 us (0.964)
  blocking collectives: 23 us -> 0 us
  starting transfers between devices: 18.7 us -> 30.2 us
  waiting for transfers between devices: 59 us -> 65.3 us
    all_to_all x1 -> x0, blocking collectives: 23 us -> none  [on_device(): kern = lax.all_to_all(sends, 'band', 0, 0, axis_index_groups=over_yx)]
    all_to_all x0 -> x2, waiting for transfers between devices: none -> 12 us  [the longest x1 12 us: on_device(): kern = lax.all_to_all(single, 'band', 0, 0, axis_index_groups=over_yx)]
    all_to_all x0 -> x2, starting transfers between devices: none -> 7.83 us  [the longest x1 4.33 us: on_device(): kern = lax.all_to_all(single, 'band', 0, 0, axis_index_groups=over_yx)]
    ppermute x4 -> x5, waiting for transfers between devices: 17.8 us -> 14.3 us  [shift(): return lax.ppermute(block, 'band', band_route(dy, dx, dz))]
    ppermute x4 -> x5, starting transfers between devices: 3.01 us -> 5.89 us  [shift(): return lax.ppermute(block, 'band', band_route(dy, dx, dz))]
    ppermute x1, waiting for transfers between devices: 4.44 us -> 2.24 us  [other_side(): return lax.ppermute(block, ('kgrp', 'band'), both)]
  transfers between devices with their start and end apart: 12 -> 15, of which waited for: 8 -> 12; matrix products, arithmetic and copies ran while one was open for 1% -> 1% of each run, Pallas kernels for 3% -> 3%
where the time goes in v9:
time: 135 us; the launch traced here: 133 us
  waiting for transfers between devices  65.3 us (48%)
  starting transfers between devices  30.2 us (22%)
  Pallas kernels  17.1 us (13%)
  between operations  14.2 us (11%)
  other arithmetic  3.51 us (3%)
  local copies, waits for them, and re-layouts  2.91 us (2%)
    all_to_all x1, waiting for transfers between devices, reduce_windows(): parts = lax.all_to_all(windows, 'band', 0, 0)  25.5 us
    ppermute x5, waiting for transfers between devices, shift(): return lax.ppermute(block, 'band', band_route(dy, dx, dz))  14.3 us
    all_to_all x1, waiting for transfers between devices, on_device(): kern = lax.all_to_all(single, 'band', 0, 0, axis_index_groups=over_yx)  12 us
    ppermute x5, waiting for transfers between devices, swap_groups(): return lax.ppermute(block, 'kgrp', [(k, k ^ bit) for k in range(4)])  11.1 us
    all_to_all x1, starting transfers between devices, reduce_windows(): parts = lax.all_to_all(windows, 'band', 0, 0)  11.1 us
    pallas_call x1, Pallas kernels, mix(): pl.pallas_call(mix_body, out_shape=[jax.ShapeDtypeStruct((2, BLOCK, BLOCK...  6.5 us
    pallas_call x1, Pallas kernels, project(): pl.pallas_call(project_body, out_shape=jax.ShapeDtypeStruct((GROUPS * NZ,...  6.15 us
    ppermute x5, starting transfers between devices, shift(): return lax.ppermute(block, 'band', band_route(dy, dx, dz))  5.89 us
  transfers between devices with their start and end apart: 15, of which 12 were waited for; matrix products, arithmetic and copies ran while one was open for 1% of the time, Pallas kernels for 3%

profile of v9, /device:TPU:6, one launch (start us, length us, event | category | flops | bytes accessed | tf_op | source)
XLA Modules:
  0.0 133.2 jit_solution(12355734243444224468)
XLA Ops:
  6.5 2.2 %collective-permute-start.2 = (bf16[2,64,432]{2,1,0:T(8,128)(2,1)}, bf16[2,64,432]{2,1,0:T(8,128)(2,1)S(1)}, u32[]{:S(2)}, u32[]{:S(2)}) collective-permute-start(bf16[2,64,432]{2,1,0:T(8,128)(2,1)} %bitcast.17), channel_id=1, source_target_pairs={{128,8},{129,9},{130,10},{131,11},{132,12},{133,13},{134,14},{135,... | collective-permute-start | bytes 331784 | tf_op jit(solution)/shard_map/ppermute | solution.py:42
  8.8 2.5 %collective-permute-start = (bf16[2,64,432]{2,1,0:T(8,128)(2,1)}, bf16[2,64,432]{2,1,0:T(8,128)(2,1)S(1)}, u32[]{:S(2)}, u32[]{:S(2)}) collective-permute-start(bf16[2,64,432]{2,1,0:T(8,128)(2,1)} %bitcast.19), channel_id=1, source_target_pairs={{0,128},{64,192},{128,0},{192,64},{1,129},{65,193},{129,1},{193,65... | collective-permute-start | bytes 331784 | tf_op jit(solution)/shard_map/ppermute | solution.py:36
  11.2 2.2 %collective-permute-done.2 = bf16[2,64,432]{2,1,0:T(8,128)(2,1)S(1)} collective-permute-done((bf16[2,64,432]{2,1,0:T(8,128)(2,1)}, bf16[2,64,432]{2,1,0:T(8,128)(2,1)S(1)}, u32[]{:S(2)}, u32[]{:S(2)}) %collective-permute-start.2) | collective-permute-done | bytes 110624 | tf_op jit(solution)/shard_map/ppermute | solution.py:42
  13.5 0.5 collective-permute-done.1
  13.9 3.3 %collective-permute-done = bf16[2,64,432]{2,1,0:T(8,128)(2,1)S(1)} collective-permute-done((bf16[2,64,432]{2,1,0:T(8,128)(2,1)}, bf16[2,64,432]{2,1,0:T(8,128)(2,1)S(1)}, u32[]{:S(2)}, u32[]{:S(2)}) %collective-permute-start) | collective-permute-done | bytes 110624 | tf_op jit(solution)/shard_map/ppermute | solution.py:36
  17.2 1.6 %pad_maximum_fusion.1 = bf16[2,2,64,432]{3,2,1,0:T(8,128)(2,1)} fusion(bf16[1,2,64,432]{3,2,1,0:T(8,128)(2,1)S(1)} %bitcast.20, bf16[1,2,64,432]{3,2,1,0:T(8,128)(2,1)} %param.4), kind=kLoop, calls=%fused_computation.2 | loop fusion | flops 110592 | bytes 442368 | tf_op jit(solution)/shard_map/stack | solution.py:220
  18.8 1.0 pad_maximum_fusion.refs_0_
  19.8 3.1 %collective-permute-start.6 = (bf16[4,2,64,432]{3,2,1,0:T(8,128)(2,1)S(1)}, bf16[4,2,64,432]{3,2,1,0:T(8,128)(2,1)S(1)}, u32[]{:S(2)}, u32[]{:S(2)}) collective-permute-start(bf16[4,2,64,432]{3,2,1,0:T(8,128)(2,1)S(1)} %pad_maximum_fusion.refs_0_), channel_id=1, source_target_pairs={{0,48},{1,49},{2,50},{3,51},{4,52},{5,53},{6,54},{7,55},{8,56},{9,... | collective-permute-start | bytes 1327112 | tf_op jit(solution)/shard_map/ppermute | solution.py:32
  22.9 0.7 collective-permute-start.4
  24.4 3.7 %collective-permute-done.4.far_ref = s32[1]{0:T(128)} collective-permute-done((s32[1]{0:T(128)}, s32[1]{0:T(128)}, u32[]{:S(2)}, u32[]{:S(2)}) %collective-permute-start.4) | collective-permute-done | bytes 36 | tf_op jit(solution)/shard_map/ppermute | solution.py:36
  28.1 4.5 %pack.1 = (bf16[8,64,512]{2,1,0:T(8,128)(2,1)}, bf16[8,2,64,512]{3,2,1,0:T(8,128)(2,1)}) custom-call(s32[1]{0:T(128)} %bitcast.8.odd_ref, s32[1]{0:T(128)S(6)} %copy.5.own_ref, s32[1]{0:T(128)} %collective-permute-done.3.core_ref, s32[1]{0:T(128)} %collective-permute-done.4.far_ref, s32[8]{0:T(128)} %stored_ref.1, bf16[4,2,64,4096]{3,2,1,0:T(8,128)(2,1)} %kernels_ref.1), custom_call_target="tpu_custom_call" | custom-call | tf_op jit(solution)/shard_map/pack/pallas_call | solution.py:73
  32.5 0.1 collective-permute-done.6.refs_4_
  32.6 3.4 %collective-permute-done.5.refs_1_ = bf16[4,2,64,432]{3,2,1,0:T(8,128)(2,1)S(1)} collective-permute-done((bf16[4,2,64,432]{3,2,1,0:T(8,128)(2,1)S(1)}, bf16[4,2,64,432]{3,2,1,0:T(8,128)(2,1)S(1)}, u32[]{:S(2)}, u32[]{:S(2)}) %collective-permute-start.5) | collective-permute-done | bytes 442400 | tf_op jit(solution)/shard_map/ppermute | solution.py:32
  36.0 3.5 %all-to-all-start = ((bf16[8,64,512]{2,1,0:T(8,128)(2,1)}), bf16[8,64,512]{2,1,0:T(8,128)(2,1)S(1)}, u32[]{:S(2)}, u32[]{:S(2)}) async-start(bf16[8,64,512]{2,1,0:T(8,128)(2,1)} %get-tuple-element.28), calls=%async_computation | async-start | bytes 1048576 | tf_op jit(solution)/shard_map/all_to_all | solution.py:226
  39.6 2.8 %collective-permute-start.8 = (bf16[2,2,64,432]{3,2,1,0:T(8,128)(2,1)S(1)}, bf16[2,2,64,432]{3,2,1,0:T(8,128)(2,1)S(1)}, u32[]{:S(2)}, u32[]{:S(2)}) collective-permute-start(bf16[2,2,64,432]{3,2,1,0:T(8,128)(2,1)S(1)} %slice.19), channel_id=1, source_target_pairs={{0,48},{1,49},{2,50},{3,51},{4,52},{5,53},{6,54},{7,55},{8,56},{9,... | collective-permute-start | bytes 663560 | tf_op jit(solution)/shard_map/ppermute | solution.py:32
  42.4 9.0 %collective-permute-done.8.refs_3_ = bf16[2,2,64,432]{3,2,1,0:T(8,128)(2,1)S(1)} collective-permute-done((bf16[2,2,64,432]{3,2,1,0:T(8,128)(2,1)S(1)}, bf16[2,2,64,432]{3,2,1,0:T(8,128)(2,1)S(1)}, u32[]{:S(2)}, u32[]{:S(2)}) %collective-permute-start.8) | collective-permute-done | bytes 221216 | tf_op jit(solution)/shard_map/ppermute | solution.py:32
  51.4 1.4 %collective-permute-done.7.refs_2_ = bf16[2,2,64,432]{3,2,1,0:T(8,128)(2,1)S(1)} collective-permute-done((bf16[2,2,64,432]{3,2,1,0:T(8,128)(2,1)S(1)}, bf16[2,2,64,432]{3,2,1,0:T(8,128)(2,1)S(1)}, u32[]{:S(2)}, u32[]{:S(2)}) %collective-permute-start.7) | collective-permute-done | bytes 221216 | tf_op jit(solution)/shard_map/ppermute | solution.py:32
  52.8 4.3 %all-to-all-start.1 = ((bf16[8,2,64,512]{3,2,1,0:T(8,128)(2,1)}), bf16[8,2,64,512]{3,2,1,0:T(8,128)(2,1)S(1)}, u32[]{:S(2)}, u32[]{:S(2)}) async-start(bf16[8,2,64,512]{3,2,1,0:T(8,128)(2,1)} %get-tuple-element.29), calls=%async_computation.1 | async-start | bytes 2097152 | tf_op jit(solution)/shard_map/all_to_all | solution.py:229
  57.1 0.6 stack.60.place_ref
  57.7 1.3 collective-permute-done.9.refs_7_
  59.0 12.0 %all-to-all-done.1.refs_8_ = bf16[8,2,64,512]{3,2,1,0:T(8,128)(2,1)S(1)} async-done(((bf16[8,2,64,512]{3,2,1,0:T(8,128)(2,1)}), bf16[8,2,64,512]{3,2,1,0:T(8,128)(2,1)S(1)}, u32[]{:S(2)}, u32[]{:S(2)}) %all-to-all-start.1) | async-done | bytes 1048608 | tf_op jit(solution)/shard_map/all_to_all | solution.py:229
  71.1 1.0 copy-done
  72.1 6.5 %mix.1 = (bf16[2,512,512]{2,1,0:T(8,128)(2,1)}, bf16[2,512,432]{2,1,0:T(8,128)(2,1)}, bf16[2,512,432]{2,1,0:T(8,128)(2,1)}) custom-call(s32[8]{0:T(128)} %stack.60.place_ref, s32[1]{0:T(128)} %bitcast.8.odd_ref, bf16[4,2,64,432]{3,2,1,0:T(8,128)(2,1)} %copy-done.1, bf16[4,2,64,432]{3,2,1,0:T(8,128)(2,1)} %copy-done.4, bf16[2,2,64,432]{3,2,1,0:T(8,128)(2,1)} %copy-done.8, ...), custom_call_target="tpu_custom_call" | custom-call | tf_op jit(solution)/shard_map/mix/pallas_call | solution.py:139
  78.6 2.9 %collective-permute-done.10.m_ref = bf16[2,512,512]{2,1,0:T(8,128)(2,1)S(1)} collective-permute-done((bf16[2,512,512]{2,1,0:T(8,128)(2,1)}, bf16[2,512,512]{2,1,0:T(8,128)(2,1)S(1)}, u32[]{:S(2)}, u32[]{:S(2)}) %collective-permute-start.10) | collective-permute-done | bytes 1048608 | tf_op jit(solution)/shard_map/ppermute | solution.py:36
  81.5 1.0 copy-done.5
  82.5 6.1 %project.1 = bf16[64,8,896]{2,1,0:T(8,128)(2,1)} custom-call(bf16[2,512,512]{2,1,0:T(8,128)(2,1)} %copy-done.5, bf16[2,512,432]{2,1,0:T(8,128)(2,1)} %get-tuple-element.31.row_ref, bf16[2,512,432]{2,1,0:T(8,128)(2,1)} %get-tuple-element.32.col_ref), custom_call_target="tpu_custom_call" | custom-call | tf_op jit(solution)/shard_map/project/pallas_call | solution.py:182
  88.6 11.1 %all-to-all-start.2 = ((bf16[64,8,896]{2,1,0:T(8,128)(2,1)}), bf16[64,8,896]{2,1,0:T(8,128)(2,1)S(1)}, u32[]{:S(2)}, u32[]{:S(2)}) async-start(bf16[64,8,896]{2,1,0:T(8,128)(2,1)} %project.1), calls=%async_computation.2 | async-start | bytes 1835008 | tf_op jit(solution)/shard_map/all_to_all | solution.py:194
  99.7 25.5 %all-to-all-done.2 = bf16[64,8,896]{2,1,0:T(8,128)(2,1)S(1)} async-done(((bf16[64,8,896]{2,1,0:T(8,128)(2,1)}), bf16[64,8,896]{2,1,0:T(8,128)(2,1)S(1)}, u32[]{:S(2)}, u32[]{:S(2)}) %all-to-all-start.2) | async-done | bytes 917536 | tf_op jit(solution)/shard_map/all_to_all | solution.py:194
  125.2 0.2 convert_reduce_fusion
  125.5 0.1 stack.66
  125.5 0.1 stack.67
  125.6 0.7 fusion.1
  (32 shorter events, 0.2 us)
Async XLA Ops:
  6.5 64.6 %all-gather.3.cloned.1.call-start = ((), (), s32[]{:S(2)}) async-start(), calls=%async_computation.3 | async-start | bytes 2359296 | tf_op jit(solution)/shard_map/all_gather | solution.py:220
  6.5 6.9 %collective-permute-start.2 = (bf16[2,64,432]{2,1,0:T(8,128)(2,1)}, bf16[2,64,432]{2,1,0:T(8,128)(2,1)S(1)}, u32[]{:S(2)}, u32[]{:S(2)}) collective-permute-start(bf16[2,64,432]{2,1,0:T(8,128)(2,1)} %bitcast.17), channel_id=1, source_target_pairs={{128,8},{129,9},{130,10},{131,11},{132,12},{133,13},{134,14},{135,... | collective-permute-start | bytes 331784 | tf_op jit(solution)/shard_map/ppermute | solution.py:42
  8.8 5.2 %collective-permute-start.1 = (bf16[2,64,432]{2,1,0:T(8,128)(2,1)}, bf16[2,64,432]{2,1,0:T(8,128)(2,1)S(1)}, u32[]{:S(2)}, u32[]{:S(2)}) collective-permute-start(bf16[2,64,432]{2,1,0:T(8,128)(2,1)} %bitcast.18), channel_id=1, source_target_pairs={{0,8},{1,9},{2,10},{3,11},{4,12},{5,13},{6,14},{7,15},{8,0},{9,1},... | collective-permute-start | bytes 331784 | tf_op jit(solution)/shard_map/ppermute | solution.py:32
  8.8 8.4 %collective-permute-start = (bf16[2,64,432]{2,1,0:T(8,128)(2,1)}, bf16[2,64,432]{2,1,0:T(8,128)(2,1)S(1)}, u32[]{:S(2)}, u32[]{:S(2)}) collective-permute-start(bf16[2,64,432]{2,1,0:T(8,128)(2,1)} %bitcast.19), channel_id=1, source_target_pairs={{0,128},{64,192},{128,0},{192,64},{1,129},{65,193},{129,1},{193,65... | collective-permute-start | bytes 331784 | tf_op jit(solution)/shard_map/ppermute | solution.py:36
  19.8 12.7 %copy-start.1 = (bf16[4,2,64,432]{3,2,1,0:T(8,128)(2,1)}, bf16[4,2,64,432]{3,2,1,0:T(8,128)(2,1)S(1)}, u32[]{:S(2)}) copy-start(bf16[4,2,64,432]{3,2,1,0:T(8,128)(2,1)S(1)} %pad_maximum_fusion.refs_0_) | copy-start | bytes 1327108
  19.8 12.8 %collective-permute-start.6 = (bf16[4,2,64,432]{3,2,1,0:T(8,128)(2,1)S(1)}, bf16[4,2,64,432]{3,2,1,0:T(8,128)(2,1)S(1)}, u32[]{:S(2)}, u32[]{:S(2)}) collective-permute-start(bf16[4,2,64,432]{3,2,1,0:T(8,128)(2,1)S(1)} %pad_maximum_fusion.refs_0_), channel_id=1, source_target_pairs={{0,48},{1,49},{2,50},{3,51},{4,52},{5,53},{6,54},{7,55},{8,56},{9,... | collective-permute-start | bytes 1327112 | tf_op jit(solution)/shard_map/ppermute | solution.py:32
  22.9 13.1 %collective-permute-start.5 = (bf16[4,2,64,432]{3,2,1,0:T(8,128)(2,1)S(1)}, bf16[4,2,64,432]{3,2,1,0:T(8,128)(2,1)S(1)}, u32[]{:S(2)}, u32[]{:S(2)}) collective-permute-start(bf16[4,2,64,432]{3,2,1,0:T(8,128)(2,1)S(1)} %pad_maximum_fusion.refs_0_), channel_id=1, source_target_pairs={{0,16},{1,17},{2,18},{3,19},{4,20},{5,21},{6,22},{7,23},{8,24},{9,... | collective-permute-start | bytes 1327112 | tf_op jit(solution)/shard_map/ppermute | solution.py:32
  22.9 1.4 %collective-permute-start.3 = (s32[1]{0:T(128)}, s32[1]{0:T(128)}, u32[]{:S(2)}, u32[]{:S(2)}) collective-permute-start(s32[1]{0:T(128)} %param.6), channel_id=1, source_target_pairs={{0,64},{64,0},{128,192},{192,128},{1,65},{65,1},{129,193},{193,129... | collective-permute-start | bytes 20 | tf_op jit(solution)/shard_map/ppermute | solution.py:36
  22.9 5.1 %collective-permute-start.4 = (s32[1]{0:T(128)}, s32[1]{0:T(128)}, u32[]{:S(2)}, u32[]{:S(2)}) collective-permute-start(s32[1]{0:T(128)} %param.6), channel_id=1, source_target_pairs={{0,128},{64,192},{128,0},{192,64},{1,129},{65,193},{129,1},{193,65... | collective-permute-start | bytes 20 | tf_op jit(solution)/shard_map/ppermute | solution.py:36
  32.6 20.2 %copy-start.3 = (bf16[4,2,64,432]{3,2,1,0:T(8,128)(2,1)}, bf16[4,2,64,432]{3,2,1,0:T(8,128)(2,1)S(1)}, u32[]{:S(2)}) copy-start(bf16[4,2,64,432]{3,2,1,0:T(8,128)(2,1)S(1)} %collective-permute-done.6.refs_4_) | copy-start | bytes 1327108
  36.0 16.8 %copy-start.4 = (bf16[4,2,64,432]{3,2,1,0:T(8,128)(2,1)}, bf16[4,2,64,432]{3,2,1,0:T(8,128)(2,1)S(1)}, u32[]{:S(2)}) copy-start(bf16[4,2,64,432]{3,2,1,0:T(8,128)(2,1)S(1)} %collective-permute-done.5.refs_1_) | copy-start | bytes 1327108
  36.0 16.7 %all-to-all-start = ((bf16[8,64,512]{2,1,0:T(8,128)(2,1)}), bf16[8,64,512]{2,1,0:T(8,128)(2,1)S(1)}, u32[]{:S(2)}, u32[]{:S(2)}) async-start(bf16[8,64,512]{2,1,0:T(8,128)(2,1)} %get-tuple-element.28), calls=%async_computation | async-start | bytes 1048576 | tf_op jit(solution)/shard_map/all_to_all | solution.py:226
  39.6 11.8 %collective-permute-start.8 = (bf16[2,2,64,432]{3,2,1,0:T(8,128)(2,1)S(1)}, bf16[2,2,64,432]{3,2,1,0:T(8,128)(2,1)S(1)}, u32[]{:S(2)}, u32[]{:S(2)}) collective-permute-start(bf16[2,2,64,432]{3,2,1,0:T(8,128)(2,1)S(1)} %slice.19), channel_id=1, source_target_pairs={{0,48},{1,49},{2,50},{3,51},{4,52},{5,53},{6,54},{7,55},{8,56},{9,... | collective-permute-start | bytes 663560 | tf_op jit(solution)/shard_map/ppermute | solution.py:32
  42.4 10.4 %collective-permute-start.7 = (bf16[2,2,64,432]{3,2,1,0:T(8,128)(2,1)S(1)}, bf16[2,2,64,432]{3,2,1,0:T(8,128)(2,1)S(1)}, u32[]{:S(2)}, u32[]{:S(2)}) collective-permute-start(bf16[2,2,64,432]{3,2,1,0:T(8,128)(2,1)S(1)} %slice.18), channel_id=1, source_target_pairs={{0,16},{1,17},{2,18},{3,19},{4,20},{5,21},{6,22},{7,23},{8,24},{9,... | collective-permute-start | bytes 663560 | tf_op jit(solution)/shard_map/ppermute | solution.py:32
  51.4 19.7 %copy-start.7 = (bf16[2,2,64,432]{3,2,1,0:T(8,128)(2,1)}, bf16[2,2,64,432]{3,2,1,0:T(8,128)(2,1)S(1)}, u32[]{:S(2)}) copy-start(bf16[2,2,64,432]{3,2,1,0:T(8,128)(2,1)S(1)} %collective-permute-done.8.refs_3_) | copy-start | bytes 663556
  52.8 18.3 %copy-start.8 = (bf16[2,2,64,432]{3,2,1,0:T(8,128)(2,1)}, bf16[2,2,64,432]{3,2,1,0:T(8,128)(2,1)S(1)}, u32[]{:S(2)}) copy-start(bf16[2,2,64,432]{3,2,1,0:T(8,128)(2,1)S(1)} %collective-permute-done.7.refs_2_) | copy-start | bytes 663556
  52.8 18.3 %copy-start.2 = (bf16[8,64,512]{2,1,0:T(8,128)(2,1)}, bf16[8,64,512]{2,1,0:T(8,128)(2,1)S(1)}, u32[]{:S(2)}) copy-start(bf16[8,64,512]{2,1,0:T(8,128)(2,1)S(1)} %all-to-all-done.refs_6_) | copy-start | bytes 1572868
  52.8 18.3 %all-to-all-start.1 = ((bf16[8,2,64,512]{3,2,1,0:T(8,128)(2,1)}), bf16[8,2,64,512]{3,2,1,0:T(8,128)(2,1)S(1)}, u32[]{:S(2)}, u32[]{:S(2)}) async-start(bf16[8,2,64,512]{3,2,1,0:T(8,128)(2,1)} %get-tuple-element.29), calls=%async_computation.1 | async-start | bytes 2097152 | tf_op jit(solution)/shard_map/all_to_all | solution.py:229
  57.1 1.9 %collective-permute-start.9 = (bf16[8,64,512]{2,1,0:T(8,128)(2,1)S(1)}, bf16[8,64,512]{2,1,0:T(8,128)(2,1)S(1)}, u32[]{:S(2)}, u32[]{:S(2)}) collective-permute-start(bf16[8,64,512]{2,1,0:T(8,128)(2,1)S(1)} %all-to-all-done.refs_6_), channel_id=1, source_target_pairs={{0,64},{64,0},{128,192},{192,128},{1,65},{65,1},{129,193},{193,129... | collective-permute-start | bytes 1572872 | tf_op jit(solution)/shard_map/ppermute | solution.py:36
  59.0 12.1 %copy-start.6 = (bf16[8,64,512]{2,1,0:T(8,128)(2,1)}, bf16[8,64,512]{2,1,0:T(8,128)(2,1)S(1)}, u32[]{:S(2)}) copy-start(bf16[8,64,512]{2,1,0:T(8,128)(2,1)S(1)} %collective-permute-done.9.refs_7_) | copy-start | bytes 1572868
  71.1 1.0 copy-start
  78.6 2.9 %collective-permute-start.10 = (bf16[2,512,512]{2,1,0:T(8,128)(2,1)}, bf16[2,512,512]{2,1,0:T(8,128)(2,1)S(1)}, u32[]{:S(2)}, u32[]{:S(2)}) collective-permute-start(bf16[2,512,512]{2,1,0:T(8,128)(2,1)} %get-tuple-element.30), channel_id=1, source_target_pairs={{0,64},{64,0},{128,192},{192,128},{1,65},{65,1},{129,193},{193,129... | collective-permute-start | bytes 3145736 | tf_op jit(solution)/shard_map/ppermute | solution.py:36
  81.5 1.0 copy-start.5
  88.6 36.6 %all-to-all-start.2 = ((bf16[64,8,896]{2,1,0:T(8,128)(2,1)}), bf16[64,8,896]{2,1,0:T(8,128)(2,1)S(1)}, u32[]{:S(2)}, u32[]{:S(2)}) async-start(bf16[64,8,896]{2,1,0:T(8,128)(2,1)} %project.1), calls=%async_computation.2 | async-start | bytes 1835008 | tf_op jit(solution)/shard_map/all_to_all | solution.py:194
Sparse Core Ops, SparseCore 0:
  19.0 43.9 all-gather.2

commit v10 on v9

v10 whole, which is shorter than its diff:
```python
import jax
import jax.numpy as jnp
from jax import lax
from jax.experimental import pallas as pl
from jax.experimental.pallas import tpu as pltpu
from jax.sharding import PartitionSpec as P

NB = 432
SLAB = 64
NY, NX, NZ = 4, 2, 8
GROUPS = NY * NX
BLOCK = NZ * SLAB
WHOLE = 384
REST = NB - WHOLE
TAIL = 2 * WHOLE
LANES = TAIL + 128
VMEM = 24 * 1024 * 1024

IN_VMEM = pl.BlockSpec(memory_space=pltpu.VMEM)
IN_SMEM = pl.BlockSpec(memory_space=pltpu.SMEM)
ANYWHERE = pl.BlockSpec(memory_space=pl.ANY)
PARAMS = pltpu.CompilerParams(vmem_limit_bytes=VMEM)


def band_route(dy, dx, dz):
    route = []
    for y in range(NY):
        for x in range(NX):
            for z in range(NZ):
                there = ((y + dy) % NY * NX + (x + dx) % NX) * NZ + (z + dz) % NZ
                route.append(((y * NX + x) * NZ + z, there))
    return route


def shift(block, dy, dx, dz):
    return lax.ppermute(block, "band", band_route(dy, dx, dz))


def swap_groups(block, bit):
    return lax.ppermute(block, "kgrp", [(k, k ^ bit) for k in range(4)])


def other_side(block):
    route = [(i, j) for i, j in band_route(0, 1, 0)]
    both = [((k ^ 2) * 64 + i, k * 64 + j) for k in range(4) for i, j in route]
    return lax.ppermute(block, ("kgrp", "band"), both)


def dot(a, b, a_axis, b_axis):
    dims = (((a_axis,), (b_axis,)), ((), ()))
    return lax.dot_general(a, b, dims, preferred_element_type=jnp.float32)


def near(array):
    return pltpu.with_memory_space_constraint(array, pltpu.VMEM)


def lay_body(orbit_ref, out_ref):
    gap = jnp.zeros((SLAB, 64 - REST), jnp.float32)
    real, imag = orbit_ref[0, 0], orbit_ref[0, 1]
    out_ref[:, :WHOLE] = real[:, :WHOLE]
    out_ref[:, WHOLE:TAIL] = imag[:, :WHOLE]
    last = [real[:, WHOLE:].astype(jnp.float32), gap, imag[:, WHOLE:].astype(jnp.float32), gap]
    out_ref[:, TAIL:] = jnp.concatenate(last, axis=1).astype(jnp.bfloat16)


def lay(orbitals):
    return pl.pallas_call(
        lay_body,
        out_shape=pltpu.VMEM((SLAB, LANES), jnp.bfloat16),
        in_specs=[IN_VMEM],
        out_specs=IN_VMEM,
        name="lay",
    )(orbitals)


def turned(rows):
    last = rows[:, TAIL:].astype(jnp.float32)
    lane = lax.broadcasted_iota(jnp.int32, last.shape, 1)
    last = pltpu.roll(last, 64, 1) * jnp.where(lane < 64, 1.0, -1.0)
    return jnp.concatenate(
        [rows[:, WHOLE:TAIL], -rows[:, :WHOLE], last.astype(rows.dtype)], axis=1
    )


def pack_body(odd_ref, own_ref, core_ref, far_ref, stored_ref, kernels_ref, shared_ref, single_ref, sem):
    odd = odd_ref[0] == 1
    own, core, far = stored_ref[own_ref[0]], stored_ref[core_ref[0]], stored_ref[far_ref[0]]
    shared = jnp.where(odd, own, core)
    single = jnp.where(odd, core, far)
    copies = []
    for i in range(GROUPS):
        at = pl.ds(i * BLOCK, BLOCK)
        copies += [
            pltpu.make_async_copy(
                kernels_ref.at[shared, odd_ref[0], :, at], shared_ref.at[i], sem.at[0, i]
            ),
            pltpu.make_async_copy(
                kernels_ref.at[single, :, :, at], single_ref.at[i], sem.at[1, i]
            ),
        ]
    for copy in copies:
        copy.start()
    for copy in copies:
        copy.wait()


def pack(odd, own, core, far, stored, kernels):
    return pl.pallas_call(
        pack_body,
        out_shape=[
            pltpu.VMEM((GROUPS, SLAB, BLOCK), jnp.bfloat16),
            pltpu.VMEM((GROUPS, 2, SLAB, BLOCK), jnp.bfloat16),
        ],
        in_specs=[IN_SMEM] * 5 + [ANYWHERE],
        out_specs=[IN_VMEM] * 2,
        scratch_shapes=[pltpu.SemaphoreType.DMA((2, GROUPS))],
        compiler_params=PARAMS,
        name="pack",
    )(odd, own, core, far, stored, kernels)


def mix_body(place_ref, odd_ref, *refs):
    four_ref, up_ref, over_here, over_side, down_ref, gathered_ref = refs[:6]
    mine_ref, half_ref, kern_ref = refs[6:9]
    m_ref, row_ref, col_ref, other_rows, other_cols = refs[9:]
    rows = ((four_ref, four_ref), (up_ref, up_ref), (over_here, over_side), (down_ref, down_ref))
    for i in range(NY):
        for side in range(NX):
            at = pl.ds(pl.multiple_of(place_ref[i * NX + side] * SLAB, SLAB), SLAB)
            piece = rows[i][side]
            first = 0 if piece is over_side else 2 * side
            row_ref[at, :] = piece[first]
            other_rows[at, :] = piece[first + 1]
    for i in range(NZ):
        at = pl.ds(i * SLAB, SLAB)
        col_ref[at, :] = gathered_ref[i, 0]
        other_cols[at, :] = gathered_ref[i, 1]
    per = BLOCK // 2
    odd = odd_ref[0] == 1
    sign = jnp.where(odd, -1.0, 1.0).astype(jnp.float32)
    a, a_other = row_ref[...], other_rows[...]
    a_turned, other_turned = turned(a), turned(a_other)
    for part in range(2):
        at = pl.ds(part * per, per)
        b = col_ref[at, :]
        p_re, p_im = dot(a, b, 1, 1), dot(a_turned, b, 1, 1)
        mine = mine_ref[:, :, at].reshape(BLOCK, per)
        other = half_ref[:, :, at].reshape(BLOCK, per)
        k_re = jnp.where(odd, other, mine).astype(jnp.float32)
        k_im = jnp.where(odd, mine, other).astype(jnp.float32) * sign
        total_re = k_re * p_re - k_im * p_im
        total_im = k_re * p_im + k_im * p_re
        b = other_cols[at, :]
        p_re, p_im = dot(a_other, b, 1, 1), dot(other_turned, b, 1, 1)
        k_re = kern_ref[:, 0, :, at].reshape(BLOCK, per).astype(jnp.float32)
        k_im = kern_ref[:, 1, :, at].reshape(BLOCK, per).astype(jnp.float32) * -sign
        total_re += k_re * p_re - k_im * p_im
        total_im += k_re * p_im + k_im * p_re
        m_ref[:, at] = total_re.astype(jnp.bfloat16)
        m_ref[:, pl.ds(BLOCK + part * per, per)] = total_im.astype(jnp.bfloat16)


def mix(place, odd, *arrays):
    points = pltpu.VMEM((BLOCK, LANES), jnp.bfloat16)
    return pl.pallas_call(
        mix_body,
        out_shape=[pltpu.VMEM((BLOCK, 2 * BLOCK), jnp.bfloat16), points, points],
        in_specs=[IN_SMEM] * 2 + [IN_VMEM] * len(arrays),
        out_specs=[IN_VMEM] * 3,
        scratch_shapes=[pltpu.VMEM((BLOCK, LANES), jnp.bfloat16)] * 2,
        compiler_params=PARAMS,
        name="mix",
    )(place, odd, *map(near, arrays))


def prepare_body(row_ref, col_ref, left_ref, right_ref):
    flipped = row_ref[...].T
    left_ref[pl.ds(0, WHOLE), :BLOCK] = flipped[:WHOLE]
    left_ref[pl.ds(WHOLE, REST), :BLOCK] = flipped[TAIL : TAIL + REST]
    left_ref[pl.ds(0, WHOLE), BLOCK:] = flipped[WHOLE:TAIL]
    left_ref[pl.ds(WHOLE, REST), BLOCK:] = flipped[TAIL + 64 : TAIL + 64 + REST]
    col = col_ref[...]
    right_ref[pl.ds(0, BLOCK), :] = col
    right_ref[pl.ds(BLOCK, BLOCK), :] = -turned(col)


def prepare(rows, cols):
    return pl.pallas_call(
        prepare_body,
        out_shape=[
            pltpu.VMEM((NB, 2 * BLOCK), jnp.bfloat16),
            pltpu.VMEM((2 * BLOCK, LANES), jnp.bfloat16),
        ],
        in_specs=[IN_VMEM] * 2,
        out_specs=[IN_VMEM] * 2,
        compiler_params=PARAMS,
        name="prepare",
    )(near(rows), near(cols))


def project_body(m_ref, left_ref, right_ref, out_ref, x_ref):
    y = dot(m_ref[...], right_ref[...], 1, 0)
    high = y.astype(jnp.bfloat16)
    low = (y - high.astype(jnp.float32)).astype(jnp.bfloat16)
    left = left_ref[...]
    x = dot(left, jnp.concatenate([high, turned(high)], axis=0), 1, 0)
    x += dot(left, jnp.concatenate([low, turned(low)], axis=0), 1, 0)
    x_ref[pl.ds(0, NB), :] = -x
    x_ref[pl.ds(NB, 8), :] = jnp.zeros((8, LANES), jnp.float32)
    for d in range(GROUPS * NZ):
        out_ref[d] = x_ref[pl.ds(27 * d // 4, 8), :].astype(jnp.bfloat16)


def project(m, left, right):
    return pl.pallas_call(
        project_body,
        out_shape=pltpu.VMEM((GROUPS * NZ, 8, LANES), jnp.bfloat16),
        in_specs=[IN_VMEM] * 3,
        out_specs=IN_VMEM,
        scratch_shapes=[pltpu.VMEM((NB + 8, LANES), jnp.float32)],
        compiler_params=PARAMS,
        name="project",
    )(near(m), near(left), near(right))


def bundle_body(own_ref, far_ref, own_side, far_side, four_ref, both_ref):
    for i, ref in enumerate((own_ref, far_ref, own_side, far_side)):
        four_ref[i] = ref[...]
    both_ref[0] = own_ref[...]
    both_ref[1] = far_ref[...]


def bundle(*blocks):
    return pl.pallas_call(
        bundle_body,
        out_shape=[
            pltpu.VMEM((4, SLAB, LANES), jnp.bfloat16),
            jax.ShapeDtypeStruct((2, SLAB, LANES), jnp.bfloat16),
        ],
        in_specs=[IN_VMEM] * 4,
        out_specs=[IN_VMEM] * 2,
        compiler_params=PARAMS,
        name="bundle",
    )(*map(near, blocks))


def reduce_windows(windows):
    parts = lax.all_to_all(windows, "band", 0, 0)
    total = jnp.sum(parts.astype(jnp.float32), axis=0)
    real = jnp.concatenate([total[:, :WHOLE], total[:, TAIL : TAIL + REST]], axis=1)
    imag = jnp.concatenate([total[:, WHOLE:TAIL], total[:, TAIL + 64 : TAIL + 64 + REST]], axis=1)
    return jnp.stack([real, imag])


def on_device(orbitals, kernels, pair_kdiff, stored_kernel_index):
    group = lax.axis_index("kgrp")
    band = lax.axis_index("band")
    y, x = band // (NX * NZ), band // NZ % NX
    odd = (group % 2).reshape(1)

    own = lay(orbitals)
    first = (
        swap_groups(pair_kdiff, 1),
        swap_groups(pair_kdiff, 2),
        swap_groups(own, 2),
        shift(own, 0, 1, 0),
        other_side(own),
    )
    diff_core, diff_far, far, own_side, far_side = lax.optimization_barrier(first)

    over_yx = [[g * NZ + z for g in range(GROUPS)] for z in range(NZ)]
    over_z = [[g * NZ + z for z in range(NZ)] for g in range(GROUPS)]
    four, both = bundle(own, far, own_side, far_side)
    gathered = lax.all_gather(both, "band", axis_index_groups=over_z)
    up, down = shift(four, 1, 0, 0), shift(four, -1, 0, 0)
    over = shift(up[:2], 1, 0, 0), shift(down[2:], -1, 0, 0)

    shared, single = pack(odd, pair_kdiff, diff_core, diff_far, stored_kernel_index, kernels)
    mine = lax.all_to_all(shared, "band", 0, 0, axis_index_groups=over_yx)
    half = swap_groups(mine, 1)
    single, over = lax.optimization_barrier((single, over))
    kern = lax.all_to_all(single, "band", 0, 0, axis_index_groups=over_yx)

    place = jnp.stack([(y - dy) % NY * NX + (x - dx) % NX for dy in range(NY) for dx in range(NX)])
    m_out, rows, cols = mix(
        place, odd, four, up, *over, down, gathered, mine, half, kern
    )
    m_own = swap_groups(m_out, 1)
    left, right = prepare(rows, cols)
    total = reduce_windows(project(m_own, left, right))
    flat = total.reshape(2, 8 * NB)
    flat = lax.dynamic_slice(flat, (0, band * 27 % 4 * 108), (2, 27 * 108))
    return flat[None]


def solution(mesh):
    return jax.shard_map(
        on_device,
        mesh=mesh,
        in_specs=(P("kgrp", None, "band", None), P(None, None, "band", None), P("kgrp"), P()),
        out_specs=P("kgrp", None, "band"),
        check_vma=False,
    )
```

time: 135 us -> 126 us (0.933)
  waiting for transfers between devices: 65.3 us -> 56.3 us
  local copies, waits for them, and re-layouts: 2.91 us -> 7.28 us
  Pallas kernels: 17.1 us -> 13.1 us
  starting transfers between devices: 30.2 us -> 33.5 us
  other arithmetic: 3.51 us -> 0.9 us
    unnamed x18 -> x14, local copies, waits for them, and re-layouts: 2 us -> 6.89 us
    ppermute x5, waiting for transfers between devices: 14.3 us -> 10.2 us  [shift(): return lax.ppermute(block, 'band', band_route(dy, dx, dz))]
    pallas_call x3 -> x6, Pallas kernels: 17.1 us -> 13.1 us  [the longest x1 4.19 us: project(): pl.pallas_call(project_body, out_shape=pltpu.VMEM((GROUPS * NZ, 8, LANES)...]
    ppermute x5, waiting for transfers between devices: 11.1 us -> 8.13 us  [swap_groups(): return lax.ppermute(block, 'kgrp', [(k, k ^ bit) for k in range(4)])]
    another operation x2 -> x0, other arithmetic: 2.61 us -> none  [the longest x1 1.62 us: on_device(): jnp.stack([own, far])]
    all_to_all x1, starting transfers between devices: 3.5 us -> 5.98 us  [on_device(): mine = lax.all_to_all(shared, 'band', 0, 0, axis_index_groups=over_yx)]
    ppermute x1, waiting for transfers between devices: 2.24 us -> 0.01 us  [other_side(): return lax.ppermute(block, ('kgrp', 'band'), both)]
  transfers between devices with their start and end apart: 15 -> 15, of which waited for: 12 -> 8; matrix products, arithmetic and copies ran while one was open for 1% -> 0% of each run, Pallas kernels for 3% -> 3%
where the time goes in v10:
time: 126 us; the launch traced here: 125 us
  waiting for transfers between devices  56.3 us (45%)
  starting transfers between devices  33.5 us (27%)
  between operations  14.2 us (11%)
  Pallas kernels  13.1 us (10%)
  local copies, waits for them, and re-layouts  7.28 us (6%)
    all_to_all x1, waiting for transfers between devices, reduce_windows(): parts = lax.all_to_all(windows, 'band', 0, 0)  25.5 us
    all_to_all x1, waiting for transfers between devices, on_device(): kern = lax.all_to_all(single, 'band', 0, 0, axis_index_groups=over_yx)  12.5 us
    all_to_all x1, starting transfers between devices, reduce_windows(): parts = lax.all_to_all(windows, 'band', 0, 0)  11.2 us
    ppermute x5, waiting for transfers between devices, shift(): return lax.ppermute(block, 'band', band_route(dy, dx, dz))  10.2 us
    ppermute x5, waiting for transfers between devices, swap_groups(): return lax.ppermute(block, 'kgrp', [(k, k ^ bit) for k in range(4)])  8.13 us
    unnamed x14, local copies, waits for them, and re-layouts  6.89 us
    all_to_all x1, starting transfers between devices, on_device(): mine = lax.all_to_all(shared, 'band', 0, 0, axis_index_groups=over_yx)  5.98 us
    ppermute x5, starting transfers between devices, shift(): return lax.ppermute(block, 'band', band_route(dy, dx, dz))  5.93 us
  transfers between devices with their start and end apart: 15, of which 8 were waited for; matrix products, arithmetic and copies ran while one was open for 0% of the time, Pallas kernels for 3%

profile of v10, /device:TPU:6, one launch (start us, length us, event | category | flops | bytes accessed | tf_op | source)
XLA Modules:
  0.0 125.2 jit_solution(13927151625458868372)
XLA Ops:
  6.5 1.0 lay.1.own_ref
  7.5 2.3 %collective-permute-start.4 = (bf16[64,896]{1,0:T(8,128)(2,1)S(1)}, bf16[64,896]{1,0:T(8,128)(2,1)S(1)}, u32[]{:S(2)}, u32[]{:S(2)}) collective-permute-start(bf16[64,896]{1,0:T(8,128)(2,1)S(1)} %lay.1.own_ref), channel_id=1, source_target_pairs={{128,8},{129,9},{130,10},{131,11},{132,12},{133,13},{134,14},{135,... | collective-permute-start | bytes 344072 | tf_op jit(solution)/shard_map/ppermute | solution.py:46
  9.8 2.5 %collective-permute-start.2 = (bf16[64,896]{1,0:T(8,128)(2,1)S(1)}, bf16[64,896]{1,0:T(8,128)(2,1)S(1)}, u32[]{:S(2)}, u32[]{:S(2)}) collective-permute-start(bf16[64,896]{1,0:T(8,128)(2,1)S(1)} %lay.1.own_ref), channel_id=1, source_target_pairs={{0,128},{64,192},{128,0},{192,64},{1,129},{65,193},{129,1},{193,65... | collective-permute-start | bytes 344072 | tf_op jit(solution)/shard_map/ppermute | solution.py:40
  12.3 1.0 collective-permute-start.1
  13.3 0.3 collective-permute-done.core_ref
  13.6 3.9 %collective-permute-done.1.far_ref = s32[1]{0:T(128)} collective-permute-done((s32[1]{0:T(128)}, s32[1]{0:T(128)}, u32[]{:S(2)}, u32[]{:S(2)}) %collective-permute-start.1) | collective-permute-done | bytes 36 | tf_op jit(solution)/shard_map/ppermute | solution.py:40
  17.6 0.7 bundle.1
  18.3 3.1 %collective-permute-start.7 = (bf16[4,64,896]{2,1,0:T(8,128)(2,1)S(1)}, bf16[4,64,896]{2,1,0:T(8,128)(2,1)S(1)}, u32[]{:S(2)}, u32[]{:S(2)}) collective-permute-start(bf16[4,64,896]{2,1,0:T(8,128)(2,1)S(1)} %get-tuple-element.25.refs_0_), channel_id=1, source_target_pairs={{0,48},{1,49},{2,50},{3,51},{4,52},{5,53},{6,54},{7,55},{8,56},{9,... | collective-permute-start | bytes 1376264 | tf_op jit(solution)/shard_map/ppermute | solution.py:36
  22.1 2.2 %copy-done = bf16[4,2,64,4096]{3,2,1,0:T(8,128)(2,1)S(1)} copy-done((bf16[4,2,64,4096]{3,2,1,0:T(8,128)(2,1)S(1)}, bf16[4,2,64,4096]{3,2,1,0:T(8,128)(2,1)}, u32[]{:S(2)}) %copy-start) | copy-done | bytes 4194328
  24.3 0.7 copy-done.6
  24.9 3.3 %pack.1 = (bf16[8,64,512]{2,1,0:T(8,128)(2,1)}, bf16[8,2,64,512]{3,2,1,0:T(8,128)(2,1)}) custom-call(s32[1]{0:T(128)} %bitcast.8.odd_ref, s32[1]{0:T(128)S(6)} %copy.5.own_ref, s32[1]{0:T(128)} %collective-permute-done.core_ref, s32[1]{0:T(128)} %collective-permute-done.1.far_ref, s32[8]{0:T(128)S(1)} %copy-done.6, bf16[4,2,64,4096]{3,2,1,0:T(8,128)(2,1)S(1)} %copy-done), custom_call_target="tpu_custom_call" | custom-call | tf_op jit(solution)/shard_map/pack/pallas_call | solution.py:109
  28.2 6.0 %all-to-all-start = ((bf16[8,64,512]{2,1,0:T(8,128)(2,1)}), bf16[8,64,512]{2,1,0:T(8,128)(2,1)S(1)}, u32[]{:S(2)}, u32[]{:S(2)}) async-start(bf16[8,64,512]{2,1,0:T(8,128)(2,1)} %get-tuple-element.32), calls=%async_computation | async-start | bytes 1048576 | tf_op jit(solution)/shard_map/all_to_all | solution.py:280
  34.2 2.8 %collective-permute-start.8 = (bf16[2,64,896]{2,1,0:T(8,128)(2,1)S(1)}, bf16[2,64,896]{2,1,0:T(8,128)(2,1)S(1)}, u32[]{:S(2)}, u32[]{:S(2)}) collective-permute-start(bf16[2,64,896]{2,1,0:T(8,128)(2,1)S(1)} %slice.25), channel_id=1, source_target_pairs={{0,48},{1,49},{2,50},{3,51},{4,52},{5,53},{6,54},{7,55},{8,56},{9,... | collective-permute-start | bytes 688136 | tf_op jit(solution)/shard_map/ppermute | solution.py:36
  37.1 8.6 %collective-permute-done.8.refs_3_ = bf16[2,64,896]{2,1,0:T(8,128)(2,1)S(1)} collective-permute-done((bf16[2,64,896]{2,1,0:T(8,128)(2,1)S(1)}, bf16[2,64,896]{2,1,0:T(8,128)(2,1)S(1)}, u32[]{:S(2)}, u32[]{:S(2)}) %collective-permute-start.8) | collective-permute-done | bytes 229408 | tf_op jit(solution)/shard_map/ppermute | solution.py:36
  45.8 1.5 %collective-permute-done.6.refs_2_ = bf16[2,64,896]{2,1,0:T(8,128)(2,1)S(1)} collective-permute-done((bf16[2,64,896]{2,1,0:T(8,128)(2,1)S(1)}, bf16[2,64,896]{2,1,0:T(8,128)(2,1)S(1)}, u32[]{:S(2)}, u32[]{:S(2)}) %collective-permute-start.6) | collective-permute-done | bytes 229408 | tf_op jit(solution)/shard_map/ppermute | solution.py:36
  47.3 0.7 copy-done.4
  48.0 4.3 %all-to-all-start.1 = ((bf16[8,2,64,512]{3,2,1,0:T(8,128)(2,1)}), bf16[8,2,64,512]{3,2,1,0:T(8,128)(2,1)S(1)}, u32[]{:S(2)}, u32[]{:S(2)}) async-start(bf16[8,2,64,512]{3,2,1,0:T(8,128)(2,1)} %get-tuple-element.33), calls=%async_computation.1 | async-start | bytes 2097152 | tf_op jit(solution)/shard_map/all_to_all | solution.py:283
  52.4 1.8 %collective-permute-done.9.refs_7_ = bf16[8,64,512]{2,1,0:T(8,128)(2,1)S(1)} collective-permute-done((bf16[8,64,512]{2,1,0:T(8,128)(2,1)S(1)}, bf16[8,64,512]{2,1,0:T(8,128)(2,1)S(1)}, u32[]{:S(2)}, u32[]{:S(2)}) %collective-permute-start.9) | collective-permute-done | bytes 524320 | tf_op jit(solution)/shard_map/ppermute | solution.py:40
  54.2 12.5 %all-to-all-done.1.refs_8_ = bf16[8,2,64,512]{3,2,1,0:T(8,128)(2,1)S(1)} async-done(((bf16[8,2,64,512]{3,2,1,0:T(8,128)(2,1)}), bf16[8,2,64,512]{3,2,1,0:T(8,128)(2,1)S(1)}, u32[]{:S(2)}, u32[]{:S(2)}) %all-to-all-start.1) | async-done | bytes 1048608 | tf_op jit(solution)/shard_map/all_to_all | solution.py:283
  66.7 1.5 %copy-done.1 = bf16[16,64,896]{2,1,0:T(8,128)(2,1)S(1)} copy-done((bf16[16,64,896]{2,1,0:T(8,128)(2,1)S(1)}, bf16[16,64,896]{2,1,0:T(8,128)(2,1)}, u32[]{:S(2)}) %copy-start.1) | copy-done | bytes 1835032
  68.2 0.9 copy-done.3
  69.1 0.9 copy-done.5
  70.0 3.3 %mix.1 = (bf16[512,1024]{1,0:T(8,128)(2,1)S(1)}, bf16[512,896]{1,0:T(8,128)(2,1)S(1)}, bf16[512,896]{1,0:T(8,128)(2,1)S(1)}) custom-call(s32[8]{0:T(128)S(1)} %stack.44.place_ref, s32[1]{0:T(128)} %bitcast.8.odd_ref, bf16[4,64,896]{2,1,0:T(8,128)(2,1)S(1)} %get-tuple-element.25.refs_0_, bf16[4,64,896]{2,1,0:T(8,128)(2,1)S(1)} %collective-permute-done.5.refs_1_, ...), custom_call_target="tpu_custom_call" | custom-call | tf_op jit(solution)/shard_map/mix/pallas_call | solution.py:166
  73.3 0.3 collective-permute-start.10
  73.6 0.6 prepare.1
  74.2 2.1 %collective-permute-done.10.m_ref = bf16[512,1024]{1,0:T(8,128)(2,1)S(1)} collective-permute-done((bf16[512,1024]{1,0:T(8,128)(2,1)S(1)}, bf16[512,1024]{1,0:T(8,128)(2,1)S(1)}, u32[]{:S(2)}, u32[]{:S(2)}) %collective-permute-start.10) | collective-permute-done | bytes 1048608 | tf_op jit(solution)/shard_map/ppermute | solution.py:40
  76.2 4.2 %project.1 = bf16[64,8,896]{2,1,0:T(8,128)(2,1)} custom-call(bf16[512,1024]{1,0:T(8,128)(2,1)S(1)} %collective-permute-done.10.m_ref, bf16[432,1024]{1,0:T(8,128)(2,1)S(1)} %get-tuple-element.37.left_ref, bf16[1024,896]{1,0:T(8,128)(2,1)S(1)} %get-tuple-element.38.right_ref), custom_call_target="tpu_custom_call" | custom-call | tf_op jit(solution)/shard_map/project/pallas_call | solution.py:216
  80.4 11.2 %all-to-all-start.2 = ((bf16[64,8,896]{2,1,0:T(8,128)(2,1)}), bf16[64,8,896]{2,1,0:T(8,128)(2,1)S(1)}, u32[]{:S(2)}, u32[]{:S(2)}) async-start(bf16[64,8,896]{2,1,0:T(8,128)(2,1)} %project.1), calls=%async_computation.2 | async-start | bytes 1835008 | tf_op jit(solution)/shard_map/all_to_all | solution.py:249
  91.6 25.5 %all-to-all-done.2 = bf16[64,8,896]{2,1,0:T(8,128)(2,1)S(1)} async-done(((bf16[64,8,896]{2,1,0:T(8,128)(2,1)}), bf16[64,8,896]{2,1,0:T(8,128)(2,1)S(1)}, u32[]{:S(2)}, u32[]{:S(2)}) %all-to-all-start.2) | async-done | bytes 917536 | tf_op jit(solution)/shard_map/all_to_all | solution.py:249
  117.2 0.2 convert_reduce_fusion
  117.4 0.1 stack.45
  117.6 0.7 fusion.1
  (29 shorter events, 0.4 us)
Async XLA Ops:
  6.5 60.1 %all-gather.3.cloned.1.call-start = ((), (), s32[]{:S(2)}) async-start(), calls=%async_computation.3 | async-start | bytes 2064384 | tf_op jit(solution)/shard_map/all_gather | solution.py:275
  7.5 10.0 %collective-permute-start.4 = (bf16[64,896]{1,0:T(8,128)(2,1)S(1)}, bf16[64,896]{1,0:T(8,128)(2,1)S(1)}, u32[]{:S(2)}, u32[]{:S(2)}) collective-permute-start(bf16[64,896]{1,0:T(8,128)(2,1)S(1)} %lay.1.own_ref), channel_id=1, source_target_pairs={{128,8},{129,9},{130,10},{131,11},{132,12},{133,13},{134,14},{135,... | collective-permute-start | bytes 344072 | tf_op jit(solution)/shard_map/ppermute | solution.py:46
  9.8 7.8 %collective-permute-start.3 = (bf16[64,896]{1,0:T(8,128)(2,1)S(1)}, bf16[64,896]{1,0:T(8,128)(2,1)S(1)}, u32[]{:S(2)}, u32[]{:S(2)}) collective-permute-start(bf16[64,896]{1,0:T(8,128)(2,1)S(1)} %lay.1.own_ref), channel_id=1, source_target_pairs={{0,8},{1,9},{2,10},{3,11},{4,12},{5,13},{6,14},{7,15},{8,0},{9,1},... | collective-permute-start | bytes 344072 | tf_op jit(solution)/shard_map/ppermute | solution.py:36
  9.8 7.8 %collective-permute-start.2 = (bf16[64,896]{1,0:T(8,128)(2,1)S(1)}, bf16[64,896]{1,0:T(8,128)(2,1)S(1)}, u32[]{:S(2)}, u32[]{:S(2)}) collective-permute-start(bf16[64,896]{1,0:T(8,128)(2,1)S(1)} %lay.1.own_ref), channel_id=1, source_target_pairs={{0,128},{64,192},{128,0},{192,64},{1,129},{65,193},{129,1},{193,65... | collective-permute-start | bytes 344072 | tf_op jit(solution)/shard_map/ppermute | solution.py:40
  12.3 1.4 %collective-permute-start = (s32[1]{0:T(128)}, s32[1]{0:T(128)}, u32[]{:S(2)}, u32[]{:S(2)}) collective-permute-start(s32[1]{0:T(128)} %param.6), channel_id=1, source_target_pairs={{0,64},{64,0},{128,192},{192,128},{1,65},{65,1},{129,193},{193,129... | collective-permute-start | bytes 20 | tf_op jit(solution)/shard_map/ppermute | solution.py:40
  12.3 5.3 %collective-permute-start.1 = (s32[1]{0:T(128)}, s32[1]{0:T(128)}, u32[]{:S(2)}, u32[]{:S(2)}) collective-permute-start(s32[1]{0:T(128)} %param.6), channel_id=1, source_target_pairs={{0,128},{64,192},{128,0},{192,64},{1,129},{65,193},{129,1},{193,65... | collective-permute-start | bytes 20 | tf_op jit(solution)/shard_map/ppermute | solution.py:40
  18.3 15.9 %collective-permute-start.7 = (bf16[4,64,896]{2,1,0:T(8,128)(2,1)S(1)}, bf16[4,64,896]{2,1,0:T(8,128)(2,1)S(1)}, u32[]{:S(2)}, u32[]{:S(2)}) collective-permute-start(bf16[4,64,896]{2,1,0:T(8,128)(2,1)S(1)} %get-tuple-element.25.refs_0_), channel_id=1, source_target_pairs={{0,48},{1,49},{2,50},{3,51},{4,52},{5,53},{6,54},{7,55},{8,56},{9,... | collective-permute-start | bytes 1376264 | tf_op jit(solution)/shard_map/ppermute | solution.py:36
  21.4 15.6 %collective-permute-start.5 = (bf16[4,64,896]{2,1,0:T(8,128)(2,1)S(1)}, bf16[4,64,896]{2,1,0:T(8,128)(2,1)S(1)}, u32[]{:S(2)}, u32[]{:S(2)}) collective-permute-start(bf16[4,64,896]{2,1,0:T(8,128)(2,1)S(1)} %get-tuple-element.25.refs_0_), channel_id=1, source_target_pairs={{0,16},{1,17},{2,18},{3,19},{4,20},{5,21},{6,22},{7,23},{8,24},{9,... | collective-permute-start | bytes 1376264 | tf_op jit(solution)/shard_map/ppermute | solution.py:36
  22.1 2.2 %copy-start = (bf16[4,2,64,4096]{3,2,1,0:T(8,128)(2,1)S(1)}, bf16[4,2,64,4096]{3,2,1,0:T(8,128)(2,1)}, u32[]{:S(2)}) copy-start(bf16[4,2,64,4096]{3,2,1,0:T(8,128)(2,1)} %kernels_ref.1) | copy-start | bytes 12582916
  24.3 0.7 copy-start.6
  28.2 19.0 %all-to-all-start = ((bf16[8,64,512]{2,1,0:T(8,128)(2,1)}), bf16[8,64,512]{2,1,0:T(8,128)(2,1)S(1)}, u32[]{:S(2)}, u32[]{:S(2)}) async-start(bf16[8,64,512]{2,1,0:T(8,128)(2,1)} %get-tuple-element.32), calls=%async_computation | async-start | bytes 1048576 | tf_op jit(solution)/shard_map/all_to_all | solution.py:280
  34.2 11.5 %collective-permute-start.8 = (bf16[2,64,896]{2,1,0:T(8,128)(2,1)S(1)}, bf16[2,64,896]{2,1,0:T(8,128)(2,1)S(1)}, u32[]{:S(2)}, u32[]{:S(2)}) collective-permute-start(bf16[2,64,896]{2,1,0:T(8,128)(2,1)S(1)} %slice.25), channel_id=1, source_target_pairs={{0,48},{1,49},{2,50},{3,51},{4,52},{5,53},{6,54},{7,55},{8,56},{9,... | collective-permute-start | bytes 688136 | tf_op jit(solution)/shard_map/ppermute | solution.py:36
  37.0 10.2 %collective-permute-start.6 = (bf16[2,64,896]{2,1,0:T(8,128)(2,1)S(1)}, bf16[2,64,896]{2,1,0:T(8,128)(2,1)S(1)}, u32[]{:S(2)}, u32[]{:S(2)}) collective-permute-start(bf16[2,64,896]{2,1,0:T(8,128)(2,1)S(1)} %slice.24), channel_id=1, source_target_pairs={{0,16},{1,17},{2,18},{3,19},{4,20},{5,21},{6,22},{7,23},{8,24},{9,... | collective-permute-start | bytes 688136 | tf_op jit(solution)/shard_map/ppermute | solution.py:36
  45.8 1.5 %copy-start.2 = (bf16[2,64,896]{2,1,0:T(8,128)(2,1)}, bf16[2,64,896]{2,1,0:T(8,128)(2,1)S(1)}, u32[]{:S(2)}) copy-start(bf16[2,64,896]{2,1,0:T(8,128)(2,1)S(1)} %collective-permute-done.8.refs_3_) | copy-start | bytes 688132
  47.3 0.7 copy-start.4
  48.0 18.7 %all-to-all-start.1 = ((bf16[8,2,64,512]{3,2,1,0:T(8,128)(2,1)}), bf16[8,2,64,512]{3,2,1,0:T(8,128)(2,1)S(1)}, u32[]{:S(2)}, u32[]{:S(2)}) async-start(bf16[8,2,64,512]{3,2,1,0:T(8,128)(2,1)} %get-tuple-element.33), calls=%async_computation.1 | async-start | bytes 2097152 | tf_op jit(solution)/shard_map/all_to_all | solution.py:283
  52.3 1.9 %collective-permute-start.9 = (bf16[8,64,512]{2,1,0:T(8,128)(2,1)S(1)}, bf16[8,64,512]{2,1,0:T(8,128)(2,1)S(1)}, u32[]{:S(2)}, u32[]{:S(2)}) collective-permute-start(bf16[8,64,512]{2,1,0:T(8,128)(2,1)S(1)} %all-to-all-done.refs_6_), channel_id=1, source_target_pairs={{0,64},{64,0},{128,192},{192,128},{1,65},{65,1},{129,193},{193,129... | collective-permute-start | bytes 1572872 | tf_op jit(solution)/shard_map/ppermute | solution.py:40
  66.7 1.5 %copy-start.1 = (bf16[16,64,896]{2,1,0:T(8,128)(2,1)S(1)}, bf16[16,64,896]{2,1,0:T(8,128)(2,1)}, u32[]{:S(2)}) copy-start(bf16[16,64,896]{2,1,0:T(8,128)(2,1)} %all-gather.3.cloned.1.call-done) | copy-start | bytes 5505028
  68.2 0.9 copy-start.3
  69.1 0.9 copy-start.5
  73.3 2.9 %collective-permute-start.10 = (bf16[512,1024]{1,0:T(8,128)(2,1)S(1)}, bf16[512,1024]{1,0:T(8,128)(2,1)S(1)}, u32[]{:S(2)}, u32[]{:S(2)}) collective-permute-start(bf16[512,1024]{1,0:T(8,128)(2,1)S(1)} %get-tuple-element.34), channel_id=1, source_target_pairs={{0,64},{64,0},{128,192},{192,128},{1,65},{65,1},{129,193},{193,129... | collective-permute-start | bytes 3145736 | tf_op jit(solution)/shard_map/ppermute | solution.py:40
  80.4 36.7 %all-to-all-start.2 = ((bf16[64,8,896]{2,1,0:T(8,128)(2,1)}), bf16[64,8,896]{2,1,0:T(8,128)(2,1)S(1)}, u32[]{:S(2)}, u32[]{:S(2)}) async-start(bf16[64,8,896]{2,1,0:T(8,128)(2,1)} %project.1), calls=%async_computation.2 | async-start | bytes 1835008 | tf_op jit(solution)/shard_map/all_to_all | solution.py:249
Sparse Core Ops, SparseCore 0:
  18.5 43.0 all-gather.2

commit v11 on v10

--- a/solution.py
+++ b/solution.py
@@ -53,6 +53,10 @@
 
 def near(array):
     return pltpu.with_memory_space_constraint(array, pltpu.VMEM)
+
+
+def away(array):
+    return pltpu.with_memory_space_constraint(array, pltpu.HBM)
 
 
 def lay_body(orbit_ref, out_ref):
@@ -117,25 +121,33 @@
         scratch_shapes=[pltpu.SemaphoreType.DMA((2, GROUPS))],
         compiler_params=PARAMS,
         name="pack",
-    )(odd, own, core, far, stored, kernels)
+    )(odd, own, core, far, stored, away(kernels))
 
 
 def mix_body(place_ref, odd_ref, *refs):
     four_ref, up_ref, over_here, over_side, down_ref, gathered_ref = refs[:6]
     mine_ref, half_ref, kern_ref = refs[6:9]
-    m_ref, row_ref, col_ref, other_rows, other_cols = refs[9:]
-    rows = ((four_ref, four_ref), (up_ref, up_ref), (over_here, over_side), (down_ref, down_ref))
-    for i in range(NY):
+    m_ref, row_ref, col_ref, other_rows, other_cols, sem = refs[9:]
+
+    def row_at(dy, side):
+        return pl.ds(pl.multiple_of(place_ref[dy * NX + side] * SLAB, SLAB), SLAB)
+
+    moves = []
+    for side, piece in enumerate((over_here, over_side)):
+        moves.append((piece.at[0], row_ref.at[row_at(2, side), :]))
+        moves.append((piece.at[1], other_rows.at[row_at(2, side), :]))
+    for target, which in ((col_ref, 0), (other_cols, 1)):
+        for i in range(NZ):
+            moves.append((gathered_ref.at[i, which], target.at[pl.ds(i * SLAB, SLAB), :]))
+    copies = [pltpu.make_async_copy(*move, sem.at[i]) for i, move in enumerate(moves)]
+    for copy in copies:
+        copy.start()
+    for dy, piece in ((0, four_ref), (1, up_ref), (3, down_ref)):
         for side in range(NX):
-            at = pl.ds(pl.multiple_of(place_ref[i * NX + side] * SLAB, SLAB), SLAB)
-            piece = rows[i][side]
-            first = 0 if piece is over_side else 2 * side
-            row_ref[at, :] = piece[first]
-            other_rows[at, :] = piece[first + 1]
-    for i in range(NZ):
-        at = pl.ds(i * SLAB, SLAB)
-        col_ref[at, :] = gathered_ref[i, 0]
-        other_cols[at, :] = gathered_ref[i, 1]
+            row_ref[row_at(dy, side), :] = piece[2 * side]
+            other_rows[row_at(dy, side), :] = piece[2 * side + 1]
+    for copy in copies:
+        copy.wait()
     per = BLOCK // 2
     odd = odd_ref[0] == 1
     sign = jnp.where(odd, -1.0, 1.0).astype(jnp.float32)
@@ -161,17 +173,21 @@
         m_ref[:, pl.ds(BLOCK + part * per, per)] = total_im.astype(jnp.bfloat16)
 
 
-def mix(place, odd, *arrays):
+def mix(place, odd, four, up, over, down, gathered, *kerns):
     points = pltpu.VMEM((BLOCK, LANES), jnp.bfloat16)
+    in_hbm = pl.BlockSpec(memory_space=pltpu.HBM)
+    specs = [IN_VMEM] * 2 + [in_hbm] * 2 + [IN_VMEM, in_hbm] + [IN_VMEM] * 3
+    arrays = [near(four), near(up), *map(away, over), near(down), away(gathered), *map(near, kerns)]
     return pl.pallas_call(
         mix_body,
         out_shape=[pltpu.VMEM((BLOCK, 2 * BLOCK), jnp.bfloat16), points, points],
-        in_specs=[IN_SMEM] * 2 + [IN_VMEM] * len(arrays),
+        in_specs=[IN_SMEM] * 2 + specs,
         out_specs=[IN_VMEM] * 3,
-        scratch_shapes=[pltpu.VMEM((BLOCK, LANES), jnp.bfloat16)] * 2,
+        scratch_shapes=[pltpu.VMEM((BLOCK, LANES), jnp.bfloat16)] * 2
+        + [pltpu.SemaphoreType.DMA((2 * NX + 2 * NZ,))],
         compiler_params=PARAMS,
         name="mix",
-    )(place, odd, *map(near, arrays))
+    )(place, odd, *arrays)
 
 
 def prepare_body(row_ref, col_ref, left_ref, right_ref):
@@ -199,26 +215,40 @@
     )(near(rows), near(cols))
 
 
-def project_body(m_ref, left_ref, right_ref, out_ref, x_ref):
+def project_body(m_ref, left_ref, right_ref, out_ref, x_ref, part_ref, sem):
     y = dot(m_ref[...], right_ref[...], 1, 0)
     high = y.astype(jnp.bfloat16)
     low = (y - high.astype(jnp.float32)).astype(jnp.bfloat16)
-    left = left_ref[...]
-    x = dot(left, jnp.concatenate([high, turned(high)], axis=0), 1, 0)
-    x += dot(left, jnp.concatenate([low, turned(low)], axis=0), 1, 0)
-    x_ref[pl.ds(0, NB), :] = -x
+    high = jnp.concatenate([high, turned(high)], axis=0)
+    low = jnp.concatenate([low, turned(low)], axis=0)
     x_ref[pl.ds(NB, 8), :] = jnp.zeros((8, LANES), jnp.float32)
-    for d in range(GROUPS * NZ):
-        out_ref[d] = x_ref[pl.ds(27 * d // 4, 8), :].astype(jnp.bfloat16)
+    copies = []
+    for part, (start, size) in enumerate(((0, 224), (224, 208))):
+        at = pl.ds(start, size)
+        x_ref[at, :] = -(dot(left_ref[at, :], high, 1, 0) + dot(left_ref[at, :], low, 1, 0))
+        some = GROUPS * NZ // 2
+        for d in range(part * some, (part + 1) * some):
+            part_ref[d] = x_ref[pl.ds(27 * d // 4, 8), :].astype(jnp.bfloat16)
+        chosen = pl.ds(part * some, some)
+        copy = pltpu.make_async_copy(part_ref.at[chosen], out_ref.at[chosen], sem.at[part])
+        copy.start()
+        copies.append(copy)
+    for copy in copies:
+        copy.wait()
 
 
 def project(m, left, right):
+    windows = (GROUPS * NZ, 8, LANES)
     return pl.pallas_call(
         project_body,
-        out_shape=pltpu.VMEM((GROUPS * NZ, 8, LANES), jnp.bfloat16),
+        out_shape=jax.ShapeDtypeStruct(windows, jnp.bfloat16),
         in_specs=[IN_VMEM] * 3,
-        out_specs=IN_VMEM,
-        scratch_shapes=[pltpu.VMEM((NB + 8, LANES), jnp.float32)],
+        out_specs=pl.BlockSpec(memory_space=pltpu.HBM),
+        scratch_shapes=[
+            pltpu.VMEM((NB + 8, LANES), jnp.float32),
+            pltpu.VMEM(windows, jnp.bfloat16),
+            pltpu.SemaphoreType.DMA((2,)),
+        ],
         compiler_params=PARAMS,
         name="project",
     )(near(m), near(left), near(right))
@@ -267,25 +297,24 @@
         shift(own, 0, 1, 0),
         other_side(own),
     )
-    diff_core, diff_far, far, own_side, far_side = lax.optimization_barrier(first)
+    diff_core, diff_far = first[:2]
+    far, own_side, far_side = lax.optimization_barrier(first)[2:]
 
     over_yx = [[g * NZ + z for g in range(GROUPS)] for z in range(NZ)]
     over_z = [[g * NZ + z for z in range(NZ)] for g in range(GROUPS)]
     four, both = bundle(own, far, own_side, far_side)
     gathered = lax.all_gather(both, "band", axis_index_groups=over_z)
     up, down = shift(four, 1, 0, 0), shift(four, -1, 0, 0)
-    over = shift(up[:2], 1, 0, 0), shift(down[2:], -1, 0, 0)
 
     shared, single = pack(odd, pair_kdiff, diff_core, diff_far, stored_kernel_index, kernels)
     mine = lax.all_to_all(shared, "band", 0, 0, axis_index_groups=over_yx)
     half = swap_groups(mine, 1)
-    single, over = lax.optimization_barrier((single, over))
+    single, up, down = lax.optimization_barrier((single, up, down))
+    over = shift(up[:2], 1, 0, 0), shift(down[2:], -1, 0, 0)
     kern = lax.all_to_all(single, "band", 0, 0, axis_index_groups=over_yx)
 
     place = jnp.stack([(y - dy) % NY * NX + (x - dx) % NX for dy in range(NY) for dx in range(NX)])
-    m_out, rows, cols = mix(
-        place, odd, four, up, *over, down, gathered, mine, half, kern
-    )
+    m_out, rows, cols = mix(place, odd, four, up, over, down, gathered, mine, half, kern)
     m_own = swap_groups(m_out, 1)
     left, right = prepare(rows, cols)
     total = reduce_windows(project(m_own, left, right))

time: 126 us -> 122 us (0.968)
  local copies, waits for them, and re-layouts: 7.28 us -> 2.41 us
  Pallas kernels: 13.1 us -> 16 us
  waiting for transfers between devices: 56.3 us -> 53.6 us
    all_to_all x1, waiting for transfers between devices: 12.5 us -> 0.01 us  [on_device(): kern = lax.all_to_all(single, 'band', 0, 0, axis_index_groups=over_yx)]
    all_to_all x1, waiting for transfers between devices: 0.01 us -> 6.36 us  [on_device(): mine = lax.all_to_all(shared, 'band', 0, 0, axis_index_groups=over_yx)]
    unnamed x14 -> x2, local copies, waits for them, and re-layouts: 6.89 us -> 0.66 us
    ppermute x5, waiting for transfers between devices: 10.2 us -> 15.4 us  [shift(): return lax.ppermute(block, 'band', band_route(dy, dx, dz))]
    ppermute x5, waiting for transfers between devices: 8.13 us -> 6.31 us  [swap_groups(): return lax.ppermute(block, 'kgrp', [(k, k ^ bit) for k in range(4)])]
    pallas_call x1, Pallas kernels: 3.28 us -> 4.97 us  [mix(): pl.pallas_call(mix_body, out_shape=[pltpu.VMEM((BLOCK, 2 * BLOCK), jnp.bf...]
    slice x2, local copies, waits for them, and re-layouts: 0.04 us -> 1.41 us  [on_device(): over = (shift(up[:2], 1, 0, 0), shift(down[2:], -1, 0, 0))]
  transfers between devices with their start and end apart: 15 -> 15, of which waited for: 8 -> 8; matrix products, arithmetic and copies ran while one was open for 0% -> 1% of each run, Pallas kernels for 3% -> 4%
where the time goes in v11:
time: 122 us; the launch traced here: 121 us
  waiting for transfers between devices  53.6 us (44%)
  starting transfers between devices  33.7 us (28%)
  Pallas kernels  16 us (13%)
  between operations  14.1 us (12%)
  local copies, waits for them, and re-layouts  2.41 us (2%)
    all_to_all x1, waiting for transfers between devices, reduce_windows(): parts = lax.all_to_all(windows, 'band', 0, 0)  25.5 us
    ppermute x5, waiting for transfers between devices, shift(): return lax.ppermute(block, 'band', band_route(dy, dx, dz))  15.4 us
    all_to_all x1, starting transfers between devices, reduce_windows(): parts = lax.all_to_all(windows, 'band', 0, 0)  11.2 us
    all_to_all x1, waiting for transfers between devices, on_device(): mine = lax.all_to_all(shared, 'band', 0, 0, axis_index_groups=over_yx)  6.36 us
    ppermute x5, waiting for transfers between devices, swap_groups(): return lax.ppermute(block, 'kgrp', [(k, k ^ bit) for k in range(4)])  6.31 us
    all_to_all x1, starting transfers between devices, on_device(): mine = lax.all_to_all(shared, 'band', 0, 0, axis_index_groups=over_yx)  5.98 us
    ppermute x5, starting transfers between devices, shift(): return lax.ppermute(block, 'band', band_route(dy, dx, dz))  5.81 us
    pallas_call x1, Pallas kernels, mix(): pl.pallas_call(mix_body, out_shape=[pltpu.VMEM((BLOCK, 2 * BLOCK), jnp.bf...  4.97 us
  transfers between devices with their start and end apart: 15, of which 8 were waited for; matrix products, arithmetic and copies ran while one was open for 1% of the time, Pallas kernels for 4%

profile of v11, /device:TPU:6, one launch (start us, length us, event | category | flops | bytes accessed | tf_op | source)
XLA Modules:
  0.0 120.7 jit_solution(14668094111207895368)
XLA Ops:
  6.5 1.0 lay.1.own_ref
  7.5 2.3 %collective-permute-start.4 = (bf16[64,896]{1,0:T(8,128)(2,1)S(1)}, bf16[64,896]{1,0:T(8,128)(2,1)S(1)}, u32[]{:S(2)}, u32[]{:S(2)}) collective-permute-start(bf16[64,896]{1,0:T(8,128)(2,1)S(1)} %lay.1.own_ref), channel_id=1, source_target_pairs={{128,8},{129,9},{130,10},{131,11},{132,12},{133,13},{134,14},{135,... | collective-permute-start | bytes 344072 | tf_op jit(solution)/shard_map/ppermute | solution.py:46
  9.8 2.5 %collective-permute-start.2 = (bf16[64,896]{1,0:T(8,128)(2,1)S(1)}, bf16[64,896]{1,0:T(8,128)(2,1)S(1)}, u32[]{:S(2)}, u32[]{:S(2)}) collective-permute-start(bf16[64,896]{1,0:T(8,128)(2,1)S(1)} %lay.1.own_ref), channel_id=1, source_target_pairs={{0,128},{64,192},{128,0},{192,64},{1,129},{65,193},{129,1},{193,65... | collective-permute-start | bytes 344072 | tf_op jit(solution)/shard_map/ppermute | solution.py:40
  12.3 1.0 collective-permute-start.1
  13.3 0.2 collective-permute-done.core_ref
  13.5 4.1 %collective-permute-done.1.far_ref = s32[1]{0:T(128)} collective-permute-done((s32[1]{0:T(128)}, s32[1]{0:T(128)}, u32[]{:S(2)}, u32[]{:S(2)}) %collective-permute-start.1) | collective-permute-done | bytes 36 | tf_op jit(solution)/shard_map/ppermute | solution.py:40
  17.6 0.7 bundle.1
  19.0 3.1 %collective-permute-start.6 = (bf16[4,64,896]{2,1,0:T(8,128)(2,1)S(1)}, bf16[4,64,896]{2,1,0:T(8,128)(2,1)S(1)}, u32[]{:S(2)}, u32[]{:S(2)}) collective-permute-start(bf16[4,64,896]{2,1,0:T(8,128)(2,1)S(1)} %get-tuple-element.23.refs_0_), channel_id=1, source_target_pairs={{0,48},{1,49},{2,50},{3,51},{4,52},{5,53},{6,54},{7,55},{8,56},{9,... | collective-permute-start | bytes 1376264 | tf_op jit(solution)/shard_map/ppermute | solution.py:36
  22.1 0.7 copy-done
  22.7 4.5 %pack.1 = (bf16[8,64,512]{2,1,0:T(8,128)(2,1)}, bf16[8,2,64,512]{3,2,1,0:T(8,128)(2,1)}) custom-call(s32[1]{0:T(128)} %bitcast.8.odd_ref, s32[1]{0:T(128)S(6)} %copy.5.own_ref, s32[1]{0:T(128)} %collective-permute-done.core_ref, s32[1]{0:T(128)} %collective-permute-done.1.far_ref, s32[8]{0:T(128)S(1)} %copy-done, bf16[4,2,64,4096]{3,2,1,0:T(8,128)(2,1)} %kernels_ref.1), custom_call_target="tpu_custom_call" | custom-call | tf_op jit(solution)/shard_map/pack/pallas_call | solution.py:113
  27.3 6.0 %all-to-all-start = ((bf16[8,64,512]{2,1,0:T(8,128)(2,1)}), bf16[8,64,512]{2,1,0:T(8,128)(2,1)S(1)}, u32[]{:S(2)}, u32[]{:S(2)}) async-start(bf16[8,64,512]{2,1,0:T(8,128)(2,1)} %get-tuple-element.28), calls=%async_computation | async-start | bytes 1048576 | tf_op jit(solution)/shard_map/all_to_all | solution.py:310
  33.3 1.8 %collective-permute-done.5.refs_1_ = bf16[4,64,896]{2,1,0:T(8,128)(2,1)S(1)} collective-permute-done((bf16[4,64,896]{2,1,0:T(8,128)(2,1)S(1)}, bf16[4,64,896]{2,1,0:T(8,128)(2,1)S(1)}, u32[]{:S(2)}, u32[]{:S(2)}) %collective-permute-start.5) | collective-permute-done | bytes 458784 | tf_op jit(solution)/shard_map/ppermute | solution.py:36
  35.0 6.4 %all-to-all-done.refs_6_ = bf16[8,64,512]{2,1,0:T(8,128)(2,1)S(1)} async-done(((bf16[8,64,512]{2,1,0:T(8,128)(2,1)}), bf16[8,64,512]{2,1,0:T(8,128)(2,1)S(1)}, u32[]{:S(2)}, u32[]{:S(2)}) %all-to-all-start) | async-done | bytes 524320 | tf_op jit(solution)/shard_map/all_to_all | solution.py:310
  41.4 4.6 %all-to-all-start.1 = ((bf16[8,2,64,512]{3,2,1,0:T(8,128)(2,1)}), bf16[8,2,64,512]{3,2,1,0:T(8,128)(2,1)S(1)}, u32[]{:S(2)}, u32[]{:S(2)}) async-start(bf16[8,2,64,512]{3,2,1,0:T(8,128)(2,1)} %get-tuple-element.29), calls=%async_computation.1 | async-start | bytes 2097152 | tf_op jit(solution)/shard_map/all_to_all | solution.py:314
  46.0 0.7 slice.18
  46.7 0.7 slice.19
  47.4 2.7 %collective-permute-start.8 = (bf16[2,64,896]{2,1,0:T(8,128)(2,1)}, bf16[2,64,896]{2,1,0:T(8,128)(2,1)}, u32[]{:S(2)}, u32[]{:S(2)}) collective-permute-start(bf16[2,64,896]{2,1,0:T(8,128)(2,1)} %slice.19), channel_id=1, source_target_pairs={{0,48},{1,49},{2,50},{3,51},{4,52},{5,53},{6,54},{7,55},{8,56},{9,... | collective-permute-start | bytes 688136 | tf_op jit(solution)/shard_map/ppermute | solution.py:36
  50.2 0.1 stack.44.place_ref
  50.2 12.1 %collective-permute-done.8.refs_3_ = bf16[2,64,896]{2,1,0:T(8,128)(2,1)} collective-permute-done((bf16[2,64,896]{2,1,0:T(8,128)(2,1)}, bf16[2,64,896]{2,1,0:T(8,128)(2,1)}, u32[]{:S(2)}, u32[]{:S(2)}) %collective-permute-start.8) | collective-permute-done | bytes 229408 | tf_op jit(solution)/shard_map/ppermute | solution.py:36
  62.4 1.5 %collective-permute-done.7.refs_2_ = bf16[2,64,896]{2,1,0:T(8,128)(2,1)} collective-permute-done((bf16[2,64,896]{2,1,0:T(8,128)(2,1)}, bf16[2,64,896]{2,1,0:T(8,128)(2,1)}, u32[]{:S(2)}, u32[]{:S(2)}) %collective-permute-start.7) | collective-permute-done | bytes 229408 | tf_op jit(solution)/shard_map/ppermute | solution.py:36
  63.9 5.0 %mix.1 = (bf16[512,1024]{1,0:T(8,128)(2,1)S(1)}, bf16[512,896]{1,0:T(8,128)(2,1)S(1)}, bf16[512,896]{1,0:T(8,128)(2,1)S(1)}) custom-call(s32[8]{0:T(128)S(1)} %stack.44.place_ref, s32[1]{0:T(128)} %bitcast.8.odd_ref, bf16[4,64,896]{2,1,0:T(8,128)(2,1)S(1)} %get-tuple-element.23.refs_0_, bf16[4,64,896]{2,1,0:T(8,128)(2,1)S(1)} %collective-permute-done.5.refs_1_, ...), custom_call_target="tpu_custom_call" | custom-call | tf_op jit(solution)/shard_map/mix/pallas_call | solution.py:181
  68.9 0.3 collective-permute-start.10
  69.1 0.6 prepare.1
  69.7 2.1 %collective-permute-done.10.m_ref = bf16[512,1024]{1,0:T(8,128)(2,1)S(1)} collective-permute-done((bf16[512,1024]{1,0:T(8,128)(2,1)S(1)}, bf16[512,1024]{1,0:T(8,128)(2,1)S(1)}, u32[]{:S(2)}, u32[]{:S(2)}) %collective-permute-start.10) | collective-permute-done | bytes 1048608 | tf_op jit(solution)/shard_map/ppermute | solution.py:40
  71.8 4.2 %project.1 = bf16[64,8,896]{2,1,0:T(8,128)(2,1)} custom-call(bf16[512,1024]{1,0:T(8,128)(2,1)S(1)} %collective-permute-done.10.m_ref, bf16[432,1024]{1,0:T(8,128)(2,1)S(1)} %get-tuple-element.33.left_ref, bf16[1024,896]{1,0:T(8,128)(2,1)S(1)} %get-tuple-element.34.right_ref), custom_call_target="tpu_custom_call" | custom-call | tf_op jit(solution)/shard_map/project/pallas_call | solution.py:242
  76.0 11.2 %all-to-all-start.2 = ((bf16[64,8,896]{2,1,0:T(8,128)(2,1)}), bf16[64,8,896]{2,1,0:T(8,128)(2,1)S(1)}, u32[]{:S(2)}, u32[]{:S(2)}) async-start(bf16[64,8,896]{2,1,0:T(8,128)(2,1)} %project.1), calls=%async_computation.2 | async-start | bytes 1835008 | tf_op jit(solution)/shard_map/all_to_all | solution.py:279
  87.2 25.5 %all-to-all-done.2 = bf16[64,8,896]{2,1,0:T(8,128)(2,1)S(1)} async-done(((bf16[64,8,896]{2,1,0:T(8,128)(2,1)}), bf16[64,8,896]{2,1,0:T(8,128)(2,1)S(1)}, u32[]{:S(2)}, u32[]{:S(2)}) %all-to-all-start.2) | async-done | bytes 917536 | tf_op jit(solution)/shard_map/all_to_all | solution.py:279
  112.7 0.2 convert_reduce_fusion
  112.9 0.1 fusion.3
  112.9 0.1 stack.45
  113.0 0.1 stack.46
  113.1 0.7 fusion.1
  (17 shorter events, 0.1 us)
Async XLA Ops:
  6.5 57.3 %all-gather.3.cloned.1.call-start = ((), (), s32[]{:S(2)}) async-start(), calls=%async_computation.3 | async-start | bytes 2064384 | tf_op jit(solution)/shard_map/all_gather | solution.py:306
  7.5 10.0 %collective-permute-start.4 = (bf16[64,896]{1,0:T(8,128)(2,1)S(1)}, bf16[64,896]{1,0:T(8,128)(2,1)S(1)}, u32[]{:S(2)}, u32[]{:S(2)}) collective-permute-start(bf16[64,896]{1,0:T(8,128)(2,1)S(1)} %lay.1.own_ref), channel_id=1, source_target_pairs={{128,8},{129,9},{130,10},{131,11},{132,12},{133,13},{134,14},{135,... | collective-permute-start | bytes 344072 | tf_op jit(solution)/shard_map/ppermute | solution.py:46
  9.8 7.8 %collective-permute-start.3 = (bf16[64,896]{1,0:T(8,128)(2,1)S(1)}, bf16[64,896]{1,0:T(8,128)(2,1)S(1)}, u32[]{:S(2)}, u32[]{:S(2)}) collective-permute-start(bf16[64,896]{1,0:T(8,128)(2,1)S(1)} %lay.1.own_ref), channel_id=1, source_target_pairs={{0,8},{1,9},{2,10},{3,11},{4,12},{5,13},{6,14},{7,15},{8,0},{9,1},... | collective-permute-start | bytes 344072 | tf_op jit(solution)/shard_map/ppermute | solution.py:36
  9.8 7.8 %collective-permute-start.2 = (bf16[64,896]{1,0:T(8,128)(2,1)S(1)}, bf16[64,896]{1,0:T(8,128)(2,1)S(1)}, u32[]{:S(2)}, u32[]{:S(2)}) collective-permute-start(bf16[64,896]{1,0:T(8,128)(2,1)S(1)} %lay.1.own_ref), channel_id=1, source_target_pairs={{0,128},{64,192},{128,0},{192,64},{1,129},{65,193},{129,1},{193,65... | collective-permute-start | bytes 344072 | tf_op jit(solution)/shard_map/ppermute | solution.py:40
  12.3 1.2 %collective-permute-start = (s32[1]{0:T(128)}, s32[1]{0:T(128)}, u32[]{:S(2)}, u32[]{:S(2)}) collective-permute-start(s32[1]{0:T(128)} %param.6), channel_id=1, source_target_pairs={{0,64},{64,0},{128,192},{192,128},{1,65},{65,1},{129,193},{193,129... | collective-permute-start | bytes 20 | tf_op jit(solution)/shard_map/ppermute | solution.py:40
  12.3 5.3 %collective-permute-start.1 = (s32[1]{0:T(128)}, s32[1]{0:T(128)}, u32[]{:S(2)}, u32[]{:S(2)}) collective-permute-start(s32[1]{0:T(128)} %param.6), channel_id=1, source_target_pairs={{0,128},{64,192},{128,0},{192,64},{1,129},{65,193},{129,1},{193,65... | collective-permute-start | bytes 20 | tf_op jit(solution)/shard_map/ppermute | solution.py:40
  19.0 14.3 %collective-permute-start.6 = (bf16[4,64,896]{2,1,0:T(8,128)(2,1)S(1)}, bf16[4,64,896]{2,1,0:T(8,128)(2,1)S(1)}, u32[]{:S(2)}, u32[]{:S(2)}) collective-permute-start(bf16[4,64,896]{2,1,0:T(8,128)(2,1)S(1)} %get-tuple-element.23.refs_0_), channel_id=1, source_target_pairs={{0,48},{1,49},{2,50},{3,51},{4,52},{5,53},{6,54},{7,55},{8,56},{9,... | collective-permute-start | bytes 1376264 | tf_op jit(solution)/shard_map/ppermute | solution.py:36
  22.1 13.0 %collective-permute-start.5 = (bf16[4,64,896]{2,1,0:T(8,128)(2,1)S(1)}, bf16[4,64,896]{2,1,0:T(8,128)(2,1)S(1)}, u32[]{:S(2)}, u32[]{:S(2)}) collective-permute-start(bf16[4,64,896]{2,1,0:T(8,128)(2,1)S(1)} %get-tuple-element.23.refs_0_), channel_id=1, source_target_pairs={{0,16},{1,17},{2,18},{3,19},{4,20},{5,21},{6,22},{7,23},{8,24},{9,... | collective-permute-start | bytes 1376264 | tf_op jit(solution)/shard_map/ppermute | solution.py:36
  22.1 0.7 copy-start
  27.3 14.1 %all-to-all-start = ((bf16[8,64,512]{2,1,0:T(8,128)(2,1)}), bf16[8,64,512]{2,1,0:T(8,128)(2,1)S(1)}, u32[]{:S(2)}, u32[]{:S(2)}) async-start(bf16[8,64,512]{2,1,0:T(8,128)(2,1)} %get-tuple-element.28), calls=%async_computation | async-start | bytes 1048576 | tf_op jit(solution)/shard_map/all_to_all | solution.py:310
  41.4 22.4 %all-to-all-start.1 = ((bf16[8,2,64,512]{3,2,1,0:T(8,128)(2,1)}), bf16[8,2,64,512]{3,2,1,0:T(8,128)(2,1)S(1)}, u32[]{:S(2)}, u32[]{:S(2)}) async-start(bf16[8,2,64,512]{3,2,1,0:T(8,128)(2,1)} %get-tuple-element.29), calls=%async_computation.1 | async-start | bytes 2097152 | tf_op jit(solution)/shard_map/all_to_all | solution.py:314
  46.0 17.8 %collective-permute-start.9 = (bf16[8,64,512]{2,1,0:T(8,128)(2,1)S(1)}, bf16[8,64,512]{2,1,0:T(8,128)(2,1)S(1)}, u32[]{:S(2)}, u32[]{:S(2)}) collective-permute-start(bf16[8,64,512]{2,1,0:T(8,128)(2,1)S(1)} %all-to-all-done.refs_6_), channel_id=1, source_target_pairs={{0,64},{64,0},{128,192},{192,128},{1,65},{65,1},{129,193},{193,129... | collective-permute-start | bytes 1572872 | tf_op jit(solution)/shard_map/ppermute | solution.py:40
  47.4 14.9 %collective-permute-start.8 = (bf16[2,64,896]{2,1,0:T(8,128)(2,1)}, bf16[2,64,896]{2,1,0:T(8,128)(2,1)}, u32[]{:S(2)}, u32[]{:S(2)}) collective-permute-start(bf16[2,64,896]{2,1,0:T(8,128)(2,1)} %slice.19), channel_id=1, source_target_pairs={{0,48},{1,49},{2,50},{3,51},{4,52},{5,53},{6,54},{7,55},{8,56},{9,... | collective-permute-start | bytes 688136 | tf_op jit(solution)/shard_map/ppermute | solution.py:36
  50.2 13.7 %collective-permute-start.7 = (bf16[2,64,896]{2,1,0:T(8,128)(2,1)}, bf16[2,64,896]{2,1,0:T(8,128)(2,1)}, u32[]{:S(2)}, u32[]{:S(2)}) collective-permute-start(bf16[2,64,896]{2,1,0:T(8,128)(2,1)} %slice.18), channel_id=1, source_target_pairs={{0,16},{1,17},{2,18},{3,19},{4,20},{5,21},{6,22},{7,23},{8,24},{9,... | collective-permute-start | bytes 688136 | tf_op jit(solution)/shard_map/ppermute | solution.py:36
  68.9 2.9 %collective-permute-start.10 = (bf16[512,1024]{1,0:T(8,128)(2,1)S(1)}, bf16[512,1024]{1,0:T(8,128)(2,1)S(1)}, u32[]{:S(2)}, u32[]{:S(2)}) collective-permute-start(bf16[512,1024]{1,0:T(8,128)(2,1)S(1)} %get-tuple-element.30), channel_id=1, source_target_pairs={{0,64},{64,0},{128,192},{192,128},{1,65},{65,1},{129,193},{193,129... | collective-permute-start | bytes 3145736 | tf_op jit(solution)/shard_map/ppermute | solution.py:40
  76.0 36.7 %all-to-all-start.2 = ((bf16[64,8,896]{2,1,0:T(8,128)(2,1)}), bf16[64,8,896]{2,1,0:T(8,128)(2,1)S(1)}, u32[]{:S(2)}, u32[]{:S(2)}) async-start(bf16[64,8,896]{2,1,0:T(8,128)(2,1)} %project.1), calls=%async_computation.2 | async-start | bytes 1835008 | tf_op jit(solution)/shard_map/all_to_all | solution.py:279
Sparse Core Ops, SparseCore 0:
  18.4 42.7 all-gather.2

commit v12 on v11

--- a/solution.py
+++ b/solution.py
@@ -14,6 +14,7 @@
 REST = NB - WHOLE
 TAIL = 2 * WHOLE
 LANES = TAIL + 128
+EARLY = 5
 VMEM = 24 * 1024 * 1024
 
 IN_VMEM = pl.BlockSpec(memory_space=pltpu.VMEM)
@@ -124,21 +125,24 @@
     )(odd, own, core, far, stored, away(kernels))
 
 
-def mix_body(place_ref, odd_ref, *refs):
-    four_ref, up_ref, over_here, over_side, down_ref, gathered_ref = refs[:6]
-    mine_ref, half_ref, kern_ref = refs[6:9]
-    m_ref, row_ref, col_ref, other_rows, other_cols, sem = refs[9:]
+def mix_body(place_ref, slot_ref, odd_ref, *refs):
+    four_ref, up_ref, over_here, over_side, down_ref = refs[:5]
+    cols, (mine_ref, half_ref, kern_ref) = refs[5 : 5 + NZ], refs[5 + NZ : 8 + NZ]
+    m_ref, row_ref, col_ref, other_rows, other_cols, sem = refs[8 + NZ :]
 
     def row_at(dy, side):
         return pl.ds(pl.multiple_of(place_ref[dy * NX + side] * SLAB, SLAB), SLAB)
+
+    def col_at(i):
+        return pl.ds(pl.multiple_of(slot_ref[i] * SLAB, SLAB), SLAB)
 
     moves = []
     for side, piece in enumerate((over_here, over_side)):
         moves.append((piece.at[0], row_ref.at[row_at(2, side), :]))
         moves.append((piece.at[1], other_rows.at[row_at(2, side), :]))
-    for target, which in ((col_ref, 0), (other_cols, 1)):
-        for i in range(NZ):
-            moves.append((gathered_ref.at[i, which], target.at[pl.ds(i * SLAB, SLAB), :]))
+    for i, piece in enumerate(cols[:EARLY]):
+        moves.append((piece.at[0], col_ref.at[col_at(i), :]))
+        moves.append((piece.at[1], other_cols.at[col_at(i), :]))
     copies = [pltpu.make_async_copy(*move, sem.at[i]) for i, move in enumerate(moves)]
     for copy in copies:
         copy.start()
@@ -146,6 +150,9 @@
         for side in range(NX):
             row_ref[row_at(dy, side), :] = piece[2 * side]
             other_rows[row_at(dy, side), :] = piece[2 * side + 1]
+    for i in range(EARLY, NZ):
+        col_ref[col_at(i), :] = cols[i][0]
+        other_cols[col_at(i), :] = cols[i][1]
     for copy in copies:
         copy.wait()
     per = BLOCK // 2
@@ -173,21 +180,23 @@
         m_ref[:, pl.ds(BLOCK + part * per, per)] = total_im.astype(jnp.bfloat16)
 
 
-def mix(place, odd, four, up, over, down, gathered, *kerns):
+def mix(place, slots, odd, four, up, over, down, cols, *kerns):
     points = pltpu.VMEM((BLOCK, LANES), jnp.bfloat16)
     in_hbm = pl.BlockSpec(memory_space=pltpu.HBM)
-    specs = [IN_VMEM] * 2 + [in_hbm] * 2 + [IN_VMEM, in_hbm] + [IN_VMEM] * 3
-    arrays = [near(four), near(up), *map(away, over), near(down), away(gathered), *map(near, kerns)]
+    late = NZ - EARLY
+    specs = [IN_VMEM] * 2 + [in_hbm] * 2 + [IN_VMEM] + [in_hbm] * EARLY + [IN_VMEM] * (late + 3)
+    arrays = [near(four), near(up), *map(away, over), near(down)]
+    arrays += [*map(away, cols[:EARLY]), *map(near, cols[EARLY:]), *map(near, kerns)]
     return pl.pallas_call(
         mix_body,
         out_shape=[pltpu.VMEM((BLOCK, 2 * BLOCK), jnp.bfloat16), points, points],
-        in_specs=[IN_SMEM] * 2 + specs,
+        in_specs=[IN_SMEM] * 3 + specs,
         out_specs=[IN_VMEM] * 3,
         scratch_shapes=[pltpu.VMEM((BLOCK, LANES), jnp.bfloat16)] * 2
-        + [pltpu.SemaphoreType.DMA((2 * NX + 2 * NZ,))],
+        + [pltpu.SemaphoreType.DMA((2 * NX + 2 * EARLY,))],
         compiler_params=PARAMS,
         name="mix",
-    )(place, odd, *arrays)
+    )(place, slots, odd, *arrays)
 
 
 def prepare_body(row_ref, col_ref, left_ref, right_ref):
@@ -213,6 +222,11 @@
         compiler_params=PARAMS,
         name="prepare",
     )(near(rows), near(cols))
+
+
+def place_of(d):
+    yx, z = d // NZ, d % NZ
+    return (yx * 2 + z % 2) * (NZ // 2) + z // 2
 
 
 def project_body(m_ref, left_ref, right_ref, out_ref, x_ref, part_ref, sem):
@@ -228,7 +242,7 @@
         x_ref[at, :] = -(dot(left_ref[at, :], high, 1, 0) + dot(left_ref[at, :], low, 1, 0))
         some = GROUPS * NZ // 2
         for d in range(part * some, (part + 1) * some):
-            part_ref[d] = x_ref[pl.ds(27 * d // 4, 8), :].astype(jnp.bfloat16)
+            part_ref[place_of(d)] = x_ref[pl.ds(27 * d // 4, 8), :].astype(jnp.bfloat16)
         chosen = pl.ds(part * some, some)
         copy = pltpu.make_async_copy(part_ref.at[chosen], out_ref.at[chosen], sem.at[part])
         copy.start()
@@ -266,7 +280,7 @@
         bundle_body,
         out_shape=[
             pltpu.VMEM((4, SLAB, LANES), jnp.bfloat16),
-            jax.ShapeDtypeStruct((2, SLAB, LANES), jnp.bfloat16),
+            pltpu.VMEM((2, SLAB, LANES), jnp.bfloat16),
         ],
         in_specs=[IN_VMEM] * 4,
         out_specs=[IN_VMEM] * 2,
@@ -276,8 +290,13 @@
 
 
 def reduce_windows(windows):
-    parts = lax.all_to_all(windows, "band", 0, 0)
-    total = jnp.sum(parts.astype(jnp.float32), axis=0)
+    quads = NZ // 2
+    wide = [[g * NZ + 2 * j + i for g in range(GROUPS) for i in range(2)] for j in range(quads)]
+    deep = [[g * NZ + 2 * j + i for j in range(quads)] for g in range(GROUPS) for i in range(2)]
+    parts = windows.reshape(2 * GROUPS, quads, 8, LANES)
+    parts = lax.all_to_all(parts, "band", 0, 0, axis_index_groups=wide)
+    parts = jnp.sum(parts.astype(jnp.float32), axis=0)
+    total = jnp.sum(lax.all_to_all(parts, "band", 0, 0, axis_index_groups=deep), axis=0)
     real = jnp.concatenate([total[:, :WHOLE], total[:, TAIL : TAIL + REST]], axis=1)
     imag = jnp.concatenate([total[:, WHOLE:TAIL], total[:, TAIL + 64 : TAIL + 64 + REST]], axis=1)
     return jnp.stack([real, imag])
@@ -286,7 +305,7 @@
 def on_device(orbitals, kernels, pair_kdiff, stored_kernel_index):
     group = lax.axis_index("kgrp")
     band = lax.axis_index("band")
-    y, x = band // (NX * NZ), band // NZ % NX
+    y, x, z = band // (NX * NZ), band // NZ % NX, band % NZ
     odd = (group % 2).reshape(1)
 
     own = lay(orbitals)
@@ -300,10 +319,13 @@
     diff_core, diff_far = first[:2]
     far, own_side, far_side = lax.optimization_barrier(first)[2:]
 
-    over_yx = [[g * NZ + z for g in range(GROUPS)] for z in range(NZ)]
-    over_z = [[g * NZ + z for z in range(NZ)] for g in range(GROUPS)]
+    over_yx = [[g * NZ + i for g in range(GROUPS)] for i in range(NZ)]
     four, both = bundle(own, far, own_side, far_side)
-    gathered = lax.all_gather(both, "band", axis_index_groups=over_z)
+    cols, ahead, behind = [both], both, both
+    for _ in range(3):
+        ahead, behind = shift(ahead, 0, 0, 1), shift(behind, 0, 0, -1)
+        cols += [ahead, behind]
+    cols.append(shift(ahead, 0, 0, 1))
     up, down = shift(four, 1, 0, 0), shift(four, -1, 0, 0)
 
     shared, single = pack(odd, pair_kdiff, diff_core, diff_far, stored_kernel_index, kernels)
@@ -314,7 +336,8 @@
     kern = lax.all_to_all(single, "band", 0, 0, axis_index_groups=over_yx)
 
     place = jnp.stack([(y - dy) % NY * NX + (x - dx) % NX for dy in range(NY) for dx in range(NX)])
-    m_out, rows, cols = mix(place, odd, four, up, over, down, gathered, mine, half, kern)
+    slots = jnp.stack([(z + i) % NZ for i in (0, -1, 1, -2, 2, -3, 3, -4)])
+    m_out, rows, cols = mix(place, slots, odd, four, up, over, down, cols, mine, half, kern)
     m_own = swap_groups(m_out, 1)
     left, right = prepare(rows, cols)
     total = reduce_windows(project(m_own, left, right))

time: 122 us -> 116 us (0.951); the launches traced: 121 us -> 116 us
  waiting for transfers between devices: 53.6 us -> 33.7 us
  blocking collectives: 0 us -> 19.3 us
  between operations: 14.1 us -> 1.11 us
  starting transfers between devices: 33.7 us -> 40.7 us
    all_to_all x0 -> x1, blocking collectives: none -> 19.3 us  [reduce_windows(): parts = lax.all_to_all(parts, 'band', 0, 0, axis_index_groups=wide)]
    all_to_all x1, waiting for transfers between devices: 25.5 us -> 8.85 us  [reduce_windows(): lax.all_to_all(parts, 'band', 0, 0, axis_index_groups=deep)]
    ppermute x5 -> x12, starting transfers between devices: 5.81 us -> 20.9 us  [shift(): return lax.ppermute(block, 'band', band_route(dy, dx, dz))]
    all_to_all x1, starting transfers between devices: 11.2 us -> 3.31 us  [reduce_windows(): lax.all_to_all(parts, 'band', 0, 0, axis_index_groups=deep)]
    ppermute x5 -> x12, waiting for transfers between devices: 15.4 us -> 13 us  [shift(): return lax.ppermute(block, 'band', band_route(dy, dx, dz))]
  transfers between devices with their start and end apart: 15 -> 21, of which waited for: 8 -> 9; matrix products, arithmetic and copies ran while one was open for 1% -> 1% of each run, Pallas kernels for 4% -> 5%
where the time goes in v12:
time: 116 us
  starting transfers between devices  40.7 us (35%)
  waiting for transfers between devices  33.7 us (29%)
  blocking collectives  19.3 us (17%)
  Pallas kernels  16.4 us (14%)
  local copies, waits for them, and re-layouts  3.26 us (3%)
  other arithmetic  1.52 us (1%)
    ppermute x12, starting transfers between devices, shift(): return lax.ppermute(block, 'band', band_route(dy, dx, dz))  20.9 us
    all_to_all x1, blocking collectives, reduce_windows(): parts = lax.all_to_all(parts, 'band', 0, 0, axis_index_groups=wide)  19.3 us
    ppermute x12, waiting for transfers between devices, shift(): return lax.ppermute(block, 'band', band_route(dy, dx, dz))  13 us
    all_to_all x1, waiting for transfers between devices, reduce_windows(): lax.all_to_all(parts, 'band', 0, 0, axis_index_groups=deep)  8.85 us
    all_to_all x1, waiting for transfers between devices, on_device(): mine = lax.all_to_all(shared, 'band', 0, 0, axis_index_groups=over_yx)  6.37 us
    all_to_all x1, starting transfers between devices, on_device(): mine = lax.all_to_all(shared, 'band', 0, 0, axis_index_groups=over_yx)  5.98 us
    ppermute x5, waiting for transfers between devices, swap_groups(): return lax.ppermute(block, 'kgrp', [(k, k ^ bit) for k in range(4)])  5.47 us
    pallas_call x1, Pallas kernels, mix(): pl.pallas_call(mix_body, out_shape=[pltpu.VMEM((BLOCK, 2 * BLOCK), jnp.bf...  5.36 us
  transfers between devices with their start and end apart: 21, of which 9 were waited for; matrix products, arithmetic and copies ran while one was open for 1% of the time, Pallas kernels for 5%

profile of v12, /device:TPU:6, one launch (start us, length us, event | category | flops | bytes accessed | tf_op | source)
XLA Modules:
  0.0 116.0 jit_solution(17995272037897062359)
XLA Ops:
  0.0 1.0 lay.1.own_ref
  1.0 2.3 %collective-permute-start.4 = (bf16[64,896]{1,0:T(8,128)(2,1)S(1)}, bf16[64,896]{1,0:T(8,128)(2,1)S(1)}, u32[]{:S(2)}, u32[]{:S(2)}) collective-permute-start(bf16[64,896]{1,0:T(8,128)(2,1)S(1)} %lay.1.own_ref), channel_id=1, source_target_pairs={{128,8},{129,9},{130,10},{131,11},{132,12},{133,13},{134,14},{135,... | collective-permute-start | bytes 344072 | tf_op jit(solution)/shard_map/ppermute | solution.py:47
  3.2 2.5 %collective-permute-start.2 = (bf16[64,896]{1,0:T(8,128)(2,1)S(1)}, bf16[64,896]{1,0:T(8,128)(2,1)S(1)}, u32[]{:S(2)}, u32[]{:S(2)}) collective-permute-start(bf16[64,896]{1,0:T(8,128)(2,1)S(1)} %lay.1.own_ref), channel_id=1, source_target_pairs={{0,128},{64,192},{128,0},{192,64},{1,129},{65,193},{129,1},{193,65... | collective-permute-start | bytes 344072 | tf_op jit(solution)/shard_map/ppermute | solution.py:41
  5.7 1.0 collective-permute-start.1
  7.5 3.4 %collective-permute-done.1.far_ref = s32[1]{0:T(128)} collective-permute-done((s32[1]{0:T(128)}, s32[1]{0:T(128)}, u32[]{:S(2)}, u32[]{:S(2)}) %collective-permute-start.1) | collective-permute-done | bytes 36 | tf_op jit(solution)/shard_map/ppermute | solution.py:41
  10.9 0.8 bundle.1
  11.6 3.0 %collective-permute-start.6 = (bf16[4,64,896]{2,1,0:T(8,128)(2,1)S(1)}, bf16[4,64,896]{2,1,0:T(8,128)(2,1)S(1)}, u32[]{:S(2)}, u32[]{:S(2)}) collective-permute-start(bf16[4,64,896]{2,1,0:T(8,128)(2,1)S(1)} %get-tuple-element.23.refs_0_), channel_id=1, source_target_pairs={{0,48},{1,49},{2,50},{3,51},{4,52},{5,53},{6,54},{7,55},{8,56},{9,... | collective-permute-start | bytes 1376264 | tf_op jit(solution)/shard_map/ppermute | solution.py:37
  15.3 4.7 %pack.1 = (bf16[8,64,512]{2,1,0:T(8,128)(2,1)}, bf16[8,2,64,512]{3,2,1,0:T(8,128)(2,1)}) custom-call(s32[1]{0:T(128)} %bitcast.16.odd_ref, s32[1]{0:T(128)S(6)} %copy.5.own_ref, s32[1]{0:T(128)} %collective-permute-done.core_ref, s32[1]{0:T(128)} %collective-permute-done.1.far_ref, s32[8]{0:T(128)S(1)} %copy-done, bf16[4,2,64,4096]{3,2,1,0:T(8,128)(2,1)} %kernels_ref.1), custom_call_target="tpu_custom_call" | custom-call | tf_op jit(solution)/shard_map/pack/pallas_call | solution.py:114
  20.0 6.0 %all-to-all-start = ((bf16[8,64,512]{2,1,0:T(8,128)(2,1)}), bf16[8,64,512]{2,1,0:T(8,128)(2,1)S(1)}, u32[]{:S(2)}, u32[]{:S(2)}) async-start(bf16[8,64,512]{2,1,0:T(8,128)(2,1)} %get-tuple-element.28), calls=%async_computation | async-start | bytes 1048576 | tf_op jit(solution)/shard_map/all_to_all | solution.py:332
  26.0 1.9 %collective-permute-start.9 = (bf16[2,64,896]{2,1,0:T(8,128)(2,1)}, bf16[2,64,896]{2,1,0:T(8,128)(2,1)}, u32[]{:S(2)}, u32[]{:S(2)}) collective-permute-start(bf16[2,64,896]{2,1,0:T(8,128)(2,1)} %get-tuple-element.27.refs_5_), channel_id=1, source_target_pairs={{0,1},{1,2},{2,3},{3,4},{4,5},{5,6},{6,7},{7,0},{8,9},{9,10},{10,1... | collective-permute-start | bytes 688136 | tf_op jit(solution)/shard_map/ppermute | solution.py:37
  27.9 6.4 %all-to-all-done.refs_13_ = bf16[8,64,512]{2,1,0:T(8,128)(2,1)S(1)} async-done(((bf16[8,64,512]{2,1,0:T(8,128)(2,1)}), bf16[8,64,512]{2,1,0:T(8,128)(2,1)S(1)}, u32[]{:S(2)}, u32[]{:S(2)}) %all-to-all-start) | async-done | bytes 524320 | tf_op jit(solution)/shard_map/all_to_all | solution.py:332
  34.3 4.6 %all-to-all-start.1 = ((bf16[8,2,64,512]{3,2,1,0:T(8,128)(2,1)}), bf16[8,2,64,512]{3,2,1,0:T(8,128)(2,1)S(1)}, u32[]{:S(2)}, u32[]{:S(2)}) async-start(bf16[8,2,64,512]{3,2,1,0:T(8,128)(2,1)} %get-tuple-element.29), calls=%async_computation.1 | async-start | bytes 2097152 | tf_op jit(solution)/shard_map/all_to_all | solution.py:336
  38.9 5.9 %collective-permute-start.10 = (bf16[2,64,896]{2,1,0:T(8,128)(2,1)}, bf16[2,64,896]{2,1,0:T(8,128)(2,1)S(1)}, u32[]{:S(2)}, u32[]{:S(2)}) collective-permute-start(bf16[2,64,896]{2,1,0:T(8,128)(2,1)} %get-tuple-element.27.refs_5_), channel_id=1, source_target_pairs={{0,7},{1,0},{2,1},{3,2},{4,3},{5,4},{6,5},{7,6},{8,15},{9,8},{10,9... | collective-permute-start | bytes 688136 | tf_op jit(solution)/shard_map/ppermute | solution.py:37
  44.8 3.8 %collective-permute-done.10.refs_7_ = bf16[2,64,896]{2,1,0:T(8,128)(2,1)S(1)} collective-permute-done((bf16[2,64,896]{2,1,0:T(8,128)(2,1)}, bf16[2,64,896]{2,1,0:T(8,128)(2,1)S(1)}, u32[]{:S(2)}, u32[]{:S(2)}) %collective-permute-start.10) | collective-permute-done | bytes 229408 | tf_op jit(solution)/shard_map/ppermute | solution.py:37
  48.6 0.7 copy-done.1
  49.3 3.6 %collective-permute-start.12 = (bf16[2,64,896]{2,1,0:T(8,128)(2,1)S(1)}, bf16[2,64,896]{2,1,0:T(8,128)(2,1)}, u32[]{:S(2)}, u32[]{:S(2)}) collective-permute-start(bf16[2,64,896]{2,1,0:T(8,128)(2,1)S(1)} %collective-permute-done.10.refs_7_), channel_id=1, source_target_pairs={{0,7},{1,0},{2,1},{3,2},{4,3},{5,4},{6,5},{7,6},{8,15},{9,8},{10,9... | collective-permute-start | bytes 688136 | tf_op jit(solution)/shard_map/ppermute | solution.py:37
  52.9 0.8 slice.18
  53.7 0.7 slice.19
  54.4 2.0 %collective-permute-done.12.refs_9_ = bf16[2,64,896]{2,1,0:T(8,128)(2,1)} collective-permute-done((bf16[2,64,896]{2,1,0:T(8,128)(2,1)S(1)}, bf16[2,64,896]{2,1,0:T(8,128)(2,1)}, u32[]{:S(2)}, u32[]{:S(2)}) %collective-permute-start.12) | collective-permute-done | bytes 229408 | tf_op jit(solution)/shard_map/ppermute | solution.py:37
  56.4 3.8 %collective-permute-start.14 = (bf16[2,64,896]{2,1,0:T(8,128)(2,1)}, bf16[2,64,896]{2,1,0:T(8,128)(2,1)}, u32[]{:S(2)}, u32[]{:S(2)}) collective-permute-start(bf16[2,64,896]{2,1,0:T(8,128)(2,1)} %collective-permute-done.12.refs_9_), channel_id=1, source_target_pairs={{0,7},{1,0},{2,1},{3,2},{4,3},{5,4},{6,5},{7,6},{8,15},{9,8},{10,9... | collective-permute-start | bytes 688136 | tf_op jit(solution)/shard_map/ppermute | solution.py:37
  60.3 2.7 %collective-permute-start.8 = (bf16[2,64,896]{2,1,0:T(8,128)(2,1)}, bf16[2,64,896]{2,1,0:T(8,128)(2,1)}, u32[]{:S(2)}, u32[]{:S(2)}) collective-permute-start(bf16[2,64,896]{2,1,0:T(8,128)(2,1)} %slice.19), channel_id=1, source_target_pairs={{0,48},{1,49},{2,50},{3,51},{4,52},{5,53},{6,54},{7,55},{8,56},{9,... | collective-permute-start | bytes 688136 | tf_op jit(solution)/shard_map/ppermute | solution.py:37
  63.4 0.7 collective-permute-done.14.refs_11_
  64.1 2.7 %collective-permute-done.8.refs_3_ = bf16[2,64,896]{2,1,0:T(8,128)(2,1)} collective-permute-done((bf16[2,64,896]{2,1,0:T(8,128)(2,1)}, bf16[2,64,896]{2,1,0:T(8,128)(2,1)}, u32[]{:S(2)}, u32[]{:S(2)}) %collective-permute-start.8) | collective-permute-done | bytes 229408 | tf_op jit(solution)/shard_map/ppermute | solution.py:37
  66.8 3.7 %collective-permute-done.7.refs_2_ = bf16[2,64,896]{2,1,0:T(8,128)(2,1)} collective-permute-done((bf16[2,64,896]{2,1,0:T(8,128)(2,1)}, bf16[2,64,896]{2,1,0:T(8,128)(2,1)}, u32[]{:S(2)}, u32[]{:S(2)}) %collective-permute-start.7) | collective-permute-done | bytes 229408 | tf_op jit(solution)/shard_map/ppermute | solution.py:37
  70.5 5.4 %mix.1 = (bf16[512,1024]{1,0:T(8,128)(2,1)S(1)}, bf16[512,896]{1,0:T(8,128)(2,1)S(1)}, bf16[512,896]{1,0:T(8,128)(2,1)S(1)}) custom-call(s32[8]{0:T(128)S(1)} %stack.71.place_ref, s32[8]{0:T(128)S(1)} %stack.80.slot_ref, s32[1]{0:T(128)} %bitcast.16.odd_ref, bf16[4,64,896]{2,1,0:T(8,128)(2,1)S(1)} %get-tuple-element.23.refs_0_, ...), custom_call_target="tpu_custom_call" | custom-call | tf_op jit(solution)/shard_map/mix/pallas_call | solution.py:190
  76.5 2.1 %collective-permute-done.17.m_ref = bf16[512,1024]{1,0:T(8,128)(2,1)S(1)} collective-permute-done((bf16[512,1024]{1,0:T(8,128)(2,1)S(1)}, bf16[512,1024]{1,0:T(8,128)(2,1)S(1)}, u32[]{:S(2)}, u32[]{:S(2)}) %collective-permute-start.17) | collective-permute-done | bytes 1048608 | tf_op jit(solution)/shard_map/ppermute | solution.py:41
  78.6 4.1 %project.1 = bf16[64,8,896]{2,1,0:T(8,128)(2,1)S(1)} custom-call(bf16[512,1024]{1,0:T(8,128)(2,1)S(1)} %collective-permute-done.17.m_ref, bf16[432,1024]{1,0:T(8,128)(2,1)S(1)} %get-tuple-element.33.left_ref, bf16[1024,896]{1,0:T(8,128)(2,1)S(1)} %get-tuple-element.34.right_ref), custom_call_target="tpu_custom_call" | custom-call | tf_op jit(solution)/shard_map/project/pallas_call | solution.py:256
  82.7 19.3 %all_to_all.20 = bf16[16,4,8,896]{3,2,1,0:T(8,128)(2,1)S(1)} all-to-all(bf16[16,4,8,896]{3,2,1,0:T(8,128)(2,1)S(1)} %bitcast.20), channel_id=1, replica_groups={{0,1,8,9,16,17,24,25,32,33,40,41,48,49,56,57},{2,3,10,11,18,19,26,27,34..., dimensions={0} | all-to-all | bytes 1835008 | tf_op jit(solution)/shard_map/all_to_all | solution.py:297
  102.0 0.8 convert_reduce_fusion
  102.8 3.3 %all-to-all-start.3 = ((f32[4,8,896]{2,1,0:T(8,128)}), f32[4,8,896]{2,1,0:T(8,128)S(1)}, u32[]{:S(2)}, u32[]{:S(2)}) async-start(f32[4,8,896]{2,1,0:T(8,128)} %convert_reduce_fusion), calls=%async_computation.3 | async-start | bytes 229376 | tf_op jit(solution)/shard_map/all_to_all | solution.py:299
  106.1 8.9 %all-to-all-done.3 = f32[4,8,896]{2,1,0:T(8,128)S(1)} async-done(((f32[4,8,896]{2,1,0:T(8,128)}), f32[4,8,896]{2,1,0:T(8,128)S(1)}, u32[]{:S(2)}, u32[]{:S(2)}) %all-to-all-start.3) | async-done | bytes 114720 | tf_op jit(solution)/shard_map/all_to_all | solution.py:299
  115.2 0.7 fusion.1
  (35 shorter events, 1.8 us)
Async XLA Ops:
  1.0 9.9 %collective-permute-start.4 = (bf16[64,896]{1,0:T(8,128)(2,1)S(1)}, bf16[64,896]{1,0:T(8,128)(2,1)S(1)}, u32[]{:S(2)}, u32[]{:S(2)}) collective-permute-start(bf16[64,896]{1,0:T(8,128)(2,1)S(1)} %lay.1.own_ref), channel_id=1, source_target_pairs={{128,8},{129,9},{130,10},{131,11},{132,12},{133,13},{134,14},{135,... | collective-permute-start | bytes 344072 | tf_op jit(solution)/shard_map/ppermute | solution.py:47
  3.2 7.6 %collective-permute-start.3 = (bf16[64,896]{1,0:T(8,128)(2,1)S(1)}, bf16[64,896]{1,0:T(8,128)(2,1)S(1)}, u32[]{:S(2)}, u32[]{:S(2)}) collective-permute-start(bf16[64,896]{1,0:T(8,128)(2,1)S(1)} %lay.1.own_ref), channel_id=1, source_target_pairs={{0,8},{1,9},{2,10},{3,11},{4,12},{5,13},{6,14},{7,15},{8,0},{9,1},... | collective-permute-start | bytes 344072 | tf_op jit(solution)/shard_map/ppermute | solution.py:37
  3.2 7.6 %collective-permute-start.2 = (bf16[64,896]{1,0:T(8,128)(2,1)S(1)}, bf16[64,896]{1,0:T(8,128)(2,1)S(1)}, u32[]{:S(2)}, u32[]{:S(2)}) collective-permute-start(bf16[64,896]{1,0:T(8,128)(2,1)S(1)} %lay.1.own_ref), channel_id=1, source_target_pairs={{0,128},{64,192},{128,0},{192,64},{1,129},{65,193},{129,1},{193,65... | collective-permute-start | bytes 344072 | tf_op jit(solution)/shard_map/ppermute | solution.py:41
  5.7 1.7 %collective-permute-start = (s32[1]{0:T(128)}, s32[1]{0:T(128)}, u32[]{:S(2)}, u32[]{:S(2)}) collective-permute-start(s32[1]{0:T(128)} %param.6), channel_id=1, source_target_pairs={{0,64},{64,0},{128,192},{192,128},{1,65},{65,1},{129,193},{193,129... | collective-permute-start | bytes 20 | tf_op jit(solution)/shard_map/ppermute | solution.py:41
  5.7 5.1 %collective-permute-start.1 = (s32[1]{0:T(128)}, s32[1]{0:T(128)}, u32[]{:S(2)}, u32[]{:S(2)}) collective-permute-start(s32[1]{0:T(128)} %param.6), channel_id=1, source_target_pairs={{0,128},{64,192},{128,0},{192,64},{1,129},{65,193},{129,1},{193,65... | collective-permute-start | bytes 20 | tf_op jit(solution)/shard_map/ppermute | solution.py:41
  11.6 16.3 %collective-permute-start.6 = (bf16[4,64,896]{2,1,0:T(8,128)(2,1)S(1)}, bf16[4,64,896]{2,1,0:T(8,128)(2,1)S(1)}, u32[]{:S(2)}, u32[]{:S(2)}) collective-permute-start(bf16[4,64,896]{2,1,0:T(8,128)(2,1)S(1)} %get-tuple-element.23.refs_0_), channel_id=1, source_target_pairs={{0,48},{1,49},{2,50},{3,51},{4,52},{5,53},{6,54},{7,55},{8,56},{9,... | collective-permute-start | bytes 1376264 | tf_op jit(solution)/shard_map/ppermute | solution.py:37
  14.7 13.3 %collective-permute-start.5 = (bf16[4,64,896]{2,1,0:T(8,128)(2,1)S(1)}, bf16[4,64,896]{2,1,0:T(8,128)(2,1)S(1)}, u32[]{:S(2)}, u32[]{:S(2)}) collective-permute-start(bf16[4,64,896]{2,1,0:T(8,128)(2,1)S(1)} %get-tuple-element.23.refs_0_), channel_id=1, source_target_pairs={{0,16},{1,17},{2,18},{3,19},{4,20},{5,21},{6,22},{7,23},{8,24},{9,... | collective-permute-start | bytes 1376264 | tf_op jit(solution)/shard_map/ppermute | solution.py:37
  14.7 0.7 copy-start
  20.0 14.3 %all-to-all-start = ((bf16[8,64,512]{2,1,0:T(8,128)(2,1)}), bf16[8,64,512]{2,1,0:T(8,128)(2,1)S(1)}, u32[]{:S(2)}, u32[]{:S(2)}) async-start(bf16[8,64,512]{2,1,0:T(8,128)(2,1)} %get-tuple-element.28), calls=%async_computation | async-start | bytes 1048576 | tf_op jit(solution)/shard_map/all_to_all | solution.py:332
  26.0 18.8 %collective-permute-start.9 = (bf16[2,64,896]{2,1,0:T(8,128)(2,1)}, bf16[2,64,896]{2,1,0:T(8,128)(2,1)}, u32[]{:S(2)}, u32[]{:S(2)}) collective-permute-start(bf16[2,64,896]{2,1,0:T(8,128)(2,1)} %get-tuple-element.27.refs_5_), channel_id=1, source_target_pairs={{0,1},{1,2},{2,3},{3,4},{4,5},{5,6},{6,7},{7,0},{8,9},{9,10},{10,1... | collective-permute-start | bytes 688136 | tf_op jit(solution)/shard_map/ppermute | solution.py:37
  34.3 36.2 %all-to-all-start.1 = ((bf16[8,2,64,512]{3,2,1,0:T(8,128)(2,1)}), bf16[8,2,64,512]{3,2,1,0:T(8,128)(2,1)S(1)}, u32[]{:S(2)}, u32[]{:S(2)}) async-start(bf16[8,2,64,512]{3,2,1,0:T(8,128)(2,1)} %get-tuple-element.29), calls=%async_computation.1 | async-start | bytes 2097152 | tf_op jit(solution)/shard_map/all_to_all | solution.py:336
  38.9 9.7 %collective-permute-start.10 = (bf16[2,64,896]{2,1,0:T(8,128)(2,1)}, bf16[2,64,896]{2,1,0:T(8,128)(2,1)S(1)}, u32[]{:S(2)}, u32[]{:S(2)}) collective-permute-start(bf16[2,64,896]{2,1,0:T(8,128)(2,1)} %get-tuple-element.27.refs_5_), channel_id=1, source_target_pairs={{0,7},{1,0},{2,1},{3,2},{4,3},{5,4},{6,5},{7,6},{8,15},{9,8},{10,9... | collective-permute-start | bytes 688136 | tf_op jit(solution)/shard_map/ppermute | solution.py:37
  44.8 8.1 %collective-permute-start.11 = (bf16[2,64,896]{2,1,0:T(8,128)(2,1)}, bf16[2,64,896]{2,1,0:T(8,128)(2,1)S(1)}, u32[]{:S(2)}, u32[]{:S(2)}) collective-permute-start(bf16[2,64,896]{2,1,0:T(8,128)(2,1)} %collective-permute-done.9.refs_6_), channel_id=1, source_target_pairs={{0,1},{1,2},{2,3},{3,4},{4,5},{5,6},{6,7},{7,0},{8,9},{9,10},{10,1... | collective-permute-start | bytes 688136 | tf_op jit(solution)/shard_map/ppermute | solution.py:37
  44.8 25.7 %collective-permute-start.16 = (bf16[8,64,512]{2,1,0:T(8,128)(2,1)S(1)}, bf16[8,64,512]{2,1,0:T(8,128)(2,1)S(1)}, u32[]{:S(2)}, u32[]{:S(2)}) collective-permute-start(bf16[8,64,512]{2,1,0:T(8,128)(2,1)S(1)} %all-to-all-done.refs_13_), channel_id=1, source_target_pairs={{0,64},{64,0},{128,192},{192,128},{1,65},{65,1},{129,193},{193,129... | collective-permute-start | bytes 1572872 | tf_op jit(solution)/shard_map/ppermute | solution.py:41
  48.6 0.7 copy-start.1
  49.3 7.1 %collective-permute-start.12 = (bf16[2,64,896]{2,1,0:T(8,128)(2,1)S(1)}, bf16[2,64,896]{2,1,0:T(8,128)(2,1)}, u32[]{:S(2)}, u32[]{:S(2)}) collective-permute-start(bf16[2,64,896]{2,1,0:T(8,128)(2,1)S(1)} %collective-permute-done.10.refs_7_), channel_id=1, source_target_pairs={{0,7},{1,0},{2,1},{3,2},{4,3},{5,4},{6,5},{7,6},{8,15},{9,8},{10,9... | collective-permute-start | bytes 688136 | tf_op jit(solution)/shard_map/ppermute | solution.py:37
  52.9 3.5 %copy-start.2 = (bf16[2,64,896]{2,1,0:T(8,128)(2,1)}, bf16[2,64,896]{2,1,0:T(8,128)(2,1)S(1)}, u32[]{:S(2)}) copy-start(bf16[2,64,896]{2,1,0:T(8,128)(2,1)S(1)} %collective-permute-done.11.refs_8_) | copy-start | bytes 688132
  52.9 10.1 %collective-permute-start.13 = (bf16[2,64,896]{2,1,0:T(8,128)(2,1)S(1)}, bf16[2,64,896]{2,1,0:T(8,128)(2,1)}, u32[]{:S(2)}, u32[]{:S(2)}) collective-permute-start(bf16[2,64,896]{2,1,0:T(8,128)(2,1)S(1)} %collective-permute-done.11.refs_8_), channel_id=1, source_target_pairs={{0,1},{1,2},{2,3},{3,4},{4,5},{5,6},{6,7},{7,0},{8,9},{9,10},{10,1... | collective-permute-start | bytes 688136 | tf_op jit(solution)/shard_map/ppermute | solution.py:37
  56.4 7.7 %collective-permute-start.14 = (bf16[2,64,896]{2,1,0:T(8,128)(2,1)}, bf16[2,64,896]{2,1,0:T(8,128)(2,1)}, u32[]{:S(2)}, u32[]{:S(2)}) collective-permute-start(bf16[2,64,896]{2,1,0:T(8,128)(2,1)} %collective-permute-done.12.refs_9_), channel_id=1, source_target_pairs={{0,7},{1,0},{2,1},{3,2},{4,3},{5,4},{6,5},{7,6},{8,15},{9,8},{10,9... | collective-permute-start | bytes 688136 | tf_op jit(solution)/shard_map/ppermute | solution.py:37
  60.3 6.5 %collective-permute-start.8 = (bf16[2,64,896]{2,1,0:T(8,128)(2,1)}, bf16[2,64,896]{2,1,0:T(8,128)(2,1)}, u32[]{:S(2)}, u32[]{:S(2)}) collective-permute-start(bf16[2,64,896]{2,1,0:T(8,128)(2,1)} %slice.19), channel_id=1, source_target_pairs={{0,48},{1,49},{2,50},{3,51},{4,52},{5,53},{6,54},{7,55},{8,56},{9,... | collective-permute-start | bytes 688136 | tf_op jit(solution)/shard_map/ppermute | solution.py:37
  62.9 7.5 %collective-permute-start.7 = (bf16[2,64,896]{2,1,0:T(8,128)(2,1)}, bf16[2,64,896]{2,1,0:T(8,128)(2,1)}, u32[]{:S(2)}, u32[]{:S(2)}) collective-permute-start(bf16[2,64,896]{2,1,0:T(8,128)(2,1)} %slice.18), channel_id=1, source_target_pairs={{0,16},{1,17},{2,18},{3,19},{4,20},{5,21},{6,22},{7,23},{8,24},{9,... | collective-permute-start | bytes 688136 | tf_op jit(solution)/shard_map/ppermute | solution.py:37
  63.0 7.5 %collective-permute-start.15 = (bf16[2,64,896]{2,1,0:T(8,128)(2,1)}, bf16[2,64,896]{2,1,0:T(8,128)(2,1)}, u32[]{:S(2)}, u32[]{:S(2)}) collective-permute-start(bf16[2,64,896]{2,1,0:T(8,128)(2,1)} %collective-permute-done.13.refs_10_), channel_id=1, source_target_pairs={{0,1},{1,2},{2,3},{3,4},{4,5},{5,6},{6,7},{7,0},{8,9},{9,10},{10,1... | collective-permute-start | bytes 688136 | tf_op jit(solution)/shard_map/ppermute | solution.py:37
  75.9 2.7 %collective-permute-start.17 = (bf16[512,1024]{1,0:T(8,128)(2,1)S(1)}, bf16[512,1024]{1,0:T(8,128)(2,1)S(1)}, u32[]{:S(2)}, u32[]{:S(2)}) collective-permute-start(bf16[512,1024]{1,0:T(8,128)(2,1)S(1)} %get-tuple-element.30), channel_id=1, source_target_pairs={{0,64},{64,0},{128,192},{192,128},{1,65},{65,1},{129,193},{193,129... | collective-permute-start | bytes 3145736 | tf_op jit(solution)/shard_map/ppermute | solution.py:41
  102.8 12.2 %all-to-all-start.3 = ((f32[4,8,896]{2,1,0:T(8,128)}), f32[4,8,896]{2,1,0:T(8,128)S(1)}, u32[]{:S(2)}, u32[]{:S(2)}) async-start(f32[4,8,896]{2,1,0:T(8,128)} %convert_reduce_fusion), calls=%async_computation.3 | async-start | bytes 229376 | tf_op jit(solution)/shard_map/all_to_all | solution.py:299

commit v13 on v12

--- a/solution.py
+++ b/solution.py
@@ -88,41 +88,31 @@
     )
 
 
-def pack_body(odd_ref, own_ref, core_ref, far_ref, stored_ref, kernels_ref, shared_ref, single_ref, sem):
-    odd = odd_ref[0] == 1
-    own, core, far = stored_ref[own_ref[0]], stored_ref[core_ref[0]], stored_ref[far_ref[0]]
-    shared = jnp.where(odd, own, core)
-    single = jnp.where(odd, core, far)
+def pack_body(slot_ref, stored_ref, kernels_ref, out_ref, sem):
+    planes = out_ref.shape[1]
+    kernel = kernels_ref.at[stored_ref[slot_ref[0]]]
     copies = []
     for i in range(GROUPS):
-        at = pl.ds(i * BLOCK, BLOCK)
-        copies += [
-            pltpu.make_async_copy(
-                kernels_ref.at[shared, odd_ref[0], :, at], shared_ref.at[i], sem.at[0, i]
-            ),
-            pltpu.make_async_copy(
-                kernels_ref.at[single, :, :, at], single_ref.at[i], sem.at[1, i]
-            ),
-        ]
+        block = kernel.at[:, :, pl.ds(i * BLOCK, BLOCK)]
+        if planes == 1:
+            block = block.at[pl.ds(slot_ref[1], 1)]
+        copies.append(pltpu.make_async_copy(block, out_ref.at[i], sem.at[i]))
     for copy in copies:
         copy.start()
     for copy in copies:
         copy.wait()
 
 
-def pack(odd, own, core, far, stored, kernels):
+def pack(slot, stored, kernels, planes):
     return pl.pallas_call(
         pack_body,
-        out_shape=[
-            pltpu.VMEM((GROUPS, SLAB, BLOCK), jnp.bfloat16),
-            pltpu.VMEM((GROUPS, 2, SLAB, BLOCK), jnp.bfloat16),
-        ],
-        in_specs=[IN_SMEM] * 5 + [ANYWHERE],
-        out_specs=[IN_VMEM] * 2,
-        scratch_shapes=[pltpu.SemaphoreType.DMA((2, GROUPS))],
+        out_shape=jax.ShapeDtypeStruct((GROUPS, planes, SLAB, BLOCK), jnp.bfloat16),
+        in_specs=[IN_SMEM] * 2 + [pl.BlockSpec(memory_space=pltpu.HBM)],
+        out_specs=IN_VMEM,
+        scratch_shapes=[pltpu.SemaphoreType.DMA((GROUPS,))],
         compiler_params=PARAMS,
         name="pack",
-    )(odd, own, core, far, stored, away(kernels))
+    )(slot, stored, away(kernels))
 
 
 def mix_body(place_ref, slot_ref, odd_ref, *refs):
@@ -164,8 +154,8 @@
         at = pl.ds(part * per, per)
         b = col_ref[at, :]
         p_re, p_im = dot(a, b, 1, 1), dot(a_turned, b, 1, 1)
-        mine = mine_ref[:, :, at].reshape(BLOCK, per)
-        other = half_ref[:, :, at].reshape(BLOCK, per)
+        mine = mine_ref[:, 0, :, at].reshape(BLOCK, per)
+        other = half_ref[:, 0, :, at].reshape(BLOCK, per)
         k_re = jnp.where(odd, other, mine).astype(jnp.float32)
         k_im = jnp.where(odd, mine, other).astype(jnp.float32) * sign
         total_re = k_re * p_re - k_im * p_im
@@ -321,18 +311,24 @@
 
     over_yx = [[g * NZ + i for g in range(GROUPS)] for i in range(NZ)]
     four, both = bundle(own, far, own_side, far_side)
-    cols, ahead, behind = [both], both, both
-    for _ in range(3):
-        ahead, behind = shift(ahead, 0, 0, 1), shift(behind, 0, 0, -1)
-        cols += [ahead, behind]
-    cols.append(shift(ahead, 0, 0, 1))
-    up, down = shift(four, 1, 0, 0), shift(four, -1, 0, 0)
-
-    shared, single = pack(odd, pair_kdiff, diff_core, diff_far, stored_kernel_index, kernels)
+    sends = shift(four, 1, 0, 0), shift(four, -1, 0, 0), shift(both, 0, 0, 1), shift(both, 0, 0, -1)
+    up, down, ahead, behind = lax.optimization_barrier(sends)
+    cols = [both, ahead, behind]
+    over = shift(up[:2], 1, 0, 0), shift(down[2:], -1, 0, 0)
+    ahead, behind = shift(ahead, 0, 0, 1), shift(behind, 0, 0, -1)
+    *over, ahead, behind = lax.optimization_barrier((*over, ahead, behind))
+    cols += [ahead, behind]
+    ahead, behind = shift(ahead, 0, 0, 1), shift(behind, 0, 0, -1)
+    cols += [ahead, behind, shift(ahead, 0, 0, 1)]
+
+    is_odd = odd[0] == 1
+    shared = jnp.stack([jnp.where(is_odd, pair_kdiff[0], diff_core[0]), odd[0]])
+    single = jnp.where(is_odd, diff_core, diff_far)
+    shared = pack(shared, stored_kernel_index, kernels, 1)
+    single = pack(single, stored_kernel_index, kernels, 2)
     mine = lax.all_to_all(shared, "band", 0, 0, axis_index_groups=over_yx)
     half = swap_groups(mine, 1)
     single, up, down = lax.optimization_barrier((single, up, down))
-    over = shift(up[:2], 1, 0, 0), shift(down[2:], -1, 0, 0)
     kern = lax.all_to_all(single, "band", 0, 0, axis_index_groups=over_yx)
 
     place = jnp.stack([(y - dy) % NY * NX + (x - dx) % NX for dy in range(NY) for dx in range(NX)])

time: 116 us -> 121 us (1.043)
  waiting for transfers between devices: 33.7 us -> 38.8 us
  between operations: 1.11 us -> 2.77 us
    ppermute x12, waiting for transfers between devices: 13 us -> 25.1 us  [shift(): return lax.ppermute(block, 'band', band_route(dy, dx, dz))]
    all_to_all x1, waiting for transfers between devices: 6.37 us -> 0.01 us  [on_device(): mine = lax.all_to_all(shared, 'band', 0, 0, axis_index_groups=over_yx)]
    ppermute x12, starting transfers between devices: 20.9 us -> 18.2 us  [shift(): return lax.ppermute(block, 'band', band_route(dy, dx, dz))]
    slice x2, local copies, waits for them, and re-layouts: 1.49 us -> 0.04 us  [on_device(): over = (shift(up[:2], 1, 0, 0), shift(down[2:], -1, 0, 0))]
    pallas_call x1 -> x2, Pallas kernels: 4.69 us -> 5.39 us  [pack(): pl.pallas_call(pack_body, out_shape=jax.ShapeDtypeStruct((GROUPS, planes,...]
  transfers between devices with their start and end apart: 21 -> 21, of which waited for: 9 -> 8; matrix products, arithmetic and copies ran while one was open for 1% -> 0% of each run, Pallas kernels for 5% -> 5%
where the time goes in v13:
time: 121 us; the launch traced here: 120 us
  starting transfers between devices  40.1 us (33%)
  waiting for transfers between devices  38.8 us (32%)
  blocking collectives  18.3 us (15%)
  Pallas kernels  16.4 us (14%)
  between operations  2.77 us (2%)
  local copies, waits for them, and re-layouts  2.51 us (2%)
  other arithmetic  1.6 us (1%)
    ppermute x12, waiting for transfers between devices, shift(): return lax.ppermute(block, 'band', band_route(dy, dx, dz))  25.1 us
    all_to_all x1, blocking collectives, reduce_windows(): parts = lax.all_to_all(parts, 'band', 0, 0, axis_index_groups=wide)  18.3 us
    ppermute x12, starting transfers between devices, shift(): return lax.ppermute(block, 'band', band_route(dy, dx, dz))  18.2 us
    all_to_all x1, waiting for transfers between devices, reduce_windows(): lax.all_to_all(parts, 'band', 0, 0, axis_index_groups=deep)  8.9 us
    all_to_all x1, starting transfers between devices, on_device(): mine = lax.all_to_all(shared, 'band', 0, 0, axis_index_groups=over_yx)  5.98 us
    all_to_all x1, starting transfers between devices, on_device(): kern = lax.all_to_all(single, 'band', 0, 0, axis_index_groups=over_yx)  5.71 us
    pallas_call x2, Pallas kernels, pack(): pl.pallas_call(pack_body, out_shape=jax.ShapeDtypeStruct((GROUPS, planes,...  5.39 us
    pallas_call x1, Pallas kernels, mix(): pl.pallas_call(mix_body, out_shape=[pltpu.VMEM((BLOCK, 2 * BLOCK), jnp.bf...  5.35 us
  transfers between devices with their start and end apart: 21, of which 8 were waited for; matrix products, arithmetic and copies ran while one was open for 0% of the time, Pallas kernels for 5%

profile of v13, /device:TPU:6, one launch (start us, length us, event | category | flops | bytes accessed | tf_op | source)
XLA Modules:
  0.0 120.5 jit_solution(13485473377883513647)
XLA Ops:
  0.0 1.0 lay.1.own_ref
  1.0 2.3 %collective-permute-start.4 = (bf16[64,896]{1,0:T(8,128)(2,1)S(1)}, bf16[64,896]{1,0:T(8,128)(2,1)S(1)}, u32[]{:S(2)}, u32[]{:S(2)}) collective-permute-start(bf16[64,896]{1,0:T(8,128)(2,1)S(1)} %lay.1.own_ref), channel_id=1, source_target_pairs={{128,8},{129,9},{130,10},{131,11},{132,12},{133,13},{134,14},{135,... | collective-permute-start | bytes 344072 | tf_op jit(solution)/shard_map/ppermute | solution.py:47
  3.2 2.5 %collective-permute-start.2 = (bf16[64,896]{1,0:T(8,128)(2,1)S(1)}, bf16[64,896]{1,0:T(8,128)(2,1)S(1)}, u32[]{:S(2)}, u32[]{:S(2)}) collective-permute-start(bf16[64,896]{1,0:T(8,128)(2,1)S(1)} %lay.1.own_ref), channel_id=1, source_target_pairs={{0,128},{64,192},{128,0},{192,64},{1,129},{65,193},{129,1},{193,65... | collective-permute-start | bytes 344072 | tf_op jit(solution)/shard_map/ppermute | solution.py:41
  5.7 1.0 collective-permute-start.1
  8.1 2.8 %collective-permute-done.1 = s32[1]{0:T(128)} collective-permute-done((s32[1]{0:T(128)}, s32[1]{0:T(128)}, u32[]{:S(2)}, u32[]{:S(2)}) %collective-permute-start.1) | collective-permute-done | bytes 36 | tf_op jit(solution)/shard_map/ppermute | solution.py:41
  10.9 3.1 %collective-permute-start.6 = (bf16[4,64,896]{2,1,0:T(8,128)(2,1)S(1)}, bf16[4,64,896]{2,1,0:T(8,128)(2,1)S(1)}, u32[]{:S(2)}, u32[]{:S(2)}) collective-permute-start(bf16[4,64,896]{2,1,0:T(8,128)(2,1)S(1)} %get-tuple-element.29.refs_0_), channel_id=1, source_target_pairs={{0,48},{1,49},{2,50},{3,51},{4,52},{5,53},{6,54},{7,55},{8,56},{9,... | collective-permute-start | bytes 1376264 | tf_op jit(solution)/shard_map/ppermute | solution.py:37
  14.1 0.7 copy-done.1
  14.8 2.5 %pack.3 = bf16[8,1,64,512]{3,2,1,0:T(8,128)(2,1)} custom-call(s32[2]{0:T(128)S(1)} %pad_add_fusion.slot_ref, s32[8]{0:T(128)S(1)} %copy-done.1, bf16[4,2,64,4096]{3,2,1,0:T(8,128)(2,1)} %kernels_ref.3), custom_call_target="tpu_custom_call" | custom-call | tf_op jit(solution)/shard_map/pack/pallas_call | solution.py:107
  17.3 6.0 %all-to-all-start = ((bf16[8,1,64,512]{3,2,1,0:T(8,128)(2,1)}), bf16[8,1,64,512]{3,2,1,0:T(8,128)(2,1)S(1)}, u32[]{:S(2)}, u32[]{:S(2)}) async-start(bf16[8,1,64,512]{3,2,1,0:T(8,128)(2,1)} %pack.3), calls=%async_computation | async-start | bytes 1048576 | tf_op jit(solution)/shard_map/all_to_all | solution.py:329
  23.3 5.9 %collective-permute-start.8 = (bf16[2,64,896]{2,1,0:T(8,128)(2,1)S(1)}, bf16[2,64,896]{2,1,0:T(8,128)(2,1)}, u32[]{:S(2)}, u32[]{:S(2)}) collective-permute-start(bf16[2,64,896]{2,1,0:T(8,128)(2,1)S(1)} %get-tuple-element.30.refs_5_), channel_id=1, source_target_pairs={{0,7},{1,0},{2,1},{3,2},{4,3},{5,4},{6,5},{7,6},{8,15},{9,8},{10,9... | collective-permute-start | bytes 688136 | tf_op jit(solution)/shard_map/ppermute | solution.py:37
  30.4 2.9 %pack.2 = bf16[8,2,64,512]{3,2,1,0:T(8,128)(2,1)} custom-call(s32[1]{0:T(128)S(6)} %select_n.136.slot_ref, s32[8]{0:T(128)S(1)} %copy-done.2, bf16[4,2,64,4096]{3,2,1,0:T(8,128)(2,1)} %kernels_ref.3), custom_call_target="tpu_custom_call" | custom-call | tf_op jit(solution)/shard_map/pack/pallas_call | solution.py:107
  33.3 3.1 %collective-permute-done.7.refs_6_ = bf16[2,64,896]{2,1,0:T(8,128)(2,1)} collective-permute-done((bf16[2,64,896]{2,1,0:T(8,128)(2,1)S(1)}, bf16[2,64,896]{2,1,0:T(8,128)(2,1)}, u32[]{:S(2)}, u32[]{:S(2)}) %collective-permute-start.7) | collective-permute-done | bytes 229408 | tf_op jit(solution)/shard_map/ppermute | solution.py:37
  36.5 5.7 %all-to-all-start.1 = ((bf16[8,2,64,512]{3,2,1,0:T(8,128)(2,1)}), bf16[8,2,64,512]{3,2,1,0:T(8,128)(2,1)S(1)}, u32[]{:S(2)}, u32[]{:S(2)}) async-start(bf16[8,2,64,512]{3,2,1,0:T(8,128)(2,1)} %pack.2), calls=%async_computation.1 | async-start | bytes 2097152 | tf_op jit(solution)/shard_map/all_to_all | solution.py:332
  42.2 2.8 %collective-permute-start.10 = (bf16[2,64,896]{2,1,0:T(8,128)(2,1)S(1)}, bf16[2,64,896]{2,1,0:T(8,128)(2,1)S(1)}, u32[]{:S(2)}, u32[]{:S(2)}) collective-permute-start(bf16[2,64,896]{2,1,0:T(8,128)(2,1)S(1)} %slice.19), channel_id=1, source_target_pairs={{0,48},{1,49},{2,50},{3,51},{4,52},{5,53},{6,54},{7,55},{8,56},{9,... | collective-permute-start | bytes 688136 | tf_op jit(solution)/shard_map/ppermute | solution.py:37
  45.0 3.2 %collective-permute-start.12 = (bf16[2,64,896]{2,1,0:T(8,128)(2,1)}, bf16[2,64,896]{2,1,0:T(8,128)(2,1)}, u32[]{:S(2)}, u32[]{:S(2)}) collective-permute-start(bf16[2,64,896]{2,1,0:T(8,128)(2,1)} %collective-permute-done.8.refs_7_), channel_id=1, source_target_pairs={{0,7},{1,0},{2,1},{3,2},{4,3},{5,4},{6,5},{7,6},{8,15},{9,8},{10,9... | collective-permute-start | bytes 688136 | tf_op jit(solution)/shard_map/ppermute | solution.py:37
  48.2 9.5 %collective-permute-done.10.refs_3_ = bf16[2,64,896]{2,1,0:T(8,128)(2,1)S(1)} collective-permute-done((bf16[2,64,896]{2,1,0:T(8,128)(2,1)S(1)}, bf16[2,64,896]{2,1,0:T(8,128)(2,1)S(1)}, u32[]{:S(2)}, u32[]{:S(2)}) %collective-permute-start.10) | collective-permute-done | bytes 229408 | tf_op jit(solution)/shard_map/ppermute | solution.py:37
  57.7 1.0 collective-permute-done.9.refs_2_
  58.7 0.7 copy-done.4
  59.4 0.7 copy-done.5
  60.1 3.2 %collective-permute-start.14 = (bf16[2,64,896]{2,1,0:T(8,128)(2,1)}, bf16[2,64,896]{2,1,0:T(8,128)(2,1)}, u32[]{:S(2)}, u32[]{:S(2)}) collective-permute-start(bf16[2,64,896]{2,1,0:T(8,128)(2,1)} %collective-permute-done.12.refs_9_), channel_id=1, source_target_pairs={{0,7},{1,0},{2,1},{3,2},{4,3},{5,4},{6,5},{7,6},{8,15},{9,8},{10,9... | collective-permute-start | bytes 688136 | tf_op jit(solution)/shard_map/ppermute | solution.py:37
  63.3 4.1 %collective-permute-done.13.refs_10_ = bf16[2,64,896]{2,1,0:T(8,128)(2,1)} collective-permute-done((bf16[2,64,896]{2,1,0:T(8,128)(2,1)S(1)}, bf16[2,64,896]{2,1,0:T(8,128)(2,1)}, u32[]{:S(2)}, u32[]{:S(2)}) %collective-permute-start.13) | collective-permute-done | bytes 229408 | tf_op jit(solution)/shard_map/ppermute | solution.py:37
  67.6 7.4 %collective-permute-done.15.refs_12_ = bf16[2,64,896]{2,1,0:T(8,128)(2,1)} collective-permute-done((bf16[2,64,896]{2,1,0:T(8,128)(2,1)}, bf16[2,64,896]{2,1,0:T(8,128)(2,1)}, u32[]{:S(2)}, u32[]{:S(2)}) %collective-permute-start.15) | collective-permute-done | bytes 229408 | tf_op jit(solution)/shard_map/ppermute | solution.py:37
  75.0 5.3 %mix.1 = (bf16[512,1024]{1,0:T(8,128)(2,1)S(1)}, bf16[512,896]{1,0:T(8,128)(2,1)S(1)}, bf16[512,896]{1,0:T(8,128)(2,1)S(1)}) custom-call(s32[8]{0:T(128)S(1)} %stack.77.place_ref, s32[8]{0:T(128)S(1)} %stack.86.slot_ref, s32[1]{0:T(128)} %bitcast.16.odd_ref, bf16[4,64,896]{2,1,0:T(8,128)(2,1)S(1)} %get-tuple-element.29.refs_0_, ...), custom_call_target="tpu_custom_call" | custom-call | tf_op jit(solution)/shard_map/mix/pallas_call | solution.py:180
  80.5 0.6 prepare.1
  81.0 2.1 %collective-permute-done.17.m_ref = bf16[512,1024]{1,0:T(8,128)(2,1)S(1)} collective-permute-done((bf16[512,1024]{1,0:T(8,128)(2,1)S(1)}, bf16[512,1024]{1,0:T(8,128)(2,1)S(1)}, u32[]{:S(2)}, u32[]{:S(2)}) %collective-permute-start.17) | collective-permute-done | bytes 1048608 | tf_op jit(solution)/shard_map/ppermute | solution.py:41
  83.1 4.1 %project.1 = bf16[64,8,896]{2,1,0:T(8,128)(2,1)S(1)} custom-call(bf16[512,1024]{1,0:T(8,128)(2,1)S(1)} %collective-permute-done.17.m_ref, bf16[432,1024]{1,0:T(8,128)(2,1)S(1)} %get-tuple-element.45.left_ref, bf16[1024,896]{1,0:T(8,128)(2,1)S(1)} %get-tuple-element.46.right_ref), custom_call_target="tpu_custom_call" | custom-call | tf_op jit(solution)/shard_map/project/pallas_call | solution.py:246
  87.2 18.3 %all_to_all.20 = bf16[16,4,8,896]{3,2,1,0:T(8,128)(2,1)S(1)} all-to-all(bf16[16,4,8,896]{3,2,1,0:T(8,128)(2,1)S(1)} %bitcast.25), channel_id=1, replica_groups={{0,1,8,9,16,17,24,25,32,33,40,41,48,49,56,57},{2,3,10,11,18,19,26,27,34..., dimensions={0} | all-to-all | bytes 1835008 | tf_op jit(solution)/shard_map/all_to_all | solution.py:287
  105.4 0.8 convert_reduce_fusion
  106.2 4.3 %all-to-all-start.3 = ((f32[4,8,896]{2,1,0:T(8,128)}), f32[4,8,896]{2,1,0:T(8,128)S(1)}, u32[]{:S(2)}, u32[]{:S(2)}) async-start(f32[4,8,896]{2,1,0:T(8,128)} %convert_reduce_fusion), calls=%async_computation.3 | async-start | bytes 229376 | tf_op jit(solution)/shard_map/all_to_all | solution.py:289
  110.5 8.9 %all-to-all-done.3 = f32[4,8,896]{2,1,0:T(8,128)S(1)} async-done(((f32[4,8,896]{2,1,0:T(8,128)}), f32[4,8,896]{2,1,0:T(8,128)S(1)}, u32[]{:S(2)}, u32[]{:S(2)}) %all-to-all-start.3) | async-done | bytes 114720 | tf_op jit(solution)/shard_map/all_to_all | solution.py:289
  119.5 0.1 stack.89
  119.7 0.7 fusion.1
  (43 shorter events, 0.7 us)
Async XLA Ops:
  1.0 9.9 %collective-permute-start.4 = (bf16[64,896]{1,0:T(8,128)(2,1)S(1)}, bf16[64,896]{1,0:T(8,128)(2,1)S(1)}, u32[]{:S(2)}, u32[]{:S(2)}) collective-permute-start(bf16[64,896]{1,0:T(8,128)(2,1)S(1)} %lay.1.own_ref), channel_id=1, source_target_pairs={{128,8},{129,9},{130,10},{131,11},{132,12},{133,13},{134,14},{135,... | collective-permute-start | bytes 344072 | tf_op jit(solution)/shard_map/ppermute | solution.py:47
  3.2 7.6 %collective-permute-start.3 = (bf16[64,896]{1,0:T(8,128)(2,1)S(1)}, bf16[64,896]{1,0:T(8,128)(2,1)S(1)}, u32[]{:S(2)}, u32[]{:S(2)}) collective-permute-start(bf16[64,896]{1,0:T(8,128)(2,1)S(1)} %lay.1.own_ref), channel_id=1, source_target_pairs={{0,8},{1,9},{2,10},{3,11},{4,12},{5,13},{6,14},{7,15},{8,0},{9,1},... | collective-permute-start | bytes 344072 | tf_op jit(solution)/shard_map/ppermute | solution.py:37
  3.2 7.6 %collective-permute-start.2 = (bf16[64,896]{1,0:T(8,128)(2,1)S(1)}, bf16[64,896]{1,0:T(8,128)(2,1)S(1)}, u32[]{:S(2)}, u32[]{:S(2)}) collective-permute-start(bf16[64,896]{1,0:T(8,128)(2,1)S(1)} %lay.1.own_ref), channel_id=1, source_target_pairs={{0,128},{64,192},{128,0},{192,64},{1,129},{65,193},{129,1},{193,65... | collective-permute-start | bytes 344072 | tf_op jit(solution)/shard_map/ppermute | solution.py:41
  5.7 1.7 %collective-permute-start = (s32[1]{0:T(128)}, s32[1]{0:T(128)}, u32[]{:S(2)}, u32[]{:S(2)}) collective-permute-start(s32[1]{0:T(128)} %param.6), channel_id=1, source_target_pairs={{0,64},{64,0},{128,192},{192,128},{1,65},{65,1},{129,193},{193,129... | collective-permute-start | bytes 20 | tf_op jit(solution)/shard_map/ppermute | solution.py:41
  5.7 5.1 %collective-permute-start.1 = (s32[1]{0:T(128)}, s32[1]{0:T(128)}, u32[]{:S(2)}, u32[]{:S(2)}) collective-permute-start(s32[1]{0:T(128)} %param.6), channel_id=1, source_target_pairs={{0,128},{64,192},{128,0},{192,64},{1,129},{65,193},{129,1},{193,65... | collective-permute-start | bytes 20 | tf_op jit(solution)/shard_map/ppermute | solution.py:41
  10.9 18.2 %copy-start = (bf16[2,64,896]{2,1,0:T(8,128)(2,1)}, bf16[2,64,896]{2,1,0:T(8,128)(2,1)S(1)}, u32[]{:S(2)}) copy-start(bf16[2,64,896]{2,1,0:T(8,128)(2,1)S(1)} %get-tuple-element.30.refs_5_) | copy-start | bytes 688132
  10.9 25.5 %collective-permute-start.6 = (bf16[4,64,896]{2,1,0:T(8,128)(2,1)S(1)}, bf16[4,64,896]{2,1,0:T(8,128)(2,1)S(1)}, u32[]{:S(2)}, u32[]{:S(2)}) collective-permute-start(bf16[4,64,896]{2,1,0:T(8,128)(2,1)S(1)} %get-tuple-element.29.refs_0_), channel_id=1, source_target_pairs={{0,48},{1,49},{2,50},{3,51},{4,52},{5,53},{6,54},{7,55},{8,56},{9,... | collective-permute-start | bytes 1376264 | tf_op jit(solution)/shard_map/ppermute | solution.py:37
  14.0 22.4 %collective-permute-start.5 = (bf16[4,64,896]{2,1,0:T(8,128)(2,1)S(1)}, bf16[4,64,896]{2,1,0:T(8,128)(2,1)S(1)}, u32[]{:S(2)}, u32[]{:S(2)}) collective-permute-start(bf16[4,64,896]{2,1,0:T(8,128)(2,1)S(1)} %get-tuple-element.29.refs_0_), channel_id=1, source_target_pairs={{0,16},{1,17},{2,18},{3,19},{4,20},{5,21},{6,22},{7,23},{8,24},{9,... | collective-permute-start | bytes 1376264 | tf_op jit(solution)/shard_map/ppermute | solution.py:37
  14.1 0.7 copy-start.1
  14.8 15.7 %copy-start.2 = (s32[8]{0:T(128)S(1)}, s32[8]{0:T(128)}, u32[]{:S(2)}) copy-start(s32[8]{0:T(128)} %stored_ref.3) | copy-start | bytes 100
  17.3 19.2 %all-to-all-start = ((bf16[8,1,64,512]{3,2,1,0:T(8,128)(2,1)}), bf16[8,1,64,512]{3,2,1,0:T(8,128)(2,1)S(1)}, u32[]{:S(2)}, u32[]{:S(2)}) async-start(bf16[8,1,64,512]{3,2,1,0:T(8,128)(2,1)} %pack.3), calls=%async_computation | async-start | bytes 1048576 | tf_op jit(solution)/shard_map/all_to_all | solution.py:329
  23.3 10.1 %collective-permute-start.8 = (bf16[2,64,896]{2,1,0:T(8,128)(2,1)S(1)}, bf16[2,64,896]{2,1,0:T(8,128)(2,1)}, u32[]{:S(2)}, u32[]{:S(2)}) collective-permute-start(bf16[2,64,896]{2,1,0:T(8,128)(2,1)S(1)} %get-tuple-element.30.refs_5_), channel_id=1, source_target_pairs={{0,7},{1,0},{2,1},{3,2},{4,3},{5,4},{6,5},{7,6},{8,15},{9,8},{10,9... | collective-permute-start | bytes 688136 | tf_op jit(solution)/shard_map/ppermute | solution.py:37
  29.1 7.3 %collective-permute-start.7 = (bf16[2,64,896]{2,1,0:T(8,128)(2,1)S(1)}, bf16[2,64,896]{2,1,0:T(8,128)(2,1)}, u32[]{:S(2)}, u32[]{:S(2)}) collective-permute-start(bf16[2,64,896]{2,1,0:T(8,128)(2,1)S(1)} %get-tuple-element.30.refs_5_), channel_id=1, source_target_pairs={{0,1},{1,2},{2,3},{3,4},{4,5},{5,6},{6,7},{7,0},{8,9},{9,10},{10,1... | collective-permute-start | bytes 688136 | tf_op jit(solution)/shard_map/ppermute | solution.py:37
  36.5 38.5 %all-to-all-start.1 = ((bf16[8,2,64,512]{3,2,1,0:T(8,128)(2,1)}), bf16[8,2,64,512]{3,2,1,0:T(8,128)(2,1)S(1)}, u32[]{:S(2)}, u32[]{:S(2)}) async-start(bf16[8,2,64,512]{3,2,1,0:T(8,128)(2,1)} %pack.2), calls=%async_computation.1 | async-start | bytes 2097152 | tf_op jit(solution)/shard_map/all_to_all | solution.py:332
  42.2 15.5 %collective-permute-start.10 = (bf16[2,64,896]{2,1,0:T(8,128)(2,1)S(1)}, bf16[2,64,896]{2,1,0:T(8,128)(2,1)S(1)}, u32[]{:S(2)}, u32[]{:S(2)}) collective-permute-start(bf16[2,64,896]{2,1,0:T(8,128)(2,1)S(1)} %slice.19), channel_id=1, source_target_pairs={{0,48},{1,49},{2,50},{3,51},{4,52},{5,53},{6,54},{7,55},{8,56},{9,... | collective-permute-start | bytes 688136 | tf_op jit(solution)/shard_map/ppermute | solution.py:37
  45.0 13.7 %collective-permute-start.9 = (bf16[2,64,896]{2,1,0:T(8,128)(2,1)S(1)}, bf16[2,64,896]{2,1,0:T(8,128)(2,1)S(1)}, u32[]{:S(2)}, u32[]{:S(2)}) collective-permute-start(bf16[2,64,896]{2,1,0:T(8,128)(2,1)S(1)} %slice.18), channel_id=1, source_target_pairs={{0,16},{1,17},{2,18},{3,19},{4,20},{5,21},{6,22},{7,23},{8,24},{9,... | collective-permute-start | bytes 688136 | tf_op jit(solution)/shard_map/ppermute | solution.py:37
  45.0 13.7 %collective-permute-start.11 = (bf16[2,64,896]{2,1,0:T(8,128)(2,1)}, bf16[2,64,896]{2,1,0:T(8,128)(2,1)S(1)}, u32[]{:S(2)}, u32[]{:S(2)}) collective-permute-start(bf16[2,64,896]{2,1,0:T(8,128)(2,1)} %collective-permute-done.7.refs_6_), channel_id=1, source_target_pairs={{0,1},{1,2},{2,3},{3,4},{4,5},{5,6},{6,7},{7,0},{8,9},{9,10},{10,1... | collective-permute-start | bytes 688136 | tf_op jit(solution)/shard_map/ppermute | solution.py:37
  45.0 14.4 %collective-permute-start.12 = (bf16[2,64,896]{2,1,0:T(8,128)(2,1)}, bf16[2,64,896]{2,1,0:T(8,128)(2,1)}, u32[]{:S(2)}, u32[]{:S(2)}) collective-permute-start(bf16[2,64,896]{2,1,0:T(8,128)(2,1)} %collective-permute-done.8.refs_7_), channel_id=1, source_target_pairs={{0,7},{1,0},{2,1},{3,2},{4,3},{5,4},{6,5},{7,6},{8,15},{9,8},{10,9... | collective-permute-start | bytes 688136 | tf_op jit(solution)/shard_map/ppermute | solution.py:37
  48.2 19.4 %collective-permute-start.16 = (bf16[8,1,64,512]{3,2,1,0:T(8,128)(2,1)S(1)}, bf16[8,1,64,512]{3,2,1,0:T(8,128)(2,1)S(1)}, u32[]{:S(2)}, u32[]{:S(2)}) collective-permute-start(bf16[8,1,64,512]{3,2,1,0:T(8,128)(2,1)S(1)} %all-to-all-done.refs_13_), channel_id=1, source_target_pairs={{0,64},{64,0},{128,192},{192,128},{1,65},{65,1},{129,193},{193,129... | collective-permute-start | bytes 1572872 | tf_op jit(solution)/shard_map/ppermute | solution.py:41
  57.7 1.0 copy-start.3
  58.7 0.7 copy-start.4
  59.4 0.7 copy-start.5
  60.1 7.3 %collective-permute-start.13 = (bf16[2,64,896]{2,1,0:T(8,128)(2,1)S(1)}, bf16[2,64,896]{2,1,0:T(8,128)(2,1)}, u32[]{:S(2)}, u32[]{:S(2)}) collective-permute-start(bf16[2,64,896]{2,1,0:T(8,128)(2,1)S(1)} %collective-permute-done.11.refs_8_), channel_id=1, source_target_pairs={{0,1},{1,2},{2,3},{3,4},{4,5},{5,6},{6,7},{7,0},{8,9},{9,10},{10,1... | collective-permute-start | bytes 688136 | tf_op jit(solution)/shard_map/ppermute | solution.py:37
  60.1 7.5 %collective-permute-start.14 = (bf16[2,64,896]{2,1,0:T(8,128)(2,1)}, bf16[2,64,896]{2,1,0:T(8,128)(2,1)}, u32[]{:S(2)}, u32[]{:S(2)}) collective-permute-start(bf16[2,64,896]{2,1,0:T(8,128)(2,1)} %collective-permute-done.12.refs_9_), channel_id=1, source_target_pairs={{0,7},{1,0},{2,1},{3,2},{4,3},{5,4},{6,5},{7,6},{8,15},{9,8},{10,9... | collective-permute-start | bytes 688136 | tf_op jit(solution)/shard_map/ppermute | solution.py:37
  67.4 7.5 %collective-permute-start.15 = (bf16[2,64,896]{2,1,0:T(8,128)(2,1)}, bf16[2,64,896]{2,1,0:T(8,128)(2,1)}, u32[]{:S(2)}, u32[]{:S(2)}) collective-permute-start(bf16[2,64,896]{2,1,0:T(8,128)(2,1)} %collective-permute-done.13.refs_10_), channel_id=1, source_target_pairs={{0,1},{1,2},{2,3},{3,4},{4,5},{5,6},{6,7},{7,0},{8,9},{9,10},{10,1... | collective-permute-start | bytes 688136 | tf_op jit(solution)/shard_map/ppermute | solution.py:37
  80.4 2.7 %collective-permute-start.17 = (bf16[512,1024]{1,0:T(8,128)(2,1)S(1)}, bf16[512,1024]{1,0:T(8,128)(2,1)S(1)}, u32[]{:S(2)}, u32[]{:S(2)}) collective-permute-start(bf16[512,1024]{1,0:T(8,128)(2,1)S(1)} %get-tuple-element.42), channel_id=1, source_target_pairs={{0,64},{64,0},{128,192},{192,128},{1,65},{65,1},{129,193},{193,129... | collective-permute-start | bytes 3145736 | tf_op jit(solution)/shard_map/ppermute | solution.py:41
  106.2 13.2 %all-to-all-start.3 = ((f32[4,8,896]{2,1,0:T(8,128)}), f32[4,8,896]{2,1,0:T(8,128)S(1)}, u32[]{:S(2)}, u32[]{:S(2)}) async-start(f32[4,8,896]{2,1,0:T(8,128)} %convert_reduce_fusion), calls=%async_computation.3 | async-start | bytes 229376 | tf_op jit(solution)/shard_map/all_to_all | solution.py:289

commit v14 on v12

--- a/solution.py
+++ b/solution.py
@@ -14,7 +14,7 @@
 REST = NB - WHOLE
 TAIL = 2 * WHOLE
 LANES = TAIL + 128
-EARLY = 5
+EARLY = 6
 VMEM = 24 * 1024 * 1024
 
 IN_VMEM = pl.BlockSpec(memory_space=pltpu.VMEM)
@@ -88,7 +88,7 @@
     )
 
 
-def pack_body(odd_ref, own_ref, core_ref, far_ref, stored_ref, kernels_ref, shared_ref, single_ref, sem):
+def pack_body(odd_ref, own_ref, core_ref, far_ref, stored_ref, kernels_ref, out_ref, sem):
     odd = odd_ref[0] == 1
     own, core, far = stored_ref[own_ref[0]], stored_ref[core_ref[0]], stored_ref[far_ref[0]]
     shared = jnp.where(odd, own, core)
@@ -96,14 +96,10 @@
     copies = []
     for i in range(GROUPS):
         at = pl.ds(i * BLOCK, BLOCK)
-        copies += [
-            pltpu.make_async_copy(
-                kernels_ref.at[shared, odd_ref[0], :, at], shared_ref.at[i], sem.at[0, i]
-            ),
-            pltpu.make_async_copy(
-                kernels_ref.at[single, :, :, at], single_ref.at[i], sem.at[1, i]
-            ),
-        ]
+        half = kernels_ref.at[shared, odd_ref[0], :, at]
+        copies.append(pltpu.make_async_copy(half, out_ref.at[i, 0], sem.at[0, i]))
+        both = kernels_ref.at[single, :, :, at]
+        copies.append(pltpu.make_async_copy(both, out_ref.at[i, pl.ds(1, 2)], sem.at[1, i]))
     for copy in copies:
         copy.start()
     for copy in copies:
@@ -113,12 +109,9 @@
 def pack(odd, own, core, far, stored, kernels):
     return pl.pallas_call(
         pack_body,
-        out_shape=[
-            pltpu.VMEM((GROUPS, SLAB, BLOCK), jnp.bfloat16),
-            pltpu.VMEM((GROUPS, 2, SLAB, BLOCK), jnp.bfloat16),
-        ],
-        in_specs=[IN_SMEM] * 5 + [ANYWHERE],
-        out_specs=[IN_VMEM] * 2,
+        out_shape=jax.ShapeDtypeStruct((GROUPS, 3, SLAB, BLOCK), jnp.bfloat16),
+        in_specs=[IN_SMEM] * 5 + [pl.BlockSpec(memory_space=pltpu.HBM)],
+        out_specs=IN_VMEM,
         scratch_shapes=[pltpu.SemaphoreType.DMA((2, GROUPS))],
         compiler_params=PARAMS,
         name="pack",
@@ -127,8 +120,8 @@
 
 def mix_body(place_ref, slot_ref, odd_ref, *refs):
     four_ref, up_ref, over_here, over_side, down_ref = refs[:5]
-    cols, (mine_ref, half_ref, kern_ref) = refs[5 : 5 + NZ], refs[5 + NZ : 8 + NZ]
-    m_ref, row_ref, col_ref, other_rows, other_cols, sem = refs[8 + NZ :]
+    cols, (half_ref, kern_ref) = refs[5 : 5 + NZ], refs[5 + NZ : 7 + NZ]
+    m_ref, row_ref, col_ref, other_rows, other_cols, sem = refs[7 + NZ :]
 
     def row_at(dy, side):
         return pl.ds(pl.multiple_of(place_ref[dy * NX + side] * SLAB, SLAB), SLAB)
@@ -164,7 +157,7 @@
         at = pl.ds(part * per, per)
         b = col_ref[at, :]
         p_re, p_im = dot(a, b, 1, 1), dot(a_turned, b, 1, 1)
-        mine = mine_ref[:, :, at].reshape(BLOCK, per)
+        mine = kern_ref[:, 0, :, at].reshape(BLOCK, per)
         other = half_ref[:, :, at].reshape(BLOCK, per)
         k_re = jnp.where(odd, other, mine).astype(jnp.float32)
         k_im = jnp.where(odd, mine, other).astype(jnp.float32) * sign
@@ -172,8 +165,8 @@
         total_im = k_re * p_im + k_im * p_re
         b = other_cols[at, :]
         p_re, p_im = dot(a_other, b, 1, 1), dot(other_turned, b, 1, 1)
-        k_re = kern_ref[:, 0, :, at].reshape(BLOCK, per).astype(jnp.float32)
-        k_im = kern_ref[:, 1, :, at].reshape(BLOCK, per).astype(jnp.float32) * -sign
+        k_re = kern_ref[:, 1, :, at].reshape(BLOCK, per).astype(jnp.float32)
+        k_im = kern_ref[:, 2, :, at].reshape(BLOCK, per).astype(jnp.float32) * -sign
         total_re += k_re * p_re - k_im * p_im
         total_im += k_re * p_im + k_im * p_re
         m_ref[:, at] = total_re.astype(jnp.bfloat16)
@@ -184,7 +177,7 @@
     points = pltpu.VMEM((BLOCK, LANES), jnp.bfloat16)
     in_hbm = pl.BlockSpec(memory_space=pltpu.HBM)
     late = NZ - EARLY
-    specs = [IN_VMEM] * 2 + [in_hbm] * 2 + [IN_VMEM] + [in_hbm] * EARLY + [IN_VMEM] * (late + 3)
+    specs = [IN_VMEM] * 2 + [in_hbm] * 2 + [IN_VMEM] + [in_hbm] * EARLY + [IN_VMEM] * (late + 2)
     arrays = [near(four), near(up), *map(away, over), near(down)]
     arrays += [*map(away, cols[:EARLY]), *map(near, cols[EARLY:]), *map(near, kerns)]
     return pl.pallas_call(
@@ -320,24 +313,24 @@
     far, own_side, far_side = lax.optimization_barrier(first)[2:]
 
     over_yx = [[g * NZ + i for g in range(GROUPS)] for i in range(NZ)]
+    sends = pack(odd, pair_kdiff, diff_core, diff_far, stored_kernel_index, kernels)
+    kern = lax.all_to_all(sends, "band", 0, 0, axis_index_groups=over_yx)
+    half = swap_groups(kern[:, 0], 1)
+
     four, both = bundle(own, far, own_side, far_side)
-    cols, ahead, behind = [both], both, both
-    for _ in range(3):
+    opposite = shift(both, 0, 0, NZ // 2)
+    steps = shift(four, 1, 0, 0), shift(four, -1, 0, 0), shift(both, 0, 0, 1), shift(both, 0, 0, -1)
+    up, down, ahead, behind = lax.optimization_barrier(steps)
+    over = shift(up[:2], 1, 0, 0), shift(down[2:], -1, 0, 0)
+    cols = [both, ahead, behind]
+    for _ in range(2):
         ahead, behind = shift(ahead, 0, 0, 1), shift(behind, 0, 0, -1)
         cols += [ahead, behind]
-    cols.append(shift(ahead, 0, 0, 1))
-    up, down = shift(four, 1, 0, 0), shift(four, -1, 0, 0)
-
-    shared, single = pack(odd, pair_kdiff, diff_core, diff_far, stored_kernel_index, kernels)
-    mine = lax.all_to_all(shared, "band", 0, 0, axis_index_groups=over_yx)
-    half = swap_groups(mine, 1)
-    single, up, down = lax.optimization_barrier((single, up, down))
-    over = shift(up[:2], 1, 0, 0), shift(down[2:], -1, 0, 0)
-    kern = lax.all_to_all(single, "band", 0, 0, axis_index_groups=over_yx)
+    cols.insert(3, opposite)
 
     place = jnp.stack([(y - dy) % NY * NX + (x - dx) % NX for dy in range(NY) for dx in range(NX)])
-    slots = jnp.stack([(z + i) % NZ for i in (0, -1, 1, -2, 2, -3, 3, -4)])
-    m_out, rows, cols = mix(place, slots, odd, four, up, over, down, cols, mine, half, kern)
+    slots = jnp.stack([(z + i) % NZ for i in (0, -1, 1, -4, -2, 2, -3, 3)])
+    m_out, rows, cols = mix(place, slots, odd, four, up, over, down, cols, half, kern)
     m_own = swap_groups(m_out, 1)
     left, right = prepare(rows, cols)
     total = reduce_windows(project(m_own, left, right))

time: 116 us -> 131 us (1.13); the launches traced: 116 us -> 130 us
  waiting for transfers between devices: 33.7 us -> 47.3 us
    ppermute x12, waiting for transfers between devices: 13 us -> 29.4 us  [shift(): return lax.ppermute(block, 'band', band_route(dy, dx, dz))]
    all_to_all x2 -> x1, waiting for transfers between devices: 6.37 us -> 0.01 us  [on_device(): kern = lax.all_to_all(sends, 'band', 0, 0, axis_index_groups=over_yx)]
    all_to_all x2 -> x1, starting transfers between devices: 10.6 us -> 5.94 us  [on_device(): kern = lax.all_to_all(sends, 'band', 0, 0, axis_index_groups=over_yx)]
    ppermute x12, starting transfers between devices: 20.9 us -> 23.9 us  [shift(): return lax.ppermute(block, 'band', band_route(dy, dx, dz))]
    ppermute x5, waiting for transfers between devices: 5.47 us -> 7.72 us  [swap_groups(): return lax.ppermute(block, 'kgrp', [(k, k ^ bit) for k in range(4)])]
    ppermute x1, starting transfers between devices: 2.25 us -> 0.04 us  [other_side(): return lax.ppermute(block, ('kgrp', 'band'), both)]
    all_to_all x1, starting transfers between devices: 3.31 us -> 5.38 us  [reduce_windows(): lax.all_to_all(parts, 'band', 0, 0, axis_index_groups=deep)]
  transfers between devices with their start and end apart: 21 -> 20, of which waited for: 9 -> 9; matrix products, arithmetic and copies ran while one was open for 1% -> 2% of each run, Pallas kernels for 5% -> 2%
where the time goes in v14:
time: 131 us; the launch traced here: 130 us
  waiting for transfers between devices  47.3 us (36%)
  starting transfers between devices  40.1 us (31%)
  blocking collectives  19.3 us (15%)
  Pallas kernels  16.5 us (13%)
  local copies, waits for them, and re-layouts  4.03 us (3%)
  other arithmetic  1.51 us (1%)
    ppermute x12, waiting for transfers between devices, shift(): return lax.ppermute(block, 'band', band_route(dy, dx, dz))  29.4 us
    ppermute x12, starting transfers between devices, shift(): return lax.ppermute(block, 'band', band_route(dy, dx, dz))  23.9 us
    all_to_all x1, blocking collectives, reduce_windows(): parts = lax.all_to_all(parts, 'band', 0, 0, axis_index_groups=wide)  19.3 us
    all_to_all x1, waiting for transfers between devices, reduce_windows(): lax.all_to_all(parts, 'band', 0, 0, axis_index_groups=deep)  8.91 us
    ppermute x5, waiting for transfers between devices, swap_groups(): return lax.ppermute(block, 'kgrp', [(k, k ^ bit) for k in range(4)])  7.72 us
    all_to_all x1, starting transfers between devices, on_device(): kern = lax.all_to_all(sends, 'band', 0, 0, axis_index_groups=over_yx)  5.94 us
    pallas_call x1, Pallas kernels, mix(): pl.pallas_call(mix_body, out_shape=[pltpu.VMEM((BLOCK, 2 * BLOCK), jnp.bf...  5.47 us
    all_to_all x1, starting transfers between devices, reduce_windows(): lax.all_to_all(parts, 'band', 0, 0, axis_index_groups=deep)  5.38 us
  transfers between devices with their start and end apart: 20, of which 9 were waited for; matrix products, arithmetic and copies ran while one was open for 2% of the time, Pallas kernels for 2%

profile of v14, /device:TPU:6, one launch (start us, length us, event | category | flops | bytes accessed | tf_op | source)
XLA Modules:
  0.0 129.6 jit_solution(3872277553107074470)
XLA Ops:
  0.0 1.4 %collective-permute-start.1 = (s32[1]{0:T(128)}, s32[1]{0:T(128)}, u32[]{:S(2)}, u32[]{:S(2)}) collective-permute-start(s32[1]{0:T(128)} %param.6), channel_id=1, source_target_pairs={{0,128},{64,192},{128,0},{192,64},{1,129},{65,193},{129,1},{193,65... | collective-permute-start | bytes 20 | tf_op jit(solution)/shard_map/ppermute | solution.py:41
  2.1 3.0 %collective-permute-done.1.far_ref = s32[1]{0:T(128)} collective-permute-done((s32[1]{0:T(128)}, s32[1]{0:T(128)}, u32[]{:S(2)}, u32[]{:S(2)}) %collective-permute-start.1) | collective-permute-done | bytes 36 | tf_op jit(solution)/shard_map/ppermute | solution.py:41
  5.8 4.6 %pack.1 = bf16[8,3,64,512]{3,2,1,0:T(8,128)(2,1)} custom-call(s32[1]{0:T(128)} %bitcast.16.odd_ref, s32[1]{0:T(128)S(6)} %copy.5.own_ref, s32[1]{0:T(128)} %collective-permute-done.core_ref, s32[1]{0:T(128)} %collective-permute-done.1.far_ref, s32[8]{0:T(128)S(1)} %copy-done.1, bf16[4,2,64,4096]{3,2,1,0:T(8,128)(2,1)} %kernels_ref.1), custom_call_target="tpu_custom_call" | custom-call | tf_op jit(solution)/shard_map/pack/pallas_call | solution.py:110
  10.4 5.9 %all-to-all-start = ((bf16[8,3,64,512]{3,2,1,0:T(8,128)(2,1)}), bf16[8,3,64,512]{3,2,1,0:T(8,128)(2,1)S(1)}, u32[]{:S(2)}, u32[]{:S(2)}) async-start(bf16[8,3,64,512]{3,2,1,0:T(8,128)(2,1)} %pack.1), calls=%async_computation | async-start | bytes 3145728 | tf_op jit(solution)/shard_map/all_to_all | solution.py:317
  16.3 1.0 lay.1.own_ref
  17.3 1.4 %collective-permute-start.3 = (bf16[64,896]{1,0:T(8,128)(2,1)S(1)}, bf16[64,896]{1,0:T(8,128)(2,1)S(1)}, u32[]{:S(2)}, u32[]{:S(2)}) collective-permute-start(bf16[64,896]{1,0:T(8,128)(2,1)S(1)} %lay.1.own_ref), channel_id=1, source_target_pairs={{0,8},{1,9},{2,10},{3,11},{4,12},{5,13},{6,14},{7,15},{8,0},{9,1},... | collective-permute-start | bytes 344072 | tf_op jit(solution)/shard_map/ppermute | solution.py:37
  18.7 3.3 %collective-permute-start.2 = (bf16[64,896]{1,0:T(8,128)(2,1)S(1)}, bf16[64,896]{1,0:T(8,128)(2,1)S(1)}, u32[]{:S(2)}, u32[]{:S(2)}) collective-permute-start(bf16[64,896]{1,0:T(8,128)(2,1)S(1)} %lay.1.own_ref), channel_id=1, source_target_pairs={{0,128},{64,192},{128,0},{192,64},{1,129},{65,193},{129,1},{193,65... | collective-permute-start | bytes 344072 | tf_op jit(solution)/shard_map/ppermute | solution.py:41
  22.0 1.3 %collective-permute-done.4.far_side = bf16[64,896]{1,0:T(8,128)(2,1)S(1)} collective-permute-done((bf16[64,896]{1,0:T(8,128)(2,1)S(1)}, bf16[64,896]{1,0:T(8,128)(2,1)S(1)}, u32[]{:S(2)}, u32[]{:S(2)}) %collective-permute-start.4) | collective-permute-done | bytes 114720 | tf_op jit(solution)/shard_map/ppermute | solution.py:47
  23.3 13.9 %collective-permute-done.3.own_side = bf16[64,896]{1,0:T(8,128)(2,1)S(1)} collective-permute-done((bf16[64,896]{1,0:T(8,128)(2,1)S(1)}, bf16[64,896]{1,0:T(8,128)(2,1)S(1)}, u32[]{:S(2)}, u32[]{:S(2)}) %collective-permute-start.3) | collective-permute-done | bytes 114720 | tf_op jit(solution)/shard_map/ppermute | solution.py:37
  37.2 2.6 %collective-permute-done.2.far_ref = bf16[64,896]{1,0:T(8,128)(2,1)S(1)} collective-permute-done((bf16[64,896]{1,0:T(8,128)(2,1)S(1)}, bf16[64,896]{1,0:T(8,128)(2,1)S(1)}, u32[]{:S(2)}, u32[]{:S(2)}) %collective-permute-start.2) | collective-permute-done | bytes 114720 | tf_op jit(solution)/shard_map/ppermute | solution.py:41
  39.8 0.8 bundle.1
  40.7 2.5 %collective-permute-start.6 = (bf16[4,64,896]{2,1,0:T(8,128)(2,1)}, bf16[4,64,896]{2,1,0:T(8,128)(2,1)S(1)}, u32[]{:S(2)}, u32[]{:S(2)}) collective-permute-start(bf16[4,64,896]{2,1,0:T(8,128)(2,1)} %get-tuple-element.22.refs_0_), channel_id=1, source_target_pairs={{0,48},{1,49},{2,50},{3,51},{4,52},{5,53},{6,54},{7,55},{8,56},{9,... | collective-permute-start | bytes 1376264 | tf_op jit(solution)/shard_map/ppermute | solution.py:37
  43.2 5.7 %collective-permute-start.8 = (bf16[2,64,896]{2,1,0:T(8,128)(2,1)S(1)}, bf16[2,64,896]{2,1,0:T(8,128)(2,1)}, u32[]{:S(2)}, u32[]{:S(2)}) collective-permute-start(bf16[2,64,896]{2,1,0:T(8,128)(2,1)S(1)} %get-tuple-element.23.refs_5_), channel_id=1, source_target_pairs={{0,7},{1,0},{2,1},{3,2},{4,3},{5,4},{6,5},{7,6},{8,15},{9,8},{10,9... | collective-permute-start | bytes 688136 | tf_op jit(solution)/shard_map/ppermute | solution.py:37
  48.9 0.8 slice_bitcast_fusion
  49.8 2.7 %collective-permute-done.8.refs_7_ = bf16[2,64,896]{2,1,0:T(8,128)(2,1)} collective-permute-done((bf16[2,64,896]{2,1,0:T(8,128)(2,1)S(1)}, bf16[2,64,896]{2,1,0:T(8,128)(2,1)}, u32[]{:S(2)}, u32[]{:S(2)}) %collective-permute-start.8) | collective-permute-done | bytes 229408 | tf_op jit(solution)/shard_map/ppermute | solution.py:37
  52.4 4.6 %collective-permute-start.11 = (bf16[2,64,896]{2,1,0:T(8,128)(2,1)S(1)}, bf16[2,64,896]{2,1,0:T(8,128)(2,1)S(1)}, u32[]{:S(2)}, u32[]{:S(2)}) collective-permute-start(bf16[2,64,896]{2,1,0:T(8,128)(2,1)S(1)} %get-tuple-element.23.refs_5_), channel_id=1, source_target_pairs={{0,4},{1,5},{2,6},{3,7},{4,0},{5,1},{6,2},{7,3},{8,12},{9,13},{10,... | collective-permute-start | bytes 688136 | tf_op jit(solution)/shard_map/ppermute | solution.py:37
  57.1 8.7 %collective-permute-done.7.refs_6_ = bf16[2,64,896]{2,1,0:T(8,128)(2,1)} collective-permute-done((bf16[2,64,896]{2,1,0:T(8,128)(2,1)S(1)}, bf16[2,64,896]{2,1,0:T(8,128)(2,1)}, u32[]{:S(2)}, u32[]{:S(2)}) %collective-permute-start.7) | collective-permute-done | bytes 229408 | tf_op jit(solution)/shard_map/ppermute | solution.py:37
  65.8 3.2 %collective-permute-start.13 = (bf16[2,64,896]{2,1,0:T(8,128)(2,1)}, bf16[2,64,896]{2,1,0:T(8,128)(2,1)}, u32[]{:S(2)}, u32[]{:S(2)}) collective-permute-start(bf16[2,64,896]{2,1,0:T(8,128)(2,1)} %collective-permute-done.8.refs_7_), channel_id=1, source_target_pairs={{0,7},{1,0},{2,1},{3,2},{4,3},{5,4},{6,5},{7,6},{8,15},{9,8},{10,9... | collective-permute-start | bytes 688136 | tf_op jit(solution)/shard_map/ppermute | solution.py:37
  69.0 0.7 slice.21
  69.7 0.7 slice.22
  70.4 3.2 %collective-permute-start.10 = (bf16[2,64,896]{2,1,0:T(8,128)(2,1)}, bf16[2,64,896]{2,1,0:T(8,128)(2,1)}, u32[]{:S(2)}, u32[]{:S(2)}) collective-permute-start(bf16[2,64,896]{2,1,0:T(8,128)(2,1)} %slice.22), channel_id=1, source_target_pairs={{0,48},{1,49},{2,50},{3,51},{4,52},{5,53},{6,54},{7,55},{8,56},{9,... | collective-permute-start | bytes 688136 | tf_op jit(solution)/shard_map/ppermute | solution.py:37
  73.6 0.7 copy-done.2
  74.4 3.3 %collective-permute-start.15 = (bf16[2,64,896]{2,1,0:T(8,128)(2,1)}, bf16[2,64,896]{2,1,0:T(8,128)(2,1)}, u32[]{:S(2)}, u32[]{:S(2)}) collective-permute-start(bf16[2,64,896]{2,1,0:T(8,128)(2,1)} %collective-permute-done.13.refs_10_), channel_id=1, source_target_pairs={{0,7},{1,0},{2,1},{3,2},{4,3},{5,4},{6,5},{7,6},{8,15},{9,8},{10,9... | collective-permute-start | bytes 688136 | tf_op jit(solution)/shard_map/ppermute | solution.py:37
  77.8 4.1 %collective-permute-done.9.refs_2_ = bf16[2,64,896]{2,1,0:T(8,128)(2,1)} collective-permute-done((bf16[2,64,896]{2,1,0:T(8,128)(2,1)}, bf16[2,64,896]{2,1,0:T(8,128)(2,1)}, u32[]{:S(2)}, u32[]{:S(2)}) %collective-permute-start.9) | collective-permute-done | bytes 229408 | tf_op jit(solution)/shard_map/ppermute | solution.py:37
  81.9 5.5 %mix.1 = (bf16[512,1024]{1,0:T(8,128)(2,1)S(1)}, bf16[512,896]{1,0:T(8,128)(2,1)S(1)}, bf16[512,896]{1,0:T(8,128)(2,1)S(1)}) custom-call(s32[8]{0:T(128)S(1)} %stack.71.place_ref, s32[8]{0:T(128)S(1)} %stack.80.slot_ref, s32[1]{0:T(128)} %bitcast.16.odd_ref, bf16[4,64,896]{2,1,0:T(8,128)(2,1)} %get-tuple-element.22.refs_0_, ...), custom_call_target="tpu_custom_call" | custom-call | tf_op jit(solution)/shard_map/mix/pallas_call | solution.py:183
  88.1 2.1 %collective-permute-done.17.m_ref = bf16[512,1024]{1,0:T(8,128)(2,1)S(1)} collective-permute-done((bf16[512,1024]{1,0:T(8,128)(2,1)S(1)}, bf16[512,1024]{1,0:T(8,128)(2,1)S(1)}, u32[]{:S(2)}, u32[]{:S(2)}) %collective-permute-start.17) | collective-permute-done | bytes 1048608 | tf_op jit(solution)/shard_map/ppermute | solution.py:41
  90.1 4.1 %project.1 = bf16[64,8,896]{2,1,0:T(8,128)(2,1)S(1)} custom-call(bf16[512,1024]{1,0:T(8,128)(2,1)S(1)} %collective-permute-done.17.m_ref, bf16[432,1024]{1,0:T(8,128)(2,1)S(1)} %get-tuple-element.31.left_ref, bf16[1024,896]{1,0:T(8,128)(2,1)S(1)} %get-tuple-element.32.right_ref), custom_call_target="tpu_custom_call" | custom-call | tf_op jit(solution)/shard_map/project/pallas_call | solution.py:249
  94.2 19.3 %all_to_all.15 = bf16[16,4,8,896]{3,2,1,0:T(8,128)(2,1)S(1)} all-to-all(bf16[16,4,8,896]{3,2,1,0:T(8,128)(2,1)S(1)} %bitcast.22), channel_id=1, replica_groups={{0,1,8,9,16,17,24,25,32,33,40,41,48,49,56,57},{2,3,10,11,18,19,26,27,34..., dimensions={0} | all-to-all | bytes 1835008 | tf_op jit(solution)/shard_map/all_to_all | solution.py:290
  113.5 0.8 convert_reduce_fusion
  114.3 5.4 %all-to-all-start.2 = ((f32[4,8,896]{2,1,0:T(8,128)}), f32[4,8,896]{2,1,0:T(8,128)S(1)}, u32[]{:S(2)}, u32[]{:S(2)}) async-start(f32[4,8,896]{2,1,0:T(8,128)} %convert_reduce_fusion), calls=%async_computation.2 | async-start | bytes 229376 | tf_op jit(solution)/shard_map/all_to_all | solution.py:292
  119.7 8.9 %all-to-all-done.2 = f32[4,8,896]{2,1,0:T(8,128)S(1)} async-done(((f32[4,8,896]{2,1,0:T(8,128)}), f32[4,8,896]{2,1,0:T(8,128)S(1)}, u32[]{:S(2)}, u32[]{:S(2)}) %all-to-all-start.2) | async-done | bytes 114720 | tf_op jit(solution)/shard_map/all_to_all | solution.py:292
  128.9 0.7 fusion.1
  (34 shorter events, 1.9 us)
Async XLA Ops:
  0.0 2.1 %collective-permute-start = (s32[1]{0:T(128)}, s32[1]{0:T(128)}, u32[]{:S(2)}, u32[]{:S(2)}) collective-permute-start(s32[1]{0:T(128)} %param.6), channel_id=1, source_target_pairs={{0,64},{64,0},{128,192},{192,128},{1,65},{65,1},{129,193},{193,129... | collective-permute-start | bytes 20 | tf_op jit(solution)/shard_map/ppermute | solution.py:41
  0.0 5.1 %collective-permute-start.1 = (s32[1]{0:T(128)}, s32[1]{0:T(128)}, u32[]{:S(2)}, u32[]{:S(2)}) collective-permute-start(s32[1]{0:T(128)} %param.6), channel_id=1, source_target_pairs={{0,128},{64,192},{128,0},{192,64},{1,129},{65,193},{129,1},{193,65... | collective-permute-start | bytes 20 | tf_op jit(solution)/shard_map/ppermute | solution.py:41
  5.1 0.7 copy-start.1
  10.4 38.6 %all-to-all-start = ((bf16[8,3,64,512]{3,2,1,0:T(8,128)(2,1)}), bf16[8,3,64,512]{3,2,1,0:T(8,128)(2,1)S(1)}, u32[]{:S(2)}, u32[]{:S(2)}) async-start(bf16[8,3,64,512]{3,2,1,0:T(8,128)(2,1)} %pack.1), calls=%async_computation | async-start | bytes 3145728 | tf_op jit(solution)/shard_map/all_to_all | solution.py:317
  17.3 6.0 %collective-permute-start.4 = (bf16[64,896]{1,0:T(8,128)(2,1)S(1)}, bf16[64,896]{1,0:T(8,128)(2,1)S(1)}, u32[]{:S(2)}, u32[]{:S(2)}) collective-permute-start(bf16[64,896]{1,0:T(8,128)(2,1)S(1)} %lay.1.own_ref), channel_id=1, source_target_pairs={{128,8},{129,9},{130,10},{131,11},{132,12},{133,13},{134,14},{135,... | collective-permute-start | bytes 344072 | tf_op jit(solution)/shard_map/ppermute | solution.py:47
  17.3 19.9 %collective-permute-start.3 = (bf16[64,896]{1,0:T(8,128)(2,1)S(1)}, bf16[64,896]{1,0:T(8,128)(2,1)S(1)}, u32[]{:S(2)}, u32[]{:S(2)}) collective-permute-start(bf16[64,896]{1,0:T(8,128)(2,1)S(1)} %lay.1.own_ref), channel_id=1, source_target_pairs={{0,8},{1,9},{2,10},{3,11},{4,12},{5,13},{6,14},{7,15},{8,0},{9,1},... | collective-permute-start | bytes 344072 | tf_op jit(solution)/shard_map/ppermute | solution.py:37
  18.7 21.1 %collective-permute-start.2 = (bf16[64,896]{1,0:T(8,128)(2,1)S(1)}, bf16[64,896]{1,0:T(8,128)(2,1)S(1)}, u32[]{:S(2)}, u32[]{:S(2)}) collective-permute-start(bf16[64,896]{1,0:T(8,128)(2,1)S(1)} %lay.1.own_ref), channel_id=1, source_target_pairs={{0,128},{64,192},{128,0},{192,64},{1,129},{65,193},{129,1},{193,65... | collective-permute-start | bytes 344072 | tf_op jit(solution)/shard_map/ppermute | solution.py:41
  40.7 41.2 %copy-start = (bf16[2,64,896]{2,1,0:T(8,128)(2,1)}, bf16[2,64,896]{2,1,0:T(8,128)(2,1)S(1)}, u32[]{:S(2)}) copy-start(bf16[2,64,896]{2,1,0:T(8,128)(2,1)S(1)} %get-tuple-element.23.refs_5_) | copy-start | bytes 688132
  40.7 25.1 %collective-permute-start.6 = (bf16[4,64,896]{2,1,0:T(8,128)(2,1)}, bf16[4,64,896]{2,1,0:T(8,128)(2,1)S(1)}, u32[]{:S(2)}, u32[]{:S(2)}) collective-permute-start(bf16[4,64,896]{2,1,0:T(8,128)(2,1)} %get-tuple-element.22.refs_0_), channel_id=1, source_target_pairs={{0,48},{1,49},{2,50},{3,51},{4,52},{5,53},{6,54},{7,55},{8,56},{9,... | collective-permute-start | bytes 1376264 | tf_op jit(solution)/shard_map/ppermute | solution.py:37
  43.2 22.6 %collective-permute-start.5 = (bf16[4,64,896]{2,1,0:T(8,128)(2,1)}, bf16[4,64,896]{2,1,0:T(8,128)(2,1)S(1)}, u32[]{:S(2)}, u32[]{:S(2)}) collective-permute-start(bf16[4,64,896]{2,1,0:T(8,128)(2,1)} %get-tuple-element.22.refs_0_), channel_id=1, source_target_pairs={{0,16},{1,17},{2,18},{3,19},{4,20},{5,21},{6,22},{7,23},{8,24},{9,... | collective-permute-start | bytes 1376264 | tf_op jit(solution)/shard_map/ppermute | solution.py:37
  43.2 9.3 %collective-permute-start.8 = (bf16[2,64,896]{2,1,0:T(8,128)(2,1)S(1)}, bf16[2,64,896]{2,1,0:T(8,128)(2,1)}, u32[]{:S(2)}, u32[]{:S(2)}) collective-permute-start(bf16[2,64,896]{2,1,0:T(8,128)(2,1)S(1)} %get-tuple-element.23.refs_5_), channel_id=1, source_target_pairs={{0,7},{1,0},{2,1},{3,2},{4,3},{5,4},{6,5},{7,6},{8,15},{9,8},{10,9... | collective-permute-start | bytes 688136 | tf_op jit(solution)/shard_map/ppermute | solution.py:37
  48.9 16.9 %collective-permute-start.7 = (bf16[2,64,896]{2,1,0:T(8,128)(2,1)S(1)}, bf16[2,64,896]{2,1,0:T(8,128)(2,1)}, u32[]{:S(2)}, u32[]{:S(2)}) collective-permute-start(bf16[2,64,896]{2,1,0:T(8,128)(2,1)S(1)} %get-tuple-element.23.refs_5_), channel_id=1, source_target_pairs={{0,1},{1,2},{2,3},{3,4},{4,5},{5,6},{6,7},{7,0},{8,9},{9,10},{10,1... | collective-permute-start | bytes 688136 | tf_op jit(solution)/shard_map/ppermute | solution.py:37
  49.8 32.1 %collective-permute-start.16 = (bf16[8,64,512]{2,1,0:T(8,128)(2,1)}, bf16[8,64,512]{2,1,0:T(8,128)(2,1)S(1)}, u32[]{:S(2)}, u32[]{:S(2)}) collective-permute-start(bf16[8,64,512]{2,1,0:T(8,128)(2,1)} %slice_bitcast_fusion), channel_id=1, source_target_pairs={{0,64},{64,0},{128,192},{192,128},{1,65},{65,1},{129,193},{193,129... | collective-permute-start | bytes 1572872 | tf_op jit(solution)/shard_map/ppermute | solution.py:41
  52.4 21.2 %collective-permute-start.11 = (bf16[2,64,896]{2,1,0:T(8,128)(2,1)S(1)}, bf16[2,64,896]{2,1,0:T(8,128)(2,1)S(1)}, u32[]{:S(2)}, u32[]{:S(2)}) collective-permute-start(bf16[2,64,896]{2,1,0:T(8,128)(2,1)S(1)} %get-tuple-element.23.refs_5_), channel_id=1, source_target_pairs={{0,4},{1,5},{2,6},{3,7},{4,0},{5,1},{6,2},{7,3},{8,12},{9,13},{10,... | collective-permute-start | bytes 688136 | tf_op jit(solution)/shard_map/ppermute | solution.py:37
  65.8 8.6 %collective-permute-start.12 = (bf16[2,64,896]{2,1,0:T(8,128)(2,1)}, bf16[2,64,896]{2,1,0:T(8,128)(2,1)}, u32[]{:S(2)}, u32[]{:S(2)}) collective-permute-start(bf16[2,64,896]{2,1,0:T(8,128)(2,1)} %collective-permute-done.7.refs_6_), channel_id=1, source_target_pairs={{0,1},{1,2},{2,3},{3,4},{4,5},{5,6},{6,7},{7,0},{8,9},{9,10},{10,1... | collective-permute-start | bytes 688136 | tf_op jit(solution)/shard_map/ppermute | solution.py:37
  65.8 8.6 %collective-permute-start.13 = (bf16[2,64,896]{2,1,0:T(8,128)(2,1)}, bf16[2,64,896]{2,1,0:T(8,128)(2,1)}, u32[]{:S(2)}, u32[]{:S(2)}) collective-permute-start(bf16[2,64,896]{2,1,0:T(8,128)(2,1)} %collective-permute-done.8.refs_7_), channel_id=1, source_target_pairs={{0,7},{1,0},{2,1},{3,2},{4,3},{5,4},{6,5},{7,6},{8,15},{9,8},{10,9... | collective-permute-start | bytes 688136 | tf_op jit(solution)/shard_map/ppermute | solution.py:37
  70.4 7.4 %collective-permute-start.10 = (bf16[2,64,896]{2,1,0:T(8,128)(2,1)}, bf16[2,64,896]{2,1,0:T(8,128)(2,1)}, u32[]{:S(2)}, u32[]{:S(2)}) collective-permute-start(bf16[2,64,896]{2,1,0:T(8,128)(2,1)} %slice.22), channel_id=1, source_target_pairs={{0,48},{1,49},{2,50},{3,51},{4,52},{5,53},{6,54},{7,55},{8,56},{9,... | collective-permute-start | bytes 688136 | tf_op jit(solution)/shard_map/ppermute | solution.py:37
  73.6 0.7 copy-start.2
  74.3 7.5 %collective-permute-start.9 = (bf16[2,64,896]{2,1,0:T(8,128)(2,1)}, bf16[2,64,896]{2,1,0:T(8,128)(2,1)}, u32[]{:S(2)}, u32[]{:S(2)}) collective-permute-start(bf16[2,64,896]{2,1,0:T(8,128)(2,1)} %slice.21), channel_id=1, source_target_pairs={{0,16},{1,17},{2,18},{3,19},{4,20},{5,21},{6,22},{7,23},{8,24},{9,... | collective-permute-start | bytes 688136 | tf_op jit(solution)/shard_map/ppermute | solution.py:37
  74.3 7.5 %collective-permute-start.14 = (bf16[2,64,896]{2,1,0:T(8,128)(2,1)}, bf16[2,64,896]{2,1,0:T(8,128)(2,1)}, u32[]{:S(2)}, u32[]{:S(2)}) collective-permute-start(bf16[2,64,896]{2,1,0:T(8,128)(2,1)} %collective-permute-done.12.refs_9_), channel_id=1, source_target_pairs={{0,1},{1,2},{2,3},{3,4},{4,5},{5,6},{6,7},{7,0},{8,9},{9,10},{10,1... | collective-permute-start | bytes 688136 | tf_op jit(solution)/shard_map/ppermute | solution.py:37
  74.4 7.5 %collective-permute-start.15 = (bf16[2,64,896]{2,1,0:T(8,128)(2,1)}, bf16[2,64,896]{2,1,0:T(8,128)(2,1)}, u32[]{:S(2)}, u32[]{:S(2)}) collective-permute-start(bf16[2,64,896]{2,1,0:T(8,128)(2,1)} %collective-permute-done.13.refs_10_), channel_id=1, source_target_pairs={{0,7},{1,0},{2,1},{3,2},{4,3},{5,4},{6,5},{7,6},{8,15},{9,8},{10,9... | collective-permute-start | bytes 688136 | tf_op jit(solution)/shard_map/ppermute | solution.py:37
  87.4 2.7 %collective-permute-start.17 = (bf16[512,1024]{1,0:T(8,128)(2,1)S(1)}, bf16[512,1024]{1,0:T(8,128)(2,1)S(1)}, u32[]{:S(2)}, u32[]{:S(2)}) collective-permute-start(bf16[512,1024]{1,0:T(8,128)(2,1)S(1)} %get-tuple-element.28), channel_id=1, source_target_pairs={{0,64},{64,0},{128,192},{192,128},{1,65},{65,1},{129,193},{193,129... | collective-permute-start | bytes 3145736 | tf_op jit(solution)/shard_map/ppermute | solution.py:41
  114.3 14.3 %all-to-all-start.2 = ((f32[4,8,896]{2,1,0:T(8,128)}), f32[4,8,896]{2,1,0:T(8,128)S(1)}, u32[]{:S(2)}, u32[]{:S(2)}) async-start(f32[4,8,896]{2,1,0:T(8,128)} %convert_reduce_fusion), calls=%async_computation.2 | async-start | bytes 229376 | tf_op jit(solution)/shard_map/all_to_all | solution.py:292

commit v15 on v14

--- a/solution.py
+++ b/solution.py
@@ -313,11 +313,11 @@
     far, own_side, far_side = lax.optimization_barrier(first)[2:]
 
     over_yx = [[g * NZ + i for g in range(GROUPS)] for i in range(NZ)]
+    four, both = bundle(own, far, own_side, far_side)
     sends = pack(odd, pair_kdiff, diff_core, diff_far, stored_kernel_index, kernels)
+    sends, four, both = lax.optimization_barrier((sends, four, both))
     kern = lax.all_to_all(sends, "band", 0, 0, axis_index_groups=over_yx)
     half = swap_groups(kern[:, 0], 1)
-
-    four, both = bundle(own, far, own_side, far_side)
     opposite = shift(both, 0, 0, NZ // 2)
     steps = shift(four, 1, 0, 0), shift(four, -1, 0, 0), shift(both, 0, 0, 1), shift(both, 0, 0, -1)
     up, down, ahead, behind = lax.optimization_barrier(steps)

time: 131 us -> 124 us (0.947); the launches traced: 130 us -> 124 us
  waiting for transfers between devices: 47.3 us -> 40.4 us
  starting transfers between devices: 40.1 us -> 44.1 us
  blocking collectives: 19.3 us -> 17.7 us
    ppermute x12, waiting for transfers between devices: 29.4 us -> 12.9 us  [shift(): return lax.ppermute(block, 'band', band_route(dy, dx, dz))]
    all_to_all x1, waiting for transfers between devices: 0.01 us -> 13.1 us  [on_device(): kern = lax.all_to_all(sends, 'band', 0, 0, axis_index_groups=over_yx)]
    ppermute x12, starting transfers between devices: 23.9 us -> 26.4 us  [shift(): return lax.ppermute(block, 'band', band_route(dy, dx, dz))]
    ppermute x5, waiting for transfers between devices: 7.72 us -> 5.46 us  [swap_groups(): return lax.ppermute(block, 'kgrp', [(k, k ^ bit) for k in range(4)])]
    ppermute x1, starting transfers between devices: 0.04 us -> 2.25 us  [other_side(): return lax.ppermute(block, ('kgrp', 'band'), both)]
    all_to_all x1, blocking collectives: 19.3 us -> 17.7 us  [reduce_windows(): parts = lax.all_to_all(parts, 'band', 0, 0, axis_index_groups=wide)]
  transfers between devices with their start and end apart: 20 -> 20, of which waited for: 9 -> 8; matrix products, arithmetic and copies ran while one was open for 2% -> 2% of each run, Pallas kernels for 2% -> 4%
where the time goes in v15:
time: 124 us
  starting transfers between devices  44.1 us (36%)
  waiting for transfers between devices  40.4 us (33%)
  blocking collectives  17.7 us (14%)
  Pallas kernels  16.2 us (13%)
  local copies, waits for them, and re-layouts  3.35 us (3%)
  other arithmetic  1.52 us (1%)
    ppermute x12, starting transfers between devices, shift(): return lax.ppermute(block, 'band', band_route(dy, dx, dz))  26.4 us
    all_to_all x1, blocking collectives, reduce_windows(): parts = lax.all_to_all(parts, 'band', 0, 0, axis_index_groups=wide)  17.7 us
    all_to_all x1, waiting for transfers between devices, on_device(): kern = lax.all_to_all(sends, 'band', 0, 0, axis_index_groups=over_yx)  13.1 us
    ppermute x12, waiting for transfers between devices, shift(): return lax.ppermute(block, 'band', band_route(dy, dx, dz))  12.9 us
    all_to_all x1, waiting for transfers between devices, reduce_windows(): lax.all_to_all(parts, 'band', 0, 0, axis_index_groups=deep)  8.9 us
    all_to_all x1, starting transfers between devices, on_device(): kern = lax.all_to_all(sends, 'band', 0, 0, axis_index_groups=over_yx)  5.93 us
    all_to_all x1, starting transfers between devices, reduce_windows(): lax.all_to_all(parts, 'band', 0, 0, axis_index_groups=deep)  5.84 us
    ppermute x5, waiting for transfers between devices, swap_groups(): return lax.ppermute(block, 'kgrp', [(k, k ^ bit) for k in range(4)])  5.46 us
  transfers between devices with their start and end apart: 20, of which 8 were waited for; matrix products, arithmetic and copies ran while one was open for 2% of the time, Pallas kernels for 4%

profile of v15, /device:TPU:6, one launch (start us, length us, event | category | flops | bytes accessed | tf_op | source)
XLA Modules:
  0.0 124.0 jit_solution(12008913957431125395)
XLA Ops:
  0.0 1.0 lay.1.own_ref
  1.0 2.3 %collective-permute-start.4 = (bf16[64,896]{1,0:T(8,128)(2,1)S(1)}, bf16[64,896]{1,0:T(8,128)(2,1)S(1)}, u32[]{:S(2)}, u32[]{:S(2)}) collective-permute-start(bf16[64,896]{1,0:T(8,128)(2,1)S(1)} %lay.1.own_ref), channel_id=1, source_target_pairs={{128,8},{129,9},{130,10},{131,11},{132,12},{133,13},{134,14},{135,... | collective-permute-start | bytes 344072 | tf_op jit(solution)/shard_map/ppermute | solution.py:47
  3.2 2.5 %collective-permute-start.2 = (bf16[64,896]{1,0:T(8,128)(2,1)S(1)}, bf16[64,896]{1,0:T(8,128)(2,1)S(1)}, u32[]{:S(2)}, u32[]{:S(2)}) collective-permute-start(bf16[64,896]{1,0:T(8,128)(2,1)S(1)} %lay.1.own_ref), channel_id=1, source_target_pairs={{0,128},{64,192},{128,0},{192,64},{1,129},{65,193},{129,1},{193,65... | collective-permute-start | bytes 344072 | tf_op jit(solution)/shard_map/ppermute | solution.py:41
  5.7 1.0 collective-permute-start.1
  7.5 3.4 %collective-permute-done.1.far_ref = s32[1]{0:T(128)} collective-permute-done((s32[1]{0:T(128)}, s32[1]{0:T(128)}, u32[]{:S(2)}, u32[]{:S(2)}) %collective-permute-start.1) | collective-permute-done | bytes 36 | tf_op jit(solution)/shard_map/ppermute | solution.py:41
  10.9 0.7 copy-done
  11.5 4.6 %pack.1 = bf16[8,3,64,512]{3,2,1,0:T(8,128)(2,1)} custom-call(s32[1]{0:T(128)} %bitcast.16.odd_ref, s32[1]{0:T(128)S(6)} %copy.5.own_ref, s32[1]{0:T(128)} %collective-permute-done.core_ref, s32[1]{0:T(128)} %collective-permute-done.1.far_ref, s32[8]{0:T(128)S(1)} %copy-done, bf16[4,2,64,4096]{3,2,1,0:T(8,128)(2,1)} %kernels_ref.1), custom_call_target="tpu_custom_call" | custom-call | tf_op jit(solution)/shard_map/pack/pallas_call | solution.py:110
  16.1 0.7 bundle.1
  16.9 5.9 %all-to-all-start = ((bf16[8,3,64,512]{3,2,1,0:T(8,128)(2,1)}), bf16[8,3,64,512]{3,2,1,0:T(8,128)(2,1)S(1)}, u32[]{:S(2)}, u32[]{:S(2)}) async-start(bf16[8,3,64,512]{3,2,1,0:T(8,128)(2,1)} %pack.1), calls=%async_computation | async-start | bytes 3145728 | tf_op jit(solution)/shard_map/all_to_all | solution.py:319
  22.8 2.7 %collective-permute-start.6 = (bf16[4,64,896]{2,1,0:T(8,128)(2,1)S(1)}, bf16[4,64,896]{2,1,0:T(8,128)(2,1)S(1)}, u32[]{:S(2)}, u32[]{:S(2)}) collective-permute-start(bf16[4,64,896]{2,1,0:T(8,128)(2,1)S(1)} %get-tuple-element.27.refs_0_), channel_id=1, source_target_pairs={{0,48},{1,49},{2,50},{3,51},{4,52},{5,53},{6,54},{7,55},{8,56},{9,... | collective-permute-start | bytes 1376264 | tf_op jit(solution)/shard_map/ppermute | solution.py:37
  25.5 5.9 %collective-permute-start.8 = (bf16[2,64,896]{2,1,0:T(8,128)(2,1)}, bf16[2,64,896]{2,1,0:T(8,128)(2,1)}, u32[]{:S(2)}, u32[]{:S(2)}) collective-permute-start(bf16[2,64,896]{2,1,0:T(8,128)(2,1)} %get-tuple-element.28.refs_5_), channel_id=1, source_target_pairs={{0,7},{1,0},{2,1},{3,2},{4,3},{5,4},{6,5},{7,6},{8,15},{9,8},{10,9... | collective-permute-start | bytes 688136 | tf_op jit(solution)/shard_map/ppermute | solution.py:37
  31.3 13.1 %all-to-all-done.refs_14_ = bf16[8,3,64,512]{3,2,1,0:T(8,128)(2,1)S(1)} async-done(((bf16[8,3,64,512]{3,2,1,0:T(8,128)(2,1)}), bf16[8,3,64,512]{3,2,1,0:T(8,128)(2,1)S(1)}, u32[]{:S(2)}, u32[]{:S(2)}) %all-to-all-start) | async-done | bytes 1572896 | tf_op jit(solution)/shard_map/all_to_all | solution.py:319
  44.4 0.9 slice_bitcast_fusion
  45.3 7.2 %collective-permute-start.11 = (bf16[2,64,896]{2,1,0:T(8,128)(2,1)}, bf16[2,64,896]{2,1,0:T(8,128)(2,1)}, u32[]{:S(2)}, u32[]{:S(2)}) collective-permute-start(bf16[2,64,896]{2,1,0:T(8,128)(2,1)} %get-tuple-element.28.refs_5_), channel_id=1, source_target_pairs={{0,4},{1,5},{2,6},{3,7},{4,0},{5,1},{6,2},{7,3},{8,12},{9,13},{10,... | collective-permute-start | bytes 688136 | tf_op jit(solution)/shard_map/ppermute | solution.py:37
  52.5 1.8 %collective-permute-start.12 = (bf16[2,64,896]{2,1,0:T(8,128)(2,1)}, bf16[2,64,896]{2,1,0:T(8,128)(2,1)}, u32[]{:S(2)}, u32[]{:S(2)}) collective-permute-start(bf16[2,64,896]{2,1,0:T(8,128)(2,1)} %collective-permute-done.7.refs_6_), channel_id=1, source_target_pairs={{0,1},{1,2},{2,3},{3,4},{4,5},{5,6},{6,7},{7,0},{8,9},{9,10},{10,1... | collective-permute-start | bytes 688136 | tf_op jit(solution)/shard_map/ppermute | solution.py:37
  54.3 3.9 %collective-permute-start.13 = (bf16[2,64,896]{2,1,0:T(8,128)(2,1)}, bf16[2,64,896]{2,1,0:T(8,128)(2,1)}, u32[]{:S(2)}, u32[]{:S(2)}) collective-permute-start(bf16[2,64,896]{2,1,0:T(8,128)(2,1)} %collective-permute-done.8.refs_7_), channel_id=1, source_target_pairs={{0,7},{1,0},{2,1},{3,2},{4,3},{5,4},{6,5},{7,6},{8,15},{9,8},{10,9... | collective-permute-start | bytes 688136 | tf_op jit(solution)/shard_map/ppermute | solution.py:37
  58.3 0.7 slice.21
  59.0 0.7 slice.22
  59.7 0.9 collective-permute-start.10
  60.5 2.1 %collective-permute-done.11.refs_8_ = bf16[2,64,896]{2,1,0:T(8,128)(2,1)} collective-permute-done((bf16[2,64,896]{2,1,0:T(8,128)(2,1)}, bf16[2,64,896]{2,1,0:T(8,128)(2,1)}, u32[]{:S(2)}, u32[]{:S(2)}) %collective-permute-start.11) | collective-permute-done | bytes 229408 | tf_op jit(solution)/shard_map/ppermute | solution.py:37
  62.6 5.6 %collective-permute-done.12.refs_9_ = bf16[2,64,896]{2,1,0:T(8,128)(2,1)} collective-permute-done((bf16[2,64,896]{2,1,0:T(8,128)(2,1)}, bf16[2,64,896]{2,1,0:T(8,128)(2,1)}, u32[]{:S(2)}, u32[]{:S(2)}) %collective-permute-start.12) | collective-permute-done | bytes 229408 | tf_op jit(solution)/shard_map/ppermute | solution.py:37
  68.3 1.7 %collective-permute-start.14 = (bf16[2,64,896]{2,1,0:T(8,128)(2,1)}, bf16[2,64,896]{2,1,0:T(8,128)(2,1)}, u32[]{:S(2)}, u32[]{:S(2)}) collective-permute-start(bf16[2,64,896]{2,1,0:T(8,128)(2,1)} %collective-permute-done.12.refs_9_), channel_id=1, source_target_pairs={{0,1},{1,2},{2,3},{3,4},{4,5},{5,6},{6,7},{7,0},{8,9},{9,10},{10,1... | collective-permute-start | bytes 688136 | tf_op jit(solution)/shard_map/ppermute | solution.py:37
  69.9 2.3 %collective-permute-start.15 = (bf16[2,64,896]{2,1,0:T(8,128)(2,1)}, bf16[2,64,896]{2,1,0:T(8,128)(2,1)}, u32[]{:S(2)}, u32[]{:S(2)}) collective-permute-start(bf16[2,64,896]{2,1,0:T(8,128)(2,1)} %collective-permute-done.13.refs_10_), channel_id=1, source_target_pairs={{0,7},{1,0},{2,1},{3,2},{4,3},{5,4},{6,5},{7,6},{8,15},{9,8},{10,9... | collective-permute-start | bytes 688136 | tf_op jit(solution)/shard_map/ppermute | solution.py:37
  72.5 4.8 %collective-permute-done.14.refs_11_ = bf16[2,64,896]{2,1,0:T(8,128)(2,1)} collective-permute-done((bf16[2,64,896]{2,1,0:T(8,128)(2,1)}, bf16[2,64,896]{2,1,0:T(8,128)(2,1)}, u32[]{:S(2)}, u32[]{:S(2)}) %collective-permute-start.14) | collective-permute-done | bytes 229408 | tf_op jit(solution)/shard_map/ppermute | solution.py:37
  77.7 5.3 %mix.1 = (bf16[512,1024]{1,0:T(8,128)(2,1)S(1)}, bf16[512,896]{1,0:T(8,128)(2,1)S(1)}, bf16[512,896]{1,0:T(8,128)(2,1)S(1)}) custom-call(s32[8]{0:T(128)S(1)} %stack.71.place_ref, s32[8]{0:T(128)S(1)} %stack.80.slot_ref, s32[1]{0:T(128)} %bitcast.16.odd_ref, bf16[4,64,896]{2,1,0:T(8,128)(2,1)S(1)} %get-tuple-element.27.refs_0_, ...), custom_call_target="tpu_custom_call" | custom-call | tf_op jit(solution)/shard_map/mix/pallas_call | solution.py:183
  83.6 2.1 %collective-permute-done.17.m_ref = bf16[512,1024]{1,0:T(8,128)(2,1)S(1)} collective-permute-done((bf16[512,1024]{1,0:T(8,128)(2,1)S(1)}, bf16[512,1024]{1,0:T(8,128)(2,1)S(1)}, u32[]{:S(2)}, u32[]{:S(2)}) %collective-permute-start.17) | collective-permute-done | bytes 1048608 | tf_op jit(solution)/shard_map/ppermute | solution.py:41
  85.7 4.0 %project.1 = bf16[64,8,896]{2,1,0:T(8,128)(2,1)S(1)} custom-call(bf16[512,1024]{1,0:T(8,128)(2,1)S(1)} %collective-permute-done.17.m_ref, bf16[432,1024]{1,0:T(8,128)(2,1)S(1)} %get-tuple-element.37.left_ref, bf16[1024,896]{1,0:T(8,128)(2,1)S(1)} %get-tuple-element.38.right_ref), custom_call_target="tpu_custom_call" | custom-call | tf_op jit(solution)/shard_map/project/pallas_call | solution.py:249
  89.8 17.7 %all_to_all.15 = bf16[16,4,8,896]{3,2,1,0:T(8,128)(2,1)S(1)} all-to-all(bf16[16,4,8,896]{3,2,1,0:T(8,128)(2,1)S(1)} %bitcast.22), channel_id=1, replica_groups={{0,1,8,9,16,17,24,25,32,33,40,41,48,49,56,57},{2,3,10,11,18,19,26,27,34..., dimensions={0} | all-to-all | bytes 1835008 | tf_op jit(solution)/shard_map/all_to_all | solution.py:290
  107.4 0.8 convert_reduce_fusion
  108.2 5.8 %all-to-all-start.2 = ((f32[4,8,896]{2,1,0:T(8,128)}), f32[4,8,896]{2,1,0:T(8,128)S(1)}, u32[]{:S(2)}, u32[]{:S(2)}) async-start(f32[4,8,896]{2,1,0:T(8,128)} %convert_reduce_fusion), calls=%async_computation.2 | async-start | bytes 229376 | tf_op jit(solution)/shard_map/all_to_all | solution.py:292
  114.1 8.9 %all-to-all-done.2 = f32[4,8,896]{2,1,0:T(8,128)S(1)} async-done(((f32[4,8,896]{2,1,0:T(8,128)}), f32[4,8,896]{2,1,0:T(8,128)S(1)}, u32[]{:S(2)}, u32[]{:S(2)}) %all-to-all-start.2) | async-done | bytes 114720 | tf_op jit(solution)/shard_map/all_to_all | solution.py:292
  123.3 0.7 fusion.1
  (30 shorter events, 1.5 us)
Async XLA Ops:
  1.0 15.1 %collective-permute-start.4 = (bf16[64,896]{1,0:T(8,128)(2,1)S(1)}, bf16[64,896]{1,0:T(8,128)(2,1)S(1)}, u32[]{:S(2)}, u32[]{:S(2)}) collective-permute-start(bf16[64,896]{1,0:T(8,128)(2,1)S(1)} %lay.1.own_ref), channel_id=1, source_target_pairs={{128,8},{129,9},{130,10},{131,11},{132,12},{133,13},{134,14},{135,... | collective-permute-start | bytes 344072 | tf_op jit(solution)/shard_map/ppermute | solution.py:47
  3.2 12.9 %collective-permute-start.3 = (bf16[64,896]{1,0:T(8,128)(2,1)S(1)}, bf16[64,896]{1,0:T(8,128)(2,1)S(1)}, u32[]{:S(2)}, u32[]{:S(2)}) collective-permute-start(bf16[64,896]{1,0:T(8,128)(2,1)S(1)} %lay.1.own_ref), channel_id=1, source_target_pairs={{0,8},{1,9},{2,10},{3,11},{4,12},{5,13},{6,14},{7,15},{8,0},{9,1},... | collective-permute-start | bytes 344072 | tf_op jit(solution)/shard_map/ppermute | solution.py:37
  3.2 12.9 %collective-permute-start.2 = (bf16[64,896]{1,0:T(8,128)(2,1)S(1)}, bf16[64,896]{1,0:T(8,128)(2,1)S(1)}, u32[]{:S(2)}, u32[]{:S(2)}) collective-permute-start(bf16[64,896]{1,0:T(8,128)(2,1)S(1)} %lay.1.own_ref), channel_id=1, source_target_pairs={{0,128},{64,192},{128,0},{192,64},{1,129},{65,193},{129,1},{193,65... | collective-permute-start | bytes 344072 | tf_op jit(solution)/shard_map/ppermute | solution.py:41
  5.7 1.7 %collective-permute-start = (s32[1]{0:T(128)}, s32[1]{0:T(128)}, u32[]{:S(2)}, u32[]{:S(2)}) collective-permute-start(s32[1]{0:T(128)} %param.6), channel_id=1, source_target_pairs={{0,64},{64,0},{128,192},{192,128},{1,65},{65,1},{129,193},{193,129... | collective-permute-start | bytes 20 | tf_op jit(solution)/shard_map/ppermute | solution.py:41
  5.7 5.1 %collective-permute-start.1 = (s32[1]{0:T(128)}, s32[1]{0:T(128)}, u32[]{:S(2)}, u32[]{:S(2)}) collective-permute-start(s32[1]{0:T(128)} %param.6), channel_id=1, source_target_pairs={{0,128},{64,192},{128,0},{192,64},{1,129},{65,193},{129,1},{193,65... | collective-permute-start | bytes 20 | tf_op jit(solution)/shard_map/ppermute | solution.py:41
  10.9 0.7 copy-start
  16.9 27.6 %all-to-all-start = ((bf16[8,3,64,512]{3,2,1,0:T(8,128)(2,1)}), bf16[8,3,64,512]{3,2,1,0:T(8,128)(2,1)S(1)}, u32[]{:S(2)}, u32[]{:S(2)}) async-start(bf16[8,3,64,512]{3,2,1,0:T(8,128)(2,1)} %pack.1), calls=%async_computation | async-start | bytes 3145728 | tf_op jit(solution)/shard_map/all_to_all | solution.py:319
  22.8 29.7 %collective-permute-start.6 = (bf16[4,64,896]{2,1,0:T(8,128)(2,1)S(1)}, bf16[4,64,896]{2,1,0:T(8,128)(2,1)S(1)}, u32[]{:S(2)}, u32[]{:S(2)}) collective-permute-start(bf16[4,64,896]{2,1,0:T(8,128)(2,1)S(1)} %get-tuple-element.27.refs_0_), channel_id=1, source_target_pairs={{0,48},{1,49},{2,50},{3,51},{4,52},{5,53},{6,54},{7,55},{8,56},{9,... | collective-permute-start | bytes 1376264 | tf_op jit(solution)/shard_map/ppermute | solution.py:37
  25.5 27.0 %collective-permute-start.5 = (bf16[4,64,896]{2,1,0:T(8,128)(2,1)S(1)}, bf16[4,64,896]{2,1,0:T(8,128)(2,1)S(1)}, u32[]{:S(2)}, u32[]{:S(2)}) collective-permute-start(bf16[4,64,896]{2,1,0:T(8,128)(2,1)S(1)} %get-tuple-element.27.refs_0_), channel_id=1, source_target_pairs={{0,16},{1,17},{2,18},{3,19},{4,20},{5,21},{6,22},{7,23},{8,24},{9,... | collective-permute-start | bytes 1376264 | tf_op jit(solution)/shard_map/ppermute | solution.py:37
  25.5 19.8 %collective-permute-start.8 = (bf16[2,64,896]{2,1,0:T(8,128)(2,1)}, bf16[2,64,896]{2,1,0:T(8,128)(2,1)}, u32[]{:S(2)}, u32[]{:S(2)}) collective-permute-start(bf16[2,64,896]{2,1,0:T(8,128)(2,1)} %get-tuple-element.28.refs_5_), channel_id=1, source_target_pairs={{0,7},{1,0},{2,1},{3,2},{4,3},{5,4},{6,5},{7,6},{8,15},{9,8},{10,9... | collective-permute-start | bytes 688136 | tf_op jit(solution)/shard_map/ppermute | solution.py:37
  31.3 21.2 %collective-permute-start.7 = (bf16[2,64,896]{2,1,0:T(8,128)(2,1)}, bf16[2,64,896]{2,1,0:T(8,128)(2,1)}, u32[]{:S(2)}, u32[]{:S(2)}) collective-permute-start(bf16[2,64,896]{2,1,0:T(8,128)(2,1)} %get-tuple-element.28.refs_5_), channel_id=1, source_target_pairs={{0,1},{1,2},{2,3},{3,4},{4,5},{5,6},{6,7},{7,0},{8,9},{9,10},{10,1... | collective-permute-start | bytes 688136 | tf_op jit(solution)/shard_map/ppermute | solution.py:37
  45.3 32.4 %collective-permute-start.16 = (bf16[8,64,512]{2,1,0:T(8,128)(2,1)}, bf16[8,64,512]{2,1,0:T(8,128)(2,1)S(1)}, u32[]{:S(2)}, u32[]{:S(2)}) collective-permute-start(bf16[8,64,512]{2,1,0:T(8,128)(2,1)} %slice_bitcast_fusion), channel_id=1, source_target_pairs={{0,64},{64,0},{128,192},{192,128},{1,65},{65,1},{129,193},{193,129... | collective-permute-start | bytes 1572872 | tf_op jit(solution)/shard_map/ppermute | solution.py:41
  45.3 17.3 %collective-permute-start.11 = (bf16[2,64,896]{2,1,0:T(8,128)(2,1)}, bf16[2,64,896]{2,1,0:T(8,128)(2,1)}, u32[]{:S(2)}, u32[]{:S(2)}) collective-permute-start(bf16[2,64,896]{2,1,0:T(8,128)(2,1)} %get-tuple-element.28.refs_5_), channel_id=1, source_target_pairs={{0,4},{1,5},{2,6},{3,7},{4,0},{5,1},{6,2},{7,3},{8,12},{9,13},{10,... | collective-permute-start | bytes 688136 | tf_op jit(solution)/shard_map/ppermute | solution.py:37
  52.5 15.8 %collective-permute-start.12 = (bf16[2,64,896]{2,1,0:T(8,128)(2,1)}, bf16[2,64,896]{2,1,0:T(8,128)(2,1)}, u32[]{:S(2)}, u32[]{:S(2)}) collective-permute-start(bf16[2,64,896]{2,1,0:T(8,128)(2,1)} %collective-permute-done.7.refs_6_), channel_id=1, source_target_pairs={{0,1},{1,2},{2,3},{3,4},{4,5},{5,6},{6,7},{7,0},{8,9},{9,10},{10,1... | collective-permute-start | bytes 688136 | tf_op jit(solution)/shard_map/ppermute | solution.py:37
  54.3 15.6 %collective-permute-start.13 = (bf16[2,64,896]{2,1,0:T(8,128)(2,1)}, bf16[2,64,896]{2,1,0:T(8,128)(2,1)}, u32[]{:S(2)}, u32[]{:S(2)}) collective-permute-start(bf16[2,64,896]{2,1,0:T(8,128)(2,1)} %collective-permute-done.8.refs_7_), channel_id=1, source_target_pairs={{0,7},{1,0},{2,1},{3,2},{4,3},{5,4},{6,5},{7,6},{8,15},{9,8},{10,9... | collective-permute-start | bytes 688136 | tf_op jit(solution)/shard_map/ppermute | solution.py:37
  59.7 12.8 %collective-permute-start.10 = (bf16[2,64,896]{2,1,0:T(8,128)(2,1)}, bf16[2,64,896]{2,1,0:T(8,128)(2,1)}, u32[]{:S(2)}, u32[]{:S(2)}) collective-permute-start(bf16[2,64,896]{2,1,0:T(8,128)(2,1)} %slice.22), channel_id=1, source_target_pairs={{0,48},{1,49},{2,50},{3,51},{4,52},{5,53},{6,54},{7,55},{8,56},{9,... | collective-permute-start | bytes 688136 | tf_op jit(solution)/shard_map/ppermute | solution.py:37
  62.6 9.9 %collective-permute-start.9 = (bf16[2,64,896]{2,1,0:T(8,128)(2,1)}, bf16[2,64,896]{2,1,0:T(8,128)(2,1)}, u32[]{:S(2)}, u32[]{:S(2)}) collective-permute-start(bf16[2,64,896]{2,1,0:T(8,128)(2,1)} %slice.21), channel_id=1, source_target_pairs={{0,16},{1,17},{2,18},{3,19},{4,20},{5,21},{6,22},{7,23},{8,24},{9,... | collective-permute-start | bytes 688136 | tf_op jit(solution)/shard_map/ppermute | solution.py:37
  68.3 9.1 %collective-permute-start.14 = (bf16[2,64,896]{2,1,0:T(8,128)(2,1)}, bf16[2,64,896]{2,1,0:T(8,128)(2,1)}, u32[]{:S(2)}, u32[]{:S(2)}) collective-permute-start(bf16[2,64,896]{2,1,0:T(8,128)(2,1)} %collective-permute-done.12.refs_9_), channel_id=1, source_target_pairs={{0,1},{1,2},{2,3},{3,4},{4,5},{5,6},{6,7},{7,0},{8,9},{9,10},{10,1... | collective-permute-start | bytes 688136 | tf_op jit(solution)/shard_map/ppermute | solution.py:37
  69.9 7.7 %collective-permute-start.15 = (bf16[2,64,896]{2,1,0:T(8,128)(2,1)}, bf16[2,64,896]{2,1,0:T(8,128)(2,1)}, u32[]{:S(2)}, u32[]{:S(2)}) collective-permute-start(bf16[2,64,896]{2,1,0:T(8,128)(2,1)} %collective-permute-done.13.refs_10_), channel_id=1, source_target_pairs={{0,7},{1,0},{2,1},{3,2},{4,3},{5,4},{6,5},{7,6},{8,15},{9,8},{10,9... | collective-permute-start | bytes 688136 | tf_op jit(solution)/shard_map/ppermute | solution.py:37
  83.0 2.7 %collective-permute-start.17 = (bf16[512,1024]{1,0:T(8,128)(2,1)S(1)}, bf16[512,1024]{1,0:T(8,128)(2,1)S(1)}, u32[]{:S(2)}, u32[]{:S(2)}) collective-permute-start(bf16[512,1024]{1,0:T(8,128)(2,1)S(1)} %get-tuple-element.34), channel_id=1, source_target_pairs={{0,64},{64,0},{128,192},{192,128},{1,65},{65,1},{129,193},{193,129... | collective-permute-start | bytes 3145736 | tf_op jit(solution)/shard_map/ppermute | solution.py:41
  108.2 14.7 %all-to-all-start.2 = ((f32[4,8,896]{2,1,0:T(8,128)}), f32[4,8,896]{2,1,0:T(8,128)S(1)}, u32[]{:S(2)}, u32[]{:S(2)}) async-start(f32[4,8,896]{2,1,0:T(8,128)} %convert_reduce_fusion), calls=%async_computation.2 | async-start | bytes 229376 | tf_op jit(solution)/shard_map/all_to_all | solution.py:292

commit v16 on v11

--- a/solution.py
+++ b/solution.py
@@ -215,6 +215,11 @@
     )(near(rows), near(cols))
 
 
+def place_of(d):
+    yx, z = d // NZ, d % NZ
+    return (yx * 2 + z % 2) * (NZ // 2) + z // 2
+
+
 def project_body(m_ref, left_ref, right_ref, out_ref, x_ref, part_ref, sem):
     y = dot(m_ref[...], right_ref[...], 1, 0)
     high = y.astype(jnp.bfloat16)
@@ -228,7 +233,7 @@
         x_ref[at, :] = -(dot(left_ref[at, :], high, 1, 0) + dot(left_ref[at, :], low, 1, 0))
         some = GROUPS * NZ // 2
         for d in range(part * some, (part + 1) * some):
-            part_ref[d] = x_ref[pl.ds(27 * d // 4, 8), :].astype(jnp.bfloat16)
+            part_ref[place_of(d)] = x_ref[pl.ds(27 * d // 4, 8), :].astype(jnp.bfloat16)
         chosen = pl.ds(part * some, some)
         copy = pltpu.make_async_copy(part_ref.at[chosen], out_ref.at[chosen], sem.at[part])
         copy.start()
@@ -254,30 +259,31 @@
     )(near(m), near(left), near(right))
 
 
-def bundle_body(own_ref, far_ref, own_side, far_side, four_ref, both_ref):
-    for i, ref in enumerate((own_ref, far_ref, own_side, far_side)):
-        four_ref[i] = ref[...]
-    both_ref[0] = own_ref[...]
-    both_ref[1] = far_ref[...]
+def bundle_body(*refs):
+    *blocks, out_ref = refs
+    for i, ref in enumerate(blocks):
+        out_ref[i] = ref[...]
 
 
 def bundle(*blocks):
     return pl.pallas_call(
         bundle_body,
-        out_shape=[
-            pltpu.VMEM((4, SLAB, LANES), jnp.bfloat16),
-            jax.ShapeDtypeStruct((2, SLAB, LANES), jnp.bfloat16),
-        ],
-        in_specs=[IN_VMEM] * 4,
-        out_specs=[IN_VMEM] * 2,
+        out_shape=jax.ShapeDtypeStruct((len(blocks), SLAB, LANES), jnp.bfloat16),
+        in_specs=[IN_VMEM] * len(blocks),
+        out_specs=IN_VMEM,
         compiler_params=PARAMS,
         name="bundle",
     )(*map(near, blocks))
 
 
 def reduce_windows(windows):
-    parts = lax.all_to_all(windows, "band", 0, 0)
-    total = jnp.sum(parts.astype(jnp.float32), axis=0)
+    quads = NZ // 2
+    wide = [[g * NZ + 2 * j + i for g in range(GROUPS) for i in range(2)] for j in range(quads)]
+    deep = [[g * NZ + 2 * j + i for j in range(quads)] for g in range(GROUPS) for i in range(2)]
+    parts = windows.reshape(2 * GROUPS, quads, 8, LANES)
+    parts = lax.all_to_all(parts, "band", 0, 0, axis_index_groups=wide)
+    parts = jnp.sum(parts.astype(jnp.float32), axis=0)
+    total = jnp.sum(lax.all_to_all(parts, "band", 0, 0, axis_index_groups=deep), axis=0)
     real = jnp.concatenate([total[:, :WHOLE], total[:, TAIL : TAIL + REST]], axis=1)
     imag = jnp.concatenate([total[:, WHOLE:TAIL], total[:, TAIL + 64 : TAIL + 64 + REST]], axis=1)
     return jnp.stack([real, imag])
@@ -290,20 +296,13 @@
     odd = (group % 2).reshape(1)
 
     own = lay(orbitals)
-    first = (
-        swap_groups(pair_kdiff, 1),
-        swap_groups(pair_kdiff, 2),
-        swap_groups(own, 2),
-        shift(own, 0, 1, 0),
-        other_side(own),
-    )
-    diff_core, diff_far = first[:2]
-    far, own_side, far_side = lax.optimization_barrier(first)[2:]
+    first = swap_groups(pair_kdiff, 1), swap_groups(pair_kdiff, 2), swap_groups(own, 2)
+    diff_core, diff_far, far = lax.optimization_barrier(first)
 
     over_yx = [[g * NZ + z for g in range(GROUPS)] for z in range(NZ)]
     over_z = [[g * NZ + z for z in range(NZ)] for g in range(GROUPS)]
-    four, both = bundle(own, far, own_side, far_side)
-    gathered = lax.all_gather(both, "band", axis_index_groups=over_z)
+    gathered = lax.all_gather(bundle(own, far), "band", axis_index_groups=over_z)
+    four = bundle(own, far, shift(own, 0, 1, 0), other_side(own))
     up, down = shift(four, 1, 0, 0), shift(four, -1, 0, 0)
 
     shared, single = pack(odd, pair_kdiff, diff_core, diff_far, stored_kernel_index, kernels)

time: 122 us -> 120 us (0.984)
  blocking collectives: 0 us -> 18.6 us
  waiting for transfers between devices: 53.6 us -> 37.9 us
  starting transfers between devices: 33.7 us -> 30 us
    all_to_all x0 -> x1, blocking collectives: none -> 18.6 us  [reduce_windows(): parts = lax.all_to_all(parts, 'band', 0, 0, axis_index_groups=wide)]
    all_to_all x1, waiting for transfers between devices: 25.5 us -> 8.9 us  [reduce_windows(): lax.all_to_all(parts, 'band', 0, 0, axis_index_groups=deep)]
    all_to_all x1, starting transfers between devices: 11.2 us -> 7.57 us  [reduce_windows(): lax.all_to_all(parts, 'band', 0, 0, axis_index_groups=deep)]
    ppermute x1, waiting for transfers between devices: 0.01 us -> 3.26 us  [other_side(): return lax.ppermute(block, ('kgrp', 'band'), both)]
    ppermute x5, waiting for transfers between devices: 6.31 us -> 5.09 us  [swap_groups(): return lax.ppermute(block, 'kgrp', [(k, k ^ bit) for k in range(4)])]
  transfers between devices with their start and end apart: 15 -> 15, of which waited for: 8 -> 9; matrix products, arithmetic and copies ran while one was open for 1% -> 1% of each run, Pallas kernels for 4% -> 4%
where the time goes in v16:
time: 120 us
  waiting for transfers between devices  37.9 us (32%)
  starting transfers between devices  30 us (25%)
  blocking collectives  18.6 us (16%)
  Pallas kernels  15.8 us (13%)
  between operations  14.1 us (12%)
  local copies, waits for them, and re-layouts  1.76 us (1%)
  other arithmetic  1.52 us (1%)
    all_to_all x1, blocking collectives, reduce_windows(): parts = lax.all_to_all(parts, 'band', 0, 0, axis_index_groups=wide)  18.6 us
    ppermute x5, waiting for transfers between devices, shift(): return lax.ppermute(block, 'band', band_route(dy, dx, dz))  14.6 us
    all_to_all x1, waiting for transfers between devices, reduce_windows(): lax.all_to_all(parts, 'band', 0, 0, axis_index_groups=deep)  8.9 us
    all_to_all x1, starting transfers between devices, reduce_windows(): lax.all_to_all(parts, 'band', 0, 0, axis_index_groups=deep)  7.57 us
    all_to_all x1, waiting for transfers between devices, on_device(): mine = lax.all_to_all(shared, 'band', 0, 0, axis_index_groups=over_yx)  6.06 us
    all_to_all x1, starting transfers between devices, on_device(): mine = lax.all_to_all(shared, 'band', 0, 0, axis_index_groups=over_yx)  5.98 us
    ppermute x5, starting transfers between devices, shift(): return lax.ppermute(block, 'band', band_route(dy, dx, dz))  5.81 us
    ppermute x5, waiting for transfers between devices, swap_groups(): return lax.ppermute(block, 'kgrp', [(k, k ^ bit) for k in range(4)])  5.09 us
  transfers between devices with their start and end apart: 15, of which 9 were waited for; matrix products, arithmetic and copies ran while one was open for 1% of the time, Pallas kernels for 4%

profile of v16, /device:TPU:6, one launch (start us, length us, event | category | flops | bytes accessed | tf_op | source)
XLA Modules:
  0.0 119.7 jit_solution(13687493645300240789)
XLA Ops:
  6.5 1.0 lay.1.refs_0_
  7.5 1.4 %collective-permute-start.2 = (bf16[64,896]{1,0:T(8,128)(2,1)S(1)}, bf16[64,896]{1,0:T(8,128)(2,1)S(1)}, u32[]{:S(2)}, u32[]{:S(2)}) collective-permute-start(bf16[64,896]{1,0:T(8,128)(2,1)S(1)} %lay.1.refs_0_), channel_id=1, source_target_pairs={{0,128},{64,192},{128,0},{192,64},{1,129},{65,193},{129,1},{193,65... | collective-permute-start | bytes 344072 | tf_op jit(solution)/shard_map/ppermute | solution.py:40
  9.0 2.1 %collective-permute-start.1 = (s32[1]{0:T(128)}, s32[1]{0:T(128)}, u32[]{:S(2)}, u32[]{:S(2)}) collective-permute-start(s32[1]{0:T(128)} %param.6), channel_id=1, source_target_pairs={{0,128},{64,192},{128,0},{192,64},{1,129},{65,193},{129,1},{193,65... | collective-permute-start | bytes 20 | tf_op jit(solution)/shard_map/ppermute | solution.py:40
  11.1 3.0 %collective-permute-done.1.far_ref = s32[1]{0:T(128)} collective-permute-done((s32[1]{0:T(128)}, s32[1]{0:T(128)}, u32[]{:S(2)}, u32[]{:S(2)}) %collective-permute-start.1) | collective-permute-done | bytes 36 | tf_op jit(solution)/shard_map/ppermute | solution.py:40
  14.1 0.7 bundle.3
  14.8 2.2 %collective-permute-start.4 = (bf16[64,896]{1,0:T(8,128)(2,1)S(1)}, bf16[64,896]{1,0:T(8,128)(2,1)S(1)}, u32[]{:S(2)}, u32[]{:S(2)}) collective-permute-start(bf16[64,896]{1,0:T(8,128)(2,1)S(1)} %lay.1.refs_0_), channel_id=1, source_target_pairs={{128,8},{129,9},{130,10},{131,11},{132,12},{133,13},{134,14},{135,... | collective-permute-start | bytes 344072 | tf_op jit(solution)/shard_map/ppermute | solution.py:46
  17.7 3.3 %collective-permute-done.4.refs_3_ = bf16[64,896]{1,0:T(8,128)(2,1)S(1)} collective-permute-done((bf16[64,896]{1,0:T(8,128)(2,1)S(1)}, bf16[64,896]{1,0:T(8,128)(2,1)S(1)}, u32[]{:S(2)}, u32[]{:S(2)}) %collective-permute-start.4) | collective-permute-done | bytes 114720 | tf_op jit(solution)/shard_map/ppermute | solution.py:46
  21.0 0.9 collective-permute-done.3.refs_2_
  21.9 3.1 %collective-permute-start.6 = (bf16[4,64,896]{2,1,0:T(8,128)(2,1)S(1)}, bf16[4,64,896]{2,1,0:T(8,128)(2,1)S(1)}, u32[]{:S(2)}, u32[]{:S(2)}) collective-permute-start(bf16[4,64,896]{2,1,0:T(8,128)(2,1)S(1)} %bundle.2.refs_0_), channel_id=1, source_target_pairs={{0,48},{1,49},{2,50},{3,51},{4,52},{5,53},{6,54},{7,55},{8,56},{9,... | collective-permute-start | bytes 1376264 | tf_op jit(solution)/shard_map/ppermute | solution.py:36
  25.0 4.5 %pack.1 = (bf16[8,64,512]{2,1,0:T(8,128)(2,1)}, bf16[8,2,64,512]{3,2,1,0:T(8,128)(2,1)}) custom-call(s32[1]{0:T(128)} %bitcast.8.odd_ref, s32[1]{0:T(128)S(6)} %copy.5.own_ref, s32[1]{0:T(128)} %collective-permute-done.core_ref, s32[1]{0:T(128)} %collective-permute-done.1.far_ref, s32[8]{0:T(128)S(1)} %copy-done, bf16[4,2,64,4096]{3,2,1,0:T(8,128)(2,1)} %kernels_ref.1), custom_call_target="tpu_custom_call" | custom-call | tf_op jit(solution)/shard_map/pack/pallas_call | solution.py:113
  29.4 6.0 %all-to-all-start = ((bf16[8,64,512]{2,1,0:T(8,128)(2,1)}), bf16[8,64,512]{2,1,0:T(8,128)(2,1)S(1)}, u32[]{:S(2)}, u32[]{:S(2)}) async-start(bf16[8,64,512]{2,1,0:T(8,128)(2,1)} %get-tuple-element.24), calls=%async_computation | async-start | bytes 1048576 | tf_op jit(solution)/shard_map/all_to_all | solution.py:309
  35.4 1.5 %collective-permute-done.5.refs_1_ = bf16[4,64,896]{2,1,0:T(8,128)(2,1)S(1)} collective-permute-done((bf16[4,64,896]{2,1,0:T(8,128)(2,1)S(1)}, bf16[4,64,896]{2,1,0:T(8,128)(2,1)S(1)}, u32[]{:S(2)}, u32[]{:S(2)}) %collective-permute-start.5) | collective-permute-done | bytes 458784 | tf_op jit(solution)/shard_map/ppermute | solution.py:36
  36.9 6.1 %all-to-all-done.refs_6_ = bf16[8,64,512]{2,1,0:T(8,128)(2,1)S(1)} async-done(((bf16[8,64,512]{2,1,0:T(8,128)(2,1)}), bf16[8,64,512]{2,1,0:T(8,128)(2,1)S(1)}, u32[]{:S(2)}, u32[]{:S(2)}) %all-to-all-start) | async-done | bytes 524320 | tf_op jit(solution)/shard_map/all_to_all | solution.py:309
  43.0 4.6 %all-to-all-start.1 = ((bf16[8,2,64,512]{3,2,1,0:T(8,128)(2,1)}), bf16[8,2,64,512]{3,2,1,0:T(8,128)(2,1)S(1)}, u32[]{:S(2)}, u32[]{:S(2)}) async-start(bf16[8,2,64,512]{3,2,1,0:T(8,128)(2,1)} %get-tuple-element.25), calls=%async_computation.1 | async-start | bytes 2097152 | tf_op jit(solution)/shard_map/all_to_all | solution.py:313
  47.6 0.7 slice.18
  48.3 0.7 slice.19
  49.0 2.7 %collective-permute-start.8 = (bf16[2,64,896]{2,1,0:T(8,128)(2,1)}, bf16[2,64,896]{2,1,0:T(8,128)(2,1)}, u32[]{:S(2)}, u32[]{:S(2)}) collective-permute-start(bf16[2,64,896]{2,1,0:T(8,128)(2,1)} %slice.19), channel_id=1, source_target_pairs={{0,48},{1,49},{2,50},{3,51},{4,52},{5,53},{6,54},{7,55},{8,56},{9,... | collective-permute-start | bytes 688136 | tf_op jit(solution)/shard_map/ppermute | solution.py:36
  51.7 0.1 stack.44.place_ref
  51.8 10.8 %collective-permute-done.8.refs_3_ = bf16[2,64,896]{2,1,0:T(8,128)(2,1)} collective-permute-done((bf16[2,64,896]{2,1,0:T(8,128)(2,1)}, bf16[2,64,896]{2,1,0:T(8,128)(2,1)}, u32[]{:S(2)}, u32[]{:S(2)}) %collective-permute-start.8) | collective-permute-done | bytes 229408 | tf_op jit(solution)/shard_map/ppermute | solution.py:36
  62.6 1.4 %collective-permute-done.7.refs_2_ = bf16[2,64,896]{2,1,0:T(8,128)(2,1)} collective-permute-done((bf16[2,64,896]{2,1,0:T(8,128)(2,1)}, bf16[2,64,896]{2,1,0:T(8,128)(2,1)}, u32[]{:S(2)}, u32[]{:S(2)}) %collective-permute-start.7) | collective-permute-done | bytes 229408 | tf_op jit(solution)/shard_map/ppermute | solution.py:36
  64.0 5.0 %mix.1 = (bf16[512,1024]{1,0:T(8,128)(2,1)S(1)}, bf16[512,896]{1,0:T(8,128)(2,1)S(1)}, bf16[512,896]{1,0:T(8,128)(2,1)S(1)}) custom-call(s32[8]{0:T(128)S(1)} %stack.44.place_ref, s32[1]{0:T(128)} %bitcast.8.odd_ref, bf16[4,64,896]{2,1,0:T(8,128)(2,1)S(1)} %bundle.2.refs_0_, bf16[4,64,896]{2,1,0:T(8,128)(2,1)S(1)} %collective-permute-done.5.refs_1_, ...), custom_call_target="tpu_custom_call" | custom-call | tf_op jit(solution)/shard_map/mix/pallas_call | solution.py:181
  69.0 0.3 collective-permute-start.10
  69.3 0.6 prepare.1
  69.9 2.1 %collective-permute-done.10.m_ref = bf16[512,1024]{1,0:T(8,128)(2,1)S(1)} collective-permute-done((bf16[512,1024]{1,0:T(8,128)(2,1)S(1)}, bf16[512,1024]{1,0:T(8,128)(2,1)S(1)}, u32[]{:S(2)}, u32[]{:S(2)}) %collective-permute-start.10) | collective-permute-done | bytes 1048608 | tf_op jit(solution)/shard_map/ppermute | solution.py:40
  72.0 4.0 %project.1 = bf16[64,8,896]{2,1,0:T(8,128)(2,1)S(1)} custom-call(bf16[512,1024]{1,0:T(8,128)(2,1)S(1)} %collective-permute-done.10.m_ref, bf16[432,1024]{1,0:T(8,128)(2,1)S(1)} %get-tuple-element.29.left_ref, bf16[1024,896]{1,0:T(8,128)(2,1)S(1)} %get-tuple-element.30.right_ref), custom_call_target="tpu_custom_call" | custom-call | tf_op jit(solution)/shard_map/project/pallas_call | solution.py:247
  76.0 18.6 %all_to_all.20 = bf16[16,4,8,896]{3,2,1,0:T(8,128)(2,1)S(1)} all-to-all(bf16[16,4,8,896]{3,2,1,0:T(8,128)(2,1)S(1)} %bitcast.13), channel_id=1, replica_groups={{0,1,8,9,16,17,24,25,32,33,40,41,48,49,56,57},{2,3,10,11,18,19,26,27,34..., dimensions={0} | all-to-all | bytes 1835008 | tf_op jit(solution)/shard_map/all_to_all | solution.py:284
  94.6 0.8 convert_reduce_fusion
  95.4 7.6 %all-to-all-start.3 = ((f32[4,8,896]{2,1,0:T(8,128)}), f32[4,8,896]{2,1,0:T(8,128)S(1)}, u32[]{:S(2)}, u32[]{:S(2)}) async-start(f32[4,8,896]{2,1,0:T(8,128)} %convert_reduce_fusion), calls=%async_computation.3 | async-start | bytes 229376 | tf_op jit(solution)/shard_map/all_to_all | solution.py:286
  103.0 8.9 %all-to-all-done.3 = f32[4,8,896]{2,1,0:T(8,128)S(1)} async-done(((f32[4,8,896]{2,1,0:T(8,128)}), f32[4,8,896]{2,1,0:T(8,128)S(1)}, u32[]{:S(2)}, u32[]{:S(2)}) %all-to-all-start.3) | async-done | bytes 114720 | tf_op jit(solution)/shard_map/all_to_all | solution.py:286
  112.0 0.1 stack.45
  112.1 0.1 stack.46
  112.2 0.7 fusion.1
  (20 shorter events, 0.2 us)
Async XLA Ops:
  6.5 18.4 %copy-start = (s32[8]{0:T(128)S(1)}, s32[8]{0:T(128)}, u32[]{:S(2)}) copy-start(s32[8]{0:T(128)} %stored_ref.1) | copy-start | bytes 100
  6.5 57.5 %all-gather.3.cloned.1.call-start = ((), (), s32[]{:S(2)}) async-start(), calls=%async_computation.4 | async-start | bytes 2064384 | tf_op jit(solution)/shard_map/all_gather | solution.py:304
  7.5 6.6 %collective-permute-start.2 = (bf16[64,896]{1,0:T(8,128)(2,1)S(1)}, bf16[64,896]{1,0:T(8,128)(2,1)S(1)}, u32[]{:S(2)}, u32[]{:S(2)}) collective-permute-start(bf16[64,896]{1,0:T(8,128)(2,1)S(1)} %lay.1.refs_0_), channel_id=1, source_target_pairs={{0,128},{64,192},{128,0},{192,64},{1,129},{65,193},{129,1},{193,65... | collective-permute-start | bytes 344072 | tf_op jit(solution)/shard_map/ppermute | solution.py:40
  9.0 2.1 %collective-permute-start = (s32[1]{0:T(128)}, s32[1]{0:T(128)}, u32[]{:S(2)}, u32[]{:S(2)}) collective-permute-start(s32[1]{0:T(128)} %param.6), channel_id=1, source_target_pairs={{0,64},{64,0},{128,192},{192,128},{1,65},{65,1},{129,193},{193,129... | collective-permute-start | bytes 20 | tf_op jit(solution)/shard_map/ppermute | solution.py:40
  9.0 5.1 %collective-permute-start.1 = (s32[1]{0:T(128)}, s32[1]{0:T(128)}, u32[]{:S(2)}, u32[]{:S(2)}) collective-permute-start(s32[1]{0:T(128)} %param.6), channel_id=1, source_target_pairs={{0,128},{64,192},{128,0},{192,64},{1,129},{65,193},{129,1},{193,65... | collective-permute-start | bytes 20 | tf_op jit(solution)/shard_map/ppermute | solution.py:40
  14.8 6.1 %collective-permute-start.4 = (bf16[64,896]{1,0:T(8,128)(2,1)S(1)}, bf16[64,896]{1,0:T(8,128)(2,1)S(1)}, u32[]{:S(2)}, u32[]{:S(2)}) collective-permute-start(bf16[64,896]{1,0:T(8,128)(2,1)S(1)} %lay.1.refs_0_), channel_id=1, source_target_pairs={{128,8},{129,9},{130,10},{131,11},{132,12},{133,13},{134,14},{135,... | collective-permute-start | bytes 344072 | tf_op jit(solution)/shard_map/ppermute | solution.py:46
  17.0 4.8 %collective-permute-start.3 = (bf16[64,896]{1,0:T(8,128)(2,1)S(1)}, bf16[64,896]{1,0:T(8,128)(2,1)S(1)}, u32[]{:S(2)}, u32[]{:S(2)}) collective-permute-start(bf16[64,896]{1,0:T(8,128)(2,1)S(1)} %lay.1.refs_0_), channel_id=1, source_target_pairs={{0,8},{1,9},{2,10},{3,11},{4,12},{5,13},{6,14},{7,15},{8,0},{9,1},... | collective-permute-start | bytes 344072 | tf_op jit(solution)/shard_map/ppermute | solution.py:36
  21.9 13.6 %collective-permute-start.6 = (bf16[4,64,896]{2,1,0:T(8,128)(2,1)S(1)}, bf16[4,64,896]{2,1,0:T(8,128)(2,1)S(1)}, u32[]{:S(2)}, u32[]{:S(2)}) collective-permute-start(bf16[4,64,896]{2,1,0:T(8,128)(2,1)S(1)} %bundle.2.refs_0_), channel_id=1, source_target_pairs={{0,48},{1,49},{2,50},{3,51},{4,52},{5,53},{6,54},{7,55},{8,56},{9,... | collective-permute-start | bytes 1376264 | tf_op jit(solution)/shard_map/ppermute | solution.py:36
  25.0 11.9 %collective-permute-start.5 = (bf16[4,64,896]{2,1,0:T(8,128)(2,1)S(1)}, bf16[4,64,896]{2,1,0:T(8,128)(2,1)S(1)}, u32[]{:S(2)}, u32[]{:S(2)}) collective-permute-start(bf16[4,64,896]{2,1,0:T(8,128)(2,1)S(1)} %bundle.2.refs_0_), channel_id=1, source_target_pairs={{0,16},{1,17},{2,18},{3,19},{4,20},{5,21},{6,22},{7,23},{8,24},{9,... | collective-permute-start | bytes 1376264 | tf_op jit(solution)/shard_map/ppermute | solution.py:36
  29.4 13.5 %all-to-all-start = ((bf16[8,64,512]{2,1,0:T(8,128)(2,1)}), bf16[8,64,512]{2,1,0:T(8,128)(2,1)S(1)}, u32[]{:S(2)}, u32[]{:S(2)}) async-start(bf16[8,64,512]{2,1,0:T(8,128)(2,1)} %get-tuple-element.24), calls=%async_computation | async-start | bytes 1048576 | tf_op jit(solution)/shard_map/all_to_all | solution.py:309
  43.0 21.1 %all-to-all-start.1 = ((bf16[8,2,64,512]{3,2,1,0:T(8,128)(2,1)}), bf16[8,2,64,512]{3,2,1,0:T(8,128)(2,1)S(1)}, u32[]{:S(2)}, u32[]{:S(2)}) async-start(bf16[8,2,64,512]{3,2,1,0:T(8,128)(2,1)} %get-tuple-element.25), calls=%async_computation.1 | async-start | bytes 2097152 | tf_op jit(solution)/shard_map/all_to_all | solution.py:313
  47.6 16.4 %collective-permute-start.9 = (bf16[8,64,512]{2,1,0:T(8,128)(2,1)S(1)}, bf16[8,64,512]{2,1,0:T(8,128)(2,1)S(1)}, u32[]{:S(2)}, u32[]{:S(2)}) collective-permute-start(bf16[8,64,512]{2,1,0:T(8,128)(2,1)S(1)} %all-to-all-done.refs_6_), channel_id=1, source_target_pairs={{0,64},{64,0},{128,192},{192,128},{1,65},{65,1},{129,193},{193,129... | collective-permute-start | bytes 1572872 | tf_op jit(solution)/shard_map/ppermute | solution.py:40
  49.0 13.6 %collective-permute-start.8 = (bf16[2,64,896]{2,1,0:T(8,128)(2,1)}, bf16[2,64,896]{2,1,0:T(8,128)(2,1)}, u32[]{:S(2)}, u32[]{:S(2)}) collective-permute-start(bf16[2,64,896]{2,1,0:T(8,128)(2,1)} %slice.19), channel_id=1, source_target_pairs={{0,48},{1,49},{2,50},{3,51},{4,52},{5,53},{6,54},{7,55},{8,56},{9,... | collective-permute-start | bytes 688136 | tf_op jit(solution)/shard_map/ppermute | solution.py:36
  51.7 12.3 %collective-permute-start.7 = (bf16[2,64,896]{2,1,0:T(8,128)(2,1)}, bf16[2,64,896]{2,1,0:T(8,128)(2,1)}, u32[]{:S(2)}, u32[]{:S(2)}) collective-permute-start(bf16[2,64,896]{2,1,0:T(8,128)(2,1)} %slice.18), channel_id=1, source_target_pairs={{0,16},{1,17},{2,18},{3,19},{4,20},{5,21},{6,22},{7,23},{8,24},{9,... | collective-permute-start | bytes 688136 | tf_op jit(solution)/shard_map/ppermute | solution.py:36
  69.0 2.9 %collective-permute-start.10 = (bf16[512,1024]{1,0:T(8,128)(2,1)S(1)}, bf16[512,1024]{1,0:T(8,128)(2,1)S(1)}, u32[]{:S(2)}, u32[]{:S(2)}) collective-permute-start(bf16[512,1024]{1,0:T(8,128)(2,1)S(1)} %get-tuple-element.26), channel_id=1, source_target_pairs={{0,64},{64,0},{128,192},{192,128},{1,65},{65,1},{129,193},{193,129... | collective-permute-start | bytes 3145736 | tf_op jit(solution)/shard_map/ppermute | solution.py:40
  95.4 16.5 %all-to-all-start.3 = ((f32[4,8,896]{2,1,0:T(8,128)}), f32[4,8,896]{2,1,0:T(8,128)S(1)}, u32[]{:S(2)}, u32[]{:S(2)}) async-start(f32[4,8,896]{2,1,0:T(8,128)} %convert_reduce_fusion), calls=%async_computation.3 | async-start | bytes 229376 | tf_op jit(solution)/shard_map/all_to_all | solution.py:286
Sparse Core Ops, SparseCore 0:
  15.0 42.8 all-gather.2

commit v17 on v12

--- a/solution.py
+++ b/solution.py
@@ -320,20 +320,20 @@
     far, own_side, far_side = lax.optimization_barrier(first)[2:]
 
     over_yx = [[g * NZ + i for g in range(GROUPS)] for i in range(NZ)]
+    shared, single = pack(odd, pair_kdiff, diff_core, diff_far, stored_kernel_index, kernels)
+
     four, both = bundle(own, far, own_side, far_side)
-    cols, ahead, behind = [both], both, both
-    for _ in range(3):
+    steps = shift(four, 1, 0, 0), shift(four, -1, 0, 0), shift(both, 0, 0, 1), shift(both, 0, 0, -1)
+    up, down, ahead, behind, shared, single = lax.optimization_barrier((*steps, shared, single))
+    over = shift(up[:2], 1, 0, 0), shift(down[2:], -1, 0, 0)
+    mine = lax.all_to_all(shared, "band", 0, 0, axis_index_groups=over_yx)
+    half = swap_groups(mine, 1)
+    kern = lax.all_to_all(single, "band", 0, 0, axis_index_groups=over_yx)
+    cols = [both, ahead, behind]
+    for _ in range(2):
         ahead, behind = shift(ahead, 0, 0, 1), shift(behind, 0, 0, -1)
         cols += [ahead, behind]
     cols.append(shift(ahead, 0, 0, 1))
-    up, down = shift(four, 1, 0, 0), shift(four, -1, 0, 0)
-
-    shared, single = pack(odd, pair_kdiff, diff_core, diff_far, stored_kernel_index, kernels)
-    mine = lax.all_to_all(shared, "band", 0, 0, axis_index_groups=over_yx)
-    half = swap_groups(mine, 1)
-    single, up, down = lax.optimization_barrier((single, up, down))
-    over = shift(up[:2], 1, 0, 0), shift(down[2:], -1, 0, 0)
-    kern = lax.all_to_all(single, "band", 0, 0, axis_index_groups=over_yx)
 
     place = jnp.stack([(y - dy) % NY * NX + (x - dx) % NX for dy in range(NY) for dx in range(NX)])
     slots = jnp.stack([(z + i) % NZ for i in (0, -1, 1, -2, 2, -3, 3, -4)])

time: 116 us -> 117 us (level)
  blocking collectives: 19.3 us -> 32.3 us
  starting transfers between devices: 40.7 us -> 34.1 us
  waiting for transfers between devices: 33.7 us -> 28.9 us
    all_to_all x0 -> x1, blocking collectives: none -> 13 us  [on_device(): mine = lax.all_to_all(shared, 'band', 0, 0, axis_index_groups=over_yx)]
    all_to_all x1 -> x0, waiting for transfers between devices: 6.37 us -> none  [on_device(): mine = lax.all_to_all(shared, 'band', 0, 0, axis_index_groups=over_yx)]
    all_to_all x1 -> x0, starting transfers between devices: 5.98 us -> none  [on_device(): mine = lax.all_to_all(shared, 'band', 0, 0, axis_index_groups=over_yx)]
    ppermute x12, starting transfers between devices: 20.9 us -> 18.1 us  [shift(): return lax.ppermute(block, 'band', band_route(dy, dx, dz))]
    all_to_all x1, starting transfers between devices: 3.31 us -> 5.43 us  [reduce_windows(): lax.all_to_all(parts, 'band', 0, 0, axis_index_groups=deep)]
  transfers between devices with their start and end apart: 21 -> 20, of which waited for: 9 -> 9; matrix products, arithmetic and copies ran while one was open for 1% -> 1% of each run, Pallas kernels for 5% -> 4%
where the time goes in v17:
time: 117 us; the launch traced here: 116 us
  starting transfers between devices  34.1 us (29%)
  blocking collectives  32.3 us (28%)
  waiting for transfers between devices  28.9 us (25%)
  Pallas kernels  15.4 us (13%)
  local copies, waits for them, and re-layouts  3.2 us (3%)
  other arithmetic  1.52 us (1%)
    all_to_all x1, blocking collectives, reduce_windows(): parts = lax.all_to_all(parts, 'band', 0, 0, axis_index_groups=wide)  19.3 us
    ppermute x12, starting transfers between devices, shift(): return lax.ppermute(block, 'band', band_route(dy, dx, dz))  18.1 us
    ppermute x12, waiting for transfers between devices, shift(): return lax.ppermute(block, 'band', band_route(dy, dx, dz))  13.9 us
    all_to_all x1, blocking collectives, on_device(): mine = lax.all_to_all(shared, 'band', 0, 0, axis_index_groups=over_yx)  13 us
    all_to_all x1, waiting for transfers between devices, reduce_windows(): lax.all_to_all(parts, 'band', 0, 0, axis_index_groups=deep)  8.9 us
    ppermute x5, waiting for transfers between devices, swap_groups(): return lax.ppermute(block, 'kgrp', [(k, k ^ bit) for k in range(4)])  6.16 us
    all_to_all x1, starting transfers between devices, reduce_windows(): lax.all_to_all(parts, 'band', 0, 0, axis_index_groups=deep)  5.43 us
    pallas_call x1, Pallas kernels, mix(): pl.pallas_call(mix_body, out_shape=[pltpu.VMEM((BLOCK, 2 * BLOCK), jnp.bf...  5.31 us
  transfers between devices with their start and end apart: 20, of which 9 were waited for; matrix products, arithmetic and copies ran while one was open for 1% of the time, Pallas kernels for 4%

profile of v17, /device:TPU:6, one launch (start us, length us, event | category | flops | bytes accessed | tf_op | source)
XLA Modules:
  0.0 116.2 jit_solution(10118272487066775986)
XLA Ops:
  0.0 1.0 lay.1.own_ref
  1.0 2.3 %collective-permute-start.4 = (bf16[64,896]{1,0:T(8,128)(2,1)S(1)}, bf16[64,896]{1,0:T(8,128)(2,1)S(1)}, u32[]{:S(2)}, u32[]{:S(2)}) collective-permute-start(bf16[64,896]{1,0:T(8,128)(2,1)S(1)} %lay.1.own_ref), channel_id=1, source_target_pairs={{128,8},{129,9},{130,10},{131,11},{132,12},{133,13},{134,14},{135,... | collective-permute-start | bytes 344072 | tf_op jit(solution)/shard_map/ppermute | solution.py:47
  3.2 2.5 %collective-permute-start.2 = (bf16[64,896]{1,0:T(8,128)(2,1)S(1)}, bf16[64,896]{1,0:T(8,128)(2,1)S(1)}, u32[]{:S(2)}, u32[]{:S(2)}) collective-permute-start(bf16[64,896]{1,0:T(8,128)(2,1)S(1)} %lay.1.own_ref), channel_id=1, source_target_pairs={{0,128},{64,192},{128,0},{192,64},{1,129},{65,193},{129,1},{193,65... | collective-permute-start | bytes 344072 | tf_op jit(solution)/shard_map/ppermute | solution.py:41
  5.7 1.0 collective-permute-start.1
  6.8 0.3 collective-permute-done.core_ref
  7.1 3.7 %collective-permute-done.1.far_ref = s32[1]{0:T(128)} collective-permute-done((s32[1]{0:T(128)}, s32[1]{0:T(128)}, u32[]{:S(2)}, u32[]{:S(2)}) %collective-permute-start.1) | collective-permute-done | bytes 36 | tf_op jit(solution)/shard_map/ppermute | solution.py:41
  10.9 3.1 %collective-permute-start.6 = (bf16[4,64,896]{2,1,0:T(8,128)(2,1)S(1)}, bf16[4,64,896]{2,1,0:T(8,128)(2,1)S(1)}, u32[]{:S(2)}, u32[]{:S(2)}) collective-permute-start(bf16[4,64,896]{2,1,0:T(8,128)(2,1)S(1)} %get-tuple-element.26.refs_0_), channel_id=1, source_target_pairs={{0,48},{1,49},{2,50},{3,51},{4,52},{5,53},{6,54},{7,55},{8,56},{9,... | collective-permute-start | bytes 1376264 | tf_op jit(solution)/shard_map/ppermute | solution.py:37
  14.0 5.9 %collective-permute-start.8 = (bf16[2,64,896]{2,1,0:T(8,128)(2,1)S(1)}, bf16[2,64,896]{2,1,0:T(8,128)(2,1)S(1)}, u32[]{:S(2)}, u32[]{:S(2)}) collective-permute-start(bf16[2,64,896]{2,1,0:T(8,128)(2,1)S(1)} %get-tuple-element.27.refs_5_), channel_id=1, source_target_pairs={{0,7},{1,0},{2,1},{3,2},{4,3},{5,4},{6,5},{7,6},{8,15},{9,8},{10,9... | collective-permute-start | bytes 688136 | tf_op jit(solution)/shard_map/ppermute | solution.py:37
  20.6 0.6 copy-done.1
  21.2 4.4 %pack.1 = (bf16[8,64,512]{2,1,0:T(8,128)(2,1)S(1)}, bf16[8,2,64,512]{3,2,1,0:T(8,128)(2,1)}) custom-call(s32[1]{0:T(128)} %bitcast.16.odd_ref, s32[1]{0:T(128)S(6)} %copy.5.own_ref, s32[1]{0:T(128)} %collective-permute-done.core_ref, s32[1]{0:T(128)} %collective-permute-done.1.far_ref, s32[8]{0:T(128)S(1)} %copy-done.1, bf16[4,2,64,4096]{3,2,1,0:T(8,128)(2,1)} %kernels_ref.1), custom_call_target="tpu_custom_call" | custom-call | tf_op jit(solution)/shard_map/pack/pallas_call | solution.py:114
  25.7 2.3 %collective-permute-done.7.refs_6_ = bf16[2,64,896]{2,1,0:T(8,128)(2,1)} collective-permute-done((bf16[2,64,896]{2,1,0:T(8,128)(2,1)S(1)}, bf16[2,64,896]{2,1,0:T(8,128)(2,1)}, u32[]{:S(2)}, u32[]{:S(2)}) %collective-permute-start.7) | collective-permute-done | bytes 229408 | tf_op jit(solution)/shard_map/ppermute | solution.py:37
  27.9 13.0 %all_to_all.20.refs_13_ = bf16[8,64,512]{2,1,0:T(8,128)(2,1)S(1)} all-to-all(bf16[8,64,512]{2,1,0:T(8,128)(2,1)S(1)} %get-tuple-element.34), channel_id=1, replica_groups={{0,8,16,24,32,40,48,56},{1,9,17,25,33,41,49,57},{2,10,18,26,34,42,50,58..., dimensions={0} | all-to-all | bytes 1048576 | tf_op jit(solution)/shard_map/all_to_all | solution.py:329
  40.9 4.6 %all-to-all-start.1 = ((bf16[8,2,64,512]{3,2,1,0:T(8,128)(2,1)}), bf16[8,2,64,512]{3,2,1,0:T(8,128)(2,1)S(1)}, u32[]{:S(2)}, u32[]{:S(2)}) async-start(bf16[8,2,64,512]{3,2,1,0:T(8,128)(2,1)} %get-tuple-element.35), calls=%async_computation.1 | async-start | bytes 2097152 | tf_op jit(solution)/shard_map/all_to_all | solution.py:331
  45.6 3.2 %collective-permute-start.12 = (bf16[2,64,896]{2,1,0:T(8,128)(2,1)}, bf16[2,64,896]{2,1,0:T(8,128)(2,1)}, u32[]{:S(2)}, u32[]{:S(2)}) collective-permute-start(bf16[2,64,896]{2,1,0:T(8,128)(2,1)} %copy-done.2), channel_id=1, source_target_pairs={{0,7},{1,0},{2,1},{3,2},{4,3},{5,4},{6,5},{7,6},{8,15},{9,8},{10,9... | collective-permute-start | bytes 688136 | tf_op jit(solution)/shard_map/ppermute | solution.py:37
  48.8 4.2 %collective-permute-done.11.refs_8_ = bf16[2,64,896]{2,1,0:T(8,128)(2,1)S(1)} collective-permute-done((bf16[2,64,896]{2,1,0:T(8,128)(2,1)}, bf16[2,64,896]{2,1,0:T(8,128)(2,1)S(1)}, u32[]{:S(2)}, u32[]{:S(2)}) %collective-permute-start.11) | collective-permute-done | bytes 229408 | tf_op jit(solution)/shard_map/ppermute | solution.py:37
  53.0 0.7 copy-done.3
  53.7 0.7 slice.18
  54.4 0.7 slice.19
  55.1 2.7 %collective-permute-start.10 = (bf16[2,64,896]{2,1,0:T(8,128)(2,1)}, bf16[2,64,896]{2,1,0:T(8,128)(2,1)}, u32[]{:S(2)}, u32[]{:S(2)}) collective-permute-start(bf16[2,64,896]{2,1,0:T(8,128)(2,1)} %slice.19), channel_id=1, source_target_pairs={{0,48},{1,49},{2,50},{3,51},{4,52},{5,53},{6,54},{7,55},{8,56},{9,... | collective-permute-start | bytes 688136 | tf_op jit(solution)/shard_map/ppermute | solution.py:37
  57.8 3.2 %collective-permute-start.14 = (bf16[2,64,896]{2,1,0:T(8,128)(2,1)}, bf16[2,64,896]{2,1,0:T(8,128)(2,1)}, u32[]{:S(2)}, u32[]{:S(2)}) collective-permute-start(bf16[2,64,896]{2,1,0:T(8,128)(2,1)} %collective-permute-done.12.refs_9_), channel_id=1, source_target_pairs={{0,7},{1,0},{2,1},{3,2},{4,3},{5,4},{6,5},{7,6},{8,15},{9,8},{10,9... | collective-permute-start | bytes 688136 | tf_op jit(solution)/shard_map/ppermute | solution.py:37
  61.3 0.4 collective-permute-done.10.refs_3_
  61.7 3.7 %collective-permute-done.9.refs_2_ = bf16[2,64,896]{2,1,0:T(8,128)(2,1)} collective-permute-done((bf16[2,64,896]{2,1,0:T(8,128)(2,1)}, bf16[2,64,896]{2,1,0:T(8,128)(2,1)}, u32[]{:S(2)}, u32[]{:S(2)}) %collective-permute-start.9) | collective-permute-done | bytes 229408 | tf_op jit(solution)/shard_map/ppermute | solution.py:37
  65.4 3.2 %collective-permute-done.15.refs_12_ = bf16[2,64,896]{2,1,0:T(8,128)(2,1)} collective-permute-done((bf16[2,64,896]{2,1,0:T(8,128)(2,1)}, bf16[2,64,896]{2,1,0:T(8,128)(2,1)}, u32[]{:S(2)}, u32[]{:S(2)}) %collective-permute-start.15) | collective-permute-done | bytes 229408 | tf_op jit(solution)/shard_map/ppermute | solution.py:37
  68.6 5.3 %mix.1 = (bf16[512,1024]{1,0:T(8,128)(2,1)S(1)}, bf16[512,896]{1,0:T(8,128)(2,1)S(1)}, bf16[512,896]{1,0:T(8,128)(2,1)S(1)}) custom-call(s32[8]{0:T(128)S(1)} %stack.71.place_ref, s32[8]{0:T(128)S(1)} %stack.80.slot_ref, s32[1]{0:T(128)} %bitcast.16.odd_ref, bf16[4,64,896]{2,1,0:T(8,128)(2,1)S(1)} %get-tuple-element.26.refs_0_, ...), custom_call_target="tpu_custom_call" | custom-call | tf_op jit(solution)/shard_map/mix/pallas_call | solution.py:190
  74.1 0.6 prepare.1
  74.6 2.1 %collective-permute-done.17.m_ref = bf16[512,1024]{1,0:T(8,128)(2,1)S(1)} collective-permute-done((bf16[512,1024]{1,0:T(8,128)(2,1)S(1)}, bf16[512,1024]{1,0:T(8,128)(2,1)S(1)}, u32[]{:S(2)}, u32[]{:S(2)}) %collective-permute-start.17) | collective-permute-done | bytes 1048608 | tf_op jit(solution)/shard_map/ppermute | solution.py:41
  76.7 4.0 %project.1 = bf16[64,8,896]{2,1,0:T(8,128)(2,1)S(1)} custom-call(bf16[512,1024]{1,0:T(8,128)(2,1)S(1)} %collective-permute-done.17.m_ref, bf16[432,1024]{1,0:T(8,128)(2,1)S(1)} %get-tuple-element.39.left_ref, bf16[1024,896]{1,0:T(8,128)(2,1)S(1)} %get-tuple-element.40.right_ref), custom_call_target="tpu_custom_call" | custom-call | tf_op jit(solution)/shard_map/project/pallas_call | solution.py:256
  80.8 19.3 %all_to_all.21 = bf16[16,4,8,896]{3,2,1,0:T(8,128)(2,1)S(1)} all-to-all(bf16[16,4,8,896]{3,2,1,0:T(8,128)(2,1)S(1)} %bitcast.20), channel_id=1, replica_groups={{0,1,8,9,16,17,24,25,32,33,40,41,48,49,56,57},{2,3,10,11,18,19,26,27,34..., dimensions={0} | all-to-all | bytes 1835008 | tf_op jit(solution)/shard_map/all_to_all | solution.py:297
  100.1 0.8 convert_reduce_fusion
  100.9 5.4 %all-to-all-start.3 = ((f32[4,8,896]{2,1,0:T(8,128)}), f32[4,8,896]{2,1,0:T(8,128)S(1)}, u32[]{:S(2)}, u32[]{:S(2)}) async-start(f32[4,8,896]{2,1,0:T(8,128)} %convert_reduce_fusion), calls=%async_computation.3 | async-start | bytes 229376 | tf_op jit(solution)/shard_map/all_to_all | solution.py:299
  106.3 8.9 %all-to-all-done.3 = f32[4,8,896]{2,1,0:T(8,128)S(1)} async-done(((f32[4,8,896]{2,1,0:T(8,128)}), f32[4,8,896]{2,1,0:T(8,128)S(1)}, u32[]{:S(2)}, u32[]{:S(2)}) %all-to-all-start.3) | async-done | bytes 114720 | tf_op jit(solution)/shard_map/all_to_all | solution.py:299
  115.5 0.7 fusion.1
  (36 shorter events, 0.7 us)
Async XLA Ops:
  1.0 9.9 %collective-permute-start.4 = (bf16[64,896]{1,0:T(8,128)(2,1)S(1)}, bf16[64,896]{1,0:T(8,128)(2,1)S(1)}, u32[]{:S(2)}, u32[]{:S(2)}) collective-permute-start(bf16[64,896]{1,0:T(8,128)(2,1)S(1)} %lay.1.own_ref), channel_id=1, source_target_pairs={{128,8},{129,9},{130,10},{131,11},{132,12},{133,13},{134,14},{135,... | collective-permute-start | bytes 344072 | tf_op jit(solution)/shard_map/ppermute | solution.py:47
  3.2 7.6 %collective-permute-start.3 = (bf16[64,896]{1,0:T(8,128)(2,1)S(1)}, bf16[64,896]{1,0:T(8,128)(2,1)S(1)}, u32[]{:S(2)}, u32[]{:S(2)}) collective-permute-start(bf16[64,896]{1,0:T(8,128)(2,1)S(1)} %lay.1.own_ref), channel_id=1, source_target_pairs={{0,8},{1,9},{2,10},{3,11},{4,12},{5,13},{6,14},{7,15},{8,0},{9,1},... | collective-permute-start | bytes 344072 | tf_op jit(solution)/shard_map/ppermute | solution.py:37
  3.2 7.6 %collective-permute-start.2 = (bf16[64,896]{1,0:T(8,128)(2,1)S(1)}, bf16[64,896]{1,0:T(8,128)(2,1)S(1)}, u32[]{:S(2)}, u32[]{:S(2)}) collective-permute-start(bf16[64,896]{1,0:T(8,128)(2,1)S(1)} %lay.1.own_ref), channel_id=1, source_target_pairs={{0,128},{64,192},{128,0},{192,64},{1,129},{65,193},{129,1},{193,65... | collective-permute-start | bytes 344072 | tf_op jit(solution)/shard_map/ppermute | solution.py:41
  5.7 1.4 %collective-permute-start = (s32[1]{0:T(128)}, s32[1]{0:T(128)}, u32[]{:S(2)}, u32[]{:S(2)}) collective-permute-start(s32[1]{0:T(128)} %param.6), channel_id=1, source_target_pairs={{0,64},{64,0},{128,192},{192,128},{1,65},{65,1},{129,193},{193,129... | collective-permute-start | bytes 20 | tf_op jit(solution)/shard_map/ppermute | solution.py:41
  5.7 5.1 %collective-permute-start.1 = (s32[1]{0:T(128)}, s32[1]{0:T(128)}, u32[]{:S(2)}, u32[]{:S(2)}) collective-permute-start(s32[1]{0:T(128)} %param.6), channel_id=1, source_target_pairs={{0,128},{64,192},{128,0},{192,64},{1,129},{65,193},{129,1},{193,65... | collective-permute-start | bytes 20 | tf_op jit(solution)/shard_map/ppermute | solution.py:41
  10.9 14.7 %copy-start = (bf16[2,64,896]{2,1,0:T(8,128)(2,1)}, bf16[2,64,896]{2,1,0:T(8,128)(2,1)S(1)}, u32[]{:S(2)}) copy-start(bf16[2,64,896]{2,1,0:T(8,128)(2,1)S(1)} %get-tuple-element.27.refs_5_) | copy-start | bytes 688132
  10.9 17.0 %collective-permute-start.6 = (bf16[4,64,896]{2,1,0:T(8,128)(2,1)S(1)}, bf16[4,64,896]{2,1,0:T(8,128)(2,1)S(1)}, u32[]{:S(2)}, u32[]{:S(2)}) collective-permute-start(bf16[4,64,896]{2,1,0:T(8,128)(2,1)S(1)} %get-tuple-element.26.refs_0_), channel_id=1, source_target_pairs={{0,48},{1,49},{2,50},{3,51},{4,52},{5,53},{6,54},{7,55},{8,56},{9,... | collective-permute-start | bytes 1376264 | tf_op jit(solution)/shard_map/ppermute | solution.py:37
  14.0 13.9 %collective-permute-start.5 = (bf16[4,64,896]{2,1,0:T(8,128)(2,1)S(1)}, bf16[4,64,896]{2,1,0:T(8,128)(2,1)S(1)}, u32[]{:S(2)}, u32[]{:S(2)}) collective-permute-start(bf16[4,64,896]{2,1,0:T(8,128)(2,1)S(1)} %get-tuple-element.26.refs_0_), channel_id=1, source_target_pairs={{0,16},{1,17},{2,18},{3,19},{4,20},{5,21},{6,22},{7,23},{8,24},{9,... | collective-permute-start | bytes 1376264 | tf_op jit(solution)/shard_map/ppermute | solution.py:37
  14.0 11.6 %collective-permute-start.8 = (bf16[2,64,896]{2,1,0:T(8,128)(2,1)S(1)}, bf16[2,64,896]{2,1,0:T(8,128)(2,1)S(1)}, u32[]{:S(2)}, u32[]{:S(2)}) collective-permute-start(bf16[2,64,896]{2,1,0:T(8,128)(2,1)S(1)} %get-tuple-element.27.refs_5_), channel_id=1, source_target_pairs={{0,7},{1,0},{2,1},{3,2},{4,3},{5,4},{6,5},{7,6},{8,15},{9,8},{10,9... | collective-permute-start | bytes 688136 | tf_op jit(solution)/shard_map/ppermute | solution.py:37
  19.9 8.0 %collective-permute-start.7 = (bf16[2,64,896]{2,1,0:T(8,128)(2,1)S(1)}, bf16[2,64,896]{2,1,0:T(8,128)(2,1)}, u32[]{:S(2)}, u32[]{:S(2)}) collective-permute-start(bf16[2,64,896]{2,1,0:T(8,128)(2,1)S(1)} %get-tuple-element.27.refs_5_), channel_id=1, source_target_pairs={{0,1},{1,2},{2,3},{3,4},{4,5},{5,6},{6,7},{7,0},{8,9},{9,10},{10,1... | collective-permute-start | bytes 688136 | tf_op jit(solution)/shard_map/ppermute | solution.py:37
  20.6 0.7 copy-start.1
  25.7 2.3 %copy-start.2 = (bf16[2,64,896]{2,1,0:T(8,128)(2,1)}, bf16[2,64,896]{2,1,0:T(8,128)(2,1)S(1)}, u32[]{:S(2)}) copy-start(bf16[2,64,896]{2,1,0:T(8,128)(2,1)S(1)} %collective-permute-done.8.refs_7_) | copy-start | bytes 688132
  40.9 27.7 %all-to-all-start.1 = ((bf16[8,2,64,512]{3,2,1,0:T(8,128)(2,1)}), bf16[8,2,64,512]{3,2,1,0:T(8,128)(2,1)S(1)}, u32[]{:S(2)}, u32[]{:S(2)}) async-start(bf16[8,2,64,512]{3,2,1,0:T(8,128)(2,1)} %get-tuple-element.35), calls=%async_computation.1 | async-start | bytes 2097152 | tf_op jit(solution)/shard_map/all_to_all | solution.py:331
  45.6 7.4 %collective-permute-start.11 = (bf16[2,64,896]{2,1,0:T(8,128)(2,1)}, bf16[2,64,896]{2,1,0:T(8,128)(2,1)S(1)}, u32[]{:S(2)}, u32[]{:S(2)}) collective-permute-start(bf16[2,64,896]{2,1,0:T(8,128)(2,1)} %collective-permute-done.7.refs_6_), channel_id=1, source_target_pairs={{0,1},{1,2},{2,3},{3,4},{4,5},{5,6},{6,7},{7,0},{8,9},{9,10},{10,1... | collective-permute-start | bytes 688136 | tf_op jit(solution)/shard_map/ppermute | solution.py:37
  45.6 23.1 %collective-permute-start.16 = (bf16[8,64,512]{2,1,0:T(8,128)(2,1)S(1)}, bf16[8,64,512]{2,1,0:T(8,128)(2,1)S(1)}, u32[]{:S(2)}, u32[]{:S(2)}) collective-permute-start(bf16[8,64,512]{2,1,0:T(8,128)(2,1)S(1)} %all_to_all.20.refs_13_), channel_id=1, source_target_pairs={{0,64},{64,0},{128,192},{192,128},{1,65},{65,1},{129,193},{193,129... | collective-permute-start | bytes 1572872 | tf_op jit(solution)/shard_map/ppermute | solution.py:41
  45.6 12.3 %collective-permute-start.12 = (bf16[2,64,896]{2,1,0:T(8,128)(2,1)}, bf16[2,64,896]{2,1,0:T(8,128)(2,1)}, u32[]{:S(2)}, u32[]{:S(2)}) collective-permute-start(bf16[2,64,896]{2,1,0:T(8,128)(2,1)} %copy-done.2), channel_id=1, source_target_pairs={{0,7},{1,0},{2,1},{3,2},{4,3},{5,4},{6,5},{7,6},{8,15},{9,8},{10,9... | collective-permute-start | bytes 688136 | tf_op jit(solution)/shard_map/ppermute | solution.py:37
  53.0 0.7 copy-start.3
  53.7 7.4 %collective-permute-start.13 = (bf16[2,64,896]{2,1,0:T(8,128)(2,1)S(1)}, bf16[2,64,896]{2,1,0:T(8,128)(2,1)}, u32[]{:S(2)}, u32[]{:S(2)}) collective-permute-start(bf16[2,64,896]{2,1,0:T(8,128)(2,1)S(1)} %collective-permute-done.11.refs_8_), channel_id=1, source_target_pairs={{0,1},{1,2},{2,3},{3,4},{4,5},{5,6},{6,7},{7,0},{8,9},{9,10},{10,1... | collective-permute-start | bytes 688136 | tf_op jit(solution)/shard_map/ppermute | solution.py:37
  55.1 6.6 %collective-permute-start.10 = (bf16[2,64,896]{2,1,0:T(8,128)(2,1)}, bf16[2,64,896]{2,1,0:T(8,128)(2,1)}, u32[]{:S(2)}, u32[]{:S(2)}) collective-permute-start(bf16[2,64,896]{2,1,0:T(8,128)(2,1)} %slice.19), channel_id=1, source_target_pairs={{0,48},{1,49},{2,50},{3,51},{4,52},{5,53},{6,54},{7,55},{8,56},{9,... | collective-permute-start | bytes 688136 | tf_op jit(solution)/shard_map/ppermute | solution.py:37
  57.8 7.5 %collective-permute-start.9 = (bf16[2,64,896]{2,1,0:T(8,128)(2,1)}, bf16[2,64,896]{2,1,0:T(8,128)(2,1)}, u32[]{:S(2)}, u32[]{:S(2)}) collective-permute-start(bf16[2,64,896]{2,1,0:T(8,128)(2,1)} %slice.18), channel_id=1, source_target_pairs={{0,16},{1,17},{2,18},{3,19},{4,20},{5,21},{6,22},{7,23},{8,24},{9,... | collective-permute-start | bytes 688136 | tf_op jit(solution)/shard_map/ppermute | solution.py:37
  57.8 7.5 %collective-permute-start.14 = (bf16[2,64,896]{2,1,0:T(8,128)(2,1)}, bf16[2,64,896]{2,1,0:T(8,128)(2,1)}, u32[]{:S(2)}, u32[]{:S(2)}) collective-permute-start(bf16[2,64,896]{2,1,0:T(8,128)(2,1)} %collective-permute-done.12.refs_9_), channel_id=1, source_target_pairs={{0,7},{1,0},{2,1},{3,2},{4,3},{5,4},{6,5},{7,6},{8,15},{9,8},{10,9... | collective-permute-start | bytes 688136 | tf_op jit(solution)/shard_map/ppermute | solution.py:37
  61.1 7.5 %collective-permute-start.15 = (bf16[2,64,896]{2,1,0:T(8,128)(2,1)}, bf16[2,64,896]{2,1,0:T(8,128)(2,1)}, u32[]{:S(2)}, u32[]{:S(2)}) collective-permute-start(bf16[2,64,896]{2,1,0:T(8,128)(2,1)} %collective-permute-done.13.refs_10_), channel_id=1, source_target_pairs={{0,1},{1,2},{2,3},{3,4},{4,5},{5,6},{6,7},{7,0},{8,9},{9,10},{10,1... | collective-permute-start | bytes 688136 | tf_op jit(solution)/shard_map/ppermute | solution.py:37
  74.0 2.7 %collective-permute-start.17 = (bf16[512,1024]{1,0:T(8,128)(2,1)S(1)}, bf16[512,1024]{1,0:T(8,128)(2,1)S(1)}, u32[]{:S(2)}, u32[]{:S(2)}) collective-permute-start(bf16[512,1024]{1,0:T(8,128)(2,1)S(1)} %get-tuple-element.36), channel_id=1, source_target_pairs={{0,64},{64,0},{128,192},{192,128},{1,65},{65,1},{129,193},{193,129... | collective-permute-start | bytes 3145736 | tf_op jit(solution)/shard_map/ppermute | solution.py:41
  100.9 14.3 %all-to-all-start.3 = ((f32[4,8,896]{2,1,0:T(8,128)}), f32[4,8,896]{2,1,0:T(8,128)S(1)}, u32[]{:S(2)}, u32[]{:S(2)}) async-start(f32[4,8,896]{2,1,0:T(8,128)} %convert_reduce_fusion), calls=%async_computation.3 | async-start | bytes 229376 | tf_op jit(solution)/shard_map/all_to_all | solution.py:299

commit v18 on v14

--- a/solution.py
+++ b/solution.py
@@ -14,7 +14,7 @@
 REST = NB - WHOLE
 TAIL = 2 * WHOLE
 LANES = TAIL + 128
-EARLY = 6
+EARLY = 5
 VMEM = 24 * 1024 * 1024
 
 IN_VMEM = pl.BlockSpec(memory_space=pltpu.VMEM)
@@ -314,22 +314,23 @@
 
     over_yx = [[g * NZ + i for g in range(GROUPS)] for i in range(NZ)]
     sends = pack(odd, pair_kdiff, diff_core, diff_far, stored_kernel_index, kernels)
+
+    four, both = bundle(own, far, own_side, far_side)
+    up, down = shift(four, 1, 0, 0), shift(four, -1, 0, 0)
+    steps = shift(both, 0, 0, 1), shift(both, 0, 0, -1)
+    ahead, behind, sends = lax.optimization_barrier((*steps, sends))
+    over = shift(up[:2], 1, 0, 0), shift(down[2:], -1, 0, 0)
     kern = lax.all_to_all(sends, "band", 0, 0, axis_index_groups=over_yx)
-    half = swap_groups(kern[:, 0], 1)
-
-    four, both = bundle(own, far, own_side, far_side)
-    opposite = shift(both, 0, 0, NZ // 2)
-    steps = shift(four, 1, 0, 0), shift(four, -1, 0, 0), shift(both, 0, 0, 1), shift(both, 0, 0, -1)
-    up, down, ahead, behind = lax.optimization_barrier(steps)
-    over = shift(up[:2], 1, 0, 0), shift(down[2:], -1, 0, 0)
     cols = [both, ahead, behind]
     for _ in range(2):
         ahead, behind = shift(ahead, 0, 0, 1), shift(behind, 0, 0, -1)
         cols += [ahead, behind]
-    cols.insert(3, opposite)
+    cols.append(shift(ahead, 0, 0, 1))
+    kern = lax.optimization_barrier((kern, ahead, behind))[0]
+    half = swap_groups(kern[:, 0], 1)
 
     place = jnp.stack([(y - dy) % NY * NX + (x - dx) % NX for dy in range(NY) for dx in range(NX)])
-    slots = jnp.stack([(z + i) % NZ for i in (0, -1, 1, -4, -2, 2, -3, 3)])
+    slots = jnp.stack([(z + i) % NZ for i in (0, -1, 1, -2, 2, -3, 3, -4)])
     m_out, rows, cols = mix(place, slots, odd, four, up, over, down, cols, half, kern)
     m_own = swap_groups(m_out, 1)
     left, right = prepare(rows, cols)

time: 131 us -> 118 us (0.901)
  starting transfers between devices: 40.1 us -> 32.7 us
  waiting for transfers between devices: 47.3 us -> 41.8 us
  local copies, waits for them, and re-layouts: 4.03 us -> 5.96 us
    ppermute x12, waiting for transfers between devices: 29.4 us -> 20.7 us  [shift(): return lax.ppermute(block, 'band', band_route(dy, dx, dz))]
    ppermute x12, starting transfers between devices: 23.9 us -> 17.4 us  [shift(): return lax.ppermute(block, 'band', band_route(dy, dx, dz))]
    all_to_all x1, waiting for transfers between devices: 0.01 us -> 5.83 us  [on_device(): kern = lax.all_to_all(sends, 'band', 0, 0, axis_index_groups=over_yx)]
    ppermute x1, starting transfers between devices: 0.04 us -> 2.25 us  [other_side(): return lax.ppermute(block, ('kgrp', 'band'), both)]
    unnamed x6 -> x20, local copies, waits for them, and re-layouts: 1.36 us -> 3.28 us
    all_to_all x1, starting transfers between devices: 5.38 us -> 3.54 us  [reduce_windows(): lax.all_to_all(parts, 'band', 0, 0, axis_index_groups=deep)]
    ppermute x5, waiting for transfers between devices: 7.72 us -> 6.31 us  [swap_groups(): return lax.ppermute(block, 'kgrp', [(k, k ^ bit) for k in range(4)])]
  transfers between devices with their start and end apart: 20 -> 20, of which waited for: 9 -> 11; matrix products, arithmetic and copies ran while one was open for 2% -> 2% of each run, Pallas kernels for 2% -> 4%
where the time goes in v18:
time: 118 us; the launch traced here: 117 us
  waiting for transfers between devices  41.8 us (35%)
  starting transfers between devices  32.7 us (28%)
  blocking collectives  19 us (16%)
  Pallas kernels  15.2 us (13%)
  local copies, waits for them, and re-layouts  5.96 us (5%)
  other arithmetic  1.52 us (1%)
    ppermute x12, waiting for transfers between devices, shift(): return lax.ppermute(block, 'band', band_route(dy, dx, dz))  20.7 us
    all_to_all x1, blocking collectives, reduce_windows(): parts = lax.all_to_all(parts, 'band', 0, 0, axis_index_groups=wide)  19 us
    ppermute x12, starting transfers between devices, shift(): return lax.ppermute(block, 'band', band_route(dy, dx, dz))  17.4 us
    all_to_all x1, waiting for transfers between devices, reduce_windows(): lax.all_to_all(parts, 'band', 0, 0, axis_index_groups=deep)  8.91 us
    ppermute x5, waiting for transfers between devices, swap_groups(): return lax.ppermute(block, 'kgrp', [(k, k ^ bit) for k in range(4)])  6.31 us
    all_to_all x1, starting transfers between devices, on_device(): kern = lax.all_to_all(sends, 'band', 0, 0, axis_index_groups=over_yx)  5.93 us
    all_to_all x1, waiting for transfers between devices, on_device(): kern = lax.all_to_all(sends, 'band', 0, 0, axis_index_groups=over_yx)  5.83 us
    pallas_call x1, Pallas kernels, mix(): pl.pallas_call(mix_body, out_shape=[pltpu.VMEM((BLOCK, 2 * BLOCK), jnp.bf...  5.08 us
  transfers between devices with their start and end apart: 20, of which 11 were waited for; matrix products, arithmetic and copies ran while one was open for 2% of the time, Pallas kernels for 4%

profile of v18, /device:TPU:6, one launch (start us, length us, event | category | flops | bytes accessed | tf_op | source)
XLA Modules:
  0.0 117.1 jit_solution(17022550614145562684)
XLA Ops:
  0.0 1.0 lay.1.own_ref
  1.0 2.3 %collective-permute-start.4 = (bf16[64,896]{1,0:T(8,128)(2,1)S(1)}, bf16[64,896]{1,0:T(8,128)(2,1)S(1)}, u32[]{:S(2)}, u32[]{:S(2)}) collective-permute-start(bf16[64,896]{1,0:T(8,128)(2,1)S(1)} %lay.1.own_ref), channel_id=1, source_target_pairs={{128,8},{129,9},{130,10},{131,11},{132,12},{133,13},{134,14},{135,... | collective-permute-start | bytes 344072 | tf_op jit(solution)/shard_map/ppermute | solution.py:47
  3.2 2.5 %collective-permute-start.2 = (bf16[64,896]{1,0:T(8,128)(2,1)S(1)}, bf16[64,896]{1,0:T(8,128)(2,1)S(1)}, u32[]{:S(2)}, u32[]{:S(2)}) collective-permute-start(bf16[64,896]{1,0:T(8,128)(2,1)S(1)} %lay.1.own_ref), channel_id=1, source_target_pairs={{0,128},{64,192},{128,0},{192,64},{1,129},{65,193},{129,1},{193,65... | collective-permute-start | bytes 344072 | tf_op jit(solution)/shard_map/ppermute | solution.py:41
  5.7 1.0 collective-permute-start.1
  7.0 4.1 %collective-permute-done.1.far_ref = s32[1]{0:T(128)} collective-permute-done((s32[1]{0:T(128)}, s32[1]{0:T(128)}, u32[]{:S(2)}, u32[]{:S(2)}) %collective-permute-start.1) | collective-permute-done | bytes 36 | tf_op jit(solution)/shard_map/ppermute | solution.py:41
  11.1 5.9 %collective-permute-start.10 = (bf16[2,64,896]{2,1,0:T(8,128)(2,1)S(1)}, bf16[2,64,896]{2,1,0:T(8,128)(2,1)S(1)}, u32[]{:S(2)}, u32[]{:S(2)}) collective-permute-start(bf16[2,64,896]{2,1,0:T(8,128)(2,1)S(1)} %get-tuple-element.23.refs_5_), channel_id=1, source_target_pairs={{0,7},{1,0},{2,1},{3,2},{4,3},{5,4},{6,5},{7,6},{8,15},{9,8},{10,9... | collective-permute-start | bytes 688136 | tf_op jit(solution)/shard_map/ppermute | solution.py:37
  18.3 4.5 %pack.1 = bf16[8,3,64,512]{3,2,1,0:T(8,128)(2,1)} custom-call(s32[1]{0:T(128)} %bitcast.16.odd_ref, s32[1]{0:T(128)S(6)} %copy.5.own_ref, s32[1]{0:T(128)} %collective-permute-done.core_ref, s32[1]{0:T(128)} %collective-permute-done.1.far_ref, s32[8]{0:T(128)S(1)} %copy-done.5, bf16[4,2,64,4096]{3,2,1,0:T(8,128)(2,1)} %kernels_ref.1), custom_call_target="tpu_custom_call" | custom-call | tf_op jit(solution)/shard_map/pack/pallas_call | solution.py:110
  22.9 2.2 %collective-permute-done.9.refs_6_ = bf16[2,64,896]{2,1,0:T(8,128)(2,1)S(1)} collective-permute-done((bf16[2,64,896]{2,1,0:T(8,128)(2,1)S(1)}, bf16[2,64,896]{2,1,0:T(8,128)(2,1)S(1)}, u32[]{:S(2)}, u32[]{:S(2)}) %collective-permute-start.9) | collective-permute-done | bytes 229408 | tf_op jit(solution)/shard_map/ppermute | solution.py:37
  25.1 5.9 %all-to-all-start = ((bf16[8,3,64,512]{3,2,1,0:T(8,128)(2,1)}), bf16[8,3,64,512]{3,2,1,0:T(8,128)(2,1)S(1)}, u32[]{:S(2)}, u32[]{:S(2)}) async-start(bf16[8,3,64,512]{3,2,1,0:T(8,128)(2,1)} %pack.1), calls=%async_computation | async-start | bytes 3145728 | tf_op jit(solution)/shard_map/all_to_all | solution.py:323
  31.0 3.2 %collective-permute-start.12 = (bf16[2,64,896]{2,1,0:T(8,128)(2,1)S(1)}, bf16[2,64,896]{2,1,0:T(8,128)(2,1)S(1)}, u32[]{:S(2)}, u32[]{:S(2)}) collective-permute-start(bf16[2,64,896]{2,1,0:T(8,128)(2,1)S(1)} %collective-permute-done.10.refs_7_), channel_id=1, source_target_pairs={{0,7},{1,0},{2,1},{3,2},{4,3},{5,4},{6,5},{7,6},{8,15},{9,8},{10,9... | collective-permute-start | bytes 688136 | tf_op jit(solution)/shard_map/ppermute | solution.py:37
  34.3 4.0 %collective-permute-done.11.refs_8_ = bf16[2,64,896]{2,1,0:T(8,128)(2,1)S(1)} collective-permute-done((bf16[2,64,896]{2,1,0:T(8,128)(2,1)S(1)}, bf16[2,64,896]{2,1,0:T(8,128)(2,1)S(1)}, u32[]{:S(2)}, u32[]{:S(2)}) %collective-permute-start.11) | collective-permute-done | bytes 229408 | tf_op jit(solution)/shard_map/ppermute | solution.py:37
  38.3 3.3 %collective-permute-start.14 = (bf16[2,64,896]{2,1,0:T(8,128)(2,1)S(1)}, bf16[2,64,896]{2,1,0:T(8,128)(2,1)S(1)}, u32[]{:S(2)}, u32[]{:S(2)}) collective-permute-start(bf16[2,64,896]{2,1,0:T(8,128)(2,1)S(1)} %collective-permute-done.12.refs_9_), channel_id=1, source_target_pairs={{0,7},{1,0},{2,1},{3,2},{4,3},{5,4},{6,5},{7,6},{8,15},{9,8},{10,9... | collective-permute-start | bytes 688136 | tf_op jit(solution)/shard_map/ppermute | solution.py:37
  41.6 2.7 %collective-permute-start.7 = (bf16[4,64,896]{2,1,0:T(8,128)(2,1)S(1)}, bf16[4,64,896]{2,1,0:T(8,128)(2,1)S(1)}, u32[]{:S(2)}, u32[]{:S(2)}) collective-permute-start(bf16[4,64,896]{2,1,0:T(8,128)(2,1)S(1)} %get-tuple-element.22.refs_0_), channel_id=1, source_target_pairs={{0,48},{1,49},{2,50},{3,51},{4,52},{5,53},{6,54},{7,55},{8,56},{9,... | collective-permute-start | bytes 1376264 | tf_op jit(solution)/shard_map/ppermute | solution.py:37
  44.2 1.2 %collective-permute-done.13.refs_10_ = bf16[2,64,896]{2,1,0:T(8,128)(2,1)S(1)} collective-permute-done((bf16[2,64,896]{2,1,0:T(8,128)(2,1)S(1)}, bf16[2,64,896]{2,1,0:T(8,128)(2,1)S(1)}, u32[]{:S(2)}, u32[]{:S(2)}) %collective-permute-start.13) | collective-permute-done | bytes 229408 | tf_op jit(solution)/shard_map/ppermute | solution.py:37
  45.5 0.7 copy-done.3
  46.2 5.8 %all-to-all-done.refs_14_ = bf16[8,3,64,512]{3,2,1,0:T(8,128)(2,1)S(1)} async-done(((bf16[8,3,64,512]{3,2,1,0:T(8,128)(2,1)}), bf16[8,3,64,512]{3,2,1,0:T(8,128)(2,1)S(1)}, u32[]{:S(2)}, u32[]{:S(2)}) %all-to-all-start) | async-done | bytes 1572896 | tf_op jit(solution)/shard_map/all_to_all | solution.py:323
  52.1 0.8 slice_bitcast_fusion
  52.9 5.2 %collective-permute-done.7.refs_4_ = bf16[4,64,896]{2,1,0:T(8,128)(2,1)S(1)} collective-permute-done((bf16[4,64,896]{2,1,0:T(8,128)(2,1)S(1)}, bf16[4,64,896]{2,1,0:T(8,128)(2,1)S(1)}, u32[]{:S(2)}, u32[]{:S(2)}) %collective-permute-start.7) | collective-permute-done | bytes 458784 | tf_op jit(solution)/shard_map/ppermute | solution.py:37
  58.1 0.7 slice.29
  58.8 2.2 %collective-permute-start.8 = (bf16[2,64,896]{2,1,0:T(8,128)(2,1)}, bf16[2,64,896]{2,1,0:T(8,128)(2,1)}, u32[]{:S(2)}, u32[]{:S(2)}) collective-permute-start(bf16[2,64,896]{2,1,0:T(8,128)(2,1)} %slice.29), channel_id=1, source_target_pairs={{0,48},{1,49},{2,50},{3,51},{4,52},{5,53},{6,54},{7,55},{8,56},{9,... | collective-permute-start | bytes 688136 | tf_op jit(solution)/shard_map/ppermute | solution.py:37
  61.9 4.0 %collective-permute-done.8.refs_3_ = bf16[2,64,896]{2,1,0:T(8,128)(2,1)} collective-permute-done((bf16[2,64,896]{2,1,0:T(8,128)(2,1)}, bf16[2,64,896]{2,1,0:T(8,128)(2,1)}, u32[]{:S(2)}, u32[]{:S(2)}) %collective-permute-start.8) | collective-permute-done | bytes 229408 | tf_op jit(solution)/shard_map/ppermute | solution.py:37
  65.9 4.1 %collective-permute-done.6.refs_2_ = bf16[2,64,896]{2,1,0:T(8,128)(2,1)} collective-permute-done((bf16[2,64,896]{2,1,0:T(8,128)(2,1)}, bf16[2,64,896]{2,1,0:T(8,128)(2,1)}, u32[]{:S(2)}, u32[]{:S(2)}) %collective-permute-start.6) | collective-permute-done | bytes 229408 | tf_op jit(solution)/shard_map/ppermute | solution.py:37
  70.0 0.9 copy-done.2
  71.0 0.9 copy-done.4
  71.9 5.1 %mix.1 = (bf16[512,1024]{1,0:T(8,128)(2,1)S(1)}, bf16[512,896]{1,0:T(8,128)(2,1)S(1)}, bf16[512,896]{1,0:T(8,128)(2,1)S(1)}) custom-call(s32[8]{0:T(128)S(1)} %stack.71.place_ref, s32[8]{0:T(128)S(1)} %stack.80.slot_ref, s32[1]{0:T(128)} %bitcast.16.odd_ref, bf16[4,64,896]{2,1,0:T(8,128)(2,1)S(1)} %get-tuple-element.22.refs_0_, ...), custom_call_target="tpu_custom_call" | custom-call | tf_op jit(solution)/shard_map/mix/pallas_call | solution.py:183
  77.7 2.1 %collective-permute-done.17.m_ref = bf16[512,1024]{1,0:T(8,128)(2,1)S(1)} collective-permute-done((bf16[512,1024]{1,0:T(8,128)(2,1)S(1)}, bf16[512,1024]{1,0:T(8,128)(2,1)S(1)}, u32[]{:S(2)}, u32[]{:S(2)}) %collective-permute-start.17) | collective-permute-done | bytes 1048608 | tf_op jit(solution)/shard_map/ppermute | solution.py:41
  79.7 4.0 %project.1 = bf16[64,8,896]{2,1,0:T(8,128)(2,1)S(1)} custom-call(bf16[512,1024]{1,0:T(8,128)(2,1)S(1)} %collective-permute-done.17.m_ref, bf16[432,1024]{1,0:T(8,128)(2,1)S(1)} %get-tuple-element.31.left_ref, bf16[1024,896]{1,0:T(8,128)(2,1)S(1)} %get-tuple-element.32.right_ref), custom_call_target="tpu_custom_call" | custom-call | tf_op jit(solution)/shard_map/project/pallas_call | solution.py:249
  83.8 19.0 %all_to_all.15 = bf16[16,4,8,896]{3,2,1,0:T(8,128)(2,1)S(1)} all-to-all(bf16[16,4,8,896]{3,2,1,0:T(8,128)(2,1)S(1)} %bitcast.22), channel_id=1, replica_groups={{0,1,8,9,16,17,24,25,32,33,40,41,48,49,56,57},{2,3,10,11,18,19,26,27,34..., dimensions={0} | all-to-all | bytes 1835008 | tf_op jit(solution)/shard_map/all_to_all | solution.py:290
  102.8 0.8 convert_reduce_fusion
  103.6 3.5 %all-to-all-start.2 = ((f32[4,8,896]{2,1,0:T(8,128)}), f32[4,8,896]{2,1,0:T(8,128)S(1)}, u32[]{:S(2)}, u32[]{:S(2)}) async-start(f32[4,8,896]{2,1,0:T(8,128)} %convert_reduce_fusion), calls=%async_computation.2 | async-start | bytes 229376 | tf_op jit(solution)/shard_map/all_to_all | solution.py:292
  107.1 8.9 %all-to-all-done.2 = f32[4,8,896]{2,1,0:T(8,128)S(1)} async-done(((f32[4,8,896]{2,1,0:T(8,128)}), f32[4,8,896]{2,1,0:T(8,128)S(1)}, u32[]{:S(2)}, u32[]{:S(2)}) %all-to-all-start.2) | async-done | bytes 114720 | tf_op jit(solution)/shard_map/all_to_all | solution.py:292
  116.3 0.7 fusion.1
  (48 shorter events, 2.8 us)
Async XLA Ops:
  1.0 10.0 %collective-permute-start.4 = (bf16[64,896]{1,0:T(8,128)(2,1)S(1)}, bf16[64,896]{1,0:T(8,128)(2,1)S(1)}, u32[]{:S(2)}, u32[]{:S(2)}) collective-permute-start(bf16[64,896]{1,0:T(8,128)(2,1)S(1)} %lay.1.own_ref), channel_id=1, source_target_pairs={{128,8},{129,9},{130,10},{131,11},{132,12},{133,13},{134,14},{135,... | collective-permute-start | bytes 344072 | tf_op jit(solution)/shard_map/ppermute | solution.py:47
  3.2 7.8 %collective-permute-start.3 = (bf16[64,896]{1,0:T(8,128)(2,1)S(1)}, bf16[64,896]{1,0:T(8,128)(2,1)S(1)}, u32[]{:S(2)}, u32[]{:S(2)}) collective-permute-start(bf16[64,896]{1,0:T(8,128)(2,1)S(1)} %lay.1.own_ref), channel_id=1, source_target_pairs={{0,8},{1,9},{2,10},{3,11},{4,12},{5,13},{6,14},{7,15},{8,0},{9,1},... | collective-permute-start | bytes 344072 | tf_op jit(solution)/shard_map/ppermute | solution.py:37
  3.2 7.8 %collective-permute-start.2 = (bf16[64,896]{1,0:T(8,128)(2,1)S(1)}, bf16[64,896]{1,0:T(8,128)(2,1)S(1)}, u32[]{:S(2)}, u32[]{:S(2)}) collective-permute-start(bf16[64,896]{1,0:T(8,128)(2,1)S(1)} %lay.1.own_ref), channel_id=1, source_target_pairs={{0,128},{64,192},{128,0},{192,64},{1,129},{65,193},{129,1},{193,65... | collective-permute-start | bytes 344072 | tf_op jit(solution)/shard_map/ppermute | solution.py:41
  5.7 1.2 %collective-permute-start = (s32[1]{0:T(128)}, s32[1]{0:T(128)}, u32[]{:S(2)}, u32[]{:S(2)}) collective-permute-start(s32[1]{0:T(128)} %param.6), channel_id=1, source_target_pairs={{0,64},{64,0},{128,192},{192,128},{1,65},{65,1},{129,193},{193,129... | collective-permute-start | bytes 20 | tf_op jit(solution)/shard_map/ppermute | solution.py:41
  5.7 5.3 %collective-permute-start.1 = (s32[1]{0:T(128)}, s32[1]{0:T(128)}, u32[]{:S(2)}, u32[]{:S(2)}) collective-permute-start(s32[1]{0:T(128)} %param.6), channel_id=1, source_target_pairs={{0,128},{64,192},{128,0},{192,64},{1,129},{65,193},{129,1},{193,65... | collective-permute-start | bytes 20 | tf_op jit(solution)/shard_map/ppermute | solution.py:41
  11.1 11.8 %copy-start = (bf16[2,64,896]{2,1,0:T(8,128)(2,1)}, bf16[2,64,896]{2,1,0:T(8,128)(2,1)S(1)}, u32[]{:S(2)}) copy-start(bf16[2,64,896]{2,1,0:T(8,128)(2,1)S(1)} %get-tuple-element.23.refs_5_) | copy-start | bytes 688132
  11.1 11.8 %collective-permute-start.10 = (bf16[2,64,896]{2,1,0:T(8,128)(2,1)S(1)}, bf16[2,64,896]{2,1,0:T(8,128)(2,1)S(1)}, u32[]{:S(2)}, u32[]{:S(2)}) collective-permute-start(bf16[2,64,896]{2,1,0:T(8,128)(2,1)S(1)} %get-tuple-element.23.refs_5_), channel_id=1, source_target_pairs={{0,7},{1,0},{2,1},{3,2},{4,3},{5,4},{6,5},{7,6},{8,15},{9,8},{10,9... | collective-permute-start | bytes 688136 | tf_op jit(solution)/shard_map/ppermute | solution.py:37
  17.0 8.1 %collective-permute-start.9 = (bf16[2,64,896]{2,1,0:T(8,128)(2,1)S(1)}, bf16[2,64,896]{2,1,0:T(8,128)(2,1)S(1)}, u32[]{:S(2)}, u32[]{:S(2)}) collective-permute-start(bf16[2,64,896]{2,1,0:T(8,128)(2,1)S(1)} %get-tuple-element.23.refs_5_), channel_id=1, source_target_pairs={{0,1},{1,2},{2,3},{3,4},{4,5},{5,6},{6,7},{7,0},{8,9},{9,10},{10,1... | collective-permute-start | bytes 688136 | tf_op jit(solution)/shard_map/ppermute | solution.py:37
  17.7 0.7 copy-start.5
  22.9 15.4 %copy-start.6 = (bf16[2,64,896]{2,1,0:T(8,128)(2,1)}, bf16[2,64,896]{2,1,0:T(8,128)(2,1)S(1)}, u32[]{:S(2)}) copy-start(bf16[2,64,896]{2,1,0:T(8,128)(2,1)S(1)} %collective-permute-done.10.refs_7_) | copy-start | bytes 688132
  25.1 16.5 %copy-start.7 = (bf16[2,64,896]{2,1,0:T(8,128)(2,1)}, bf16[2,64,896]{2,1,0:T(8,128)(2,1)S(1)}, u32[]{:S(2)}) copy-start(bf16[2,64,896]{2,1,0:T(8,128)(2,1)S(1)} %collective-permute-done.9.refs_6_) | copy-start | bytes 688132
  25.1 27.0 %all-to-all-start = ((bf16[8,3,64,512]{3,2,1,0:T(8,128)(2,1)}), bf16[8,3,64,512]{3,2,1,0:T(8,128)(2,1)S(1)}, u32[]{:S(2)}, u32[]{:S(2)}) async-start(bf16[8,3,64,512]{3,2,1,0:T(8,128)(2,1)} %pack.1), calls=%async_computation | async-start | bytes 3145728 | tf_op jit(solution)/shard_map/all_to_all | solution.py:323
  31.0 7.2 %collective-permute-start.11 = (bf16[2,64,896]{2,1,0:T(8,128)(2,1)S(1)}, bf16[2,64,896]{2,1,0:T(8,128)(2,1)S(1)}, u32[]{:S(2)}, u32[]{:S(2)}) collective-permute-start(bf16[2,64,896]{2,1,0:T(8,128)(2,1)S(1)} %collective-permute-done.9.refs_6_), channel_id=1, source_target_pairs={{0,1},{1,2},{2,3},{3,4},{4,5},{5,6},{6,7},{7,0},{8,9},{9,10},{10,1... | collective-permute-start | bytes 688136 | tf_op jit(solution)/shard_map/ppermute | solution.py:37
  31.0 7.2 %collective-permute-start.12 = (bf16[2,64,896]{2,1,0:T(8,128)(2,1)S(1)}, bf16[2,64,896]{2,1,0:T(8,128)(2,1)S(1)}, u32[]{:S(2)}, u32[]{:S(2)}) collective-permute-start(bf16[2,64,896]{2,1,0:T(8,128)(2,1)S(1)} %collective-permute-done.10.refs_7_), channel_id=1, source_target_pairs={{0,7},{1,0},{2,1},{3,2},{4,3},{5,4},{6,5},{7,6},{8,15},{9,8},{10,9... | collective-permute-start | bytes 688136 | tf_op jit(solution)/shard_map/ppermute | solution.py:37
  38.2 7.2 %copy-start.8 = (bf16[2,64,896]{2,1,0:T(8,128)(2,1)}, bf16[2,64,896]{2,1,0:T(8,128)(2,1)S(1)}, u32[]{:S(2)}) copy-start(bf16[2,64,896]{2,1,0:T(8,128)(2,1)S(1)} %collective-permute-done.11.refs_8_) | copy-start | bytes 688132
  38.2 7.2 %collective-permute-start.13 = (bf16[2,64,896]{2,1,0:T(8,128)(2,1)S(1)}, bf16[2,64,896]{2,1,0:T(8,128)(2,1)S(1)}, u32[]{:S(2)}, u32[]{:S(2)}) collective-permute-start(bf16[2,64,896]{2,1,0:T(8,128)(2,1)S(1)} %collective-permute-done.11.refs_8_), channel_id=1, source_target_pairs={{0,1},{1,2},{2,3},{3,4},{4,5},{5,6},{6,7},{7,0},{8,9},{9,10},{10,1... | collective-permute-start | bytes 688136 | tf_op jit(solution)/shard_map/ppermute | solution.py:37
  38.3 7.2 %copy-start.9 = (bf16[2,64,896]{2,1,0:T(8,128)(2,1)}, bf16[2,64,896]{2,1,0:T(8,128)(2,1)S(1)}, u32[]{:S(2)}) copy-start(bf16[2,64,896]{2,1,0:T(8,128)(2,1)S(1)} %collective-permute-done.12.refs_9_) | copy-start | bytes 688132
  38.3 7.2 %collective-permute-start.14 = (bf16[2,64,896]{2,1,0:T(8,128)(2,1)S(1)}, bf16[2,64,896]{2,1,0:T(8,128)(2,1)S(1)}, u32[]{:S(2)}, u32[]{:S(2)}) collective-permute-start(bf16[2,64,896]{2,1,0:T(8,128)(2,1)S(1)} %collective-permute-done.12.refs_9_), channel_id=1, source_target_pairs={{0,7},{1,0},{2,1},{3,2},{4,3},{5,4},{6,5},{7,6},{8,15},{9,8},{10,9... | collective-permute-start | bytes 688136 | tf_op jit(solution)/shard_map/ppermute | solution.py:37
  41.6 16.5 %collective-permute-start.7 = (bf16[4,64,896]{2,1,0:T(8,128)(2,1)S(1)}, bf16[4,64,896]{2,1,0:T(8,128)(2,1)S(1)}, u32[]{:S(2)}, u32[]{:S(2)}) collective-permute-start(bf16[4,64,896]{2,1,0:T(8,128)(2,1)S(1)} %get-tuple-element.22.refs_0_), channel_id=1, source_target_pairs={{0,48},{1,49},{2,50},{3,51},{4,52},{5,53},{6,54},{7,55},{8,56},{9,... | collective-permute-start | bytes 1376264 | tf_op jit(solution)/shard_map/ppermute | solution.py:37
  44.2 16.8 %collective-permute-start.5 = (bf16[4,64,896]{2,1,0:T(8,128)(2,1)S(1)}, bf16[4,64,896]{2,1,0:T(8,128)(2,1)S(1)}, u32[]{:S(2)}, u32[]{:S(2)}) collective-permute-start(bf16[4,64,896]{2,1,0:T(8,128)(2,1)S(1)} %get-tuple-element.22.refs_0_), channel_id=1, source_target_pairs={{0,16},{1,17},{2,18},{3,19},{4,20},{5,21},{6,22},{7,23},{8,24},{9,... | collective-permute-start | bytes 1376264 | tf_op jit(solution)/shard_map/ppermute | solution.py:37
  45.5 6.6 %copy-start.1 = (bf16[2,64,896]{2,1,0:T(8,128)(2,1)}, bf16[2,64,896]{2,1,0:T(8,128)(2,1)S(1)}, u32[]{:S(2)}) copy-start(bf16[2,64,896]{2,1,0:T(8,128)(2,1)S(1)} %collective-permute-done.13.refs_10_) | copy-start | bytes 688132
  45.5 0.7 copy-start.3
  52.9 17.1 %collective-permute-start.16 = (bf16[8,64,512]{2,1,0:T(8,128)(2,1)}, bf16[8,64,512]{2,1,0:T(8,128)(2,1)S(1)}, u32[]{:S(2)}, u32[]{:S(2)}) collective-permute-start(bf16[8,64,512]{2,1,0:T(8,128)(2,1)} %slice_bitcast_fusion), channel_id=1, source_target_pairs={{0,64},{64,0},{128,192},{192,128},{1,65},{65,1},{129,193},{193,129... | collective-permute-start | bytes 1572872 | tf_op jit(solution)/shard_map/ppermute | solution.py:41
  58.8 7.1 %collective-permute-start.8 = (bf16[2,64,896]{2,1,0:T(8,128)(2,1)}, bf16[2,64,896]{2,1,0:T(8,128)(2,1)}, u32[]{:S(2)}, u32[]{:S(2)}) collective-permute-start(bf16[2,64,896]{2,1,0:T(8,128)(2,1)} %slice.29), channel_id=1, source_target_pairs={{0,48},{1,49},{2,50},{3,51},{4,52},{5,53},{6,54},{7,55},{8,56},{9,... | collective-permute-start | bytes 688136 | tf_op jit(solution)/shard_map/ppermute | solution.py:37
  61.7 8.3 %collective-permute-start.6 = (bf16[2,64,896]{2,1,0:T(8,128)(2,1)}, bf16[2,64,896]{2,1,0:T(8,128)(2,1)}, u32[]{:S(2)}, u32[]{:S(2)}) collective-permute-start(bf16[2,64,896]{2,1,0:T(8,128)(2,1)} %slice.28), channel_id=1, source_target_pairs={{0,16},{1,17},{2,18},{3,19},{4,20},{5,21},{6,22},{7,23},{8,24},{9,... | collective-permute-start | bytes 688136 | tf_op jit(solution)/shard_map/ppermute | solution.py:37
  61.7 8.3 %collective-permute-start.15 = (bf16[2,64,896]{2,1,0:T(8,128)(2,1)}, bf16[2,64,896]{2,1,0:T(8,128)(2,1)}, u32[]{:S(2)}, u32[]{:S(2)}) collective-permute-start(bf16[2,64,896]{2,1,0:T(8,128)(2,1)} %copy-done.1), channel_id=1, source_target_pairs={{0,1},{1,2},{2,3},{3,4},{4,5},{5,6},{6,7},{7,0},{8,9},{9,10},{10,1... | collective-permute-start | bytes 688136 | tf_op jit(solution)/shard_map/ppermute | solution.py:37
  70.0 0.9 copy-start.2
  71.0 0.9 copy-start.4
  77.0 2.7 %collective-permute-start.17 = (bf16[512,1024]{1,0:T(8,128)(2,1)S(1)}, bf16[512,1024]{1,0:T(8,128)(2,1)S(1)}, u32[]{:S(2)}, u32[]{:S(2)}) collective-permute-start(bf16[512,1024]{1,0:T(8,128)(2,1)S(1)} %get-tuple-element.28), channel_id=1, source_target_pairs={{0,64},{64,0},{128,192},{192,128},{1,65},{65,1},{129,193},{193,129... | collective-permute-start | bytes 3145736 | tf_op jit(solution)/shard_map/ppermute | solution.py:41
  103.6 12.4 %all-to-all-start.2 = ((f32[4,8,896]{2,1,0:T(8,128)}), f32[4,8,896]{2,1,0:T(8,128)S(1)}, u32[]{:S(2)}, u32[]{:S(2)}) async-start(f32[4,8,896]{2,1,0:T(8,128)} %convert_reduce_fusion), calls=%async_computation.2 | async-start | bytes 229376 | tf_op jit(solution)/shard_map/all_to_all | solution.py:292

commit v19 on v18

--- a/solution.py
+++ b/solution.py
@@ -316,9 +316,8 @@
     sends = pack(odd, pair_kdiff, diff_core, diff_far, stored_kernel_index, kernels)
 
     four, both = bundle(own, far, own_side, far_side)
-    up, down = shift(four, 1, 0, 0), shift(four, -1, 0, 0)
-    steps = shift(both, 0, 0, 1), shift(both, 0, 0, -1)
-    ahead, behind, sends = lax.optimization_barrier((*steps, sends))
+    steps = shift(four, 1, 0, 0), shift(four, -1, 0, 0), shift(both, 0, 0, 1), shift(both, 0, 0, -1)
+    up, down, ahead, behind, sends = lax.optimization_barrier((*steps, sends))
     over = shift(up[:2], 1, 0, 0), shift(down[2:], -1, 0, 0)
     kern = lax.all_to_all(sends, "band", 0, 0, axis_index_groups=over_yx)
     cols = [both, ahead, behind]
@@ -326,7 +325,7 @@
         ahead, behind = shift(ahead, 0, 0, 1), shift(behind, 0, 0, -1)
         cols += [ahead, behind]
     cols.append(shift(ahead, 0, 0, 1))
-    kern = lax.optimization_barrier((kern, ahead, behind))[0]
+    kern, over, cols = lax.optimization_barrier((kern, over, cols))
     half = swap_groups(kern[:, 0], 1)
 
     place = jnp.stack([(y - dy) % NY * NX + (x - dx) % NX for dy in range(NY) for dx in range(NX)])

time: 118 us -> 112 us (0.949)
  waiting for transfers between devices: 41.8 us -> 32.1 us
  starting transfers between devices: 32.7 us -> 36.2 us
  local copies, waits for them, and re-layouts: 5.96 us -> 7.48 us
  blocking collectives: 19 us -> 17.6 us
    all_to_all x1, waiting for transfers between devices: 5.83 us -> 0.01 us  [on_device(): kern = lax.all_to_all(sends, 'band', 0, 0, axis_index_groups=over_yx)]
    ppermute x12, waiting for transfers between devices: 20.7 us -> 15.2 us  [shift(): return lax.ppermute(block, 'band', band_route(dy, dx, dz))]
    unnamed x20 -> x26, local copies, waits for them, and re-layouts: 3.28 us -> 6.19 us
    all_to_all x1, starting transfers between devices: 3.54 us -> 6.34 us  [reduce_windows(): lax.all_to_all(parts, 'band', 0, 0, axis_index_groups=deep)]
    ppermute x5, waiting for transfers between devices: 6.31 us -> 7.99 us  [swap_groups(): return lax.ppermute(block, 'kgrp', [(k, k ^ bit) for k in range(4)])]
    all_to_all x1, blocking collectives: 19 us -> 17.6 us  [reduce_windows(): parts = lax.all_to_all(parts, 'band', 0, 0, axis_index_groups=wide)]
    slice x2, local copies, waits for them, and re-layouts: 1.4 us -> 0.04 us  [on_device(): over = (shift(up[:2], 1, 0, 0), shift(down[2:], -1, 0, 0))]
  transfers between devices with their start and end apart: 20 -> 20, of which waited for: 11 -> 10; matrix products, arithmetic and copies ran while one was open for 2% -> 0% of each run, Pallas kernels for 4% -> 5%
where the time goes in v19:
time: 112 us; the launch traced here: 111 us
  starting transfers between devices  36.2 us (32%)
  waiting for transfers between devices  32.1 us (29%)
  blocking collectives  17.6 us (16%)
  Pallas kernels  14.9 us (13%)
  local copies, waits for them, and re-layouts  7.48 us (7%)
  other arithmetic  1.51 us (1%)
    ppermute x12, starting transfers between devices, shift(): return lax.ppermute(block, 'band', band_route(dy, dx, dz))  18.1 us
    all_to_all x1, blocking collectives, reduce_windows(): parts = lax.all_to_all(parts, 'band', 0, 0, axis_index_groups=wide)  17.6 us
    ppermute x12, waiting for transfers between devices, shift(): return lax.ppermute(block, 'band', band_route(dy, dx, dz))  15.2 us
    all_to_all x1, waiting for transfers between devices, reduce_windows(): lax.all_to_all(parts, 'band', 0, 0, axis_index_groups=deep)  8.9 us
    ppermute x5, waiting for transfers between devices, swap_groups(): return lax.ppermute(block, 'kgrp', [(k, k ^ bit) for k in range(4)])  7.99 us
    all_to_all x1, starting transfers between devices, reduce_windows(): lax.all_to_all(parts, 'band', 0, 0, axis_index_groups=deep)  6.34 us
    unnamed x26, local copies, waits for them, and re-layouts  6.19 us
    all_to_all x1, starting transfers between devices, on_device(): kern = lax.all_to_all(sends, 'band', 0, 0, axis_index_groups=over_yx)  5.69 us
  transfers between devices with their start and end apart: 20, of which 10 were waited for; matrix products, arithmetic and copies ran while one was open for 0% of the time, Pallas kernels for 5%

profile of v19, /device:TPU:6, one launch (start us, length us, event | category | flops | bytes accessed | tf_op | source)
XLA Modules:
  0.0 110.5 jit_solution(13003122055393855890)
XLA Ops:
  0.0 1.0 lay.1.own_ref
  1.0 2.3 %collective-permute-start.4 = (bf16[64,896]{1,0:T(8,128)(2,1)S(1)}, bf16[64,896]{1,0:T(8,128)(2,1)S(1)}, u32[]{:S(2)}, u32[]{:S(2)}) collective-permute-start(bf16[64,896]{1,0:T(8,128)(2,1)S(1)} %lay.1.own_ref), channel_id=1, source_target_pairs={{128,8},{129,9},{130,10},{131,11},{132,12},{133,13},{134,14},{135,... | collective-permute-start | bytes 344072 | tf_op jit(solution)/shard_map/ppermute | solution.py:47
  3.2 2.5 %collective-permute-start.2 = (bf16[64,896]{1,0:T(8,128)(2,1)S(1)}, bf16[64,896]{1,0:T(8,128)(2,1)S(1)}, u32[]{:S(2)}, u32[]{:S(2)}) collective-permute-start(bf16[64,896]{1,0:T(8,128)(2,1)S(1)} %lay.1.own_ref), channel_id=1, source_target_pairs={{0,128},{64,192},{128,0},{192,64},{1,129},{65,193},{129,1},{193,65... | collective-permute-start | bytes 344072 | tf_op jit(solution)/shard_map/ppermute | solution.py:41
  5.7 1.0 collective-permute-start.1
  7.1 3.7 %collective-permute-done.1.far_ref = s32[1]{0:T(128)} collective-permute-done((s32[1]{0:T(128)}, s32[1]{0:T(128)}, u32[]{:S(2)}, u32[]{:S(2)}) %collective-permute-start.1) | collective-permute-done | bytes 36 | tf_op jit(solution)/shard_map/ppermute | solution.py:41
  10.9 3.1 %collective-permute-start.6 = (bf16[4,64,896]{2,1,0:T(8,128)(2,1)S(1)}, bf16[4,64,896]{2,1,0:T(8,128)(2,1)S(1)}, u32[]{:S(2)}, u32[]{:S(2)}) collective-permute-start(bf16[4,64,896]{2,1,0:T(8,128)(2,1)S(1)} %get-tuple-element.34.refs_0_), channel_id=1, source_target_pairs={{0,48},{1,49},{2,50},{3,51},{4,52},{5,53},{6,54},{7,55},{8,56},{9,... | collective-permute-start | bytes 1376264 | tf_op jit(solution)/shard_map/ppermute | solution.py:37
  14.0 5.9 %collective-permute-start.8 = (bf16[2,64,896]{2,1,0:T(8,128)(2,1)S(1)}, bf16[2,64,896]{2,1,0:T(8,128)(2,1)S(1)}, u32[]{:S(2)}, u32[]{:S(2)}) collective-permute-start(bf16[2,64,896]{2,1,0:T(8,128)(2,1)S(1)} %get-tuple-element.43.refs_5_), channel_id=1, source_target_pairs={{0,7},{1,0},{2,1},{3,2},{4,3},{5,4},{6,5},{7,6},{8,15},{9,8},{10,9... | collective-permute-start | bytes 688136 | tf_op jit(solution)/shard_map/ppermute | solution.py:37
  21.2 4.6 %pack.1 = bf16[8,3,64,512]{3,2,1,0:T(8,128)(2,1)} custom-call(s32[1]{0:T(128)} %bitcast.16.odd_ref, s32[1]{0:T(128)S(6)} %copy.5.own_ref, s32[1]{0:T(128)} %collective-permute-done.core_ref, s32[1]{0:T(128)} %collective-permute-done.1.far_ref, s32[8]{0:T(128)S(1)} %copy-done.7, bf16[4,2,64,4096]{3,2,1,0:T(8,128)(2,1)} %kernels_ref.1), custom_call_target="tpu_custom_call" | custom-call | tf_op jit(solution)/shard_map/pack/pallas_call | solution.py:110
  25.8 2.1 %collective-permute-done.7.refs_6_ = bf16[2,64,896]{2,1,0:T(8,128)(2,1)} collective-permute-done((bf16[2,64,896]{2,1,0:T(8,128)(2,1)S(1)}, bf16[2,64,896]{2,1,0:T(8,128)(2,1)}, u32[]{:S(2)}, u32[]{:S(2)}) %collective-permute-start.7) | collective-permute-done | bytes 229408 | tf_op jit(solution)/shard_map/ppermute | solution.py:37
  27.9 5.7 %all-to-all-start = ((bf16[8,3,64,512]{3,2,1,0:T(8,128)(2,1)}), bf16[8,3,64,512]{3,2,1,0:T(8,128)(2,1)S(1)}, u32[]{:S(2)}, u32[]{:S(2)}) async-start(bf16[8,3,64,512]{3,2,1,0:T(8,128)(2,1)} %pack.1), calls=%async_computation | async-start | bytes 3145728 | tf_op jit(solution)/shard_map/all_to_all | solution.py:322
  33.6 3.2 %collective-permute-start.12 = (bf16[2,64,896]{2,1,0:T(8,128)(2,1)S(1)}, bf16[2,64,896]{2,1,0:T(8,128)(2,1)S(1)}, u32[]{:S(2)}, u32[]{:S(2)}) collective-permute-start(bf16[2,64,896]{2,1,0:T(8,128)(2,1)S(1)} %collective-permute-done.8.refs_7_), channel_id=1, source_target_pairs={{0,7},{1,0},{2,1},{3,2},{4,3},{5,4},{6,5},{7,6},{8,15},{9,8},{10,9... | collective-permute-start | bytes 688136 | tf_op jit(solution)/shard_map/ppermute | solution.py:37
  36.9 4.3 %collective-permute-done.11.refs_8_ = bf16[2,64,896]{2,1,0:T(8,128)(2,1)S(1)} collective-permute-done((bf16[2,64,896]{2,1,0:T(8,128)(2,1)}, bf16[2,64,896]{2,1,0:T(8,128)(2,1)S(1)}, u32[]{:S(2)}, u32[]{:S(2)}) %collective-permute-start.11) | collective-permute-done | bytes 229408 | tf_op jit(solution)/shard_map/ppermute | solution.py:37
  41.2 2.6 %collective-permute-start.10 = (bf16[2,64,896]{2,1,0:T(8,128)(2,1)S(1)}, bf16[2,64,896]{2,1,0:T(8,128)(2,1)S(1)}, u32[]{:S(2)}, u32[]{:S(2)}) collective-permute-start(bf16[2,64,896]{2,1,0:T(8,128)(2,1)S(1)} %slice.22), channel_id=1, source_target_pairs={{0,48},{1,49},{2,50},{3,51},{4,52},{5,53},{6,54},{7,55},{8,56},{9,... | collective-permute-start | bytes 688136 | tf_op jit(solution)/shard_map/ppermute | solution.py:37
  43.9 3.3 %collective-permute-start.14 = (bf16[2,64,896]{2,1,0:T(8,128)(2,1)S(1)}, bf16[2,64,896]{2,1,0:T(8,128)(2,1)S(1)}, u32[]{:S(2)}, u32[]{:S(2)}) collective-permute-start(bf16[2,64,896]{2,1,0:T(8,128)(2,1)S(1)} %collective-permute-done.12.refs_9_), channel_id=1, source_target_pairs={{0,7},{1,0},{2,1},{3,2},{4,3},{5,4},{6,5},{7,6},{8,15},{9,8},{10,9... | collective-permute-start | bytes 688136 | tf_op jit(solution)/shard_map/ppermute | solution.py:37
  47.2 1.2 %collective-permute-done.13.refs_10_ = bf16[2,64,896]{2,1,0:T(8,128)(2,1)S(1)} collective-permute-done((bf16[2,64,896]{2,1,0:T(8,128)(2,1)S(1)}, bf16[2,64,896]{2,1,0:T(8,128)(2,1)S(1)}, u32[]{:S(2)}, u32[]{:S(2)}) %collective-permute-start.13) | collective-permute-done | bytes 229408 | tf_op jit(solution)/shard_map/ppermute | solution.py:37
  48.4 0.7 copy-done.1
  49.1 6.3 %collective-permute-done.10.refs_3_ = bf16[2,64,896]{2,1,0:T(8,128)(2,1)S(1)} collective-permute-done((bf16[2,64,896]{2,1,0:T(8,128)(2,1)S(1)}, bf16[2,64,896]{2,1,0:T(8,128)(2,1)S(1)}, u32[]{:S(2)}, u32[]{:S(2)}) %collective-permute-start.10) | collective-permute-done | bytes 229408 | tf_op jit(solution)/shard_map/ppermute | solution.py:37
  55.4 1.3 %collective-permute-done.9.refs_2_ = bf16[2,64,896]{2,1,0:T(8,128)(2,1)S(1)} collective-permute-done((bf16[2,64,896]{2,1,0:T(8,128)(2,1)S(1)}, bf16[2,64,896]{2,1,0:T(8,128)(2,1)S(1)}, u32[]{:S(2)}, u32[]{:S(2)}) %collective-permute-start.9) | collective-permute-done | bytes 229408 | tf_op jit(solution)/shard_map/ppermute | solution.py:37
  57.3 0.7 copy-done.3
  58.7 0.8 slice_bitcast_fusion
  59.7 1.9 %collective-permute-done.16.refs_13_ = bf16[8,64,512]{2,1,0:T(8,128)(2,1)S(1)} collective-permute-done((bf16[8,64,512]{2,1,0:T(8,128)(2,1)}, bf16[8,64,512]{2,1,0:T(8,128)(2,1)S(1)}, u32[]{:S(2)}, u32[]{:S(2)}) %collective-permute-start.16) | collective-permute-done | bytes 524320 | tf_op jit(solution)/shard_map/ppermute | solution.py:41
  61.6 0.9 copy-done.2
  62.6 0.9 copy-done.4
  63.5 0.9 copy-done.6
  64.4 4.7 %mix.1 = (bf16[512,1024]{1,0:T(8,128)(2,1)S(1)}, bf16[512,896]{1,0:T(8,128)(2,1)S(1)}, bf16[512,896]{1,0:T(8,128)(2,1)S(1)}) custom-call(s32[8]{0:T(128)S(1)} %stack.71.place_ref, s32[8]{0:T(128)S(1)} %stack.80.slot_ref, s32[1]{0:T(128)} %bitcast.16.odd_ref, bf16[4,64,896]{2,1,0:T(8,128)(2,1)S(1)} %get-tuple-element.34.refs_0_, ...), custom_call_target="tpu_custom_call" | custom-call | tf_op jit(solution)/shard_map/mix/pallas_call | solution.py:183
  69.9 2.0 %collective-permute-done.17.m_ref = bf16[512,1024]{1,0:T(8,128)(2,1)S(1)} collective-permute-done((bf16[512,1024]{1,0:T(8,128)(2,1)S(1)}, bf16[512,1024]{1,0:T(8,128)(2,1)S(1)}, u32[]{:S(2)}, u32[]{:S(2)}) %collective-permute-start.17) | collective-permute-done | bytes 1048608 | tf_op jit(solution)/shard_map/ppermute | solution.py:41
  71.9 4.0 %project.1 = bf16[64,8,896]{2,1,0:T(8,128)(2,1)S(1)} custom-call(bf16[512,1024]{1,0:T(8,128)(2,1)S(1)} %collective-permute-done.17.m_ref, bf16[432,1024]{1,0:T(8,128)(2,1)S(1)} %get-tuple-element.55.left_ref, bf16[1024,896]{1,0:T(8,128)(2,1)S(1)} %get-tuple-element.56.right_ref), custom_call_target="tpu_custom_call" | custom-call | tf_op jit(solution)/shard_map/project/pallas_call | solution.py:249
  75.9 17.6 %all_to_all.15 = bf16[16,4,8,896]{3,2,1,0:T(8,128)(2,1)S(1)} all-to-all(bf16[16,4,8,896]{3,2,1,0:T(8,128)(2,1)S(1)} %bitcast.22), channel_id=1, replica_groups={{0,1,8,9,16,17,24,25,32,33,40,41,48,49,56,57},{2,3,10,11,18,19,26,27,34..., dimensions={0} | all-to-all | bytes 1835008 | tf_op jit(solution)/shard_map/all_to_all | solution.py:290
  93.5 0.8 convert_reduce_fusion
  94.3 6.3 %all-to-all-start.2 = ((f32[4,8,896]{2,1,0:T(8,128)}), f32[4,8,896]{2,1,0:T(8,128)S(1)}, u32[]{:S(2)}, u32[]{:S(2)}) async-start(f32[4,8,896]{2,1,0:T(8,128)} %convert_reduce_fusion), calls=%async_computation.2 | async-start | bytes 229376 | tf_op jit(solution)/shard_map/all_to_all | solution.py:292
  100.6 8.9 %all-to-all-done.2 = f32[4,8,896]{2,1,0:T(8,128)S(1)} async-done(((f32[4,8,896]{2,1,0:T(8,128)}), f32[4,8,896]{2,1,0:T(8,128)S(1)}, u32[]{:S(2)}, u32[]{:S(2)}) %all-to-all-start.2) | async-done | bytes 114720 | tf_op jit(solution)/shard_map/all_to_all | solution.py:292
  109.8 0.7 fusion.1
  (54 shorter events, 3.7 us)
Async XLA Ops:
  1.0 9.9 %collective-permute-start.4 = (bf16[64,896]{1,0:T(8,128)(2,1)S(1)}, bf16[64,896]{1,0:T(8,128)(2,1)S(1)}, u32[]{:S(2)}, u32[]{:S(2)}) collective-permute-start(bf16[64,896]{1,0:T(8,128)(2,1)S(1)} %lay.1.own_ref), channel_id=1, source_target_pairs={{128,8},{129,9},{130,10},{131,11},{132,12},{133,13},{134,14},{135,... | collective-permute-start | bytes 344072 | tf_op jit(solution)/shard_map/ppermute | solution.py:47
  3.2 7.6 %collective-permute-start.3 = (bf16[64,896]{1,0:T(8,128)(2,1)S(1)}, bf16[64,896]{1,0:T(8,128)(2,1)S(1)}, u32[]{:S(2)}, u32[]{:S(2)}) collective-permute-start(bf16[64,896]{1,0:T(8,128)(2,1)S(1)} %lay.1.own_ref), channel_id=1, source_target_pairs={{0,8},{1,9},{2,10},{3,11},{4,12},{5,13},{6,14},{7,15},{8,0},{9,1},... | collective-permute-start | bytes 344072 | tf_op jit(solution)/shard_map/ppermute | solution.py:37
  3.2 7.6 %collective-permute-start.2 = (bf16[64,896]{1,0:T(8,128)(2,1)S(1)}, bf16[64,896]{1,0:T(8,128)(2,1)S(1)}, u32[]{:S(2)}, u32[]{:S(2)}) collective-permute-start(bf16[64,896]{1,0:T(8,128)(2,1)S(1)} %lay.1.own_ref), channel_id=1, source_target_pairs={{0,128},{64,192},{128,0},{192,64},{1,129},{65,193},{129,1},{193,65... | collective-permute-start | bytes 344072 | tf_op jit(solution)/shard_map/ppermute | solution.py:41
  5.7 1.4 %collective-permute-start = (s32[1]{0:T(128)}, s32[1]{0:T(128)}, u32[]{:S(2)}, u32[]{:S(2)}) collective-permute-start(s32[1]{0:T(128)} %param.6), channel_id=1, source_target_pairs={{0,64},{64,0},{128,192},{192,128},{1,65},{65,1},{129,193},{193,129... | collective-permute-start | bytes 20 | tf_op jit(solution)/shard_map/ppermute | solution.py:41
  5.7 5.1 %collective-permute-start.1 = (s32[1]{0:T(128)}, s32[1]{0:T(128)}, u32[]{:S(2)}, u32[]{:S(2)}) collective-permute-start(s32[1]{0:T(128)} %param.6), channel_id=1, source_target_pairs={{0,128},{64,192},{128,0},{192,64},{1,129},{65,193},{129,1},{193,65... | collective-permute-start | bytes 20 | tf_op jit(solution)/shard_map/ppermute | solution.py:41
  10.9 14.9 %copy-start = (bf16[2,64,896]{2,1,0:T(8,128)(2,1)}, bf16[2,64,896]{2,1,0:T(8,128)(2,1)S(1)}, u32[]{:S(2)}) copy-start(bf16[2,64,896]{2,1,0:T(8,128)(2,1)S(1)} %get-tuple-element.43.refs_5_) | copy-start | bytes 688132
  10.9 17.0 %collective-permute-start.6 = (bf16[4,64,896]{2,1,0:T(8,128)(2,1)S(1)}, bf16[4,64,896]{2,1,0:T(8,128)(2,1)S(1)}, u32[]{:S(2)}, u32[]{:S(2)}) collective-permute-start(bf16[4,64,896]{2,1,0:T(8,128)(2,1)S(1)} %get-tuple-element.34.refs_0_), channel_id=1, source_target_pairs={{0,48},{1,49},{2,50},{3,51},{4,52},{5,53},{6,54},{7,55},{8,56},{9,... | collective-permute-start | bytes 1376264 | tf_op jit(solution)/shard_map/ppermute | solution.py:37
  14.0 13.9 %collective-permute-start.5 = (bf16[4,64,896]{2,1,0:T(8,128)(2,1)S(1)}, bf16[4,64,896]{2,1,0:T(8,128)(2,1)S(1)}, u32[]{:S(2)}, u32[]{:S(2)}) collective-permute-start(bf16[4,64,896]{2,1,0:T(8,128)(2,1)S(1)} %get-tuple-element.34.refs_0_), channel_id=1, source_target_pairs={{0,16},{1,17},{2,18},{3,19},{4,20},{5,21},{6,22},{7,23},{8,24},{9,... | collective-permute-start | bytes 1376264 | tf_op jit(solution)/shard_map/ppermute | solution.py:37
  14.0 11.8 %collective-permute-start.8 = (bf16[2,64,896]{2,1,0:T(8,128)(2,1)S(1)}, bf16[2,64,896]{2,1,0:T(8,128)(2,1)S(1)}, u32[]{:S(2)}, u32[]{:S(2)}) collective-permute-start(bf16[2,64,896]{2,1,0:T(8,128)(2,1)S(1)} %get-tuple-element.43.refs_5_), channel_id=1, source_target_pairs={{0,7},{1,0},{2,1},{3,2},{4,3},{5,4},{6,5},{7,6},{8,15},{9,8},{10,9... | collective-permute-start | bytes 688136 | tf_op jit(solution)/shard_map/ppermute | solution.py:37
  19.9 8.0 %collective-permute-start.7 = (bf16[2,64,896]{2,1,0:T(8,128)(2,1)S(1)}, bf16[2,64,896]{2,1,0:T(8,128)(2,1)}, u32[]{:S(2)}, u32[]{:S(2)}) collective-permute-start(bf16[2,64,896]{2,1,0:T(8,128)(2,1)S(1)} %get-tuple-element.43.refs_5_), channel_id=1, source_target_pairs={{0,1},{1,2},{2,3},{3,4},{4,5},{5,6},{6,7},{7,0},{8,9},{9,10},{10,1... | collective-permute-start | bytes 688136 | tf_op jit(solution)/shard_map/ppermute | solution.py:37
  25.8 15.4 %copy-start.8 = (bf16[2,64,896]{2,1,0:T(8,128)(2,1)}, bf16[2,64,896]{2,1,0:T(8,128)(2,1)S(1)}, u32[]{:S(2)}) copy-start(bf16[2,64,896]{2,1,0:T(8,128)(2,1)S(1)} %collective-permute-done.8.refs_7_) | copy-start | bytes 688132
  27.9 30.7 %all-to-all-start = ((bf16[8,3,64,512]{3,2,1,0:T(8,128)(2,1)}), bf16[8,3,64,512]{3,2,1,0:T(8,128)(2,1)S(1)}, u32[]{:S(2)}, u32[]{:S(2)}) async-start(bf16[8,3,64,512]{3,2,1,0:T(8,128)(2,1)} %pack.1), calls=%async_computation | async-start | bytes 3145728 | tf_op jit(solution)/shard_map/all_to_all | solution.py:322
  33.6 7.6 %collective-permute-start.11 = (bf16[2,64,896]{2,1,0:T(8,128)(2,1)}, bf16[2,64,896]{2,1,0:T(8,128)(2,1)S(1)}, u32[]{:S(2)}, u32[]{:S(2)}) collective-permute-start(bf16[2,64,896]{2,1,0:T(8,128)(2,1)} %collective-permute-done.7.refs_6_), channel_id=1, source_target_pairs={{0,1},{1,2},{2,3},{3,4},{4,5},{5,6},{6,7},{7,0},{8,9},{9,10},{10,1... | collective-permute-start | bytes 688136 | tf_op jit(solution)/shard_map/ppermute | solution.py:37
  33.6 10.3 %collective-permute-start.12 = (bf16[2,64,896]{2,1,0:T(8,128)(2,1)S(1)}, bf16[2,64,896]{2,1,0:T(8,128)(2,1)S(1)}, u32[]{:S(2)}, u32[]{:S(2)}) collective-permute-start(bf16[2,64,896]{2,1,0:T(8,128)(2,1)S(1)} %collective-permute-done.8.refs_7_), channel_id=1, source_target_pairs={{0,7},{1,0},{2,1},{3,2},{4,3},{5,4},{6,5},{7,6},{8,15},{9,8},{10,9... | collective-permute-start | bytes 688136 | tf_op jit(solution)/shard_map/ppermute | solution.py:37
  41.2 15.4 %copy-start.9 = (bf16[2,64,896]{2,1,0:T(8,128)(2,1)}, bf16[2,64,896]{2,1,0:T(8,128)(2,1)S(1)}, u32[]{:S(2)}) copy-start(bf16[2,64,896]{2,1,0:T(8,128)(2,1)S(1)} %collective-permute-done.11.refs_8_) | copy-start | bytes 688132
  41.2 7.2 %collective-permute-start.13 = (bf16[2,64,896]{2,1,0:T(8,128)(2,1)S(1)}, bf16[2,64,896]{2,1,0:T(8,128)(2,1)S(1)}, u32[]{:S(2)}, u32[]{:S(2)}) collective-permute-start(bf16[2,64,896]{2,1,0:T(8,128)(2,1)S(1)} %collective-permute-done.11.refs_8_), channel_id=1, source_target_pairs={{0,1},{1,2},{2,3},{3,4},{4,5},{5,6},{6,7},{7,0},{8,9},{9,10},{10,1... | collective-permute-start | bytes 688136 | tf_op jit(solution)/shard_map/ppermute | solution.py:37
  41.2 14.1 %collective-permute-start.10 = (bf16[2,64,896]{2,1,0:T(8,128)(2,1)S(1)}, bf16[2,64,896]{2,1,0:T(8,128)(2,1)S(1)}, u32[]{:S(2)}, u32[]{:S(2)}) collective-permute-start(bf16[2,64,896]{2,1,0:T(8,128)(2,1)S(1)} %slice.22), channel_id=1, source_target_pairs={{0,48},{1,49},{2,50},{3,51},{4,52},{5,53},{6,54},{7,55},{8,56},{9,... | collective-permute-start | bytes 688136 | tf_op jit(solution)/shard_map/ppermute | solution.py:37
  43.9 12.7 %collective-permute-start.9 = (bf16[2,64,896]{2,1,0:T(8,128)(2,1)S(1)}, bf16[2,64,896]{2,1,0:T(8,128)(2,1)S(1)}, u32[]{:S(2)}, u32[]{:S(2)}) collective-permute-start(bf16[2,64,896]{2,1,0:T(8,128)(2,1)S(1)} %slice.21), channel_id=1, source_target_pairs={{0,16},{1,17},{2,18},{3,19},{4,20},{5,21},{6,22},{7,23},{8,24},{9,... | collective-permute-start | bytes 688136 | tf_op jit(solution)/shard_map/ppermute | solution.py:37
  43.9 12.7 %copy-start.10 = (bf16[2,64,896]{2,1,0:T(8,128)(2,1)}, bf16[2,64,896]{2,1,0:T(8,128)(2,1)S(1)}, u32[]{:S(2)}) copy-start(bf16[2,64,896]{2,1,0:T(8,128)(2,1)S(1)} %collective-permute-done.12.refs_9_) | copy-start | bytes 688132
  43.9 12.7 %collective-permute-start.14 = (bf16[2,64,896]{2,1,0:T(8,128)(2,1)S(1)}, bf16[2,64,896]{2,1,0:T(8,128)(2,1)S(1)}, u32[]{:S(2)}, u32[]{:S(2)}) collective-permute-start(bf16[2,64,896]{2,1,0:T(8,128)(2,1)S(1)} %collective-permute-done.12.refs_9_), channel_id=1, source_target_pairs={{0,7},{1,0},{2,1},{3,2},{4,3},{5,4},{6,5},{7,6},{8,15},{9,8},{10,9... | collective-permute-start | bytes 688136 | tf_op jit(solution)/shard_map/ppermute | solution.py:37
  48.4 9.6 %collective-permute-start.15 = (bf16[2,64,896]{2,1,0:T(8,128)(2,1)S(1)}, bf16[2,64,896]{2,1,0:T(8,128)(2,1)S(1)}, u32[]{:S(2)}, u32[]{:S(2)}) collective-permute-start(bf16[2,64,896]{2,1,0:T(8,128)(2,1)S(1)} %collective-permute-done.13.refs_10_), channel_id=1, source_target_pairs={{0,1},{1,2},{2,3},{3,4},{4,5},{5,6},{6,7},{7,0},{8,9},{9,10},{10,1... | collective-permute-start | bytes 688136 | tf_op jit(solution)/shard_map/ppermute | solution.py:37
  48.4 0.7 copy-start.1
  55.4 1.3 %copy-start.11 = (bf16[2,64,896]{2,1,0:T(8,128)(2,1)}, bf16[2,64,896]{2,1,0:T(8,128)(2,1)S(1)}, u32[]{:S(2)}) copy-start(bf16[2,64,896]{2,1,0:T(8,128)(2,1)S(1)} %collective-permute-done.10.refs_3_) | copy-start | bytes 688132
  56.6 0.7 copy-start.12
  57.3 0.7 copy-start.3
  58.0 0.7 copy-start.5
  59.5 2.1 %collective-permute-start.16 = (bf16[8,64,512]{2,1,0:T(8,128)(2,1)}, bf16[8,64,512]{2,1,0:T(8,128)(2,1)S(1)}, u32[]{:S(2)}, u32[]{:S(2)}) collective-permute-start(bf16[8,64,512]{2,1,0:T(8,128)(2,1)} %slice_bitcast_fusion), channel_id=1, source_target_pairs={{0,64},{64,0},{128,192},{192,128},{1,65},{65,1},{129,193},{193,129... | collective-permute-start | bytes 1572872 | tf_op jit(solution)/shard_map/ppermute | solution.py:41
  61.6 0.9 copy-start.2
  62.6 0.9 copy-start.4
  63.5 0.9 copy-start.6
  69.1 2.7 %collective-permute-start.17 = (bf16[512,1024]{1,0:T(8,128)(2,1)S(1)}, bf16[512,1024]{1,0:T(8,128)(2,1)S(1)}, u32[]{:S(2)}, u32[]{:S(2)}) collective-permute-start(bf16[512,1024]{1,0:T(8,128)(2,1)S(1)} %get-tuple-element.52), channel_id=1, source_target_pairs={{0,64},{64,0},{128,192},{192,128},{1,65},{65,1},{129,193},{193,129... | collective-permute-start | bytes 3145736 | tf_op jit(solution)/shard_map/ppermute | solution.py:41
  94.3 15.2 %all-to-all-start.2 = ((f32[4,8,896]{2,1,0:T(8,128)}), f32[4,8,896]{2,1,0:T(8,128)S(1)}, u32[]{:S(2)}, u32[]{:S(2)}) async-start(f32[4,8,896]{2,1,0:T(8,128)} %convert_reduce_fusion), calls=%async_computation.2 | async-start | bytes 229376 | tf_op jit(solution)/shard_map/all_to_all | solution.py:292
  (1 other events, 0.7 us)

commit v20 on v19

--- a/solution.py
+++ b/solution.py
@@ -14,7 +14,6 @@
 REST = NB - WHOLE
 TAIL = 2 * WHOLE
 LANES = TAIL + 128
-EARLY = 5
 VMEM = 24 * 1024 * 1024
 
 IN_VMEM = pl.BlockSpec(memory_space=pltpu.VMEM)
@@ -118,24 +117,22 @@
     )(odd, own, core, far, stored, away(kernels))
 
 
-def mix_body(place_ref, slot_ref, odd_ref, *refs):
+def density_body(place_ref, slot_ref, *refs):
     four_ref, up_ref, over_here, over_side, down_ref = refs[:5]
-    cols, (half_ref, kern_ref) = refs[5 : 5 + NZ], refs[5 + NZ : 7 + NZ]
-    m_ref, row_ref, col_ref, other_rows, other_cols, sem = refs[7 + NZ :]
+    cols = refs[5 : 5 + NZ]
+    own_ref, far_ref, row_ref, col_ref, other_rows, other_cols, sem = refs[5 + NZ :]
 
     def row_at(dy, side):
         return pl.ds(pl.multiple_of(place_ref[dy * NX + side] * SLAB, SLAB), SLAB)
 
-    def col_at(i):
-        return pl.ds(pl.multiple_of(slot_ref[i] * SLAB, SLAB), SLAB)
-
     moves = []
+    for i, piece in enumerate(cols):
+        at = pl.ds(pl.multiple_of(slot_ref[i] * SLAB, SLAB), SLAB)
+        moves.append((piece.at[0], col_ref.at[at, :]))
+        moves.append((piece.at[1], other_cols.at[at, :]))
     for side, piece in enumerate((over_here, over_side)):
         moves.append((piece.at[0], row_ref.at[row_at(2, side), :]))
         moves.append((piece.at[1], other_rows.at[row_at(2, side), :]))
-    for i, piece in enumerate(cols[:EARLY]):
-        moves.append((piece.at[0], col_ref.at[col_at(i), :]))
-        moves.append((piece.at[1], other_cols.at[col_at(i), :]))
     copies = [pltpu.make_async_copy(*move, sem.at[i]) for i, move in enumerate(moves)]
     for copy in copies:
         copy.start()
@@ -143,53 +140,61 @@
         for side in range(NX):
             row_ref[row_at(dy, side), :] = piece[2 * side]
             other_rows[row_at(dy, side), :] = piece[2 * side + 1]
-    for i in range(EARLY, NZ):
-        col_ref[col_at(i), :] = cols[i][0]
-        other_cols[col_at(i), :] = cols[i][1]
     for copy in copies:
         copy.wait()
-    per = BLOCK // 2
+    for rows, columns, out in ((row_ref, col_ref, own_ref), (other_rows, other_cols, far_ref)):
+        a, b = rows[...], columns[...]
+        out[:, :BLOCK] = dot(a, b, 1, 1)
+        out[:, BLOCK:] = dot(turned(a), b, 1, 1)
+
+
+def density(place, slots, four, up, over, down, cols):
+    product = pltpu.VMEM((BLOCK, 2 * BLOCK), jnp.float32)
+    points = pltpu.VMEM((BLOCK, LANES), jnp.bfloat16)
+    in_hbm = pl.BlockSpec(memory_space=pltpu.HBM)
+    specs = [IN_VMEM] * 2 + [in_hbm] * 2 + [IN_VMEM] + [in_hbm] * NZ
+    arrays = [near(four), near(up), *map(away, over), near(down), *map(away, cols)]
+    return pl.pallas_call(
+        density_body,
+        out_shape=[product, product, points, points],
+        in_specs=[IN_SMEM] * 2 + specs,
+        out_specs=[IN_VMEM] * 4,
+        scratch_shapes=[pltpu.VMEM((BLOCK, LANES), jnp.bfloat16)] * 2
+        + [pltpu.SemaphoreType.DMA((2 * NX + 2 * NZ,))],
+        compiler_params=PARAMS,
+        name="density",
+    )(place, slots, *arrays)
+
+
+def mix_body(odd_ref, own_ref, far_ref, half_ref, kern_ref, m_ref):
     odd = odd_ref[0] == 1
     sign = jnp.where(odd, -1.0, 1.0).astype(jnp.float32)
-    a, a_other = row_ref[...], other_rows[...]
-    a_turned, other_turned = turned(a), turned(a_other)
-    for part in range(2):
-        at = pl.ds(part * per, per)
-        b = col_ref[at, :]
-        p_re, p_im = dot(a, b, 1, 1), dot(a_turned, b, 1, 1)
-        mine = kern_ref[:, 0, :, at].reshape(BLOCK, per)
-        other = half_ref[:, :, at].reshape(BLOCK, per)
+    for i in range(GROUPS):
+        at = pl.ds(i * SLAB, SLAB)
+        mine, other = kern_ref[i, 0], half_ref[i]
         k_re = jnp.where(odd, other, mine).astype(jnp.float32)
         k_im = jnp.where(odd, mine, other).astype(jnp.float32) * sign
+        p_re, p_im = own_ref[at, :BLOCK], own_ref[at, BLOCK:]
         total_re = k_re * p_re - k_im * p_im
         total_im = k_re * p_im + k_im * p_re
-        b = other_cols[at, :]
-        p_re, p_im = dot(a_other, b, 1, 1), dot(other_turned, b, 1, 1)
-        k_re = kern_ref[:, 1, :, at].reshape(BLOCK, per).astype(jnp.float32)
-        k_im = kern_ref[:, 2, :, at].reshape(BLOCK, per).astype(jnp.float32) * -sign
+        k_re = kern_ref[i, 1].astype(jnp.float32)
+        k_im = kern_ref[i, 2].astype(jnp.float32) * -sign
+        p_re, p_im = far_ref[at, :BLOCK], far_ref[at, BLOCK:]
         total_re += k_re * p_re - k_im * p_im
         total_im += k_re * p_im + k_im * p_re
-        m_ref[:, at] = total_re.astype(jnp.bfloat16)
-        m_ref[:, pl.ds(BLOCK + part * per, per)] = total_im.astype(jnp.bfloat16)
-
-
-def mix(place, slots, odd, four, up, over, down, cols, *kerns):
-    points = pltpu.VMEM((BLOCK, LANES), jnp.bfloat16)
-    in_hbm = pl.BlockSpec(memory_space=pltpu.HBM)
-    late = NZ - EARLY
-    specs = [IN_VMEM] * 2 + [in_hbm] * 2 + [IN_VMEM] + [in_hbm] * EARLY + [IN_VMEM] * (late + 2)
-    arrays = [near(four), near(up), *map(away, over), near(down)]
-    arrays += [*map(away, cols[:EARLY]), *map(near, cols[EARLY:]), *map(near, kerns)]
+        m_ref[at, :BLOCK] = total_re.astype(jnp.bfloat16)
+        m_ref[at, BLOCK:] = total_im.astype(jnp.bfloat16)
+
+
+def mix(odd, *arrays):
     return pl.pallas_call(
         mix_body,
-        out_shape=[pltpu.VMEM((BLOCK, 2 * BLOCK), jnp.bfloat16), points, points],
-        in_specs=[IN_SMEM] * 3 + specs,
-        out_specs=[IN_VMEM] * 3,
-        scratch_shapes=[pltpu.VMEM((BLOCK, LANES), jnp.bfloat16)] * 2
-        + [pltpu.SemaphoreType.DMA((2 * NX + 2 * EARLY,))],
+        out_shape=pltpu.VMEM((BLOCK, 2 * BLOCK), jnp.bfloat16),
+        in_specs=[IN_SMEM] + [IN_VMEM] * 4,
+        out_specs=IN_VMEM,
         compiler_params=PARAMS,
         name="mix",
-    )(place, slots, odd, *arrays)
+    )(odd, *map(near, arrays))
 
 
 def prepare_body(row_ref, col_ref, left_ref, right_ref):
@@ -330,8 +335,8 @@
 
     place = jnp.stack([(y - dy) % NY * NX + (x - dx) % NX for dy in range(NY) for dx in range(NX)])
     slots = jnp.stack([(z + i) % NZ for i in (0, -1, 1, -2, 2, -3, 3, -4)])
-    m_out, rows, cols = mix(place, slots, odd, four, up, over, down, cols, half, kern)
-    m_own = swap_groups(m_out, 1)
+    p_own, p_far, rows, cols = density(place, slots, four, up, over, down, cols)
+    m_own = swap_groups(mix(odd, p_own, p_far, half, kern), 1)
     left, right = prepare(rows, cols)
     total = reduce_windows(project(m_own, left, right))
     flat = total.reshape(2, 8 * NB)

time: 112 us -> 105 us (0.938); the launches traced: 111 us -> 105 us
  waiting for transfers between devices: 32.1 us -> 26.9 us
  local copies, waits for them, and re-layouts: 7.48 us -> 3.32 us
  starting transfers between devices: 36.2 us -> 38.4 us
    unnamed x26 -> x18, local copies, waits for them, and re-layouts: 6.19 us -> 2 us
    ppermute x12, starting transfers between devices: 18.1 us -> 21.8 us  [shift(): return lax.ppermute(block, 'band', band_route(dy, dx, dz))]
    ppermute x12, waiting for transfers between devices: 15.2 us -> 12.4 us  [shift(): return lax.ppermute(block, 'band', band_route(dy, dx, dz))]
    ppermute x5, waiting for transfers between devices: 7.99 us -> 5.6 us  [swap_groups(): return lax.ppermute(block, 'kgrp', [(k, k ^ bit) for k in range(4)])]
    ppermute x1, starting transfers between devices: 2.25 us -> 1.02 us  [other_side(): return lax.ppermute(block, ('kgrp', 'band'), both)]
    pallas_call x1 -> x2, Pallas kernels: 4.68 us -> 5.6 us  [the longest x1 4.76 us: density(): pl.pallas_call(density_body, out_shape=[product, product, points, points]...]
  transfers between devices with their start and end apart: 20 -> 20, of which waited for: 10 -> 7; matrix products, arithmetic and copies ran while one was open for 0% -> 0% of each run, Pallas kernels for 5% -> 9%
where the time goes in v20:
time: 105 us
  starting transfers between devices  38.4 us (37%)
  waiting for transfers between devices  26.9 us (26%)
  blocking collectives  18 us (17%)
  Pallas kernels  15.8 us (15%)
  local copies, waits for them, and re-layouts  3.32 us (3%)
  other arithmetic  1.52 us (1%)
    ppermute x12, starting transfers between devices, shift(): return lax.ppermute(block, 'band', band_route(dy, dx, dz))  21.8 us
    all_to_all x1, blocking collectives, reduce_windows(): parts = lax.all_to_all(parts, 'band', 0, 0, axis_index_groups=wide)  18 us
    ppermute x12, waiting for transfers between devices, shift(): return lax.ppermute(block, 'band', band_route(dy, dx, dz))  12.4 us
    all_to_all x1, waiting for transfers between devices, reduce_windows(): lax.all_to_all(parts, 'band', 0, 0, axis_index_groups=deep)  8.91 us
    all_to_all x1, starting transfers between devices, reduce_windows(): lax.all_to_all(parts, 'band', 0, 0, axis_index_groups=deep)  7.42 us
    ppermute x5, waiting for transfers between devices, swap_groups(): return lax.ppermute(block, 'kgrp', [(k, k ^ bit) for k in range(4)])  5.6 us
    pallas_call x1, Pallas kernels, density(): pl.pallas_call(density_body, out_shape=[product, product, points, points]...  4.76 us
    all_to_all x1, starting transfers between devices, on_device(): kern = lax.all_to_all(sends, 'band', 0, 0, axis_index_groups=over_yx)  4.73 us
  transfers between devices with their start and end apart: 20, of which 7 were waited for; matrix products, arithmetic and copies ran while one was open for 0% of the time, Pallas kernels for 9%

profile of v20, /device:TPU:6, one launch (start us, length us, event | category | flops | bytes accessed | tf_op | source)
XLA Modules:
  0.0 104.8 jit_solution(11044100518629933633)
XLA Ops:
  0.0 1.0 lay.1.own_ref
  1.0 1.4 %collective-permute-start.2 = (bf16[64,896]{1,0:T(8,128)(2,1)S(1)}, bf16[64,896]{1,0:T(8,128)(2,1)S(1)}, u32[]{:S(2)}, u32[]{:S(2)}) collective-permute-start(bf16[64,896]{1,0:T(8,128)(2,1)S(1)} %lay.1.own_ref), channel_id=1, source_target_pairs={{0,128},{64,192},{128,0},{192,64},{1,129},{65,193},{129,1},{193,65... | collective-permute-start | bytes 344072 | tf_op jit(solution)/shard_map/ppermute | solution.py:40
  2.4 1.7 %collective-permute-start.3 = (bf16[64,896]{1,0:T(8,128)(2,1)S(1)}, bf16[64,896]{1,0:T(8,128)(2,1)S(1)}, u32[]{:S(2)}, u32[]{:S(2)}) collective-permute-start(bf16[64,896]{1,0:T(8,128)(2,1)S(1)} %lay.1.own_ref), channel_id=1, source_target_pairs={{0,8},{1,9},{2,10},{3,11},{4,12},{5,13},{6,14},{7,15},{8,0},{9,1},... | collective-permute-start | bytes 344072 | tf_op jit(solution)/shard_map/ppermute | solution.py:36
  4.1 1.0 collective-permute-start.4
  5.1 1.4 %collective-permute-start.1 = (s32[1]{0:T(128)}, s32[1]{0:T(128)}, u32[]{:S(2)}, u32[]{:S(2)}) collective-permute-start(s32[1]{0:T(128)} %param.6), channel_id=1, source_target_pairs={{0,128},{64,192},{128,0},{192,64},{1,129},{65,193},{129,1},{193,65... | collective-permute-start | bytes 20 | tf_op jit(solution)/shard_map/ppermute | solution.py:40
  6.5 3.9 %collective-permute-done.1.far_ref = s32[1]{0:T(128)} collective-permute-done((s32[1]{0:T(128)}, s32[1]{0:T(128)}, u32[]{:S(2)}, u32[]{:S(2)}) %collective-permute-start.1) | collective-permute-done | bytes 36 | tf_op jit(solution)/shard_map/ppermute | solution.py:40
  10.5 1.7 %collective-permute-start.5 = (bf16[4,64,896]{2,1,0:T(8,128)(2,1)S(1)}, bf16[4,64,896]{2,1,0:T(8,128)(2,1)S(1)}, u32[]{:S(2)}, u32[]{:S(2)}) collective-permute-start(bf16[4,64,896]{2,1,0:T(8,128)(2,1)S(1)} %get-tuple-element.35.refs_0_), channel_id=1, source_target_pairs={{0,16},{1,17},{2,18},{3,19},{4,20},{5,21},{6,22},{7,23},{8,24},{9,... | collective-permute-start | bytes 1376264 | tf_op jit(solution)/shard_map/ppermute | solution.py:36
  12.1 1.7 %collective-permute-start.6 = (bf16[4,64,896]{2,1,0:T(8,128)(2,1)S(1)}, bf16[4,64,896]{2,1,0:T(8,128)(2,1)S(1)}, u32[]{:S(2)}, u32[]{:S(2)}) collective-permute-start(bf16[4,64,896]{2,1,0:T(8,128)(2,1)S(1)} %get-tuple-element.35.refs_0_), channel_id=1, source_target_pairs={{0,48},{1,49},{2,50},{3,51},{4,52},{5,53},{6,54},{7,55},{8,56},{9,... | collective-permute-start | bytes 1376264 | tf_op jit(solution)/shard_map/ppermute | solution.py:36
  13.8 1.9 %collective-permute-start.7 = (bf16[2,64,896]{2,1,0:T(8,128)(2,1)S(1)}, bf16[2,64,896]{2,1,0:T(8,128)(2,1)S(1)}, u32[]{:S(2)}, u32[]{:S(2)}) collective-permute-start(bf16[2,64,896]{2,1,0:T(8,128)(2,1)S(1)} %get-tuple-element.44.refs_5_), channel_id=1, source_target_pairs={{0,1},{1,2},{2,3},{3,4},{4,5},{5,6},{6,7},{7,0},{8,9},{9,10},{10,1... | collective-permute-start | bytes 688136 | tf_op jit(solution)/shard_map/ppermute | solution.py:36
  15.7 3.9 %collective-permute-start.8 = (bf16[2,64,896]{2,1,0:T(8,128)(2,1)S(1)}, bf16[2,64,896]{2,1,0:T(8,128)(2,1)}, u32[]{:S(2)}, u32[]{:S(2)}) collective-permute-start(bf16[2,64,896]{2,1,0:T(8,128)(2,1)S(1)} %get-tuple-element.44.refs_5_), channel_id=1, source_target_pairs={{0,7},{1,0},{2,1},{3,2},{4,3},{5,4},{6,5},{7,6},{8,15},{9,8},{10,9... | collective-permute-start | bytes 688136 | tf_op jit(solution)/shard_map/ppermute | solution.py:36
  20.3 0.6 copy-done.1
  21.0 4.6 %pack.1 = bf16[8,3,64,512]{3,2,1,0:T(8,128)(2,1)} custom-call(s32[1]{0:T(128)} %bitcast.odd_ref, s32[1]{0:T(128)S(6)} %copy.5.own_ref, s32[1]{0:T(128)} %collective-permute-done.core_ref, s32[1]{0:T(128)} %collective-permute-done.1.far_ref, s32[8]{0:T(128)S(1)} %copy-done.1, bf16[4,2,64,4096]{3,2,1,0:T(8,128)(2,1)} %kernels_ref.1), custom_call_target="tpu_custom_call" | custom-call | tf_op jit(solution)/shard_map/pack/pallas_call | solution.py:109
  25.6 4.7 %all-to-all-start = ((bf16[8,3,64,512]{3,2,1,0:T(8,128)(2,1)}), bf16[8,3,64,512]{3,2,1,0:T(8,128)(2,1)S(1)}, u32[]{:S(2)}, u32[]{:S(2)}) async-start(bf16[8,3,64,512]{3,2,1,0:T(8,128)(2,1)} %pack.1), calls=%async_computation | async-start | bytes 3145728 | tf_op jit(solution)/shard_map/all_to_all | solution.py:327
  30.3 0.8 collective-permute-start.11
  31.2 3.9 %collective-permute-start.12 = (bf16[2,64,896]{2,1,0:T(8,128)(2,1)}, bf16[2,64,896]{2,1,0:T(8,128)(2,1)S(1)}, u32[]{:S(2)}, u32[]{:S(2)}) collective-permute-start(bf16[2,64,896]{2,1,0:T(8,128)(2,1)} %collective-permute-done.8.refs_7_), channel_id=1, source_target_pairs={{0,7},{1,0},{2,1},{3,2},{4,3},{5,4},{6,5},{7,6},{8,15},{9,8},{10,9... | collective-permute-start | bytes 688136 | tf_op jit(solution)/shard_map/ppermute | solution.py:36
  35.1 4.0 %collective-permute-done.11.refs_8_ = bf16[2,64,896]{2,1,0:T(8,128)(2,1)S(1)} collective-permute-done((bf16[2,64,896]{2,1,0:T(8,128)(2,1)S(1)}, bf16[2,64,896]{2,1,0:T(8,128)(2,1)S(1)}, u32[]{:S(2)}, u32[]{:S(2)}) %collective-permute-start.11) | collective-permute-done | bytes 229408 | tf_op jit(solution)/shard_map/ppermute | solution.py:36
  39.1 2.8 %collective-permute-start.10 = (bf16[2,64,896]{2,1,0:T(8,128)(2,1)S(1)}, bf16[2,64,896]{2,1,0:T(8,128)(2,1)S(1)}, u32[]{:S(2)}, u32[]{:S(2)}) collective-permute-start(bf16[2,64,896]{2,1,0:T(8,128)(2,1)S(1)} %slice.22), channel_id=1, source_target_pairs={{0,48},{1,49},{2,50},{3,51},{4,52},{5,53},{6,54},{7,55},{8,56},{9,... | collective-permute-start | bytes 688136 | tf_op jit(solution)/shard_map/ppermute | solution.py:36
  42.0 3.3 %collective-permute-start.14 = (bf16[2,64,896]{2,1,0:T(8,128)(2,1)S(1)}, bf16[2,64,896]{2,1,0:T(8,128)(2,1)S(1)}, u32[]{:S(2)}, u32[]{:S(2)}) collective-permute-start(bf16[2,64,896]{2,1,0:T(8,128)(2,1)S(1)} %collective-permute-done.12.refs_9_), channel_id=1, source_target_pairs={{0,7},{1,0},{2,1},{3,2},{4,3},{5,4},{6,5},{7,6},{8,15},{9,8},{10,9... | collective-permute-start | bytes 688136 | tf_op jit(solution)/shard_map/ppermute | solution.py:36
  45.3 1.0 collective-permute-done.13.refs_10_
  46.4 6.1 %collective-permute-done.10.refs_3_ = bf16[2,64,896]{2,1,0:T(8,128)(2,1)S(1)} collective-permute-done((bf16[2,64,896]{2,1,0:T(8,128)(2,1)S(1)}, bf16[2,64,896]{2,1,0:T(8,128)(2,1)S(1)}, u32[]{:S(2)}, u32[]{:S(2)}) %collective-permute-start.10) | collective-permute-done | bytes 229408 | tf_op jit(solution)/shard_map/ppermute | solution.py:36
  52.5 1.3 %collective-permute-done.9.refs_2_ = bf16[2,64,896]{2,1,0:T(8,128)(2,1)S(1)} collective-permute-done((bf16[2,64,896]{2,1,0:T(8,128)(2,1)S(1)}, bf16[2,64,896]{2,1,0:T(8,128)(2,1)S(1)}, u32[]{:S(2)}, u32[]{:S(2)}) %collective-permute-start.9) | collective-permute-done | bytes 229408 | tf_op jit(solution)/shard_map/ppermute | solution.py:36
  54.4 0.7 copy-done.8
  55.1 0.8 slice_bitcast_fusion
  56.2 4.8 %density.1 = (f32[512,1024]{1,0:T(8,128)S(1)}, f32[512,1024]{1,0:T(8,128)S(1)}, bf16[512,896]{1,0:T(8,128)(2,1)S(1)}, bf16[512,896]{1,0:T(8,128)(2,1)S(1)}) custom-call(s32[8]{0:T(128)S(1)} %stack.71.place_ref, s32[8]{0:T(128)S(1)} %stack.80.slot_ref, bf16[4,64,896]{2,1,0:T(8,128)(2,1)S(1)} %get-tuple-element.35.refs_0_, ...), custom_call_target="tpu_custom_call" | custom-call | tf_op jit(solution)/shard_map/density/pallas_call | solution.py:157
  60.9 0.8 mix.1
  62.9 1.7 %collective-permute-done.17.m_ref = bf16[512,1024]{1,0:T(8,128)(2,1)S(1)} collective-permute-done((bf16[512,1024]{1,0:T(8,128)(2,1)S(1)}, bf16[512,1024]{1,0:T(8,128)(2,1)S(1)}, u32[]{:S(2)}, u32[]{:S(2)}) %collective-permute-start.17) | collective-permute-done | bytes 1048608 | tf_op jit(solution)/shard_map/ppermute | solution.py:40
  64.7 4.0 %project.1 = bf16[64,8,896]{2,1,0:T(8,128)(2,1)S(1)} custom-call(bf16[512,1024]{1,0:T(8,128)(2,1)S(1)} %collective-permute-done.17.m_ref, bf16[432,1024]{1,0:T(8,128)(2,1)S(1)} %get-tuple-element.57.left_ref, bf16[1024,896]{1,0:T(8,128)(2,1)S(1)} %get-tuple-element.58.right_ref), custom_call_target="tpu_custom_call" | custom-call | tf_op jit(solution)/shard_map/project/pallas_call | solution.py:254
  68.7 18.0 %all_to_all.15 = bf16[16,4,8,896]{3,2,1,0:T(8,128)(2,1)S(1)} all-to-all(bf16[16,4,8,896]{3,2,1,0:T(8,128)(2,1)S(1)} %bitcast.22), channel_id=1, replica_groups={{0,1,8,9,16,17,24,25,32,33,40,41,48,49,56,57},{2,3,10,11,18,19,26,27,34..., dimensions={0} | all-to-all | bytes 1835008 | tf_op jit(solution)/shard_map/all_to_all | solution.py:295
  86.7 0.8 convert_reduce_fusion
  87.4 7.4 %all-to-all-start.2 = ((f32[4,8,896]{2,1,0:T(8,128)}), f32[4,8,896]{2,1,0:T(8,128)S(1)}, u32[]{:S(2)}, u32[]{:S(2)}) async-start(f32[4,8,896]{2,1,0:T(8,128)} %convert_reduce_fusion), calls=%async_computation.2 | async-start | bytes 229376 | tf_op jit(solution)/shard_map/all_to_all | solution.py:297
  94.9 8.9 %all-to-all-done.2 = f32[4,8,896]{2,1,0:T(8,128)S(1)} async-done(((f32[4,8,896]{2,1,0:T(8,128)}), f32[4,8,896]{2,1,0:T(8,128)S(1)}, u32[]{:S(2)}, u32[]{:S(2)}) %all-to-all-start.2) | async-done | bytes 114720 | tf_op jit(solution)/shard_map/all_to_all | solution.py:297
  104.1 0.7 fusion.1
  (47 shorter events, 2.5 us)
Async XLA Ops:
  1.0 9.4 %collective-permute-start.2 = (bf16[64,896]{1,0:T(8,128)(2,1)S(1)}, bf16[64,896]{1,0:T(8,128)(2,1)S(1)}, u32[]{:S(2)}, u32[]{:S(2)}) collective-permute-start(bf16[64,896]{1,0:T(8,128)(2,1)S(1)} %lay.1.own_ref), channel_id=1, source_target_pairs={{0,128},{64,192},{128,0},{192,64},{1,129},{65,193},{129,1},{193,65... | collective-permute-start | bytes 344072 | tf_op jit(solution)/shard_map/ppermute | solution.py:40
  2.4 8.0 %collective-permute-start.3 = (bf16[64,896]{1,0:T(8,128)(2,1)S(1)}, bf16[64,896]{1,0:T(8,128)(2,1)S(1)}, u32[]{:S(2)}, u32[]{:S(2)}) collective-permute-start(bf16[64,896]{1,0:T(8,128)(2,1)S(1)} %lay.1.own_ref), channel_id=1, source_target_pairs={{0,8},{1,9},{2,10},{3,11},{4,12},{5,13},{6,14},{7,15},{8,0},{9,1},... | collective-permute-start | bytes 344072 | tf_op jit(solution)/shard_map/ppermute | solution.py:36
  4.1 6.3 %collective-permute-start.4 = (bf16[64,896]{1,0:T(8,128)(2,1)S(1)}, bf16[64,896]{1,0:T(8,128)(2,1)S(1)}, u32[]{:S(2)}, u32[]{:S(2)}) collective-permute-start(bf16[64,896]{1,0:T(8,128)(2,1)S(1)} %lay.1.own_ref), channel_id=1, source_target_pairs={{128,8},{129,9},{130,10},{131,11},{132,12},{133,13},{134,14},{135,... | collective-permute-start | bytes 344072 | tf_op jit(solution)/shard_map/ppermute | solution.py:46
  5.1 1.4 %collective-permute-start = (s32[1]{0:T(128)}, s32[1]{0:T(128)}, u32[]{:S(2)}, u32[]{:S(2)}) collective-permute-start(s32[1]{0:T(128)} %param.6), channel_id=1, source_target_pairs={{0,64},{64,0},{128,192},{192,128},{1,65},{65,1},{129,193},{193,129... | collective-permute-start | bytes 20 | tf_op jit(solution)/shard_map/ppermute | solution.py:40
  5.1 5.3 %collective-permute-start.1 = (s32[1]{0:T(128)}, s32[1]{0:T(128)}, u32[]{:S(2)}, u32[]{:S(2)}) collective-permute-start(s32[1]{0:T(128)} %param.6), channel_id=1, source_target_pairs={{0,128},{64,192},{128,0},{192,64},{1,129},{65,193},{129,1},{193,65... | collective-permute-start | bytes 20 | tf_op jit(solution)/shard_map/ppermute | solution.py:40
  10.5 15.1 %copy-start = (bf16[2,64,896]{2,1,0:T(8,128)(2,1)}, bf16[2,64,896]{2,1,0:T(8,128)(2,1)S(1)}, u32[]{:S(2)}) copy-start(bf16[2,64,896]{2,1,0:T(8,128)(2,1)S(1)} %get-tuple-element.44.refs_5_) | copy-start | bytes 688132
  10.5 15.1 %collective-permute-start.5 = (bf16[4,64,896]{2,1,0:T(8,128)(2,1)S(1)}, bf16[4,64,896]{2,1,0:T(8,128)(2,1)S(1)}, u32[]{:S(2)}, u32[]{:S(2)}) collective-permute-start(bf16[4,64,896]{2,1,0:T(8,128)(2,1)S(1)} %get-tuple-element.35.refs_0_), channel_id=1, source_target_pairs={{0,16},{1,17},{2,18},{3,19},{4,20},{5,21},{6,22},{7,23},{8,24},{9,... | collective-permute-start | bytes 1376264 | tf_op jit(solution)/shard_map/ppermute | solution.py:36
  12.1 13.5 %collective-permute-start.6 = (bf16[4,64,896]{2,1,0:T(8,128)(2,1)S(1)}, bf16[4,64,896]{2,1,0:T(8,128)(2,1)S(1)}, u32[]{:S(2)}, u32[]{:S(2)}) collective-permute-start(bf16[4,64,896]{2,1,0:T(8,128)(2,1)S(1)} %get-tuple-element.35.refs_0_), channel_id=1, source_target_pairs={{0,48},{1,49},{2,50},{3,51},{4,52},{5,53},{6,54},{7,55},{8,56},{9,... | collective-permute-start | bytes 1376264 | tf_op jit(solution)/shard_map/ppermute | solution.py:36
  13.8 11.8 %collective-permute-start.7 = (bf16[2,64,896]{2,1,0:T(8,128)(2,1)S(1)}, bf16[2,64,896]{2,1,0:T(8,128)(2,1)S(1)}, u32[]{:S(2)}, u32[]{:S(2)}) collective-permute-start(bf16[2,64,896]{2,1,0:T(8,128)(2,1)S(1)} %get-tuple-element.44.refs_5_), channel_id=1, source_target_pairs={{0,1},{1,2},{2,3},{3,4},{4,5},{5,6},{6,7},{7,0},{8,9},{9,10},{10,1... | collective-permute-start | bytes 688136 | tf_op jit(solution)/shard_map/ppermute | solution.py:36
  15.7 9.9 %collective-permute-start.8 = (bf16[2,64,896]{2,1,0:T(8,128)(2,1)S(1)}, bf16[2,64,896]{2,1,0:T(8,128)(2,1)}, u32[]{:S(2)}, u32[]{:S(2)}) collective-permute-start(bf16[2,64,896]{2,1,0:T(8,128)(2,1)S(1)} %get-tuple-element.44.refs_5_), channel_id=1, source_target_pairs={{0,7},{1,0},{2,1},{3,2},{4,3},{5,4},{6,5},{7,6},{8,15},{9,8},{10,9... | collective-permute-start | bytes 688136 | tf_op jit(solution)/shard_map/ppermute | solution.py:36
  20.3 0.7 copy-start.1
  25.6 13.6 %copy-start.2 = (bf16[2,64,896]{2,1,0:T(8,128)(2,1)}, bf16[2,64,896]{2,1,0:T(8,128)(2,1)S(1)}, u32[]{:S(2)}) copy-start(bf16[2,64,896]{2,1,0:T(8,128)(2,1)S(1)} %collective-permute-done.7.refs_6_) | copy-start | bytes 688132
  25.6 29.5 %all-to-all-start = ((bf16[8,3,64,512]{3,2,1,0:T(8,128)(2,1)}), bf16[8,3,64,512]{3,2,1,0:T(8,128)(2,1)S(1)}, u32[]{:S(2)}, u32[]{:S(2)}) async-start(bf16[8,3,64,512]{3,2,1,0:T(8,128)(2,1)} %pack.1), calls=%async_computation | async-start | bytes 3145728 | tf_op jit(solution)/shard_map/all_to_all | solution.py:327
  30.3 8.8 %collective-permute-start.11 = (bf16[2,64,896]{2,1,0:T(8,128)(2,1)S(1)}, bf16[2,64,896]{2,1,0:T(8,128)(2,1)S(1)}, u32[]{:S(2)}, u32[]{:S(2)}) collective-permute-start(bf16[2,64,896]{2,1,0:T(8,128)(2,1)S(1)} %collective-permute-done.7.refs_6_), channel_id=1, source_target_pairs={{0,1},{1,2},{2,3},{3,4},{4,5},{5,6},{6,7},{7,0},{8,9},{9,10},{10,1... | collective-permute-start | bytes 688136 | tf_op jit(solution)/shard_map/ppermute | solution.py:36
  31.2 10.8 %collective-permute-start.12 = (bf16[2,64,896]{2,1,0:T(8,128)(2,1)}, bf16[2,64,896]{2,1,0:T(8,128)(2,1)S(1)}, u32[]{:S(2)}, u32[]{:S(2)}) collective-permute-start(bf16[2,64,896]{2,1,0:T(8,128)(2,1)} %collective-permute-done.8.refs_7_), channel_id=1, source_target_pairs={{0,7},{1,0},{2,1},{3,2},{4,3},{5,4},{6,5},{7,6},{8,15},{9,8},{10,9... | collective-permute-start | bytes 688136 | tf_op jit(solution)/shard_map/ppermute | solution.py:36
  39.1 14.7 %copy-start.3 = (bf16[2,64,896]{2,1,0:T(8,128)(2,1)}, bf16[2,64,896]{2,1,0:T(8,128)(2,1)S(1)}, u32[]{:S(2)}) copy-start(bf16[2,64,896]{2,1,0:T(8,128)(2,1)S(1)} %collective-permute-done.11.refs_8_) | copy-start | bytes 688132
  39.1 7.2 %collective-permute-start.13 = (bf16[2,64,896]{2,1,0:T(8,128)(2,1)S(1)}, bf16[2,64,896]{2,1,0:T(8,128)(2,1)S(1)}, u32[]{:S(2)}, u32[]{:S(2)}) collective-permute-start(bf16[2,64,896]{2,1,0:T(8,128)(2,1)S(1)} %collective-permute-done.11.refs_8_), channel_id=1, source_target_pairs={{0,1},{1,2},{2,3},{3,4},{4,5},{5,6},{6,7},{7,0},{8,9},{9,10},{10,1... | collective-permute-start | bytes 688136 | tf_op jit(solution)/shard_map/ppermute | solution.py:36
  39.1 13.3 %collective-permute-start.10 = (bf16[2,64,896]{2,1,0:T(8,128)(2,1)S(1)}, bf16[2,64,896]{2,1,0:T(8,128)(2,1)S(1)}, u32[]{:S(2)}, u32[]{:S(2)}) collective-permute-start(bf16[2,64,896]{2,1,0:T(8,128)(2,1)S(1)} %slice.22), channel_id=1, source_target_pairs={{0,48},{1,49},{2,50},{3,51},{4,52},{5,53},{6,54},{7,55},{8,56},{9,... | collective-permute-start | bytes 688136 | tf_op jit(solution)/shard_map/ppermute | solution.py:36
  41.9 11.8 %collective-permute-start.9 = (bf16[2,64,896]{2,1,0:T(8,128)(2,1)S(1)}, bf16[2,64,896]{2,1,0:T(8,128)(2,1)S(1)}, u32[]{:S(2)}, u32[]{:S(2)}) collective-permute-start(bf16[2,64,896]{2,1,0:T(8,128)(2,1)S(1)} %slice.21), channel_id=1, source_target_pairs={{0,16},{1,17},{2,18},{3,19},{4,20},{5,21},{6,22},{7,23},{8,24},{9,... | collective-permute-start | bytes 688136 | tf_op jit(solution)/shard_map/ppermute | solution.py:36
  42.0 11.7 %copy-start.4 = (bf16[2,64,896]{2,1,0:T(8,128)(2,1)}, bf16[2,64,896]{2,1,0:T(8,128)(2,1)S(1)}, u32[]{:S(2)}) copy-start(bf16[2,64,896]{2,1,0:T(8,128)(2,1)S(1)} %collective-permute-done.12.refs_9_) | copy-start | bytes 688132
  42.0 11.7 %collective-permute-start.14 = (bf16[2,64,896]{2,1,0:T(8,128)(2,1)S(1)}, bf16[2,64,896]{2,1,0:T(8,128)(2,1)S(1)}, u32[]{:S(2)}, u32[]{:S(2)}) collective-permute-start(bf16[2,64,896]{2,1,0:T(8,128)(2,1)S(1)} %collective-permute-done.12.refs_9_), channel_id=1, source_target_pairs={{0,7},{1,0},{2,1},{3,2},{4,3},{5,4},{6,5},{7,6},{8,15},{9,8},{10,9... | collective-permute-start | bytes 688136 | tf_op jit(solution)/shard_map/ppermute | solution.py:36
  46.3 7.4 %copy-start.5 = (bf16[2,64,896]{2,1,0:T(8,128)(2,1)}, bf16[2,64,896]{2,1,0:T(8,128)(2,1)S(1)}, u32[]{:S(2)}) copy-start(bf16[2,64,896]{2,1,0:T(8,128)(2,1)S(1)} %collective-permute-done.13.refs_10_) | copy-start | bytes 688132
  46.3 8.8 %collective-permute-start.15 = (bf16[2,64,896]{2,1,0:T(8,128)(2,1)S(1)}, bf16[2,64,896]{2,1,0:T(8,128)(2,1)}, u32[]{:S(2)}, u32[]{:S(2)}) collective-permute-start(bf16[2,64,896]{2,1,0:T(8,128)(2,1)S(1)} %collective-permute-done.13.refs_10_), channel_id=1, source_target_pairs={{0,1},{1,2},{2,3},{3,4},{4,5},{5,6},{6,7},{7,0},{8,9},{9,10},{10,1... | collective-permute-start | bytes 688136 | tf_op jit(solution)/shard_map/ppermute | solution.py:36
  52.5 1.3 %copy-start.6 = (bf16[2,64,896]{2,1,0:T(8,128)(2,1)}, bf16[2,64,896]{2,1,0:T(8,128)(2,1)S(1)}, u32[]{:S(2)}) copy-start(bf16[2,64,896]{2,1,0:T(8,128)(2,1)S(1)} %collective-permute-done.10.refs_3_) | copy-start | bytes 688132
  53.8 0.7 copy-start.7
  54.4 0.7 copy-start.8
  56.0 4.9 %collective-permute-start.16 = (bf16[8,64,512]{2,1,0:T(8,128)(2,1)}, bf16[8,64,512]{2,1,0:T(8,128)(2,1)S(1)}, u32[]{:S(2)}, u32[]{:S(2)}) collective-permute-start(bf16[8,64,512]{2,1,0:T(8,128)(2,1)} %slice_bitcast_fusion), channel_id=1, source_target_pairs={{0,64},{64,0},{128,192},{192,128},{1,65},{65,1},{129,193},{193,129... | collective-permute-start | bytes 1572872 | tf_op jit(solution)/shard_map/ppermute | solution.py:40
  61.8 2.9 %collective-permute-start.17 = (bf16[512,1024]{1,0:T(8,128)(2,1)S(1)}, bf16[512,1024]{1,0:T(8,128)(2,1)S(1)}, u32[]{:S(2)}, u32[]{:S(2)}) collective-permute-start(bf16[512,1024]{1,0:T(8,128)(2,1)S(1)} %mix.1), channel_id=1, source_target_pairs={{0,64},{64,0},{128,192},{192,128},{1,65},{65,1},{129,193},{193,129... | collective-permute-start | bytes 3145736 | tf_op jit(solution)/shard_map/ppermute | solution.py:40
  87.4 16.3 %all-to-all-start.2 = ((f32[4,8,896]{2,1,0:T(8,128)}), f32[4,8,896]{2,1,0:T(8,128)S(1)}, u32[]{:S(2)}, u32[]{:S(2)}) async-start(f32[4,8,896]{2,1,0:T(8,128)} %convert_reduce_fusion), calls=%async_computation.2 | async-start | bytes 229376 | tf_op jit(solution)/shard_map/all_to_all | solution.py:297

commit v21 on v20

--- a/solution.py
+++ b/solution.py
@@ -14,6 +14,7 @@
 REST = NB - WHOLE
 TAIL = 2 * WHOLE
 LANES = TAIL + 128
+Z_ORDER = (0, -1, 1, -2, 2, -3, 3, -4)
 VMEM = 24 * 1024 * 1024
 
 IN_VMEM = pl.BlockSpec(memory_space=pltpu.VMEM)
@@ -117,22 +118,25 @@
     )(odd, own, core, far, stored, away(kernels))
 
 
-def density_body(place_ref, slot_ref, *refs):
+def density_body(band_ref, *refs):
     four_ref, up_ref, over_here, over_side, down_ref = refs[:5]
     cols = refs[5 : 5 + NZ]
     own_ref, far_ref, row_ref, col_ref, other_rows, other_cols, sem = refs[5 + NZ :]
 
+    band = band_ref[0]
+    y, x, z = band // (NX * NZ), band // NZ % NX, band % NZ
+
     def row_at(dy, side):
-        return pl.ds(pl.multiple_of(place_ref[dy * NX + side] * SLAB, SLAB), SLAB)
+        place = (y + NY - dy) % NY * NX + (x + side) % NX
+        return pl.ds(pl.multiple_of(place * SLAB, SLAB), SLAB)
+
+    def col_at(dz):
+        return pl.ds(pl.multiple_of((z + NZ + dz) % NZ * SLAB, SLAB), SLAB)
 
     moves = []
-    for i, piece in enumerate(cols):
-        at = pl.ds(pl.multiple_of(slot_ref[i] * SLAB, SLAB), SLAB)
-        moves.append((piece.at[0], col_ref.at[at, :]))
-        moves.append((piece.at[1], other_cols.at[at, :]))
-    for side, piece in enumerate((over_here, over_side)):
-        moves.append((piece.at[0], row_ref.at[row_at(2, side), :]))
-        moves.append((piece.at[1], other_rows.at[row_at(2, side), :]))
+    for piece, dz in zip(cols[:-1], Z_ORDER):
+        moves.append((piece.at[0], col_ref.at[col_at(dz), :]))
+        moves.append((piece.at[1], other_cols.at[col_at(dz), :]))
     copies = [pltpu.make_async_copy(*move, sem.at[i]) for i, move in enumerate(moves)]
     for copy in copies:
         copy.start()
@@ -140,6 +144,11 @@
         for side in range(NX):
             row_ref[row_at(dy, side), :] = piece[2 * side]
             other_rows[row_at(dy, side), :] = piece[2 * side + 1]
+    for side, piece in enumerate((over_here, over_side)):
+        row_ref[row_at(2, side), :] = piece[0]
+        other_rows[row_at(2, side), :] = piece[1]
+    col_ref[col_at(Z_ORDER[-1]), :] = cols[-1][0]
+    other_cols[col_at(Z_ORDER[-1]), :] = cols[-1][1]
     for copy in copies:
         copy.wait()
     for rows, columns, out in ((row_ref, col_ref, own_ref), (other_rows, other_cols, far_ref)):
@@ -148,30 +157,30 @@
         out[:, BLOCK:] = dot(turned(a), b, 1, 1)
 
 
-def density(place, slots, four, up, over, down, cols):
+def density(band, four, up, over, down, cols):
     product = pltpu.VMEM((BLOCK, 2 * BLOCK), jnp.float32)
     points = pltpu.VMEM((BLOCK, LANES), jnp.bfloat16)
     in_hbm = pl.BlockSpec(memory_space=pltpu.HBM)
-    specs = [IN_VMEM] * 2 + [in_hbm] * 2 + [IN_VMEM] + [in_hbm] * NZ
-    arrays = [near(four), near(up), *map(away, over), near(down), *map(away, cols)]
+    specs = [IN_VMEM] * 5 + [in_hbm] * (NZ - 1) + [IN_VMEM]
+    arrays = [*map(near, (four, up, *over, down)), *map(away, cols[:-1]), near(cols[-1])]
     return pl.pallas_call(
         density_body,
         out_shape=[product, product, points, points],
-        in_specs=[IN_SMEM] * 2 + specs,
+        in_specs=[IN_SMEM] + specs,
         out_specs=[IN_VMEM] * 4,
         scratch_shapes=[pltpu.VMEM((BLOCK, LANES), jnp.bfloat16)] * 2
-        + [pltpu.SemaphoreType.DMA((2 * NX + 2 * NZ,))],
+        + [pltpu.SemaphoreType.DMA((2 * (NZ - 1),))],
         compiler_params=PARAMS,
         name="density",
-    )(place, slots, *arrays)
-
-
-def mix_body(odd_ref, own_ref, far_ref, half_ref, kern_ref, m_ref):
+    )(band, *arrays)
+
+
+def mix_body(odd_ref, own_ref, far_ref, core_ref, kern_ref, m_ref):
     odd = odd_ref[0] == 1
     sign = jnp.where(odd, -1.0, 1.0).astype(jnp.float32)
     for i in range(GROUPS):
         at = pl.ds(i * SLAB, SLAB)
-        mine, other = kern_ref[i, 0], half_ref[i]
+        mine, other = kern_ref[i, 0], core_ref[i, 0]
         k_re = jnp.where(odd, other, mine).astype(jnp.float32)
         k_im = jnp.where(odd, mine, other).astype(jnp.float32) * sign
         p_re, p_im = own_ref[at, :BLOCK], own_ref[at, BLOCK:]
@@ -303,7 +312,6 @@
 def on_device(orbitals, kernels, pair_kdiff, stored_kernel_index):
     group = lax.axis_index("kgrp")
     band = lax.axis_index("band")
-    y, x, z = band // (NX * NZ), band // NZ % NX, band % NZ
     odd = (group % 2).reshape(1)
 
     own = lay(orbitals)
@@ -331,12 +339,10 @@
         cols += [ahead, behind]
     cols.append(shift(ahead, 0, 0, 1))
     kern, over, cols = lax.optimization_barrier((kern, over, cols))
-    half = swap_groups(kern[:, 0], 1)
-
-    place = jnp.stack([(y - dy) % NY * NX + (x - dx) % NX for dy in range(NY) for dx in range(NX)])
-    slots = jnp.stack([(z + i) % NZ for i in (0, -1, 1, -2, 2, -3, 3, -4)])
-    p_own, p_far, rows, cols = density(place, slots, four, up, over, down, cols)
-    m_own = swap_groups(mix(odd, p_own, p_far, half, kern), 1)
+    kern_core = swap_groups(kern, 1)
+
+    p_own, p_far, rows, cols = density(band.reshape(1), four, up, over, down, cols)
+    m_own = swap_groups(mix(odd, p_own, p_far, kern_core, kern), 1)
     left, right = prepare(rows, cols)
     total = reduce_windows(project(m_own, left, right))
     flat = total.reshape(2, 8 * NB)

time: 105 us -> 110 us (1.048)
  local copies, waits for them, and re-layouts: 3.32 us -> 7.99 us
    unnamed x18 -> x36, local copies, waits for them, and re-layouts: 2 us -> 7.69 us
  transfers between devices with their start and end apart: 20 -> 20, of which waited for: 7 -> 7; matrix products, arithmetic and copies ran while one was open for 0% -> 0% of each run, Pallas kernels for 9% -> 8%
where the time goes in v21:
time: 110 us; the launch traced here: 109 us
  starting transfers between devices  38.7 us (35%)
  waiting for transfers between devices  26.9 us (24%)
  blocking collectives  17.9 us (16%)
  Pallas kernels  15.2 us (14%)
  local copies, waits for them, and re-layouts  7.99 us (7%)
  other arithmetic  1.51 us (1%)
    ppermute x12, starting transfers between devices, shift(): return lax.ppermute(block, 'band', band_route(dy, dx, dz))  21.9 us
    all_to_all x1, blocking collectives, reduce_windows(): parts = lax.all_to_all(parts, 'band', 0, 0, axis_index_groups=wide)  17.9 us
    ppermute x12, waiting for transfers between devices, shift(): return lax.ppermute(block, 'band', band_route(dy, dx, dz))  12.5 us
    all_to_all x1, waiting for transfers between devices, reduce_windows(): lax.all_to_all(parts, 'band', 0, 0, axis_index_groups=deep)  8.91 us
    unnamed x36, local copies, waits for them, and re-layouts  7.69 us
    all_to_all x1, starting transfers between devices, reduce_windows(): lax.all_to_all(parts, 'band', 0, 0, axis_index_groups=deep)  7.56 us
    ppermute x5, waiting for transfers between devices, swap_groups(): return lax.ppermute(block, 'kgrp', [(k, k ^ bit) for k in range(4)])  5.45 us
    all_to_all x1, starting transfers between devices, on_device(): kern = lax.all_to_all(sends, 'band', 0, 0, axis_index_groups=over_yx)  4.73 us
  transfers between devices with their start and end apart: 20, of which 7 were waited for; matrix products, arithmetic and copies ran while one was open for 0% of the time, Pallas kernels for 8%

profile of v21, /device:TPU:6, one launch (start us, length us, event | category | flops | bytes accessed | tf_op | source)
XLA Modules:
  0.0 109.1 jit_solution(5346280953759534904)
XLA Ops:
  0.0 1.0 lay.1.own_ref
  1.0 1.4 %collective-permute-start.2 = (bf16[64,896]{1,0:T(8,128)(2,1)S(1)}, bf16[64,896]{1,0:T(8,128)(2,1)S(1)}, u32[]{:S(2)}, u32[]{:S(2)}) collective-permute-start(bf16[64,896]{1,0:T(8,128)(2,1)S(1)} %lay.1.own_ref), channel_id=1, source_target_pairs={{0,128},{64,192},{128,0},{192,64},{1,129},{65,193},{129,1},{193,65... | collective-permute-start | bytes 344072 | tf_op jit(solution)/shard_map/ppermute | solution.py:41
  2.4 1.7 %collective-permute-start.3 = (bf16[64,896]{1,0:T(8,128)(2,1)S(1)}, bf16[64,896]{1,0:T(8,128)(2,1)S(1)}, u32[]{:S(2)}, u32[]{:S(2)}) collective-permute-start(bf16[64,896]{1,0:T(8,128)(2,1)S(1)} %lay.1.own_ref), channel_id=1, source_target_pairs={{0,8},{1,9},{2,10},{3,11},{4,12},{5,13},{6,14},{7,15},{8,0},{9,1},... | collective-permute-start | bytes 344072 | tf_op jit(solution)/shard_map/ppermute | solution.py:37
  4.1 1.0 collective-permute-start.4
  5.1 1.4 %collective-permute-start.1 = (s32[1]{0:T(128)}, s32[1]{0:T(128)}, u32[]{:S(2)}, u32[]{:S(2)}) collective-permute-start(s32[1]{0:T(128)} %param.6), channel_id=1, source_target_pairs={{0,128},{64,192},{128,0},{192,64},{1,129},{65,193},{129,1},{193,65... | collective-permute-start | bytes 20 | tf_op jit(solution)/shard_map/ppermute | solution.py:41
  6.5 3.7 %collective-permute-done.1.far_ref = s32[1]{0:T(128)} collective-permute-done((s32[1]{0:T(128)}, s32[1]{0:T(128)}, u32[]{:S(2)}, u32[]{:S(2)}) %collective-permute-start.1) | collective-permute-done | bytes 36 | tf_op jit(solution)/shard_map/ppermute | solution.py:41
  10.3 1.7 %collective-permute-start.5 = (bf16[4,64,896]{2,1,0:T(8,128)(2,1)S(1)}, bf16[4,64,896]{2,1,0:T(8,128)(2,1)S(1)}, u32[]{:S(2)}, u32[]{:S(2)}) collective-permute-start(bf16[4,64,896]{2,1,0:T(8,128)(2,1)S(1)} %get-tuple-element.35.refs_0_), channel_id=1, source_target_pairs={{0,16},{1,17},{2,18},{3,19},{4,20},{5,21},{6,22},{7,23},{8,24},{9,... | collective-permute-start | bytes 1376264 | tf_op jit(solution)/shard_map/ppermute | solution.py:37
  12.0 1.7 %collective-permute-start.6 = (bf16[4,64,896]{2,1,0:T(8,128)(2,1)S(1)}, bf16[4,64,896]{2,1,0:T(8,128)(2,1)S(1)}, u32[]{:S(2)}, u32[]{:S(2)}) collective-permute-start(bf16[4,64,896]{2,1,0:T(8,128)(2,1)S(1)} %get-tuple-element.35.refs_0_), channel_id=1, source_target_pairs={{0,48},{1,49},{2,50},{3,51},{4,52},{5,53},{6,54},{7,55},{8,56},{9,... | collective-permute-start | bytes 1376264 | tf_op jit(solution)/shard_map/ppermute | solution.py:37
  13.7 1.9 %collective-permute-start.7 = (bf16[2,64,896]{2,1,0:T(8,128)(2,1)S(1)}, bf16[2,64,896]{2,1,0:T(8,128)(2,1)S(1)}, u32[]{:S(2)}, u32[]{:S(2)}) collective-permute-start(bf16[2,64,896]{2,1,0:T(8,128)(2,1)S(1)} %get-tuple-element.44.refs_5_), channel_id=1, source_target_pairs={{0,1},{1,2},{2,3},{3,4},{4,5},{5,6},{6,7},{7,0},{8,9},{9,10},{10,1... | collective-permute-start | bytes 688136 | tf_op jit(solution)/shard_map/ppermute | solution.py:37
  15.6 3.9 %collective-permute-start.8 = (bf16[2,64,896]{2,1,0:T(8,128)(2,1)S(1)}, bf16[2,64,896]{2,1,0:T(8,128)(2,1)S(1)}, u32[]{:S(2)}, u32[]{:S(2)}) collective-permute-start(bf16[2,64,896]{2,1,0:T(8,128)(2,1)S(1)} %get-tuple-element.44.refs_5_), channel_id=1, source_target_pairs={{0,7},{1,0},{2,1},{3,2},{4,3},{5,4},{6,5},{7,6},{8,15},{9,8},{10,9... | collective-permute-start | bytes 688136 | tf_op jit(solution)/shard_map/ppermute | solution.py:37
  20.8 4.6 %pack.1 = bf16[8,3,64,512]{3,2,1,0:T(8,128)(2,1)} custom-call(s32[1]{0:T(128)} %bitcast.odd_ref, s32[1]{0:T(128)S(6)} %copy.5.own_ref, s32[1]{0:T(128)} %collective-permute-done.core_ref, s32[1]{0:T(128)} %collective-permute-done.1.far_ref, s32[8]{0:T(128)S(1)} %copy-done.11, bf16[4,2,64,4096]{3,2,1,0:T(8,128)(2,1)} %kernels_ref.1), custom_call_target="tpu_custom_call" | custom-call | tf_op jit(solution)/shard_map/pack/pallas_call | solution.py:110
  25.6 4.7 %all-to-all-start = ((bf16[8,3,64,512]{3,2,1,0:T(8,128)(2,1)}), bf16[8,3,64,512]{3,2,1,0:T(8,128)(2,1)S(1)}, u32[]{:S(2)}, u32[]{:S(2)}) async-start(bf16[8,3,64,512]{3,2,1,0:T(8,128)(2,1)} %pack.1), calls=%async_computation | async-start | bytes 3145728 | tf_op jit(solution)/shard_map/all_to_all | solution.py:335
  30.3 1.0 collective-permute-start.11
  31.3 3.9 %collective-permute-start.12 = (bf16[2,64,896]{2,1,0:T(8,128)(2,1)S(1)}, bf16[2,64,896]{2,1,0:T(8,128)(2,1)S(1)}, u32[]{:S(2)}, u32[]{:S(2)}) collective-permute-start(bf16[2,64,896]{2,1,0:T(8,128)(2,1)S(1)} %collective-permute-done.8.refs_7_), channel_id=1, source_target_pairs={{0,7},{1,0},{2,1},{3,2},{4,3},{5,4},{6,5},{7,6},{8,15},{9,8},{10,9... | collective-permute-start | bytes 688136 | tf_op jit(solution)/shard_map/ppermute | solution.py:37
  35.3 4.0 %collective-permute-done.11.refs_8_ = bf16[2,64,896]{2,1,0:T(8,128)(2,1)S(1)} collective-permute-done((bf16[2,64,896]{2,1,0:T(8,128)(2,1)S(1)}, bf16[2,64,896]{2,1,0:T(8,128)(2,1)S(1)}, u32[]{:S(2)}, u32[]{:S(2)}) %collective-permute-start.11) | collective-permute-done | bytes 229408 | tf_op jit(solution)/shard_map/ppermute | solution.py:37
  39.3 2.8 %collective-permute-start.10 = (bf16[2,64,896]{2,1,0:T(8,128)(2,1)S(1)}, bf16[2,64,896]{2,1,0:T(8,128)(2,1)S(1)}, u32[]{:S(2)}, u32[]{:S(2)}) collective-permute-start(bf16[2,64,896]{2,1,0:T(8,128)(2,1)S(1)} %slice.19), channel_id=1, source_target_pairs={{0,48},{1,49},{2,50},{3,51},{4,52},{5,53},{6,54},{7,55},{8,56},{9,... | collective-permute-start | bytes 688136 | tf_op jit(solution)/shard_map/ppermute | solution.py:37
  42.2 3.3 %collective-permute-start.14 = (bf16[2,64,896]{2,1,0:T(8,128)(2,1)S(1)}, bf16[2,64,896]{2,1,0:T(8,128)(2,1)S(1)}, u32[]{:S(2)}, u32[]{:S(2)}) collective-permute-start(bf16[2,64,896]{2,1,0:T(8,128)(2,1)S(1)} %collective-permute-done.12.refs_9_), channel_id=1, source_target_pairs={{0,7},{1,0},{2,1},{3,2},{4,3},{5,4},{6,5},{7,6},{8,15},{9,8},{10,9... | collective-permute-start | bytes 688136 | tf_op jit(solution)/shard_map/ppermute | solution.py:37
  45.5 1.0 collective-permute-done.13.refs_10_
  46.5 6.2 %collective-permute-done.10.refs_3_ = bf16[2,64,896]{2,1,0:T(8,128)(2,1)S(1)} collective-permute-done((bf16[2,64,896]{2,1,0:T(8,128)(2,1)S(1)}, bf16[2,64,896]{2,1,0:T(8,128)(2,1)S(1)}, u32[]{:S(2)}, u32[]{:S(2)}) %collective-permute-start.10) | collective-permute-done | bytes 229408 | tf_op jit(solution)/shard_map/ppermute | solution.py:37
  52.8 1.3 %collective-permute-done.9.refs_2_ = bf16[2,64,896]{2,1,0:T(8,128)(2,1)S(1)} collective-permute-done((bf16[2,64,896]{2,1,0:T(8,128)(2,1)S(1)}, bf16[2,64,896]{2,1,0:T(8,128)(2,1)S(1)}, u32[]{:S(2)}, u32[]{:S(2)}) %collective-permute-start.9) | collective-permute-done | bytes 229408 | tf_op jit(solution)/shard_map/ppermute | solution.py:37
  56.2 1.0 copy-done.1
  57.2 1.0 copy-done.3
  58.2 1.0 copy-done.5
  59.2 0.9 copy-done.8
  60.2 0.9 copy-done.10
  61.1 4.0 %density.1 = (f32[512,1024]{1,0:T(8,128)S(1)}, f32[512,1024]{1,0:T(8,128)S(1)}, bf16[512,896]{1,0:T(8,128)(2,1)S(1)}, bf16[512,896]{1,0:T(8,128)(2,1)S(1)}) custom-call(s32[1]{0:T(128)} %bitcast.1.band_ref, bf16[4,64,896]{2,1,0:T(8,128)(2,1)S(1)} %copy-done.5, bf16[4,64,896]{2,1,0:T(8,128)(2,1)S(1)} %copy-done.1, bf16[2,64,896]{2,1,0:T(8,128)(2,1)S(1)} %copy-done.8, ...), custom_call_target="tpu_custom_call" | custom-call | tf_op jit(solution)/shard_map/density/pallas_call | solution.py:166
  65.1 0.9 mix.1
  67.2 1.7 %collective-permute-done.17.m_ref = bf16[512,1024]{1,0:T(8,128)(2,1)S(1)} collective-permute-done((bf16[512,1024]{1,0:T(8,128)(2,1)S(1)}, bf16[512,1024]{1,0:T(8,128)(2,1)S(1)}, u32[]{:S(2)}, u32[]{:S(2)}) %collective-permute-start.17) | collective-permute-done | bytes 1048608 | tf_op jit(solution)/shard_map/ppermute | solution.py:41
  68.9 4.0 %project.1 = bf16[64,8,896]{2,1,0:T(8,128)(2,1)S(1)} custom-call(bf16[512,1024]{1,0:T(8,128)(2,1)S(1)} %collective-permute-done.17.m_ref, bf16[432,1024]{1,0:T(8,128)(2,1)S(1)} %get-tuple-element.57.left_ref, bf16[1024,896]{1,0:T(8,128)(2,1)S(1)} %get-tuple-element.58.right_ref), custom_call_target="tpu_custom_call" | custom-call | tf_op jit(solution)/shard_map/project/pallas_call | solution.py:263
  72.9 17.9 %all_to_all.15 = bf16[16,4,8,896]{3,2,1,0:T(8,128)(2,1)S(1)} all-to-all(bf16[16,4,8,896]{3,2,1,0:T(8,128)(2,1)S(1)} %bitcast.5), channel_id=1, replica_groups={{0,1,8,9,16,17,24,25,32,33,40,41,48,49,56,57},{2,3,10,11,18,19,26,27,34..., dimensions={0} | all-to-all | bytes 1835008 | tf_op jit(solution)/shard_map/all_to_all | solution.py:304
  91.6 7.6 %all-to-all-start.2 = ((f32[4,8,896]{2,1,0:T(8,128)}), f32[4,8,896]{2,1,0:T(8,128)S(1)}, u32[]{:S(2)}, u32[]{:S(2)}) async-start(f32[4,8,896]{2,1,0:T(8,128)} %convert_reduce_fusion), calls=%async_computation.2 | async-start | bytes 229376 | tf_op jit(solution)/shard_map/all_to_all | solution.py:306
  99.2 8.9 %all-to-all-done.2 = f32[4,8,896]{2,1,0:T(8,128)S(1)} async-done(((f32[4,8,896]{2,1,0:T(8,128)}), f32[4,8,896]{2,1,0:T(8,128)S(1)}, u32[]{:S(2)}, u32[]{:S(2)}) %all-to-all-start.2) | async-done | bytes 114720 | tf_op jit(solution)/shard_map/all_to_all | solution.py:306
  (62 shorter events, 5.9 us)
Async XLA Ops:
  1.0 9.3 %collective-permute-start.2 = (bf16[64,896]{1,0:T(8,128)(2,1)S(1)}, bf16[64,896]{1,0:T(8,128)(2,1)S(1)}, u32[]{:S(2)}, u32[]{:S(2)}) collective-permute-start(bf16[64,896]{1,0:T(8,128)(2,1)S(1)} %lay.1.own_ref), channel_id=1, source_target_pairs={{0,128},{64,192},{128,0},{192,64},{1,129},{65,193},{129,1},{193,65... | collective-permute-start | bytes 344072 | tf_op jit(solution)/shard_map/ppermute | solution.py:41
  2.4 7.8 %collective-permute-start.3 = (bf16[64,896]{1,0:T(8,128)(2,1)S(1)}, bf16[64,896]{1,0:T(8,128)(2,1)S(1)}, u32[]{:S(2)}, u32[]{:S(2)}) collective-permute-start(bf16[64,896]{1,0:T(8,128)(2,1)S(1)} %lay.1.own_ref), channel_id=1, source_target_pairs={{0,8},{1,9},{2,10},{3,11},{4,12},{5,13},{6,14},{7,15},{8,0},{9,1},... | collective-permute-start | bytes 344072 | tf_op jit(solution)/shard_map/ppermute | solution.py:37
  4.1 6.2 %collective-permute-start.4 = (bf16[64,896]{1,0:T(8,128)(2,1)S(1)}, bf16[64,896]{1,0:T(8,128)(2,1)S(1)}, u32[]{:S(2)}, u32[]{:S(2)}) collective-permute-start(bf16[64,896]{1,0:T(8,128)(2,1)S(1)} %lay.1.own_ref), channel_id=1, source_target_pairs={{128,8},{129,9},{130,10},{131,11},{132,12},{133,13},{134,14},{135,... | collective-permute-start | bytes 344072 | tf_op jit(solution)/shard_map/ppermute | solution.py:47
  5.1 1.4 %collective-permute-start = (s32[1]{0:T(128)}, s32[1]{0:T(128)}, u32[]{:S(2)}, u32[]{:S(2)}) collective-permute-start(s32[1]{0:T(128)} %param.6), channel_id=1, source_target_pairs={{0,64},{64,0},{128,192},{192,128},{1,65},{65,1},{129,193},{193,129... | collective-permute-start | bytes 20 | tf_op jit(solution)/shard_map/ppermute | solution.py:41
  5.1 5.1 %collective-permute-start.1 = (s32[1]{0:T(128)}, s32[1]{0:T(128)}, u32[]{:S(2)}, u32[]{:S(2)}) collective-permute-start(s32[1]{0:T(128)} %param.6), channel_id=1, source_target_pairs={{0,128},{64,192},{128,0},{192,64},{1,129},{65,193},{129,1},{193,65... | collective-permute-start | bytes 20 | tf_op jit(solution)/shard_map/ppermute | solution.py:41
  10.3 15.2 %copy-start.4 = (bf16[4,64,896]{2,1,0:T(8,128)(2,1)}, bf16[4,64,896]{2,1,0:T(8,128)(2,1)S(1)}, u32[]{:S(2)}) copy-start(bf16[4,64,896]{2,1,0:T(8,128)(2,1)S(1)} %get-tuple-element.35.refs_0_) | copy-start | bytes 1376260
  10.3 15.2 %copy-start.6 = (bf16[2,64,896]{2,1,0:T(8,128)(2,1)}, bf16[2,64,896]{2,1,0:T(8,128)(2,1)S(1)}, u32[]{:S(2)}) copy-start(bf16[2,64,896]{2,1,0:T(8,128)(2,1)S(1)} %get-tuple-element.44.refs_5_) | copy-start | bytes 688132
  10.3 15.2 %collective-permute-start.5 = (bf16[4,64,896]{2,1,0:T(8,128)(2,1)S(1)}, bf16[4,64,896]{2,1,0:T(8,128)(2,1)S(1)}, u32[]{:S(2)}, u32[]{:S(2)}) collective-permute-start(bf16[4,64,896]{2,1,0:T(8,128)(2,1)S(1)} %get-tuple-element.35.refs_0_), channel_id=1, source_target_pairs={{0,16},{1,17},{2,18},{3,19},{4,20},{5,21},{6,22},{7,23},{8,24},{9,... | collective-permute-start | bytes 1376264 | tf_op jit(solution)/shard_map/ppermute | solution.py:37
  12.0 13.6 %collective-permute-start.6 = (bf16[4,64,896]{2,1,0:T(8,128)(2,1)S(1)}, bf16[4,64,896]{2,1,0:T(8,128)(2,1)S(1)}, u32[]{:S(2)}, u32[]{:S(2)}) collective-permute-start(bf16[4,64,896]{2,1,0:T(8,128)(2,1)S(1)} %get-tuple-element.35.refs_0_), channel_id=1, source_target_pairs={{0,48},{1,49},{2,50},{3,51},{4,52},{5,53},{6,54},{7,55},{8,56},{9,... | collective-permute-start | bytes 1376264 | tf_op jit(solution)/shard_map/ppermute | solution.py:37
  13.7 11.9 %collective-permute-start.7 = (bf16[2,64,896]{2,1,0:T(8,128)(2,1)S(1)}, bf16[2,64,896]{2,1,0:T(8,128)(2,1)S(1)}, u32[]{:S(2)}, u32[]{:S(2)}) collective-permute-start(bf16[2,64,896]{2,1,0:T(8,128)(2,1)S(1)} %get-tuple-element.44.refs_5_), channel_id=1, source_target_pairs={{0,1},{1,2},{2,3},{3,4},{4,5},{5,6},{6,7},{7,0},{8,9},{9,10},{10,1... | collective-permute-start | bytes 688136 | tf_op jit(solution)/shard_map/ppermute | solution.py:37
  15.6 10.0 %collective-permute-start.8 = (bf16[2,64,896]{2,1,0:T(8,128)(2,1)S(1)}, bf16[2,64,896]{2,1,0:T(8,128)(2,1)S(1)}, u32[]{:S(2)}, u32[]{:S(2)}) collective-permute-start(bf16[2,64,896]{2,1,0:T(8,128)(2,1)S(1)} %get-tuple-element.44.refs_5_), channel_id=1, source_target_pairs={{0,7},{1,0},{2,1},{3,2},{4,3},{5,4},{6,5},{7,6},{8,15},{9,8},{10,9... | collective-permute-start | bytes 688136 | tf_op jit(solution)/shard_map/ppermute | solution.py:37
  25.5 16.5 %copy-start.12 = (bf16[2,64,896]{2,1,0:T(8,128)(2,1)}, bf16[2,64,896]{2,1,0:T(8,128)(2,1)S(1)}, u32[]{:S(2)}) copy-start(bf16[2,64,896]{2,1,0:T(8,128)(2,1)S(1)} %collective-permute-done.7.refs_6_) | copy-start | bytes 688132
  25.5 16.5 %copy-start.13 = (bf16[2,64,896]{2,1,0:T(8,128)(2,1)}, bf16[2,64,896]{2,1,0:T(8,128)(2,1)S(1)}, u32[]{:S(2)}) copy-start(bf16[2,64,896]{2,1,0:T(8,128)(2,1)S(1)} %collective-permute-done.8.refs_7_) | copy-start | bytes 688132
  25.6 16.5 %copy-start = (bf16[4,64,896]{2,1,0:T(8,128)(2,1)}, bf16[4,64,896]{2,1,0:T(8,128)(2,1)S(1)}, u32[]{:S(2)}) copy-start(bf16[4,64,896]{2,1,0:T(8,128)(2,1)S(1)} %collective-permute-done.5.refs_1_) | copy-start | bytes 1376260
  25.6 16.5 %copy-start.2 = (bf16[4,64,896]{2,1,0:T(8,128)(2,1)}, bf16[4,64,896]{2,1,0:T(8,128)(2,1)S(1)}, u32[]{:S(2)}) copy-start(bf16[4,64,896]{2,1,0:T(8,128)(2,1)S(1)} %collective-permute-done.6.refs_4_) | copy-start | bytes 1376260
  25.6 30.6 %all-to-all-start = ((bf16[8,3,64,512]{3,2,1,0:T(8,128)(2,1)}), bf16[8,3,64,512]{3,2,1,0:T(8,128)(2,1)S(1)}, u32[]{:S(2)}, u32[]{:S(2)}) async-start(bf16[8,3,64,512]{3,2,1,0:T(8,128)(2,1)} %pack.1), calls=%async_computation | async-start | bytes 3145728 | tf_op jit(solution)/shard_map/all_to_all | solution.py:335
  30.3 8.9 %collective-permute-start.11 = (bf16[2,64,896]{2,1,0:T(8,128)(2,1)S(1)}, bf16[2,64,896]{2,1,0:T(8,128)(2,1)S(1)}, u32[]{:S(2)}, u32[]{:S(2)}) collective-permute-start(bf16[2,64,896]{2,1,0:T(8,128)(2,1)S(1)} %collective-permute-done.7.refs_6_), channel_id=1, source_target_pairs={{0,1},{1,2},{2,3},{3,4},{4,5},{5,6},{6,7},{7,0},{8,9},{9,10},{10,1... | collective-permute-start | bytes 688136 | tf_op jit(solution)/shard_map/ppermute | solution.py:37
  31.3 10.9 %collective-permute-start.12 = (bf16[2,64,896]{2,1,0:T(8,128)(2,1)S(1)}, bf16[2,64,896]{2,1,0:T(8,128)(2,1)S(1)}, u32[]{:S(2)}, u32[]{:S(2)}) collective-permute-start(bf16[2,64,896]{2,1,0:T(8,128)(2,1)S(1)} %collective-permute-done.8.refs_7_), channel_id=1, source_target_pairs={{0,7},{1,0},{2,1},{3,2},{4,3},{5,4},{6,5},{7,6},{8,15},{9,8},{10,9... | collective-permute-start | bytes 688136 | tf_op jit(solution)/shard_map/ppermute | solution.py:37
  39.3 15.5 %copy-start.14 = (bf16[2,64,896]{2,1,0:T(8,128)(2,1)}, bf16[2,64,896]{2,1,0:T(8,128)(2,1)S(1)}, u32[]{:S(2)}) copy-start(bf16[2,64,896]{2,1,0:T(8,128)(2,1)S(1)} %collective-permute-done.11.refs_8_) | copy-start | bytes 688132
  39.3 7.2 %collective-permute-start.13 = (bf16[2,64,896]{2,1,0:T(8,128)(2,1)S(1)}, bf16[2,64,896]{2,1,0:T(8,128)(2,1)S(1)}, u32[]{:S(2)}, u32[]{:S(2)}) collective-permute-start(bf16[2,64,896]{2,1,0:T(8,128)(2,1)S(1)} %collective-permute-done.11.refs_8_), channel_id=1, source_target_pairs={{0,1},{1,2},{2,3},{3,4},{4,5},{5,6},{6,7},{7,0},{8,9},{9,10},{10,1... | collective-permute-start | bytes 688136 | tf_op jit(solution)/shard_map/ppermute | solution.py:37
  39.3 13.5 %collective-permute-start.10 = (bf16[2,64,896]{2,1,0:T(8,128)(2,1)S(1)}, bf16[2,64,896]{2,1,0:T(8,128)(2,1)S(1)}, u32[]{:S(2)}, u32[]{:S(2)}) collective-permute-start(bf16[2,64,896]{2,1,0:T(8,128)(2,1)S(1)} %slice.19), channel_id=1, source_target_pairs={{0,48},{1,49},{2,50},{3,51},{4,52},{5,53},{6,54},{7,55},{8,56},{9,... | collective-permute-start | bytes 688136 | tf_op jit(solution)/shard_map/ppermute | solution.py:37
  42.1 11.9 %collective-permute-start.9 = (bf16[2,64,896]{2,1,0:T(8,128)(2,1)S(1)}, bf16[2,64,896]{2,1,0:T(8,128)(2,1)S(1)}, u32[]{:S(2)}, u32[]{:S(2)}) collective-permute-start(bf16[2,64,896]{2,1,0:T(8,128)(2,1)S(1)} %slice.18), channel_id=1, source_target_pairs={{0,16},{1,17},{2,18},{3,19},{4,20},{5,21},{6,22},{7,23},{8,24},{9,... | collective-permute-start | bytes 688136 | tf_op jit(solution)/shard_map/ppermute | solution.py:37
  42.2 12.5 %copy-start.15 = (bf16[2,64,896]{2,1,0:T(8,128)(2,1)}, bf16[2,64,896]{2,1,0:T(8,128)(2,1)S(1)}, u32[]{:S(2)}) copy-start(bf16[2,64,896]{2,1,0:T(8,128)(2,1)S(1)} %collective-permute-done.12.refs_9_) | copy-start | bytes 688132
  42.2 12.5 %collective-permute-start.14 = (bf16[2,64,896]{2,1,0:T(8,128)(2,1)S(1)}, bf16[2,64,896]{2,1,0:T(8,128)(2,1)S(1)}, u32[]{:S(2)}, u32[]{:S(2)}) collective-permute-start(bf16[2,64,896]{2,1,0:T(8,128)(2,1)S(1)} %collective-permute-done.12.refs_9_), channel_id=1, source_target_pairs={{0,7},{1,0},{2,1},{3,2},{4,3},{5,4},{6,5},{7,6},{8,15},{9,8},{10,9... | collective-permute-start | bytes 688136 | tf_op jit(solution)/shard_map/ppermute | solution.py:37
  46.5 8.2 %copy-start.16 = (bf16[2,64,896]{2,1,0:T(8,128)(2,1)}, bf16[2,64,896]{2,1,0:T(8,128)(2,1)S(1)}, u32[]{:S(2)}) copy-start(bf16[2,64,896]{2,1,0:T(8,128)(2,1)S(1)} %collective-permute-done.13.refs_10_) | copy-start | bytes 688132
  46.5 8.2 %collective-permute-start.15 = (bf16[2,64,896]{2,1,0:T(8,128)(2,1)S(1)}, bf16[2,64,896]{2,1,0:T(8,128)(2,1)S(1)}, u32[]{:S(2)}, u32[]{:S(2)}) collective-permute-start(bf16[2,64,896]{2,1,0:T(8,128)(2,1)S(1)} %collective-permute-done.13.refs_10_), channel_id=1, source_target_pairs={{0,1},{1,2},{2,3},{3,4},{4,5},{5,6},{6,7},{7,0},{8,9},{9,10},{10,1... | collective-permute-start | bytes 688136 | tf_op jit(solution)/shard_map/ppermute | solution.py:37
  56.2 8.9 %collective-permute-start.16 = (bf16[8,3,64,512]{3,2,1,0:T(8,128)(2,1)S(1)}, bf16[8,3,64,512]{3,2,1,0:T(8,128)(2,1)S(1)}, u32[]{:S(2)}, u32[]{:S(2)}) collective-permute-start(bf16[8,3,64,512]{3,2,1,0:T(8,128)(2,1)S(1)} %all-to-all-done.kern_ref), channel_id=1, source_target_pairs={{0,64},{64,0},{128,192},{192,128},{1,65},{65,1},{129,193},{193,129... | collective-permute-start | bytes 4718600 | tf_op jit(solution)/shard_map/ppermute | solution.py:41
  56.2 1.0 copy-start.1
  57.2 1.0 copy-start.3
  58.2 1.0 copy-start.5
  66.0 2.9 %collective-permute-start.17 = (bf16[512,1024]{1,0:T(8,128)(2,1)S(1)}, bf16[512,1024]{1,0:T(8,128)(2,1)S(1)}, u32[]{:S(2)}, u32[]{:S(2)}) collective-permute-start(bf16[512,1024]{1,0:T(8,128)(2,1)S(1)} %mix.1), channel_id=1, source_target_pairs={{0,64},{64,0},{128,192},{192,128},{1,65},{65,1},{129,193},{193,129... | collective-permute-start | bytes 3145736 | tf_op jit(solution)/shard_map/ppermute | solution.py:41
  91.6 16.5 %all-to-all-start.2 = ((f32[4,8,896]{2,1,0:T(8,128)}), f32[4,8,896]{2,1,0:T(8,128)S(1)}, u32[]{:S(2)}, u32[]{:S(2)}) async-start(f32[4,8,896]{2,1,0:T(8,128)} %convert_reduce_fusion), calls=%async_computation.2 | async-start | bytes 229376 | tf_op jit(solution)/shard_map/all_to_all | solution.py:306
  (6 other events, 4.6 us)

commit v22 on v20

--- a/solution.py
+++ b/solution.py
@@ -14,6 +14,7 @@
 REST = NB - WHOLE
 TAIL = 2 * WHOLE
 LANES = TAIL + 128
+Z_ORDER = (0, -1, 1, -2, 2, -3, 3, -4)
 VMEM = 24 * 1024 * 1024
 
 IN_VMEM = pl.BlockSpec(memory_space=pltpu.VMEM)
@@ -117,29 +118,29 @@
     )(odd, own, core, far, stored, away(kernels))
 
 
-def density_body(place_ref, slot_ref, *refs):
-    four_ref, up_ref, over_here, over_side, down_ref = refs[:5]
-    cols = refs[5 : 5 + NZ]
-    own_ref, far_ref, row_ref, col_ref, other_rows, other_cols, sem = refs[5 + NZ :]
+def density_body(band_ref, *refs):
+    steps, (own_side, far_side), cols = refs[:NY], refs[NY : NY + 2], refs[NY + 2 : NY + 2 + NZ]
+    own_ref, far_ref, row_ref, col_ref, other_rows, other_cols, sem = refs[NY + 2 + NZ :]
+    band = band_ref[0]
+    y, x, z = band // (NX * NZ), band // NZ % NX, band % NZ
 
     def row_at(dy, side):
-        return pl.ds(pl.multiple_of(place_ref[dy * NX + side] * SLAB, SLAB), SLAB)
+        place = (y + NY - dy) % NY * NX + (x + side) % NX
+        return pl.ds(pl.multiple_of(place * SLAB, SLAB), SLAB)
 
     moves = []
-    for i, piece in enumerate(cols):
-        at = pl.ds(pl.multiple_of(slot_ref[i] * SLAB, SLAB), SLAB)
+    for piece, dz in zip(cols, Z_ORDER):
+        at = pl.ds(pl.multiple_of((z + NZ + dz) % NZ * SLAB, SLAB), SLAB)
         moves.append((piece.at[0], col_ref.at[at, :]))
         moves.append((piece.at[1], other_cols.at[at, :]))
-    for side, piece in enumerate((over_here, over_side)):
-        moves.append((piece.at[0], row_ref.at[row_at(2, side), :]))
-        moves.append((piece.at[1], other_rows.at[row_at(2, side), :]))
+    for dy, piece in enumerate(steps):
+        moves.append((piece.at[0], row_ref.at[row_at(dy, 0), :]))
+        moves.append((piece.at[1], other_rows.at[row_at(dy, 0), :]))
+        moves.append((own_side.at[dy], row_ref.at[row_at(dy, 1), :]))
+        moves.append((far_side.at[dy], other_rows.at[row_at(dy, 1), :]))
     copies = [pltpu.make_async_copy(*move, sem.at[i]) for i, move in enumerate(moves)]
     for copy in copies:
         copy.start()
-    for dy, piece in ((0, four_ref), (1, up_ref), (3, down_ref)):
-        for side in range(NX):
-            row_ref[row_at(dy, side), :] = piece[2 * side]
-            other_rows[row_at(dy, side), :] = piece[2 * side + 1]
     for copy in copies:
         copy.wait()
     for rows, columns, out in ((row_ref, col_ref, own_ref), (other_rows, other_cols, far_ref)):
@@ -148,22 +149,20 @@
         out[:, BLOCK:] = dot(turned(a), b, 1, 1)
 
 
-def density(place, slots, four, up, over, down, cols):
+def density(band, *arrays):
     product = pltpu.VMEM((BLOCK, 2 * BLOCK), jnp.float32)
     points = pltpu.VMEM((BLOCK, LANES), jnp.bfloat16)
     in_hbm = pl.BlockSpec(memory_space=pltpu.HBM)
-    specs = [IN_VMEM] * 2 + [in_hbm] * 2 + [IN_VMEM] + [in_hbm] * NZ
-    arrays = [near(four), near(up), *map(away, over), near(down), *map(away, cols)]
     return pl.pallas_call(
         density_body,
         out_shape=[product, product, points, points],
-        in_specs=[IN_SMEM] * 2 + specs,
+        in_specs=[IN_SMEM] + [in_hbm] * len(arrays),
         out_specs=[IN_VMEM] * 4,
         scratch_shapes=[pltpu.VMEM((BLOCK, LANES), jnp.bfloat16)] * 2
-        + [pltpu.SemaphoreType.DMA((2 * NX + 2 * NZ,))],
+        + [pltpu.SemaphoreType.DMA((4 * NY + 2 * NZ,))],
         compiler_params=PARAMS,
         name="density",
-    )(place, slots, *arrays)
+    )(band, *map(away, arrays))
 
 
 def mix_body(odd_ref, own_ref, far_ref, half_ref, kern_ref, m_ref):
@@ -266,22 +265,18 @@
     )(near(m), near(left), near(right))
 
 
-def bundle_body(own_ref, far_ref, own_side, far_side, four_ref, both_ref):
-    for i, ref in enumerate((own_ref, far_ref, own_side, far_side)):
-        four_ref[i] = ref[...]
-    both_ref[0] = own_ref[...]
-    both_ref[1] = far_ref[...]
+def bundle_body(*refs):
+    *blocks, out_ref = refs
+    for i, ref in enumerate(blocks):
+        out_ref[i] = ref[...]
 
 
 def bundle(*blocks):
     return pl.pallas_call(
         bundle_body,
-        out_shape=[
-            pltpu.VMEM((4, SLAB, LANES), jnp.bfloat16),
-            pltpu.VMEM((2, SLAB, LANES), jnp.bfloat16),
-        ],
-        in_specs=[IN_VMEM] * 4,
-        out_specs=[IN_VMEM] * 2,
+        out_shape=pltpu.VMEM((len(blocks), SLAB, LANES), jnp.bfloat16),
+        in_specs=[IN_VMEM] * len(blocks),
+        out_specs=IN_VMEM,
         compiler_params=PARAMS,
         name="bundle",
     )(*map(near, blocks))
@@ -303,39 +298,31 @@
 def on_device(orbitals, kernels, pair_kdiff, stored_kernel_index):
     group = lax.axis_index("kgrp")
     band = lax.axis_index("band")
-    y, x, z = band // (NX * NZ), band // NZ % NX, band % NZ
     odd = (group % 2).reshape(1)
 
     own = lay(orbitals)
-    first = (
-        swap_groups(pair_kdiff, 1),
-        swap_groups(pair_kdiff, 2),
-        swap_groups(own, 2),
-        shift(own, 0, 1, 0),
-        other_side(own),
-    )
-    diff_core, diff_far = first[:2]
-    far, own_side, far_side = lax.optimization_barrier(first)[2:]
+    first = swap_groups(pair_kdiff, 1), swap_groups(pair_kdiff, 2), swap_groups(own, 2)
+    diff_core, diff_far, far = lax.optimization_barrier(first)
 
     over_yx = [[g * NZ + i for g in range(GROUPS)] for i in range(NZ)]
     sends = pack(odd, pair_kdiff, diff_core, diff_far, stored_kernel_index, kernels)
 
-    four, both = bundle(own, far, own_side, far_side)
-    steps = shift(four, 1, 0, 0), shift(four, -1, 0, 0), shift(both, 0, 0, 1), shift(both, 0, 0, -1)
+    both = bundle(own, far)
+    steps = [shift(both, 1, 0, 0), shift(both, -1, 0, 0), shift(both, 0, 0, 1), shift(both, 0, 0, -1)]
     up, down, ahead, behind, sends = lax.optimization_barrier((*steps, sends))
-    over = shift(up[:2], 1, 0, 0), shift(down[2:], -1, 0, 0)
+    over = shift(up, 1, 0, 0)
     kern = lax.all_to_all(sends, "band", 0, 0, axis_index_groups=over_yx)
     cols = [both, ahead, behind]
     for _ in range(2):
         ahead, behind = shift(ahead, 0, 0, 1), shift(behind, 0, 0, -1)
         cols += [ahead, behind]
     cols.append(shift(ahead, 0, 0, 1))
-    kern, over, cols = lax.optimization_barrier((kern, over, cols))
+    owns = bundle(own, up[0], over[0], down[0])
+    sides = shift(owns, 0, 1, 0), other_side(owns)
+    kern, over, sides, cols = lax.optimization_barrier((kern, over, sides, cols))
     half = swap_groups(kern[:, 0], 1)
 
-    place = jnp.stack([(y - dy) % NY * NX + (x - dx) % NX for dy in range(NY) for dx in range(NX)])
-    slots = jnp.stack([(z + i) % NZ for i in (0, -1, 1, -2, 2, -3, 3, -4)])
-    p_own, p_far, rows, cols = density(place, slots, four, up, over, down, cols)
+    p_own, p_far, rows, cols = density(band.reshape(1), both, up, over, down, *sides, *cols)
     m_own = swap_groups(mix(odd, p_own, p_far, half, kern), 1)
     left, right = prepare(rows, cols)
     total = reduce_windows(project(m_own, left, right))

time: 105 us -> 116 us (1.10)
  waiting for transfers between devices: 26.9 us -> 44 us
  starting transfers between devices: 38.4 us -> 34.9 us
  local copies, waits for them, and re-layouts: 3.32 us -> 1.03 us
    ppermute x12 -> x11, waiting for transfers between devices: 12.4 us -> 29 us  [shift(): return lax.ppermute(block, 'band', band_route(dy, dx, dz))]
    ppermute x12 -> x11, starting transfers between devices: 21.8 us -> 17.7 us  [shift(): return lax.ppermute(block, 'band', band_route(dy, dx, dz))]
    all_to_all x1, starting transfers between devices: 7.42 us -> 5.56 us  [reduce_windows(): lax.all_to_all(parts, 'band', 0, 0, axis_index_groups=deep)]
    ppermute x1, starting transfers between devices: 1.02 us -> 2.44 us  [other_side(): return lax.ppermute(block, ('kgrp', 'band'), both)]
    unnamed x18 -> x26, local copies, waits for them, and re-layouts: 2 us -> 0.7 us
    ppermute x1, waiting for transfers between devices: 0.01 us -> 1.25 us  [other_side(): return lax.ppermute(block, ('kgrp', 'band'), both)]
  transfers between devices with their start and end apart: 20 -> 19, of which waited for: 7 -> 7; matrix products, arithmetic and copies ran while one was open for 0% -> 0% of each run, Pallas kernels for 9% -> 9%
where the time goes in v22:
time: 116 us; the launch traced here: 115 us
  waiting for transfers between devices  44 us (38%)
  starting transfers between devices  34.9 us (30%)
  blocking collectives  17.2 us (15%)
  Pallas kernels  15.8 us (14%)
  other arithmetic  1.53 us (1%)
    ppermute x11, waiting for transfers between devices, shift(): return lax.ppermute(block, 'band', band_route(dy, dx, dz))  29 us
    ppermute x11, starting transfers between devices, shift(): return lax.ppermute(block, 'band', band_route(dy, dx, dz))  17.7 us
    all_to_all x1, blocking collectives, reduce_windows(): parts = lax.all_to_all(parts, 'band', 0, 0, axis_index_groups=wide)  17.2 us
    all_to_all x1, waiting for transfers between devices, reduce_windows(): lax.all_to_all(parts, 'band', 0, 0, axis_index_groups=deep)  8.91 us
    all_to_all x1, starting transfers between devices, reduce_windows(): lax.all_to_all(parts, 'band', 0, 0, axis_index_groups=deep)  5.56 us
    ppermute x5, waiting for transfers between devices, swap_groups(): return lax.ppermute(block, 'kgrp', [(k, k ^ bit) for k in range(4)])  4.88 us
    pallas_call x1, Pallas kernels, density(): pl.pallas_call(density_body, out_shape=[product, product, points, points]...  4.76 us
    all_to_all x1, starting transfers between devices, on_device(): kern = lax.all_to_all(sends, 'band', 0, 0, axis_index_groups=over_yx)  4.73 us
  transfers between devices with their start and end apart: 19, of which 7 were waited for; matrix products, arithmetic and copies ran while one was open for 0% of the time, Pallas kernels for 9%

profile of v22, /device:TPU:6, one launch (start us, length us, event | category | flops | bytes accessed | tf_op | source)
XLA Modules:
  0.0 115.4 jit_solution(9305455977694564382)
XLA Ops:
  0.0 1.0 lay.1.refs_0_
  1.0 1.4 %collective-permute-start.2 = (bf16[64,896]{1,0:T(8,128)(2,1)S(1)}, bf16[64,896]{1,0:T(8,128)(2,1)S(1)}, u32[]{:S(2)}, u32[]{:S(2)}) collective-permute-start(bf16[64,896]{1,0:T(8,128)(2,1)S(1)} %lay.1.refs_0_), channel_id=1, source_target_pairs={{0,128},{64,192},{128,0},{192,64},{1,129},{65,193},{129,1},{193,65... | collective-permute-start | bytes 344072 | tf_op jit(solution)/shard_map/ppermute | solution.py:41
  2.4 2.1 %collective-permute-start.1 = (s32[1]{0:T(128)}, s32[1]{0:T(128)}, u32[]{:S(2)}, u32[]{:S(2)}) collective-permute-start(s32[1]{0:T(128)} %param.6), channel_id=1, source_target_pairs={{0,128},{64,192},{128,0},{192,64},{1,129},{65,193},{129,1},{193,65... | collective-permute-start | bytes 20 | tf_op jit(solution)/shard_map/ppermute | solution.py:41
  4.6 3.2 %collective-permute-done.1.far_ref = s32[1]{0:T(128)} collective-permute-done((s32[1]{0:T(128)}, s32[1]{0:T(128)}, u32[]{:S(2)}, u32[]{:S(2)}) %collective-permute-start.1) | collective-permute-done | bytes 36 | tf_op jit(solution)/shard_map/ppermute | solution.py:41
  7.8 1.7 %collective-permute-start.3 = (bf16[2,64,896]{2,1,0:T(8,128)(2,1)S(1)}, bf16[2,64,896]{2,1,0:T(8,128)(2,1)S(1)}, u32[]{:S(2)}, u32[]{:S(2)}) collective-permute-start(bf16[2,64,896]{2,1,0:T(8,128)(2,1)S(1)} %bundle.2.refs_0_.refs_6_), channel_id=1, source_target_pairs={{0,16},{1,17},{2,18},{3,19},{4,20},{5,21},{6,22},{7,23},{8,24},{9,... | collective-permute-start | bytes 688136 | tf_op jit(solution)/shard_map/ppermute | solution.py:37
  9.4 1.7 %collective-permute-start.4 = (bf16[2,64,896]{2,1,0:T(8,128)(2,1)S(1)}, bf16[2,64,896]{2,1,0:T(8,128)(2,1)S(1)}, u32[]{:S(2)}, u32[]{:S(2)}) collective-permute-start(bf16[2,64,896]{2,1,0:T(8,128)(2,1)S(1)} %bundle.2.refs_0_.refs_6_), channel_id=1, source_target_pairs={{0,48},{1,49},{2,50},{3,51},{4,52},{5,53},{6,54},{7,55},{8,56},{9,... | collective-permute-start | bytes 688136 | tf_op jit(solution)/shard_map/ppermute | solution.py:37
  11.1 1.9 %collective-permute-start.5 = (bf16[2,64,896]{2,1,0:T(8,128)(2,1)S(1)}, bf16[2,64,896]{2,1,0:T(8,128)(2,1)S(1)}, u32[]{:S(2)}, u32[]{:S(2)}) collective-permute-start(bf16[2,64,896]{2,1,0:T(8,128)(2,1)S(1)} %bundle.2.refs_0_.refs_6_), channel_id=1, source_target_pairs={{0,1},{1,2},{2,3},{3,4},{4,5},{5,6},{6,7},{7,0},{8,9},{9,10},{10,1... | collective-permute-start | bytes 688136 | tf_op jit(solution)/shard_map/ppermute | solution.py:37
  13.0 3.9 %collective-permute-start.6 = (bf16[2,64,896]{2,1,0:T(8,128)(2,1)S(1)}, bf16[2,64,896]{2,1,0:T(8,128)(2,1)S(1)}, u32[]{:S(2)}, u32[]{:S(2)}) collective-permute-start(bf16[2,64,896]{2,1,0:T(8,128)(2,1)S(1)} %bundle.2.refs_0_.refs_6_), channel_id=1, source_target_pairs={{0,7},{1,0},{2,1},{3,2},{4,3},{5,4},{6,5},{7,6},{8,15},{9,8},{10,9... | collective-permute-start | bytes 688136 | tf_op jit(solution)/shard_map/ppermute | solution.py:37
  17.6 0.6 copy-done.1
  18.2 4.5 %pack.1 = bf16[8,3,64,512]{3,2,1,0:T(8,128)(2,1)} custom-call(s32[1]{0:T(128)} %bitcast.odd_ref, s32[1]{0:T(128)S(6)} %copy.5.own_ref, s32[1]{0:T(128)} %collective-permute-done.core_ref, s32[1]{0:T(128)} %collective-permute-done.1.far_ref, s32[8]{0:T(128)S(1)} %copy-done.1, bf16[4,2,64,4096]{3,2,1,0:T(8,128)(2,1)} %kernels_ref.1), custom_call_target="tpu_custom_call" | custom-call | tf_op jit(solution)/shard_map/pack/pallas_call | solution.py:110
  22.8 4.7 %all-to-all-start = ((bf16[8,3,64,512]{3,2,1,0:T(8,128)(2,1)}), bf16[8,3,64,512]{3,2,1,0:T(8,128)(2,1)S(1)}, u32[]{:S(2)}, u32[]{:S(2)}) async-start(bf16[8,3,64,512]{3,2,1,0:T(8,128)(2,1)} %pack.1), calls=%async_computation | async-start | bytes 3145728 | tf_op jit(solution)/shard_map/all_to_all | solution.py:314
  27.6 1.5 %collective-permute-start.7 = (bf16[2,64,896]{2,1,0:T(8,128)(2,1)S(1)}, bf16[2,64,896]{2,1,0:T(8,128)(2,1)S(1)}, u32[]{:S(2)}, u32[]{:S(2)}) collective-permute-start(bf16[2,64,896]{2,1,0:T(8,128)(2,1)S(1)} %collective-permute-done.3.refs_1_), channel_id=1, source_target_pairs={{0,16},{1,17},{2,18},{3,19},{4,20},{5,21},{6,22},{7,23},{8,24},{9,... | collective-permute-start | bytes 688136 | tf_op jit(solution)/shard_map/ppermute | solution.py:37
  29.0 3.2 %collective-permute-start.11 = (bf16[2,64,896]{2,1,0:T(8,128)(2,1)S(1)}, bf16[2,64,896]{2,1,0:T(8,128)(2,1)S(1)}, u32[]{:S(2)}, u32[]{:S(2)}) collective-permute-start(bf16[2,64,896]{2,1,0:T(8,128)(2,1)S(1)} %collective-permute-done.6.refs_8_), channel_id=1, source_target_pairs={{0,7},{1,0},{2,1},{3,2},{4,3},{5,4},{6,5},{7,6},{8,15},{9,8},{10,9... | collective-permute-start | bytes 688136 | tf_op jit(solution)/shard_map/ppermute | solution.py:37
  32.3 18.9 %collective-permute-done.7.refs_2_ = bf16[2,64,896]{2,1,0:T(8,128)(2,1)S(1)} collective-permute-done((bf16[2,64,896]{2,1,0:T(8,128)(2,1)S(1)}, bf16[2,64,896]{2,1,0:T(8,128)(2,1)S(1)}, u32[]{:S(2)}, u32[]{:S(2)}) %collective-permute-start.7) | collective-permute-done | bytes 229408 | tf_op jit(solution)/shard_map/ppermute | solution.py:37
  51.3 0.6 collective-permute-start.8
  52.0 2.4 %collective-permute-start.9 = (bf16[4,64,896]{2,1,0:T(8,128)(2,1)S(1)}, bf16[4,64,896]{2,1,0:T(8,128)(2,1)S(1)}, u32[]{:S(2)}, u32[]{:S(2)}) collective-permute-start(bf16[4,64,896]{2,1,0:T(8,128)(2,1)S(1)} %bundle.3), channel_id=1, source_target_pairs={{128,8},{129,9},{130,10},{131,11},{132,12},{133,13},{134,14},{135,... | collective-permute-start | bytes 1376264 | tf_op jit(solution)/shard_map/ppermute | solution.py:47
  54.4 3.2 %collective-permute-start.13 = (bf16[2,64,896]{2,1,0:T(8,128)(2,1)S(1)}, bf16[2,64,896]{2,1,0:T(8,128)(2,1)S(1)}, u32[]{:S(2)}, u32[]{:S(2)}) collective-permute-start(bf16[2,64,896]{2,1,0:T(8,128)(2,1)S(1)} %collective-permute-done.11.refs_10_), channel_id=1, source_target_pairs={{0,7},{1,0},{2,1},{3,2},{4,3},{5,4},{6,5},{7,6},{8,15},{9,8},{10,9... | collective-permute-start | bytes 688136 | tf_op jit(solution)/shard_map/ppermute | solution.py:37
  57.7 4.0 %collective-permute-done.12.refs_11_ = bf16[2,64,896]{2,1,0:T(8,128)(2,1)S(1)} collective-permute-done((bf16[2,64,896]{2,1,0:T(8,128)(2,1)S(1)}, bf16[2,64,896]{2,1,0:T(8,128)(2,1)S(1)}, u32[]{:S(2)}, u32[]{:S(2)}) %collective-permute-start.12) | collective-permute-done | bytes 229408 | tf_op jit(solution)/shard_map/ppermute | solution.py:37
  61.7 1.2 %collective-permute-done.9.refs_5_ = bf16[4,64,896]{2,1,0:T(8,128)(2,1)S(1)} collective-permute-done((bf16[4,64,896]{2,1,0:T(8,128)(2,1)S(1)}, bf16[4,64,896]{2,1,0:T(8,128)(2,1)S(1)}, u32[]{:S(2)}, u32[]{:S(2)}) %collective-permute-start.9) | collective-permute-done | bytes 458784 | tf_op jit(solution)/shard_map/ppermute | solution.py:47
  62.9 6.0 %collective-permute-done.14.refs_13_ = bf16[2,64,896]{2,1,0:T(8,128)(2,1)} collective-permute-done((bf16[2,64,896]{2,1,0:T(8,128)(2,1)S(1)}, bf16[2,64,896]{2,1,0:T(8,128)(2,1)}, u32[]{:S(2)}, u32[]{:S(2)}) %collective-permute-start.14) | collective-permute-done | bytes 229408 | tf_op jit(solution)/shard_map/ppermute | solution.py:37
  69.0 0.3 collective-permute-start.15
  69.4 4.8 %density.1 = (f32[512,1024]{1,0:T(8,128)S(1)}, f32[512,1024]{1,0:T(8,128)S(1)}, bf16[512,896]{1,0:T(8,128)(2,1)S(1)}, bf16[512,896]{1,0:T(8,128)(2,1)S(1)}) custom-call(s32[1]{0:T(128)} %bitcast.1.band_ref, bf16[2,64,896]{2,1,0:T(8,128)(2,1)} %copy-done, bf16[2,64,896]{2,1,0:T(8,128)(2,1)} %copy-done.2, bf16[2,64,896]{2,1,0:T(8,128)(2,1)} %copy-done.4, ...), custom_call_target="tpu_custom_call" | custom-call | tf_op jit(solution)/shard_map/density/pallas_call | solution.py:156
  74.1 0.9 mix.1
  75.0 0.6 collective-permute-start.16
  75.6 0.6 prepare.1
  76.2 1.7 %collective-permute-done.16.m_ref = bf16[512,1024]{1,0:T(8,128)(2,1)S(1)} collective-permute-done((bf16[512,1024]{1,0:T(8,128)(2,1)S(1)}, bf16[512,1024]{1,0:T(8,128)(2,1)S(1)}, u32[]{:S(2)}, u32[]{:S(2)}) %collective-permute-start.16) | collective-permute-done | bytes 1048608 | tf_op jit(solution)/shard_map/ppermute | solution.py:41
  77.9 4.0 %project.1 = bf16[64,8,896]{2,1,0:T(8,128)(2,1)S(1)} custom-call(bf16[512,1024]{1,0:T(8,128)(2,1)S(1)} %collective-permute-done.16.m_ref, bf16[432,1024]{1,0:T(8,128)(2,1)S(1)} %get-tuple-element.55.left_ref, bf16[1024,896]{1,0:T(8,128)(2,1)S(1)} %get-tuple-element.56.right_ref), custom_call_target="tpu_custom_call" | custom-call | tf_op jit(solution)/shard_map/project/pallas_call | solution.py:253
  81.9 17.2 %all_to_all.15 = bf16[16,4,8,896]{3,2,1,0:T(8,128)(2,1)S(1)} all-to-all(bf16[16,4,8,896]{3,2,1,0:T(8,128)(2,1)S(1)} %bitcast.13), channel_id=1, replica_groups={{0,1,8,9,16,17,24,25,32,33,40,41,48,49,56,57},{2,3,10,11,18,19,26,27,34..., dimensions={0} | all-to-all | bytes 1835008 | tf_op jit(solution)/shard_map/all_to_all | solution.py:290
  99.1 0.8 convert_reduce_fusion
  99.9 5.6 %all-to-all-start.2 = ((f32[4,8,896]{2,1,0:T(8,128)}), f32[4,8,896]{2,1,0:T(8,128)S(1)}, u32[]{:S(2)}, u32[]{:S(2)}) async-start(f32[4,8,896]{2,1,0:T(8,128)} %convert_reduce_fusion), calls=%async_computation.2 | async-start | bytes 229376 | tf_op jit(solution)/shard_map/all_to_all | solution.py:292
  105.4 8.9 %all-to-all-done.2 = f32[4,8,896]{2,1,0:T(8,128)S(1)} async-done(((f32[4,8,896]{2,1,0:T(8,128)}), f32[4,8,896]{2,1,0:T(8,128)S(1)}, u32[]{:S(2)}, u32[]{:S(2)}) %all-to-all-start.2) | async-done | bytes 114720 | tf_op jit(solution)/shard_map/all_to_all | solution.py:292
  114.6 0.7 fusion.1
  (53 shorter events, 0.5 us)
Async XLA Ops:
  1.0 6.7 %collective-permute-start.2 = (bf16[64,896]{1,0:T(8,128)(2,1)S(1)}, bf16[64,896]{1,0:T(8,128)(2,1)S(1)}, u32[]{:S(2)}, u32[]{:S(2)}) collective-permute-start(bf16[64,896]{1,0:T(8,128)(2,1)S(1)} %lay.1.refs_0_), channel_id=1, source_target_pairs={{0,128},{64,192},{128,0},{192,64},{1,129},{65,193},{129,1},{193,65... | collective-permute-start | bytes 344072 | tf_op jit(solution)/shard_map/ppermute | solution.py:41
  2.4 2.1 %collective-permute-start = (s32[1]{0:T(128)}, s32[1]{0:T(128)}, u32[]{:S(2)}, u32[]{:S(2)}) collective-permute-start(s32[1]{0:T(128)} %param.6), channel_id=1, source_target_pairs={{0,64},{64,0},{128,192},{192,128},{1,65},{65,1},{129,193},{193,129... | collective-permute-start | bytes 20 | tf_op jit(solution)/shard_map/ppermute | solution.py:41
  2.4 5.3 %collective-permute-start.1 = (s32[1]{0:T(128)}, s32[1]{0:T(128)}, u32[]{:S(2)}, u32[]{:S(2)}) collective-permute-start(s32[1]{0:T(128)} %param.6), channel_id=1, source_target_pairs={{0,128},{64,192},{128,0},{192,64},{1,129},{65,193},{129,1},{193,65... | collective-permute-start | bytes 20 | tf_op jit(solution)/shard_map/ppermute | solution.py:41
  7.7 15.0 %copy-start = (bf16[2,64,896]{2,1,0:T(8,128)(2,1)}, bf16[2,64,896]{2,1,0:T(8,128)(2,1)S(1)}, u32[]{:S(2)}) copy-start(bf16[2,64,896]{2,1,0:T(8,128)(2,1)S(1)} %bundle.2.refs_0_.refs_6_) | copy-start | bytes 688132
  7.8 15.0 %collective-permute-start.3 = (bf16[2,64,896]{2,1,0:T(8,128)(2,1)S(1)}, bf16[2,64,896]{2,1,0:T(8,128)(2,1)S(1)}, u32[]{:S(2)}, u32[]{:S(2)}) collective-permute-start(bf16[2,64,896]{2,1,0:T(8,128)(2,1)S(1)} %bundle.2.refs_0_.refs_6_), channel_id=1, source_target_pairs={{0,16},{1,17},{2,18},{3,19},{4,20},{5,21},{6,22},{7,23},{8,24},{9,... | collective-permute-start | bytes 688136 | tf_op jit(solution)/shard_map/ppermute | solution.py:37
  9.4 13.4 %collective-permute-start.4 = (bf16[2,64,896]{2,1,0:T(8,128)(2,1)S(1)}, bf16[2,64,896]{2,1,0:T(8,128)(2,1)S(1)}, u32[]{:S(2)}, u32[]{:S(2)}) collective-permute-start(bf16[2,64,896]{2,1,0:T(8,128)(2,1)S(1)} %bundle.2.refs_0_.refs_6_), channel_id=1, source_target_pairs={{0,48},{1,49},{2,50},{3,51},{4,52},{5,53},{6,54},{7,55},{8,56},{9,... | collective-permute-start | bytes 688136 | tf_op jit(solution)/shard_map/ppermute | solution.py:37
  11.1 11.7 %collective-permute-start.5 = (bf16[2,64,896]{2,1,0:T(8,128)(2,1)S(1)}, bf16[2,64,896]{2,1,0:T(8,128)(2,1)S(1)}, u32[]{:S(2)}, u32[]{:S(2)}) collective-permute-start(bf16[2,64,896]{2,1,0:T(8,128)(2,1)S(1)} %bundle.2.refs_0_.refs_6_), channel_id=1, source_target_pairs={{0,1},{1,2},{2,3},{3,4},{4,5},{5,6},{6,7},{7,0},{8,9},{9,10},{10,1... | collective-permute-start | bytes 688136 | tf_op jit(solution)/shard_map/ppermute | solution.py:37
  13.0 9.8 %collective-permute-start.6 = (bf16[2,64,896]{2,1,0:T(8,128)(2,1)S(1)}, bf16[2,64,896]{2,1,0:T(8,128)(2,1)S(1)}, u32[]{:S(2)}, u32[]{:S(2)}) collective-permute-start(bf16[2,64,896]{2,1,0:T(8,128)(2,1)S(1)} %bundle.2.refs_0_.refs_6_), channel_id=1, source_target_pairs={{0,7},{1,0},{2,1},{3,2},{4,3},{5,4},{6,5},{7,6},{8,15},{9,8},{10,9... | collective-permute-start | bytes 688136 | tf_op jit(solution)/shard_map/ppermute | solution.py:37
  17.6 0.7 copy-start.1
  22.8 28.5 %copy-start.2 = (bf16[2,64,896]{2,1,0:T(8,128)(2,1)}, bf16[2,64,896]{2,1,0:T(8,128)(2,1)S(1)}, u32[]{:S(2)}) copy-start(bf16[2,64,896]{2,1,0:T(8,128)(2,1)S(1)} %collective-permute-done.3.refs_1_) | copy-start | bytes 688132
  22.8 28.5 %copy-start.3 = (bf16[2,64,896]{2,1,0:T(8,128)(2,1)}, bf16[2,64,896]{2,1,0:T(8,128)(2,1)S(1)}, u32[]{:S(2)}) copy-start(bf16[2,64,896]{2,1,0:T(8,128)(2,1)S(1)} %collective-permute-done.4.refs_3_) | copy-start | bytes 688132
  22.8 28.5 %copy-start.7 = (bf16[2,64,896]{2,1,0:T(8,128)(2,1)}, bf16[2,64,896]{2,1,0:T(8,128)(2,1)S(1)}, u32[]{:S(2)}) copy-start(bf16[2,64,896]{2,1,0:T(8,128)(2,1)S(1)} %collective-permute-done.5.refs_7_) | copy-start | bytes 688132
  22.8 28.4 %copy-start.8 = (bf16[2,64,896]{2,1,0:T(8,128)(2,1)}, bf16[2,64,896]{2,1,0:T(8,128)(2,1)S(1)}, u32[]{:S(2)}) copy-start(bf16[2,64,896]{2,1,0:T(8,128)(2,1)S(1)} %collective-permute-done.6.refs_8_) | copy-start | bytes 688132
  22.8 46.2 %all-to-all-start = ((bf16[8,3,64,512]{3,2,1,0:T(8,128)(2,1)}), bf16[8,3,64,512]{3,2,1,0:T(8,128)(2,1)S(1)}, u32[]{:S(2)}, u32[]{:S(2)}) async-start(bf16[8,3,64,512]{3,2,1,0:T(8,128)(2,1)} %pack.1), calls=%async_computation | async-start | bytes 3145728 | tf_op jit(solution)/shard_map/all_to_all | solution.py:314
  27.6 23.7 %collective-permute-start.7 = (bf16[2,64,896]{2,1,0:T(8,128)(2,1)S(1)}, bf16[2,64,896]{2,1,0:T(8,128)(2,1)S(1)}, u32[]{:S(2)}, u32[]{:S(2)}) collective-permute-start(bf16[2,64,896]{2,1,0:T(8,128)(2,1)S(1)} %collective-permute-done.3.refs_1_), channel_id=1, source_target_pairs={{0,16},{1,17},{2,18},{3,19},{4,20},{5,21},{6,22},{7,23},{8,24},{9,... | collective-permute-start | bytes 688136 | tf_op jit(solution)/shard_map/ppermute | solution.py:37
  29.0 25.4 %collective-permute-start.10 = (bf16[2,64,896]{2,1,0:T(8,128)(2,1)S(1)}, bf16[2,64,896]{2,1,0:T(8,128)(2,1)S(1)}, u32[]{:S(2)}, u32[]{:S(2)}) collective-permute-start(bf16[2,64,896]{2,1,0:T(8,128)(2,1)S(1)} %collective-permute-done.5.refs_7_), channel_id=1, source_target_pairs={{0,1},{1,2},{2,3},{3,4},{4,5},{5,6},{6,7},{7,0},{8,9},{9,10},{10,1... | collective-permute-start | bytes 688136 | tf_op jit(solution)/shard_map/ppermute | solution.py:37
  29.0 25.4 %collective-permute-start.11 = (bf16[2,64,896]{2,1,0:T(8,128)(2,1)S(1)}, bf16[2,64,896]{2,1,0:T(8,128)(2,1)S(1)}, u32[]{:S(2)}, u32[]{:S(2)}) collective-permute-start(bf16[2,64,896]{2,1,0:T(8,128)(2,1)S(1)} %collective-permute-done.6.refs_8_), channel_id=1, source_target_pairs={{0,7},{1,0},{2,1},{3,2},{4,3},{5,4},{6,5},{7,6},{8,15},{9,8},{10,9... | collective-permute-start | bytes 688136 | tf_op jit(solution)/shard_map/ppermute | solution.py:37
  51.2 18.1 %copy-start.4 = (bf16[2,64,896]{2,1,0:T(8,128)(2,1)}, bf16[2,64,896]{2,1,0:T(8,128)(2,1)S(1)}, u32[]{:S(2)}) copy-start(bf16[2,64,896]{2,1,0:T(8,128)(2,1)S(1)} %collective-permute-done.7.refs_2_) | copy-start | bytes 688132
  51.3 10.3 %collective-permute-start.8 = (bf16[4,64,896]{2,1,0:T(8,128)(2,1)S(1)}, bf16[4,64,896]{2,1,0:T(8,128)(2,1)S(1)}, u32[]{:S(2)}, u32[]{:S(2)}) collective-permute-start(bf16[4,64,896]{2,1,0:T(8,128)(2,1)S(1)} %bundle.3), channel_id=1, source_target_pairs={{0,8},{1,9},{2,10},{3,11},{4,12},{5,13},{6,14},{7,15},{8,0},{9,1},... | collective-permute-start | bytes 1376264 | tf_op jit(solution)/shard_map/ppermute | solution.py:37
  52.0 11.0 %collective-permute-start.9 = (bf16[4,64,896]{2,1,0:T(8,128)(2,1)S(1)}, bf16[4,64,896]{2,1,0:T(8,128)(2,1)S(1)}, u32[]{:S(2)}, u32[]{:S(2)}) collective-permute-start(bf16[4,64,896]{2,1,0:T(8,128)(2,1)S(1)} %bundle.3), channel_id=1, source_target_pairs={{128,8},{129,9},{130,10},{131,11},{132,12},{133,13},{134,14},{135,... | collective-permute-start | bytes 1376264 | tf_op jit(solution)/shard_map/ppermute | solution.py:47
  54.4 14.6 %copy-start.9 = (bf16[2,64,896]{2,1,0:T(8,128)(2,1)}, bf16[2,64,896]{2,1,0:T(8,128)(2,1)S(1)}, u32[]{:S(2)}) copy-start(bf16[2,64,896]{2,1,0:T(8,128)(2,1)S(1)} %collective-permute-done.10.refs_9_) | copy-start | bytes 688132
  54.4 7.2 %collective-permute-start.12 = (bf16[2,64,896]{2,1,0:T(8,128)(2,1)S(1)}, bf16[2,64,896]{2,1,0:T(8,128)(2,1)S(1)}, u32[]{:S(2)}, u32[]{:S(2)}) collective-permute-start(bf16[2,64,896]{2,1,0:T(8,128)(2,1)S(1)} %collective-permute-done.10.refs_9_), channel_id=1, source_target_pairs={{0,1},{1,2},{2,3},{3,4},{4,5},{5,6},{6,7},{7,0},{8,9},{9,10},{10,1... | collective-permute-start | bytes 688136 | tf_op jit(solution)/shard_map/ppermute | solution.py:37
  54.4 8.5 %copy-start.10 = (bf16[2,64,896]{2,1,0:T(8,128)(2,1)}, bf16[2,64,896]{2,1,0:T(8,128)(2,1)S(1)}, u32[]{:S(2)}) copy-start(bf16[2,64,896]{2,1,0:T(8,128)(2,1)S(1)} %collective-permute-done.11.refs_10_) | copy-start | bytes 688132
  54.4 7.2 %collective-permute-start.13 = (bf16[2,64,896]{2,1,0:T(8,128)(2,1)S(1)}, bf16[2,64,896]{2,1,0:T(8,128)(2,1)S(1)}, u32[]{:S(2)}, u32[]{:S(2)}) collective-permute-start(bf16[2,64,896]{2,1,0:T(8,128)(2,1)S(1)} %collective-permute-done.11.refs_10_), channel_id=1, source_target_pairs={{0,7},{1,0},{2,1},{3,2},{4,3},{5,4},{6,5},{7,6},{8,15},{9,8},{10,9... | collective-permute-start | bytes 688136 | tf_op jit(solution)/shard_map/ppermute | solution.py:37
  61.6 7.7 %copy-start.11 = (bf16[2,64,896]{2,1,0:T(8,128)(2,1)}, bf16[2,64,896]{2,1,0:T(8,128)(2,1)S(1)}, u32[]{:S(2)}) copy-start(bf16[2,64,896]{2,1,0:T(8,128)(2,1)S(1)} %collective-permute-done.12.refs_11_) | copy-start | bytes 688132
  61.6 7.3 %collective-permute-start.14 = (bf16[2,64,896]{2,1,0:T(8,128)(2,1)S(1)}, bf16[2,64,896]{2,1,0:T(8,128)(2,1)}, u32[]{:S(2)}, u32[]{:S(2)}) collective-permute-start(bf16[2,64,896]{2,1,0:T(8,128)(2,1)S(1)} %collective-permute-done.12.refs_11_), channel_id=1, source_target_pairs={{0,1},{1,2},{2,3},{3,4},{4,5},{5,6},{6,7},{7,0},{8,9},{9,10},{10,1... | collective-permute-start | bytes 688136 | tf_op jit(solution)/shard_map/ppermute | solution.py:37
  61.7 7.3 %copy-start.12 = (bf16[2,64,896]{2,1,0:T(8,128)(2,1)}, bf16[2,64,896]{2,1,0:T(8,128)(2,1)S(1)}, u32[]{:S(2)}) copy-start(bf16[2,64,896]{2,1,0:T(8,128)(2,1)S(1)} %collective-permute-done.13.refs_12_) | copy-start | bytes 688132
  61.7 7.7 %copy-start.5 = (bf16[4,64,896]{2,1,0:T(8,128)(2,1)}, bf16[4,64,896]{2,1,0:T(8,128)(2,1)S(1)}, u32[]{:S(2)}) copy-start(bf16[4,64,896]{2,1,0:T(8,128)(2,1)S(1)} %collective-permute-done.8.refs_4_) | copy-start | bytes 1376260
  62.9 6.1 %copy-start.6 = (bf16[4,64,896]{2,1,0:T(8,128)(2,1)}, bf16[4,64,896]{2,1,0:T(8,128)(2,1)S(1)}, u32[]{:S(2)}) copy-start(bf16[4,64,896]{2,1,0:T(8,128)(2,1)S(1)} %collective-permute-done.9.refs_5_) | copy-start | bytes 1376260
  69.0 5.1 %collective-permute-start.15 = (bf16[8,64,512]{2,1,0:T(8,128)(2,1)S(1)}, bf16[8,64,512]{2,1,0:T(8,128)(2,1)S(1)}, u32[]{:S(2)}, u32[]{:S(2)}) collective-permute-start(bf16[8,64,512]{2,1,0:T(8,128)(2,1)S(1)} %slice_bitcast_fusion), channel_id=1, source_target_pairs={{0,64},{64,0},{128,192},{192,128},{1,65},{65,1},{129,193},{193,129... | collective-permute-start | bytes 1572872 | tf_op jit(solution)/shard_map/ppermute | solution.py:41
  75.0 2.8 %collective-permute-start.16 = (bf16[512,1024]{1,0:T(8,128)(2,1)S(1)}, bf16[512,1024]{1,0:T(8,128)(2,1)S(1)}, u32[]{:S(2)}, u32[]{:S(2)}) collective-permute-start(bf16[512,1024]{1,0:T(8,128)(2,1)S(1)} %mix.1), channel_id=1, source_target_pairs={{0,64},{64,0},{128,192},{192,128},{1,65},{65,1},{129,193},{193,129... | collective-permute-start | bytes 3145736 | tf_op jit(solution)/shard_map/ppermute | solution.py:41
  99.9 14.5 %all-to-all-start.2 = ((f32[4,8,896]{2,1,0:T(8,128)}), f32[4,8,896]{2,1,0:T(8,128)S(1)}, u32[]{:S(2)}, u32[]{:S(2)}) async-start(f32[4,8,896]{2,1,0:T(8,128)} %convert_reduce_fusion), calls=%async_computation.2 | async-start | bytes 229376 | tf_op jit(solution)/shard_map/all_to_all | solution.py:292

commit v23 on v21

--- a/solution.py
+++ b/solution.py
@@ -88,7 +88,7 @@
     )
 
 
-def pack_body(odd_ref, own_ref, core_ref, far_ref, stored_ref, kernels_ref, out_ref, sem):
+def pack_body(odd_ref, own_ref, core_ref, far_ref, stored_ref, kernels_ref, out_ref, held, sem, out_sem):
     odd = odd_ref[0] == 1
     own, core, far = stored_ref[own_ref[0]], stored_ref[core_ref[0]], stored_ref[far_ref[0]]
     shared = jnp.where(odd, own, core)
@@ -97,25 +97,37 @@
     for i in range(GROUPS):
         at = pl.ds(i * BLOCK, BLOCK)
         half = kernels_ref.at[shared, odd_ref[0], :, at]
-        copies.append(pltpu.make_async_copy(half, out_ref.at[i, 0], sem.at[0, i]))
+        copies.append(pltpu.make_async_copy(half, held.at[i, 0], sem.at[0, i]))
         both = kernels_ref.at[single, :, :, at]
-        copies.append(pltpu.make_async_copy(both, out_ref.at[i, pl.ds(1, 2)], sem.at[1, i]))
+        copies.append(pltpu.make_async_copy(both, held.at[i, pl.ds(1, 2)], sem.at[1, i]))
     for copy in copies:
         copy.start()
-    for copy in copies:
+    sent = []
+    for i in range(GROUPS):
+        copies[2 * i].wait()
+        copies[2 * i + 1].wait()
+        sent.append(pltpu.make_async_copy(held.at[i], out_ref.at[i], out_sem.at[i]))
+        sent[i].start()
+    for copy in sent:
         copy.wait()
 
 
 def pack(odd, own, core, far, stored, kernels):
+    blocks = (GROUPS, 3, SLAB, BLOCK)
+    in_hbm = pl.BlockSpec(memory_space=pltpu.HBM)
     return pl.pallas_call(
         pack_body,
-        out_shape=jax.ShapeDtypeStruct((GROUPS, 3, SLAB, BLOCK), jnp.bfloat16),
-        in_specs=[IN_SMEM] * 5 + [pl.BlockSpec(memory_space=pltpu.HBM)],
-        out_specs=IN_VMEM,
-        scratch_shapes=[pltpu.SemaphoreType.DMA((2, GROUPS))],
+        out_shape=jax.ShapeDtypeStruct(blocks, jnp.bfloat16),
+        in_specs=[IN_SMEM] * 5 + [in_hbm],
+        out_specs=in_hbm,
+        scratch_shapes=[
+            pltpu.VMEM(blocks, jnp.bfloat16),
+            pltpu.SemaphoreType.DMA((2, GROUPS)),
+            pltpu.SemaphoreType.DMA((GROUPS,)),
+        ],
         compiler_params=PARAMS,
         name="pack",
-    )(odd, own, core, far, stored, away(kernels))
+    )(odd, own, core, far, away(stored), away(kernels))
 
 
 def density_body(band_ref, *refs):
@@ -130,13 +142,14 @@
         place = (y + NY - dy) % NY * NX + (x + side) % NX
         return pl.ds(pl.multiple_of(place * SLAB, SLAB), SLAB)
 
-    def col_at(dz):
-        return pl.ds(pl.multiple_of((z + NZ + dz) % NZ * SLAB, SLAB), SLAB)
-
     moves = []
-    for piece, dz in zip(cols[:-1], Z_ORDER):
-        moves.append((piece.at[0], col_ref.at[col_at(dz), :]))
-        moves.append((piece.at[1], other_cols.at[col_at(dz), :]))
+    for piece, dz in zip(cols, Z_ORDER):
+        at = pl.ds(pl.multiple_of((z + NZ + dz) % NZ * SLAB, SLAB), SLAB)
+        moves.append((piece.at[0], col_ref.at[at, :]))
+        moves.append((piece.at[1], other_cols.at[at, :]))
+    for side, piece in enumerate((over_here, over_side)):
+        moves.append((piece.at[0], row_ref.at[row_at(2, side), :]))
+        moves.append((piece.at[1], other_rows.at[row_at(2, side), :]))
     copies = [pltpu.make_async_copy(*move, sem.at[i]) for i, move in enumerate(moves)]
     for copy in copies:
         copy.start()
@@ -144,11 +157,6 @@
         for side in range(NX):
             row_ref[row_at(dy, side), :] = piece[2 * side]
             other_rows[row_at(dy, side), :] = piece[2 * side + 1]
-    for side, piece in enumerate((over_here, over_side)):
-        row_ref[row_at(2, side), :] = piece[0]
-        other_rows[row_at(2, side), :] = piece[1]
-    col_ref[col_at(Z_ORDER[-1]), :] = cols[-1][0]
-    other_cols[col_at(Z_ORDER[-1]), :] = cols[-1][1]
     for copy in copies:
         copy.wait()
     for rows, columns, out in ((row_ref, col_ref, own_ref), (other_rows, other_cols, far_ref)):
@@ -161,15 +169,15 @@
     product = pltpu.VMEM((BLOCK, 2 * BLOCK), jnp.float32)
     points = pltpu.VMEM((BLOCK, LANES), jnp.bfloat16)
     in_hbm = pl.BlockSpec(memory_space=pltpu.HBM)
-    specs = [IN_VMEM] * 5 + [in_hbm] * (NZ - 1) + [IN_VMEM]
-    arrays = [*map(near, (four, up, *over, down)), *map(away, cols[:-1]), near(cols[-1])]
+    specs = [IN_VMEM] * 2 + [in_hbm] * 2 + [IN_VMEM] + [in_hbm] * NZ
+    arrays = [near(four), near(up), *map(away, over), near(down), *map(away, cols)]
     return pl.pallas_call(
         density_body,
         out_shape=[product, product, points, points],
         in_specs=[IN_SMEM] + specs,
         out_specs=[IN_VMEM] * 4,
         scratch_shapes=[pltpu.VMEM((BLOCK, LANES), jnp.bfloat16)] * 2
-        + [pltpu.SemaphoreType.DMA((2 * (NZ - 1),))],
+        + [pltpu.SemaphoreType.DMA((2 * NX + 2 * NZ,))],
         compiler_params=PARAMS,
         name="density",
     )(band, *arrays)

time: 110 us -> 108 us (0.982)
  local copies, waits for them, and re-layouts: 7.99 us -> 5.45 us
    unnamed x36 -> x32, local copies, waits for them, and re-layouts: 7.69 us -> 5.15 us
  transfers between devices with their start and end apart: 20 -> 20, of which waited for: 7 -> 7; matrix products, arithmetic and copies ran while one was open for 0% -> 0% of each run, Pallas kernels for 8% -> 9%
where the time goes in v23:
time: 108 us
  starting transfers between devices  39.5 us (37%)
  waiting for transfers between devices  26 us (24%)
  blocking collectives  18.9 us (17%)
  Pallas kernels  15.2 us (14%)
  local copies, waits for them, and re-layouts  5.45 us (5%)
  other arithmetic  1.52 us (1%)
    ppermute x12, starting transfers between devices, shift(): return lax.ppermute(block, 'band', band_route(dy, dx, dz))  22.8 us
    all_to_all x1, blocking collectives, reduce_windows(): parts = lax.all_to_all(parts, 'band', 0, 0, axis_index_groups=wide)  18.9 us
    ppermute x12, waiting for transfers between devices, shift(): return lax.ppermute(block, 'band', band_route(dy, dx, dz))  11.7 us
    all_to_all x1, waiting for transfers between devices, reduce_windows(): lax.all_to_all(parts, 'band', 0, 0, axis_index_groups=deep)  8.91 us
    all_to_all x1, starting transfers between devices, reduce_windows(): lax.all_to_all(parts, 'band', 0, 0, axis_index_groups=deep)  7.55 us
    ppermute x5, waiting for transfers between devices, swap_groups(): return lax.ppermute(block, 'kgrp', [(k, k ^ bit) for k in range(4)])  5.45 us
    unnamed x32, local copies, waits for them, and re-layouts  5.15 us
    all_to_all x1, starting transfers between devices, on_device(): kern = lax.all_to_all(sends, 'band', 0, 0, axis_index_groups=over_yx)  4.73 us
  transfers between devices with their start and end apart: 20, of which 7 were waited for; matrix products, arithmetic and copies ran while one was open for 0% of the time, Pallas kernels for 9%

profile of v23, /device:TPU:6, one launch (start us, length us, event | category | flops | bytes accessed | tf_op | source)
XLA Modules:
  0.0 107.6 jit_solution(13996595085333202111)
XLA Ops:
  0.0 1.0 lay.1.own_ref
  1.0 1.4 %collective-permute-start.2 = (bf16[64,896]{1,0:T(8,128)(2,1)S(1)}, bf16[64,896]{1,0:T(8,128)(2,1)S(1)}, u32[]{:S(2)}, u32[]{:S(2)}) collective-permute-start(bf16[64,896]{1,0:T(8,128)(2,1)S(1)} %lay.1.own_ref), channel_id=1, source_target_pairs={{0,128},{64,192},{128,0},{192,64},{1,129},{65,193},{129,1},{193,65... | collective-permute-start | bytes 344072 | tf_op jit(solution)/shard_map/ppermute | solution.py:41
  2.4 1.7 %collective-permute-start.3 = (bf16[64,896]{1,0:T(8,128)(2,1)S(1)}, bf16[64,896]{1,0:T(8,128)(2,1)S(1)}, u32[]{:S(2)}, u32[]{:S(2)}) collective-permute-start(bf16[64,896]{1,0:T(8,128)(2,1)S(1)} %lay.1.own_ref), channel_id=1, source_target_pairs={{0,8},{1,9},{2,10},{3,11},{4,12},{5,13},{6,14},{7,15},{8,0},{9,1},... | collective-permute-start | bytes 344072 | tf_op jit(solution)/shard_map/ppermute | solution.py:37
  4.1 1.0 collective-permute-start.4
  5.1 1.4 %collective-permute-start.1 = (s32[1]{0:T(128)}, s32[1]{0:T(128)}, u32[]{:S(2)}, u32[]{:S(2)}) collective-permute-start(s32[1]{0:T(128)} %param.6), channel_id=1, source_target_pairs={{0,128},{64,192},{128,0},{192,64},{1,129},{65,193},{129,1},{193,65... | collective-permute-start | bytes 20 | tf_op jit(solution)/shard_map/ppermute | solution.py:41
  6.5 3.7 %collective-permute-done.1.far_ref = s32[1]{0:T(128)} collective-permute-done((s32[1]{0:T(128)}, s32[1]{0:T(128)}, u32[]{:S(2)}, u32[]{:S(2)}) %collective-permute-start.1) | collective-permute-done | bytes 36 | tf_op jit(solution)/shard_map/ppermute | solution.py:41
  10.3 1.7 %collective-permute-start.5 = (bf16[4,64,896]{2,1,0:T(8,128)(2,1)S(1)}, bf16[4,64,896]{2,1,0:T(8,128)(2,1)S(1)}, u32[]{:S(2)}, u32[]{:S(2)}) collective-permute-start(bf16[4,64,896]{2,1,0:T(8,128)(2,1)S(1)} %get-tuple-element.35.refs_0_), channel_id=1, source_target_pairs={{0,16},{1,17},{2,18},{3,19},{4,20},{5,21},{6,22},{7,23},{8,24},{9,... | collective-permute-start | bytes 1376264 | tf_op jit(solution)/shard_map/ppermute | solution.py:37
  12.0 1.7 %collective-permute-start.6 = (bf16[4,64,896]{2,1,0:T(8,128)(2,1)S(1)}, bf16[4,64,896]{2,1,0:T(8,128)(2,1)S(1)}, u32[]{:S(2)}, u32[]{:S(2)}) collective-permute-start(bf16[4,64,896]{2,1,0:T(8,128)(2,1)S(1)} %get-tuple-element.35.refs_0_), channel_id=1, source_target_pairs={{0,48},{1,49},{2,50},{3,51},{4,52},{5,53},{6,54},{7,55},{8,56},{9,... | collective-permute-start | bytes 1376264 | tf_op jit(solution)/shard_map/ppermute | solution.py:37
  13.7 1.9 %collective-permute-start.7 = (bf16[2,64,896]{2,1,0:T(8,128)(2,1)S(1)}, bf16[2,64,896]{2,1,0:T(8,128)(2,1)S(1)}, u32[]{:S(2)}, u32[]{:S(2)}) collective-permute-start(bf16[2,64,896]{2,1,0:T(8,128)(2,1)S(1)} %get-tuple-element.44.refs_5_), channel_id=1, source_target_pairs={{0,1},{1,2},{2,3},{3,4},{4,5},{5,6},{6,7},{7,0},{8,9},{9,10},{10,1... | collective-permute-start | bytes 688136 | tf_op jit(solution)/shard_map/ppermute | solution.py:37
  15.6 3.9 %collective-permute-start.8 = (bf16[2,64,896]{2,1,0:T(8,128)(2,1)S(1)}, bf16[2,64,896]{2,1,0:T(8,128)(2,1)S(1)}, u32[]{:S(2)}, u32[]{:S(2)}) collective-permute-start(bf16[2,64,896]{2,1,0:T(8,128)(2,1)S(1)} %get-tuple-element.44.refs_5_), channel_id=1, source_target_pairs={{0,7},{1,0},{2,1},{3,2},{4,3},{5,4},{6,5},{7,6},{8,15},{9,8},{10,9... | collective-permute-start | bytes 688136 | tf_op jit(solution)/shard_map/ppermute | solution.py:37
  20.2 4.5 %pack.1 = bf16[8,3,64,512]{3,2,1,0:T(8,128)(2,1)} custom-call(s32[1]{0:T(128)} %bitcast.odd_ref, s32[1]{0:T(128)S(6)} %copy.5.own_ref, s32[1]{0:T(128)} %collective-permute-done.core_ref, s32[1]{0:T(128)} %collective-permute-done.1.far_ref, s32[8]{0:T(128)} %stored_ref.1, bf16[4,2,64,4096]{3,2,1,0:T(8,128)(2,1)} %kernels_ref.1), custom_call_target="tpu_custom_call" | custom-call | tf_op jit(solution)/shard_map/pack/pallas_call | solution.py:118
  24.8 4.7 %all-to-all-start = ((bf16[8,3,64,512]{3,2,1,0:T(8,128)(2,1)}), bf16[8,3,64,512]{3,2,1,0:T(8,128)(2,1)S(1)}, u32[]{:S(2)}, u32[]{:S(2)}) async-start(bf16[8,3,64,512]{3,2,1,0:T(8,128)(2,1)} %pack.1), calls=%async_computation | async-start | bytes 3145728 | tf_op jit(solution)/shard_map/all_to_all | solution.py:343
  29.5 1.8 %collective-permute-start.11 = (bf16[2,64,896]{2,1,0:T(8,128)(2,1)S(1)}, bf16[2,64,896]{2,1,0:T(8,128)(2,1)S(1)}, u32[]{:S(2)}, u32[]{:S(2)}) collective-permute-start(bf16[2,64,896]{2,1,0:T(8,128)(2,1)S(1)} %collective-permute-done.7.refs_6_), channel_id=1, source_target_pairs={{0,1},{1,2},{2,3},{3,4},{4,5},{5,6},{6,7},{7,0},{8,9},{9,10},{10,1... | collective-permute-start | bytes 688136 | tf_op jit(solution)/shard_map/ppermute | solution.py:37
  31.3 3.9 %collective-permute-start.12 = (bf16[2,64,896]{2,1,0:T(8,128)(2,1)S(1)}, bf16[2,64,896]{2,1,0:T(8,128)(2,1)S(1)}, u32[]{:S(2)}, u32[]{:S(2)}) collective-permute-start(bf16[2,64,896]{2,1,0:T(8,128)(2,1)S(1)} %collective-permute-done.8.refs_7_), channel_id=1, source_target_pairs={{0,7},{1,0},{2,1},{3,2},{4,3},{5,4},{6,5},{7,6},{8,15},{9,8},{10,9... | collective-permute-start | bytes 688136 | tf_op jit(solution)/shard_map/ppermute | solution.py:37
  35.3 4.0 %collective-permute-done.11.refs_8_ = bf16[2,64,896]{2,1,0:T(8,128)(2,1)S(1)} collective-permute-done((bf16[2,64,896]{2,1,0:T(8,128)(2,1)S(1)}, bf16[2,64,896]{2,1,0:T(8,128)(2,1)S(1)}, u32[]{:S(2)}, u32[]{:S(2)}) %collective-permute-start.11) | collective-permute-done | bytes 229408 | tf_op jit(solution)/shard_map/ppermute | solution.py:37
  39.3 2.8 %collective-permute-start.10 = (bf16[2,64,896]{2,1,0:T(8,128)(2,1)S(1)}, bf16[2,64,896]{2,1,0:T(8,128)(2,1)S(1)}, u32[]{:S(2)}, u32[]{:S(2)}) collective-permute-start(bf16[2,64,896]{2,1,0:T(8,128)(2,1)S(1)} %slice.19), channel_id=1, source_target_pairs={{0,48},{1,49},{2,50},{3,51},{4,52},{5,53},{6,54},{7,55},{8,56},{9,... | collective-permute-start | bytes 688136 | tf_op jit(solution)/shard_map/ppermute | solution.py:37
  42.2 3.3 %collective-permute-start.14 = (bf16[2,64,896]{2,1,0:T(8,128)(2,1)S(1)}, bf16[2,64,896]{2,1,0:T(8,128)(2,1)S(1)}, u32[]{:S(2)}, u32[]{:S(2)}) collective-permute-start(bf16[2,64,896]{2,1,0:T(8,128)(2,1)S(1)} %collective-permute-done.12.refs_9_), channel_id=1, source_target_pairs={{0,7},{1,0},{2,1},{3,2},{4,3},{5,4},{6,5},{7,6},{8,15},{9,8},{10,9... | collective-permute-start | bytes 688136 | tf_op jit(solution)/shard_map/ppermute | solution.py:37
  45.5 1.0 collective-permute-done.13.refs_10_
  46.5 5.4 %collective-permute-done.10.refs_3_ = bf16[2,64,896]{2,1,0:T(8,128)(2,1)S(1)} collective-permute-done((bf16[2,64,896]{2,1,0:T(8,128)(2,1)S(1)}, bf16[2,64,896]{2,1,0:T(8,128)(2,1)S(1)}, u32[]{:S(2)}, u32[]{:S(2)}) %collective-permute-start.10) | collective-permute-done | bytes 229408 | tf_op jit(solution)/shard_map/ppermute | solution.py:37
  51.9 1.3 %collective-permute-done.9.refs_2_ = bf16[2,64,896]{2,1,0:T(8,128)(2,1)S(1)} collective-permute-done((bf16[2,64,896]{2,1,0:T(8,128)(2,1)S(1)}, bf16[2,64,896]{2,1,0:T(8,128)(2,1)S(1)}, u32[]{:S(2)}, u32[]{:S(2)}) %collective-permute-start.9) | collective-permute-done | bytes 229408 | tf_op jit(solution)/shard_map/ppermute | solution.py:37
  55.3 1.0 copy-done.1
  56.3 1.0 copy-done.3
  57.4 1.0 copy-done.5
  58.4 4.2 %density.1 = (f32[512,1024]{1,0:T(8,128)S(1)}, f32[512,1024]{1,0:T(8,128)S(1)}, bf16[512,896]{1,0:T(8,128)(2,1)S(1)}, bf16[512,896]{1,0:T(8,128)(2,1)S(1)}) custom-call(s32[1]{0:T(128)} %bitcast.1.band_ref, bf16[4,64,896]{2,1,0:T(8,128)(2,1)S(1)} %copy-done.5, bf16[4,64,896]{2,1,0:T(8,128)(2,1)S(1)} %copy-done.1, bf16[2,64,896]{2,1,0:T(8,128)(2,1)} %copy-done.13, ...), custom_call_target="tpu_custom_call" | custom-call | tf_op jit(solution)/shard_map/density/pallas_call | solution.py:174
  62.6 0.9 mix.1
  64.7 1.7 %collective-permute-done.17.m_ref = bf16[512,1024]{1,0:T(8,128)(2,1)S(1)} collective-permute-done((bf16[512,1024]{1,0:T(8,128)(2,1)S(1)}, bf16[512,1024]{1,0:T(8,128)(2,1)S(1)}, u32[]{:S(2)}, u32[]{:S(2)}) %collective-permute-start.17) | collective-permute-done | bytes 1048608 | tf_op jit(solution)/shard_map/ppermute | solution.py:41
  66.4 4.0 %project.1 = bf16[64,8,896]{2,1,0:T(8,128)(2,1)S(1)} custom-call(bf16[512,1024]{1,0:T(8,128)(2,1)S(1)} %collective-permute-done.17.m_ref, bf16[432,1024]{1,0:T(8,128)(2,1)S(1)} %get-tuple-element.57.left_ref, bf16[1024,896]{1,0:T(8,128)(2,1)S(1)} %get-tuple-element.58.right_ref), custom_call_target="tpu_custom_call" | custom-call | tf_op jit(solution)/shard_map/project/pallas_call | solution.py:271
  70.4 18.9 %all_to_all.15 = bf16[16,4,8,896]{3,2,1,0:T(8,128)(2,1)S(1)} all-to-all(bf16[16,4,8,896]{3,2,1,0:T(8,128)(2,1)S(1)} %bitcast.5), channel_id=1, replica_groups={{0,1,8,9,16,17,24,25,32,33,40,41,48,49,56,57},{2,3,10,11,18,19,26,27,34..., dimensions={0} | all-to-all | bytes 1835008 | tf_op jit(solution)/shard_map/all_to_all | solution.py:312
  89.3 0.8 convert_reduce_fusion
  90.1 7.6 %all-to-all-start.2 = ((f32[4,8,896]{2,1,0:T(8,128)}), f32[4,8,896]{2,1,0:T(8,128)S(1)}, u32[]{:S(2)}, u32[]{:S(2)}) async-start(f32[4,8,896]{2,1,0:T(8,128)} %convert_reduce_fusion), calls=%async_computation.2 | async-start | bytes 229376 | tf_op jit(solution)/shard_map/all_to_all | solution.py:314
  97.6 8.9 %all-to-all-done.2 = f32[4,8,896]{2,1,0:T(8,128)S(1)} async-done(((f32[4,8,896]{2,1,0:T(8,128)}), f32[4,8,896]{2,1,0:T(8,128)S(1)}, u32[]{:S(2)}, u32[]{:S(2)}) %all-to-all-start.2) | async-done | bytes 114720 | tf_op jit(solution)/shard_map/all_to_all | solution.py:314
  106.8 0.7 fusion.1
  (58 shorter events, 3.8 us)
Async XLA Ops:
  1.0 9.3 %collective-permute-start.2 = (bf16[64,896]{1,0:T(8,128)(2,1)S(1)}, bf16[64,896]{1,0:T(8,128)(2,1)S(1)}, u32[]{:S(2)}, u32[]{:S(2)}) collective-permute-start(bf16[64,896]{1,0:T(8,128)(2,1)S(1)} %lay.1.own_ref), channel_id=1, source_target_pairs={{0,128},{64,192},{128,0},{192,64},{1,129},{65,193},{129,1},{193,65... | collective-permute-start | bytes 344072 | tf_op jit(solution)/shard_map/ppermute | solution.py:41
  2.4 7.8 %collective-permute-start.3 = (bf16[64,896]{1,0:T(8,128)(2,1)S(1)}, bf16[64,896]{1,0:T(8,128)(2,1)S(1)}, u32[]{:S(2)}, u32[]{:S(2)}) collective-permute-start(bf16[64,896]{1,0:T(8,128)(2,1)S(1)} %lay.1.own_ref), channel_id=1, source_target_pairs={{0,8},{1,9},{2,10},{3,11},{4,12},{5,13},{6,14},{7,15},{8,0},{9,1},... | collective-permute-start | bytes 344072 | tf_op jit(solution)/shard_map/ppermute | solution.py:37
  4.1 6.2 %collective-permute-start.4 = (bf16[64,896]{1,0:T(8,128)(2,1)S(1)}, bf16[64,896]{1,0:T(8,128)(2,1)S(1)}, u32[]{:S(2)}, u32[]{:S(2)}) collective-permute-start(bf16[64,896]{1,0:T(8,128)(2,1)S(1)} %lay.1.own_ref), channel_id=1, source_target_pairs={{128,8},{129,9},{130,10},{131,11},{132,12},{133,13},{134,14},{135,... | collective-permute-start | bytes 344072 | tf_op jit(solution)/shard_map/ppermute | solution.py:47
  5.1 1.4 %collective-permute-start = (s32[1]{0:T(128)}, s32[1]{0:T(128)}, u32[]{:S(2)}, u32[]{:S(2)}) collective-permute-start(s32[1]{0:T(128)} %param.6), channel_id=1, source_target_pairs={{0,64},{64,0},{128,192},{192,128},{1,65},{65,1},{129,193},{193,129... | collective-permute-start | bytes 20 | tf_op jit(solution)/shard_map/ppermute | solution.py:41
  5.1 5.1 %collective-permute-start.1 = (s32[1]{0:T(128)}, s32[1]{0:T(128)}, u32[]{:S(2)}, u32[]{:S(2)}) collective-permute-start(s32[1]{0:T(128)} %param.6), channel_id=1, source_target_pairs={{0,128},{64,192},{128,0},{192,64},{1,129},{65,193},{129,1},{193,65... | collective-permute-start | bytes 20 | tf_op jit(solution)/shard_map/ppermute | solution.py:41
  10.3 14.3 %copy-start.4 = (bf16[4,64,896]{2,1,0:T(8,128)(2,1)}, bf16[4,64,896]{2,1,0:T(8,128)(2,1)S(1)}, u32[]{:S(2)}) copy-start(bf16[4,64,896]{2,1,0:T(8,128)(2,1)S(1)} %get-tuple-element.35.refs_0_) | copy-start | bytes 1376260
  10.3 14.3 %copy-start.6 = (bf16[2,64,896]{2,1,0:T(8,128)(2,1)}, bf16[2,64,896]{2,1,0:T(8,128)(2,1)S(1)}, u32[]{:S(2)}) copy-start(bf16[2,64,896]{2,1,0:T(8,128)(2,1)S(1)} %get-tuple-element.44.refs_5_) | copy-start | bytes 688132
  10.3 14.4 %collective-permute-start.5 = (bf16[4,64,896]{2,1,0:T(8,128)(2,1)S(1)}, bf16[4,64,896]{2,1,0:T(8,128)(2,1)S(1)}, u32[]{:S(2)}, u32[]{:S(2)}) collective-permute-start(bf16[4,64,896]{2,1,0:T(8,128)(2,1)S(1)} %get-tuple-element.35.refs_0_), channel_id=1, source_target_pairs={{0,16},{1,17},{2,18},{3,19},{4,20},{5,21},{6,22},{7,23},{8,24},{9,... | collective-permute-start | bytes 1376264 | tf_op jit(solution)/shard_map/ppermute | solution.py:37
  12.0 12.7 %collective-permute-start.6 = (bf16[4,64,896]{2,1,0:T(8,128)(2,1)S(1)}, bf16[4,64,896]{2,1,0:T(8,128)(2,1)S(1)}, u32[]{:S(2)}, u32[]{:S(2)}) collective-permute-start(bf16[4,64,896]{2,1,0:T(8,128)(2,1)S(1)} %get-tuple-element.35.refs_0_), channel_id=1, source_target_pairs={{0,48},{1,49},{2,50},{3,51},{4,52},{5,53},{6,54},{7,55},{8,56},{9,... | collective-permute-start | bytes 1376264 | tf_op jit(solution)/shard_map/ppermute | solution.py:37
  13.7 11.0 %collective-permute-start.7 = (bf16[2,64,896]{2,1,0:T(8,128)(2,1)S(1)}, bf16[2,64,896]{2,1,0:T(8,128)(2,1)S(1)}, u32[]{:S(2)}, u32[]{:S(2)}) collective-permute-start(bf16[2,64,896]{2,1,0:T(8,128)(2,1)S(1)} %get-tuple-element.44.refs_5_), channel_id=1, source_target_pairs={{0,1},{1,2},{2,3},{3,4},{4,5},{5,6},{6,7},{7,0},{8,9},{9,10},{10,1... | collective-permute-start | bytes 688136 | tf_op jit(solution)/shard_map/ppermute | solution.py:37
  15.6 9.1 %collective-permute-start.8 = (bf16[2,64,896]{2,1,0:T(8,128)(2,1)S(1)}, bf16[2,64,896]{2,1,0:T(8,128)(2,1)S(1)}, u32[]{:S(2)}, u32[]{:S(2)}) collective-permute-start(bf16[2,64,896]{2,1,0:T(8,128)(2,1)S(1)} %get-tuple-element.44.refs_5_), channel_id=1, source_target_pairs={{0,7},{1,0},{2,1},{3,2},{4,3},{5,4},{6,5},{7,6},{8,15},{9,8},{10,9... | collective-permute-start | bytes 688136 | tf_op jit(solution)/shard_map/ppermute | solution.py:37
  24.7 17.4 %copy-start.7 = (bf16[2,64,896]{2,1,0:T(8,128)(2,1)}, bf16[2,64,896]{2,1,0:T(8,128)(2,1)S(1)}, u32[]{:S(2)}) copy-start(bf16[2,64,896]{2,1,0:T(8,128)(2,1)S(1)} %collective-permute-done.7.refs_6_) | copy-start | bytes 688132
  24.7 17.4 %copy-start.8 = (bf16[2,64,896]{2,1,0:T(8,128)(2,1)}, bf16[2,64,896]{2,1,0:T(8,128)(2,1)S(1)}, u32[]{:S(2)}) copy-start(bf16[2,64,896]{2,1,0:T(8,128)(2,1)S(1)} %collective-permute-done.8.refs_7_) | copy-start | bytes 688132
  24.7 17.4 %copy-start = (bf16[4,64,896]{2,1,0:T(8,128)(2,1)}, bf16[4,64,896]{2,1,0:T(8,128)(2,1)S(1)}, u32[]{:S(2)}) copy-start(bf16[4,64,896]{2,1,0:T(8,128)(2,1)S(1)} %collective-permute-done.5.refs_1_) | copy-start | bytes 1376260
  24.8 17.4 %copy-start.2 = (bf16[4,64,896]{2,1,0:T(8,128)(2,1)}, bf16[4,64,896]{2,1,0:T(8,128)(2,1)S(1)}, u32[]{:S(2)}) copy-start(bf16[4,64,896]{2,1,0:T(8,128)(2,1)S(1)} %collective-permute-done.6.refs_4_) | copy-start | bytes 1376260
  24.8 30.5 %all-to-all-start = ((bf16[8,3,64,512]{3,2,1,0:T(8,128)(2,1)}), bf16[8,3,64,512]{3,2,1,0:T(8,128)(2,1)S(1)}, u32[]{:S(2)}, u32[]{:S(2)}) async-start(bf16[8,3,64,512]{3,2,1,0:T(8,128)(2,1)} %pack.1), calls=%async_computation | async-start | bytes 3145728 | tf_op jit(solution)/shard_map/all_to_all | solution.py:343
  29.5 9.8 %collective-permute-start.11 = (bf16[2,64,896]{2,1,0:T(8,128)(2,1)S(1)}, bf16[2,64,896]{2,1,0:T(8,128)(2,1)S(1)}, u32[]{:S(2)}, u32[]{:S(2)}) collective-permute-start(bf16[2,64,896]{2,1,0:T(8,128)(2,1)S(1)} %collective-permute-done.7.refs_6_), channel_id=1, source_target_pairs={{0,1},{1,2},{2,3},{3,4},{4,5},{5,6},{6,7},{7,0},{8,9},{9,10},{10,1... | collective-permute-start | bytes 688136 | tf_op jit(solution)/shard_map/ppermute | solution.py:37
  31.3 10.9 %collective-permute-start.12 = (bf16[2,64,896]{2,1,0:T(8,128)(2,1)S(1)}, bf16[2,64,896]{2,1,0:T(8,128)(2,1)S(1)}, u32[]{:S(2)}, u32[]{:S(2)}) collective-permute-start(bf16[2,64,896]{2,1,0:T(8,128)(2,1)S(1)} %collective-permute-done.8.refs_7_), channel_id=1, source_target_pairs={{0,7},{1,0},{2,1},{3,2},{4,3},{5,4},{6,5},{7,6},{8,15},{9,8},{10,9... | collective-permute-start | bytes 688136 | tf_op jit(solution)/shard_map/ppermute | solution.py:37
  39.3 16.0 %copy-start.9 = (bf16[2,64,896]{2,1,0:T(8,128)(2,1)}, bf16[2,64,896]{2,1,0:T(8,128)(2,1)S(1)}, u32[]{:S(2)}) copy-start(bf16[2,64,896]{2,1,0:T(8,128)(2,1)S(1)} %collective-permute-done.11.refs_8_) | copy-start | bytes 688132
  39.3 7.2 %collective-permute-start.13 = (bf16[2,64,896]{2,1,0:T(8,128)(2,1)S(1)}, bf16[2,64,896]{2,1,0:T(8,128)(2,1)S(1)}, u32[]{:S(2)}, u32[]{:S(2)}) collective-permute-start(bf16[2,64,896]{2,1,0:T(8,128)(2,1)S(1)} %collective-permute-done.11.refs_8_), channel_id=1, source_target_pairs={{0,1},{1,2},{2,3},{3,4},{4,5},{5,6},{6,7},{7,0},{8,9},{9,10},{10,1... | collective-permute-start | bytes 688136 | tf_op jit(solution)/shard_map/ppermute | solution.py:37
  39.3 12.6 %collective-permute-start.10 = (bf16[2,64,896]{2,1,0:T(8,128)(2,1)S(1)}, bf16[2,64,896]{2,1,0:T(8,128)(2,1)S(1)}, u32[]{:S(2)}, u32[]{:S(2)}) collective-permute-start(bf16[2,64,896]{2,1,0:T(8,128)(2,1)S(1)} %slice.19), channel_id=1, source_target_pairs={{0,48},{1,49},{2,50},{3,51},{4,52},{5,53},{6,54},{7,55},{8,56},{9,... | collective-permute-start | bytes 688136 | tf_op jit(solution)/shard_map/ppermute | solution.py:37
  42.1 11.1 %collective-permute-start.9 = (bf16[2,64,896]{2,1,0:T(8,128)(2,1)S(1)}, bf16[2,64,896]{2,1,0:T(8,128)(2,1)S(1)}, u32[]{:S(2)}, u32[]{:S(2)}) collective-permute-start(bf16[2,64,896]{2,1,0:T(8,128)(2,1)S(1)} %slice.18), channel_id=1, source_target_pairs={{0,16},{1,17},{2,18},{3,19},{4,20},{5,21},{6,22},{7,23},{8,24},{9,... | collective-permute-start | bytes 688136 | tf_op jit(solution)/shard_map/ppermute | solution.py:37
  42.2 11.0 %copy-start.10 = (bf16[2,64,896]{2,1,0:T(8,128)(2,1)}, bf16[2,64,896]{2,1,0:T(8,128)(2,1)S(1)}, u32[]{:S(2)}) copy-start(bf16[2,64,896]{2,1,0:T(8,128)(2,1)S(1)} %collective-permute-done.12.refs_9_) | copy-start | bytes 688132
  42.2 11.0 %collective-permute-start.14 = (bf16[2,64,896]{2,1,0:T(8,128)(2,1)S(1)}, bf16[2,64,896]{2,1,0:T(8,128)(2,1)S(1)}, u32[]{:S(2)}, u32[]{:S(2)}) collective-permute-start(bf16[2,64,896]{2,1,0:T(8,128)(2,1)S(1)} %collective-permute-done.12.refs_9_), channel_id=1, source_target_pairs={{0,7},{1,0},{2,1},{3,2},{4,3},{5,4},{6,5},{7,6},{8,15},{9,8},{10,9... | collective-permute-start | bytes 688136 | tf_op jit(solution)/shard_map/ppermute | solution.py:37
  46.5 6.7 %copy-start.11 = (bf16[2,64,896]{2,1,0:T(8,128)(2,1)}, bf16[2,64,896]{2,1,0:T(8,128)(2,1)S(1)}, u32[]{:S(2)}) copy-start(bf16[2,64,896]{2,1,0:T(8,128)(2,1)S(1)} %collective-permute-done.13.refs_10_) | copy-start | bytes 688132
  46.5 7.4 %collective-permute-start.15 = (bf16[2,64,896]{2,1,0:T(8,128)(2,1)S(1)}, bf16[2,64,896]{2,1,0:T(8,128)(2,1)S(1)}, u32[]{:S(2)}, u32[]{:S(2)}) collective-permute-start(bf16[2,64,896]{2,1,0:T(8,128)(2,1)S(1)} %collective-permute-done.13.refs_10_), channel_id=1, source_target_pairs={{0,1},{1,2},{2,3},{3,4},{4,5},{5,6},{6,7},{7,0},{8,9},{9,10},{10,1... | collective-permute-start | bytes 688136 | tf_op jit(solution)/shard_map/ppermute | solution.py:37
  51.9 1.3 %copy-start.12 = (bf16[2,64,896]{2,1,0:T(8,128)(2,1)}, bf16[2,64,896]{2,1,0:T(8,128)(2,1)S(1)}, u32[]{:S(2)}) copy-start(bf16[2,64,896]{2,1,0:T(8,128)(2,1)S(1)} %collective-permute-done.10.refs_3_) | copy-start | bytes 688132
  55.3 7.3 %collective-permute-start.16 = (bf16[8,3,64,512]{3,2,1,0:T(8,128)(2,1)S(1)}, bf16[8,3,64,512]{3,2,1,0:T(8,128)(2,1)S(1)}, u32[]{:S(2)}, u32[]{:S(2)}) collective-permute-start(bf16[8,3,64,512]{3,2,1,0:T(8,128)(2,1)S(1)} %all-to-all-done.kern_ref), channel_id=1, source_target_pairs={{0,64},{64,0},{128,192},{192,128},{1,65},{65,1},{129,193},{193,129... | collective-permute-start | bytes 4718600 | tf_op jit(solution)/shard_map/ppermute | solution.py:41
  55.3 1.0 copy-start.1
  56.3 1.0 copy-start.3
  63.5 2.9 %collective-permute-start.17 = (bf16[512,1024]{1,0:T(8,128)(2,1)S(1)}, bf16[512,1024]{1,0:T(8,128)(2,1)S(1)}, u32[]{:S(2)}, u32[]{:S(2)}) collective-permute-start(bf16[512,1024]{1,0:T(8,128)(2,1)S(1)} %mix.1), channel_id=1, source_target_pairs={{0,64},{64,0},{128,192},{192,128},{1,65},{65,1},{129,193},{193,129... | collective-permute-start | bytes 3145736 | tf_op jit(solution)/shard_map/ppermute | solution.py:41
  90.1 16.5 %all-to-all-start.2 = ((f32[4,8,896]{2,1,0:T(8,128)}), f32[4,8,896]{2,1,0:T(8,128)S(1)}, u32[]{:S(2)}, u32[]{:S(2)}) async-start(f32[4,8,896]{2,1,0:T(8,128)} %convert_reduce_fusion), calls=%async_computation.2 | async-start | bytes 229376 | tf_op jit(solution)/shard_map/all_to_all | solution.py:314
  (4 other events, 3.1 us)

commit v24 on v20

--- a/solution.py
+++ b/solution.py
@@ -14,6 +14,7 @@
 REST = NB - WHOLE
 TAIL = 2 * WHOLE
 LANES = TAIL + 128
+Z_ORDER = (0, -1, 1, -2, 2, -3, 3, -4)
 VMEM = 24 * 1024 * 1024
 
 IN_VMEM = pl.BlockSpec(memory_space=pltpu.VMEM)
@@ -117,17 +118,21 @@
     )(odd, own, core, far, stored, away(kernels))
 
 
-def density_body(place_ref, slot_ref, *refs):
+def density_body(band_ref, *refs):
     four_ref, up_ref, over_here, over_side, down_ref = refs[:5]
     cols = refs[5 : 5 + NZ]
     own_ref, far_ref, row_ref, col_ref, other_rows, other_cols, sem = refs[5 + NZ :]
 
+    band = band_ref[0]
+    y, x, z = band // (NX * NZ), band // NZ % NX, band % NZ
+
     def row_at(dy, side):
-        return pl.ds(pl.multiple_of(place_ref[dy * NX + side] * SLAB, SLAB), SLAB)
+        place = (y + NY - dy) % NY * NX + (x + side) % NX
+        return pl.ds(pl.multiple_of(place * SLAB, SLAB), SLAB)
 
     moves = []
-    for i, piece in enumerate(cols):
-        at = pl.ds(pl.multiple_of(slot_ref[i] * SLAB, SLAB), SLAB)
+    for piece, dz in zip(cols, Z_ORDER):
+        at = pl.ds(pl.multiple_of((z + NZ + dz) % NZ * SLAB, SLAB), SLAB)
         moves.append((piece.at[0], col_ref.at[at, :]))
         moves.append((piece.at[1], other_cols.at[at, :]))
     for side, piece in enumerate((over_here, over_side)):
@@ -148,7 +153,7 @@
         out[:, BLOCK:] = dot(turned(a), b, 1, 1)
 
 
-def density(place, slots, four, up, over, down, cols):
+def density(band, four, up, over, down, cols):
     product = pltpu.VMEM((BLOCK, 2 * BLOCK), jnp.float32)
     points = pltpu.VMEM((BLOCK, LANES), jnp.bfloat16)
     in_hbm = pl.BlockSpec(memory_space=pltpu.HBM)
@@ -157,13 +162,13 @@
     return pl.pallas_call(
         density_body,
         out_shape=[product, product, points, points],
-        in_specs=[IN_SMEM] * 2 + specs,
+        in_specs=[IN_SMEM] + specs,
         out_specs=[IN_VMEM] * 4,
         scratch_shapes=[pltpu.VMEM((BLOCK, LANES), jnp.bfloat16)] * 2
         + [pltpu.SemaphoreType.DMA((2 * NX + 2 * NZ,))],
         compiler_params=PARAMS,
         name="density",
-    )(place, slots, *arrays)
+    )(band, *arrays)
 
 
 def mix_body(odd_ref, own_ref, far_ref, half_ref, kern_ref, m_ref):
@@ -303,7 +308,6 @@
 def on_device(orbitals, kernels, pair_kdiff, stored_kernel_index):
     group = lax.axis_index("kgrp")
     band = lax.axis_index("band")
-    y, x, z = band // (NX * NZ), band // NZ % NX, band % NZ
     odd = (group % 2).reshape(1)
 
     own = lay(orbitals)
@@ -330,12 +334,11 @@
         ahead, behind = shift(ahead, 0, 0, 1), shift(behind, 0, 0, -1)
         cols += [ahead, behind]
     cols.append(shift(ahead, 0, 0, 1))
-    kern, over, cols = lax.optimization_barrier((kern, over, cols))
+    late = sum(block[0, 0, :1] for block in (*over, cols[-1]))
+    kern = lax.optimization_barrier((kern, late))[0]
     half = swap_groups(kern[:, 0], 1)
 
-    place = jnp.stack([(y - dy) % NY * NX + (x - dx) % NX for dy in range(NY) for dx in range(NX)])
-    slots = jnp.stack([(z + i) % NZ for i in (0, -1, 1, -2, 2, -3, 3, -4)])
-    p_own, p_far, rows, cols = density(place, slots, four, up, over, down, cols)
+    p_own, p_far, rows, cols = density(band.reshape(1), four, up, over, down, cols)
     m_own = swap_groups(mix(odd, p_own, p_far, half, kern), 1)
     left, right = prepare(rows, cols)
     total = reduce_windows(project(m_own, left, right))

time: 105 us -> 117 us (1.11)
  waiting for transfers between devices: 26.9 us -> 44.1 us
  starting transfers between devices: 38.4 us -> 33.3 us
    all_to_all x1, waiting for transfers between devices: 0.01 us -> 18.5 us  [on_device(): kern = lax.all_to_all(sends, 'band', 0, 0, axis_index_groups=over_yx)]
    all_to_all x1, starting transfers between devices: 7.42 us -> 3.31 us  [reduce_windows(): lax.all_to_all(parts, 'band', 0, 0, axis_index_groups=deep)]
    ppermute x12, waiting for transfers between devices: 12.4 us -> 10.9 us  [shift(): return lax.ppermute(block, 'band', band_route(dy, dx, dz))]
    slice x2, local copies, waits for them, and re-layouts: 0.04 us -> 1.43 us  [on_device(): over = (shift(up[:2], 1, 0, 0), shift(down[2:], -1, 0, 0))]
  transfers between devices with their start and end apart: 20 -> 20, of which waited for: 7 -> 8; matrix products, arithmetic and copies ran while one was open for 0% -> 2% of each run, Pallas kernels for 9% -> 8%
where the time goes in v24:
time: 117 us; the launch traced here: 116 us
  waiting for transfers between devices  44.1 us (38%)
  starting transfers between devices  33.3 us (28%)
  blocking collectives  17.5 us (15%)
  Pallas kernels  15.2 us (13%)
  local copies, waits for them, and re-layouts  3.87 us (3%)
  other arithmetic  1.51 us (1%)
    ppermute x12, starting transfers between devices, shift(): return lax.ppermute(block, 'band', band_route(dy, dx, dz))  21.3 us
    all_to_all x1, waiting for transfers between devices, on_device(): kern = lax.all_to_all(sends, 'band', 0, 0, axis_index_groups=over_yx)  18.5 us
    all_to_all x1, blocking collectives, reduce_windows(): parts = lax.all_to_all(parts, 'band', 0, 0, axis_index_groups=wide)  17.5 us
    ppermute x12, waiting for transfers between devices, shift(): return lax.ppermute(block, 'band', band_route(dy, dx, dz))  10.9 us
    all_to_all x1, waiting for transfers between devices, reduce_windows(): lax.all_to_all(parts, 'band', 0, 0, axis_index_groups=deep)  8.85 us
    ppermute x5, waiting for transfers between devices, swap_groups(): return lax.ppermute(block, 'kgrp', [(k, k ^ bit) for k in range(4)])  5.8 us
    all_to_all x1, starting transfers between devices, on_device(): kern = lax.all_to_all(sends, 'band', 0, 0, axis_index_groups=over_yx)  4.72 us
    pallas_call x1, Pallas kernels, pack(): pl.pallas_call(pack_body, out_shape=jax.ShapeDtypeStruct((GROUPS, 3, SLAB...  4.52 us
  transfers between devices with their start and end apart: 20, of which 8 were waited for; matrix products, arithmetic and copies ran while one was open for 2% of the time, Pallas kernels for 8%

profile of v24, /device:TPU:6, one launch (start us, length us, event | category | flops | bytes accessed | tf_op | source)
XLA Modules:
  0.0 116.3 jit_solution(908704294860560585)
XLA Ops:
  0.0 1.0 lay.1.own_ref
  1.0 1.4 %collective-permute-start.2 = (bf16[64,896]{1,0:T(8,128)(2,1)S(1)}, bf16[64,896]{1,0:T(8,128)(2,1)S(1)}, u32[]{:S(2)}, u32[]{:S(2)}) collective-permute-start(bf16[64,896]{1,0:T(8,128)(2,1)S(1)} %lay.1.own_ref), channel_id=1, source_target_pairs={{0,128},{64,192},{128,0},{192,64},{1,129},{65,193},{129,1},{193,65... | collective-permute-start | bytes 344072 | tf_op jit(solution)/shard_map/ppermute | solution.py:41
  2.4 1.7 %collective-permute-start.3 = (bf16[64,896]{1,0:T(8,128)(2,1)S(1)}, bf16[64,896]{1,0:T(8,128)(2,1)S(1)}, u32[]{:S(2)}, u32[]{:S(2)}) collective-permute-start(bf16[64,896]{1,0:T(8,128)(2,1)S(1)} %lay.1.own_ref), channel_id=1, source_target_pairs={{0,8},{1,9},{2,10},{3,11},{4,12},{5,13},{6,14},{7,15},{8,0},{9,1},... | collective-permute-start | bytes 344072 | tf_op jit(solution)/shard_map/ppermute | solution.py:37
  4.1 1.0 collective-permute-start.4
  5.1 1.4 %collective-permute-start.1 = (s32[1]{0:T(128)}, s32[1]{0:T(128)}, u32[]{:S(2)}, u32[]{:S(2)}) collective-permute-start(s32[1]{0:T(128)} %param.6), channel_id=1, source_target_pairs={{0,128},{64,192},{128,0},{192,64},{1,129},{65,193},{129,1},{193,65... | collective-permute-start | bytes 20 | tf_op jit(solution)/shard_map/ppermute | solution.py:41
  6.5 3.7 %collective-permute-done.1.far_ref = s32[1]{0:T(128)} collective-permute-done((s32[1]{0:T(128)}, s32[1]{0:T(128)}, u32[]{:S(2)}, u32[]{:S(2)}) %collective-permute-start.1) | collective-permute-done | bytes 36 | tf_op jit(solution)/shard_map/ppermute | solution.py:41
  10.3 1.7 %collective-permute-start.5 = (bf16[4,64,896]{2,1,0:T(8,128)(2,1)S(1)}, bf16[4,64,896]{2,1,0:T(8,128)(2,1)S(1)}, u32[]{:S(2)}, u32[]{:S(2)}) collective-permute-start(bf16[4,64,896]{2,1,0:T(8,128)(2,1)S(1)} %get-tuple-element.24.refs_0_), channel_id=1, source_target_pairs={{0,16},{1,17},{2,18},{3,19},{4,20},{5,21},{6,22},{7,23},{8,24},{9,... | collective-permute-start | bytes 1376264 | tf_op jit(solution)/shard_map/ppermute | solution.py:37
  12.0 1.7 %collective-permute-start.6 = (bf16[4,64,896]{2,1,0:T(8,128)(2,1)S(1)}, bf16[4,64,896]{2,1,0:T(8,128)(2,1)S(1)}, u32[]{:S(2)}, u32[]{:S(2)}) collective-permute-start(bf16[4,64,896]{2,1,0:T(8,128)(2,1)S(1)} %get-tuple-element.24.refs_0_), channel_id=1, source_target_pairs={{0,48},{1,49},{2,50},{3,51},{4,52},{5,53},{6,54},{7,55},{8,56},{9,... | collective-permute-start | bytes 1376264 | tf_op jit(solution)/shard_map/ppermute | solution.py:37
  13.7 1.9 %collective-permute-start.7 = (bf16[2,64,896]{2,1,0:T(8,128)(2,1)S(1)}, bf16[2,64,896]{2,1,0:T(8,128)(2,1)}, u32[]{:S(2)}, u32[]{:S(2)}) collective-permute-start(bf16[2,64,896]{2,1,0:T(8,128)(2,1)S(1)} %get-tuple-element.25.refs_5_), channel_id=1, source_target_pairs={{0,1},{1,2},{2,3},{3,4},{4,5},{5,6},{6,7},{7,0},{8,9},{9,10},{10,1... | collective-permute-start | bytes 688136 | tf_op jit(solution)/shard_map/ppermute | solution.py:37
  15.6 3.9 %collective-permute-start.8 = (bf16[2,64,896]{2,1,0:T(8,128)(2,1)S(1)}, bf16[2,64,896]{2,1,0:T(8,128)(2,1)S(1)}, u32[]{:S(2)}, u32[]{:S(2)}) collective-permute-start(bf16[2,64,896]{2,1,0:T(8,128)(2,1)S(1)} %get-tuple-element.25.refs_5_), channel_id=1, source_target_pairs={{0,7},{1,0},{2,1},{3,2},{4,3},{5,4},{6,5},{7,6},{8,15},{9,8},{10,9... | collective-permute-start | bytes 688136 | tf_op jit(solution)/shard_map/ppermute | solution.py:37
  20.8 4.5 %pack.1 = bf16[8,3,64,512]{3,2,1,0:T(8,128)(2,1)} custom-call(s32[1]{0:T(128)} %bitcast.odd_ref, s32[1]{0:T(128)S(6)} %copy.5.own_ref, s32[1]{0:T(128)} %collective-permute-done.core_ref, s32[1]{0:T(128)} %collective-permute-done.1.far_ref, s32[8]{0:T(128)S(1)} %copy-done.1, bf16[4,2,64,4096]{3,2,1,0:T(8,128)(2,1)} %kernels_ref.1), custom_call_target="tpu_custom_call" | custom-call | tf_op jit(solution)/shard_map/pack/pallas_call | solution.py:110
  26.1 4.7 %all-to-all-start = ((bf16[8,3,64,512]{3,2,1,0:T(8,128)(2,1)}), bf16[8,3,64,512]{3,2,1,0:T(8,128)(2,1)S(1)}, u32[]{:S(2)}, u32[]{:S(2)}) async-start(bf16[8,3,64,512]{3,2,1,0:T(8,128)(2,1)} %pack.1), calls=%async_computation | async-start | bytes 3145728 | tf_op jit(solution)/shard_map/all_to_all | solution.py:331
  31.3 18.5 %all-to-all-done.kern_ref = bf16[8,3,64,512]{3,2,1,0:T(8,128)(2,1)S(1)} async-done(((bf16[8,3,64,512]{3,2,1,0:T(8,128)(2,1)}), bf16[8,3,64,512]{3,2,1,0:T(8,128)(2,1)S(1)}, u32[]{:S(2)}, u32[]{:S(2)}) %all-to-all-start) | async-done | bytes 1572896 | tf_op jit(solution)/shard_map/all_to_all | solution.py:331
  49.8 0.9 slice_bitcast_fusion
  50.7 4.2 %collective-permute-start.12 = (bf16[2,64,896]{2,1,0:T(8,128)(2,1)}, bf16[2,64,896]{2,1,0:T(8,128)(2,1)}, u32[]{:S(2)}, u32[]{:S(2)}) collective-permute-start(bf16[2,64,896]{2,1,0:T(8,128)(2,1)} %copy-done.2), channel_id=1, source_target_pairs={{0,7},{1,0},{2,1},{3,2},{4,3},{5,4},{6,5},{7,6},{8,15},{9,8},{10,9... | collective-permute-start | bytes 688136 | tf_op jit(solution)/shard_map/ppermute | solution.py:37
  55.6 1.2 %collective-permute-start.10 = (bf16[2,64,896]{2,1,0:T(8,128)(2,1)}, bf16[2,64,896]{2,1,0:T(8,128)(2,1)}, u32[]{:S(2)}, u32[]{:S(2)}) collective-permute-start(bf16[2,64,896]{2,1,0:T(8,128)(2,1)} %slice.25), channel_id=1, source_target_pairs={{0,48},{1,49},{2,50},{3,51},{4,52},{5,53},{6,54},{7,55},{8,56},{9,... | collective-permute-start | bytes 688136 | tf_op jit(solution)/shard_map/ppermute | solution.py:37
  56.8 0.7 slice.24
  57.5 0.9 collective-permute-start.9
  58.4 2.4 %collective-permute-done.12.refs_9_ = bf16[2,64,896]{2,1,0:T(8,128)(2,1)} collective-permute-done((bf16[2,64,896]{2,1,0:T(8,128)(2,1)}, bf16[2,64,896]{2,1,0:T(8,128)(2,1)}, u32[]{:S(2)}, u32[]{:S(2)}) %collective-permute-start.12) | collective-permute-done | bytes 229408 | tf_op jit(solution)/shard_map/ppermute | solution.py:37
  60.8 3.7 %collective-permute-start.14 = (bf16[2,64,896]{2,1,0:T(8,128)(2,1)}, bf16[2,64,896]{2,1,0:T(8,128)(2,1)}, u32[]{:S(2)}, u32[]{:S(2)}) collective-permute-start(bf16[2,64,896]{2,1,0:T(8,128)(2,1)} %collective-permute-done.12.refs_9_), channel_id=1, source_target_pairs={{0,7},{1,0},{2,1},{3,2},{4,3},{5,4},{6,5},{7,6},{8,15},{9,8},{10,9... | collective-permute-start | bytes 688136 | tf_op jit(solution)/shard_map/ppermute | solution.py:37
  64.5 2.0 %collective-permute-done.9.refs_2_ = bf16[2,64,896]{2,1,0:T(8,128)(2,1)} collective-permute-done((bf16[2,64,896]{2,1,0:T(8,128)(2,1)}, bf16[2,64,896]{2,1,0:T(8,128)(2,1)}, u32[]{:S(2)}, u32[]{:S(2)}) %collective-permute-start.9) | collective-permute-done | bytes 229408 | tf_op jit(solution)/shard_map/ppermute | solution.py:37
  66.5 3.0 %collective-permute-done.14.refs_11_ = bf16[2,64,896]{2,1,0:T(8,128)(2,1)} collective-permute-done((bf16[2,64,896]{2,1,0:T(8,128)(2,1)}, bf16[2,64,896]{2,1,0:T(8,128)(2,1)}, u32[]{:S(2)}, u32[]{:S(2)}) %collective-permute-start.14) | collective-permute-done | bytes 229408 | tf_op jit(solution)/shard_map/ppermute | solution.py:37
  69.5 3.4 %collective-permute-done.15.refs_12_ = bf16[2,64,896]{2,1,0:T(8,128)(2,1)} collective-permute-done((bf16[2,64,896]{2,1,0:T(8,128)(2,1)}, bf16[2,64,896]{2,1,0:T(8,128)(2,1)}, u32[]{:S(2)}, u32[]{:S(2)}) %collective-permute-start.15) | collective-permute-done | bytes 229408 | tf_op jit(solution)/shard_map/ppermute | solution.py:37
  72.9 4.2 %density.1 = (f32[512,1024]{1,0:T(8,128)S(1)}, f32[512,1024]{1,0:T(8,128)S(1)}, bf16[512,896]{1,0:T(8,128)(2,1)S(1)}, bf16[512,896]{1,0:T(8,128)(2,1)S(1)}) custom-call(s32[1]{0:T(128)} %bitcast.1.band_ref, bf16[4,64,896]{2,1,0:T(8,128)(2,1)S(1)} %get-tuple-element.24.refs_0_, bf16[4,64,896]{2,1,0:T(8,128)(2,1)S(1)} %collective-permute-done.5.refs_1_, ...), custom_call_target="tpu_custom_call" | custom-call | tf_op jit(solution)/shard_map/density/pallas_call | solution.py:162
  77.2 0.8 mix.1
  78.7 2.1 %collective-permute-done.17.m_ref = bf16[512,1024]{1,0:T(8,128)(2,1)S(1)} collective-permute-done((bf16[512,1024]{1,0:T(8,128)(2,1)S(1)}, bf16[512,1024]{1,0:T(8,128)(2,1)S(1)}, u32[]{:S(2)}, u32[]{:S(2)}) %collective-permute-start.17) | collective-permute-done | bytes 1048608 | tf_op jit(solution)/shard_map/ppermute | solution.py:41
  80.8 4.0 %project.1 = bf16[64,8,896]{2,1,0:T(8,128)(2,1)S(1)} custom-call(bf16[512,1024]{1,0:T(8,128)(2,1)S(1)} %collective-permute-done.17.m_ref, bf16[432,1024]{1,0:T(8,128)(2,1)S(1)} %get-tuple-element.35.left_ref, bf16[1024,896]{1,0:T(8,128)(2,1)S(1)} %get-tuple-element.36.right_ref), custom_call_target="tpu_custom_call" | custom-call | tf_op jit(solution)/shard_map/project/pallas_call | solution.py:259
  84.8 17.5 %all_to_all.15 = bf16[16,4,8,896]{3,2,1,0:T(8,128)(2,1)S(1)} all-to-all(bf16[16,4,8,896]{3,2,1,0:T(8,128)(2,1)S(1)} %bitcast.7), channel_id=1, replica_groups={{0,1,8,9,16,17,24,25,32,33,40,41,48,49,56,57},{2,3,10,11,18,19,26,27,34..., dimensions={0} | all-to-all | bytes 1835008 | tf_op jit(solution)/shard_map/all_to_all | solution.py:300
  102.3 0.8 convert_reduce_fusion
  103.0 3.3 %all-to-all-start.2 = ((f32[4,8,896]{2,1,0:T(8,128)}), f32[4,8,896]{2,1,0:T(8,128)S(1)}, u32[]{:S(2)}, u32[]{:S(2)}) async-start(f32[4,8,896]{2,1,0:T(8,128)} %convert_reduce_fusion), calls=%async_computation.2 | async-start | bytes 229376 | tf_op jit(solution)/shard_map/all_to_all | solution.py:302
  106.4 8.9 %all-to-all-done.2 = f32[4,8,896]{2,1,0:T(8,128)S(1)} async-done(((f32[4,8,896]{2,1,0:T(8,128)}), f32[4,8,896]{2,1,0:T(8,128)S(1)}, u32[]{:S(2)}, u32[]{:S(2)}) %all-to-all-start.2) | async-done | bytes 114720 | tf_op jit(solution)/shard_map/all_to_all | solution.py:302
  115.5 0.7 fusion.1
  (33 shorter events, 3.6 us)
Async XLA Ops:
  1.0 9.3 %collective-permute-start.2 = (bf16[64,896]{1,0:T(8,128)(2,1)S(1)}, bf16[64,896]{1,0:T(8,128)(2,1)S(1)}, u32[]{:S(2)}, u32[]{:S(2)}) collective-permute-start(bf16[64,896]{1,0:T(8,128)(2,1)S(1)} %lay.1.own_ref), channel_id=1, source_target_pairs={{0,128},{64,192},{128,0},{192,64},{1,129},{65,193},{129,1},{193,65... | collective-permute-start | bytes 344072 | tf_op jit(solution)/shard_map/ppermute | solution.py:41
  2.4 7.8 %collective-permute-start.3 = (bf16[64,896]{1,0:T(8,128)(2,1)S(1)}, bf16[64,896]{1,0:T(8,128)(2,1)S(1)}, u32[]{:S(2)}, u32[]{:S(2)}) collective-permute-start(bf16[64,896]{1,0:T(8,128)(2,1)S(1)} %lay.1.own_ref), channel_id=1, source_target_pairs={{0,8},{1,9},{2,10},{3,11},{4,12},{5,13},{6,14},{7,15},{8,0},{9,1},... | collective-permute-start | bytes 344072 | tf_op jit(solution)/shard_map/ppermute | solution.py:37
  4.1 6.2 %collective-permute-start.4 = (bf16[64,896]{1,0:T(8,128)(2,1)S(1)}, bf16[64,896]{1,0:T(8,128)(2,1)S(1)}, u32[]{:S(2)}, u32[]{:S(2)}) collective-permute-start(bf16[64,896]{1,0:T(8,128)(2,1)S(1)} %lay.1.own_ref), channel_id=1, source_target_pairs={{128,8},{129,9},{130,10},{131,11},{132,12},{133,13},{134,14},{135,... | collective-permute-start | bytes 344072 | tf_op jit(solution)/shard_map/ppermute | solution.py:47
  5.1 1.4 %collective-permute-start = (s32[1]{0:T(128)}, s32[1]{0:T(128)}, u32[]{:S(2)}, u32[]{:S(2)}) collective-permute-start(s32[1]{0:T(128)} %param.6), channel_id=1, source_target_pairs={{0,64},{64,0},{128,192},{192,128},{1,65},{65,1},{129,193},{193,129... | collective-permute-start | bytes 20 | tf_op jit(solution)/shard_map/ppermute | solution.py:41
  5.1 5.1 %collective-permute-start.1 = (s32[1]{0:T(128)}, s32[1]{0:T(128)}, u32[]{:S(2)}, u32[]{:S(2)}) collective-permute-start(s32[1]{0:T(128)} %param.6), channel_id=1, source_target_pairs={{0,128},{64,192},{128,0},{192,64},{1,129},{65,193},{129,1},{193,65... | collective-permute-start | bytes 20 | tf_op jit(solution)/shard_map/ppermute | solution.py:41
  10.3 15.0 %copy-start = (bf16[2,64,896]{2,1,0:T(8,128)(2,1)}, bf16[2,64,896]{2,1,0:T(8,128)(2,1)S(1)}, u32[]{:S(2)}) copy-start(bf16[2,64,896]{2,1,0:T(8,128)(2,1)S(1)} %get-tuple-element.25.refs_5_) | copy-start | bytes 688132
  10.3 15.1 %collective-permute-start.5 = (bf16[4,64,896]{2,1,0:T(8,128)(2,1)S(1)}, bf16[4,64,896]{2,1,0:T(8,128)(2,1)S(1)}, u32[]{:S(2)}, u32[]{:S(2)}) collective-permute-start(bf16[4,64,896]{2,1,0:T(8,128)(2,1)S(1)} %get-tuple-element.24.refs_0_), channel_id=1, source_target_pairs={{0,16},{1,17},{2,18},{3,19},{4,20},{5,21},{6,22},{7,23},{8,24},{9,... | collective-permute-start | bytes 1376264 | tf_op jit(solution)/shard_map/ppermute | solution.py:37
  12.0 13.4 %collective-permute-start.6 = (bf16[4,64,896]{2,1,0:T(8,128)(2,1)S(1)}, bf16[4,64,896]{2,1,0:T(8,128)(2,1)S(1)}, u32[]{:S(2)}, u32[]{:S(2)}) collective-permute-start(bf16[4,64,896]{2,1,0:T(8,128)(2,1)S(1)} %get-tuple-element.24.refs_0_), channel_id=1, source_target_pairs={{0,48},{1,49},{2,50},{3,51},{4,52},{5,53},{6,54},{7,55},{8,56},{9,... | collective-permute-start | bytes 1376264 | tf_op jit(solution)/shard_map/ppermute | solution.py:37
  13.7 11.7 %collective-permute-start.7 = (bf16[2,64,896]{2,1,0:T(8,128)(2,1)S(1)}, bf16[2,64,896]{2,1,0:T(8,128)(2,1)}, u32[]{:S(2)}, u32[]{:S(2)}) collective-permute-start(bf16[2,64,896]{2,1,0:T(8,128)(2,1)S(1)} %get-tuple-element.25.refs_5_), channel_id=1, source_target_pairs={{0,1},{1,2},{2,3},{3,4},{4,5},{5,6},{6,7},{7,0},{8,9},{9,10},{10,1... | collective-permute-start | bytes 688136 | tf_op jit(solution)/shard_map/ppermute | solution.py:37
  15.6 9.8 %collective-permute-start.8 = (bf16[2,64,896]{2,1,0:T(8,128)(2,1)S(1)}, bf16[2,64,896]{2,1,0:T(8,128)(2,1)S(1)}, u32[]{:S(2)}, u32[]{:S(2)}) collective-permute-start(bf16[2,64,896]{2,1,0:T(8,128)(2,1)S(1)} %get-tuple-element.25.refs_5_), channel_id=1, source_target_pairs={{0,7},{1,0},{2,1},{3,2},{4,3},{5,4},{6,5},{7,6},{8,15},{9,8},{10,9... | collective-permute-start | bytes 688136 | tf_op jit(solution)/shard_map/ppermute | solution.py:37
  20.2 0.7 copy-start.1
  25.4 0.7 copy-start.2
  26.1 23.8 %all-to-all-start = ((bf16[8,3,64,512]{3,2,1,0:T(8,128)(2,1)}), bf16[8,3,64,512]{3,2,1,0:T(8,128)(2,1)S(1)}, u32[]{:S(2)}, u32[]{:S(2)}) async-start(bf16[8,3,64,512]{3,2,1,0:T(8,128)(2,1)} %pack.1), calls=%async_computation | async-start | bytes 3145728 | tf_op jit(solution)/shard_map/all_to_all | solution.py:331
  30.8 24.1 %collective-permute-start.11 = (bf16[2,64,896]{2,1,0:T(8,128)(2,1)}, bf16[2,64,896]{2,1,0:T(8,128)(2,1)}, u32[]{:S(2)}, u32[]{:S(2)}) collective-permute-start(bf16[2,64,896]{2,1,0:T(8,128)(2,1)} %collective-permute-done.7.refs_6_), channel_id=1, source_target_pairs={{0,1},{1,2},{2,3},{3,4},{4,5},{5,6},{6,7},{7,0},{8,9},{9,10},{10,1... | collective-permute-start | bytes 688136 | tf_op jit(solution)/shard_map/ppermute | solution.py:37
  50.7 26.5 %collective-permute-start.16 = (bf16[8,64,512]{2,1,0:T(8,128)(2,1)}, bf16[8,64,512]{2,1,0:T(8,128)(2,1)S(1)}, u32[]{:S(2)}, u32[]{:S(2)}) collective-permute-start(bf16[8,64,512]{2,1,0:T(8,128)(2,1)} %slice_bitcast_fusion), channel_id=1, source_target_pairs={{0,64},{64,0},{128,192},{192,128},{1,65},{65,1},{129,193},{193,129... | collective-permute-start | bytes 1572872 | tf_op jit(solution)/shard_map/ppermute | solution.py:41
  50.7 10.1 %collective-permute-start.12 = (bf16[2,64,896]{2,1,0:T(8,128)(2,1)}, bf16[2,64,896]{2,1,0:T(8,128)(2,1)}, u32[]{:S(2)}, u32[]{:S(2)}) collective-permute-start(bf16[2,64,896]{2,1,0:T(8,128)(2,1)} %copy-done.2), channel_id=1, source_target_pairs={{0,7},{1,0},{2,1},{3,2},{4,3},{5,4},{6,5},{7,6},{8,15},{9,8},{10,9... | collective-permute-start | bytes 688136 | tf_op jit(solution)/shard_map/ppermute | solution.py:37
  54.9 9.5 %collective-permute-start.13 = (bf16[2,64,896]{2,1,0:T(8,128)(2,1)}, bf16[2,64,896]{2,1,0:T(8,128)(2,1)}, u32[]{:S(2)}, u32[]{:S(2)}) collective-permute-start(bf16[2,64,896]{2,1,0:T(8,128)(2,1)} %collective-permute-done.11.refs_8_), channel_id=1, source_target_pairs={{0,1},{1,2},{2,3},{3,4},{4,5},{5,6},{6,7},{7,0},{8,9},{9,10},{10,1... | collective-permute-start | bytes 688136 | tf_op jit(solution)/shard_map/ppermute | solution.py:37
  55.6 8.8 %collective-permute-start.10 = (bf16[2,64,896]{2,1,0:T(8,128)(2,1)}, bf16[2,64,896]{2,1,0:T(8,128)(2,1)}, u32[]{:S(2)}, u32[]{:S(2)}) collective-permute-start(bf16[2,64,896]{2,1,0:T(8,128)(2,1)} %slice.25), channel_id=1, source_target_pairs={{0,48},{1,49},{2,50},{3,51},{4,52},{5,53},{6,54},{7,55},{8,56},{9,... | collective-permute-start | bytes 688136 | tf_op jit(solution)/shard_map/ppermute | solution.py:37
  57.5 9.0 %collective-permute-start.9 = (bf16[2,64,896]{2,1,0:T(8,128)(2,1)}, bf16[2,64,896]{2,1,0:T(8,128)(2,1)}, u32[]{:S(2)}, u32[]{:S(2)}) collective-permute-start(bf16[2,64,896]{2,1,0:T(8,128)(2,1)} %slice.24), channel_id=1, source_target_pairs={{0,16},{1,17},{2,18},{3,19},{4,20},{5,21},{6,22},{7,23},{8,24},{9,... | collective-permute-start | bytes 688136 | tf_op jit(solution)/shard_map/ppermute | solution.py:37
  60.8 8.8 %collective-permute-start.14 = (bf16[2,64,896]{2,1,0:T(8,128)(2,1)}, bf16[2,64,896]{2,1,0:T(8,128)(2,1)}, u32[]{:S(2)}, u32[]{:S(2)}) collective-permute-start(bf16[2,64,896]{2,1,0:T(8,128)(2,1)} %collective-permute-done.12.refs_9_), channel_id=1, source_target_pairs={{0,7},{1,0},{2,1},{3,2},{4,3},{5,4},{6,5},{7,6},{8,15},{9,8},{10,9... | collective-permute-start | bytes 688136 | tf_op jit(solution)/shard_map/ppermute | solution.py:37
  64.5 8.5 %collective-permute-start.15 = (bf16[2,64,896]{2,1,0:T(8,128)(2,1)}, bf16[2,64,896]{2,1,0:T(8,128)(2,1)}, u32[]{:S(2)}, u32[]{:S(2)}) collective-permute-start(bf16[2,64,896]{2,1,0:T(8,128)(2,1)} %collective-permute-done.13.refs_10_), channel_id=1, source_target_pairs={{0,1},{1,2},{2,3},{3,4},{4,5},{5,6},{6,7},{7,0},{8,9},{9,10},{10,1... | collective-permute-start | bytes 688136 | tf_op jit(solution)/shard_map/ppermute | solution.py:37
  78.0 2.7 %collective-permute-start.17 = (bf16[512,1024]{1,0:T(8,128)(2,1)S(1)}, bf16[512,1024]{1,0:T(8,128)(2,1)S(1)}, u32[]{:S(2)}, u32[]{:S(2)}) collective-permute-start(bf16[512,1024]{1,0:T(8,128)(2,1)S(1)} %mix.1), channel_id=1, source_target_pairs={{0,64},{64,0},{128,192},{192,128},{1,65},{65,1},{129,193},{193,129... | collective-permute-start | bytes 3145736 | tf_op jit(solution)/shard_map/ppermute | solution.py:41
  103.0 12.2 %all-to-all-start.2 = ((f32[4,8,896]{2,1,0:T(8,128)}), f32[4,8,896]{2,1,0:T(8,128)S(1)}, u32[]{:S(2)}, u32[]{:S(2)}) async-start(f32[4,8,896]{2,1,0:T(8,128)} %convert_reduce_fusion), calls=%async_computation.2 | async-start | bytes 229376 | tf_op jit(solution)/shard_map/all_to_all | solution.py:302

commit v25 on v20

--- a/solution.py
+++ b/solution.py
@@ -222,9 +222,9 @@
     )(near(rows), near(cols))
 
 
-def place_of(d):
-    yx, z = d // NZ, d % NZ
-    return (yx * 2 + z % 2) * (NZ // 2) + z // 2
+def window_at(place):
+    outer, half = place // (NZ // 2), place % (NZ // 2)
+    return outer // 2 * NZ + 2 * half + outer % 2
 
 
 def project_body(m_ref, left_ref, right_ref, out_ref, x_ref, part_ref, sem):
@@ -238,9 +238,11 @@
     for part, (start, size) in enumerate(((0, 224), (224, 208))):
         at = pl.ds(start, size)
         x_ref[at, :] = -(dot(left_ref[at, :], high, 1, 0) + dot(left_ref[at, :], low, 1, 0))
-        some = GROUPS * NZ // 2
-        for d in range(part * some, (part + 1) * some):
-            part_ref[place_of(d)] = x_ref[pl.ds(27 * d // 4, 8), :].astype(jnp.bfloat16)
+        some = GROUPS * NZ // 4
+        for pair in range(part * some, (part + 1) * some):
+            starts = [27 * window_at(2 * pair + i) // 4 for i in range(2)]
+            rows = [x_ref[pl.ds(first, 8), :] for first in starts]
+            part_ref[pair] = jnp.concatenate(rows, axis=0).astype(jnp.bfloat16)
         chosen = pl.ds(part * some, some)
         copy = pltpu.make_async_copy(part_ref.at[chosen], out_ref.at[chosen], sem.at[part])
         copy.start()
@@ -250,7 +252,7 @@
 
 
 def project(m, left, right):
-    windows = (GROUPS * NZ, 8, LANES)
+    windows = (GROUPS * NZ // 2, 16, LANES)
     return pl.pallas_call(
         project_body,
         out_shape=jax.ShapeDtypeStruct(windows, jnp.bfloat16),

time: 105 us -> 105 us (level)
  no operation moved by 1% of the time
where the time goes in v25:
time: 105 us
  starting transfers between devices  38.4 us (37%)
  waiting for transfers between devices  26.9 us (26%)
  blocking collectives  18 us (17%)
  Pallas kernels  15.7 us (15%)
  local copies, waits for them, and re-layouts  3.32 us (3%)
  other arithmetic  1.52 us (1%)
    ppermute x12, starting transfers between devices, shift(): return lax.ppermute(block, 'band', band_route(dy, dx, dz))  21.8 us
    all_to_all x1, blocking collectives, reduce_windows(): parts = lax.all_to_all(parts, 'band', 0, 0, axis_index_groups=wide)  18 us
    ppermute x12, waiting for transfers between devices, shift(): return lax.ppermute(block, 'band', band_route(dy, dx, dz))  12.4 us
    all_to_all x1, waiting for transfers between devices, reduce_windows(): lax.all_to_all(parts, 'band', 0, 0, axis_index_groups=deep)  8.91 us
    all_to_all x1, starting transfers between devices, reduce_windows(): lax.all_to_all(parts, 'band', 0, 0, axis_index_groups=deep)  7.43 us
    ppermute x5, waiting for transfers between devices, swap_groups(): return lax.ppermute(block, 'kgrp', [(k, k ^ bit) for k in range(4)])  5.6 us
    pallas_call x1, Pallas kernels, density(): pl.pallas_call(density_body, out_shape=[product, product, points, points]...  4.76 us
    all_to_all x1, starting transfers between devices, on_device(): kern = lax.all_to_all(sends, 'band', 0, 0, axis_index_groups=over_yx)  4.73 us
  transfers between devices with their start and end apart: 20, of which 7 were waited for; matrix products, arithmetic and copies ran while one was open for 0% of the time, Pallas kernels for 9%

profile of v25, /device:TPU:6, one launch (start us, length us, event | category | flops | bytes accessed | tf_op | source)
XLA Modules:
  0.0 104.7 jit_solution(6732504937291354574)
XLA Ops:
  0.0 1.0 lay.1.own_ref
  1.0 1.4 %collective-permute-start.2 = (bf16[64,896]{1,0:T(8,128)(2,1)S(1)}, bf16[64,896]{1,0:T(8,128)(2,1)S(1)}, u32[]{:S(2)}, u32[]{:S(2)}) collective-permute-start(bf16[64,896]{1,0:T(8,128)(2,1)S(1)} %lay.1.own_ref), channel_id=1, source_target_pairs={{0,128},{64,192},{128,0},{192,64},{1,129},{65,193},{129,1},{193,65... | collective-permute-start | bytes 344072 | tf_op jit(solution)/shard_map/ppermute | solution.py:40
  2.4 1.7 %collective-permute-start.3 = (bf16[64,896]{1,0:T(8,128)(2,1)S(1)}, bf16[64,896]{1,0:T(8,128)(2,1)S(1)}, u32[]{:S(2)}, u32[]{:S(2)}) collective-permute-start(bf16[64,896]{1,0:T(8,128)(2,1)S(1)} %lay.1.own_ref), channel_id=1, source_target_pairs={{0,8},{1,9},{2,10},{3,11},{4,12},{5,13},{6,14},{7,15},{8,0},{9,1},... | collective-permute-start | bytes 344072 | tf_op jit(solution)/shard_map/ppermute | solution.py:36
  4.1 1.0 collective-permute-start.4
  5.1 1.4 %collective-permute-start.1 = (s32[1]{0:T(128)}, s32[1]{0:T(128)}, u32[]{:S(2)}, u32[]{:S(2)}) collective-permute-start(s32[1]{0:T(128)} %param.6), channel_id=1, source_target_pairs={{0,128},{64,192},{128,0},{192,64},{1,129},{65,193},{129,1},{193,65... | collective-permute-start | bytes 20 | tf_op jit(solution)/shard_map/ppermute | solution.py:40
  6.5 3.9 %collective-permute-done.1.far_ref = s32[1]{0:T(128)} collective-permute-done((s32[1]{0:T(128)}, s32[1]{0:T(128)}, u32[]{:S(2)}, u32[]{:S(2)}) %collective-permute-start.1) | collective-permute-done | bytes 36 | tf_op jit(solution)/shard_map/ppermute | solution.py:40
  10.5 1.7 %collective-permute-start.5 = (bf16[4,64,896]{2,1,0:T(8,128)(2,1)S(1)}, bf16[4,64,896]{2,1,0:T(8,128)(2,1)S(1)}, u32[]{:S(2)}, u32[]{:S(2)}) collective-permute-start(bf16[4,64,896]{2,1,0:T(8,128)(2,1)S(1)} %get-tuple-element.35.refs_0_), channel_id=1, source_target_pairs={{0,16},{1,17},{2,18},{3,19},{4,20},{5,21},{6,22},{7,23},{8,24},{9,... | collective-permute-start | bytes 1376264 | tf_op jit(solution)/shard_map/ppermute | solution.py:36
  12.1 1.7 %collective-permute-start.6 = (bf16[4,64,896]{2,1,0:T(8,128)(2,1)S(1)}, bf16[4,64,896]{2,1,0:T(8,128)(2,1)S(1)}, u32[]{:S(2)}, u32[]{:S(2)}) collective-permute-start(bf16[4,64,896]{2,1,0:T(8,128)(2,1)S(1)} %get-tuple-element.35.refs_0_), channel_id=1, source_target_pairs={{0,48},{1,49},{2,50},{3,51},{4,52},{5,53},{6,54},{7,55},{8,56},{9,... | collective-permute-start | bytes 1376264 | tf_op jit(solution)/shard_map/ppermute | solution.py:36
  13.8 1.9 %collective-permute-start.7 = (bf16[2,64,896]{2,1,0:T(8,128)(2,1)S(1)}, bf16[2,64,896]{2,1,0:T(8,128)(2,1)S(1)}, u32[]{:S(2)}, u32[]{:S(2)}) collective-permute-start(bf16[2,64,896]{2,1,0:T(8,128)(2,1)S(1)} %get-tuple-element.44.refs_5_), channel_id=1, source_target_pairs={{0,1},{1,2},{2,3},{3,4},{4,5},{5,6},{6,7},{7,0},{8,9},{9,10},{10,1... | collective-permute-start | bytes 688136 | tf_op jit(solution)/shard_map/ppermute | solution.py:36
  15.7 3.9 %collective-permute-start.8 = (bf16[2,64,896]{2,1,0:T(8,128)(2,1)S(1)}, bf16[2,64,896]{2,1,0:T(8,128)(2,1)}, u32[]{:S(2)}, u32[]{:S(2)}) collective-permute-start(bf16[2,64,896]{2,1,0:T(8,128)(2,1)S(1)} %get-tuple-element.44.refs_5_), channel_id=1, source_target_pairs={{0,7},{1,0},{2,1},{3,2},{4,3},{5,4},{6,5},{7,6},{8,15},{9,8},{10,9... | collective-permute-start | bytes 688136 | tf_op jit(solution)/shard_map/ppermute | solution.py:36
  20.3 0.6 copy-done.1
  21.0 4.6 %pack.1 = bf16[8,3,64,512]{3,2,1,0:T(8,128)(2,1)} custom-call(s32[1]{0:T(128)} %bitcast.odd_ref, s32[1]{0:T(128)S(6)} %copy.5.own_ref, s32[1]{0:T(128)} %collective-permute-done.core_ref, s32[1]{0:T(128)} %collective-permute-done.1.far_ref, s32[8]{0:T(128)S(1)} %copy-done.1, bf16[4,2,64,4096]{3,2,1,0:T(8,128)(2,1)} %kernels_ref.1), custom_call_target="tpu_custom_call" | custom-call | tf_op jit(solution)/shard_map/pack/pallas_call | solution.py:109
  25.6 4.7 %all-to-all-start = ((bf16[8,3,64,512]{3,2,1,0:T(8,128)(2,1)}), bf16[8,3,64,512]{3,2,1,0:T(8,128)(2,1)S(1)}, u32[]{:S(2)}, u32[]{:S(2)}) async-start(bf16[8,3,64,512]{3,2,1,0:T(8,128)(2,1)} %pack.1), calls=%async_computation | async-start | bytes 3145728 | tf_op jit(solution)/shard_map/all_to_all | solution.py:329
  30.3 0.8 collective-permute-start.11
  31.2 3.9 %collective-permute-start.12 = (bf16[2,64,896]{2,1,0:T(8,128)(2,1)}, bf16[2,64,896]{2,1,0:T(8,128)(2,1)S(1)}, u32[]{:S(2)}, u32[]{:S(2)}) collective-permute-start(bf16[2,64,896]{2,1,0:T(8,128)(2,1)} %collective-permute-done.8.refs_7_), channel_id=1, source_target_pairs={{0,7},{1,0},{2,1},{3,2},{4,3},{5,4},{6,5},{7,6},{8,15},{9,8},{10,9... | collective-permute-start | bytes 688136 | tf_op jit(solution)/shard_map/ppermute | solution.py:36
  35.1 4.0 %collective-permute-done.11.refs_8_ = bf16[2,64,896]{2,1,0:T(8,128)(2,1)S(1)} collective-permute-done((bf16[2,64,896]{2,1,0:T(8,128)(2,1)S(1)}, bf16[2,64,896]{2,1,0:T(8,128)(2,1)S(1)}, u32[]{:S(2)}, u32[]{:S(2)}) %collective-permute-start.11) | collective-permute-done | bytes 229408 | tf_op jit(solution)/shard_map/ppermute | solution.py:36
  39.1 2.8 %collective-permute-start.10 = (bf16[2,64,896]{2,1,0:T(8,128)(2,1)S(1)}, bf16[2,64,896]{2,1,0:T(8,128)(2,1)S(1)}, u32[]{:S(2)}, u32[]{:S(2)}) collective-permute-start(bf16[2,64,896]{2,1,0:T(8,128)(2,1)S(1)} %slice.22), channel_id=1, source_target_pairs={{0,48},{1,49},{2,50},{3,51},{4,52},{5,53},{6,54},{7,55},{8,56},{9,... | collective-permute-start | bytes 688136 | tf_op jit(solution)/shard_map/ppermute | solution.py:36
  42.0 3.3 %collective-permute-start.14 = (bf16[2,64,896]{2,1,0:T(8,128)(2,1)S(1)}, bf16[2,64,896]{2,1,0:T(8,128)(2,1)S(1)}, u32[]{:S(2)}, u32[]{:S(2)}) collective-permute-start(bf16[2,64,896]{2,1,0:T(8,128)(2,1)S(1)} %collective-permute-done.12.refs_9_), channel_id=1, source_target_pairs={{0,7},{1,0},{2,1},{3,2},{4,3},{5,4},{6,5},{7,6},{8,15},{9,8},{10,9... | collective-permute-start | bytes 688136 | tf_op jit(solution)/shard_map/ppermute | solution.py:36
  45.3 1.0 collective-permute-done.13.refs_10_
  46.4 6.1 %collective-permute-done.10.refs_3_ = bf16[2,64,896]{2,1,0:T(8,128)(2,1)S(1)} collective-permute-done((bf16[2,64,896]{2,1,0:T(8,128)(2,1)S(1)}, bf16[2,64,896]{2,1,0:T(8,128)(2,1)S(1)}, u32[]{:S(2)}, u32[]{:S(2)}) %collective-permute-start.10) | collective-permute-done | bytes 229408 | tf_op jit(solution)/shard_map/ppermute | solution.py:36
  52.5 1.3 %collective-permute-done.9.refs_2_ = bf16[2,64,896]{2,1,0:T(8,128)(2,1)S(1)} collective-permute-done((bf16[2,64,896]{2,1,0:T(8,128)(2,1)S(1)}, bf16[2,64,896]{2,1,0:T(8,128)(2,1)S(1)}, u32[]{:S(2)}, u32[]{:S(2)}) %collective-permute-start.9) | collective-permute-done | bytes 229408 | tf_op jit(solution)/shard_map/ppermute | solution.py:36
  54.4 0.7 copy-done.8
  55.1 0.8 slice_bitcast_fusion
  56.1 4.8 %density.1 = (f32[512,1024]{1,0:T(8,128)S(1)}, f32[512,1024]{1,0:T(8,128)S(1)}, bf16[512,896]{1,0:T(8,128)(2,1)S(1)}, bf16[512,896]{1,0:T(8,128)(2,1)S(1)}) custom-call(s32[8]{0:T(128)S(1)} %stack.71.place_ref, s32[8]{0:T(128)S(1)} %stack.80.slot_ref, bf16[4,64,896]{2,1,0:T(8,128)(2,1)S(1)} %get-tuple-element.35.refs_0_, ...), custom_call_target="tpu_custom_call" | custom-call | tf_op jit(solution)/shard_map/density/pallas_call | solution.py:157
  60.9 0.8 mix.1
  62.9 1.7 %collective-permute-done.17.m_ref = bf16[512,1024]{1,0:T(8,128)(2,1)S(1)} collective-permute-done((bf16[512,1024]{1,0:T(8,128)(2,1)S(1)}, bf16[512,1024]{1,0:T(8,128)(2,1)S(1)}, u32[]{:S(2)}, u32[]{:S(2)}) %collective-permute-start.17) | collective-permute-done | bytes 1048608 | tf_op jit(solution)/shard_map/ppermute | solution.py:40
  64.7 4.0 %project.1 = bf16[32,16,896]{2,1,0:T(8,128)(2,1)S(1)} custom-call(bf16[512,1024]{1,0:T(8,128)(2,1)S(1)} %collective-permute-done.17.m_ref, bf16[432,1024]{1,0:T(8,128)(2,1)S(1)} %get-tuple-element.57.left_ref, bf16[1024,896]{1,0:T(8,128)(2,1)S(1)} %get-tuple-element.58.right_ref), custom_call_target="tpu_custom_call" | custom-call | tf_op jit(solution)/shard_map/project/pallas_call | solution.py:256
  68.6 18.0 %all_to_all.15 = bf16[16,4,8,896]{3,2,1,0:T(8,128)(2,1)S(1)} all-to-all(bf16[16,4,8,896]{3,2,1,0:T(8,128)(2,1)S(1)} %bitcast.22), channel_id=1, replica_groups={{0,1,8,9,16,17,24,25,32,33,40,41,48,49,56,57},{2,3,10,11,18,19,26,27,34..., dimensions={0} | all-to-all | bytes 1835008 | tf_op jit(solution)/shard_map/all_to_all | solution.py:297
  86.6 0.8 convert_reduce_fusion
  87.4 7.4 %all-to-all-start.2 = ((f32[4,8,896]{2,1,0:T(8,128)}), f32[4,8,896]{2,1,0:T(8,128)S(1)}, u32[]{:S(2)}, u32[]{:S(2)}) async-start(f32[4,8,896]{2,1,0:T(8,128)} %convert_reduce_fusion), calls=%async_computation.2 | async-start | bytes 229376 | tf_op jit(solution)/shard_map/all_to_all | solution.py:299
  94.8 8.9 %all-to-all-done.2 = f32[4,8,896]{2,1,0:T(8,128)S(1)} async-done(((f32[4,8,896]{2,1,0:T(8,128)}), f32[4,8,896]{2,1,0:T(8,128)S(1)}, u32[]{:S(2)}, u32[]{:S(2)}) %all-to-all-start.2) | async-done | bytes 114720 | tf_op jit(solution)/shard_map/all_to_all | solution.py:299
  104.0 0.7 fusion.1
  (47 shorter events, 2.5 us)
Async XLA Ops:
  1.0 9.4 %collective-permute-start.2 = (bf16[64,896]{1,0:T(8,128)(2,1)S(1)}, bf16[64,896]{1,0:T(8,128)(2,1)S(1)}, u32[]{:S(2)}, u32[]{:S(2)}) collective-permute-start(bf16[64,896]{1,0:T(8,128)(2,1)S(1)} %lay.1.own_ref), channel_id=1, source_target_pairs={{0,128},{64,192},{128,0},{192,64},{1,129},{65,193},{129,1},{193,65... | collective-permute-start | bytes 344072 | tf_op jit(solution)/shard_map/ppermute | solution.py:40
  2.4 8.0 %collective-permute-start.3 = (bf16[64,896]{1,0:T(8,128)(2,1)S(1)}, bf16[64,896]{1,0:T(8,128)(2,1)S(1)}, u32[]{:S(2)}, u32[]{:S(2)}) collective-permute-start(bf16[64,896]{1,0:T(8,128)(2,1)S(1)} %lay.1.own_ref), channel_id=1, source_target_pairs={{0,8},{1,9},{2,10},{3,11},{4,12},{5,13},{6,14},{7,15},{8,0},{9,1},... | collective-permute-start | bytes 344072 | tf_op jit(solution)/shard_map/ppermute | solution.py:36
  4.1 6.3 %collective-permute-start.4 = (bf16[64,896]{1,0:T(8,128)(2,1)S(1)}, bf16[64,896]{1,0:T(8,128)(2,1)S(1)}, u32[]{:S(2)}, u32[]{:S(2)}) collective-permute-start(bf16[64,896]{1,0:T(8,128)(2,1)S(1)} %lay.1.own_ref), channel_id=1, source_target_pairs={{128,8},{129,9},{130,10},{131,11},{132,12},{133,13},{134,14},{135,... | collective-permute-start | bytes 344072 | tf_op jit(solution)/shard_map/ppermute | solution.py:46
  5.1 1.4 %collective-permute-start = (s32[1]{0:T(128)}, s32[1]{0:T(128)}, u32[]{:S(2)}, u32[]{:S(2)}) collective-permute-start(s32[1]{0:T(128)} %param.6), channel_id=1, source_target_pairs={{0,64},{64,0},{128,192},{192,128},{1,65},{65,1},{129,193},{193,129... | collective-permute-start | bytes 20 | tf_op jit(solution)/shard_map/ppermute | solution.py:40
  5.1 5.3 %collective-permute-start.1 = (s32[1]{0:T(128)}, s32[1]{0:T(128)}, u32[]{:S(2)}, u32[]{:S(2)}) collective-permute-start(s32[1]{0:T(128)} %param.6), channel_id=1, source_target_pairs={{0,128},{64,192},{128,0},{192,64},{1,129},{65,193},{129,1},{193,65... | collective-permute-start | bytes 20 | tf_op jit(solution)/shard_map/ppermute | solution.py:40
  10.5 15.1 %copy-start = (bf16[2,64,896]{2,1,0:T(8,128)(2,1)}, bf16[2,64,896]{2,1,0:T(8,128)(2,1)S(1)}, u32[]{:S(2)}) copy-start(bf16[2,64,896]{2,1,0:T(8,128)(2,1)S(1)} %get-tuple-element.44.refs_5_) | copy-start | bytes 688132
  10.5 15.1 %collective-permute-start.5 = (bf16[4,64,896]{2,1,0:T(8,128)(2,1)S(1)}, bf16[4,64,896]{2,1,0:T(8,128)(2,1)S(1)}, u32[]{:S(2)}, u32[]{:S(2)}) collective-permute-start(bf16[4,64,896]{2,1,0:T(8,128)(2,1)S(1)} %get-tuple-element.35.refs_0_), channel_id=1, source_target_pairs={{0,16},{1,17},{2,18},{3,19},{4,20},{5,21},{6,22},{7,23},{8,24},{9,... | collective-permute-start | bytes 1376264 | tf_op jit(solution)/shard_map/ppermute | solution.py:36
  12.1 13.5 %collective-permute-start.6 = (bf16[4,64,896]{2,1,0:T(8,128)(2,1)S(1)}, bf16[4,64,896]{2,1,0:T(8,128)(2,1)S(1)}, u32[]{:S(2)}, u32[]{:S(2)}) collective-permute-start(bf16[4,64,896]{2,1,0:T(8,128)(2,1)S(1)} %get-tuple-element.35.refs_0_), channel_id=1, source_target_pairs={{0,48},{1,49},{2,50},{3,51},{4,52},{5,53},{6,54},{7,55},{8,56},{9,... | collective-permute-start | bytes 1376264 | tf_op jit(solution)/shard_map/ppermute | solution.py:36
  13.8 11.8 %collective-permute-start.7 = (bf16[2,64,896]{2,1,0:T(8,128)(2,1)S(1)}, bf16[2,64,896]{2,1,0:T(8,128)(2,1)S(1)}, u32[]{:S(2)}, u32[]{:S(2)}) collective-permute-start(bf16[2,64,896]{2,1,0:T(8,128)(2,1)S(1)} %get-tuple-element.44.refs_5_), channel_id=1, source_target_pairs={{0,1},{1,2},{2,3},{3,4},{4,5},{5,6},{6,7},{7,0},{8,9},{9,10},{10,1... | collective-permute-start | bytes 688136 | tf_op jit(solution)/shard_map/ppermute | solution.py:36
  15.7 9.9 %collective-permute-start.8 = (bf16[2,64,896]{2,1,0:T(8,128)(2,1)S(1)}, bf16[2,64,896]{2,1,0:T(8,128)(2,1)}, u32[]{:S(2)}, u32[]{:S(2)}) collective-permute-start(bf16[2,64,896]{2,1,0:T(8,128)(2,1)S(1)} %get-tuple-element.44.refs_5_), channel_id=1, source_target_pairs={{0,7},{1,0},{2,1},{3,2},{4,3},{5,4},{6,5},{7,6},{8,15},{9,8},{10,9... | collective-permute-start | bytes 688136 | tf_op jit(solution)/shard_map/ppermute | solution.py:36
  20.3 0.7 copy-start.1
  25.6 13.6 %copy-start.2 = (bf16[2,64,896]{2,1,0:T(8,128)(2,1)}, bf16[2,64,896]{2,1,0:T(8,128)(2,1)S(1)}, u32[]{:S(2)}) copy-start(bf16[2,64,896]{2,1,0:T(8,128)(2,1)S(1)} %collective-permute-done.7.refs_6_) | copy-start | bytes 688132
  25.6 29.5 %all-to-all-start = ((bf16[8,3,64,512]{3,2,1,0:T(8,128)(2,1)}), bf16[8,3,64,512]{3,2,1,0:T(8,128)(2,1)S(1)}, u32[]{:S(2)}, u32[]{:S(2)}) async-start(bf16[8,3,64,512]{3,2,1,0:T(8,128)(2,1)} %pack.1), calls=%async_computation | async-start | bytes 3145728 | tf_op jit(solution)/shard_map/all_to_all | solution.py:329
  30.3 8.8 %collective-permute-start.11 = (bf16[2,64,896]{2,1,0:T(8,128)(2,1)S(1)}, bf16[2,64,896]{2,1,0:T(8,128)(2,1)S(1)}, u32[]{:S(2)}, u32[]{:S(2)}) collective-permute-start(bf16[2,64,896]{2,1,0:T(8,128)(2,1)S(1)} %collective-permute-done.7.refs_6_), channel_id=1, source_target_pairs={{0,1},{1,2},{2,3},{3,4},{4,5},{5,6},{6,7},{7,0},{8,9},{9,10},{10,1... | collective-permute-start | bytes 688136 | tf_op jit(solution)/shard_map/ppermute | solution.py:36
  31.2 10.8 %collective-permute-start.12 = (bf16[2,64,896]{2,1,0:T(8,128)(2,1)}, bf16[2,64,896]{2,1,0:T(8,128)(2,1)S(1)}, u32[]{:S(2)}, u32[]{:S(2)}) collective-permute-start(bf16[2,64,896]{2,1,0:T(8,128)(2,1)} %collective-permute-done.8.refs_7_), channel_id=1, source_target_pairs={{0,7},{1,0},{2,1},{3,2},{4,3},{5,4},{6,5},{7,6},{8,15},{9,8},{10,9... | collective-permute-start | bytes 688136 | tf_op jit(solution)/shard_map/ppermute | solution.py:36
  39.1 14.7 %copy-start.3 = (bf16[2,64,896]{2,1,0:T(8,128)(2,1)}, bf16[2,64,896]{2,1,0:T(8,128)(2,1)S(1)}, u32[]{:S(2)}) copy-start(bf16[2,64,896]{2,1,0:T(8,128)(2,1)S(1)} %collective-permute-done.11.refs_8_) | copy-start | bytes 688132
  39.1 7.2 %collective-permute-start.13 = (bf16[2,64,896]{2,1,0:T(8,128)(2,1)S(1)}, bf16[2,64,896]{2,1,0:T(8,128)(2,1)S(1)}, u32[]{:S(2)}, u32[]{:S(2)}) collective-permute-start(bf16[2,64,896]{2,1,0:T(8,128)(2,1)S(1)} %collective-permute-done.11.refs_8_), channel_id=1, source_target_pairs={{0,1},{1,2},{2,3},{3,4},{4,5},{5,6},{6,7},{7,0},{8,9},{9,10},{10,1... | collective-permute-start | bytes 688136 | tf_op jit(solution)/shard_map/ppermute | solution.py:36
  39.1 13.3 %collective-permute-start.10 = (bf16[2,64,896]{2,1,0:T(8,128)(2,1)S(1)}, bf16[2,64,896]{2,1,0:T(8,128)(2,1)S(1)}, u32[]{:S(2)}, u32[]{:S(2)}) collective-permute-start(bf16[2,64,896]{2,1,0:T(8,128)(2,1)S(1)} %slice.22), channel_id=1, source_target_pairs={{0,48},{1,49},{2,50},{3,51},{4,52},{5,53},{6,54},{7,55},{8,56},{9,... | collective-permute-start | bytes 688136 | tf_op jit(solution)/shard_map/ppermute | solution.py:36
  41.9 11.8 %collective-permute-start.9 = (bf16[2,64,896]{2,1,0:T(8,128)(2,1)S(1)}, bf16[2,64,896]{2,1,0:T(8,128)(2,1)S(1)}, u32[]{:S(2)}, u32[]{:S(2)}) collective-permute-start(bf16[2,64,896]{2,1,0:T(8,128)(2,1)S(1)} %slice.21), channel_id=1, source_target_pairs={{0,16},{1,17},{2,18},{3,19},{4,20},{5,21},{6,22},{7,23},{8,24},{9,... | collective-permute-start | bytes 688136 | tf_op jit(solution)/shard_map/ppermute | solution.py:36
  42.0 11.7 %copy-start.4 = (bf16[2,64,896]{2,1,0:T(8,128)(2,1)}, bf16[2,64,896]{2,1,0:T(8,128)(2,1)S(1)}, u32[]{:S(2)}) copy-start(bf16[2,64,896]{2,1,0:T(8,128)(2,1)S(1)} %collective-permute-done.12.refs_9_) | copy-start | bytes 688132
  42.0 11.7 %collective-permute-start.14 = (bf16[2,64,896]{2,1,0:T(8,128)(2,1)S(1)}, bf16[2,64,896]{2,1,0:T(8,128)(2,1)S(1)}, u32[]{:S(2)}, u32[]{:S(2)}) collective-permute-start(bf16[2,64,896]{2,1,0:T(8,128)(2,1)S(1)} %collective-permute-done.12.refs_9_), channel_id=1, source_target_pairs={{0,7},{1,0},{2,1},{3,2},{4,3},{5,4},{6,5},{7,6},{8,15},{9,8},{10,9... | collective-permute-start | bytes 688136 | tf_op jit(solution)/shard_map/ppermute | solution.py:36
  46.3 7.4 %copy-start.5 = (bf16[2,64,896]{2,1,0:T(8,128)(2,1)}, bf16[2,64,896]{2,1,0:T(8,128)(2,1)S(1)}, u32[]{:S(2)}) copy-start(bf16[2,64,896]{2,1,0:T(8,128)(2,1)S(1)} %collective-permute-done.13.refs_10_) | copy-start | bytes 688132
  46.3 8.8 %collective-permute-start.15 = (bf16[2,64,896]{2,1,0:T(8,128)(2,1)S(1)}, bf16[2,64,896]{2,1,0:T(8,128)(2,1)}, u32[]{:S(2)}, u32[]{:S(2)}) collective-permute-start(bf16[2,64,896]{2,1,0:T(8,128)(2,1)S(1)} %collective-permute-done.13.refs_10_), channel_id=1, source_target_pairs={{0,1},{1,2},{2,3},{3,4},{4,5},{5,6},{6,7},{7,0},{8,9},{9,10},{10,1... | collective-permute-start | bytes 688136 | tf_op jit(solution)/shard_map/ppermute | solution.py:36
  52.5 1.3 %copy-start.6 = (bf16[2,64,896]{2,1,0:T(8,128)(2,1)}, bf16[2,64,896]{2,1,0:T(8,128)(2,1)S(1)}, u32[]{:S(2)}) copy-start(bf16[2,64,896]{2,1,0:T(8,128)(2,1)S(1)} %collective-permute-done.10.refs_3_) | copy-start | bytes 688132
  53.8 0.7 copy-start.7
  54.4 0.7 copy-start.8
  56.0 4.9 %collective-permute-start.16 = (bf16[8,64,512]{2,1,0:T(8,128)(2,1)}, bf16[8,64,512]{2,1,0:T(8,128)(2,1)S(1)}, u32[]{:S(2)}, u32[]{:S(2)}) collective-permute-start(bf16[8,64,512]{2,1,0:T(8,128)(2,1)} %slice_bitcast_fusion), channel_id=1, source_target_pairs={{0,64},{64,0},{128,192},{192,128},{1,65},{65,1},{129,193},{193,129... | collective-permute-start | bytes 1572872 | tf_op jit(solution)/shard_map/ppermute | solution.py:40
  61.8 2.9 %collective-permute-start.17 = (bf16[512,1024]{1,0:T(8,128)(2,1)S(1)}, bf16[512,1024]{1,0:T(8,128)(2,1)S(1)}, u32[]{:S(2)}, u32[]{:S(2)}) collective-permute-start(bf16[512,1024]{1,0:T(8,128)(2,1)S(1)} %mix.1), channel_id=1, source_target_pairs={{0,64},{64,0},{128,192},{192,128},{1,65},{65,1},{129,193},{193,129... | collective-permute-start | bytes 3145736 | tf_op jit(solution)/shard_map/ppermute | solution.py:40
  87.4 16.3 %all-to-all-start.2 = ((f32[4,8,896]{2,1,0:T(8,128)}), f32[4,8,896]{2,1,0:T(8,128)S(1)}, u32[]{:S(2)}, u32[]{:S(2)}) async-start(f32[4,8,896]{2,1,0:T(8,128)} %convert_reduce_fusion), calls=%async_computation.2 | async-start | bytes 229376 | tf_op jit(solution)/shard_map/all_to_all | solution.py:299

commit v26 on v25

--- a/solution.py
+++ b/solution.py
@@ -151,9 +151,8 @@
 def density(place, slots, four, up, over, down, cols):
     product = pltpu.VMEM((BLOCK, 2 * BLOCK), jnp.float32)
     points = pltpu.VMEM((BLOCK, LANES), jnp.bfloat16)
-    in_hbm = pl.BlockSpec(memory_space=pltpu.HBM)
-    specs = [IN_VMEM] * 2 + [in_hbm] * 2 + [IN_VMEM] + [in_hbm] * NZ
-    arrays = [near(four), near(up), *map(away, over), near(down), *map(away, cols)]
+    specs = [IN_VMEM] * 2 + [ANYWHERE] * 2 + [IN_VMEM] + [ANYWHERE] * NZ
+    arrays = [near(four), near(up), *over, near(down), *cols]
     return pl.pallas_call(
         density_body,
         out_shape=[product, product, points, points],

time: 105 us -> 117 us (1.11)
  local copies, waits for them, and re-layouts: 3.32 us -> 14.5 us
  waiting for transfers between devices: 26.9 us -> 24.8 us
  Pallas kernels: 15.7 us -> 17.4 us
    unnamed x18 -> x38, local copies, waits for them, and re-layouts: 2 us -> 13.3 us
    ppermute x12, waiting for transfers between devices: 12.4 us -> 10.4 us  [shift(): return lax.ppermute(block, 'band', band_route(dy, dx, dz))]
    pallas_call x1, Pallas kernels: 4.76 us -> 6.33 us  [density(): pl.pallas_call(density_body, out_shape=[product, product, points, points]...]
  transfers between devices with their start and end apart: 20 -> 20, of which waited for: 7 -> 7; matrix products, arithmetic and copies ran while one was open for 0% -> 0% of each run, Pallas kernels for 9% -> 10%
where the time goes in v26:
time: 117 us; the launch traced here: 116 us
  starting transfers between devices  38.7 us (33%)
  waiting for transfers between devices  24.8 us (21%)
  blocking collectives  18.7 us (16%)
  Pallas kernels  17.4 us (15%)
  local copies, waits for them, and re-layouts  14.5 us (12%)
  other arithmetic  1.52 us (1%)
    ppermute x12, starting transfers between devices, shift(): return lax.ppermute(block, 'band', band_route(dy, dx, dz))  22 us
    all_to_all x1, blocking collectives, reduce_windows(): parts = lax.all_to_all(parts, 'band', 0, 0, axis_index_groups=wide)  18.7 us
    unnamed x38, local copies, waits for them, and re-layouts  13.3 us
    ppermute x12, waiting for transfers between devices, shift(): return lax.ppermute(block, 'band', band_route(dy, dx, dz))  10.4 us
    all_to_all x1, waiting for transfers between devices, reduce_windows(): lax.all_to_all(parts, 'band', 0, 0, axis_index_groups=deep)  8.91 us
    all_to_all x1, starting transfers between devices, reduce_windows(): lax.all_to_all(parts, 'band', 0, 0, axis_index_groups=deep)  7.55 us
    pallas_call x1, Pallas kernels, density(): pl.pallas_call(density_body, out_shape=[product, product, points, points]...  6.33 us
    ppermute x5, waiting for transfers between devices, swap_groups(): return lax.ppermute(block, 'kgrp', [(k, k ^ bit) for k in range(4)])  5.45 us
  transfers between devices with their start and end apart: 20, of which 7 were waited for; matrix products, arithmetic and copies ran while one was open for 0% of the time, Pallas kernels for 10%

profile of v26, /device:TPU:6, one launch (start us, length us, event | category | flops | bytes accessed | tf_op | source)
XLA Modules:
  0.0 116.5 jit_solution(15844428088556413749)
XLA Ops:
  0.0 1.0 lay.1.own_ref
  1.0 1.4 %collective-permute-start.2 = (bf16[64,896]{1,0:T(8,128)(2,1)S(1)}, bf16[64,896]{1,0:T(8,128)(2,1)S(1)}, u32[]{:S(2)}, u32[]{:S(2)}) collective-permute-start(bf16[64,896]{1,0:T(8,128)(2,1)S(1)} %lay.1.own_ref), channel_id=1, source_target_pairs={{0,128},{64,192},{128,0},{192,64},{1,129},{65,193},{129,1},{193,65... | collective-permute-start | bytes 344072 | tf_op jit(solution)/shard_map/ppermute | solution.py:40
  2.4 1.7 %collective-permute-start.3 = (bf16[64,896]{1,0:T(8,128)(2,1)S(1)}, bf16[64,896]{1,0:T(8,128)(2,1)S(1)}, u32[]{:S(2)}, u32[]{:S(2)}) collective-permute-start(bf16[64,896]{1,0:T(8,128)(2,1)S(1)} %lay.1.own_ref), channel_id=1, source_target_pairs={{0,8},{1,9},{2,10},{3,11},{4,12},{5,13},{6,14},{7,15},{8,0},{9,1},... | collective-permute-start | bytes 344072 | tf_op jit(solution)/shard_map/ppermute | solution.py:36
  4.1 1.0 collective-permute-start.4
  5.1 1.4 %collective-permute-start.1 = (s32[1]{0:T(128)}, s32[1]{0:T(128)}, u32[]{:S(2)}, u32[]{:S(2)}) collective-permute-start(s32[1]{0:T(128)} %param.6), channel_id=1, source_target_pairs={{0,128},{64,192},{128,0},{192,64},{1,129},{65,193},{129,1},{193,65... | collective-permute-start | bytes 20 | tf_op jit(solution)/shard_map/ppermute | solution.py:40
  6.5 3.7 %collective-permute-done.1.far_ref = s32[1]{0:T(128)} collective-permute-done((s32[1]{0:T(128)}, s32[1]{0:T(128)}, u32[]{:S(2)}, u32[]{:S(2)}) %collective-permute-start.1) | collective-permute-done | bytes 36 | tf_op jit(solution)/shard_map/ppermute | solution.py:40
  10.3 1.7 %collective-permute-start.5 = (bf16[4,64,896]{2,1,0:T(8,128)(2,1)S(1)}, bf16[4,64,896]{2,1,0:T(8,128)(2,1)S(1)}, u32[]{:S(2)}, u32[]{:S(2)}) collective-permute-start(bf16[4,64,896]{2,1,0:T(8,128)(2,1)S(1)} %get-tuple-element.35.refs_0_), channel_id=1, source_target_pairs={{0,16},{1,17},{2,18},{3,19},{4,20},{5,21},{6,22},{7,23},{8,24},{9,... | collective-permute-start | bytes 1376264 | tf_op jit(solution)/shard_map/ppermute | solution.py:36
  12.0 1.7 %collective-permute-start.6 = (bf16[4,64,896]{2,1,0:T(8,128)(2,1)S(1)}, bf16[4,64,896]{2,1,0:T(8,128)(2,1)S(1)}, u32[]{:S(2)}, u32[]{:S(2)}) collective-permute-start(bf16[4,64,896]{2,1,0:T(8,128)(2,1)S(1)} %get-tuple-element.35.refs_0_), channel_id=1, source_target_pairs={{0,48},{1,49},{2,50},{3,51},{4,52},{5,53},{6,54},{7,55},{8,56},{9,... | collective-permute-start | bytes 1376264 | tf_op jit(solution)/shard_map/ppermute | solution.py:36
  13.7 1.9 %collective-permute-start.7 = (bf16[2,64,896]{2,1,0:T(8,128)(2,1)S(1)}, bf16[2,64,896]{2,1,0:T(8,128)(2,1)S(1)}, u32[]{:S(2)}, u32[]{:S(2)}) collective-permute-start(bf16[2,64,896]{2,1,0:T(8,128)(2,1)S(1)} %get-tuple-element.44.refs_5_), channel_id=1, source_target_pairs={{0,1},{1,2},{2,3},{3,4},{4,5},{5,6},{6,7},{7,0},{8,9},{9,10},{10,1... | collective-permute-start | bytes 688136 | tf_op jit(solution)/shard_map/ppermute | solution.py:36
  15.6 3.9 %collective-permute-start.8 = (bf16[2,64,896]{2,1,0:T(8,128)(2,1)S(1)}, bf16[2,64,896]{2,1,0:T(8,128)(2,1)}, u32[]{:S(2)}, u32[]{:S(2)}) collective-permute-start(bf16[2,64,896]{2,1,0:T(8,128)(2,1)S(1)} %get-tuple-element.44.refs_5_), channel_id=1, source_target_pairs={{0,7},{1,0},{2,1},{3,2},{4,3},{5,4},{6,5},{7,6},{8,15},{9,8},{10,9... | collective-permute-start | bytes 688136 | tf_op jit(solution)/shard_map/ppermute | solution.py:36
  20.8 4.6 %pack.1 = bf16[8,3,64,512]{3,2,1,0:T(8,128)(2,1)} custom-call(s32[1]{0:T(128)} %bitcast.odd_ref, s32[1]{0:T(128)S(6)} %copy.5.own_ref, s32[1]{0:T(128)} %collective-permute-done.core_ref, s32[1]{0:T(128)} %collective-permute-done.1.far_ref, s32[8]{0:T(128)S(1)} %copy-done.18, bf16[4,2,64,4096]{3,2,1,0:T(8,128)(2,1)} %kernels_ref.1), custom_call_target="tpu_custom_call" | custom-call | tf_op jit(solution)/shard_map/pack/pallas_call | solution.py:109
  25.5 4.7 %all-to-all-start = ((bf16[8,3,64,512]{3,2,1,0:T(8,128)(2,1)}), bf16[8,3,64,512]{3,2,1,0:T(8,128)(2,1)S(1)}, u32[]{:S(2)}, u32[]{:S(2)}) async-start(bf16[8,3,64,512]{3,2,1,0:T(8,128)(2,1)} %pack.1), calls=%async_computation | async-start | bytes 3145728 | tf_op jit(solution)/shard_map/all_to_all | solution.py:328
  30.3 1.1 collective-permute-start.11
  31.3 3.9 %collective-permute-start.12 = (bf16[2,64,896]{2,1,0:T(8,128)(2,1)}, bf16[2,64,896]{2,1,0:T(8,128)(2,1)S(1)}, u32[]{:S(2)}, u32[]{:S(2)}) collective-permute-start(bf16[2,64,896]{2,1,0:T(8,128)(2,1)} %collective-permute-done.8.refs_7_), channel_id=1, source_target_pairs={{0,7},{1,0},{2,1},{3,2},{4,3},{5,4},{6,5},{7,6},{8,15},{9,8},{10,9... | collective-permute-start | bytes 688136 | tf_op jit(solution)/shard_map/ppermute | solution.py:36
  35.3 4.0 %collective-permute-done.11.refs_8_ = bf16[2,64,896]{2,1,0:T(8,128)(2,1)S(1)} collective-permute-done((bf16[2,64,896]{2,1,0:T(8,128)(2,1)S(1)}, bf16[2,64,896]{2,1,0:T(8,128)(2,1)S(1)}, u32[]{:S(2)}, u32[]{:S(2)}) %collective-permute-start.11) | collective-permute-done | bytes 229408 | tf_op jit(solution)/shard_map/ppermute | solution.py:36
  39.3 2.8 %collective-permute-start.10 = (bf16[2,64,896]{2,1,0:T(8,128)(2,1)S(1)}, bf16[2,64,896]{2,1,0:T(8,128)(2,1)S(1)}, u32[]{:S(2)}, u32[]{:S(2)}) collective-permute-start(bf16[2,64,896]{2,1,0:T(8,128)(2,1)S(1)} %slice.22), channel_id=1, source_target_pairs={{0,48},{1,49},{2,50},{3,51},{4,52},{5,53},{6,54},{7,55},{8,56},{9,... | collective-permute-start | bytes 688136 | tf_op jit(solution)/shard_map/ppermute | solution.py:36
  42.2 3.3 %collective-permute-start.14 = (bf16[2,64,896]{2,1,0:T(8,128)(2,1)S(1)}, bf16[2,64,896]{2,1,0:T(8,128)(2,1)S(1)}, u32[]{:S(2)}, u32[]{:S(2)}) collective-permute-start(bf16[2,64,896]{2,1,0:T(8,128)(2,1)S(1)} %collective-permute-done.12.refs_9_), channel_id=1, source_target_pairs={{0,7},{1,0},{2,1},{3,2},{4,3},{5,4},{6,5},{7,6},{8,15},{9,8},{10,9... | collective-permute-start | bytes 688136 | tf_op jit(solution)/shard_map/ppermute | solution.py:36
  47.2 5.5 %collective-permute-done.10.refs_3_ = bf16[2,64,896]{2,1,0:T(8,128)(2,1)S(1)} collective-permute-done((bf16[2,64,896]{2,1,0:T(8,128)(2,1)S(1)}, bf16[2,64,896]{2,1,0:T(8,128)(2,1)S(1)}, u32[]{:S(2)}, u32[]{:S(2)}) %collective-permute-start.10) | collective-permute-done | bytes 229408 | tf_op jit(solution)/shard_map/ppermute | solution.py:36
  57.0 0.9 copy-done.1
  58.0 0.9 copy-done.3
  58.9 0.9 copy-done.5
  59.9 0.9 copy-done.7
  60.8 0.9 copy-done.9
  61.7 0.9 copy-done.11
  63.6 0.9 copy-done.15
  64.6 0.9 copy-done.17
  65.5 6.3 %density.1 = (f32[512,1024]{1,0:T(8,128)S(1)}, f32[512,1024]{1,0:T(8,128)S(1)}, bf16[512,896]{1,0:T(8,128)(2,1)S(1)}, bf16[512,896]{1,0:T(8,128)(2,1)S(1)}) custom-call(s32[8]{0:T(128)S(1)} %stack.71.place_ref, s32[8]{0:T(128)S(1)} %stack.80.slot_ref, bf16[4,64,896]{2,1,0:T(8,128)(2,1)S(1)} %get-tuple-element.35.refs_0_, ...), custom_call_target="tpu_custom_call" | custom-call | tf_op jit(solution)/shard_map/density/pallas_call | solution.py:156
  73.9 1.7 %collective-permute-done.17.m_ref = bf16[512,1024]{1,0:T(8,128)(2,1)S(1)} collective-permute-done((bf16[512,1024]{1,0:T(8,128)(2,1)S(1)}, bf16[512,1024]{1,0:T(8,128)(2,1)S(1)}, u32[]{:S(2)}, u32[]{:S(2)}) %collective-permute-start.17) | collective-permute-done | bytes 1048608 | tf_op jit(solution)/shard_map/ppermute | solution.py:40
  75.6 4.0 %project.1 = bf16[32,16,896]{2,1,0:T(8,128)(2,1)S(1)} custom-call(bf16[512,1024]{1,0:T(8,128)(2,1)S(1)} %collective-permute-done.17.m_ref, bf16[432,1024]{1,0:T(8,128)(2,1)S(1)} %get-tuple-element.57.left_ref, bf16[1024,896]{1,0:T(8,128)(2,1)S(1)} %get-tuple-element.58.right_ref), custom_call_target="tpu_custom_call" | custom-call | tf_op jit(solution)/shard_map/project/pallas_call | solution.py:255
  79.5 18.7 %all_to_all.15 = bf16[16,4,8,896]{3,2,1,0:T(8,128)(2,1)S(1)} all-to-all(bf16[16,4,8,896]{3,2,1,0:T(8,128)(2,1)S(1)} %bitcast.22), channel_id=1, replica_groups={{0,1,8,9,16,17,24,25,32,33,40,41,48,49,56,57},{2,3,10,11,18,19,26,27,34..., dimensions={0} | all-to-all | bytes 1835008 | tf_op jit(solution)/shard_map/all_to_all | solution.py:296
  99.0 7.6 %all-to-all-start.2 = ((f32[4,8,896]{2,1,0:T(8,128)}), f32[4,8,896]{2,1,0:T(8,128)S(1)}, u32[]{:S(2)}, u32[]{:S(2)}) async-start(f32[4,8,896]{2,1,0:T(8,128)} %convert_reduce_fusion), calls=%async_computation.2 | async-start | bytes 229376 | tf_op jit(solution)/shard_map/all_to_all | solution.py:298
  106.5 8.9 %all-to-all-done.2 = f32[4,8,896]{2,1,0:T(8,128)S(1)} async-done(((f32[4,8,896]{2,1,0:T(8,128)}), f32[4,8,896]{2,1,0:T(8,128)S(1)}, u32[]{:S(2)}, u32[]{:S(2)}) %all-to-all-start.2) | async-done | bytes 114720 | tf_op jit(solution)/shard_map/all_to_all | solution.py:298
  (67 shorter events, 11.6 us)
Async XLA Ops:
  1.0 9.3 %collective-permute-start.2 = (bf16[64,896]{1,0:T(8,128)(2,1)S(1)}, bf16[64,896]{1,0:T(8,128)(2,1)S(1)}, u32[]{:S(2)}, u32[]{:S(2)}) collective-permute-start(bf16[64,896]{1,0:T(8,128)(2,1)S(1)} %lay.1.own_ref), channel_id=1, source_target_pairs={{0,128},{64,192},{128,0},{192,64},{1,129},{65,193},{129,1},{193,65... | collective-permute-start | bytes 344072 | tf_op jit(solution)/shard_map/ppermute | solution.py:40
  2.4 7.8 %collective-permute-start.3 = (bf16[64,896]{1,0:T(8,128)(2,1)S(1)}, bf16[64,896]{1,0:T(8,128)(2,1)S(1)}, u32[]{:S(2)}, u32[]{:S(2)}) collective-permute-start(bf16[64,896]{1,0:T(8,128)(2,1)S(1)} %lay.1.own_ref), channel_id=1, source_target_pairs={{0,8},{1,9},{2,10},{3,11},{4,12},{5,13},{6,14},{7,15},{8,0},{9,1},... | collective-permute-start | bytes 344072 | tf_op jit(solution)/shard_map/ppermute | solution.py:36
  4.1 6.2 %collective-permute-start.4 = (bf16[64,896]{1,0:T(8,128)(2,1)S(1)}, bf16[64,896]{1,0:T(8,128)(2,1)S(1)}, u32[]{:S(2)}, u32[]{:S(2)}) collective-permute-start(bf16[64,896]{1,0:T(8,128)(2,1)S(1)} %lay.1.own_ref), channel_id=1, source_target_pairs={{128,8},{129,9},{130,10},{131,11},{132,12},{133,13},{134,14},{135,... | collective-permute-start | bytes 344072 | tf_op jit(solution)/shard_map/ppermute | solution.py:46
  5.1 1.4 %collective-permute-start = (s32[1]{0:T(128)}, s32[1]{0:T(128)}, u32[]{:S(2)}, u32[]{:S(2)}) collective-permute-start(s32[1]{0:T(128)} %param.6), channel_id=1, source_target_pairs={{0,64},{64,0},{128,192},{192,128},{1,65},{65,1},{129,193},{193,129... | collective-permute-start | bytes 20 | tf_op jit(solution)/shard_map/ppermute | solution.py:40
  5.1 5.1 %collective-permute-start.1 = (s32[1]{0:T(128)}, s32[1]{0:T(128)}, u32[]{:S(2)}, u32[]{:S(2)}) collective-permute-start(s32[1]{0:T(128)} %param.6), channel_id=1, source_target_pairs={{0,128},{64,192},{128,0},{192,64},{1,129},{65,193},{129,1},{193,65... | collective-permute-start | bytes 20 | tf_op jit(solution)/shard_map/ppermute | solution.py:40
  10.3 15.2 %copy-start = (bf16[2,64,896]{2,1,0:T(8,128)(2,1)}, bf16[2,64,896]{2,1,0:T(8,128)(2,1)S(1)}, u32[]{:S(2)}) copy-start(bf16[2,64,896]{2,1,0:T(8,128)(2,1)S(1)} %get-tuple-element.44.refs_5_) | copy-start | bytes 688132
  10.3 15.2 %collective-permute-start.5 = (bf16[4,64,896]{2,1,0:T(8,128)(2,1)S(1)}, bf16[4,64,896]{2,1,0:T(8,128)(2,1)S(1)}, u32[]{:S(2)}, u32[]{:S(2)}) collective-permute-start(bf16[4,64,896]{2,1,0:T(8,128)(2,1)S(1)} %get-tuple-element.35.refs_0_), channel_id=1, source_target_pairs={{0,16},{1,17},{2,18},{3,19},{4,20},{5,21},{6,22},{7,23},{8,24},{9,... | collective-permute-start | bytes 1376264 | tf_op jit(solution)/shard_map/ppermute | solution.py:36
  12.0 13.5 %collective-permute-start.6 = (bf16[4,64,896]{2,1,0:T(8,128)(2,1)S(1)}, bf16[4,64,896]{2,1,0:T(8,128)(2,1)S(1)}, u32[]{:S(2)}, u32[]{:S(2)}) collective-permute-start(bf16[4,64,896]{2,1,0:T(8,128)(2,1)S(1)} %get-tuple-element.35.refs_0_), channel_id=1, source_target_pairs={{0,48},{1,49},{2,50},{3,51},{4,52},{5,53},{6,54},{7,55},{8,56},{9,... | collective-permute-start | bytes 1376264 | tf_op jit(solution)/shard_map/ppermute | solution.py:36
  13.7 11.8 %collective-permute-start.7 = (bf16[2,64,896]{2,1,0:T(8,128)(2,1)S(1)}, bf16[2,64,896]{2,1,0:T(8,128)(2,1)S(1)}, u32[]{:S(2)}, u32[]{:S(2)}) collective-permute-start(bf16[2,64,896]{2,1,0:T(8,128)(2,1)S(1)} %get-tuple-element.44.refs_5_), channel_id=1, source_target_pairs={{0,1},{1,2},{2,3},{3,4},{4,5},{5,6},{6,7},{7,0},{8,9},{9,10},{10,1... | collective-permute-start | bytes 688136 | tf_op jit(solution)/shard_map/ppermute | solution.py:36
  15.6 9.9 %collective-permute-start.8 = (bf16[2,64,896]{2,1,0:T(8,128)(2,1)S(1)}, bf16[2,64,896]{2,1,0:T(8,128)(2,1)}, u32[]{:S(2)}, u32[]{:S(2)}) collective-permute-start(bf16[2,64,896]{2,1,0:T(8,128)(2,1)S(1)} %get-tuple-element.44.refs_5_), channel_id=1, source_target_pairs={{0,7},{1,0},{2,1},{3,2},{4,3},{5,4},{6,5},{7,6},{8,15},{9,8},{10,9... | collective-permute-start | bytes 688136 | tf_op jit(solution)/shard_map/ppermute | solution.py:36
  25.5 16.6 %copy-start.2 = (bf16[2,64,896]{2,1,0:T(8,128)(2,1)}, bf16[2,64,896]{2,1,0:T(8,128)(2,1)S(1)}, u32[]{:S(2)}) copy-start(bf16[2,64,896]{2,1,0:T(8,128)(2,1)S(1)} %collective-permute-done.7.refs_6_) | copy-start | bytes 688132
  25.5 30.5 %all-to-all-start = ((bf16[8,3,64,512]{3,2,1,0:T(8,128)(2,1)}), bf16[8,3,64,512]{3,2,1,0:T(8,128)(2,1)S(1)}, u32[]{:S(2)}, u32[]{:S(2)}) async-start(bf16[8,3,64,512]{3,2,1,0:T(8,128)(2,1)} %pack.1), calls=%async_computation | async-start | bytes 3145728 | tf_op jit(solution)/shard_map/all_to_all | solution.py:328
  30.3 9.0 %collective-permute-start.11 = (bf16[2,64,896]{2,1,0:T(8,128)(2,1)S(1)}, bf16[2,64,896]{2,1,0:T(8,128)(2,1)S(1)}, u32[]{:S(2)}, u32[]{:S(2)}) collective-permute-start(bf16[2,64,896]{2,1,0:T(8,128)(2,1)S(1)} %collective-permute-done.7.refs_6_), channel_id=1, source_target_pairs={{0,1},{1,2},{2,3},{3,4},{4,5},{5,6},{6,7},{7,0},{8,9},{9,10},{10,1... | collective-permute-start | bytes 688136 | tf_op jit(solution)/shard_map/ppermute | solution.py:36
  31.3 10.8 %collective-permute-start.12 = (bf16[2,64,896]{2,1,0:T(8,128)(2,1)}, bf16[2,64,896]{2,1,0:T(8,128)(2,1)S(1)}, u32[]{:S(2)}, u32[]{:S(2)}) collective-permute-start(bf16[2,64,896]{2,1,0:T(8,128)(2,1)} %collective-permute-done.8.refs_7_), channel_id=1, source_target_pairs={{0,7},{1,0},{2,1},{3,2},{4,3},{5,4},{6,5},{7,6},{8,15},{9,8},{10,9... | collective-permute-start | bytes 688136 | tf_op jit(solution)/shard_map/ppermute | solution.py:36
  39.3 16.8 %copy-start.4 = (bf16[2,64,896]{2,1,0:T(8,128)(2,1)}, bf16[2,64,896]{2,1,0:T(8,128)(2,1)S(1)}, u32[]{:S(2)}) copy-start(bf16[2,64,896]{2,1,0:T(8,128)(2,1)S(1)} %collective-permute-done.11.refs_8_) | copy-start | bytes 688132
  39.3 7.2 %collective-permute-start.13 = (bf16[2,64,896]{2,1,0:T(8,128)(2,1)S(1)}, bf16[2,64,896]{2,1,0:T(8,128)(2,1)S(1)}, u32[]{:S(2)}, u32[]{:S(2)}) collective-permute-start(bf16[2,64,896]{2,1,0:T(8,128)(2,1)S(1)} %collective-permute-done.11.refs_8_), channel_id=1, source_target_pairs={{0,1},{1,2},{2,3},{3,4},{4,5},{5,6},{6,7},{7,0},{8,9},{9,10},{10,1... | collective-permute-start | bytes 688136 | tf_op jit(solution)/shard_map/ppermute | solution.py:36
  39.3 13.4 %collective-permute-start.10 = (bf16[2,64,896]{2,1,0:T(8,128)(2,1)S(1)}, bf16[2,64,896]{2,1,0:T(8,128)(2,1)S(1)}, u32[]{:S(2)}, u32[]{:S(2)}) collective-permute-start(bf16[2,64,896]{2,1,0:T(8,128)(2,1)S(1)} %slice.22), channel_id=1, source_target_pairs={{0,48},{1,49},{2,50},{3,51},{4,52},{5,53},{6,54},{7,55},{8,56},{9,... | collective-permute-start | bytes 688136 | tf_op jit(solution)/shard_map/ppermute | solution.py:36
  42.1 11.9 %collective-permute-start.9 = (bf16[2,64,896]{2,1,0:T(8,128)(2,1)S(1)}, bf16[2,64,896]{2,1,0:T(8,128)(2,1)S(1)}, u32[]{:S(2)}, u32[]{:S(2)}) collective-permute-start(bf16[2,64,896]{2,1,0:T(8,128)(2,1)S(1)} %slice.21), channel_id=1, source_target_pairs={{0,16},{1,17},{2,18},{3,19},{4,20},{5,21},{6,22},{7,23},{8,24},{9,... | collective-permute-start | bytes 688136 | tf_op jit(solution)/shard_map/ppermute | solution.py:36
  42.2 12.5 %collective-permute-start.14 = (bf16[2,64,896]{2,1,0:T(8,128)(2,1)S(1)}, bf16[2,64,896]{2,1,0:T(8,128)(2,1)S(1)}, u32[]{:S(2)}, u32[]{:S(2)}) collective-permute-start(bf16[2,64,896]{2,1,0:T(8,128)(2,1)S(1)} %collective-permute-done.12.refs_9_), channel_id=1, source_target_pairs={{0,7},{1,0},{2,1},{3,2},{4,3},{5,4},{6,5},{7,6},{8,15},{9,8},{10,9... | collective-permute-start | bytes 688136 | tf_op jit(solution)/shard_map/ppermute | solution.py:36
  46.5 8.9 %collective-permute-start.15 = (bf16[2,64,896]{2,1,0:T(8,128)(2,1)S(1)}, bf16[2,64,896]{2,1,0:T(8,128)(2,1)S(1)}, u32[]{:S(2)}, u32[]{:S(2)}) collective-permute-start(bf16[2,64,896]{2,1,0:T(8,128)(2,1)S(1)} %collective-permute-done.13.refs_10_), channel_id=1, source_target_pairs={{0,1},{1,2},{2,3},{3,4},{4,5},{5,6},{6,7},{7,0},{8,9},{9,10},{10,1... | collective-permute-start | bytes 688136 | tf_op jit(solution)/shard_map/ppermute | solution.py:36
  56.9 15.0 %collective-permute-start.16 = (bf16[8,64,512]{2,1,0:T(8,128)(2,1)}, bf16[8,64,512]{2,1,0:T(8,128)(2,1)S(1)}, u32[]{:S(2)}, u32[]{:S(2)}) collective-permute-start(bf16[8,64,512]{2,1,0:T(8,128)(2,1)} %slice_bitcast_fusion), channel_id=1, source_target_pairs={{0,64},{64,0},{128,192},{192,128},{1,65},{65,1},{129,193},{193,129... | collective-permute-start | bytes 1572872 | tf_op jit(solution)/shard_map/ppermute | solution.py:40
  57.0 0.9 copy-start.1
  58.0 0.9 copy-start.3
  58.9 0.9 copy-start.5
  59.9 0.9 copy-start.7
  60.8 0.9 copy-start.9
  61.7 0.9 copy-start.11
  62.7 0.9 copy-start.13
  63.6 0.9 copy-start.15
  64.6 0.9 copy-start.17
  72.7 2.9 %collective-permute-start.17 = (bf16[512,1024]{1,0:T(8,128)(2,1)S(1)}, bf16[512,1024]{1,0:T(8,128)(2,1)S(1)}, u32[]{:S(2)}, u32[]{:S(2)}) collective-permute-start(bf16[512,1024]{1,0:T(8,128)(2,1)S(1)} %mix.1), channel_id=1, source_target_pairs={{0,64},{64,0},{128,192},{192,128},{1,65},{65,1},{129,193},{193,129... | collective-permute-start | bytes 3145736 | tf_op jit(solution)/shard_map/ppermute | solution.py:40
  99.0 16.5 %all-to-all-start.2 = ((f32[4,8,896]{2,1,0:T(8,128)}), f32[4,8,896]{2,1,0:T(8,128)S(1)}, u32[]{:S(2)}, u32[]{:S(2)}) async-start(f32[4,8,896]{2,1,0:T(8,128)} %convert_reduce_fusion), calls=%async_computation.2 | async-start | bytes 229376 | tf_op jit(solution)/shard_map/all_to_all | solution.py:298
  (7 other events, 4.8 us)

commit v27 on v25

--- a/solution.py
+++ b/solution.py
@@ -133,13 +133,13 @@
     for side, piece in enumerate((over_here, over_side)):
         moves.append((piece.at[0], row_ref.at[row_at(2, side), :]))
         moves.append((piece.at[1], other_rows.at[row_at(2, side), :]))
-    copies = [pltpu.make_async_copy(*move, sem.at[i]) for i, move in enumerate(moves)]
-    for copy in copies:
-        copy.start()
     for dy, piece in ((0, four_ref), (1, up_ref), (3, down_ref)):
         for side in range(NX):
-            row_ref[row_at(dy, side), :] = piece[2 * side]
-            other_rows[row_at(dy, side), :] = piece[2 * side + 1]
+            moves.append((piece.at[2 * side], row_ref.at[row_at(dy, side), :]))
+            moves.append((piece.at[2 * side + 1], other_rows.at[row_at(dy, side), :]))
+    copies = [pltpu.make_async_copy(*move, sem.at[i]) for i, move in enumerate(moves)]
+    for copy in copies:
+        copy.start()
     for copy in copies:
         copy.wait()
     for rows, columns, out in ((row_ref, col_ref, own_ref), (other_rows, other_cols, far_ref)):
@@ -152,26 +152,26 @@
     product = pltpu.VMEM((BLOCK, 2 * BLOCK), jnp.float32)
     points = pltpu.VMEM((BLOCK, LANES), jnp.bfloat16)
     in_hbm = pl.BlockSpec(memory_space=pltpu.HBM)
-    specs = [IN_VMEM] * 2 + [in_hbm] * 2 + [IN_VMEM] + [in_hbm] * NZ
-    arrays = [near(four), near(up), *map(away, over), near(down), *map(away, cols)]
+    specs = [in_hbm] * (5 + NZ)
+    arrays = map(away, (four, up, *over, down, *cols))
     return pl.pallas_call(
         density_body,
         out_shape=[product, product, points, points],
         in_specs=[IN_SMEM] * 2 + specs,
         out_specs=[IN_VMEM] * 4,
         scratch_shapes=[pltpu.VMEM((BLOCK, LANES), jnp.bfloat16)] * 2
-        + [pltpu.SemaphoreType.DMA((2 * NX + 2 * NZ,))],
+        + [pltpu.SemaphoreType.DMA((2 * NX * NY + 2 * NZ,))],
         compiler_params=PARAMS,
         name="density",
     )(place, slots, *arrays)
 
 
-def mix_body(odd_ref, own_ref, far_ref, half_ref, kern_ref, m_ref):
+def mix_body(odd_ref, own_ref, far_ref, core_ref, kern_ref, m_ref):
     odd = odd_ref[0] == 1
     sign = jnp.where(odd, -1.0, 1.0).astype(jnp.float32)
     for i in range(GROUPS):
         at = pl.ds(i * SLAB, SLAB)
-        mine, other = kern_ref[i, 0], half_ref[i]
+        mine, other = kern_ref[i, 0], core_ref[i, 0]
         k_re = jnp.where(odd, other, mine).astype(jnp.float32)
         k_im = jnp.where(odd, mine, other).astype(jnp.float32) * sign
         p_re, p_im = own_ref[at, :BLOCK], own_ref[at, BLOCK:]
@@ -333,12 +333,12 @@
         cols += [ahead, behind]
     cols.append(shift(ahead, 0, 0, 1))
     kern, over, cols = lax.optimization_barrier((kern, over, cols))
-    half = swap_groups(kern[:, 0], 1)
+    kern_core = swap_groups(kern, 1)
 
     place = jnp.stack([(y - dy) % NY * NX + (x - dx) % NX for dy in range(NY) for dx in range(NX)])
     slots = jnp.stack([(z + i) % NZ for i in (0, -1, 1, -2, 2, -3, 3, -4)])
     p_own, p_far, rows, cols = density(place, slots, four, up, over, down, cols)
-    m_own = swap_groups(mix(odd, p_own, p_far, half, kern), 1)
+    m_own = swap_groups(mix(odd, p_own, p_far, kern_core, kern), 1)
     left, right = prepare(rows, cols)
     total = reduce_windows(project(m_own, left, right))
     flat = total.reshape(2, 8 * NB)

time: 105 us -> 106 us (level)
    unnamed x18 -> x28, local copies, waits for them, and re-layouts: 2 us -> 2.73 us
  transfers between devices with their start and end apart: 20 -> 20, of which waited for: 7 -> 7; matrix products, arithmetic and copies ran while one was open for 0% -> 0% of each run, Pallas kernels for 9% -> 10%
where the time goes in v27:
time: 106 us; the launch traced here: 105 us
  starting transfers between devices  38.5 us (36%)
  waiting for transfers between devices  26.9 us (25%)
  blocking collectives  17.9 us (17%)
  Pallas kernels  16.3 us (15%)
  local copies, waits for them, and re-layouts  3.2 us (3%)
  other arithmetic  1.51 us (1%)
    ppermute x12, starting transfers between devices, shift(): return lax.ppermute(block, 'band', band_route(dy, dx, dz))  21.8 us
    all_to_all x1, blocking collectives, reduce_windows(): parts = lax.all_to_all(parts, 'band', 0, 0, axis_index_groups=wide)  17.9 us
    ppermute x12, waiting for transfers between devices, shift(): return lax.ppermute(block, 'band', band_route(dy, dx, dz))  12.4 us
    all_to_all x1, waiting for transfers between devices, reduce_windows(): lax.all_to_all(parts, 'band', 0, 0, axis_index_groups=deep)  8.91 us
    all_to_all x1, starting transfers between devices, reduce_windows(): lax.all_to_all(parts, 'band', 0, 0, axis_index_groups=deep)  7.53 us
    ppermute x5, waiting for transfers between devices, swap_groups(): return lax.ppermute(block, 'kgrp', [(k, k ^ bit) for k in range(4)])  5.6 us
    pallas_call x1, Pallas kernels, density(): pl.pallas_call(density_body, out_shape=[product, product, points, points]...  5.3 us
    all_to_all x1, starting transfers between devices, on_device(): kern = lax.all_to_all(sends, 'band', 0, 0, axis_index_groups=over_yx)  4.73 us
  transfers between devices with their start and end apart: 20, of which 7 were waited for; matrix products, arithmetic and copies ran while one was open for 0% of the time, Pallas kernels for 10%

profile of v27, /device:TPU:6, one launch (start us, length us, event | category | flops | bytes accessed | tf_op | source)
XLA Modules:
  0.0 105.2 jit_solution(7175107507501916228)
XLA Ops:
  0.0 1.0 lay.1.own_ref
  1.0 1.4 %collective-permute-start.2 = (bf16[64,896]{1,0:T(8,128)(2,1)S(1)}, bf16[64,896]{1,0:T(8,128)(2,1)S(1)}, u32[]{:S(2)}, u32[]{:S(2)}) collective-permute-start(bf16[64,896]{1,0:T(8,128)(2,1)S(1)} %lay.1.own_ref), channel_id=1, source_target_pairs={{0,128},{64,192},{128,0},{192,64},{1,129},{65,193},{129,1},{193,65... | collective-permute-start | bytes 344072 | tf_op jit(solution)/shard_map/ppermute | solution.py:40
  2.4 1.7 %collective-permute-start.3 = (bf16[64,896]{1,0:T(8,128)(2,1)S(1)}, bf16[64,896]{1,0:T(8,128)(2,1)S(1)}, u32[]{:S(2)}, u32[]{:S(2)}) collective-permute-start(bf16[64,896]{1,0:T(8,128)(2,1)S(1)} %lay.1.own_ref), channel_id=1, source_target_pairs={{0,8},{1,9},{2,10},{3,11},{4,12},{5,13},{6,14},{7,15},{8,0},{9,1},... | collective-permute-start | bytes 344072 | tf_op jit(solution)/shard_map/ppermute | solution.py:36
  4.1 1.0 collective-permute-start.4
  5.1 1.4 %collective-permute-start.1 = (s32[1]{0:T(128)}, s32[1]{0:T(128)}, u32[]{:S(2)}, u32[]{:S(2)}) collective-permute-start(s32[1]{0:T(128)} %param.6), channel_id=1, source_target_pairs={{0,128},{64,192},{128,0},{192,64},{1,129},{65,193},{129,1},{193,65... | collective-permute-start | bytes 20 | tf_op jit(solution)/shard_map/ppermute | solution.py:40
  6.5 3.9 %collective-permute-done.1.far_ref = s32[1]{0:T(128)} collective-permute-done((s32[1]{0:T(128)}, s32[1]{0:T(128)}, u32[]{:S(2)}, u32[]{:S(2)}) %collective-permute-start.1) | collective-permute-done | bytes 36 | tf_op jit(solution)/shard_map/ppermute | solution.py:40
  10.5 1.7 %collective-permute-start.5 = (bf16[4,64,896]{2,1,0:T(8,128)(2,1)S(1)}, bf16[4,64,896]{2,1,0:T(8,128)(2,1)S(1)}, u32[]{:S(2)}, u32[]{:S(2)}) collective-permute-start(bf16[4,64,896]{2,1,0:T(8,128)(2,1)S(1)} %get-tuple-element.35.refs_0_), channel_id=1, source_target_pairs={{0,16},{1,17},{2,18},{3,19},{4,20},{5,21},{6,22},{7,23},{8,24},{9,... | collective-permute-start | bytes 1376264 | tf_op jit(solution)/shard_map/ppermute | solution.py:36
  12.2 1.7 %collective-permute-start.6 = (bf16[4,64,896]{2,1,0:T(8,128)(2,1)S(1)}, bf16[4,64,896]{2,1,0:T(8,128)(2,1)S(1)}, u32[]{:S(2)}, u32[]{:S(2)}) collective-permute-start(bf16[4,64,896]{2,1,0:T(8,128)(2,1)S(1)} %get-tuple-element.35.refs_0_), channel_id=1, source_target_pairs={{0,48},{1,49},{2,50},{3,51},{4,52},{5,53},{6,54},{7,55},{8,56},{9,... | collective-permute-start | bytes 1376264 | tf_op jit(solution)/shard_map/ppermute | solution.py:36
  13.8 1.9 %collective-permute-start.7 = (bf16[2,64,896]{2,1,0:T(8,128)(2,1)S(1)}, bf16[2,64,896]{2,1,0:T(8,128)(2,1)S(1)}, u32[]{:S(2)}, u32[]{:S(2)}) collective-permute-start(bf16[2,64,896]{2,1,0:T(8,128)(2,1)S(1)} %get-tuple-element.44.refs_5_), channel_id=1, source_target_pairs={{0,1},{1,2},{2,3},{3,4},{4,5},{5,6},{6,7},{7,0},{8,9},{9,10},{10,1... | collective-permute-start | bytes 688136 | tf_op jit(solution)/shard_map/ppermute | solution.py:36
  15.7 3.9 %collective-permute-start.8 = (bf16[2,64,896]{2,1,0:T(8,128)(2,1)S(1)}, bf16[2,64,896]{2,1,0:T(8,128)(2,1)S(1)}, u32[]{:S(2)}, u32[]{:S(2)}) collective-permute-start(bf16[2,64,896]{2,1,0:T(8,128)(2,1)S(1)} %get-tuple-element.44.refs_5_), channel_id=1, source_target_pairs={{0,7},{1,0},{2,1},{3,2},{4,3},{5,4},{6,5},{7,6},{8,15},{9,8},{10,9... | collective-permute-start | bytes 688136 | tf_op jit(solution)/shard_map/ppermute | solution.py:36
  21.0 4.5 %pack.1 = bf16[8,3,64,512]{3,2,1,0:T(8,128)(2,1)} custom-call(s32[1]{0:T(128)} %bitcast.odd_ref, s32[1]{0:T(128)S(6)} %copy.5.own_ref, s32[1]{0:T(128)} %collective-permute-done.core_ref, s32[1]{0:T(128)} %collective-permute-done.1.far_ref, s32[8]{0:T(128)S(1)} %copy-done.2, bf16[4,2,64,4096]{3,2,1,0:T(8,128)(2,1)} %kernels_ref.1), custom_call_target="tpu_custom_call" | custom-call | tf_op jit(solution)/shard_map/pack/pallas_call | solution.py:109
  25.6 4.7 %all-to-all-start = ((bf16[8,3,64,512]{3,2,1,0:T(8,128)(2,1)}), bf16[8,3,64,512]{3,2,1,0:T(8,128)(2,1)S(1)}, u32[]{:S(2)}, u32[]{:S(2)}) async-start(bf16[8,3,64,512]{3,2,1,0:T(8,128)(2,1)} %pack.1), calls=%async_computation | async-start | bytes 3145728 | tf_op jit(solution)/shard_map/all_to_all | solution.py:329
  30.3 0.9 collective-permute-start.11
  31.2 3.9 %collective-permute-start.12 = (bf16[2,64,896]{2,1,0:T(8,128)(2,1)S(1)}, bf16[2,64,896]{2,1,0:T(8,128)(2,1)S(1)}, u32[]{:S(2)}, u32[]{:S(2)}) collective-permute-start(bf16[2,64,896]{2,1,0:T(8,128)(2,1)S(1)} %collective-permute-done.8.refs_7_), channel_id=1, source_target_pairs={{0,7},{1,0},{2,1},{3,2},{4,3},{5,4},{6,5},{7,6},{8,15},{9,8},{10,9... | collective-permute-start | bytes 688136 | tf_op jit(solution)/shard_map/ppermute | solution.py:36
  35.1 4.0 %collective-permute-done.11.refs_8_ = bf16[2,64,896]{2,1,0:T(8,128)(2,1)S(1)} collective-permute-done((bf16[2,64,896]{2,1,0:T(8,128)(2,1)S(1)}, bf16[2,64,896]{2,1,0:T(8,128)(2,1)S(1)}, u32[]{:S(2)}, u32[]{:S(2)}) %collective-permute-start.11) | collective-permute-done | bytes 229408 | tf_op jit(solution)/shard_map/ppermute | solution.py:36
  39.2 2.8 %collective-permute-start.10 = (bf16[2,64,896]{2,1,0:T(8,128)(2,1)S(1)}, bf16[2,64,896]{2,1,0:T(8,128)(2,1)S(1)}, u32[]{:S(2)}, u32[]{:S(2)}) collective-permute-start(bf16[2,64,896]{2,1,0:T(8,128)(2,1)S(1)} %slice.19), channel_id=1, source_target_pairs={{0,48},{1,49},{2,50},{3,51},{4,52},{5,53},{6,54},{7,55},{8,56},{9,... | collective-permute-start | bytes 688136 | tf_op jit(solution)/shard_map/ppermute | solution.py:36
  42.1 3.3 %collective-permute-start.14 = (bf16[2,64,896]{2,1,0:T(8,128)(2,1)S(1)}, bf16[2,64,896]{2,1,0:T(8,128)(2,1)S(1)}, u32[]{:S(2)}, u32[]{:S(2)}) collective-permute-start(bf16[2,64,896]{2,1,0:T(8,128)(2,1)S(1)} %collective-permute-done.12.refs_9_), channel_id=1, source_target_pairs={{0,7},{1,0},{2,1},{3,2},{4,3},{5,4},{6,5},{7,6},{8,15},{9,8},{10,9... | collective-permute-start | bytes 688136 | tf_op jit(solution)/shard_map/ppermute | solution.py:36
  45.4 1.0 collective-permute-done.13.refs_10_
  46.4 6.1 %collective-permute-done.10.refs_3_ = bf16[2,64,896]{2,1,0:T(8,128)(2,1)S(1)} collective-permute-done((bf16[2,64,896]{2,1,0:T(8,128)(2,1)S(1)}, bf16[2,64,896]{2,1,0:T(8,128)(2,1)S(1)}, u32[]{:S(2)}, u32[]{:S(2)}) %collective-permute-start.10) | collective-permute-done | bytes 229408 | tf_op jit(solution)/shard_map/ppermute | solution.py:36
  52.5 1.3 %collective-permute-done.9.refs_2_ = bf16[2,64,896]{2,1,0:T(8,128)(2,1)S(1)} collective-permute-done((bf16[2,64,896]{2,1,0:T(8,128)(2,1)S(1)}, bf16[2,64,896]{2,1,0:T(8,128)(2,1)S(1)}, u32[]{:S(2)}, u32[]{:S(2)}) %collective-permute-start.9) | collective-permute-done | bytes 229408 | tf_op jit(solution)/shard_map/ppermute | solution.py:36
  53.8 0.7 copy-done.11
  54.4 0.7 copy-done.12
  55.1 0.7 copy-done.13
  56.0 5.3 %density.1 = (f32[512,1024]{1,0:T(8,128)S(1)}, f32[512,1024]{1,0:T(8,128)S(1)}, bf16[512,896]{1,0:T(8,128)(2,1)S(1)}, bf16[512,896]{1,0:T(8,128)(2,1)S(1)}) custom-call(s32[8]{0:T(128)S(1)} %stack.71.place_ref, s32[8]{0:T(128)S(1)} %stack.80.slot_ref, bf16[4,64,896]{2,1,0:T(8,128)(2,1)} %copy-done, bf16[4,64,896]{2,1,0:T(8,128)(2,1)} %copy-done.3, ...), custom_call_target="tpu_custom_call" | custom-call | tf_op jit(solution)/shard_map/density/pallas_call | solution.py:157
  61.3 0.9 mix.1
  63.4 1.7 %collective-permute-done.17.m_ref = bf16[512,1024]{1,0:T(8,128)(2,1)S(1)} collective-permute-done((bf16[512,1024]{1,0:T(8,128)(2,1)S(1)}, bf16[512,1024]{1,0:T(8,128)(2,1)S(1)}, u32[]{:S(2)}, u32[]{:S(2)}) %collective-permute-start.17) | collective-permute-done | bytes 1048608 | tf_op jit(solution)/shard_map/ppermute | solution.py:40
  65.1 4.0 %project.1 = bf16[32,16,896]{2,1,0:T(8,128)(2,1)S(1)} custom-call(bf16[512,1024]{1,0:T(8,128)(2,1)S(1)} %collective-permute-done.17.m_ref, bf16[432,1024]{1,0:T(8,128)(2,1)S(1)} %get-tuple-element.57.left_ref, bf16[1024,896]{1,0:T(8,128)(2,1)S(1)} %get-tuple-element.58.right_ref), custom_call_target="tpu_custom_call" | custom-call | tf_op jit(solution)/shard_map/project/pallas_call | solution.py:256
  69.1 17.9 %all_to_all.15 = bf16[16,4,8,896]{3,2,1,0:T(8,128)(2,1)S(1)} all-to-all(bf16[16,4,8,896]{3,2,1,0:T(8,128)(2,1)S(1)} %bitcast.20), channel_id=1, replica_groups={{0,1,8,9,16,17,24,25,32,33,40,41,48,49,56,57},{2,3,10,11,18,19,26,27,34..., dimensions={0} | all-to-all | bytes 1835008 | tf_op jit(solution)/shard_map/all_to_all | solution.py:297
  87.0 0.8 convert_reduce_fusion
  87.7 7.5 %all-to-all-start.2 = ((f32[4,8,896]{2,1,0:T(8,128)}), f32[4,8,896]{2,1,0:T(8,128)S(1)}, u32[]{:S(2)}, u32[]{:S(2)}) async-start(f32[4,8,896]{2,1,0:T(8,128)} %convert_reduce_fusion), calls=%async_computation.2 | async-start | bytes 229376 | tf_op jit(solution)/shard_map/all_to_all | solution.py:299
  95.3 8.9 %all-to-all-done.2 = f32[4,8,896]{2,1,0:T(8,128)S(1)} async-done(((f32[4,8,896]{2,1,0:T(8,128)}), f32[4,8,896]{2,1,0:T(8,128)S(1)}, u32[]{:S(2)}, u32[]{:S(2)}) %all-to-all-start.2) | async-done | bytes 114720 | tf_op jit(solution)/shard_map/all_to_all | solution.py:299
  104.5 0.7 fusion.1
  (56 shorter events, 2.5 us)
Async XLA Ops:
  1.0 9.4 %collective-permute-start.2 = (bf16[64,896]{1,0:T(8,128)(2,1)S(1)}, bf16[64,896]{1,0:T(8,128)(2,1)S(1)}, u32[]{:S(2)}, u32[]{:S(2)}) collective-permute-start(bf16[64,896]{1,0:T(8,128)(2,1)S(1)} %lay.1.own_ref), channel_id=1, source_target_pairs={{0,128},{64,192},{128,0},{192,64},{1,129},{65,193},{129,1},{193,65... | collective-permute-start | bytes 344072 | tf_op jit(solution)/shard_map/ppermute | solution.py:40
  2.4 8.0 %collective-permute-start.3 = (bf16[64,896]{1,0:T(8,128)(2,1)S(1)}, bf16[64,896]{1,0:T(8,128)(2,1)S(1)}, u32[]{:S(2)}, u32[]{:S(2)}) collective-permute-start(bf16[64,896]{1,0:T(8,128)(2,1)S(1)} %lay.1.own_ref), channel_id=1, source_target_pairs={{0,8},{1,9},{2,10},{3,11},{4,12},{5,13},{6,14},{7,15},{8,0},{9,1},... | collective-permute-start | bytes 344072 | tf_op jit(solution)/shard_map/ppermute | solution.py:36
  4.1 6.3 %collective-permute-start.4 = (bf16[64,896]{1,0:T(8,128)(2,1)S(1)}, bf16[64,896]{1,0:T(8,128)(2,1)S(1)}, u32[]{:S(2)}, u32[]{:S(2)}) collective-permute-start(bf16[64,896]{1,0:T(8,128)(2,1)S(1)} %lay.1.own_ref), channel_id=1, source_target_pairs={{128,8},{129,9},{130,10},{131,11},{132,12},{133,13},{134,14},{135,... | collective-permute-start | bytes 344072 | tf_op jit(solution)/shard_map/ppermute | solution.py:46
  5.1 1.4 %collective-permute-start = (s32[1]{0:T(128)}, s32[1]{0:T(128)}, u32[]{:S(2)}, u32[]{:S(2)}) collective-permute-start(s32[1]{0:T(128)} %param.6), channel_id=1, source_target_pairs={{0,64},{64,0},{128,192},{192,128},{1,65},{65,1},{129,193},{193,129... | collective-permute-start | bytes 20 | tf_op jit(solution)/shard_map/ppermute | solution.py:40
  5.1 5.3 %collective-permute-start.1 = (s32[1]{0:T(128)}, s32[1]{0:T(128)}, u32[]{:S(2)}, u32[]{:S(2)}) collective-permute-start(s32[1]{0:T(128)} %param.6), channel_id=1, source_target_pairs={{0,128},{64,192},{128,0},{192,64},{1,129},{65,193},{129,1},{193,65... | collective-permute-start | bytes 20 | tf_op jit(solution)/shard_map/ppermute | solution.py:40
  10.5 15.0 %copy-start = (bf16[4,64,896]{2,1,0:T(8,128)(2,1)}, bf16[4,64,896]{2,1,0:T(8,128)(2,1)S(1)}, u32[]{:S(2)}) copy-start(bf16[4,64,896]{2,1,0:T(8,128)(2,1)S(1)} %get-tuple-element.35.refs_0_) | copy-start | bytes 1376260
  10.5 15.0 %copy-start.1 = (bf16[2,64,896]{2,1,0:T(8,128)(2,1)}, bf16[2,64,896]{2,1,0:T(8,128)(2,1)S(1)}, u32[]{:S(2)}) copy-start(bf16[2,64,896]{2,1,0:T(8,128)(2,1)S(1)} %get-tuple-element.44.refs_5_) | copy-start | bytes 688132
  10.5 15.1 %collective-permute-start.5 = (bf16[4,64,896]{2,1,0:T(8,128)(2,1)S(1)}, bf16[4,64,896]{2,1,0:T(8,128)(2,1)S(1)}, u32[]{:S(2)}, u32[]{:S(2)}) collective-permute-start(bf16[4,64,896]{2,1,0:T(8,128)(2,1)S(1)} %get-tuple-element.35.refs_0_), channel_id=1, source_target_pairs={{0,16},{1,17},{2,18},{3,19},{4,20},{5,21},{6,22},{7,23},{8,24},{9,... | collective-permute-start | bytes 1376264 | tf_op jit(solution)/shard_map/ppermute | solution.py:36
  12.2 13.4 %collective-permute-start.6 = (bf16[4,64,896]{2,1,0:T(8,128)(2,1)S(1)}, bf16[4,64,896]{2,1,0:T(8,128)(2,1)S(1)}, u32[]{:S(2)}, u32[]{:S(2)}) collective-permute-start(bf16[4,64,896]{2,1,0:T(8,128)(2,1)S(1)} %get-tuple-element.35.refs_0_), channel_id=1, source_target_pairs={{0,48},{1,49},{2,50},{3,51},{4,52},{5,53},{6,54},{7,55},{8,56},{9,... | collective-permute-start | bytes 1376264 | tf_op jit(solution)/shard_map/ppermute | solution.py:36
  13.8 11.7 %collective-permute-start.7 = (bf16[2,64,896]{2,1,0:T(8,128)(2,1)S(1)}, bf16[2,64,896]{2,1,0:T(8,128)(2,1)S(1)}, u32[]{:S(2)}, u32[]{:S(2)}) collective-permute-start(bf16[2,64,896]{2,1,0:T(8,128)(2,1)S(1)} %get-tuple-element.44.refs_5_), channel_id=1, source_target_pairs={{0,1},{1,2},{2,3},{3,4},{4,5},{5,6},{6,7},{7,0},{8,9},{9,10},{10,1... | collective-permute-start | bytes 688136 | tf_op jit(solution)/shard_map/ppermute | solution.py:36
  15.7 9.8 %collective-permute-start.8 = (bf16[2,64,896]{2,1,0:T(8,128)(2,1)S(1)}, bf16[2,64,896]{2,1,0:T(8,128)(2,1)S(1)}, u32[]{:S(2)}, u32[]{:S(2)}) collective-permute-start(bf16[2,64,896]{2,1,0:T(8,128)(2,1)S(1)} %get-tuple-element.44.refs_5_), channel_id=1, source_target_pairs={{0,7},{1,0},{2,1},{3,2},{4,3},{5,4},{6,5},{7,6},{8,15},{9,8},{10,9... | collective-permute-start | bytes 688136 | tf_op jit(solution)/shard_map/ppermute | solution.py:36
  25.5 16.4 %copy-start.5 = (bf16[2,64,896]{2,1,0:T(8,128)(2,1)}, bf16[2,64,896]{2,1,0:T(8,128)(2,1)S(1)}, u32[]{:S(2)}) copy-start(bf16[2,64,896]{2,1,0:T(8,128)(2,1)S(1)} %collective-permute-done.7.refs_6_) | copy-start | bytes 688132
  25.6 16.4 %copy-start.6 = (bf16[2,64,896]{2,1,0:T(8,128)(2,1)}, bf16[2,64,896]{2,1,0:T(8,128)(2,1)S(1)}, u32[]{:S(2)}) copy-start(bf16[2,64,896]{2,1,0:T(8,128)(2,1)S(1)} %collective-permute-done.8.refs_7_) | copy-start | bytes 688132
  25.6 16.4 %copy-start.3 = (bf16[4,64,896]{2,1,0:T(8,128)(2,1)}, bf16[4,64,896]{2,1,0:T(8,128)(2,1)S(1)}, u32[]{:S(2)}) copy-start(bf16[4,64,896]{2,1,0:T(8,128)(2,1)S(1)} %collective-permute-done.5.refs_1_) | copy-start | bytes 1376260
  25.6 16.4 %copy-start.4 = (bf16[4,64,896]{2,1,0:T(8,128)(2,1)}, bf16[4,64,896]{2,1,0:T(8,128)(2,1)S(1)}, u32[]{:S(2)}) copy-start(bf16[4,64,896]{2,1,0:T(8,128)(2,1)S(1)} %collective-permute-done.6.refs_4_) | copy-start | bytes 1376260
  25.6 30.2 %all-to-all-start = ((bf16[8,3,64,512]{3,2,1,0:T(8,128)(2,1)}), bf16[8,3,64,512]{3,2,1,0:T(8,128)(2,1)S(1)}, u32[]{:S(2)}, u32[]{:S(2)}) async-start(bf16[8,3,64,512]{3,2,1,0:T(8,128)(2,1)} %pack.1), calls=%async_computation | async-start | bytes 3145728 | tf_op jit(solution)/shard_map/all_to_all | solution.py:329
  30.3 8.8 %collective-permute-start.11 = (bf16[2,64,896]{2,1,0:T(8,128)(2,1)S(1)}, bf16[2,64,896]{2,1,0:T(8,128)(2,1)S(1)}, u32[]{:S(2)}, u32[]{:S(2)}) collective-permute-start(bf16[2,64,896]{2,1,0:T(8,128)(2,1)S(1)} %collective-permute-done.7.refs_6_), channel_id=1, source_target_pairs={{0,1},{1,2},{2,3},{3,4},{4,5},{5,6},{6,7},{7,0},{8,9},{9,10},{10,1... | collective-permute-start | bytes 688136 | tf_op jit(solution)/shard_map/ppermute | solution.py:36
  31.2 10.9 %collective-permute-start.12 = (bf16[2,64,896]{2,1,0:T(8,128)(2,1)S(1)}, bf16[2,64,896]{2,1,0:T(8,128)(2,1)S(1)}, u32[]{:S(2)}, u32[]{:S(2)}) collective-permute-start(bf16[2,64,896]{2,1,0:T(8,128)(2,1)S(1)} %collective-permute-done.8.refs_7_), channel_id=1, source_target_pairs={{0,7},{1,0},{2,1},{3,2},{4,3},{5,4},{6,5},{7,6},{8,15},{9,8},{10,9... | collective-permute-start | bytes 688136 | tf_op jit(solution)/shard_map/ppermute | solution.py:36
  39.1 16.9 %copy-start.7 = (bf16[2,64,896]{2,1,0:T(8,128)(2,1)}, bf16[2,64,896]{2,1,0:T(8,128)(2,1)S(1)}, u32[]{:S(2)}) copy-start(bf16[2,64,896]{2,1,0:T(8,128)(2,1)S(1)} %collective-permute-done.11.refs_8_) | copy-start | bytes 688132
  39.1 7.2 %collective-permute-start.13 = (bf16[2,64,896]{2,1,0:T(8,128)(2,1)S(1)}, bf16[2,64,896]{2,1,0:T(8,128)(2,1)S(1)}, u32[]{:S(2)}, u32[]{:S(2)}) collective-permute-start(bf16[2,64,896]{2,1,0:T(8,128)(2,1)S(1)} %collective-permute-done.11.refs_8_), channel_id=1, source_target_pairs={{0,1},{1,2},{2,3},{3,4},{4,5},{5,6},{6,7},{7,0},{8,9},{9,10},{10,1... | collective-permute-start | bytes 688136 | tf_op jit(solution)/shard_map/ppermute | solution.py:36
  39.2 13.3 %collective-permute-start.10 = (bf16[2,64,896]{2,1,0:T(8,128)(2,1)S(1)}, bf16[2,64,896]{2,1,0:T(8,128)(2,1)S(1)}, u32[]{:S(2)}, u32[]{:S(2)}) collective-permute-start(bf16[2,64,896]{2,1,0:T(8,128)(2,1)S(1)} %slice.19), channel_id=1, source_target_pairs={{0,48},{1,49},{2,50},{3,51},{4,52},{5,53},{6,54},{7,55},{8,56},{9,... | collective-permute-start | bytes 688136 | tf_op jit(solution)/shard_map/ppermute | solution.py:36
  42.0 11.8 %collective-permute-start.9 = (bf16[2,64,896]{2,1,0:T(8,128)(2,1)S(1)}, bf16[2,64,896]{2,1,0:T(8,128)(2,1)S(1)}, u32[]{:S(2)}, u32[]{:S(2)}) collective-permute-start(bf16[2,64,896]{2,1,0:T(8,128)(2,1)S(1)} %slice.18), channel_id=1, source_target_pairs={{0,16},{1,17},{2,18},{3,19},{4,20},{5,21},{6,22},{7,23},{8,24},{9,... | collective-permute-start | bytes 688136 | tf_op jit(solution)/shard_map/ppermute | solution.py:36
  42.1 11.7 %copy-start.8 = (bf16[2,64,896]{2,1,0:T(8,128)(2,1)}, bf16[2,64,896]{2,1,0:T(8,128)(2,1)S(1)}, u32[]{:S(2)}) copy-start(bf16[2,64,896]{2,1,0:T(8,128)(2,1)S(1)} %collective-permute-done.12.refs_9_) | copy-start | bytes 688132
  42.1 11.7 %collective-permute-start.14 = (bf16[2,64,896]{2,1,0:T(8,128)(2,1)S(1)}, bf16[2,64,896]{2,1,0:T(8,128)(2,1)S(1)}, u32[]{:S(2)}, u32[]{:S(2)}) collective-permute-start(bf16[2,64,896]{2,1,0:T(8,128)(2,1)S(1)} %collective-permute-done.12.refs_9_), channel_id=1, source_target_pairs={{0,7},{1,0},{2,1},{3,2},{4,3},{5,4},{6,5},{7,6},{8,15},{9,8},{10,9... | collective-permute-start | bytes 688136 | tf_op jit(solution)/shard_map/ppermute | solution.py:36
  46.4 7.4 %copy-start.9 = (bf16[2,64,896]{2,1,0:T(8,128)(2,1)}, bf16[2,64,896]{2,1,0:T(8,128)(2,1)S(1)}, u32[]{:S(2)}) copy-start(bf16[2,64,896]{2,1,0:T(8,128)(2,1)S(1)} %collective-permute-done.13.refs_10_) | copy-start | bytes 688132
  46.4 8.1 %collective-permute-start.15 = (bf16[2,64,896]{2,1,0:T(8,128)(2,1)S(1)}, bf16[2,64,896]{2,1,0:T(8,128)(2,1)S(1)}, u32[]{:S(2)}, u32[]{:S(2)}) collective-permute-start(bf16[2,64,896]{2,1,0:T(8,128)(2,1)S(1)} %collective-permute-done.13.refs_10_), channel_id=1, source_target_pairs={{0,1},{1,2},{2,3},{3,4},{4,5},{5,6},{6,7},{7,0},{8,9},{9,10},{10,1... | collective-permute-start | bytes 688136 | tf_op jit(solution)/shard_map/ppermute | solution.py:36
  52.5 1.3 %copy-start.10 = (bf16[2,64,896]{2,1,0:T(8,128)(2,1)}, bf16[2,64,896]{2,1,0:T(8,128)(2,1)S(1)}, u32[]{:S(2)}) copy-start(bf16[2,64,896]{2,1,0:T(8,128)(2,1)S(1)} %collective-permute-done.10.refs_3_) | copy-start | bytes 688132
  54.4 0.7 copy-start.12
  55.1 0.7 copy-start.13
  55.8 5.5 %collective-permute-start.16 = (bf16[8,3,64,512]{3,2,1,0:T(8,128)(2,1)S(1)}, bf16[8,3,64,512]{3,2,1,0:T(8,128)(2,1)S(1)}, u32[]{:S(2)}, u32[]{:S(2)}) collective-permute-start(bf16[8,3,64,512]{3,2,1,0:T(8,128)(2,1)S(1)} %all-to-all-done.kern_ref), channel_id=1, source_target_pairs={{0,64},{64,0},{128,192},{192,128},{1,65},{65,1},{129,193},{193,129... | collective-permute-start | bytes 4718600 | tf_op jit(solution)/shard_map/ppermute | solution.py:40
  62.2 2.9 %collective-permute-start.17 = (bf16[512,1024]{1,0:T(8,128)(2,1)S(1)}, bf16[512,1024]{1,0:T(8,128)(2,1)S(1)}, u32[]{:S(2)}, u32[]{:S(2)}) collective-permute-start(bf16[512,1024]{1,0:T(8,128)(2,1)S(1)} %mix.1), channel_id=1, source_target_pairs={{0,64},{64,0},{128,192},{192,128},{1,65},{65,1},{129,193},{193,129... | collective-permute-start | bytes 3145736 | tf_op jit(solution)/shard_map/ppermute | solution.py:40
  87.7 16.4 %all-to-all-start.2 = ((f32[4,8,896]{2,1,0:T(8,128)}), f32[4,8,896]{2,1,0:T(8,128)S(1)}, u32[]{:S(2)}, u32[]{:S(2)}) async-start(f32[4,8,896]{2,1,0:T(8,128)} %convert_reduce_fusion), calls=%async_computation.2 | async-start | bytes 229376 | tf_op jit(solution)/shard_map/all_to_all | solution.py:299
  (2 other events, 1.3 us)

commit v28 on v25

--- a/solution.py
+++ b/solution.py
@@ -1,3 +1,5 @@
+import functools
+
 import jax
 import jax.numpy as jnp
 from jax import lax
@@ -166,11 +168,12 @@
     )(place, slots, *arrays)
 
 
-def mix_body(odd_ref, own_ref, far_ref, half_ref, kern_ref, m_ref):
+def mix_body(part, odd_ref, own_ref, far_ref, half_ref, kern_ref, m_ref):
     odd = odd_ref[0] == 1
     sign = jnp.where(odd, -1.0, 1.0).astype(jnp.float32)
-    for i in range(GROUPS):
-        at = pl.ds(i * SLAB, SLAB)
+    for step in range(GROUPS // 2):
+        i = part * (GROUPS // 2) + step
+        at, to = pl.ds(i * SLAB, SLAB), pl.ds(step * SLAB, SLAB)
         mine, other = kern_ref[i, 0], half_ref[i]
         k_re = jnp.where(odd, other, mine).astype(jnp.float32)
         k_im = jnp.where(odd, mine, other).astype(jnp.float32) * sign
@@ -182,14 +185,14 @@
         p_re, p_im = far_ref[at, :BLOCK], far_ref[at, BLOCK:]
         total_re += k_re * p_re - k_im * p_im
         total_im += k_re * p_im + k_im * p_re
-        m_ref[at, :BLOCK] = total_re.astype(jnp.bfloat16)
-        m_ref[at, BLOCK:] = total_im.astype(jnp.bfloat16)
-
-
-def mix(odd, *arrays):
-    return pl.pallas_call(
-        mix_body,
-        out_shape=pltpu.VMEM((BLOCK, 2 * BLOCK), jnp.bfloat16),
+        m_ref[to, :BLOCK] = total_re.astype(jnp.bfloat16)
+        m_ref[to, BLOCK:] = total_im.astype(jnp.bfloat16)
+
+
+def mix(part, odd, *arrays):
+    return pl.pallas_call(
+        functools.partial(mix_body, part),
+        out_shape=pltpu.VMEM((BLOCK // 2, 2 * BLOCK), jnp.bfloat16),
         in_specs=[IN_SMEM] + [IN_VMEM] * 4,
         out_specs=IN_VMEM,
         compiler_params=PARAMS,
@@ -227,8 +230,9 @@
     return outer // 2 * NZ + 2 * half + outer % 2
 
 
-def project_body(m_ref, left_ref, right_ref, out_ref, x_ref, part_ref, sem):
-    y = dot(m_ref[...], right_ref[...], 1, 0)
+def project_body(top_ref, low_ref, left_ref, right_ref, out_ref, x_ref, part_ref, sem):
+    right = right_ref[...]
+    y = jnp.concatenate([dot(m_ref[...], right, 1, 0) for m_ref in (top_ref, low_ref)], axis=0)
     high = y.astype(jnp.bfloat16)
     low = (y - high.astype(jnp.float32)).astype(jnp.bfloat16)
     high = jnp.concatenate([high, turned(high)], axis=0)
@@ -256,7 +260,7 @@
     return pl.pallas_call(
         project_body,
         out_shape=jax.ShapeDtypeStruct(windows, jnp.bfloat16),
-        in_specs=[IN_VMEM] * 3,
+        in_specs=[IN_VMEM] * 4,
         out_specs=pl.BlockSpec(memory_space=pltpu.HBM),
         scratch_shapes=[
             pltpu.VMEM((NB + 8, LANES), jnp.float32),
@@ -265,7 +269,7 @@
         ],
         compiler_params=PARAMS,
         name="project",
-    )(near(m), near(left), near(right))
+    )(*map(near, m), near(left), near(right))
 
 
 def bundle_body(own_ref, far_ref, own_side, far_side, four_ref, both_ref):
@@ -338,7 +342,7 @@
     place = jnp.stack([(y - dy) % NY * NX + (x - dx) % NX for dy in range(NY) for dx in range(NX)])
     slots = jnp.stack([(z + i) % NZ for i in (0, -1, 1, -2, 2, -3, 3, -4)])
     p_own, p_far, rows, cols = density(place, slots, four, up, over, down, cols)
-    m_own = swap_groups(mix(odd, p_own, p_far, half, kern), 1)
+    m_own = [swap_groups(mix(part, odd, p_own, p_far, half, kern), 1) for part in range(2)]
     left, right = prepare(rows, cols)
     total = reduce_windows(project(m_own, left, right))
     flat = total.reshape(2, 8 * NB)

time: 105 us -> 105 us (level)
    ppermute x5 -> x6, waiting for transfers between devices: 5.6 us -> 5.2 us  [swap_groups(): return lax.ppermute(block, 'kgrp', [(k, k ^ bit) for k in range(4)])]
    ppermute x5 -> x6, starting transfers between devices: 3.45 us -> 3.55 us  [swap_groups(): return lax.ppermute(block, 'kgrp', [(k, k ^ bit) for k in range(4)])]
  transfers between devices with their start and end apart: 20 -> 21, of which waited for: 7 -> 8; matrix products, arithmetic and copies ran while one was open for 0% -> 0% of each run, Pallas kernels for 9% -> 10%
where the time goes in v28:
time: 105 us; the launch traced here: 104 us
  starting transfers between devices  38.5 us (37%)
  waiting for transfers between devices  26.5 us (25%)
  blocking collectives  17.8 us (17%)
  Pallas kernels  15.8 us (15%)
  local copies, waits for them, and re-layouts  3.36 us (3%)
  other arithmetic  1.52 us (1%)
    ppermute x12, starting transfers between devices, shift(): return lax.ppermute(block, 'band', band_route(dy, dx, dz))  21.8 us
    all_to_all x1, blocking collectives, reduce_windows(): parts = lax.all_to_all(parts, 'band', 0, 0, axis_index_groups=wide)  17.8 us
    ppermute x12, waiting for transfers between devices, shift(): return lax.ppermute(block, 'band', band_route(dy, dx, dz))  12.4 us
    all_to_all x1, waiting for transfers between devices, reduce_windows(): lax.all_to_all(parts, 'band', 0, 0, axis_index_groups=deep)  8.91 us
    all_to_all x1, starting transfers between devices, reduce_windows(): lax.all_to_all(parts, 'band', 0, 0, axis_index_groups=deep)  7.44 us
    ppermute x6, waiting for transfers between devices, swap_groups(): return lax.ppermute(block, 'kgrp', [(k, k ^ bit) for k in range(4)])  5.2 us
    pallas_call x1, Pallas kernels, density(): pl.pallas_call(density_body, out_shape=[product, product, points, points]...  4.77 us
    all_to_all x1, starting transfers between devices, on_device(): kern = lax.all_to_all(sends, 'band', 0, 0, axis_index_groups=over_yx)  4.73 us
  transfers between devices with their start and end apart: 21, of which 8 were waited for; matrix products, arithmetic and copies ran while one was open for 0% of the time, Pallas kernels for 10%

profile of v28, /device:TPU:6, one launch (start us, length us, event | category | flops | bytes accessed | tf_op | source)
XLA Modules:
  0.0 104.4 jit_solution(15054025265328138477)
XLA Ops:
  0.0 1.0 lay.1.own_ref
  1.0 1.4 %collective-permute-start.2 = (bf16[64,896]{1,0:T(8,128)(2,1)S(1)}, bf16[64,896]{1,0:T(8,128)(2,1)S(1)}, u32[]{:S(2)}, u32[]{:S(2)}) collective-permute-start(bf16[64,896]{1,0:T(8,128)(2,1)S(1)} %lay.1.own_ref), channel_id=1, source_target_pairs={{0,128},{64,192},{128,0},{192,64},{1,129},{65,193},{129,1},{193,65... | collective-permute-start | bytes 344072 | tf_op jit(solution)/shard_map/ppermute | solution.py:42
  2.4 1.7 %collective-permute-start.3 = (bf16[64,896]{1,0:T(8,128)(2,1)S(1)}, bf16[64,896]{1,0:T(8,128)(2,1)S(1)}, u32[]{:S(2)}, u32[]{:S(2)}) collective-permute-start(bf16[64,896]{1,0:T(8,128)(2,1)S(1)} %lay.1.own_ref), channel_id=1, source_target_pairs={{0,8},{1,9},{2,10},{3,11},{4,12},{5,13},{6,14},{7,15},{8,0},{9,1},... | collective-permute-start | bytes 344072 | tf_op jit(solution)/shard_map/ppermute | solution.py:38
  4.1 1.0 collective-permute-start.4
  5.1 1.4 %collective-permute-start.1 = (s32[1]{0:T(128)}, s32[1]{0:T(128)}, u32[]{:S(2)}, u32[]{:S(2)}) collective-permute-start(s32[1]{0:T(128)} %param.6), channel_id=1, source_target_pairs={{0,128},{64,192},{128,0},{192,64},{1,129},{65,193},{129,1},{193,65... | collective-permute-start | bytes 20 | tf_op jit(solution)/shard_map/ppermute | solution.py:42
  6.5 3.9 %collective-permute-done.1.far_ref = s32[1]{0:T(128)} collective-permute-done((s32[1]{0:T(128)}, s32[1]{0:T(128)}, u32[]{:S(2)}, u32[]{:S(2)}) %collective-permute-start.1) | collective-permute-done | bytes 36 | tf_op jit(solution)/shard_map/ppermute | solution.py:42
  10.5 1.7 %collective-permute-start.5 = (bf16[4,64,896]{2,1,0:T(8,128)(2,1)S(1)}, bf16[4,64,896]{2,1,0:T(8,128)(2,1)S(1)}, u32[]{:S(2)}, u32[]{:S(2)}) collective-permute-start(bf16[4,64,896]{2,1,0:T(8,128)(2,1)S(1)} %get-tuple-element.35.refs_0_), channel_id=1, source_target_pairs={{0,16},{1,17},{2,18},{3,19},{4,20},{5,21},{6,22},{7,23},{8,24},{9,... | collective-permute-start | bytes 1376264 | tf_op jit(solution)/shard_map/ppermute | solution.py:38
  12.1 1.7 %collective-permute-start.6 = (bf16[4,64,896]{2,1,0:T(8,128)(2,1)S(1)}, bf16[4,64,896]{2,1,0:T(8,128)(2,1)S(1)}, u32[]{:S(2)}, u32[]{:S(2)}) collective-permute-start(bf16[4,64,896]{2,1,0:T(8,128)(2,1)S(1)} %get-tuple-element.35.refs_0_), channel_id=1, source_target_pairs={{0,48},{1,49},{2,50},{3,51},{4,52},{5,53},{6,54},{7,55},{8,56},{9,... | collective-permute-start | bytes 1376264 | tf_op jit(solution)/shard_map/ppermute | solution.py:38
  13.8 1.9 %collective-permute-start.7 = (bf16[2,64,896]{2,1,0:T(8,128)(2,1)S(1)}, bf16[2,64,896]{2,1,0:T(8,128)(2,1)S(1)}, u32[]{:S(2)}, u32[]{:S(2)}) collective-permute-start(bf16[2,64,896]{2,1,0:T(8,128)(2,1)S(1)} %get-tuple-element.44.refs_5_), channel_id=1, source_target_pairs={{0,1},{1,2},{2,3},{3,4},{4,5},{5,6},{6,7},{7,0},{8,9},{9,10},{10,1... | collective-permute-start | bytes 688136 | tf_op jit(solution)/shard_map/ppermute | solution.py:38
  15.7 3.9 %collective-permute-start.8 = (bf16[2,64,896]{2,1,0:T(8,128)(2,1)S(1)}, bf16[2,64,896]{2,1,0:T(8,128)(2,1)}, u32[]{:S(2)}, u32[]{:S(2)}) collective-permute-start(bf16[2,64,896]{2,1,0:T(8,128)(2,1)S(1)} %get-tuple-element.44.refs_5_), channel_id=1, source_target_pairs={{0,7},{1,0},{2,1},{3,2},{4,3},{5,4},{6,5},{7,6},{8,15},{9,8},{10,9... | collective-permute-start | bytes 688136 | tf_op jit(solution)/shard_map/ppermute | solution.py:38
  20.3 0.6 copy-done.1
  21.0 4.5 %pack.1 = bf16[8,3,64,512]{3,2,1,0:T(8,128)(2,1)} custom-call(s32[1]{0:T(128)} %bitcast.odd_ref, s32[1]{0:T(128)S(6)} %copy.5.own_ref, s32[1]{0:T(128)} %collective-permute-done.core_ref, s32[1]{0:T(128)} %collective-permute-done.1.far_ref, s32[8]{0:T(128)S(1)} %copy-done.1, bf16[4,2,64,4096]{3,2,1,0:T(8,128)(2,1)} %kernels_ref.1), custom_call_target="tpu_custom_call" | custom-call | tf_op jit(solution)/shard_map/pack/pallas_call | solution.py:111
  25.6 4.7 %all-to-all-start = ((bf16[8,3,64,512]{3,2,1,0:T(8,128)(2,1)}), bf16[8,3,64,512]{3,2,1,0:T(8,128)(2,1)S(1)}, u32[]{:S(2)}, u32[]{:S(2)}) async-start(bf16[8,3,64,512]{3,2,1,0:T(8,128)(2,1)} %pack.1), calls=%async_computation | async-start | bytes 3145728 | tf_op jit(solution)/shard_map/all_to_all | solution.py:333
  30.3 0.9 collective-permute-start.11
  31.2 3.9 %collective-permute-start.12 = (bf16[2,64,896]{2,1,0:T(8,128)(2,1)}, bf16[2,64,896]{2,1,0:T(8,128)(2,1)S(1)}, u32[]{:S(2)}, u32[]{:S(2)}) collective-permute-start(bf16[2,64,896]{2,1,0:T(8,128)(2,1)} %collective-permute-done.8.refs_7_), channel_id=1, source_target_pairs={{0,7},{1,0},{2,1},{3,2},{4,3},{5,4},{6,5},{7,6},{8,15},{9,8},{10,9... | collective-permute-start | bytes 688136 | tf_op jit(solution)/shard_map/ppermute | solution.py:38
  35.1 4.0 %collective-permute-done.11.refs_8_ = bf16[2,64,896]{2,1,0:T(8,128)(2,1)S(1)} collective-permute-done((bf16[2,64,896]{2,1,0:T(8,128)(2,1)S(1)}, bf16[2,64,896]{2,1,0:T(8,128)(2,1)S(1)}, u32[]{:S(2)}, u32[]{:S(2)}) %collective-permute-start.11) | collective-permute-done | bytes 229408 | tf_op jit(solution)/shard_map/ppermute | solution.py:38
  39.1 2.8 %collective-permute-start.10 = (bf16[2,64,896]{2,1,0:T(8,128)(2,1)S(1)}, bf16[2,64,896]{2,1,0:T(8,128)(2,1)S(1)}, u32[]{:S(2)}, u32[]{:S(2)}) collective-permute-start(bf16[2,64,896]{2,1,0:T(8,128)(2,1)S(1)} %slice.22), channel_id=1, source_target_pairs={{0,48},{1,49},{2,50},{3,51},{4,52},{5,53},{6,54},{7,55},{8,56},{9,... | collective-permute-start | bytes 688136 | tf_op jit(solution)/shard_map/ppermute | solution.py:38
  42.0 3.3 %collective-permute-start.14 = (bf16[2,64,896]{2,1,0:T(8,128)(2,1)S(1)}, bf16[2,64,896]{2,1,0:T(8,128)(2,1)S(1)}, u32[]{:S(2)}, u32[]{:S(2)}) collective-permute-start(bf16[2,64,896]{2,1,0:T(8,128)(2,1)S(1)} %collective-permute-done.12.refs_9_), channel_id=1, source_target_pairs={{0,7},{1,0},{2,1},{3,2},{4,3},{5,4},{6,5},{7,6},{8,15},{9,8},{10,9... | collective-permute-start | bytes 688136 | tf_op jit(solution)/shard_map/ppermute | solution.py:38
  45.3 1.0 collective-permute-done.13.refs_10_
  46.4 6.1 %collective-permute-done.10.refs_3_ = bf16[2,64,896]{2,1,0:T(8,128)(2,1)S(1)} collective-permute-done((bf16[2,64,896]{2,1,0:T(8,128)(2,1)S(1)}, bf16[2,64,896]{2,1,0:T(8,128)(2,1)S(1)}, u32[]{:S(2)}, u32[]{:S(2)}) %collective-permute-start.10) | collective-permute-done | bytes 229408 | tf_op jit(solution)/shard_map/ppermute | solution.py:38
  52.4 1.3 %collective-permute-done.9.refs_2_ = bf16[2,64,896]{2,1,0:T(8,128)(2,1)S(1)} collective-permute-done((bf16[2,64,896]{2,1,0:T(8,128)(2,1)S(1)}, bf16[2,64,896]{2,1,0:T(8,128)(2,1)S(1)}, u32[]{:S(2)}, u32[]{:S(2)}) %collective-permute-start.9) | collective-permute-done | bytes 229408 | tf_op jit(solution)/shard_map/ppermute | solution.py:38
  53.8 0.6 copy-done.7
  54.4 0.7 copy-done.8
  55.1 0.9 slice_bitcast_fusion
  56.1 4.8 %density.1 = (f32[512,1024]{1,0:T(8,128)S(1)}, f32[512,1024]{1,0:T(8,128)S(1)}, bf16[512,896]{1,0:T(8,128)(2,1)S(1)}, bf16[512,896]{1,0:T(8,128)(2,1)S(1)}) custom-call(s32[8]{0:T(128)S(1)} %stack.71.place_ref, s32[8]{0:T(128)S(1)} %stack.80.slot_ref, bf16[4,64,896]{2,1,0:T(8,128)(2,1)S(1)} %get-tuple-element.35.refs_0_, ...), custom_call_target="tpu_custom_call" | custom-call | tf_op jit(solution)/shard_map/density/pallas_call | solution.py:159
  63.5 0.9 collective-permute-done.17.top_ref
  64.4 4.0 %project.1 = bf16[32,16,896]{2,1,0:T(8,128)(2,1)S(1)} custom-call(bf16[256,1024]{1,0:T(8,128)(2,1)S(1)} %collective-permute-done.17.top_ref, bf16[256,1024]{1,0:T(8,128)(2,1)S(1)} %collective-permute-done.18.low_ref, bf16[432,1024]{1,0:T(8,128)(2,1)S(1)} %get-tuple-element.57.left_ref, bf16[1024,896]{1,0:T(8,128)(2,1)S(1)} %get-tuple-element.58.right_ref), custom_call_target="tpu_custom_call" | custom-call | tf_op jit(solution)/shard_map/project/pallas_call | solution.py:260
  68.4 17.8 %all_to_all.15 = bf16[16,4,8,896]{3,2,1,0:T(8,128)(2,1)S(1)} all-to-all(bf16[16,4,8,896]{3,2,1,0:T(8,128)(2,1)S(1)} %bitcast.22), channel_id=1, replica_groups={{0,1,8,9,16,17,24,25,32,33,40,41,48,49,56,57},{2,3,10,11,18,19,26,27,34..., dimensions={0} | all-to-all | bytes 1835008 | tf_op jit(solution)/shard_map/all_to_all | solution.py:301
  86.3 0.8 convert_reduce_fusion
  87.0 7.4 %all-to-all-start.2 = ((f32[4,8,896]{2,1,0:T(8,128)}), f32[4,8,896]{2,1,0:T(8,128)S(1)}, u32[]{:S(2)}, u32[]{:S(2)}) async-start(f32[4,8,896]{2,1,0:T(8,128)} %convert_reduce_fusion), calls=%async_computation.2 | async-start | bytes 229376 | tf_op jit(solution)/shard_map/all_to_all | solution.py:303
  94.5 8.9 %all-to-all-done.2 = f32[4,8,896]{2,1,0:T(8,128)S(1)} async-done(((f32[4,8,896]{2,1,0:T(8,128)}), f32[4,8,896]{2,1,0:T(8,128)S(1)}, u32[]{:S(2)}, u32[]{:S(2)}) %all-to-all-start.2) | async-done | bytes 114720 | tf_op jit(solution)/shard_map/all_to_all | solution.py:303
  103.7 0.7 fusion.1
  (50 shorter events, 3.3 us)
Async XLA Ops:
  1.0 9.4 %collective-permute-start.2 = (bf16[64,896]{1,0:T(8,128)(2,1)S(1)}, bf16[64,896]{1,0:T(8,128)(2,1)S(1)}, u32[]{:S(2)}, u32[]{:S(2)}) collective-permute-start(bf16[64,896]{1,0:T(8,128)(2,1)S(1)} %lay.1.own_ref), channel_id=1, source_target_pairs={{0,128},{64,192},{128,0},{192,64},{1,129},{65,193},{129,1},{193,65... | collective-permute-start | bytes 344072 | tf_op jit(solution)/shard_map/ppermute | solution.py:42
  2.4 8.0 %collective-permute-start.3 = (bf16[64,896]{1,0:T(8,128)(2,1)S(1)}, bf16[64,896]{1,0:T(8,128)(2,1)S(1)}, u32[]{:S(2)}, u32[]{:S(2)}) collective-permute-start(bf16[64,896]{1,0:T(8,128)(2,1)S(1)} %lay.1.own_ref), channel_id=1, source_target_pairs={{0,8},{1,9},{2,10},{3,11},{4,12},{5,13},{6,14},{7,15},{8,0},{9,1},... | collective-permute-start | bytes 344072 | tf_op jit(solution)/shard_map/ppermute | solution.py:38
  4.1 6.3 %collective-permute-start.4 = (bf16[64,896]{1,0:T(8,128)(2,1)S(1)}, bf16[64,896]{1,0:T(8,128)(2,1)S(1)}, u32[]{:S(2)}, u32[]{:S(2)}) collective-permute-start(bf16[64,896]{1,0:T(8,128)(2,1)S(1)} %lay.1.own_ref), channel_id=1, source_target_pairs={{128,8},{129,9},{130,10},{131,11},{132,12},{133,13},{134,14},{135,... | collective-permute-start | bytes 344072 | tf_op jit(solution)/shard_map/ppermute | solution.py:48
  5.1 1.4 %collective-permute-start = (s32[1]{0:T(128)}, s32[1]{0:T(128)}, u32[]{:S(2)}, u32[]{:S(2)}) collective-permute-start(s32[1]{0:T(128)} %param.6), channel_id=1, source_target_pairs={{0,64},{64,0},{128,192},{192,128},{1,65},{65,1},{129,193},{193,129... | collective-permute-start | bytes 20 | tf_op jit(solution)/shard_map/ppermute | solution.py:42
  5.1 5.3 %collective-permute-start.1 = (s32[1]{0:T(128)}, s32[1]{0:T(128)}, u32[]{:S(2)}, u32[]{:S(2)}) collective-permute-start(s32[1]{0:T(128)} %param.6), channel_id=1, source_target_pairs={{0,128},{64,192},{128,0},{192,64},{1,129},{65,193},{129,1},{193,65... | collective-permute-start | bytes 20 | tf_op jit(solution)/shard_map/ppermute | solution.py:42
  10.5 15.0 %copy-start = (bf16[2,64,896]{2,1,0:T(8,128)(2,1)}, bf16[2,64,896]{2,1,0:T(8,128)(2,1)S(1)}, u32[]{:S(2)}) copy-start(bf16[2,64,896]{2,1,0:T(8,128)(2,1)S(1)} %get-tuple-element.44.refs_5_) | copy-start | bytes 688132
  10.5 15.1 %collective-permute-start.5 = (bf16[4,64,896]{2,1,0:T(8,128)(2,1)S(1)}, bf16[4,64,896]{2,1,0:T(8,128)(2,1)S(1)}, u32[]{:S(2)}, u32[]{:S(2)}) collective-permute-start(bf16[4,64,896]{2,1,0:T(8,128)(2,1)S(1)} %get-tuple-element.35.refs_0_), channel_id=1, source_target_pairs={{0,16},{1,17},{2,18},{3,19},{4,20},{5,21},{6,22},{7,23},{8,24},{9,... | collective-permute-start | bytes 1376264 | tf_op jit(solution)/shard_map/ppermute | solution.py:38
  12.1 13.4 %collective-permute-start.6 = (bf16[4,64,896]{2,1,0:T(8,128)(2,1)S(1)}, bf16[4,64,896]{2,1,0:T(8,128)(2,1)S(1)}, u32[]{:S(2)}, u32[]{:S(2)}) collective-permute-start(bf16[4,64,896]{2,1,0:T(8,128)(2,1)S(1)} %get-tuple-element.35.refs_0_), channel_id=1, source_target_pairs={{0,48},{1,49},{2,50},{3,51},{4,52},{5,53},{6,54},{7,55},{8,56},{9,... | collective-permute-start | bytes 1376264 | tf_op jit(solution)/shard_map/ppermute | solution.py:38
  13.8 11.7 %collective-permute-start.7 = (bf16[2,64,896]{2,1,0:T(8,128)(2,1)S(1)}, bf16[2,64,896]{2,1,0:T(8,128)(2,1)S(1)}, u32[]{:S(2)}, u32[]{:S(2)}) collective-permute-start(bf16[2,64,896]{2,1,0:T(8,128)(2,1)S(1)} %get-tuple-element.44.refs_5_), channel_id=1, source_target_pairs={{0,1},{1,2},{2,3},{3,4},{4,5},{5,6},{6,7},{7,0},{8,9},{9,10},{10,1... | collective-permute-start | bytes 688136 | tf_op jit(solution)/shard_map/ppermute | solution.py:38
  15.7 9.8 %collective-permute-start.8 = (bf16[2,64,896]{2,1,0:T(8,128)(2,1)S(1)}, bf16[2,64,896]{2,1,0:T(8,128)(2,1)}, u32[]{:S(2)}, u32[]{:S(2)}) collective-permute-start(bf16[2,64,896]{2,1,0:T(8,128)(2,1)S(1)} %get-tuple-element.44.refs_5_), channel_id=1, source_target_pairs={{0,7},{1,0},{2,1},{3,2},{4,3},{5,4},{6,5},{7,6},{8,15},{9,8},{10,9... | collective-permute-start | bytes 688136 | tf_op jit(solution)/shard_map/ppermute | solution.py:38
  20.3 0.7 copy-start.1
  25.5 13.6 %copy-start.2 = (bf16[2,64,896]{2,1,0:T(8,128)(2,1)}, bf16[2,64,896]{2,1,0:T(8,128)(2,1)S(1)}, u32[]{:S(2)}) copy-start(bf16[2,64,896]{2,1,0:T(8,128)(2,1)S(1)} %collective-permute-done.7.refs_6_) | copy-start | bytes 688132
  25.6 29.5 %all-to-all-start = ((bf16[8,3,64,512]{3,2,1,0:T(8,128)(2,1)}), bf16[8,3,64,512]{3,2,1,0:T(8,128)(2,1)S(1)}, u32[]{:S(2)}, u32[]{:S(2)}) async-start(bf16[8,3,64,512]{3,2,1,0:T(8,128)(2,1)} %pack.1), calls=%async_computation | async-start | bytes 3145728 | tf_op jit(solution)/shard_map/all_to_all | solution.py:333
  30.3 8.8 %collective-permute-start.11 = (bf16[2,64,896]{2,1,0:T(8,128)(2,1)S(1)}, bf16[2,64,896]{2,1,0:T(8,128)(2,1)S(1)}, u32[]{:S(2)}, u32[]{:S(2)}) collective-permute-start(bf16[2,64,896]{2,1,0:T(8,128)(2,1)S(1)} %collective-permute-done.7.refs_6_), channel_id=1, source_target_pairs={{0,1},{1,2},{2,3},{3,4},{4,5},{5,6},{6,7},{7,0},{8,9},{9,10},{10,1... | collective-permute-start | bytes 688136 | tf_op jit(solution)/shard_map/ppermute | solution.py:38
  31.2 10.8 %collective-permute-start.12 = (bf16[2,64,896]{2,1,0:T(8,128)(2,1)}, bf16[2,64,896]{2,1,0:T(8,128)(2,1)S(1)}, u32[]{:S(2)}, u32[]{:S(2)}) collective-permute-start(bf16[2,64,896]{2,1,0:T(8,128)(2,1)} %collective-permute-done.8.refs_7_), channel_id=1, source_target_pairs={{0,7},{1,0},{2,1},{3,2},{4,3},{5,4},{6,5},{7,6},{8,15},{9,8},{10,9... | collective-permute-start | bytes 688136 | tf_op jit(solution)/shard_map/ppermute | solution.py:38
  39.1 14.6 %copy-start.3 = (bf16[2,64,896]{2,1,0:T(8,128)(2,1)}, bf16[2,64,896]{2,1,0:T(8,128)(2,1)S(1)}, u32[]{:S(2)}) copy-start(bf16[2,64,896]{2,1,0:T(8,128)(2,1)S(1)} %collective-permute-done.11.refs_8_) | copy-start | bytes 688132
  39.1 7.2 %collective-permute-start.13 = (bf16[2,64,896]{2,1,0:T(8,128)(2,1)S(1)}, bf16[2,64,896]{2,1,0:T(8,128)(2,1)S(1)}, u32[]{:S(2)}, u32[]{:S(2)}) collective-permute-start(bf16[2,64,896]{2,1,0:T(8,128)(2,1)S(1)} %collective-permute-done.11.refs_8_), channel_id=1, source_target_pairs={{0,1},{1,2},{2,3},{3,4},{4,5},{5,6},{6,7},{7,0},{8,9},{9,10},{10,1... | collective-permute-start | bytes 688136 | tf_op jit(solution)/shard_map/ppermute | solution.py:38
  39.1 13.3 %collective-permute-start.10 = (bf16[2,64,896]{2,1,0:T(8,128)(2,1)S(1)}, bf16[2,64,896]{2,1,0:T(8,128)(2,1)S(1)}, u32[]{:S(2)}, u32[]{:S(2)}) collective-permute-start(bf16[2,64,896]{2,1,0:T(8,128)(2,1)S(1)} %slice.22), channel_id=1, source_target_pairs={{0,48},{1,49},{2,50},{3,51},{4,52},{5,53},{6,54},{7,55},{8,56},{9,... | collective-permute-start | bytes 688136 | tf_op jit(solution)/shard_map/ppermute | solution.py:38
  41.9 11.8 %collective-permute-start.9 = (bf16[2,64,896]{2,1,0:T(8,128)(2,1)S(1)}, bf16[2,64,896]{2,1,0:T(8,128)(2,1)S(1)}, u32[]{:S(2)}, u32[]{:S(2)}) collective-permute-start(bf16[2,64,896]{2,1,0:T(8,128)(2,1)S(1)} %slice.21), channel_id=1, source_target_pairs={{0,16},{1,17},{2,18},{3,19},{4,20},{5,21},{6,22},{7,23},{8,24},{9,... | collective-permute-start | bytes 688136 | tf_op jit(solution)/shard_map/ppermute | solution.py:38
  42.0 11.7 %copy-start.4 = (bf16[2,64,896]{2,1,0:T(8,128)(2,1)}, bf16[2,64,896]{2,1,0:T(8,128)(2,1)S(1)}, u32[]{:S(2)}) copy-start(bf16[2,64,896]{2,1,0:T(8,128)(2,1)S(1)} %collective-permute-done.12.refs_9_) | copy-start | bytes 688132
  42.0 11.7 %collective-permute-start.14 = (bf16[2,64,896]{2,1,0:T(8,128)(2,1)S(1)}, bf16[2,64,896]{2,1,0:T(8,128)(2,1)S(1)}, u32[]{:S(2)}, u32[]{:S(2)}) collective-permute-start(bf16[2,64,896]{2,1,0:T(8,128)(2,1)S(1)} %collective-permute-done.12.refs_9_), channel_id=1, source_target_pairs={{0,7},{1,0},{2,1},{3,2},{4,3},{5,4},{6,5},{7,6},{8,15},{9,8},{10,9... | collective-permute-start | bytes 688136 | tf_op jit(solution)/shard_map/ppermute | solution.py:38
  46.3 7.4 %copy-start.5 = (bf16[2,64,896]{2,1,0:T(8,128)(2,1)}, bf16[2,64,896]{2,1,0:T(8,128)(2,1)S(1)}, u32[]{:S(2)}) copy-start(bf16[2,64,896]{2,1,0:T(8,128)(2,1)S(1)} %collective-permute-done.13.refs_10_) | copy-start | bytes 688132
  46.4 8.8 %collective-permute-start.15 = (bf16[2,64,896]{2,1,0:T(8,128)(2,1)S(1)}, bf16[2,64,896]{2,1,0:T(8,128)(2,1)}, u32[]{:S(2)}, u32[]{:S(2)}) collective-permute-start(bf16[2,64,896]{2,1,0:T(8,128)(2,1)S(1)} %collective-permute-done.13.refs_10_), channel_id=1, source_target_pairs={{0,1},{1,2},{2,3},{3,4},{4,5},{5,6},{6,7},{7,0},{8,9},{9,10},{10,1... | collective-permute-start | bytes 688136 | tf_op jit(solution)/shard_map/ppermute | solution.py:38
  52.4 1.3 %copy-start.6 = (bf16[2,64,896]{2,1,0:T(8,128)(2,1)}, bf16[2,64,896]{2,1,0:T(8,128)(2,1)S(1)}, u32[]{:S(2)}) copy-start(bf16[2,64,896]{2,1,0:T(8,128)(2,1)S(1)} %collective-permute-done.10.refs_3_) | copy-start | bytes 688132
  53.7 0.7 copy-start.7
  54.4 0.7 copy-start.8
  56.0 5.0 %collective-permute-start.16 = (bf16[8,64,512]{2,1,0:T(8,128)(2,1)}, bf16[8,64,512]{2,1,0:T(8,128)(2,1)S(1)}, u32[]{:S(2)}, u32[]{:S(2)}) collective-permute-start(bf16[8,64,512]{2,1,0:T(8,128)(2,1)} %slice_bitcast_fusion), channel_id=1, source_target_pairs={{0,64},{64,0},{128,192},{192,128},{1,65},{65,1},{129,193},{193,129... | collective-permute-start | bytes 1572872 | tf_op jit(solution)/shard_map/ppermute | solution.py:42
  61.4 2.1 %collective-permute-start.18 = (bf16[256,1024]{1,0:T(8,128)(2,1)S(1)}, bf16[256,1024]{1,0:T(8,128)(2,1)S(1)}, u32[]{:S(2)}, u32[]{:S(2)}) collective-permute-start(bf16[256,1024]{1,0:T(8,128)(2,1)S(1)} %mix.3), channel_id=1, source_target_pairs={{0,64},{64,0},{128,192},{192,128},{1,65},{65,1},{129,193},{193,129... | collective-permute-start | bytes 1572872 | tf_op jit(solution)/shard_map/ppermute | solution.py:42
  62.5 2.0 %collective-permute-start.17 = (bf16[256,1024]{1,0:T(8,128)(2,1)S(1)}, bf16[256,1024]{1,0:T(8,128)(2,1)S(1)}, u32[]{:S(2)}, u32[]{:S(2)}) collective-permute-start(bf16[256,1024]{1,0:T(8,128)(2,1)S(1)} %mix.2), channel_id=1, source_target_pairs={{0,64},{64,0},{128,192},{192,128},{1,65},{65,1},{129,193},{193,129... | collective-permute-start | bytes 1572872 | tf_op jit(solution)/shard_map/ppermute | solution.py:42
  87.0 16.3 %all-to-all-start.2 = ((f32[4,8,896]{2,1,0:T(8,128)}), f32[4,8,896]{2,1,0:T(8,128)S(1)}, u32[]{:S(2)}, u32[]{:S(2)}) async-start(f32[4,8,896]{2,1,0:T(8,128)} %convert_reduce_fusion), calls=%async_computation.2 | async-start | bytes 229376 | tf_op jit(solution)/shard_map/all_to_all | solution.py:303
